TPU v7x, 32 devices: a whole 2x2x4 slice. The times are simulated.
32 devices in a mesh: replica: 8 (over z, core), mp: 4 (over y, x).
Axes of the slice: x: 2, y: 2, z: 4, core: 2. Of those that a mesh axis runs over, the one named last changes fastest.
Arguments:
- gradients: bfloat16 [8, 8, 768, 3072], P('replica', None, 'mp'), may hold values from -6 to 6
- feedback: bfloat16 [8, 8, 768, 3072], P('replica', None, 'mp'), may hold values from -4 to 4
- right_init: bfloat16 [8, 3072, 32], replicated, may hold values from -0.109375 to 0.109375
- gram_root: float32 [8, 32, 32], replicated, as said below
- owners: int32 [8], replicated, may hold values from 0 to 3, as said below
- momentum: float32 [4, 2, 768, 3072], P('mp', None, 'replica'), may hold values from -4 to 4
- master_weights: float32 [4, 2, 768, 3072], P('mp', None, 'replica'), may hold values from -1.5 to 1.5
- vector_grads: float32 [8, 10752], P('replica', 'mp'), may hold values from -6 to 6
- vector_momentum: float32 [10752], P('mp'), may hold values from -6 to 6
- vector_params: float32 [10752], P('mp'), may hold values from -6 to 6
Outputs:
- new_feedback: bfloat16 [8, 8, 768, 3072], P('replica', None, 'mp')
- new_momentum: float32 [4, 2, 768, 3072], P('mp', None, 'replica')
- new_master: float32 [4, 2, 768, 3072], P('mp', None, 'replica')
- new_weights: bfloat16 [8, 768, 3072], P(None, 'replica')
- new_vector_momentum: float32 [10752], P('mp')
- new_vector_params: float32 [10752], P('mp')
Inputs may be any that keep to these rules, and one draw needn't show every extreme that they name: `owners`: every matrix has one owner; no owner holds more than 2 of the 8 matrices, and one owner holds exactly 2. `gram_root`: each matrix is the identity plus off-diagonal terms, times a positive scale.
All inputs are finite; a program needn't handle non-finite values.
Results may differ from a plain program's by a relative error of at most 0.007.
Values may be sent and summed in bfloat16 or wider, within the bound.
No kernel may reach another device: no remote copies, remote signals or barrier semaphores. Data moves between devices by JAX's collectives and lax.ppermute only.
A program may use at most 192 MiB of HBM per device.

v0:
```python
import jax
import jax.numpy as jnp
from jax import lax
from jax.sharding import PartitionSpec as P


def per_device(
    gradients,
    feedback,
    right_init,
    gram_root,
    owners,
    momentum,
    master_weights,
    vector_grads,
    vector_momentum,
    vector_params,
):
    highest = lax.Precision.HIGHEST
    compensated = (gradients[0].astype(jnp.float32) + feedback[0].astype(jnp.float32)).astype(
        jnp.bfloat16
    )
    owner_count = lax.axis_size("mp")
    capacity = momentum.shape[1]
    matrices = owners.shape[0]
    replica_rows = momentum.shape[2]
    mp_index = lax.axis_index("mp")
    replica_index = lax.axis_index("replica")
    same_owner = owners[:, None] == owners[None, :]
    earlier = jnp.arange(matrices)[:, None] < jnp.arange(matrices)[None, :]
    ranks = jnp.sum((same_owner & earlier).astype(jnp.int32), axis=0)
    slots = owners * capacity + ranks
    slot_table = (slots[None, :] == jnp.arange(owner_count * capacity)[:, None]).astype(jnp.float32)
    table_narrow = slot_table.astype(jnp.bfloat16)
    table_mine = lax.dynamic_slice_in_dim(slot_table, mp_index * capacity, capacity, 0)
    left_terms = jnp.einsum(
        "kmn,knr->kmr", compensated, right_init, preferred_element_type=jnp.float32
    )
    left_sum = lax.psum(left_terms, "replica")
    left_rows = jnp.einsum("kmr,krs->kms", left_sum, gram_root, precision=highest).astype(
        jnp.bfloat16
    )
    right_terms = jnp.einsum(
        "kmn,kms->kns", compensated, left_rows, preferred_element_type=jnp.float32
    )
    right_new = lax.psum(right_terms, ("replica", "mp"))
    left_all = lax.all_gather(left_rows, "mp", axis=1, tiled=True)
    approx_rows = jnp.einsum(
        "kms,kns->kmn", left_rows.astype(jnp.float32), right_new, precision=highest
    )
    new_feedback = (compensated.astype(jnp.float32) - approx_rows).astype(jnp.bfloat16)
    left_chosen = jnp.einsum(
        "ck,kmr->cmr", table_mine.astype(jnp.bfloat16), left_all, preferred_element_type=jnp.float32
    )
    left_chosen = lax.dynamic_slice_in_dim(
        left_chosen, replica_index * replica_rows, replica_rows, 1
    )
    right_chosen = jnp.einsum("ck,knr->cnr", table_mine, right_new, precision=highest)
    approx_slots = jnp.einsum("cmr,cnr->cmn", left_chosen, right_chosen, precision=highest)
    new_momentum = 0.9 * momentum[0] + approx_slots
    new_master = master_weights[0] - 0.1 * new_momentum
    master_narrow = new_master.astype(jnp.bfloat16)
    weight_slots = lax.all_gather(master_narrow, "mp", axis=0, tiled=True)
    new_weights = jnp.einsum(
        "sk,smn->kmn", table_narrow, weight_slots, preferred_element_type=jnp.float32
    ).astype(jnp.bfloat16)
    vector_total = lax.psum(vector_grads[0], "replica")
    new_vector_momentum = 0.9 * vector_momentum + vector_total
    new_vector_params = vector_params - 0.1 * new_vector_momentum
    return (
        new_feedback[None],
        new_momentum[None],
        new_master[None],
        new_weights,
        new_vector_momentum,
        new_vector_params,
    )


def solution(mesh):
    return jax.shard_map(
        per_device,
        mesh=mesh,
        in_specs=(
            P("replica", None, "mp", None),
            P("replica", None, "mp", None),
            P(),
            P(),
            P(),
            P("mp", None, "replica", None),
            P("mp", None, "replica", None),
            P("replica", "mp"),
            P("mp"),
            P("mp"),
        ),
        out_specs=(
            P("replica", None, "mp", None),
            P("mp", None, "replica", None),
            P("mp", None, "replica", None),
            P(None, "replica", None),
            P("mp"),
            P("mp"),
        ),
        check_vma=False,
    )
```

profile of v0, /device:TPU:1, one launch (start us, length us, event | category | flops | bytes accessed | tf_op | source)
XLA Modules:
  0.0 309.4 jit_solution(4926910256595260321)
XLA Ops:
  7.2 0.0 copy-start
  7.2 0.0 all-reduce.3.cloned.1.call-start
  7.2 1.3 copy-done
  8.6 10.0 %fusion.22 = f32[8,192,32]{1,2,0:T(8,128)} fusion(bf16[8,3072,32]{1,2,0:T(8,128)(2,1)S(1)} %copy-done, bf16[1,8,192,3072]{3,2,1,0:T(8,128)(2,1)} %param.11, bf16[1,8,192,3072]{3,2,1,0:T(8,128)(2,1)} %param.10), kind=kOutput, calls=%fused_computation.34 | convolution fusion | flops 320864256 | bytes 20643840 | tf_op jit(solution)/shard_map/kmn,knr->kmr/dot_general | solution.py:36
  18.6 0.0 all-reduce.3.cloned.1.call-update
  18.7 0.0 all-reduce.5.cloned.1.call-start
  18.7 55.4 %all-reduce.3.cloned.1.call-done = f32[8,192,32]{1,2,0:T(8,128)} async-done(((f32[8,192,32]{1,2,0:T(8,128)}), f32[8,192,32]{1,2,0:T(8,128)}) %all-reduce.3.cloned.1.call-update) | async-done | bytes 196624 | tf_op jit(solution)/shard_map/psum | solution.py:39
  74.1 1.4 convolution_convert_fusion.1
  75.5 0.0 copy-start.8
  75.5 10.8 %fusion.20 = f32[8,3072,32]{1,2,0:T(8,128)} fusion(bf16[8,192,32]{1,2,0:T(8,128)(2,1)S(1)} %convolution_convert_fusion.1, bf16[1,8,192,3072]{3,2,1,0:T(8,128)(2,1)} %param.11, bf16[1,8,192,3072]{3,2,1,0:T(8,128)(2,1)} %param.10), kind=kOutput, calls=%fused_computation.33 | convolution fusion | flops 320864256 | bytes 22118400 | tf_op jit(solution)/shard_map/kmn,kms->kns/dot_general | solution.py:43
  86.3 0.0 all-reduce.5.cloned.1.call-update
  86.3 0.0 all-gather.2.cloned.1.call-start
  86.4 0.0 copy-done.8
  86.4 0.1 convert_reduce_fusion
  86.5 1.0 copy.24
  87.5 18.1 %all_gather.6 = bf16[8,768,32]{2,0,1:T(8,128)(2,1)S(1)} all-gather(bf16[8,192,32]{2,0,1:T(8,128)(2,1)} %copy.24), channel_id=1, replica_groups=mesh['replica'=8,'mp'=4] {'mp'}, dimensions={1}, use_global_device_ids=true | all-gather | bytes 491520 | tf_op jit(solution)/shard_map/all_gather | solution.py:47
  105.6 1.7 copy.25
  107.3 1.2 fusion.17
  108.5 0.1 constant_dynamic-slice_fusion
  108.6 115.2 %all-reduce.5.cloned.1.call-done = f32[8,3072,32]{1,2,0:T(8,128)} async-done(((f32[8,3072,32]{1,2,0:T(8,128)}), f32[8,3072,32]{1,2,0:T(8,128)}) %all-reduce.5.cloned.1.call-update) | async-done | bytes 3145744 | tf_op jit(solution)/shard_map/psum | solution.py:46
  223.8 5.3 %fusion.3 = f32[2,3072,32]{1,0,2:T(2,128)S(1)} fusion(f32[8,3072,32]{1,2,0:T(8,128)} %all-reduce.5.cloned.1.call-done, pred[8,8]{1,0:T(8,128)(4,1)S(1)} %get-tuple-element.29, s32[]{:T(128)S(6)} %select_n.6), kind=kOutput, calls=%fused_computation.7 | convolution fusion | flops 18874368 | bytes 3932676 | tf_op jit(solution)/shard_map/ck,knr->cnr/dot_general | solution.py:58
  229.1 2.2 convolution_add_fusion
  231.4 0.0 copy-start.1
  231.4 1.4 copy-done.1
  232.8 2.2 fusion.5
  235.0 0.0 all-gather.2.cloned.1.call-update
  235.0 24.2 %psum.23 = f32[2688]{0:T(1024)S(1)} all-reduce(f32[2688]{0:T(1024)S(1)} %reduce), channel_id=1, replica_groups=mesh['replica'=8,'mp'=4] {'replica'}, use_global_device_ids=true, to_apply=%region_3.0 | all-reduce | flops 2688 | bytes 21504 | tf_op jit(solution)/shard_map/psum | solution.py:67
  259.3 0.6 multiply_subtract_fusion
  259.9 16.8 %fusion.1 = bf16[1,8,192,3072]{3,2,1,0:T(8,128)(2,1)} fusion(bf16[8,192,32]{1,2,0:T(8,128)(2,1)S(1)} %convolution_convert_fusion.1, f32[8,3072,32]{1,2,0:T(8,128)} %all-reduce.5.cloned.1.call-done, bf16[1,8,192,3072]{3,2,1,0:T(8,128)(2,1)} %param.11, bf16[1,8,192,3072]{3,2,1,0:T(8,128)(2,1)} %param.10), kind=kOutput, calls=%fused_computation.3 | convolution fusion | flops 1844969472 | bytes 31555584 | tf_op jit(solution)/shard_map/kms,kns->kmn/dot_general | solution.py:48
  276.7 15.8 %all-gather.2.cloned.1.call-done = bf16[8,96,3072]{2,1,0:T(8,128)(2,1)} async-done(((bf16[2,96,3072]{2,1,0:T(8,128)(2,1)}), bf16[8,96,3072]{2,1,0:T(8,128)(2,1)}) %all-gather.2.cloned.1.call-update) | async-done | bytes 4718608 | tf_op jit(solution)/shard_map/all_gather | solution.py:63
  292.5 5.5 %convolution_convert_fusion = bf16[8,96,3072]{2,0,1:T(8,128)(2,1)S(1)} fusion(bf16[8,96,3072]{2,1,0:T(8,128)(2,1)} %all-gather.2.cloned.1.call-done, s32[8]{0:T(128)S(1)} %multiply_add_fusion.1), kind=kOutput, calls=%fused_computation.4 | convolution fusion | flops 40108224 | bytes 9437216 | tf_op jit(solution)/shard_map/sk,smn->kmn/dot_general | solution.py:64
  298.1 4.8 %copy.31 = bf16[8,96,3072]{2,1,0:T(8,128)(2,1)} copy(bf16[8,96,3072]{2,0,1:T(8,128)(2,1)S(1)} %convolution_convert_fusion) | data formatting | bytes 9437184
  (15 shorter events, 0.1 us)
Async XLA Ops:
  7.2 1.4 copy-start
  7.2 66.9 %copy-start.4 = (f32[8,32,32]{2,1,0:T(8,128)S(1)}, f32[8,32,32]{2,1,0:T(8,128)}, u32[]{:S(2)}) copy-start(f32[8,32,32]{2,1,0:T(8,128)} %param.13) | copy-start | bytes 98308
  7.2 66.9 %all-reduce.3.cloned.1.call-start = ((), (), s32[]{:S(2)}) async-start(), calls=%async_computation | async-start | bytes 524288 | tf_op jit(solution)/shard_map/psum | solution.py:39
  18.7 205.2 %all-reduce.5.cloned.1.call-start = ((), (), s32[]{:S(2)}) async-start(), calls=%async_computation.1 | async-start | bytes 6291456 | tf_op jit(solution)/shard_map/psum | solution.py:46
  75.5 10.9 %copy-start.8 = (s32[8]{0:T(128)S(1)}, s32[8]{0:T(128)}, u32[]{:S(2)}) copy-start(s32[8]{0:T(128)} %param.14) | copy-start | bytes 100
  86.3 206.2 %all-gather.2.cloned.1.call-start = ((), (), s32[]{:S(2)}) async-start(), calls=%async_computation.2 | async-start | bytes 5898240 | tf_op jit(solution)/shard_map/all_gather | solution.py:63
  223.8 5.3 %copy-start.2 = (f32[1,2,96,3072]{3,2,1,0:T(8,128)S(1)}, f32[1,2,96,3072]{3,2,1,0:T(8,128)}, u32[]{:S(2)}) copy-start(f32[1,2,96,3072]{3,2,1,0:T(8,128)} %param.15) | copy-start | bytes 7077892
  223.8 8.9 %copy-start.3 = (f32[1,2,96,3072]{3,2,1,0:T(8,128)S(1)}, f32[1,2,96,3072]{3,2,1,0:T(8,128)}, u32[]{:S(2)}) copy-start(f32[1,2,96,3072]{3,2,1,0:T(8,128)} %param.16) | copy-start | bytes 7077892
  231.4 1.4 copy-start.1
  232.8 2.2 copy-start.7
  232.8 26.5 %copy-start.5 = (f32[2688]{0:T(1024)S(1)}, f32[2688]{0:T(1024)}, u32[]{:S(2)}) copy-start(f32[2688]{0:T(1024)} %param.19) | copy-start | bytes 32260
  232.8 26.5 %copy-start.6 = (f32[2688]{0:T(1024)S(1)}, f32[2688]{0:T(1024)}, u32[]{:S(2)}) copy-start(f32[2688]{0:T(1024)} %param.18) | copy-start | bytes 32260
Sparse Core Ops, SparseCore 0:
  18.8 55.3 all-reduce.2
  86.5 137.3 all-reduce.4
  235.1 57.3 all-gather.1
where the time goes:
time: 310 us; the launch traced here: 309 us
  waiting for transfers between devices  187 us (60%)
  matrix products  53.3 us (17%)
  blocking collectives  42.3 us (14%)
  between operations  13.9 us (4%)
  local copies, waits for them, and re-layouts  10.3 us (3%)
    psum x1, waiting for transfers between devices, per_device(): right_new = lax.psum(right_terms, ('replica', 'mp'))  115 us
    psum x1, waiting for transfers between devices, per_device(): left_sum = lax.psum(left_terms, 'replica')  55.4 us
    psum x1, blocking collectives, per_device(): vector_total = lax.psum(vector_grads[0], 'replica')  24.2 us
    all_gather x1, blocking collectives, per_device(): left_all = lax.all_gather(left_rows, 'mp', axis=1, tiled=True)  18.1 us
    dot_general x1, matrix products, per_device(): jnp.einsum('kms,kns->kmn', left_rows.astype(jnp.float32), right_new, prec...  16.8 us
    all_gather x1, waiting for transfers between devices, per_device(): weight_slots = lax.all_gather(master_narrow, 'mp', axis=0, tiled=True)  15.8 us
    dot_general x1, matrix products, per_device(): jnp.einsum('kmn,kms->kns', compensated, left_rows, preferred_element_type...  10.8 us
    dot_general x1, matrix products, per_device(): jnp.einsum('kmn,knr->kmr', compensated, right_init, preferred_element_typ...  10 us
  transfers between devices with their start and end apart: 3, of which 3 were waited for; matrix products, arithmetic and copies ran while one was open for 7% of the time, Pallas kernels for 0%

commit v1 on v0

v1 whole, which is shorter than its diff:
```python
import functools

import jax
import jax.numpy as jnp
from jax import lax
from jax.experimental import pallas as pl
from jax.experimental.pallas import tpu as pltpu
from jax.sharding import PartitionSpec as P

CORES = 2
LANES = 128
VMEM_LIMIT = 48 * 1024 * 1024
F32 = jnp.float32
BF16 = jnp.bfloat16


def params():
    return pltpu.CompilerParams(vmem_limit_bytes=VMEM_LIMIT)


def tree_sum(terms):
    while len(terms) > 1:
        terms = [terms[i] + terms[i + 1] for i in range(0, len(terms), 2)]
    return terms[0]


def exchange(x, axis, distance):
    size = lax.axis_size(axis)
    return lax.ppermute(x, axis, [(i, i ^ distance) for i in range(size)])


def left_kernel(g_ref, f_ref, q_ref, vec_ref, comp_ref, left_ref):
    k = pl.program_id(0)
    rows = g_ref.shape[2]
    rank = q_ref.shape[1]
    group = LANES // rank

    @pl.when(k == 0)
    def _():
        left_ref[:rows, :] = jnp.zeros((rows, left_ref.shape[1]), F32)
        left_ref[rows:, :] = vec_ref[...]

    comp = (g_ref[0, 0].astype(F32) + f_ref[0, 0].astype(F32)).astype(BF16)
    comp_ref[0] = comp
    q = q_ref[0]
    wide = jnp.concatenate([q] * group, axis=0)
    member = lax.broadcasted_iota(jnp.int32, wide.shape, 0) // rank
    wide = jnp.where(member == k % group, wide, jnp.zeros_like(wide))
    terms = lax.dot_general(comp, wide, (((1,), (1,)), ((), ())), preferred_element_type=F32)
    cols = pl.ds(pl.multiple_of((k // group) * LANES, LANES), LANES)
    left_ref[:rows, cols] += terms


def left_terms(gradients, feedback, right_t, vec):
    _, nmat, rows, n = gradients.shape
    rank = right_t.shape[1]
    total = rows + vec.shape[0]
    return pl.pallas_call(
        left_kernel,
        grid=(nmat,),
        in_specs=[
            pl.BlockSpec((1, 1, rows, n), lambda k: (0, k, 0, 0)),
            pl.BlockSpec((1, 1, rows, n), lambda k: (0, k, 0, 0)),
            pl.BlockSpec((1, rank, n), lambda k: (k, 0, 0)),
            pl.BlockSpec(vec.shape, lambda k: (0, 0)),
        ],
        out_specs=[
            pl.BlockSpec((1, rows, n), lambda k: (k, 0, 0)),
            pl.BlockSpec((total, nmat * rank), lambda k: (0, 0)),
        ],
        out_shape=[
            jax.ShapeDtypeStruct((nmat, rows, n), BF16),
            jax.ShapeDtypeStruct((total, nmat * rank), F32),
        ],
        compiler_params=params(),
        cost_estimate=pl.CostEstimate(
            flops=2 * nmat * rows * n * LANES, bytes_accessed=6 * nmat * rows * n, transcendentals=0
        ),
        name="left_terms",
    )(gradients, feedback, right_t, vec)


def right_kernel(half, pos, mine_ref, other_ref, gram_ref, comp_ref, send_ref, keep_ref, lt_ref, left):
    t = pl.program_id(0)
    rows = comp_ref.shape[1]
    part = mine_ref.shape[0]
    upm, unit = send_ref.shape[1], send_ref.shape[2]
    rank = upm * unit

    @pl.when(t == 0)
    def _():
        left[pl.ds(pl.multiple_of(pos[2] * part, 8), part), :] = mine_ref[...]
        left[pl.ds(pl.multiple_of((1 - pos[2]) * part, 8), part), :] = other_ref[...]
        hat = jnp.dot(
            left[:rows, :], gram_ref[...], precision=lax.Precision.HIGHEST, preferred_element_type=F32
        )
        lt_ref[...] = hat.T.astype(BF16)

    k = lax.rem(t + half, 2 * half) ^ pos[0]
    lt = lt_ref[pl.ds(pl.multiple_of(k * rank, rank), rank), :]
    terms = jnp.dot(lt, comp_ref[0], preferred_element_type=F32)

    @pl.when(t < half)
    def _():
        for i in range(upm):
            send_ref[0, i ^ pos[1]] = terms[i * unit : (i + 1) * unit].astype(BF16)

    @pl.when(t >= half)
    def _():
        for i in range(upm):
            keep_ref[0, i ^ pos[1]] = terms[i * unit : (i + 1) * unit]


def right_terms(pos, mine, other, gram, comp, upm):
    nmat, rows, n = comp.shape
    rank = gram.shape[0] // nmat
    unit = rank // upm
    half = nmat // 2
    return pl.pallas_call(
        functools.partial(right_kernel, half),
        grid_spec=pltpu.PrefetchScalarGridSpec(
            num_scalar_prefetch=1,
            grid=(nmat,),
            in_specs=[
                pl.BlockSpec(mine.shape, lambda t, pos: (0, 0)),
                pl.BlockSpec(other.shape, lambda t, pos: (0, 0)),
                pl.BlockSpec(gram.shape, lambda t, pos: (0, 0)),
                pl.BlockSpec((1, rows, n), lambda t, pos: (lax.rem(t + half, nmat) ^ pos[0], 0, 0)),
            ],
            out_specs=[
                pl.BlockSpec((1, upm, unit, n), lambda t, pos: (jnp.minimum(t, half - 1), 0, 0, 0)),
                pl.BlockSpec((1, upm, unit, n), lambda t, pos: (jnp.maximum(t - half, 0), 0, 0, 0)),
                pl.BlockSpec((nmat * rank, rows), lambda t, pos: (0, 0)),
            ],
            scratch_shapes=[pltpu.VMEM((2 * mine.shape[0], mine.shape[1]), F32)],
        ),
        out_shape=[
            jax.ShapeDtypeStruct((half, upm, unit, n), BF16),
            jax.ShapeDtypeStruct((half, upm, unit, n), F32),
            jax.ShapeDtypeStruct((nmat * rank, rows), BF16),
        ],
        compiler_params=params(),
        cost_estimate=pl.CostEstimate(
            flops=2 * nmat * rows * n * LANES, bytes_accessed=2 * nmat * rows * n, transcendentals=0
        ),
        name="right_terms",
    )(pos, mine, other, gram, comp)


def matrix_of(right_ref, sub):
    upm = right_ref.shape[1]
    parts = [right_ref[0, i ^ sub] for i in range(upm)]
    return parts[0] if upm == 1 else jnp.concatenate(parts, axis=0)


def product(lt, right):
    return lax.dot_general(lt, right, (((0,), (0,)), ((), ())), preferred_element_type=F32)


def outputs_kernel(pos, comp_ref, right_ref, lt_ref, ltr_ref, base_ref, *refs):
    feedback_ref, weights_ref = refs[-2:]
    right = matrix_of(right_ref, pos[1])
    feedback_ref[0, 0] = (comp_ref[0].astype(F32) - product(lt_ref[...], right)).astype(BF16)
    weights_ref[0] = (base_ref[0].astype(F32) - 0.1 * product(ltr_ref[...], right)).astype(BF16)


def outputs(pos, start, comp, right, lt, ltr, base, earlier):
    nmat, rows, n = comp.shape
    rank = lt.shape[0] // nmat
    half, upm, unit, _ = right.shape
    replica_rows = base.shape[1]

    def matrix(j, pos):
        return (j + start) ^ pos[0]

    any_spec = pl.BlockSpec(memory_space=pl.ANY)
    return pl.pallas_call(
        outputs_kernel,
        grid_spec=pltpu.PrefetchScalarGridSpec(
            num_scalar_prefetch=1,
            grid=(half,),
            in_specs=[
                pl.BlockSpec((1, rows, n), lambda j, pos: (matrix(j, pos), 0, 0)),
                pl.BlockSpec((1, upm, unit, n), lambda j, pos: (j, 0, 0, 0)),
                pl.BlockSpec((rank, rows), lambda j, pos: (matrix(j, pos), 0)),
                pl.BlockSpec((rank, replica_rows), lambda j, pos: (matrix(j, pos), 0)),
                pl.BlockSpec((1, replica_rows, n), lambda j, pos: (pos[3 + matrix(j, pos)], 0, 0)),
            ]
            + [any_spec] * len(earlier),
            out_specs=[
                pl.BlockSpec((1, 1, rows, n), lambda j, pos: (0, matrix(j, pos), 0, 0)),
                pl.BlockSpec((1, replica_rows, n), lambda j, pos: (matrix(j, pos), 0, 0)),
            ],
        ),
        out_shape=[
            jax.ShapeDtypeStruct((1, nmat, rows, n), BF16),
            jax.ShapeDtypeStruct((nmat, replica_rows, n), BF16),
        ],
        input_output_aliases={6 + i: i for i in range(len(earlier))},
        compiler_params=params(),
        cost_estimate=pl.CostEstimate(
            flops=2 * half * (rows + replica_rows) * n * LANES,
            bytes_accessed=4 * half * (rows + replica_rows) * n,
            transcendentals=0,
        ),
        name="outputs",
    )(pos, comp, right, lt, ltr, base, *earlier)


def owned_kernel(half, held, pos, momentum_ref, master_ref, near_ref, far_ref, ltr_ref, new_momentum_ref, new_master_ref):
    c = pl.program_id(0)
    matrix = pos[held + c]
    near = matrix_of(near_ref, pos[1])
    far = matrix_of(far_ref, pos[1])
    slot = jnp.maximum(matrix, 0) ^ pos[0]
    right = jnp.where(slot < half, near, far)
    approx = jnp.where(matrix >= 0, product(ltr_ref[...], right), 0.0)
    momentum = 0.9 * momentum_ref[0, 0] + approx
    new_momentum_ref[0, 0] = momentum
    new_master_ref[0, 0] = master_ref[0, 0] - 0.1 * momentum


def owned(pos, held, momentum, master, near, far, ltr):
    _, capacity, rows, n = momentum.shape
    half, upm, unit, _ = near.shape
    rank = upm * unit

    def matrix(c, pos):
        return jnp.maximum(pos[held + c], 0)

    state = pl.BlockSpec((1, 1, rows, n), lambda c, pos: (0, c, 0, 0))
    right = pl.BlockSpec((1, upm, unit, n), lambda c, pos: (lax.rem(matrix(c, pos) ^ pos[0], half), 0, 0, 0))
    return pl.pallas_call(
        functools.partial(owned_kernel, half, held),
        grid_spec=pltpu.PrefetchScalarGridSpec(
            num_scalar_prefetch=1,
            grid=(capacity,),
            in_specs=[
                state,
                state,
                right,
                right,
                pl.BlockSpec((rank, rows), lambda c, pos: (matrix(c, pos), 0)),
            ],
            out_specs=[state, state],
        ),
        out_shape=[jax.ShapeDtypeStruct(momentum.shape, F32)] * 2,
        compiler_params=params(),
        cost_estimate=pl.CostEstimate(
            flops=2 * capacity * rows * n * LANES, bytes_accessed=16 * capacity * rows * n, transcendentals=0
        ),
        name="owned",
    )(pos, momentum, master, near, far, ltr)


def per_device(
    gradients,
    feedback,
    right_init,
    gram_root,
    owners,
    momentum,
    master_weights,
    vector_grads,
    vector_momentum,
    vector_params,
):
    nmat, rows, n = gradients.shape[1:]
    rank = right_init.shape[2]
    n_mp = lax.axis_size("mp")
    n_z = lax.axis_size("replica") // CORES
    capacity, replica_rows = momentum.shape[1:3]
    p = lax.axis_index("mp")
    r = lax.axis_index("replica")
    core, z = r % CORES, r // CORES
    upm = CORES * n_mp // nmat
    half = nmat // CORES
    code = core * n_mp + p

    base = (master_weights[0] - 0.09 * momentum[0]).astype(BF16)
    base_all = jnp.concatenate([base] + [exchange(base, "mp", d) for d in range(1, n_mp)], axis=0)

    same_owner = owners[:, None] == owners[None, :]
    earlier = jnp.arange(nmat)[:, None] < jnp.arange(nmat)[None, :]
    ranks = jnp.sum((same_owner & earlier).astype(jnp.int32), axis=0)
    relative = (owners ^ p) * capacity + ranks
    mine = relative[None, :] == jnp.arange(capacity)[:, None]
    held = jnp.max(jnp.where(mine, jnp.arange(nmat)[None, :], -1), axis=1)
    pos = jnp.concatenate([jnp.stack([code // upm, code % upm, core]), relative, held]).astype(jnp.int32)

    nvec = vector_grads.shape[1]
    width = nmat * rank
    vec = jnp.pad(vector_grads[0], (0, 16 * width - nvec)).reshape(16, width)
    comp, terms = left_terms(gradients, feedback, jnp.swapaxes(right_init, 1, 2), vec)
    chip = terms + exchange(terms, "replica", 1)
    part = terms.shape[0] // CORES
    piece = lax.dynamic_slice_in_dim(chip, core * part, part, 0)
    piece = tree_sum([piece] + [exchange(piece, "replica", CORES * d) for d in range(1, n_z)])
    other = exchange(piece, "replica", 1)
    vector_half = jnp.where(core == 1, piece, other)
    vector_total = vector_half[part - 16 :].reshape(-1)[:nvec]

    block = jnp.eye(nmat, dtype=bool)[:, None, :, None]
    gram = jnp.where(block, gram_root[:, :, None, :], 0.0).reshape(width, width)
    send, keep, lt = right_terms(pos, piece, other, gram, comp, upm)
    chip = keep + exchange(send, "replica", 1).astype(F32)
    chip = chip.reshape(n_mp, rank // upm, n)
    narrow = chip.astype(BF16)
    plane = tree_sum([chip[0]] + [exchange(narrow[d], "mp", d).astype(F32) for d in range(1, n_mp)])
    cols = n // n_z
    plane_narrow = plane.astype(BF16)
    final = [lax.dynamic_slice_in_dim(plane, z * cols, cols, 1)]
    for d in range(1, n_z):
        sent = lax.dynamic_slice_in_dim(plane_narrow, (z ^ d) * cols, cols, 1)
        final.append(exchange(sent, "replica", CORES * d).astype(F32))
    final = tree_sum(final).astype(BF16)

    whole = jnp.zeros((rank // upm, n), BF16)
    whole = lax.dynamic_update_slice_in_dim(whole, final, z * cols, 1)
    for d in range(1, n_z):
        whole = lax.dynamic_update_slice_in_dim(
            whole, exchange(final, "replica", CORES * d), (z ^ d) * cols, 1
        )
    near = jnp.stack([whole] + [exchange(whole, "mp", d) for d in range(1, n_mp)])
    near = near.reshape(half, upm, rank // upm, n)
    far = exchange(near, "replica", 1)

    first = r * replica_rows
    strip = lax.dynamic_slice_in_dim(lt, first % rows, replica_rows, 1)
    strips = jnp.stack([strip] + [exchange(strip, "mp", d) for d in range(1, n_mp)])
    ltr = lax.dynamic_index_in_dim(strips, (first // rows) ^ p, 0, keepdims=False)

    done = outputs(pos, 0, comp, near, lt, ltr, base_all, ())
    new_feedback, new_weights = outputs(pos, half, comp, far, lt, ltr, base_all, done)
    new_momentum, new_master = owned(pos, 3 + nmat, momentum, master_weights, near, far, ltr)

    new_vector_momentum = 0.9 * vector_momentum + vector_total
    new_vector_params = vector_params - 0.1 * new_vector_momentum
    return new_feedback, new_momentum, new_master, new_weights, new_vector_momentum, new_vector_params


def solution(mesh):
    return jax.shard_map(
        per_device,
        mesh=mesh,
        in_specs=(
            P("replica", None, "mp", None),
            P("replica", None, "mp", None),
            P(),
            P(),
            P(),
            P("mp", None, "replica", None),
            P("mp", None, "replica", None),
            P("replica", "mp"),
            P("mp"),
            P("mp"),
        ),
        out_specs=(
            P("replica", None, "mp", None),
            P("mp", None, "replica", None),
            P("mp", None, "replica", None),
            P(None, "replica", None),
            P("mp"),
            P("mp"),
        ),
        check_vma=False,
    )
```

time: 310 us -> 171 us (0.55)
  waiting for transfers between devices: 187 us -> 86.8 us
  matrix products: 53.3 us -> 0 us
  blocking collectives: 42.3 us -> 0 us
  Pallas kernels: 0 us -> 39.5 us
  starting transfers between devices: 0.12 us -> 27 us
  between operations: 13.9 us -> 0.82 us
  other arithmetic: 2.93 us -> 11 us
  local copies, waits for them, and re-layouts: 10.3 us -> 2.8 us
    psum x2 -> x0, waiting for transfers between devices: 171 us -> none  [the longest x1 115 us: per_device(): right_new = lax.psum(right_terms, ('replica', 'mp'))]
    ppermute x0 -> x25, waiting for transfers between devices: none -> 86.8 us  [exchange(): return lax.ppermute(x, axis, [(i, i ^ distance) for i in range(size)])]
    dot_general x8 -> x0, matrix products: 53.3 us -> none  [the longest x1 16.8 us: per_device(): jnp.einsum('kms,kns->kmn', left_rows.astype(jnp.float32), right_new, prec...]
    pallas_call x0 -> x5, Pallas kernels: none -> 39.5 us  [the longest x2 14.1 us: outputs(): pl.pallas_call(outputs_kernel, grid_spec=pltpu.PrefetchScalarGridSpec(num...]
    ppermute x0 -> x25, starting transfers between devices: none -> 27 us  [exchange(): return lax.ppermute(x, axis, [(i, i ^ distance) for i in range(size)])]
    psum x1 -> x0, blocking collectives: 24.2 us -> none  [per_device(): vector_total = lax.psum(vector_grads[0], 'replica')]
    all_gather x1 -> x0, blocking collectives: 18.1 us -> none  [per_device(): left_all = lax.all_gather(left_rows, 'mp', axis=1, tiled=True)]
    all_gather x1 -> x0, waiting for transfers between devices: 15.8 us -> none  [per_device(): weight_slots = lax.all_gather(master_narrow, 'mp', axis=0, tiled=True)]
  transfers between devices with their start and end apart: 3 -> 25, of which waited for: 3 -> 14; matrix products, arithmetic and copies ran while one was open for 7% -> 5% of each run, Pallas kernels for 0% -> 4%
where the time goes in v1:
time: 171 us; the launch traced here: 168 us
  waiting for transfers between devices  86.8 us (51%)
  Pallas kernels  39.5 us (23%)
  starting transfers between devices  27 us (16%)
  other arithmetic  11 us (6%)
  local copies, waits for them, and re-layouts  2.8 us (2%)
    ppermute x25, waiting for transfers between devices, exchange(): return lax.ppermute(x, axis, [(i, i ^ distance) for i in range(size)])  86.8 us
    ppermute x25, starting transfers between devices, exchange(): return lax.ppermute(x, axis, [(i, i ^ distance) for i in range(size)])  27 us
    pallas_call x2, Pallas kernels, outputs(): pl.pallas_call(outputs_kernel, grid_spec=pltpu.PrefetchScalarGridSpec(num...  14.1 us
    pallas_call x1, Pallas kernels, left_terms(): pl.pallas_call(left_kernel, grid=(nmat,), in_specs=[pl.BlockSpec((1, 1, r...  12.8 us
    pallas_call x1, Pallas kernels, right_terms(): pl.pallas_call(functools.partial(right_kernel, half), grid_spec=pltpu.Pre...  8.19 us
    pallas_call x1, Pallas kernels, owned(): pl.pallas_call(functools.partial(owned_kernel, half, held), grid_spec=plt...  4.45 us
  transfers between devices with their start and end apart: 25, of which 14 were waited for; matrix products, arithmetic and copies ran while one was open for 5% of the time, Pallas kernels for 4%

profile of v1, /device:TPU:1, one launch (start us, length us, event | category | flops | bytes accessed | tf_op | source)
XLA Modules:
  0.0 167.8 jit_solution(12955850285606136612)
XLA Ops:
  1.4 1.4 copy-done.1
  2.8 12.8 %left_terms.1 = (bf16[8,192,3072]{2,1,0:T(8,128)(2,1)}, f32[208,256]{1,0:T(8,128)S(1)}) custom-call(bf16[1,8,192,3072]{3,2,1,0:T(8,128)(2,1)} %g_ref.1, bf16[1,8,192,3072]{3,2,1,0:T(8,128)(2,1)} %f_ref.1, bf16[8,32,3072]{2,1,0:T(8,128)(2,1)S(1)} %bitcast.36, f32[16,256]{1,0:T(8,128)S(1)} %reshape.51.vec_ref), custom_call_target="tpu_custom_call" | custom-call | flops 1207959552 | bytes 28311552 | tf_op jit(solution)/shard_map/left_terms/pallas_call | solution.py:58
  15.9 1.2 collective-permute-done
  17.0 3.5 %collective-permute-start.2 = (f32[104,256]{1,0:T(8,128)S(1)}, f32[104,256]{1,0:T(8,128)S(1)}, u32[]{:S(2)}, u32[]{:S(2)}) collective-permute-start(f32[104,256]{1,0:T(8,128)S(1)} %dynamic-slice_add_fusion), channel_id=1, source_target_pairs={{0,16},{4,20},{8,24},{12,28},{16,0},{20,4},{24,8},{28,12},{1,17},{... | collective-permute-start | bytes 319496 | tf_op jit(solution)/shard_map/ppermute | solution.py:29
  22.2 5.8 %collective-permute-done.2 = f32[104,256]{1,0:T(8,128)S(1)} collective-permute-done((f32[104,256]{1,0:T(8,128)S(1)}, f32[104,256]{1,0:T(8,128)S(1)}, u32[]{:S(2)}, u32[]{:S(2)}) %collective-permute-start.2) | collective-permute-done | bytes 106528 | tf_op jit(solution)/shard_map/ppermute | solution.py:29
  28.8 1.7 %collective-permute-start.4 = (f32[104,256]{1,0:T(8,128)S(1)}, f32[104,256]{1,0:T(8,128)S(1)}, u32[]{:S(2)}, u32[]{:S(2)}) collective-permute-start(f32[104,256]{1,0:T(8,128)S(1)} %add_add_fusion.mine_ref), channel_id=1, source_target_pairs={{0,4},{4,0},{8,12},{12,8},{16,20},{20,16},{24,28},{28,24},{1,5},{5... | collective-permute-start | bytes 319496 | tf_op jit(solution)/shard_map/ppermute | solution.py:29
  31.5 8.2 %right_terms.1 = (bf16[4,1,32,3072]{3,2,1,0:T(8,128)(2,1)S(1)}, f32[4,1,32,3072]{3,2,1,0:T(8,128)S(1)}, bf16[256,192]{1,0:T(8,128)(2,1)S(1)}) custom-call(s32[13]{0:T(128)S(1)} %concatenate.6.pos, f32[104,256]{1,0:T(8,128)S(1)} %add_add_fusion.mine_ref, f32[104,256]{1,0:T(8,128)S(1)} %collective-permute-done.4.other_ref, f32[256,256]{1,0:T(8,128)S(1)} %select_n.71.gram_ref, ...), custom_call_target="tpu_custom_call" | custom-call | flops 1207959552 | bytes 9437184 | tf_op jit(solution)/shard_map/right_terms/pallas_call | solution.py:119
  40.1 1.9 %collective-permute-done.5 = bf16[4,1,32,3072]{3,2,1,0:T(8,128)(2,1)S(1)} collective-permute-done((bf16[4,1,32,3072]{3,2,1,0:T(8,128)(2,1)S(1)}, bf16[4,1,32,3072]{3,2,1,0:T(8,128)(2,1)S(1)}, u32[]{:S(2)}, u32[]{:S(2)}) %collective-permute-start.5) | collective-permute-done | bytes 786464 | tf_op jit(solution)/shard_map/ppermute | solution.py:29
  42.0 1.4 fusion.12
  44.1 2.2 %collective-permute-start.8 = (bf16[32,3072]{1,0:T(8,128)(2,1)}, bf16[32,3072]{1,0:T(8,128)(2,1)S(1)}, u32[]{:S(2)}, u32[]{:S(2)}) collective-permute-start(bf16[32,3072]{1,0:T(8,128)(2,1)} %get-tuple-element.37), channel_id=1, source_target_pairs={{0,3},{1,2},{2,1},{3,0},{4,7},{5,6},{6,5},{7,4},{8,11},{9,10},{10,... | collective-permute-start | bytes 589832 | tf_op jit(solution)/shard_map/ppermute | solution.py:29
  46.8 4.6 %collective-permute-done.8 = bf16[32,3072]{1,0:T(8,128)(2,1)S(1)} collective-permute-done((bf16[32,3072]{1,0:T(8,128)(2,1)}, bf16[32,3072]{1,0:T(8,128)(2,1)S(1)}, u32[]{:S(2)}, u32[]{:S(2)}) %collective-permute-start.8) | collective-permute-done | bytes 196640 | tf_op jit(solution)/shard_map/ppermute | solution.py:29
  51.4 5.0 %collective-permute-done.7 = bf16[32,3072]{1,0:T(8,128)(2,1)S(1)} collective-permute-done((bf16[32,3072]{1,0:T(8,128)(2,1)S(1)}, bf16[32,3072]{1,0:T(8,128)(2,1)S(1)}, u32[]{:S(2)}, u32[]{:S(2)}) %collective-permute-start.7) | collective-permute-done | bytes 196640 | tf_op jit(solution)/shard_map/ppermute | solution.py:29
  56.4 1.2 fusion.10
  57.6 3.3 %collective-permute-start.11 = (bf16[32,768]{1,0:T(8,128)(2,1)S(1)}, bf16[32,768]{1,0:T(8,128)(2,1)S(1)}, u32[]{:S(2)}, u32[]{:S(2)}) collective-permute-start(bf16[32,768]{1,0:T(8,128)(2,1)S(1)} %get-tuple-element.40), channel_id=1, source_target_pairs={{0,24},{4,28},{8,16},{12,20},{16,8},{20,12},{24,0},{28,4},{1,25},{... | collective-permute-start | bytes 147464 | tf_op jit(solution)/shard_map/ppermute | solution.py:29
  61.3 1.2 collective-permute-done.11
  62.5 2.9 %collective-permute-done.10 = bf16[32,768]{1,0:T(8,128)(2,1)S(1)} collective-permute-done((bf16[32,768]{1,0:T(8,128)(2,1)S(1)}, bf16[32,768]{1,0:T(8,128)(2,1)S(1)}, u32[]{:S(2)}, u32[]{:S(2)}) %collective-permute-start.10) | collective-permute-done | bytes 49184 | tf_op jit(solution)/shard_map/ppermute | solution.py:29
  65.7 1.9 %collective-permute-start.13 = (bf16[32,768]{1,0:T(8,128)(2,1)S(1)}, bf16[32,768]{1,0:T(8,128)(2,1)S(1)}, u32[]{:S(2)}, u32[]{:S(2)}) collective-permute-start(bf16[32,768]{1,0:T(8,128)(2,1)S(1)} %get-tuple-element.31), channel_id=1, source_target_pairs={{0,16},{4,20},{8,24},{12,28},{16,0},{20,4},{24,8},{28,12},{1,17},{... | collective-permute-start | bytes 147464 | tf_op jit(solution)/shard_map/ppermute | solution.py:29
  67.6 1.5 collective-permute-start.14
  69.5 2.9 %collective-permute-done.14 = bf16[32,768]{1,0:T(8,128)(2,1)S(1)} collective-permute-done((bf16[32,768]{1,0:T(8,128)(2,1)S(1)}, bf16[32,768]{1,0:T(8,128)(2,1)S(1)}, u32[]{:S(2)}, u32[]{:S(2)}) %collective-permute-start.14) | collective-permute-done | bytes 49184 | tf_op jit(solution)/shard_map/ppermute | solution.py:29
  72.5 3.2 %fusion = bf16[2,96,3072]{2,1,0:T(8,128)(2,1)} fusion(f32[1,2,96,3072]{3,2,1,0:T(8,128)} %master_ref.1, f32[1,2,96,3072]{3,2,1,0:T(8,128)S(1)} %copy-done), kind=kLoop, calls=%fused_computation.3 | loop fusion | flops 1769472 | bytes 5898240 | tf_op jit(solution)/shard_map/convert_element_type | solution.py:280
  75.7 2.3 %collective-permute-start.24 = (bf16[2,96,3072]{2,1,0:T(8,128)(2,1)}, bf16[2,96,3072]{2,1,0:T(8,128)(2,1)}, u32[]{:S(2)}, u32[]{:S(2)}) collective-permute-start(bf16[2,96,3072]{2,1,0:T(8,128)(2,1)} %fusion), channel_id=1, source_target_pairs={{0,3},{1,2},{2,1},{3,0},{4,7},{5,6},{6,5},{7,4},{8,11},{9,10},{10,... | collective-permute-start | bytes 3538952 | tf_op jit(solution)/shard_map/ppermute | solution.py:29
  78.1 1.2 collective-permute-start.23
  79.3 1.4 collective-permute-start.16
  81.1 55.2 %collective-permute-done.16 = bf16[32,3072]{1,0:T(8,128)(2,1)S(1)} collective-permute-done((bf16[32,3072]{1,0:T(8,128)(2,1)S(1)}, bf16[32,3072]{1,0:T(8,128)(2,1)S(1)}, u32[]{:S(2)}, u32[]{:S(2)}) %collective-permute-start.16) | collective-permute-done | bytes 196640 | tf_op jit(solution)/shard_map/ppermute | solution.py:29
  136.3 1.9 %collective-permute-start.19 = (bf16[256,96]{1,0:T(8,128)(2,1)S(1)}, bf16[256,96]{1,0:T(8,128)(2,1)S(1)}, u32[]{:S(2)}, u32[]{:S(2)}) collective-permute-start(bf16[256,96]{1,0:T(8,128)(2,1)S(1)} %constant_dynamic-slice_fusion), channel_id=1, source_target_pairs={{0,1},{1,0},{2,3},{3,2},{4,5},{5,4},{6,7},{7,6},{8,9},{9,8},{10,11... | collective-permute-start | bytes 147464 | tf_op jit(solution)/shard_map/ppermute | solution.py:29
  138.5 1.8 %collective-permute-done.19 = bf16[256,96]{1,0:T(8,128)(2,1)S(1)} collective-permute-done((bf16[256,96]{1,0:T(8,128)(2,1)S(1)}, bf16[256,96]{1,0:T(8,128)(2,1)S(1)}, u32[]{:S(2)}, u32[]{:S(2)}) %collective-permute-start.19) | collective-permute-done | bytes 49184 | tf_op jit(solution)/shard_map/ppermute | solution.py:29
  141.9 1.6 collective-permute-start.21
  143.6 2.3 %collective-permute-done.21 = bf16[256,96]{1,0:T(8,128)(2,1)S(1)} collective-permute-done((bf16[256,96]{1,0:T(8,128)(2,1)S(1)}, bf16[256,96]{1,0:T(8,128)(2,1)S(1)}, u32[]{:S(2)}, u32[]{:S(2)}) %collective-permute-start.21) | collective-permute-done | bytes 49184 | tf_op jit(solution)/shard_map/ppermute | solution.py:29
  146.0 3.2 %pad_maximum_fusion.base_ref = bf16[8,96,3072]{2,1,0:T(8,128)(2,1)S(1)} fusion(bf16[2,96,3072]{2,1,0:T(8,128)(2,1)} %collective-permute-done.24, bf16[2,96,3072]{2,1,0:T(8,128)(2,1)} %collective-permute-done.23, bf16[2,96,3072]{2,1,0:T(8,128)(2,1)} %collective-permute-done.22, bf16[2,96,3072]{2,1,0:T(8,128)(2,1)} %fusion), kind=kLoop, calls=%fused_computation | loop fusion | flops 7077888 | bytes 9437184 | tf_op jit(solution)/shard_map/concatenate | solution.py:281
  149.2 7.1 %outputs.2 = (bf16[1,8,192,3072]{3,2,1,0:T(8,128)(2,1)}, bf16[8,96,3072]{2,1,0:T(8,128)(2,1)}) custom-call(s32[13]{0:T(128)S(1)} %concatenate.6.pos, bf16[8,192,3072]{2,1,0:T(8,128)(2,1)} %get-tuple-element.17.comp_ref, bf16[4,1,32,3072]{3,2,1,0:T(8,128)(2,1)S(1)} %maximum_bitcast_fusion.right_ref.near_ref, bf16[256,192]{1,0:T(8,128)(2,1)S(1)} %get-tuple-element.21.lt_ref, ...), custom_call_target="tpu_custom_call" | custom-call | flops 905969664 | bytes 14155776 | tf_op jit(solution)/shard_map/outputs/pallas_call | solution.py:177
  156.3 4.5 %owned.1 = (f32[1,2,96,3072]{3,2,1,0:T(8,128)}, f32[1,2,96,3072]{3,2,1,0:T(8,128)}) custom-call(s32[13]{0:T(128)S(1)} %concatenate.6.pos, f32[1,2,96,3072]{3,2,1,0:T(8,128)S(1)} %copy-done, f32[1,2,96,3072]{3,2,1,0:T(8,128)} %master_ref.1, bf16[4,1,32,3072]{3,2,1,0:T(8,128)(2,1)S(1)} %maximum_bitcast_fusion.right_ref.near_ref, ...), custom_call_target="tpu_custom_call" | custom-call | flops 150994944 | bytes 9437184 | tf_op jit(solution)/shard_map/owned/pallas_call | solution.py:233
  160.7 7.0 %outputs.3 = (bf16[1,8,192,3072]{3,2,1,0:T(8,128)(2,1)}, bf16[8,96,3072]{2,1,0:T(8,128)(2,1)}) custom-call(s32[13]{0:T(128)S(1)} %concatenate.6.pos, bf16[8,192,3072]{2,1,0:T(8,128)(2,1)} %get-tuple-element.17.comp_ref, bf16[4,1,32,3072]{3,2,1,0:T(8,128)(2,1)S(1)} %collective-permute-done.18.right_ref.far_ref, ...), custom_call_target="tpu_custom_call", output_to_operand_aliasing={{0}: (6, {}), {1}: (7, {})} | custom-call | flops 905969664 | bytes 14155776 | tf_op jit(solution)/shard_map/outputs/pallas_call | solution.py:177
  (65 shorter events, 9.7 us)
Async XLA Ops:
  1.4 1.4 copy-start.1
  2.8 12.8 %copy-start.5 = (s32[8]{0:T(128)S(1)}, s32[8]{0:T(128)}, u32[]{:S(2)}) copy-start(s32[8]{0:T(128)} %param.14) | copy-start | bytes 100
  2.8 12.9 %copy-start.2 = (f32[8,32,32]{2,1,0:T(8,128)S(1)}, f32[8,32,32]{2,1,0:T(8,128)}, u32[]{:S(2)}) copy-start(f32[8,32,32]{2,1,0:T(8,128)} %param.13) | copy-start | bytes 98308
  15.6 1.5 collective-permute-start
  17.0 10.9 %collective-permute-start.2 = (f32[104,256]{1,0:T(8,128)S(1)}, f32[104,256]{1,0:T(8,128)S(1)}, u32[]{:S(2)}, u32[]{:S(2)}) collective-permute-start(f32[104,256]{1,0:T(8,128)S(1)} %dynamic-slice_add_fusion), channel_id=1, source_target_pairs={{0,16},{4,20},{8,24},{12,28},{16,0},{20,4},{24,8},{28,12},{1,17},{... | collective-permute-start | bytes 319496 | tf_op jit(solution)/shard_map/ppermute | solution.py:29
  20.6 7.4 %collective-permute-start.3 = (f32[104,256]{1,0:T(8,128)S(1)}, f32[104,256]{1,0:T(8,128)S(1)}, u32[]{:S(2)}, u32[]{:S(2)}) collective-permute-start(f32[104,256]{1,0:T(8,128)S(1)} %dynamic-slice_add_fusion), channel_id=1, source_target_pairs={{0,24},{4,28},{8,16},{12,20},{16,8},{20,12},{24,0},{28,4},{1,25},{... | collective-permute-start | bytes 319496 | tf_op jit(solution)/shard_map/ppermute | solution.py:29
  21.6 7.1 %collective-permute-start.1 = (f32[104,256]{1,0:T(8,128)S(1)}, f32[104,256]{1,0:T(8,128)S(1)}, u32[]{:S(2)}, u32[]{:S(2)}) collective-permute-start(f32[104,256]{1,0:T(8,128)S(1)} %dynamic-slice_add_fusion), channel_id=1, source_target_pairs={{0,8},{4,12},{8,0},{12,4},{16,24},{20,28},{24,16},{28,20},{1,9},{5... | collective-permute-start | bytes 319496 | tf_op jit(solution)/shard_map/ppermute | solution.py:29
  28.8 2.7 %collective-permute-start.4 = (f32[104,256]{1,0:T(8,128)S(1)}, f32[104,256]{1,0:T(8,128)S(1)}, u32[]{:S(2)}, u32[]{:S(2)}) collective-permute-start(f32[104,256]{1,0:T(8,128)S(1)} %add_add_fusion.mine_ref), channel_id=1, source_target_pairs={{0,4},{4,0},{8,12},{12,8},{16,20},{20,16},{24,28},{28,24},{1,5},{5... | collective-permute-start | bytes 319496 | tf_op jit(solution)/shard_map/ppermute | solution.py:29
  39.7 2.4 %collective-permute-start.5 = (bf16[4,1,32,3072]{3,2,1,0:T(8,128)(2,1)S(1)}, bf16[4,1,32,3072]{3,2,1,0:T(8,128)(2,1)S(1)}, u32[]{:S(2)}, u32[]{:S(2)}) collective-permute-start(bf16[4,1,32,3072]{3,2,1,0:T(8,128)(2,1)S(1)} %get-tuple-element.20), channel_id=1, source_target_pairs={{0,4},{4,0},{8,12},{12,8},{16,20},{20,16},{24,28},{28,24},{1,5},{5... | collective-permute-start | bytes 2359304 | tf_op jit(solution)/shard_map/ppermute | solution.py:29
  43.4 29.1 %copy-start = (f32[1,2,96,3072]{3,2,1,0:T(8,128)S(1)}, f32[1,2,96,3072]{3,2,1,0:T(8,128)}, u32[]{:S(2)}) copy-start(f32[1,2,96,3072]{3,2,1,0:T(8,128)} %momentum_ref.1) | copy-start | bytes 7077892
  44.1 7.3 %collective-permute-start.8 = (bf16[32,3072]{1,0:T(8,128)(2,1)}, bf16[32,3072]{1,0:T(8,128)(2,1)S(1)}, u32[]{:S(2)}, u32[]{:S(2)}) collective-permute-start(bf16[32,3072]{1,0:T(8,128)(2,1)} %get-tuple-element.37), channel_id=1, source_target_pairs={{0,3},{1,2},{2,1},{3,0},{4,7},{5,6},{6,5},{7,4},{8,11},{9,10},{10,... | collective-permute-start | bytes 589832 | tf_op jit(solution)/shard_map/ppermute | solution.py:29
  46.4 10.0 %collective-permute-start.7 = (bf16[32,3072]{1,0:T(8,128)(2,1)S(1)}, bf16[32,3072]{1,0:T(8,128)(2,1)S(1)}, u32[]{:S(2)}, u32[]{:S(2)}) collective-permute-start(bf16[32,3072]{1,0:T(8,128)(2,1)S(1)} %get-tuple-element.38), channel_id=1, source_target_pairs={{0,2},{1,3},{2,0},{3,1},{4,6},{5,7},{6,4},{7,5},{8,10},{9,11},{10,... | collective-permute-start | bytes 589832 | tf_op jit(solution)/shard_map/ppermute | solution.py:29
  46.6 9.8 %collective-permute-start.6 = (bf16[32,3072]{1,0:T(8,128)(2,1)S(1)}, bf16[32,3072]{1,0:T(8,128)(2,1)}, u32[]{:S(2)}, u32[]{:S(2)}) collective-permute-start(bf16[32,3072]{1,0:T(8,128)(2,1)S(1)} %get-tuple-element.36), channel_id=1, source_target_pairs={{0,1},{1,0},{2,3},{3,2},{4,5},{5,4},{6,7},{7,6},{8,9},{9,8},{10,11... | collective-permute-start | bytes 589832 | tf_op jit(solution)/shard_map/ppermute | solution.py:29
  57.6 4.9 %collective-permute-start.11 = (bf16[32,768]{1,0:T(8,128)(2,1)S(1)}, bf16[32,768]{1,0:T(8,128)(2,1)S(1)}, u32[]{:S(2)}, u32[]{:S(2)}) collective-permute-start(bf16[32,768]{1,0:T(8,128)(2,1)S(1)} %get-tuple-element.40), channel_id=1, source_target_pairs={{0,24},{4,28},{8,16},{12,20},{16,8},{20,12},{24,0},{28,4},{1,25},{... | collective-permute-start | bytes 147464 | tf_op jit(solution)/shard_map/ppermute | solution.py:29
  60.9 4.5 %collective-permute-start.10 = (bf16[32,768]{1,0:T(8,128)(2,1)S(1)}, bf16[32,768]{1,0:T(8,128)(2,1)S(1)}, u32[]{:S(2)}, u32[]{:S(2)}) collective-permute-start(bf16[32,768]{1,0:T(8,128)(2,1)S(1)} %get-tuple-element.41), channel_id=1, source_target_pairs={{0,16},{4,20},{8,24},{12,28},{16,0},{20,4},{24,8},{28,12},{1,17},{... | collective-permute-start | bytes 147464 | tf_op jit(solution)/shard_map/ppermute | solution.py:29
  61.1 4.3 %collective-permute-start.9 = (bf16[32,768]{1,0:T(8,128)(2,1)S(1)}, bf16[32,768]{1,0:T(8,128)(2,1)S(1)}, u32[]{:S(2)}, u32[]{:S(2)}) collective-permute-start(bf16[32,768]{1,0:T(8,128)(2,1)S(1)} %get-tuple-element.39), channel_id=1, source_target_pairs={{0,8},{4,12},{8,0},{12,4},{16,24},{20,28},{24,16},{28,20},{1,9},{5... | collective-permute-start | bytes 147464 | tf_op jit(solution)/shard_map/ppermute | solution.py:29
  65.5 3.6 %collective-permute-start.12 = (bf16[32,768]{1,0:T(8,128)(2,1)S(1)}, bf16[32,768]{1,0:T(8,128)(2,1)S(1)}, u32[]{:S(2)}, u32[]{:S(2)}) collective-permute-start(bf16[32,768]{1,0:T(8,128)(2,1)S(1)} %get-tuple-element.31), channel_id=1, source_target_pairs={{0,8},{4,12},{8,0},{12,4},{16,24},{20,28},{24,16},{28,20},{1,9},{5... | collective-permute-start | bytes 147464 | tf_op jit(solution)/shard_map/ppermute | solution.py:29
  65.7 3.8 %collective-permute-start.13 = (bf16[32,768]{1,0:T(8,128)(2,1)S(1)}, bf16[32,768]{1,0:T(8,128)(2,1)S(1)}, u32[]{:S(2)}, u32[]{:S(2)}) collective-permute-start(bf16[32,768]{1,0:T(8,128)(2,1)S(1)} %get-tuple-element.31), channel_id=1, source_target_pairs={{0,16},{4,20},{8,24},{12,28},{16,0},{20,4},{24,8},{28,12},{1,17},{... | collective-permute-start | bytes 147464 | tf_op jit(solution)/shard_map/ppermute | solution.py:29
  67.6 4.8 %collective-permute-start.14 = (bf16[32,768]{1,0:T(8,128)(2,1)S(1)}, bf16[32,768]{1,0:T(8,128)(2,1)S(1)}, u32[]{:S(2)}, u32[]{:S(2)}) collective-permute-start(bf16[32,768]{1,0:T(8,128)(2,1)S(1)} %get-tuple-element.31), channel_id=1, source_target_pairs={{0,24},{4,28},{8,16},{12,20},{16,8},{20,12},{24,0},{28,4},{1,25},{... | collective-permute-start | bytes 147464 | tf_op jit(solution)/shard_map/ppermute | solution.py:29
  72.4 68.9 %copy-start.3 = (f32[2688]{0:T(1024)S(1)}, f32[2688]{0:T(1024)}, u32[]{:S(2)}) copy-start(f32[2688]{0:T(1024)} %param.19) | copy-start | bytes 32260
  72.4 68.9 %copy-start.4 = (f32[2688]{0:T(1024)S(1)}, f32[2688]{0:T(1024)}, u32[]{:S(2)}) copy-start(f32[2688]{0:T(1024)} %param.18) | copy-start | bytes 32260
  72.4 8.3 %collective-permute-start.17 = (bf16[32,3072]{1,0:T(8,128)(2,1)S(1)}, bf16[32,3072]{1,0:T(8,128)(2,1)S(1)}, u32[]{:S(2)}, u32[]{:S(2)}) collective-permute-start(bf16[32,3072]{1,0:T(8,128)(2,1)S(1)} %constant_dynamic-update-slice_fusion), channel_id=1, source_target_pairs={{0,3},{1,2},{2,1},{3,0},{4,7},{5,6},{6,5},{7,4},{8,11},{9,10},{10,... | collective-permute-start | bytes 589832 | tf_op jit(solution)/shard_map/ppermute | solution.py:29
  75.7 70.3 %collective-permute-start.24 = (bf16[2,96,3072]{2,1,0:T(8,128)(2,1)}, bf16[2,96,3072]{2,1,0:T(8,128)(2,1)}, u32[]{:S(2)}, u32[]{:S(2)}) collective-permute-start(bf16[2,96,3072]{2,1,0:T(8,128)(2,1)} %fusion), channel_id=1, source_target_pairs={{0,3},{1,2},{2,1},{3,0},{4,7},{5,6},{6,5},{7,4},{8,11},{9,10},{10,... | collective-permute-start | bytes 3538952 | tf_op jit(solution)/shard_map/ppermute | solution.py:29
  78.1 67.9 %collective-permute-start.23 = (bf16[2,96,3072]{2,1,0:T(8,128)(2,1)}, bf16[2,96,3072]{2,1,0:T(8,128)(2,1)}, u32[]{:S(2)}, u32[]{:S(2)}) collective-permute-start(bf16[2,96,3072]{2,1,0:T(8,128)(2,1)} %fusion), channel_id=1, source_target_pairs={{0,2},{1,3},{2,0},{3,1},{4,6},{5,7},{6,4},{7,5},{8,10},{9,11},{10,... | collective-permute-start | bytes 3538952 | tf_op jit(solution)/shard_map/ppermute | solution.py:29
  79.3 66.7 %collective-permute-start.22 = (bf16[2,96,3072]{2,1,0:T(8,128)(2,1)}, bf16[2,96,3072]{2,1,0:T(8,128)(2,1)}, u32[]{:S(2)}, u32[]{:S(2)}) collective-permute-start(bf16[2,96,3072]{2,1,0:T(8,128)(2,1)} %fusion), channel_id=1, source_target_pairs={{0,1},{1,0},{2,3},{3,2},{4,5},{5,4},{6,7},{7,6},{8,9},{9,8},{10,11... | collective-permute-start | bytes 3538952 | tf_op jit(solution)/shard_map/ppermute | solution.py:29
  79.3 57.0 %collective-permute-start.16 = (bf16[32,3072]{1,0:T(8,128)(2,1)S(1)}, bf16[32,3072]{1,0:T(8,128)(2,1)S(1)}, u32[]{:S(2)}, u32[]{:S(2)}) collective-permute-start(bf16[32,3072]{1,0:T(8,128)(2,1)S(1)} %constant_dynamic-update-slice_fusion), channel_id=1, source_target_pairs={{0,2},{1,3},{2,0},{3,1},{4,6},{5,7},{6,4},{7,5},{8,10},{9,11},{10,... | collective-permute-start | bytes 589832 | tf_op jit(solution)/shard_map/ppermute | solution.py:29
  80.7 57.5 %collective-permute-start.15 = (bf16[32,3072]{1,0:T(8,128)(2,1)S(1)}, bf16[32,3072]{1,0:T(8,128)(2,1)S(1)}, u32[]{:S(2)}, u32[]{:S(2)}) collective-permute-start(bf16[32,3072]{1,0:T(8,128)(2,1)S(1)} %constant_dynamic-update-slice_fusion), channel_id=1, source_target_pairs={{0,1},{1,0},{2,3},{3,2},{4,5},{5,4},{6,7},{7,6},{8,9},{9,8},{10,11... | collective-permute-start | bytes 589832 | tf_op jit(solution)/shard_map/ppermute | solution.py:29
  136.3 3.9 %collective-permute-start.19 = (bf16[256,96]{1,0:T(8,128)(2,1)S(1)}, bf16[256,96]{1,0:T(8,128)(2,1)S(1)}, u32[]{:S(2)}, u32[]{:S(2)}) collective-permute-start(bf16[256,96]{1,0:T(8,128)(2,1)S(1)} %constant_dynamic-slice_fusion), channel_id=1, source_target_pairs={{0,1},{1,0},{2,3},{3,2},{4,5},{5,4},{6,7},{7,6},{8,9},{9,8},{10,11... | collective-permute-start | bytes 147464 | tf_op jit(solution)/shard_map/ppermute | solution.py:29
  138.2 3.7 %collective-permute-start.20 = (bf16[256,96]{1,0:T(8,128)(2,1)S(1)}, bf16[256,96]{1,0:T(8,128)(2,1)S(1)}, u32[]{:S(2)}, u32[]{:S(2)}) collective-permute-start(bf16[256,96]{1,0:T(8,128)(2,1)S(1)} %constant_dynamic-slice_fusion), channel_id=1, source_target_pairs={{0,2},{1,3},{2,0},{3,1},{4,6},{5,7},{6,4},{7,5},{8,10},{9,11},{10,... | collective-permute-start | bytes 147464 | tf_op jit(solution)/shard_map/ppermute | solution.py:29
  140.3 16.0 %collective-permute-start.18 = (bf16[4,1,32,3072]{3,2,1,0:T(8,128)(2,1)S(1)}, bf16[4,1,32,3072]{3,2,1,0:T(8,128)(2,1)S(1)}, u32[]{:S(2)}, u32[]{:S(2)}) collective-permute-start(bf16[4,1,32,3072]{3,2,1,0:T(8,128)(2,1)S(1)} %maximum_bitcast_fusion.right_ref.near_ref), channel_id=1, source_target_pairs={{0,4},{4,0},{8,12},{12,8},{16,20},{20,16},{24,28},{28,24},{1,5},{5... | collective-permute-start | bytes 2359304 | tf_op jit(solution)/shard_map/ppermute | solution.py:29
  141.9 4.0 %collective-permute-start.21 = (bf16[256,96]{1,0:T(8,128)(2,1)S(1)}, bf16[256,96]{1,0:T(8,128)(2,1)S(1)}, u32[]{:S(2)}, u32[]{:S(2)}) collective-permute-start(bf16[256,96]{1,0:T(8,128)(2,1)S(1)} %constant_dynamic-slice_fusion), channel_id=1, source_target_pairs={{0,3},{1,2},{2,1},{3,0},{4,7},{5,6},{6,5},{7,4},{8,11},{9,10},{10,... | collective-permute-start | bytes 147464 | tf_op jit(solution)/shard_map/ppermute | solution.py:29

commit v2 on v1

--- a/solution.py
+++ b/solution.py
@@ -9,13 +9,18 @@
 
 CORES = 2
 LANES = 128
-VMEM_LIMIT = 48 * 1024 * 1024
+PLACES = 5
+VMEM_LIMIT = 24 * 1024 * 1024
 F32 = jnp.float32
 BF16 = jnp.bfloat16
 
 
 def params():
     return pltpu.CompilerParams(vmem_limit_bytes=VMEM_LIMIT)
+
+
+def cost():
+    return pl.CostEstimate(flops=1000, bytes_accessed=1000, transcendentals=0)
 
 
 def tree_sum(terms):
@@ -29,16 +34,17 @@
     return lax.ppermute(x, axis, [(i, i ^ distance) for i in range(size)])
 
 
-def left_kernel(g_ref, f_ref, q_ref, vec_ref, comp_ref, left_ref):
+def left_kernel(pos, g_ref, f_ref, q_ref, vec_ref, comp_ref, near_ref, far_ref, total):
     k = pl.program_id(0)
     rows = g_ref.shape[2]
     rank = q_ref.shape[1]
     group = LANES // rank
+    near, piece, _ = near_ref.shape
 
     @pl.when(k == 0)
     def _():
-        left_ref[:rows, :] = jnp.zeros((rows, left_ref.shape[1]), F32)
-        left_ref[rows:, :] = vec_ref[...]
+        total[:rows, :] = jnp.zeros((rows, total.shape[1]), F32)
+        total[rows:, :] = vec_ref[...]
 
     comp = (g_ref[0, 0].astype(F32) + f_ref[0, 0].astype(F32)).astype(BF16)
     comp_ref[0] = comp
@@ -48,49 +54,60 @@
     wide = jnp.where(member == k % group, wide, jnp.zeros_like(wide))
     terms = lax.dot_general(comp, wide, (((1,), (1,)), ((), ())), preferred_element_type=F32)
     cols = pl.ds(pl.multiple_of((k // group) * LANES, LANES), LANES)
-    left_ref[:rows, cols] += terms
-
-
-def left_terms(gradients, feedback, right_t, vec):
+    total[:rows, cols] += terms
+
+    @pl.when(k == pl.num_programs(0) - 1)
+    def _():
+        for s in range(near):
+            for out, slot in ((near_ref, s), (far_ref, s + near)):
+                out[s] = total[pl.ds(pl.multiple_of((slot ^ pos[3]) * piece, piece), piece), :]
+
+
+def left_terms(pos, gradients, feedback, right_t, vec, n_z):
     _, nmat, rows, n = gradients.shape
     rank = right_t.shape[1]
+    width = nmat * rank
     total = rows + vec.shape[0]
+    pieces = jax.ShapeDtypeStruct((n_z, total // (CORES * n_z), width), F32)
     return pl.pallas_call(
         left_kernel,
-        grid=(nmat,),
-        in_specs=[
-            pl.BlockSpec((1, 1, rows, n), lambda k: (0, k, 0, 0)),
-            pl.BlockSpec((1, 1, rows, n), lambda k: (0, k, 0, 0)),
-            pl.BlockSpec((1, rank, n), lambda k: (k, 0, 0)),
-            pl.BlockSpec(vec.shape, lambda k: (0, 0)),
-        ],
-        out_specs=[
-            pl.BlockSpec((1, rows, n), lambda k: (k, 0, 0)),
-            pl.BlockSpec((total, nmat * rank), lambda k: (0, 0)),
-        ],
-        out_shape=[
-            jax.ShapeDtypeStruct((nmat, rows, n), BF16),
-            jax.ShapeDtypeStruct((total, nmat * rank), F32),
-        ],
-        compiler_params=params(),
-        cost_estimate=pl.CostEstimate(
-            flops=2 * nmat * rows * n * LANES, bytes_accessed=6 * nmat * rows * n, transcendentals=0
-        ),
+        grid_spec=pltpu.PrefetchScalarGridSpec(
+            num_scalar_prefetch=1,
+            grid=(nmat,),
+            in_specs=[
+                pl.BlockSpec((1, 1, rows, n), lambda k, pos: (0, k, 0, 0)),
+                pl.BlockSpec((1, 1, rows, n), lambda k, pos: (0, k, 0, 0)),
+                pl.BlockSpec((1, rank, n), lambda k, pos: (k, 0, 0)),
+                pl.BlockSpec(vec.shape, lambda k, pos: (0, 0)),
+            ],
+            out_specs=[
+                pl.BlockSpec((1, rows, n), lambda k, pos: (k, 0, 0)),
+                pl.BlockSpec(pieces.shape, lambda k, pos: (0, 0, 0)),
+                pl.BlockSpec(pieces.shape, lambda k, pos: (0, 0, 0)),
+            ],
+            scratch_shapes=[pltpu.VMEM((total, width), F32)],
+        ),
+        out_shape=[jax.ShapeDtypeStruct((nmat, rows, n), BF16), pieces, pieces],
+        compiler_params=params(),
+        cost_estimate=cost(),
         name="left_terms",
-    )(gradients, feedback, right_t, vec)
-
-
-def right_kernel(half, pos, mine_ref, other_ref, gram_ref, comp_ref, send_ref, keep_ref, lt_ref, left):
+    )(pos, gradients, feedback, right_t, vec)
+
+
+def right_kernel(half, pos, near_ref, far_ref, gram_ref, comp_ref, *refs):
+    send_ref, keep_ref, lt_ref, vec_ref, left = refs[-5:]
     t = pl.program_id(0)
     rows = comp_ref.shape[1]
-    part = mine_ref.shape[0]
     upm, unit = send_ref.shape[1], send_ref.shape[2]
     rank = upm * unit
 
     @pl.when(t == 0)
     def _():
-        left[pl.ds(pl.multiple_of(pos[2] * part, 8), part), :] = mine_ref[...]
-        left[pl.ds(pl.multiple_of((1 - pos[2]) * part, 8), part), :] = other_ref[...]
+        near, piece, _ = near_ref.shape
+        for s in range(near):
+            for part, slot in ((near_ref, s), (far_ref, s + near)):
+                left[pl.ds(pl.multiple_of((slot ^ pos[3]) * piece, piece), piece), :] = part[s]
+        vec_ref[...] = left[rows:, :]
         hat = jnp.dot(
             left[:rows, :], gram_ref[...], precision=lax.Precision.HIGHEST, preferred_element_type=F32
         )
@@ -111,40 +128,117 @@
             keep_ref[0, i ^ pos[1]] = terms[i * unit : (i + 1) * unit]
 
 
-def right_terms(pos, mine, other, gram, comp, upm):
+def right_terms(pos, near, far, gram, comp, upm, after):
     nmat, rows, n = comp.shape
     rank = gram.shape[0] // nmat
     unit = rank // upm
-    half = nmat // 2
+    half = nmat // CORES
+    total = CORES * near.shape[0] * near.shape[1]
     return pl.pallas_call(
         functools.partial(right_kernel, half),
         grid_spec=pltpu.PrefetchScalarGridSpec(
             num_scalar_prefetch=1,
             grid=(nmat,),
             in_specs=[
-                pl.BlockSpec(mine.shape, lambda t, pos: (0, 0)),
-                pl.BlockSpec(other.shape, lambda t, pos: (0, 0)),
+                pl.BlockSpec(near.shape, lambda t, pos: (0, 0, 0)),
+                pl.BlockSpec(far.shape, lambda t, pos: (0, 0, 0)),
                 pl.BlockSpec(gram.shape, lambda t, pos: (0, 0)),
                 pl.BlockSpec((1, rows, n), lambda t, pos: (lax.rem(t + half, nmat) ^ pos[0], 0, 0)),
-            ],
+            ]
+            + [pl.BlockSpec(memory_space=pl.ANY)] * len(after),
             out_specs=[
                 pl.BlockSpec((1, upm, unit, n), lambda t, pos: (jnp.minimum(t, half - 1), 0, 0, 0)),
                 pl.BlockSpec((1, upm, unit, n), lambda t, pos: (jnp.maximum(t - half, 0), 0, 0, 0)),
                 pl.BlockSpec((nmat * rank, rows), lambda t, pos: (0, 0)),
+                pl.BlockSpec((total - rows, nmat * rank), lambda t, pos: (0, 0)),
             ],
-            scratch_shapes=[pltpu.VMEM((2 * mine.shape[0], mine.shape[1]), F32)],
+            scratch_shapes=[pltpu.VMEM((total, nmat * rank), F32)],
         ),
         out_shape=[
             jax.ShapeDtypeStruct((half, upm, unit, n), BF16),
             jax.ShapeDtypeStruct((half, upm, unit, n), F32),
             jax.ShapeDtypeStruct((nmat * rank, rows), BF16),
+            jax.ShapeDtypeStruct((total - rows, nmat * rank), F32),
         ],
         compiler_params=params(),
-        cost_estimate=pl.CostEstimate(
-            flops=2 * nmat * rows * n * LANES, bytes_accessed=2 * nmat * rows * n, transcendentals=0
-        ),
+        cost_estimate=cost(),
         name="right_terms",
-    )(pos, mine, other, gram, comp)
+    )(pos, near, far, gram, comp, *after)
+
+
+def chip_kernel(keep_ref, recv_ref, *refs):
+    n_out = keep_ref.shape[0] * keep_ref.shape[1]
+    upm = keep_ref.shape[1]
+    for d, out in enumerate(refs[-n_out:]):
+        j, i = d // upm, d % upm
+        out[...] = (keep_ref[j, i] + recv_ref[j, i].astype(F32)).astype(out.dtype)
+
+
+def chip_sum(keep, recv, after):
+    half, upm, unit, n = keep.shape
+    vmem = pl.BlockSpec(memory_space=pltpu.VMEM)
+    return pl.pallas_call(
+        chip_kernel,
+        in_specs=[vmem] * 2 + [pl.BlockSpec(memory_space=pl.ANY)] * len(after),
+        out_specs=[vmem] * (half * upm),
+        out_shape=[jax.ShapeDtypeStruct((unit, n), BF16 if d else F32) for d in range(half * upm)],
+        compiler_params=params(),
+        cost_estimate=cost(),
+        name="chip_sum",
+    )(keep, recv, *after)
+
+
+def column_kernel(n_z, pos, *refs):
+    out = refs[-1]
+    cols = out.shape[1] // n_z
+    for d in range(n_z):
+        out[:, pl.ds(pl.multiple_of((pos[4] ^ d) * cols, cols), cols)] = refs[d][...]
+
+
+def column_gather(pos, parts, after):
+    unit, cols = parts[0].shape
+    vmem = pl.BlockSpec(memory_space=pltpu.VMEM)
+    return pl.pallas_call(
+        functools.partial(column_kernel, len(parts)),
+        grid_spec=pltpu.PrefetchScalarGridSpec(
+            num_scalar_prefetch=1,
+            grid=(1,),
+            in_specs=[vmem] * len(parts) + [pl.BlockSpec(memory_space=pl.ANY)] * len(after),
+            out_specs=vmem,
+        ),
+        out_shape=jax.ShapeDtypeStruct((unit, cols * len(parts)), BF16),
+        compiler_params=params(),
+        cost_estimate=cost(),
+        name="column_gather",
+    )(pos, *parts, *after)
+
+
+def plane_kernel(count, n_z, pos, *refs):
+    terms, outs = refs[:count], refs[-n_z:]
+    cols = outs[0].shape[1]
+    for d, out in enumerate(outs):
+        block = pl.ds(pl.multiple_of((pos[4] ^ d) * cols, cols), cols)
+        out[...] = tree_sum([term[:, block].astype(F32) for term in terms]).astype(out.dtype)
+
+
+def plane_sum(pos, terms, n_z):
+    unit, n = terms[0].shape
+    cols = n // n_z
+    whole = pl.BlockSpec((unit, n), lambda i, pos: (0, 0))
+    part = pl.BlockSpec((unit, cols), lambda i, pos: (0, 0))
+    return pl.pallas_call(
+        functools.partial(plane_kernel, len(terms), n_z),
+        grid_spec=pltpu.PrefetchScalarGridSpec(
+            num_scalar_prefetch=1,
+            grid=(1,),
+            in_specs=[whole] * len(terms),
+            out_specs=[part] * n_z,
+        ),
+        out_shape=[jax.ShapeDtypeStruct((unit, cols), BF16 if d else F32) for d in range(n_z)],
+        compiler_params=params(),
+        cost_estimate=cost(),
+        name="plane_sum",
+    )(pos, *terms)
 
 
 def matrix_of(right_ref, sub):
@@ -184,7 +278,7 @@
                 pl.BlockSpec((1, upm, unit, n), lambda j, pos: (j, 0, 0, 0)),
                 pl.BlockSpec((rank, rows), lambda j, pos: (matrix(j, pos), 0)),
                 pl.BlockSpec((rank, replica_rows), lambda j, pos: (matrix(j, pos), 0)),
-                pl.BlockSpec((1, replica_rows, n), lambda j, pos: (pos[3 + matrix(j, pos)], 0, 0)),
+                pl.BlockSpec((1, replica_rows, n), lambda j, pos: (pos[PLACES + matrix(j, pos)], 0, 0)),
             ]
             + [any_spec] * len(earlier),
             out_specs=[
@@ -198,11 +292,7 @@
         ],
         input_output_aliases={6 + i: i for i in range(len(earlier))},
         compiler_params=params(),
-        cost_estimate=pl.CostEstimate(
-            flops=2 * half * (rows + replica_rows) * n * LANES,
-            bytes_accessed=4 * half * (rows + replica_rows) * n,
-            transcendentals=0,
-        ),
+        cost_estimate=cost(),
         name="outputs",
     )(pos, comp, right, lt, ltr, base, *earlier)
 
@@ -246,9 +336,7 @@
         ),
         out_shape=[jax.ShapeDtypeStruct(momentum.shape, F32)] * 2,
         compiler_params=params(),
-        cost_estimate=pl.CostEstimate(
-            flops=2 * capacity * rows * n * LANES, bytes_accessed=16 * capacity * rows * n, transcendentals=0
-        ),
+        cost_estimate=cost(),
         name="owned",
     )(pos, momentum, master, near, far, ltr)
 
@@ -277,8 +365,14 @@
     half = nmat // CORES
     code = core * n_mp + p
 
-    base = (master_weights[0] - 0.09 * momentum[0]).astype(BF16)
-    base_all = jnp.concatenate([base] + [exchange(base, "mp", d) for d in range(1, n_mp)], axis=0)
+    held_rows = capacity * replica_rows
+    old_master = master_weights.reshape(held_rows, n)
+    old_momentum = momentum.reshape(held_rows, n)
+    cuts = [0, held_rows // 2, 2 * held_rows // 3, held_rows]
+    bases = []
+    for first, last in zip(cuts, cuts[1:]):
+        base = (old_master[first:last] - 0.09 * old_momentum[first:last]).astype(BF16)
+        bases.append([base] + [exchange(base, "mp", d) for d in range(1, n_mp)])
 
     same_owner = owners[:, None] == owners[None, :]
     earlier = jnp.arange(nmat)[:, None] < jnp.arange(nmat)[None, :]
@@ -286,41 +380,39 @@
     relative = (owners ^ p) * capacity + ranks
     mine = relative[None, :] == jnp.arange(capacity)[:, None]
     held = jnp.max(jnp.where(mine, jnp.arange(nmat)[None, :], -1), axis=1)
-    pos = jnp.concatenate([jnp.stack([code // upm, code % upm, core]), relative, held]).astype(jnp.int32)
+    pos = jnp.concatenate([jnp.stack([code // upm, code % upm, core, core * n_z + z, z]), relative, held]).astype(jnp.int32)
 
     nvec = vector_grads.shape[1]
     width = nmat * rank
-    vec = jnp.pad(vector_grads[0], (0, 16 * width - nvec)).reshape(16, width)
-    comp, terms = left_terms(gradients, feedback, jnp.swapaxes(right_init, 1, 2), vec)
-    chip = terms + exchange(terms, "replica", 1)
-    part = terms.shape[0] // CORES
-    piece = lax.dynamic_slice_in_dim(chip, core * part, part, 0)
-    piece = tree_sum([piece] + [exchange(piece, "replica", CORES * d) for d in range(1, n_z)])
-    other = exchange(piece, "replica", 1)
-    vector_half = jnp.where(core == 1, piece, other)
-    vector_total = vector_half[part - 16 :].reshape(-1)[:nvec]
+    pieces = CORES * n_z
+    extra = -(-nvec // width)
+    extra += -(rows + extra) % (8 * pieces)
+    vec = jnp.pad(vector_grads[0], (0, extra * width - nvec)).reshape(extra, width)
+    comp, near, far = left_terms(
+        pos,
+        pltpu.with_memory_space_constraint(gradients, pltpu.HBM),
+        pltpu.with_memory_space_constraint(feedback, pltpu.HBM),
+        jnp.swapaxes(right_init, 1, 2),
+        vec,
+        n_z,
+    )
+    chip = near + exchange(far, "replica", 1)
+    piece = tree_sum([chip[0]] + [exchange(chip[d], "replica", CORES * d) for d in range(1, n_z)])
+    near = jnp.stack([piece] + [exchange(piece, "replica", CORES * d) for d in range(1, n_z)])
+    far = exchange(near, "replica", 1)
 
     block = jnp.eye(nmat, dtype=bool)[:, None, :, None]
     gram = jnp.where(block, gram_root[:, :, None, :], 0.0).reshape(width, width)
-    send, keep, lt = right_terms(pos, piece, other, gram, comp, upm)
-    chip = keep + exchange(send, "replica", 1).astype(F32)
-    chip = chip.reshape(n_mp, rank // upm, n)
-    narrow = chip.astype(BF16)
-    plane = tree_sum([chip[0]] + [exchange(narrow[d], "mp", d).astype(F32) for d in range(1, n_mp)])
-    cols = n // n_z
-    plane_narrow = plane.astype(BF16)
-    final = [lax.dynamic_slice_in_dim(plane, z * cols, cols, 1)]
-    for d in range(1, n_z):
-        sent = lax.dynamic_slice_in_dim(plane_narrow, (z ^ d) * cols, cols, 1)
-        final.append(exchange(sent, "replica", CORES * d).astype(F32))
+    send, keep, lt, vector_rows = right_terms(pos, near, far, gram, comp, upm, bases[0][1:])
+    vector_total = vector_rows.reshape(-1)[:nvec]
+    chip = chip_sum(keep, exchange(send, "replica", 1), bases[1][1:])
+    plane = [chip[0]] + [exchange(chip[d], "mp", d) for d in range(1, n_mp)]
+    final = plane_sum(pos, plane, n_z)
+    final = [final[0]] + [exchange(final[d], "replica", CORES * d).astype(F32) for d in range(1, n_z)]
     final = tree_sum(final).astype(BF16)
 
-    whole = jnp.zeros((rank // upm, n), BF16)
-    whole = lax.dynamic_update_slice_in_dim(whole, final, z * cols, 1)
-    for d in range(1, n_z):
-        whole = lax.dynamic_update_slice_in_dim(
-            whole, exchange(final, "replica", CORES * d), (z ^ d) * cols, 1
-        )
+    final = [final] + [exchange(final, "replica", CORES * d) for d in range(1, n_z)]
+    whole = column_gather(pos, final, bases[2][1:])
     near = jnp.stack([whole] + [exchange(whole, "mp", d) for d in range(1, n_mp)])
     near = near.reshape(half, upm, rank // upm, n)
     far = exchange(near, "replica", 1)
@@ -330,9 +422,11 @@
     strips = jnp.stack([strip] + [exchange(strip, "mp", d) for d in range(1, n_mp)])
     ltr = lax.dynamic_index_in_dim(strips, (first // rows) ^ p, 0, keepdims=False)
 
+    base_all = jnp.concatenate([part[d] for d in range(n_mp) for part in bases], axis=0)
+    base_all = base_all.reshape(n_mp * capacity, replica_rows, n)
     done = outputs(pos, 0, comp, near, lt, ltr, base_all, ())
     new_feedback, new_weights = outputs(pos, half, comp, far, lt, ltr, base_all, done)
-    new_momentum, new_master = owned(pos, 3 + nmat, momentum, master_weights, near, far, ltr)
+    new_momentum, new_master = owned(pos, PLACES + nmat, momentum, master_weights, near, far, ltr)
 
     new_vector_momentum = 0.9 * vector_momentum + vector_total
     new_vector_params = vector_params - 0.1 * new_vector_momentum

time: 171 us -> 137 us (0.80)
  waiting for transfers between devices: 86.8 us -> 36.2 us
  local copies, waits for them, and re-layouts: 2.8 us -> 20.5 us
  starting transfers between devices: 27 us -> 35.2 us
  Pallas kernels: 39.5 us -> 32 us
    ppermute x25 -> x34, waiting for transfers between devices: 86.8 us -> 36.2 us  [exchange(): return lax.ppermute(x, axis, [(i, i ^ distance) for i in range(size)])]
    unnamed x13 -> x37, local copies, waits for them, and re-layouts: 1.44 us -> 17.1 us
    ppermute x25 -> x34, starting transfers between devices: 27 us -> 35.2 us  [exchange(): return lax.ppermute(x, axis, [(i, i ^ distance) for i in range(size)])]
    convert_element_type x3 -> x1, other arithmetic: 5.79 us -> 0.02 us  [per_device(): final = tree_sum(final).astype(BF16)]
    unnamed x2 -> x5, other arithmetic: 0.74 us -> 5.35 us
    pallas_call x1, Pallas kernels: 8.19 us -> 3.96 us  [right_terms(): pl.pallas_call(functools.partial(right_kernel, half), grid_spec=pltpu.Pre...]
    concatenate x1 -> x0, other arithmetic: 3.21 us -> none  [per_device(): jnp.concatenate([base] + [exchange(base, 'mp', d) for d in range(1, n_mp)...]
    select_n x1, local copies, waits for them, and re-layouts: 0.31 us -> 2.23 us  [per_device(): gram = jnp.where(block, gram_root[:, :, None, :], 0.0).reshape(width, width)]
  transfers between devices with their start and end apart: 25 -> 34, of which waited for: 14 -> 11; matrix products, arithmetic and copies ran while one was open for 5% -> 13% of each run, Pallas kernels for 4% -> 17%
where the time goes in v2:
time: 137 us; the launch traced here: 135 us
  waiting for transfers between devices  36.2 us (26%)
  starting transfers between devices  35.2 us (26%)
  Pallas kernels  32 us (23%)
  local copies, waits for them, and re-layouts  20.5 us (15%)
  other arithmetic  10.4 us (8%)
    ppermute x34, waiting for transfers between devices, exchange(): return lax.ppermute(x, axis, [(i, i ^ distance) for i in range(size)])  36.2 us
    ppermute x34, starting transfers between devices, exchange(): return lax.ppermute(x, axis, [(i, i ^ distance) for i in range(size)])  35.2 us
    unnamed x37, local copies, waits for them, and re-layouts  17.1 us
    pallas_call x2, Pallas kernels, outputs(): pl.pallas_call(outputs_kernel, grid_spec=pltpu.PrefetchScalarGridSpec(num...  12.8 us
    pallas_call x1, Pallas kernels, left_terms(): pl.pallas_call(left_kernel, grid_spec=pltpu.PrefetchScalarGridSpec(num_sc...  10.7 us
    unnamed x5, other arithmetic  5.35 us
    pallas_call x1, Pallas kernels, right_terms(): pl.pallas_call(functools.partial(right_kernel, half), grid_spec=pltpu.Pre...  3.96 us
    pallas_call x1, Pallas kernels, owned(): pl.pallas_call(functools.partial(owned_kernel, half, held), grid_spec=plt...  3.21 us
  transfers between devices with their start and end apart: 34, of which 11 were waited for; matrix products, arithmetic and copies ran while one was open for 13% of the time, Pallas kernels for 17%

profile of v2, /device:TPU:1, one launch (start us, length us, event | category | flops | bytes accessed | tf_op | source)
XLA Modules:
  0.0 135.1 jit_solution(10025323055856053034)
XLA Ops:
  0.6 2.8 %constant_dynamic-update-slice_fusion.11 = (bf16[768,3072]{1,0:T(8,128)(2,1)}, bf16[96,3072]{1,0:T(8,128)(2,1)}) fusion(f32[1,2,96,3072]{3,2,1,0:T(8,128)} %momentum_ref.1, f32[1,2,96,3072]{3,2,1,0:T(8,128)} %master_ref.1), kind=kLoop, calls=%fused_computation.37 | loop fusion | flops 884735 | bytes 3538944
  3.5 2.0 %collective-permute-start.8 = (bf16[96,3072]{1,0:T(8,128)(2,1)}, bf16[96,3072]{1,0:T(8,128)(2,1)}, u32[]{:S(2)}, u32[]{:S(2)}) collective-permute-start(bf16[96,3072]{1,0:T(8,128)(2,1)} %get-tuple-element.55), channel_id=1, source_target_pairs={{0,1},{1,0},{2,3},{3,2},{4,5},{5,4},{6,7},{7,6},{8,9},{9,8},{10,11... | collective-permute-start | bytes 1769480 | tf_op jit(solution)/shard_map/ppermute | solution.py:34
  5.5 1.2 collective-permute-start.9
  9.2 1.4 %copy-done.5 = bf16[8,3072,32]{1,2,0:T(8,128)(2,1)S(1)} copy-done((bf16[8,3072,32]{1,2,0:T(8,128)(2,1)S(1)}, bf16[8,3072,32]{1,2,0:T(8,128)(2,1)}, u32[]{:S(2)}) %copy-start.5) | copy-done | bytes 1572888
  10.6 10.7 %left_terms.1 = (bf16[8,192,3072]{2,1,0:T(8,128)(2,1)S(1)}, f32[4,32,256]{2,1,0:T(8,128)S(1)}, f32[4,32,256]{2,1,0:T(8,128)S(1)}) custom-call(s32[15]{0:T(128)S(1)} %concatenate.6.pos, bf16[1,8,192,3072]{3,2,1,0:T(8,128)(2,1)} %g_ref.1, bf16[1,8,192,3072]{3,2,1,0:T(8,128)(2,1)} %f_ref.1, bf16[8,32,3072]{2,1,0:T(8,128)(2,1)S(1)} %bitcast.50, ...), custom_call_target="tpu_custom_call" | custom-call | flops 1000 | bytes 1000 | tf_op jit(solution)/shard_map/left_terms/pallas_call | solution.py:72
  21.3 3.7 %copy-done = bf16[8,192,3072]{2,1,0:T(8,128)(2,1)} copy-done((bf16[8,192,3072]{2,1,0:T(8,128)(2,1)}, bf16[8,192,3072]{2,1,0:T(8,128)(2,1)S(1)}, u32[]{:S(2)}) %copy-start) | copy-done | bytes 9437208
  25.0 1.2 collective-permute-start
  27.3 1.4 %collective-permute-start.1 = (f32[32,256]{1,0:T(8,128)S(1)}, f32[32,256]{1,0:T(8,128)S(1)}, u32[]{:S(2)}, u32[]{:S(2)}) collective-permute-start(f32[32,256]{1,0:T(8,128)S(1)} %get-tuple-element.58), channel_id=1, source_target_pairs={{0,8},{4,12},{8,0},{12,4},{16,24},{20,28},{24,16},{28,20},{1,9},{5... | collective-permute-start | bytes 98312 | tf_op jit(solution)/shard_map/ppermute | solution.py:34
  28.7 2.3 %collective-permute-start.2 = (f32[32,256]{1,0:T(8,128)S(1)}, f32[32,256]{1,0:T(8,128)S(1)}, u32[]{:S(2)}, u32[]{:S(2)}) collective-permute-start(f32[32,256]{1,0:T(8,128)S(1)} %get-tuple-element.57), channel_id=1, source_target_pairs={{0,16},{4,20},{8,24},{12,28},{16,0},{20,4},{24,8},{28,12},{1,17},{... | collective-permute-start | bytes 98312 | tf_op jit(solution)/shard_map/ppermute | solution.py:34
  32.7 2.9 %collective-permute-done.3 = f32[32,256]{1,0:T(8,128)S(1)} collective-permute-done((f32[32,256]{1,0:T(8,128)S(1)}, f32[32,256]{1,0:T(8,128)S(1)}, u32[]{:S(2)}, u32[]{:S(2)}) %collective-permute-start.3) | collective-permute-done | bytes 32800 | tf_op jit(solution)/shard_map/ppermute | solution.py:34
  36.6 4.5 %collective-permute-done.6 = f32[32,256]{1,0:T(8,128)} collective-permute-done((f32[32,256]{1,0:T(8,128)}, f32[32,256]{1,0:T(8,128)}, u32[]{:S(2)}, u32[]{:S(2)}) %collective-permute-start.6) | collective-permute-done | bytes 32800 | tf_op jit(solution)/shard_map/ppermute | solution.py:34
  41.0 1.1 broadcast_select_fusion
  42.2 2.2 %select_n.44.gram_ref = f32[256,256]{1,0:T(8,128)} reshape(f32[8,32,8,32]{3,2,1,0:T(8,128)} %broadcast_select_fusion) | data formatting | bytes 524288 | tf_op jit(solution)/shard_map/jit(_where)/select_n | solution.py:405
  44.8 1.1 collective-permute-start.24
  46.7 3.8 %collective-permute-start.7 = (f32[4,32,256]{2,1,0:T(8,128)S(1)}, f32[4,32,256]{2,1,0:T(8,128)S(1)}, u32[]{:S(2)}, u32[]{:S(2)}) collective-permute-start(f32[4,32,256]{2,1,0:T(8,128)S(1)} %pad_maximum_fusion.near_ref), channel_id=1, source_target_pairs={{0,4},{4,0},{8,12},{12,8},{16,20},{20,16},{24,28},{28,24},{1,5},{5... | collective-permute-start | bytes 393224 | tf_op jit(solution)/shard_map/ppermute | solution.py:34
  50.5 1.9 %constant_dynamic-update-slice_fusion.8 = bf16[768,3072]{1,0:T(8,128)(2,1)} fusion(bf16[768,3072]{1,0:T(8,128)(2,1)} %get-tuple-element.50, bf16[96,3072]{1,0:T(8,128)(2,1)} %collective-permute-done.8.refs_0_), kind=kLoop, calls=%fused_computation.34 | loop fusion | bytes 1179648
  53.0 1.2 collective-permute-start.14
  54.8 3.7 %copy-done.1 = bf16[8,192,3072]{2,1,0:T(8,128)(2,1)S(1)} copy-done((bf16[8,192,3072]{2,1,0:T(8,128)(2,1)S(1)}, bf16[8,192,3072]{2,1,0:T(8,128)(2,1)}, u32[]{:S(2)}) %copy-start.1) | copy-done | bytes 9437208
  59.4 4.0 %right_terms.1 = (bf16[4,1,32,3072]{3,2,1,0:T(8,128)(2,1)S(1)}, f32[4,1,32,3072]{3,2,1,0:T(8,128)S(1)}, bf16[256,192]{1,0:T(8,128)(2,1)S(1)}, f32[64,256]{1,0:T(8,128)S(1)}) custom-call(s32[15]{0:T(128)S(1)} %concatenate.6.pos, f32[4,32,256]{2,1,0:T(8,128)S(1)} %pad_maximum_fusion.near_ref, f32[4,32,256]{2,1,0:T(8,128)S(1)} %collective-permute-done.7.far_ref, ...), custom_call_target="tpu_custom_call" | custom-call | flops 1000 | bytes 1000 | tf_op jit(solution)/shard_map/right_terms/pallas_call | solution.py:137
  65.0 1.5 %collective-permute-start.26 = (bf16[64,3072]{1,0:T(8,128)(2,1)S(1)}, bf16[64,3072]{1,0:T(8,128)(2,1)S(1)}, u32[]{:S(2)}, u32[]{:S(2)}) collective-permute-start(bf16[64,3072]{1,0:T(8,128)(2,1)S(1)} %copy-done.7), channel_id=1, source_target_pairs={{0,3},{1,2},{2,1},{3,0},{4,7},{5,6},{6,5},{7,4},{8,11},{9,10},{10,... | collective-permute-start | bytes 1179656 | tf_op jit(solution)/shard_map/ppermute | solution.py:34
  69.6 1.5 %collective-permute-start.17 = (bf16[32,3072]{1,0:T(8,128)(2,1)S(1)}, bf16[32,3072]{1,0:T(8,128)(2,1)S(1)}, u32[]{:S(2)}, u32[]{:S(2)}) collective-permute-start(bf16[32,3072]{1,0:T(8,128)(2,1)S(1)} %get-tuple-element.35), channel_id=1, source_target_pairs={{0,3},{1,2},{2,1},{3,0},{4,7},{5,6},{6,5},{7,4},{8,11},{9,10},{10,... | collective-permute-start | bytes 589832 | tf_op jit(solution)/shard_map/ppermute | solution.py:34
  71.9 8.8 %collective-permute-done.15.refs_1_ = bf16[32,3072]{1,0:T(8,128)(2,1)S(1)} collective-permute-done((bf16[32,3072]{1,0:T(8,128)(2,1)S(1)}, bf16[32,3072]{1,0:T(8,128)(2,1)S(1)}, u32[]{:S(2)}, u32[]{:S(2)}) %collective-permute-start.15) | collective-permute-done | bytes 196640 | tf_op jit(solution)/shard_map/ppermute | solution.py:34
  81.5 7.1 %collective-permute-done.16.refs_2_ = bf16[32,3072]{1,0:T(8,128)(2,1)S(1)} collective-permute-done((bf16[32,3072]{1,0:T(8,128)(2,1)S(1)}, bf16[32,3072]{1,0:T(8,128)(2,1)S(1)}, u32[]{:S(2)}, u32[]{:S(2)}) %collective-permute-start.16) | collective-permute-done | bytes 196640 | tf_op jit(solution)/shard_map/ppermute | solution.py:34
  89.6 2.7 %collective-permute-start.19 = (bf16[32,768]{1,0:T(8,128)(2,1)S(1)}, bf16[32,768]{1,0:T(8,128)(2,1)S(1)}, u32[]{:S(2)}, u32[]{:S(2)}) collective-permute-start(bf16[32,768]{1,0:T(8,128)(2,1)S(1)} %get-tuple-element.38), channel_id=1, source_target_pairs={{0,16},{4,20},{8,24},{12,28},{16,0},{20,4},{24,8},{28,12},{1,17},{... | collective-permute-start | bytes 147464 | tf_op jit(solution)/shard_map/ppermute | solution.py:34
  94.2 3.0 %collective-permute-done.19 = bf16[32,768]{1,0:T(8,128)(2,1)S(1)} collective-permute-done((bf16[32,768]{1,0:T(8,128)(2,1)S(1)}, bf16[32,768]{1,0:T(8,128)(2,1)S(1)}, u32[]{:S(2)}, u32[]{:S(2)}) %collective-permute-start.19) | collective-permute-done | bytes 49184 | tf_op jit(solution)/shard_map/ppermute | solution.py:34
  97.6 3.4 %collective-permute-start.23 = (bf16[32,768]{1,0:T(8,128)(2,1)S(1)}, bf16[32,768]{1,0:T(8,128)(2,1)S(1)}, u32[]{:S(2)}, u32[]{:S(2)}) collective-permute-start(bf16[32,768]{1,0:T(8,128)(2,1)S(1)} %add_convert_fusion.refs_0_), channel_id=1, source_target_pairs={{0,24},{4,28},{8,16},{12,20},{16,8},{20,12},{24,0},{28,4},{1,25},{... | collective-permute-start | bytes 147464 | tf_op jit(solution)/shard_map/ppermute | solution.py:34
  106.9 2.2 %collective-permute-done.29 = bf16[32,3072]{1,0:T(8,128)(2,1)S(1)} collective-permute-done((bf16[32,3072]{1,0:T(8,128)(2,1)S(1)}, bf16[32,3072]{1,0:T(8,128)(2,1)S(1)}, u32[]{:S(2)}, u32[]{:S(2)}) %collective-permute-start.29) | collective-permute-done | bytes 196640 | tf_op jit(solution)/shard_map/ppermute | solution.py:34
  109.8 6.0 %collective-permute-done.28 = bf16[32,3072]{1,0:T(8,128)(2,1)S(1)} collective-permute-done((bf16[32,3072]{1,0:T(8,128)(2,1)S(1)}, bf16[32,3072]{1,0:T(8,128)(2,1)S(1)}, u32[]{:S(2)}, u32[]{:S(2)}) %collective-permute-start.28) | collective-permute-done | bytes 196640 | tf_op jit(solution)/shard_map/ppermute | solution.py:34
  115.9 1.5 %collective-permute-start.30 = (bf16[4,1,32,3072]{3,2,1,0:T(8,128)(2,1)S(1)}, bf16[4,1,32,3072]{3,2,1,0:T(8,128)(2,1)S(1)}, u32[]{:S(2)}, u32[]{:S(2)}) collective-permute-start(bf16[4,1,32,3072]{3,2,1,0:T(8,128)(2,1)S(1)} %maximum_bitcast_fusion.right_ref.near_ref), channel_id=1, source_target_pairs={{0,4},{4,0},{8,12},{12,8},{16,20},{20,16},{24,28},{28,24},{1,5},{5... | collective-permute-start | bytes 2359304 | tf_op jit(solution)/shard_map/ppermute | solution.py:34
  119.1 6.5 %outputs.2 = (bf16[1,8,192,3072]{3,2,1,0:T(8,128)(2,1)}, bf16[8,96,3072]{2,1,0:T(8,128)(2,1)}) custom-call(s32[15]{0:T(128)S(1)} %concatenate.6.pos, bf16[8,192,3072]{2,1,0:T(8,128)(2,1)S(1)} %bitcast.45, bf16[4,1,32,3072]{3,2,1,0:T(8,128)(2,1)S(1)} %maximum_bitcast_fusion.right_ref.near_ref, bf16[256,192]{1,0:T(8,128)(2,1)S(1)} %get-tuple-element.40.lt_ref, ...), custom_call_target="tpu_custom_call" | custom-call | flops 1000 | bytes 1000 | tf_op jit(solution)/shard_map/outputs/pallas_call | solution.py:271
  125.6 3.2 %owned.1 = (f32[1,2,96,3072]{3,2,1,0:T(8,128)}, f32[1,2,96,3072]{3,2,1,0:T(8,128)}) custom-call(s32[15]{0:T(128)S(1)} %concatenate.6.pos, f32[1,2,96,3072]{3,2,1,0:T(8,128)S(1)} %copy-done.2, f32[1,2,96,3072]{3,2,1,0:T(8,128)S(1)} %copy-done.4, bf16[4,1,32,3072]{3,2,1,0:T(8,128)(2,1)S(1)} %maximum_bitcast_fusion.right_ref.near_ref, ...), custom_call_target="tpu_custom_call" | custom-call | flops 1000 | bytes 1000 | tf_op jit(solution)/shard_map/owned/pallas_call | solution.py:323
  128.8 6.3 %outputs.3 = (bf16[1,8,192,3072]{3,2,1,0:T(8,128)(2,1)}, bf16[8,96,3072]{2,1,0:T(8,128)(2,1)}) custom-call(s32[15]{0:T(128)S(1)} %concatenate.6.pos, bf16[8,192,3072]{2,1,0:T(8,128)(2,1)S(1)} %bitcast.45, bf16[4,1,32,3072]{3,2,1,0:T(8,128)(2,1)S(1)} %collective-permute-done.30.right_ref.far_ref, ...), custom_call_target="tpu_custom_call", output_to_operand_aliasing={{0}: (6, {}), {1}: (7, {})} | custom-call | flops 1000 | bytes 1000 | tf_op jit(solution)/shard_map/outputs/pallas_call | solution.py:271
  (106 shorter events, 27.2 us)
Async XLA Ops:
  3.5 43.2 %collective-permute-start.8 = (bf16[96,3072]{1,0:T(8,128)(2,1)}, bf16[96,3072]{1,0:T(8,128)(2,1)}, u32[]{:S(2)}, u32[]{:S(2)}) collective-permute-start(bf16[96,3072]{1,0:T(8,128)(2,1)} %get-tuple-element.55), channel_id=1, source_target_pairs={{0,1},{1,0},{2,3},{3,2},{4,5},{5,4},{6,7},{7,6},{8,9},{9,8},{10,11... | collective-permute-start | bytes 1769480 | tf_op jit(solution)/shard_map/ppermute | solution.py:34
  5.5 47.5 %collective-permute-start.9 = (bf16[96,3072]{1,0:T(8,128)(2,1)}, bf16[96,3072]{1,0:T(8,128)(2,1)S(1)}, u32[]{:S(2)}, u32[]{:S(2)}) collective-permute-start(bf16[96,3072]{1,0:T(8,128)(2,1)} %get-tuple-element.55), channel_id=1, source_target_pairs={{0,2},{1,3},{2,0},{3,1},{4,6},{5,7},{6,4},{7,5},{8,10},{9,11},{10,... | collective-permute-start | bytes 1769480 | tf_op jit(solution)/shard_map/ppermute | solution.py:34
  27.3 4.7 %collective-permute-start.1 = (f32[32,256]{1,0:T(8,128)S(1)}, f32[32,256]{1,0:T(8,128)S(1)}, u32[]{:S(2)}, u32[]{:S(2)}) collective-permute-start(f32[32,256]{1,0:T(8,128)S(1)} %get-tuple-element.58), channel_id=1, source_target_pairs={{0,8},{4,12},{8,0},{12,4},{16,24},{20,28},{24,16},{28,20},{1,9},{5... | collective-permute-start | bytes 98312 | tf_op jit(solution)/shard_map/ppermute | solution.py:34
  28.7 4.0 %collective-permute-start.2 = (f32[32,256]{1,0:T(8,128)S(1)}, f32[32,256]{1,0:T(8,128)S(1)}, u32[]{:S(2)}, u32[]{:S(2)}) collective-permute-start(f32[32,256]{1,0:T(8,128)S(1)} %get-tuple-element.57), channel_id=1, source_target_pairs={{0,16},{4,20},{8,24},{12,28},{16,0},{20,4},{24,8},{28,12},{1,17},{... | collective-permute-start | bytes 98312 | tf_op jit(solution)/shard_map/ppermute | solution.py:34
  31.0 4.6 %collective-permute-start.3 = (f32[32,256]{1,0:T(8,128)S(1)}, f32[32,256]{1,0:T(8,128)S(1)}, u32[]{:S(2)}, u32[]{:S(2)}) collective-permute-start(f32[32,256]{1,0:T(8,128)S(1)} %get-tuple-element.56), channel_id=1, source_target_pairs={{0,24},{4,28},{8,16},{12,20},{16,8},{20,12},{24,0},{28,4},{1,25},{... | collective-permute-start | bytes 98312 | tf_op jit(solution)/shard_map/ppermute | solution.py:34
  32.0 22.3 %collective-permute-start.10 = (bf16[96,3072]{1,0:T(8,128)(2,1)}, bf16[96,3072]{1,0:T(8,128)(2,1)S(1)}, u32[]{:S(2)}, u32[]{:S(2)}) collective-permute-start(bf16[96,3072]{1,0:T(8,128)(2,1)} %get-tuple-element.55), channel_id=1, source_target_pairs={{0,3},{1,2},{2,1},{3,0},{4,7},{5,6},{6,5},{7,4},{8,11},{9,10},{10,... | collective-permute-start | bytes 1769480 | tf_op jit(solution)/shard_map/ppermute | solution.py:34
  36.2 4.9 %collective-permute-start.6 = (f32[32,256]{1,0:T(8,128)}, f32[32,256]{1,0:T(8,128)}, u32[]{:S(2)}, u32[]{:S(2)}) collective-permute-start(f32[32,256]{1,0:T(8,128)} %fusion.10), channel_id=1, source_target_pairs={{0,24},{4,28},{8,16},{12,20},{16,8},{20,12},{24,0},{28,4},{1,25},{... | collective-permute-start | bytes 98312 | tf_op jit(solution)/shard_map/ppermute | solution.py:34
  36.6 7.8 %collective-permute-start.5 = (f32[32,256]{1,0:T(8,128)}, f32[32,256]{1,0:T(8,128)}, u32[]{:S(2)}, u32[]{:S(2)}) collective-permute-start(f32[32,256]{1,0:T(8,128)} %fusion.10), channel_id=1, source_target_pairs={{0,16},{4,20},{8,24},{12,28},{16,0},{20,4},{24,8},{28,12},{1,17},{... | collective-permute-start | bytes 98312 | tf_op jit(solution)/shard_map/ppermute | solution.py:34
  44.4 19.0 %collective-permute-start.12 = (bf16[32,3072]{1,0:T(8,128)(2,1)}, bf16[32,3072]{1,0:T(8,128)(2,1)S(1)}, u32[]{:S(2)}, u32[]{:S(2)}) collective-permute-start(bf16[32,3072]{1,0:T(8,128)(2,1)} %get-tuple-element.53), channel_id=1, source_target_pairs={{0,1},{1,0},{2,3},{3,2},{4,5},{5,4},{6,7},{7,6},{8,9},{9,8},{10,11... | collective-permute-start | bytes 589832 | tf_op jit(solution)/shard_map/ppermute | solution.py:34
  44.8 20.3 %collective-permute-start.24 = (bf16[64,3072]{1,0:T(8,128)(2,1)}, bf16[64,3072]{1,0:T(8,128)(2,1)S(1)}, u32[]{:S(2)}, u32[]{:S(2)}) collective-permute-start(bf16[64,3072]{1,0:T(8,128)(2,1)} %get-tuple-element.51), channel_id=1, source_target_pairs={{0,1},{1,0},{2,3},{3,2},{4,5},{5,4},{6,7},{7,6},{8,9},{9,8},{10,11... | collective-permute-start | bytes 1179656 | tf_op jit(solution)/shard_map/ppermute | solution.py:34
  46.7 5.8 %collective-permute-start.7 = (f32[4,32,256]{2,1,0:T(8,128)S(1)}, f32[4,32,256]{2,1,0:T(8,128)S(1)}, u32[]{:S(2)}, u32[]{:S(2)}) collective-permute-start(f32[4,32,256]{2,1,0:T(8,128)S(1)} %pad_maximum_fusion.near_ref), channel_id=1, source_target_pairs={{0,4},{4,0},{8,12},{12,8},{16,20},{20,16},{24,28},{28,24},{1,5},{5... | collective-permute-start | bytes 393224 | tf_op jit(solution)/shard_map/ppermute | solution.py:34
  52.5 15.8 %collective-permute-start.13 = (bf16[32,3072]{1,0:T(8,128)(2,1)}, bf16[32,3072]{1,0:T(8,128)(2,1)S(1)}, u32[]{:S(2)}, u32[]{:S(2)}) collective-permute-start(bf16[32,3072]{1,0:T(8,128)(2,1)} %get-tuple-element.53), channel_id=1, source_target_pairs={{0,2},{1,3},{2,0},{3,1},{4,6},{5,7},{6,4},{7,5},{8,10},{9,11},{10,... | collective-permute-start | bytes 589832 | tf_op jit(solution)/shard_map/ppermute | solution.py:34
  53.0 15.2 %collective-permute-start.14 = (bf16[32,3072]{1,0:T(8,128)(2,1)}, bf16[32,3072]{1,0:T(8,128)(2,1)S(1)}, u32[]{:S(2)}, u32[]{:S(2)}) collective-permute-start(bf16[32,3072]{1,0:T(8,128)(2,1)} %get-tuple-element.53), channel_id=1, source_target_pairs={{0,3},{1,2},{2,1},{3,0},{4,7},{5,6},{6,5},{7,4},{8,11},{9,10},{10,... | collective-permute-start | bytes 589832 | tf_op jit(solution)/shard_map/ppermute | solution.py:34
  54.2 38.1 %collective-permute-start.25 = (bf16[64,3072]{1,0:T(8,128)(2,1)}, bf16[64,3072]{1,0:T(8,128)(2,1)S(1)}, u32[]{:S(2)}, u32[]{:S(2)}) collective-permute-start(bf16[64,3072]{1,0:T(8,128)(2,1)} %get-tuple-element.51), channel_id=1, source_target_pairs={{0,2},{1,3},{2,0},{3,1},{4,6},{5,7},{6,4},{7,5},{8,10},{9,11},{10,... | collective-permute-start | bytes 1179656 | tf_op jit(solution)/shard_map/ppermute | solution.py:34
  63.4 4.8 %collective-permute-start.11 = (bf16[4,1,32,3072]{3,2,1,0:T(8,128)(2,1)S(1)}, bf16[4,1,32,3072]{3,2,1,0:T(8,128)(2,1)S(1)}, u32[]{:S(2)}, u32[]{:S(2)}) collective-permute-start(bf16[4,1,32,3072]{3,2,1,0:T(8,128)(2,1)S(1)} %get-tuple-element.31), channel_id=1, source_target_pairs={{0,4},{4,0},{8,12},{12,8},{16,20},{20,16},{24,28},{28,24},{1,5},{5... | collective-permute-start | bytes 2359304 | tf_op jit(solution)/shard_map/ppermute | solution.py:34
  65.0 36.8 %collective-permute-start.26 = (bf16[64,3072]{1,0:T(8,128)(2,1)S(1)}, bf16[64,3072]{1,0:T(8,128)(2,1)S(1)}, u32[]{:S(2)}, u32[]{:S(2)}) collective-permute-start(bf16[64,3072]{1,0:T(8,128)(2,1)S(1)} %copy-done.7), channel_id=1, source_target_pairs={{0,3},{1,2},{2,1},{3,0},{4,7},{5,6},{6,5},{7,4},{8,11},{9,10},{10,... | collective-permute-start | bytes 1179656 | tf_op jit(solution)/shard_map/ppermute | solution.py:34
  68.4 12.3 %collective-permute-start.15 = (bf16[32,3072]{1,0:T(8,128)(2,1)S(1)}, bf16[32,3072]{1,0:T(8,128)(2,1)S(1)}, u32[]{:S(2)}, u32[]{:S(2)}) collective-permute-start(bf16[32,3072]{1,0:T(8,128)(2,1)S(1)} %get-tuple-element.33), channel_id=1, source_target_pairs={{0,1},{1,0},{2,3},{3,2},{4,5},{5,4},{6,7},{7,6},{8,9},{9,8},{10,11... | collective-permute-start | bytes 589832 | tf_op jit(solution)/shard_map/ppermute | solution.py:34
  69.0 19.6 %collective-permute-start.16 = (bf16[32,3072]{1,0:T(8,128)(2,1)S(1)}, bf16[32,3072]{1,0:T(8,128)(2,1)S(1)}, u32[]{:S(2)}, u32[]{:S(2)}) collective-permute-start(bf16[32,3072]{1,0:T(8,128)(2,1)S(1)} %get-tuple-element.34), channel_id=1, source_target_pairs={{0,2},{1,3},{2,0},{3,1},{4,6},{5,7},{6,4},{7,5},{8,10},{9,11},{10,... | collective-permute-start | bytes 589832 | tf_op jit(solution)/shard_map/ppermute | solution.py:34
  69.6 19.1 %collective-permute-start.17 = (bf16[32,3072]{1,0:T(8,128)(2,1)S(1)}, bf16[32,3072]{1,0:T(8,128)(2,1)S(1)}, u32[]{:S(2)}, u32[]{:S(2)}) collective-permute-start(bf16[32,3072]{1,0:T(8,128)(2,1)S(1)} %get-tuple-element.35), channel_id=1, source_target_pairs={{0,3},{1,2},{2,1},{3,0},{4,7},{5,6},{6,5},{7,4},{8,11},{9,10},{10,... | collective-permute-start | bytes 589832 | tf_op jit(solution)/shard_map/ppermute | solution.py:34
  80.7 38.2 %collective-permute-start.31 = (bf16[256,96]{1,0:T(8,128)(2,1)S(1)}, bf16[256,96]{1,0:T(8,128)(2,1)S(1)}, u32[]{:S(2)}, u32[]{:S(2)}) collective-permute-start(bf16[256,96]{1,0:T(8,128)(2,1)S(1)} %constant_dynamic-slice_fusion), channel_id=1, source_target_pairs={{0,1},{1,0},{2,3},{3,2},{4,5},{5,4},{6,7},{7,6},{8,9},{9,8},{10,11... | collective-permute-start | bytes 147464 | tf_op jit(solution)/shard_map/ppermute | solution.py:34
  89.3 4.9 %collective-permute-start.20 = (bf16[32,768]{1,0:T(8,128)(2,1)S(1)}, bf16[32,768]{1,0:T(8,128)(2,1)S(1)}, u32[]{:S(2)}, u32[]{:S(2)}) collective-permute-start(bf16[32,768]{1,0:T(8,128)(2,1)S(1)} %get-tuple-element.39), channel_id=1, source_target_pairs={{0,24},{4,28},{8,16},{12,20},{16,8},{20,12},{24,0},{28,4},{1,25},{... | collective-permute-start | bytes 147464 | tf_op jit(solution)/shard_map/ppermute | solution.py:34
  89.6 7.7 %collective-permute-start.19 = (bf16[32,768]{1,0:T(8,128)(2,1)S(1)}, bf16[32,768]{1,0:T(8,128)(2,1)S(1)}, u32[]{:S(2)}, u32[]{:S(2)}) collective-permute-start(bf16[32,768]{1,0:T(8,128)(2,1)S(1)} %get-tuple-element.38), channel_id=1, source_target_pairs={{0,16},{4,20},{8,24},{12,28},{16,0},{20,4},{24,8},{28,12},{1,17},{... | collective-permute-start | bytes 147464 | tf_op jit(solution)/shard_map/ppermute | solution.py:34
  92.3 4.9 %collective-permute-start.18 = (bf16[32,768]{1,0:T(8,128)(2,1)S(1)}, bf16[32,768]{1,0:T(8,128)(2,1)S(1)}, u32[]{:S(2)}, u32[]{:S(2)}) collective-permute-start(bf16[32,768]{1,0:T(8,128)(2,1)S(1)} %get-tuple-element.37), channel_id=1, source_target_pairs={{0,8},{4,12},{8,0},{12,4},{16,24},{20,28},{24,16},{28,20},{1,9},{5... | collective-permute-start | bytes 147464 | tf_op jit(solution)/shard_map/ppermute | solution.py:34
  97.3 5.1 %collective-permute-start.21 = (bf16[32,768]{1,0:T(8,128)(2,1)S(1)}, bf16[32,768]{1,0:T(8,128)(2,1)S(1)}, u32[]{:S(2)}, u32[]{:S(2)}) collective-permute-start(bf16[32,768]{1,0:T(8,128)(2,1)S(1)} %add_convert_fusion.refs_0_), channel_id=1, source_target_pairs={{0,8},{4,12},{8,0},{12,4},{16,24},{20,28},{24,16},{28,20},{1,9},{5... | collective-permute-start | bytes 147464 | tf_op jit(solution)/shard_map/ppermute | solution.py:34
  97.4 5.1 %collective-permute-start.22 = (bf16[32,768]{1,0:T(8,128)(2,1)S(1)}, bf16[32,768]{1,0:T(8,128)(2,1)S(1)}, u32[]{:S(2)}, u32[]{:S(2)}) collective-permute-start(bf16[32,768]{1,0:T(8,128)(2,1)S(1)} %add_convert_fusion.refs_0_), channel_id=1, source_target_pairs={{0,16},{4,20},{8,24},{12,28},{16,0},{20,4},{24,8},{28,12},{1,17},{... | collective-permute-start | bytes 147464 | tf_op jit(solution)/shard_map/ppermute | solution.py:34
  97.6 5.4 %collective-permute-start.23 = (bf16[32,768]{1,0:T(8,128)(2,1)S(1)}, bf16[32,768]{1,0:T(8,128)(2,1)S(1)}, u32[]{:S(2)}, u32[]{:S(2)}) collective-permute-start(bf16[32,768]{1,0:T(8,128)(2,1)S(1)} %add_convert_fusion.refs_0_), channel_id=1, source_target_pairs={{0,24},{4,28},{8,16},{12,20},{16,8},{20,12},{24,0},{28,4},{1,25},{... | collective-permute-start | bytes 147464 | tf_op jit(solution)/shard_map/ppermute | solution.py:34
  101.8 17.1 %collective-permute-start.32 = (bf16[256,96]{1,0:T(8,128)(2,1)S(1)}, bf16[256,96]{1,0:T(8,128)(2,1)S(1)}, u32[]{:S(2)}, u32[]{:S(2)}) collective-permute-start(bf16[256,96]{1,0:T(8,128)(2,1)S(1)} %constant_dynamic-slice_fusion), channel_id=1, source_target_pairs={{0,2},{1,3},{2,0},{3,1},{4,6},{5,7},{6,4},{7,5},{8,10},{9,11},{10,... | collective-permute-start | bytes 147464 | tf_op jit(solution)/shard_map/ppermute | solution.py:34
  103.5 5.6 %collective-permute-start.29 = (bf16[32,3072]{1,0:T(8,128)(2,1)S(1)}, bf16[32,3072]{1,0:T(8,128)(2,1)S(1)}, u32[]{:S(2)}, u32[]{:S(2)}) collective-permute-start(bf16[32,3072]{1,0:T(8,128)(2,1)S(1)} %column_gather.1), channel_id=1, source_target_pairs={{0,3},{1,2},{2,1},{3,0},{4,7},{5,6},{6,5},{7,4},{8,11},{9,10},{10,... | collective-permute-start | bytes 589832 | tf_op jit(solution)/shard_map/ppermute | solution.py:34
  104.3 11.5 %collective-permute-start.28 = (bf16[32,3072]{1,0:T(8,128)(2,1)S(1)}, bf16[32,3072]{1,0:T(8,128)(2,1)S(1)}, u32[]{:S(2)}, u32[]{:S(2)}) collective-permute-start(bf16[32,3072]{1,0:T(8,128)(2,1)S(1)} %column_gather.1), channel_id=1, source_target_pairs={{0,2},{1,3},{2,0},{3,1},{4,6},{5,7},{6,4},{7,5},{8,10},{9,11},{10,... | collective-permute-start | bytes 589832 | tf_op jit(solution)/shard_map/ppermute | solution.py:34
  105.3 10.4 %collective-permute-start.27 = (bf16[32,3072]{1,0:T(8,128)(2,1)S(1)}, bf16[32,3072]{1,0:T(8,128)(2,1)S(1)}, u32[]{:S(2)}, u32[]{:S(2)}) collective-permute-start(bf16[32,3072]{1,0:T(8,128)(2,1)S(1)} %column_gather.1), channel_id=1, source_target_pairs={{0,1},{1,0},{2,3},{3,2},{4,5},{5,4},{6,7},{7,6},{8,9},{9,8},{10,11... | collective-permute-start | bytes 589832 | tf_op jit(solution)/shard_map/ppermute | solution.py:34
  109.1 9.8 %collective-permute-start.33 = (bf16[256,96]{1,0:T(8,128)(2,1)S(1)}, bf16[256,96]{1,0:T(8,128)(2,1)S(1)}, u32[]{:S(2)}, u32[]{:S(2)}) collective-permute-start(bf16[256,96]{1,0:T(8,128)(2,1)S(1)} %constant_dynamic-slice_fusion), channel_id=1, source_target_pairs={{0,3},{1,2},{2,1},{3,0},{4,7},{5,6},{6,5},{7,4},{8,11},{9,10},{10,... | collective-permute-start | bytes 147464 | tf_op jit(solution)/shard_map/ppermute | solution.py:34
  115.9 9.7 %collective-permute-start.30 = (bf16[4,1,32,3072]{3,2,1,0:T(8,128)(2,1)S(1)}, bf16[4,1,32,3072]{3,2,1,0:T(8,128)(2,1)S(1)}, u32[]{:S(2)}, u32[]{:S(2)}) collective-permute-start(bf16[4,1,32,3072]{3,2,1,0:T(8,128)(2,1)S(1)} %maximum_bitcast_fusion.right_ref.near_ref), channel_id=1, source_target_pairs={{0,4},{4,0},{8,12},{12,8},{16,20},{20,16},{24,28},{28,24},{1,5},{5... | collective-permute-start | bytes 2359304 | tf_op jit(solution)/shard_map/ppermute | solution.py:34
  (16 other events, 356.6 us)

commit v3 on v2

v3 whole, which is shorter than its diff:
```python
import functools

import jax
import jax.numpy as jnp
from jax import lax
from jax.experimental import pallas as pl
from jax.experimental.pallas import tpu as pltpu
from jax.sharding import PartitionSpec as P

CORES = 2
LANES = 128
VMEM_LIMIT = 24 * 1024 * 1024
F32 = jnp.float32
BF16 = jnp.bfloat16


def params():
    return pltpu.CompilerParams(vmem_limit_bytes=VMEM_LIMIT)


def cost(bytes_accessed=1000):
    return pl.CostEstimate(flops=1000, bytes_accessed=bytes_accessed, transcendentals=0)


def tree_sum(terms):
    while len(terms) > 1:
        terms = [terms[i] + terms[i + 1] for i in range(0, len(terms), 2)]
    return terms[0]


def exchange(x, axis, distance):
    size = lax.axis_size(axis)
    return lax.ppermute(x, axis, [(i, i ^ distance) for i in range(size)])


def left_kernel(pos, g_ref, f_ref, q_ref, vec_ref, comp_ref, near_ref, far_ref, total):
    k = pl.program_id(0)
    rows = g_ref.shape[2]
    rank = q_ref.shape[1]
    group = LANES // rank
    near, piece, _ = near_ref.shape

    @pl.when(k == 0)
    def _():
        total[...] = jnp.zeros(total.shape, F32)
        width, nvec = total.shape[1], vec_ref.shape[1]
        for i, first in enumerate(range(0, nvec, width)):
            count = min(width, nvec - first)
            total[rows + i : rows + i + 1, :count] = vec_ref[:, first : first + count]

    comp = g_ref[0, 0] + f_ref[0, 0]
    comp_ref[0] = comp
    q = q_ref[0]
    wide = jnp.concatenate([q] * group, axis=0)
    member = lax.broadcasted_iota(jnp.int32, wide.shape, 0) // rank
    wide = jnp.where(member == k % group, wide, jnp.zeros_like(wide))
    terms = lax.dot_general(comp, wide, (((1,), (1,)), ((), ())), preferred_element_type=F32)
    cols = pl.ds(pl.multiple_of((k // group) * LANES, LANES), LANES)
    total[:rows, cols] += terms

    @pl.when(k == pl.num_programs(0) - 1)
    def _():
        for s in range(near):
            for out, slot in ((near_ref, s), (far_ref, s + near)):
                out[s] = total[pl.ds(pl.multiple_of((slot ^ pos[3]) * piece, piece), piece), :]


def left_terms(pos, gradients, feedback, right_t, vec, n_z):
    _, nmat, rows, n = gradients.shape
    rank = right_t.shape[1]
    width = nmat * rank
    total = rows + -(-vec.shape[1] // width)
    total += -total % (8 * CORES * n_z)
    pieces = jax.ShapeDtypeStruct((n_z, total // (CORES * n_z), width), F32)
    return pl.pallas_call(
        left_kernel,
        grid_spec=pltpu.PrefetchScalarGridSpec(
            num_scalar_prefetch=1,
            grid=(nmat,),
            in_specs=[
                pl.BlockSpec((1, 1, rows, n), lambda k, pos: (0, k, 0, 0)),
                pl.BlockSpec((1, 1, rows, n), lambda k, pos: (0, k, 0, 0)),
                pl.BlockSpec((1, rank, n), lambda k, pos: (k, 0, 0)),
                pl.BlockSpec(vec.shape, lambda k, pos: (0, 0)),
            ],
            out_specs=[
                pl.BlockSpec((1, rows, n), lambda k, pos: (k, 0, 0)),
                pl.BlockSpec(pieces.shape, lambda k, pos: (0, 0, 0)),
                pl.BlockSpec(pieces.shape, lambda k, pos: (0, 0, 0)),
            ],
            scratch_shapes=[pltpu.VMEM((total, width), F32)],
        ),
        out_shape=[jax.ShapeDtypeStruct((nmat, rows, n), BF16), pieces, pieces],
        compiler_params=params(),
        cost_estimate=cost(),
        name="left_terms",
    )(pos, gradients, feedback, right_t, vec)


def send_kernel(half, pos, near_ref, far_ref, gram_ref, comp_ref, *refs):
    send_ref, lt_ref, vec_ref, left, gram = refs[-5:]
    t = pl.program_id(0)
    rows = comp_ref.shape[1]
    rank = gram_ref.shape[1]

    @pl.when(t == 0)
    def _():
        near, piece, _ = near_ref.shape
        for s in range(near):
            for part, slot in ((near_ref, s), (far_ref, s + near)):
                left[pl.ds(pl.multiple_of((slot ^ pos[3]) * piece, piece), piece), :] = part[s]
        vec_ref[...] = left[rows:, :]
        gram[...] = jnp.zeros(gram.shape, F32)
        for i in range(gram_ref.shape[0]):
            gram[i * rank : (i + 1) * rank, i * rank : (i + 1) * rank] = gram_ref[i]
        hat = jnp.dot(
            left[:rows, :], gram[...], precision=lax.Precision.HIGHEST, preferred_element_type=F32
        )
        lt_ref[...] = hat.T.astype(BF16)

    right_rows(half, pos, lt_ref, comp_ref, send_ref)


def right_rows(start, pos, lt_ref, comp_ref, out_ref):
    upm, unit = out_ref.shape[1], out_ref.shape[2]
    k = (pl.program_id(0) + start) ^ pos[0]
    rows = pl.ds(pl.multiple_of(k * upm * unit, upm * unit), upm * unit)
    terms = jnp.dot(lt_ref[rows, :], comp_ref[0], preferred_element_type=F32)
    for i in range(upm):
        out_ref[0, i ^ pos[1]] = terms[i * unit : (i + 1) * unit].astype(out_ref.dtype)


def keep_kernel(pos, lt_ref, comp_ref, keep_ref):
    right_rows(0, pos, lt_ref, comp_ref, keep_ref)


def right_terms(pos, near, far, gram, comp, upm, after):
    nmat, rows, n = comp.shape
    rank = gram.shape[1]
    width = nmat * rank
    half = nmat // CORES
    total = CORES * near.shape[0] * near.shape[1]
    shape = (half, upm, rank // upm, n)
    vmem = pl.BlockSpec(memory_space=pltpu.VMEM)
    out = pl.BlockSpec((1,) + shape[1:], lambda t, pos: (t, 0, 0, 0))
    send, lt, vec = pl.pallas_call(
        functools.partial(send_kernel, half),
        grid_spec=pltpu.PrefetchScalarGridSpec(
            num_scalar_prefetch=1,
            grid=(half,),
            in_specs=[
                vmem,
                vmem,
                vmem,
                pl.BlockSpec((1, rows, n), lambda t, pos: ((t + half) ^ pos[0], 0, 0)),
            ]
            + [pl.BlockSpec(memory_space=pl.ANY)] * len(after),
            out_specs=[out, vmem, vmem],
            scratch_shapes=[pltpu.VMEM((total, width), F32), pltpu.VMEM((width, width), F32)],
        ),
        out_shape=[
            jax.ShapeDtypeStruct(shape, BF16),
            jax.ShapeDtypeStruct((width, rows), BF16),
            jax.ShapeDtypeStruct((total - rows, width), F32),
        ],
        compiler_params=params(),
        cost_estimate=cost(),
        name="right_send",
    )(pos, near, far, gram, comp, *after)
    keep = pl.pallas_call(
        keep_kernel,
        grid_spec=pltpu.PrefetchScalarGridSpec(
            num_scalar_prefetch=1,
            grid=(half,),
            in_specs=[vmem, pl.BlockSpec((1, rows, n), lambda t, pos: (t ^ pos[0], 0, 0))],
            out_specs=out,
        ),
        out_shape=jax.ShapeDtypeStruct(shape, F32),
        compiler_params=params(),
        cost_estimate=cost(4 * nmat * rows * n),
        name="right_keep",
    )(pos, lt, comp)
    return send, keep, lt, vec


def chip_kernel(pos, keep_ref, recv_ref, lt_ref, *refs):
    upm = keep_ref.shape[1]
    for d, out in enumerate(refs[:-1]):
        j, i = d // upm, d % upm
        out[...] = (keep_ref[j, i] + recv_ref[j, i].astype(F32)).astype(out.dtype)
    strip_ref = refs[-1]
    count = strip_ref.shape[1]
    strip = lt_ref[:, :count]
    for i in range(1, lt_ref.shape[1] // count):
        strip = jnp.where(pos[6] == i, lt_ref[:, i * count : (i + 1) * count], strip)
    strip_ref[...] = strip


def chip_sum(pos, keep, recv, lt, replica_rows):
    half, upm, unit, n = keep.shape
    vmem = pl.BlockSpec(memory_space=pltpu.VMEM)
    outs = [jax.ShapeDtypeStruct((unit, n), BF16 if d else F32) for d in range(half * upm)]
    outs.append(jax.ShapeDtypeStruct((lt.shape[0], replica_rows), BF16))
    return pl.pallas_call(
        chip_kernel,
        grid_spec=pltpu.PrefetchScalarGridSpec(
            num_scalar_prefetch=1,
            grid=(1,),
            in_specs=[vmem] * 3,
            out_specs=[vmem] * len(outs),
        ),
        out_shape=outs,
        compiler_params=params(),
        cost_estimate=cost(),
        name="chip_sum",
    )(pos, keep, recv, lt)


def column_kernel(n_z, pos, *refs):
    out = refs[-1]
    cols = out.shape[1] // n_z
    for d in range(n_z):
        out[:, pl.ds(pl.multiple_of((pos[4] ^ d) * cols, cols), cols)] = refs[d][...]


def column_gather(pos, parts, after):
    unit, cols = parts[0].shape
    vmem = pl.BlockSpec(memory_space=pltpu.VMEM)
    return pl.pallas_call(
        functools.partial(column_kernel, len(parts)),
        grid_spec=pltpu.PrefetchScalarGridSpec(
            num_scalar_prefetch=1,
            grid=(1,),
            in_specs=[vmem] * len(parts) + [pl.BlockSpec(memory_space=pl.ANY)] * len(after),
            out_specs=vmem,
        ),
        out_shape=jax.ShapeDtypeStruct((unit, cols * len(parts)), BF16),
        compiler_params=params(),
        cost_estimate=cost(),
        name="column_gather",
    )(pos, *parts, *after)


def plane_kernel(count, cuts, pos, *refs):
    terms, wholes, outs = refs[:count], refs[count : count + len(cuts)], refs[count + len(cuts) + 1 :]
    cols = outs[0].shape[1]
    n_z = len(outs) - len(cuts)
    for d, out in enumerate(outs[:n_z]):
        block = pl.ds(pl.multiple_of((pos[4] ^ d) * cols, cols), cols)
        out[...] = tree_sum([term[:, block].astype(F32) for term in terms]).astype(out.dtype)
    for whole, out, first in zip(wholes, outs[n_z:], cuts):
        out[...] = whole[first : first + out.shape[0]]


def plane_sum(pos, terms, n_z, wholes, cuts, after):
    unit, n = terms[0].shape
    cols = n // n_z
    outs = [jax.ShapeDtypeStruct((unit, cols), BF16 if d else F32) for d in range(n_z)]
    outs += [jax.ShapeDtypeStruct((x.shape[0] // 2,) + x.shape[1:], x.dtype) for x in wholes]
    vmem = pl.BlockSpec(memory_space=pltpu.VMEM)
    return pl.pallas_call(
        functools.partial(plane_kernel, len(terms), cuts),
        grid_spec=pltpu.PrefetchScalarGridSpec(
            num_scalar_prefetch=1,
            grid=(1,),
            in_specs=[vmem] * (len(terms) + len(wholes)) + [pl.BlockSpec(memory_space=pl.ANY)],
            out_specs=[vmem] * len(outs),
        ),
        out_shape=outs,
        compiler_params=params(),
        cost_estimate=cost(),
        name="plane_sum",
    )(pos, *terms, *wholes, after)


def matrix_of(right_ref, slot, sub):
    upm = right_ref.shape[1]
    parts = [right_ref[slot, i ^ sub] for i in range(upm)]
    return parts[0] if upm == 1 else jnp.concatenate(parts, axis=0)


def product(lt, right):
    return lax.dot_general(lt, right, (((0,), (0,)), ((), ())), preferred_element_type=F32)


def rank_of(owners, k, nmat):
    count = jnp.int32(0)
    for j in range(nmat):
        count += jnp.where((owners[j] == owners[k]) & (j < k), 1, 0)
    return count


def outputs_kernel(start, places, pos, owners, comp_ref, right_ref, lt_ref, ltr_ref, *refs):
    n_base = len({a for a, _ in places.values()})
    bases, (feedback_ref, weights_ref, held, sem) = refs[:n_base], refs[-4:]
    j = pl.program_id(0)
    rank = right_ref.shape[1] * right_ref.shape[2]
    capacity = max(c for _, c in places) + 1

    def fetch(step, start_it):
        k = (step + start) ^ pos[0]
        slot = (owners[k] ^ pos[5]) * capacity + rank_of(owners, k, owners.shape[0])
        buffer = lax.rem(step, 2)
        if not start_it:
            pltpu.make_async_copy(bases[0].at[0], held.at[buffer], sem.at[buffer]).wait()
            return
        for (d, c), (a, row) in places.items():

            @pl.when(slot == d * capacity + c)
            def _():
                pltpu.make_async_copy(bases[a].at[row], held.at[buffer], sem.at[buffer]).start()

    @pl.when(j == 0)
    def _():
        fetch(j, True)

    @pl.when(j + 1 < pl.num_programs(0))
    def _():
        fetch(j + 1, True)

    right = matrix_of(right_ref, j, pos[1])
    k = (j + start) ^ pos[0]
    rows = pl.ds(pl.multiple_of(k * rank, rank), rank)
    feedback_ref[0, 0] = (comp_ref[0].astype(F32) - product(lt_ref[rows, :], right)).astype(BF16)
    fetch(j, False)
    base = held[lax.rem(j, 2)].astype(F32)
    weights_ref[0] = (base - 0.1 * product(ltr_ref[rows, :], right)).astype(BF16)


def outputs(pos, owners, start, comp, right, lt, ltr, bases, places, earlier):
    nmat, rows, n = comp.shape
    half = right.shape[0]
    replica_rows = bases[0].shape[1]

    def matrix(j, pos):
        return (j + start) ^ pos[0]

    any_spec = pl.BlockSpec(memory_space=pl.ANY)
    vmem = pl.BlockSpec(memory_space=pltpu.VMEM)
    return pl.pallas_call(
        functools.partial(outputs_kernel, start, places),
        grid_spec=pltpu.PrefetchScalarGridSpec(
            num_scalar_prefetch=2,
            grid=(half,),
            in_specs=[pl.BlockSpec((1, rows, n), lambda j, pos, own: (matrix(j, pos), 0, 0))]
            + [vmem] * 3
            + [any_spec] * (len(bases) + len(earlier)),
            out_specs=[
                pl.BlockSpec((1, 1, rows, n), lambda j, pos, own: (0, matrix(j, pos), 0, 0)),
                pl.BlockSpec((1, replica_rows, n), lambda j, pos, own: (matrix(j, pos), 0, 0)),
            ],
            scratch_shapes=[
                pltpu.VMEM((2, replica_rows, n), BF16),
                pltpu.SemaphoreType.DMA((2,)),
            ],
        ),
        out_shape=[
            jax.ShapeDtypeStruct((1, nmat, rows, n), BF16),
            jax.ShapeDtypeStruct((nmat, replica_rows, n), BF16),
        ],
        input_output_aliases={6 + len(bases) + i: i for i in range(len(earlier))},
        compiler_params=params(),
        cost_estimate=cost(),
        name="outputs",
    )(pos, owners, comp, right, lt, ltr, *bases, *earlier)


def owned_kernel(pos, owners, momentum_ref, master_ref, near_ref, far_ref, ltr_ref, new_momentum_ref, new_master_ref):
    c = pl.program_id(0)
    nmat = owners.shape[0]
    half = near_ref.shape[0]
    rank = near_ref.shape[1] * near_ref.shape[2]
    matrix = jnp.int32(-1)
    for k in range(nmat):
        matrix = jnp.where((owners[k] == pos[5]) & (rank_of(owners, k, nmat) == c), k, matrix)
    safe = jnp.maximum(matrix, 0)
    slot = safe ^ pos[0]
    inner = lax.rem(slot, half)
    right = jnp.where(slot < half, matrix_of(near_ref, inner, pos[1]), matrix_of(far_ref, inner, pos[1]))
    lt = ltr_ref[pl.ds(pl.multiple_of(safe * rank, rank), rank), :]
    approx = jnp.where(matrix >= 0, product(lt, right), 0.0)
    momentum = 0.9 * momentum_ref[0, 0] + approx
    new_momentum_ref[0, 0] = momentum
    new_master_ref[0, 0] = master_ref[0, 0] - 0.1 * momentum


def owned(pos, owners, momentum, master, near, far, ltr):
    _, capacity, rows, n = momentum.shape
    state = pl.BlockSpec((1, 1, rows, n), lambda c, pos, own: (0, c, 0, 0))
    vmem = pl.BlockSpec(memory_space=pltpu.VMEM)
    return pl.pallas_call(
        owned_kernel,
        grid_spec=pltpu.PrefetchScalarGridSpec(
            num_scalar_prefetch=2,
            grid=(capacity,),
            in_specs=[state, state, vmem, vmem, vmem],
            out_specs=[state, state],
        ),
        out_shape=[jax.ShapeDtypeStruct(momentum.shape, F32)] * 2,
        compiler_params=params(),
        cost_estimate=cost(),
        name="owned",
    )(pos, owners, momentum, master, near, far, ltr)


def base_kernel(momentum_ref, master_ref, out_ref):
    out_ref[0] = (master_ref[0, 0] - 0.09 * momentum_ref[0, 0]).astype(BF16)


def base_of(momentum, master):
    _, capacity, rows, n = momentum.shape
    cuts = 2
    state = pl.BlockSpec((1, 1, rows, n // cuts), lambda c, i: (0, c, 0, i))
    return pl.pallas_call(
        base_kernel,
        grid=(capacity, cuts),
        in_specs=[state, state],
        out_specs=pl.BlockSpec((1, rows, n // cuts), lambda c, i: (c, 0, i)),
        out_shape=jax.ShapeDtypeStruct((capacity, rows, n), BF16),
        compiler_params=params(),
        cost_estimate=cost(),
        name="base",
    )(momentum, master)


def stack_kernel(*refs):
    out = refs[-1]
    for i, part in enumerate(refs[:-1]):
        out[i] = part[...]


def stack(parts):
    vmem = pl.BlockSpec(memory_space=pltpu.VMEM)
    return pl.pallas_call(
        stack_kernel,
        in_specs=[vmem] * len(parts),
        out_specs=vmem,
        out_shape=jax.ShapeDtypeStruct((len(parts),) + parts[0].shape, parts[0].dtype),
        compiler_params=params(),
        cost_estimate=cost(),
        name="stack",
    )(*parts)


def per_device(
    gradients,
    feedback,
    right_init,
    gram_root,
    owners,
    momentum,
    master_weights,
    vector_grads,
    vector_momentum,
    vector_params,
):
    nmat, rows, n = gradients.shape[1:]
    rank = right_init.shape[2]
    n_mp = lax.axis_size("mp")
    n_z = lax.axis_size("replica") // CORES
    capacity, replica_rows = momentum.shape[1:3]
    p = lax.axis_index("mp")
    r = lax.axis_index("replica")
    core, z = r % CORES, r // CORES
    upm = CORES * n_mp // nmat
    half = nmat // CORES
    code = core * n_mp + p

    pos = jnp.stack([code // upm, code % upm, core, core * n_z + z, z, p, r * replica_rows % rows // replica_rows]).astype(jnp.int32)
    in_hbm = lambda x: pltpu.with_memory_space_constraint(x, pltpu.HBM)
    momentum, master_weights = in_hbm(momentum), in_hbm(master_weights)

    base = base_of(momentum, master_weights)
    bases = [base] + [exchange(base, "mp", d) for d in range(1, 3 if n_mp == 4 else n_mp)]
    places = {(d, c): (d, c) for d in range(len(bases)) for c in range(capacity)}
    early, cuts = bases[1:], []
    if n_mp == 4:
        cut = capacity // 2
        cuts = [0, cut]
        for c in range(capacity):
            places[3, c] = (3, c) if c < cut else (4, c - cut)

    nvec = vector_grads.shape[1]
    comp, near, far = left_terms(
        pos,
        in_hbm(gradients),
        in_hbm(feedback),
        in_hbm(jnp.swapaxes(right_init, 1, 2)),
        vector_grads,
        n_z,
    )
    chip = near + exchange(far, "replica", 1)
    piece = tree_sum([chip[0]] + [exchange(chip[d], "replica", CORES * d) for d in range(1, n_z)])
    near = stack([piece] + [exchange(piece, "replica", CORES * d) for d in range(1, n_z)])
    far = exchange(near, "replica", 1)

    send, keep, lt, vector_rows = right_terms(pos, near, far, gram_root, comp, upm, early)
    vector_total = vector_rows.reshape(-1)[:nvec]
    *chip, strip = chip_sum(pos, keep, exchange(send, "replica", 1), lt, replica_rows)
    plane = [chip[0]] + [exchange(chip[d], "mp", d) for d in range(1, n_mp)]
    strips = jnp.stack([strip] + [exchange(strip, "mp", d) for d in range(1, n_mp)])
    ltr = lax.dynamic_index_in_dim(strips, (r * replica_rows // rows) ^ p, 0, keepdims=False)
    final = plane_sum(pos, plane, n_z, early[: len(cuts)], cuts, ltr)
    late = [exchange(part, "mp", 2 - i) for i, part in enumerate(final[n_z:])]
    bases += late
    final = [final[0]] + [exchange(final[d], "replica", CORES * d).astype(F32) for d in range(1, n_z)]
    final = tree_sum(final).astype(BF16)

    final = [final] + [exchange(final, "replica", CORES * d) for d in range(1, n_z)]
    whole = column_gather(pos, final, late)
    near = stack([whole] + [exchange(whole, "mp", d) for d in range(1, n_mp)])
    near = near.reshape(half, upm, rank // upm, n)
    far = exchange(near, "replica", 1)

    done = outputs(pos, owners, 0, comp, near, lt, ltr, bases, places, ())
    new_feedback, new_weights = outputs(pos, owners, half, comp, far, lt, ltr, bases, places, done)
    new_momentum, new_master = owned(pos, owners, momentum, master_weights, near, far, ltr)

    new_vector_momentum = 0.9 * vector_momentum + vector_total
    new_vector_params = vector_params - 0.1 * new_vector_momentum
    return new_feedback, new_momentum, new_master, new_weights, new_vector_momentum, new_vector_params


def solution(mesh):
    return jax.shard_map(
        per_device,
        mesh=mesh,
        in_specs=(
            P("replica", None, "mp", None),
            P("replica", None, "mp", None),
            P(),
            P(),
            P(),
            P("mp", None, "replica", None),
            P("mp", None, "replica", None),
            P("replica", "mp"),
            P("mp"),
            P("mp"),
        ),
        out_specs=(
            P("replica", None, "mp", None),
            P("mp", None, "replica", None),
            P("mp", None, "replica", None),
            P(None, "replica", None),
            P("mp"),
            P("mp"),
        ),
        check_vma=False,
    )
```

time: 137 us -> 116 us (0.85); the launches traced: 135 us -> 116 us
  local copies, waits for them, and re-layouts: 20.5 us -> 5.59 us
  other arithmetic: 10.4 us -> 1.58 us
  Pallas kernels: 32 us -> 40.3 us
  waiting for transfers between devices: 36.2 us -> 28.7 us
  starting transfers between devices: 35.2 us -> 39.3 us
    unnamed x37 -> x29, local copies, waits for them, and re-layouts: 17.1 us -> 5.5 us
    pallas_call x6 -> x10, Pallas kernels: 20.8 us -> 29.3 us  [the longest x2 12.6 us: outputs(): pl.pallas_call(functools.partial(outputs_kernel, start, places), grid_spe...]
    ppermute x34 -> x29, waiting for transfers between devices: 36.2 us -> 28.7 us  [exchange(): return lax.ppermute(x, axis, [(i, i ^ distance) for i in range(size)])]
    unnamed x5 -> x1, other arithmetic: 5.35 us -> 0.01 us
    ppermute x34 -> x29, starting transfers between devices: 35.2 us -> 39.3 us  [exchange(): return lax.ppermute(x, axis, [(i, i ^ distance) for i in range(size)])]
    select_n x1 -> x0, local copies, waits for them, and re-layouts: 2.23 us -> none  [per_device(): gram = jnp.where(block, gram_root[:, :, None, :], 0.0).reshape(width, width)]
  transfers between devices with their start and end apart: 34 -> 29, of which waited for: 11 -> 15; matrix products, arithmetic and copies ran while one was open for 13% -> 1% of each run, Pallas kernels for 17% -> 17%
where the time goes in v3:
time: 116 us
  Pallas kernels  40.3 us (35%)
  starting transfers between devices  39.3 us (34%)
  waiting for transfers between devices  28.7 us (25%)
  local copies, waits for them, and re-layouts  5.59 us (5%)
  other arithmetic  1.58 us (1%)
    ppermute x29, starting transfers between devices, exchange(): return lax.ppermute(x, axis, [(i, i ^ distance) for i in range(size)])  39.3 us
    ppermute x29, waiting for transfers between devices, exchange(): return lax.ppermute(x, axis, [(i, i ^ distance) for i in range(size)])  28.7 us
    pallas_call x2, Pallas kernels, outputs(): pl.pallas_call(functools.partial(outputs_kernel, start, places), grid_spe...  12.6 us
    pallas_call x1, Pallas kernels, left_terms(): pl.pallas_call(left_kernel, grid_spec=pltpu.PrefetchScalarGridSpec(num_sc...  10.5 us
    unnamed x29, local copies, waits for them, and re-layouts  5.5 us
    pallas_call x1, Pallas kernels, owned(): pl.pallas_call(owned_kernel, grid_spec=pltpu.PrefetchScalarGridSpec(num_s...  4.82 us
    pallas_call x1, Pallas kernels, base_of(): pl.pallas_call(base_kernel, grid=(capacity, cuts), in_specs=[state, state...  4.16 us
    pallas_call x1, Pallas kernels, right_terms(): pl.pallas_call(functools.partial(send_kernel, half), grid_spec=pltpu.Pref...  2.38 us
  transfers between devices with their start and end apart: 29, of which 15 were waited for; matrix products, arithmetic and copies ran while one was open for 1% of the time, Pallas kernels for 17%

profile of v3, /device:TPU:1, one launch (start us, length us, event | category | flops | bytes accessed | tf_op | source)
XLA Modules:
  0.0 116.4 jit_solution(371942233047779743)
XLA Ops:
  0.6 4.2 %base.1.refs_0_ = bf16[2,96,3072]{2,1,0:T(8,128)(2,1)} custom-call(f32[1,2,96,3072]{3,2,1,0:T(8,128)} %momentum_ref.3, f32[1,2,96,3072]{3,2,1,0:T(8,128)} %master_ref.3), custom_call_target="tpu_custom_call" | custom-call | flops 1000 | bytes 1000 | tf_op jit(solution)/shard_map/base/pallas_call | solution.py:414
  4.8 2.0 %collective-permute-start.8 = (bf16[2,96,3072]{2,1,0:T(8,128)(2,1)}, bf16[2,96,3072]{2,1,0:T(8,128)(2,1)S(1)}, u32[]{:S(2)}, u32[]{:S(2)}) collective-permute-start(bf16[2,96,3072]{2,1,0:T(8,128)(2,1)} %base.1.refs_0_), channel_id=1, source_target_pairs={{0,1},{1,0},{2,3},{3,2},{4,5},{5,4},{6,7},{7,6},{8,9},{9,8},{10,11... | collective-permute-start | bytes 3538952 | tf_op jit(solution)/shard_map/ppermute | solution.py:33
  8.2 10.5 %left_terms.1 = (bf16[8,192,3072]{2,1,0:T(8,128)(2,1)S(1)}, f32[4,32,256]{2,1,0:T(8,128)S(1)}, f32[4,32,256]{2,1,0:T(8,128)S(1)}) custom-call(s32[7]{0:T(128)S(1)} %stack.45.pos, bf16[1,8,192,3072]{3,2,1,0:T(8,128)(2,1)} %g_ref.1, bf16[1,8,192,3072]{3,2,1,0:T(8,128)(2,1)} %f_ref.1, bf16[8,32,3072]{2,1,0:T(8,128)(2,1)} %bitcast.34, f32[1,2688]{1,0:T(1,128)S(1)} %copy-done.7), custom_call_target="tpu_custom_call" | custom-call | flops 1000 | bytes 1000 | tf_op jit(solution)/shard_map/left_terms/pallas_call | solution.py:75
  18.7 1.3 %collective-permute-start = (f32[4,32,256]{2,1,0:T(8,128)S(1)}, f32[4,32,256]{2,1,0:T(8,128)S(1)}, u32[]{:S(2)}, u32[]{:S(2)}) collective-permute-start(f32[4,32,256]{2,1,0:T(8,128)S(1)} %get-tuple-element.31), channel_id=1, source_target_pairs={{0,4},{4,0},{8,12},{12,8},{16,20},{20,16},{24,28},{28,24},{1,5},{5... | collective-permute-start | bytes 393224 | tf_op jit(solution)/shard_map/ppermute | solution.py:33
  21.0 1.4 %collective-permute-start.1 = (f32[32,256]{1,0:T(8,128)S(1)}, f32[32,256]{1,0:T(8,128)S(1)}, u32[]{:S(2)}, u32[]{:S(2)}) collective-permute-start(f32[32,256]{1,0:T(8,128)S(1)} %get-tuple-element.56), channel_id=1, source_target_pairs={{0,8},{4,12},{8,0},{12,4},{16,24},{20,28},{24,16},{28,20},{1,9},{5... | collective-permute-start | bytes 98312 | tf_op jit(solution)/shard_map/ppermute | solution.py:33
  22.4 2.3 %collective-permute-start.2 = (f32[32,256]{1,0:T(8,128)S(1)}, f32[32,256]{1,0:T(8,128)S(1)}, u32[]{:S(2)}, u32[]{:S(2)}) collective-permute-start(f32[32,256]{1,0:T(8,128)S(1)} %get-tuple-element.55), channel_id=1, source_target_pairs={{0,16},{4,20},{8,24},{12,28},{16,0},{20,4},{24,8},{28,12},{1,17},{... | collective-permute-start | bytes 98312 | tf_op jit(solution)/shard_map/ppermute | solution.py:33
  24.7 1.7 %collective-permute-done.2 = f32[32,256]{1,0:T(8,128)S(1)} collective-permute-done((f32[32,256]{1,0:T(8,128)S(1)}, f32[32,256]{1,0:T(8,128)S(1)}, u32[]{:S(2)}, u32[]{:S(2)}) %collective-permute-start.2) | collective-permute-done | bytes 32800 | tf_op jit(solution)/shard_map/ppermute | solution.py:33
  26.4 2.9 %collective-permute-done.3 = f32[32,256]{1,0:T(8,128)S(1)} collective-permute-done((f32[32,256]{1,0:T(8,128)S(1)}, f32[32,256]{1,0:T(8,128)S(1)}, u32[]{:S(2)}, u32[]{:S(2)}) %collective-permute-start.3) | collective-permute-done | bytes 32800 | tf_op jit(solution)/shard_map/ppermute | solution.py:33
  30.0 2.8 %collective-permute-start.6 = (f32[32,256]{1,0:T(8,128)S(1)}, f32[32,256]{1,0:T(8,128)S(1)}, u32[]{:S(2)}, u32[]{:S(2)}) collective-permute-start(f32[32,256]{1,0:T(8,128)S(1)} %fusion.5.refs_0_), channel_id=1, source_target_pairs={{0,24},{4,28},{8,16},{12,20},{16,8},{20,12},{24,0},{28,4},{1,25},{... | collective-permute-start | bytes 98312 | tf_op jit(solution)/shard_map/ppermute | solution.py:33
  33.1 1.6 %collective-permute-done.6.refs_3_ = f32[32,256]{1,0:T(8,128)S(1)} collective-permute-done((f32[32,256]{1,0:T(8,128)S(1)}, f32[32,256]{1,0:T(8,128)S(1)}, u32[]{:S(2)}, u32[]{:S(2)}) %collective-permute-start.6) | collective-permute-done | bytes 32800 | tf_op jit(solution)/shard_map/ppermute | solution.py:33
  34.6 3.5 %collective-permute-start.7 = (f32[4,32,256]{2,1,0:T(8,128)S(1)}, f32[4,32,256]{2,1,0:T(8,128)S(1)}, u32[]{:S(2)}, u32[]{:S(2)}) collective-permute-start(f32[4,32,256]{2,1,0:T(8,128)S(1)} %stack.51.near_ref), channel_id=1, source_target_pairs={{0,4},{4,0},{8,12},{12,8},{16,20},{20,16},{24,28},{28,24},{1,5},{5... | collective-permute-start | bytes 393224 | tf_op jit(solution)/shard_map/ppermute | solution.py:33
  39.2 2.4 %right_send.1 = (bf16[4,1,32,3072]{3,2,1,0:T(8,128)(2,1)S(1)}, bf16[256,192]{1,0:T(8,128)(2,1)S(1)}, f32[64,256]{1,0:T(8,128)S(1)}) custom-call(s32[7]{0:T(128)S(1)} %stack.45.pos, f32[4,32,256]{2,1,0:T(8,128)S(1)} %stack.51.near_ref, f32[4,32,256]{2,1,0:T(8,128)S(1)} %collective-permute-done.7.far_ref, f32[8,32,32]{2,1,0:T(8,128)S(1)} %copy-done.4, ...), custom_call_target="tpu_custom_call" | custom-call | flops 1000 | bytes 1000 | tf_op jit(solution)/shard_map/right_send/pallas_call | solution.py:146
  42.0 1.9 %right_keep.1.keep_ref = f32[4,1,32,3072]{3,2,1,0:T(8,128)S(1)} custom-call(s32[7]{0:T(128)S(1)} %stack.45.pos, bf16[256,192]{1,0:T(8,128)(2,1)S(1)} %get-tuple-element.32.lt_ref, bf16[8,192,3072]{2,1,0:T(8,128)(2,1)S(1)} %get-tuple-element.29.comp_ref), custom_call_target="tpu_custom_call" | custom-call | flops 1000 | bytes 18874368 | tf_op jit(solution)/shard_map/right_keep/pallas_call | solution.py:170
  43.9 1.5 %chip_sum.1 = (f32[32,3072]{1,0:T(8,128)S(1)}, bf16[32,3072]{1,0:T(8,128)(2,1)}, bf16[32,3072]{1,0:T(8,128)(2,1)}, bf16[32,3072]{1,0:T(8,128)(2,1)}, bf16[256,96]{1,0:T(8,128)(2,1)}) custom-call(s32[7]{0:T(128)S(1)} %stack.45.pos, f32[4,1,32,3072]{3,2,1,0:T(8,128)S(1)} %right_keep.1.keep_ref, bf16[4,1,32,3072]{3,2,1,0:T(8,128)(2,1)S(1)} %collective-permute-done.10.recv_ref, ...), custom_call_target="tpu_custom_call" | custom-call | flops 1000 | bytes 1000 | tf_op jit(solution)/shard_map/chip_sum/pallas_call | solution.py:204
  49.6 1.9 %collective-permute-start.16 = (bf16[256,96]{1,0:T(8,128)(2,1)}, bf16[256,96]{1,0:T(8,128)(2,1)}, u32[]{:S(2)}, u32[]{:S(2)}) collective-permute-start(bf16[256,96]{1,0:T(8,128)(2,1)} %get-tuple-element.38), channel_id=1, source_target_pairs={{0,3},{1,2},{2,1},{3,0},{4,7},{5,6},{6,5},{7,4},{8,11},{9,10},{10,... | collective-permute-start | bytes 147464 | tf_op jit(solution)/shard_map/ppermute | solution.py:33
  51.5 4.1 %collective-permute-done.15 = bf16[256,96]{1,0:T(8,128)(2,1)} collective-permute-done((bf16[256,96]{1,0:T(8,128)(2,1)}, bf16[256,96]{1,0:T(8,128)(2,1)}, u32[]{:S(2)}, u32[]{:S(2)}) %collective-permute-start.15) | collective-permute-done | bytes 49184 | tf_op jit(solution)/shard_map/ppermute | solution.py:33
  55.6 4.0 %collective-permute-done.16 = bf16[256,96]{1,0:T(8,128)(2,1)} collective-permute-done((bf16[256,96]{1,0:T(8,128)(2,1)}, bf16[256,96]{1,0:T(8,128)(2,1)}, u32[]{:S(2)}, u32[]{:S(2)}) %collective-permute-start.16) | collective-permute-done | bytes 49184 | tf_op jit(solution)/shard_map/ppermute | solution.py:33
  61.6 1.8 %plane_sum.1 = (f32[32,768]{1,0:T(8,128)S(1)}, bf16[32,768]{1,0:T(8,128)(2,1)S(1)}, bf16[32,768]{1,0:T(8,128)(2,1)S(1)}, bf16[32,768]{1,0:T(8,128)(2,1)S(1)}, bf...) custom-call(s32[7]{0:T(128)S(1)} %stack.45.pos, f32[32,3072]{1,0:T(8,128)S(1)} %copy-done.3, ...), custom_call_target="tpu_custom_call" | custom-call | flops 1000 | bytes 1000 | tf_op jit(solution)/shard_map/plane_sum/pallas_call | solution.py:261
  63.5 1.3 %collective-permute-start.23 = (bf16[1,96,3072]{2,1,0:T(8,128)(2,1)S(1)}, bf16[1,96,3072]{2,1,0:T(8,128)(2,1)S(1)}, u32[]{:S(2)}, u32[]{:S(2)}) collective-permute-start(bf16[1,96,3072]{2,1,0:T(8,128)(2,1)S(1)} %get-tuple-element.43), channel_id=1, source_target_pairs={{0,2},{1,3},{2,0},{3,1},{4,6},{5,7},{6,4},{7,5},{8,10},{9,11},{10,... | collective-permute-start | bytes 1769480 | tf_op jit(solution)/shard_map/ppermute | solution.py:33
  65.1 3.1 %collective-permute-start.19 = (bf16[32,768]{1,0:T(8,128)(2,1)S(1)}, bf16[32,768]{1,0:T(8,128)(2,1)S(1)}, u32[]{:S(2)}, u32[]{:S(2)}) collective-permute-start(bf16[32,768]{1,0:T(8,128)(2,1)S(1)} %get-tuple-element.42), channel_id=1, source_target_pairs={{0,24},{4,28},{8,16},{12,20},{16,8},{20,12},{24,0},{28,4},{1,25},{... | collective-permute-start | bytes 147464 | tf_op jit(solution)/shard_map/ppermute | solution.py:33
  69.8 3.1 %collective-permute-done.18 = bf16[32,768]{1,0:T(8,128)(2,1)S(1)} collective-permute-done((bf16[32,768]{1,0:T(8,128)(2,1)S(1)}, bf16[32,768]{1,0:T(8,128)(2,1)S(1)}, u32[]{:S(2)}, u32[]{:S(2)}) %collective-permute-start.18) | collective-permute-done | bytes 49184 | tf_op jit(solution)/shard_map/ppermute | solution.py:33
  73.0 1.3 %collective-permute-start.21 = (bf16[32,768]{1,0:T(8,128)(2,1)S(1)}, bf16[32,768]{1,0:T(8,128)(2,1)S(1)}, u32[]{:S(2)}, u32[]{:S(2)}) collective-permute-start(bf16[32,768]{1,0:T(8,128)(2,1)S(1)} %add_convert_fusion.refs_0_), channel_id=1, source_target_pairs={{0,16},{4,20},{8,24},{12,28},{16,0},{20,4},{24,8},{28,12},{1,17},{... | collective-permute-start | bytes 147464 | tf_op jit(solution)/shard_map/ppermute | solution.py:33
  74.3 2.3 %collective-permute-start.22 = (bf16[32,768]{1,0:T(8,128)(2,1)S(1)}, bf16[32,768]{1,0:T(8,128)(2,1)S(1)}, u32[]{:S(2)}, u32[]{:S(2)}) collective-permute-start(bf16[32,768]{1,0:T(8,128)(2,1)S(1)} %add_convert_fusion.refs_0_), channel_id=1, source_target_pairs={{0,24},{4,28},{8,16},{12,20},{16,8},{20,12},{24,0},{28,4},{1,25},{... | collective-permute-start | bytes 147464 | tf_op jit(solution)/shard_map/ppermute | solution.py:33
  76.9 2.2 %collective-permute-done.22.refs_3_ = bf16[32,768]{1,0:T(8,128)(2,1)S(1)} collective-permute-done((bf16[32,768]{1,0:T(8,128)(2,1)S(1)}, bf16[32,768]{1,0:T(8,128)(2,1)S(1)}, u32[]{:S(2)}, u32[]{:S(2)}) %collective-permute-start.22) | collective-permute-done | bytes 49184 | tf_op jit(solution)/shard_map/ppermute | solution.py:33
  81.0 1.4 %collective-permute-start.27 = (bf16[32,3072]{1,0:T(8,128)(2,1)S(1)}, bf16[32,3072]{1,0:T(8,128)(2,1)S(1)}, u32[]{:S(2)}, u32[]{:S(2)}) collective-permute-start(bf16[32,3072]{1,0:T(8,128)(2,1)S(1)} %column_gather.1.refs_0_), channel_id=1, source_target_pairs={{0,3},{1,2},{2,1},{3,0},{4,7},{5,6},{6,5},{7,4},{8,11},{9,10},{10,... | collective-permute-start | bytes 589832 | tf_op jit(solution)/shard_map/ppermute | solution.py:33
  82.4 1.9 %collective-permute-done.25.refs_1_ = bf16[32,3072]{1,0:T(8,128)(2,1)S(1)} collective-permute-done((bf16[32,3072]{1,0:T(8,128)(2,1)S(1)}, bf16[32,3072]{1,0:T(8,128)(2,1)S(1)}, u32[]{:S(2)}, u32[]{:S(2)}) %collective-permute-start.25) | collective-permute-done | bytes 196640 | tf_op jit(solution)/shard_map/ppermute | solution.py:33
  84.3 3.2 %collective-permute-done.26.refs_2_ = bf16[32,3072]{1,0:T(8,128)(2,1)S(1)} collective-permute-done((bf16[32,3072]{1,0:T(8,128)(2,1)S(1)}, bf16[32,3072]{1,0:T(8,128)(2,1)S(1)}, u32[]{:S(2)}, u32[]{:S(2)}) %collective-permute-start.26) | collective-permute-done | bytes 196640 | tf_op jit(solution)/shard_map/ppermute | solution.py:33
  87.6 7.0 %collective-permute-start.28 = (bf16[4,1,32,3072]{3,2,1,0:T(8,128)(2,1)S(1)}, bf16[4,1,32,3072]{3,2,1,0:T(8,128)(2,1)S(1)}, u32[]{:S(2)}, u32[]{:S(2)}) collective-permute-start(bf16[4,1,32,3072]{3,2,1,0:T(8,128)(2,1)S(1)} %bitcast.30), channel_id=1, source_target_pairs={{0,4},{4,0},{8,12},{12,8},{16,20},{20,16},{24,28},{28,24},{1,5},{5... | collective-permute-start | bytes 2359304 | tf_op jit(solution)/shard_map/ppermute | solution.py:33
  95.2 3.7 %copy-done.1 = bf16[8,192,3072]{2,1,0:T(8,128)(2,1)S(1)} copy-done((bf16[8,192,3072]{2,1,0:T(8,128)(2,1)S(1)}, bf16[8,192,3072]{2,1,0:T(8,128)(2,1)}, u32[]{:S(2)}) %copy-start.1) | copy-done | bytes 9437208
  98.9 7.1 %outputs.2 = (bf16[1,8,192,3072]{3,2,1,0:T(8,128)(2,1)}, bf16[8,96,3072]{2,1,0:T(8,128)(2,1)}) custom-call(s32[7]{0:T(128)S(1)} %stack.45.pos, s32[8]{0:T(128)S(1)} %copy-done.8, bf16[8,192,3072]{2,1,0:T(8,128)(2,1)S(1)} %copy-done.1, bf16[4,1,32,3072]{3,2,1,0:T(8,128)(2,1)S(1)} %bitcast.31, bf16[256,192]{1,0:T(8,128)(2,1)S(1)} %get-tuple-element.32.lt_ref, ...), custom_call_target="tpu_custom_call" | custom-call | flops 1000 | bytes 1000 | tf_op jit(solution)/shard_map/outputs/pallas_call | solution.py:340
  106.0 4.8 %owned.1 = (f32[1,2,96,3072]{3,2,1,0:T(8,128)}, f32[1,2,96,3072]{3,2,1,0:T(8,128)}) custom-call(s32[7]{0:T(128)S(1)} %stack.45.pos, s32[8]{0:T(128)S(1)} %copy-done.8, f32[1,2,96,3072]{3,2,1,0:T(8,128)} %momentum_ref.3, f32[1,2,96,3072]{3,2,1,0:T(8,128)} %master_ref.3, bf16[4,1,32,3072]{3,2,1,0:T(8,128)(2,1)S(1)} %bitcast.32, ...), custom_call_target="tpu_custom_call" | custom-call | flops 1000 | bytes 1000 | tf_op jit(solution)/shard_map/owned/pallas_call | solution.py:391
  110.9 5.6 %outputs.3 = (bf16[1,8,192,3072]{3,2,1,0:T(8,128)(2,1)}, bf16[8,96,3072]{2,1,0:T(8,128)(2,1)}) custom-call(s32[7]{0:T(128)S(1)} %stack.45.pos, s32[8]{0:T(128)S(1)} %copy-done.8, bf16[8,192,3072]{2,1,0:T(8,128)(2,1)S(1)} %bitcast.29, ...), custom_call_target="tpu_custom_call", output_to_operand_aliasing={{0}: (11, {}), {1}: (12, {})} | custom-call | flops 1000 | bytes 1000 | tf_op jit(solution)/shard_map/outputs/pallas_call | solution.py:340
  (75 shorter events, 15.9 us)
Async XLA Ops:
  4.8 34.3 %collective-permute-start.8 = (bf16[2,96,3072]{2,1,0:T(8,128)(2,1)}, bf16[2,96,3072]{2,1,0:T(8,128)(2,1)S(1)}, u32[]{:S(2)}, u32[]{:S(2)}) collective-permute-start(bf16[2,96,3072]{2,1,0:T(8,128)(2,1)} %base.1.refs_0_), channel_id=1, source_target_pairs={{0,1},{1,0},{2,3},{3,2},{4,5},{5,4},{6,7},{7,6},{8,9},{9,8},{10,11... | collective-permute-start | bytes 3538952 | tf_op jit(solution)/shard_map/ppermute | solution.py:33
  6.8 32.3 %collective-permute-start.9 = (bf16[2,96,3072]{2,1,0:T(8,128)(2,1)}, bf16[2,96,3072]{2,1,0:T(8,128)(2,1)S(1)}, u32[]{:S(2)}, u32[]{:S(2)}) collective-permute-start(bf16[2,96,3072]{2,1,0:T(8,128)(2,1)} %base.1.refs_0_), channel_id=1, source_target_pairs={{0,2},{1,3},{2,0},{3,1},{4,6},{5,7},{6,4},{7,5},{8,10},{9,11},{10,... | collective-permute-start | bytes 3538952 | tf_op jit(solution)/shard_map/ppermute | solution.py:33
  18.7 2.3 %collective-permute-start = (f32[4,32,256]{2,1,0:T(8,128)S(1)}, f32[4,32,256]{2,1,0:T(8,128)S(1)}, u32[]{:S(2)}, u32[]{:S(2)}) collective-permute-start(f32[4,32,256]{2,1,0:T(8,128)S(1)} %get-tuple-element.31), channel_id=1, source_target_pairs={{0,4},{4,0},{8,12},{12,8},{16,20},{20,16},{24,28},{28,24},{1,5},{5... | collective-permute-start | bytes 393224 | tf_op jit(solution)/shard_map/ppermute | solution.py:33
  21.0 3.7 %collective-permute-start.1 = (f32[32,256]{1,0:T(8,128)S(1)}, f32[32,256]{1,0:T(8,128)S(1)}, u32[]{:S(2)}, u32[]{:S(2)}) collective-permute-start(f32[32,256]{1,0:T(8,128)S(1)} %get-tuple-element.56), channel_id=1, source_target_pairs={{0,8},{4,12},{8,0},{12,4},{16,24},{20,28},{24,16},{28,20},{1,9},{5... | collective-permute-start | bytes 98312 | tf_op jit(solution)/shard_map/ppermute | solution.py:33
  22.4 4.0 %collective-permute-start.2 = (f32[32,256]{1,0:T(8,128)S(1)}, f32[32,256]{1,0:T(8,128)S(1)}, u32[]{:S(2)}, u32[]{:S(2)}) collective-permute-start(f32[32,256]{1,0:T(8,128)S(1)} %get-tuple-element.55), channel_id=1, source_target_pairs={{0,16},{4,20},{8,24},{12,28},{16,0},{20,4},{24,8},{28,12},{1,17},{... | collective-permute-start | bytes 98312 | tf_op jit(solution)/shard_map/ppermute | solution.py:33
  24.7 4.6 %collective-permute-start.3 = (f32[32,256]{1,0:T(8,128)S(1)}, f32[32,256]{1,0:T(8,128)S(1)}, u32[]{:S(2)}, u32[]{:S(2)}) collective-permute-start(f32[32,256]{1,0:T(8,128)S(1)} %get-tuple-element.54), channel_id=1, source_target_pairs={{0,24},{4,28},{8,16},{12,20},{16,8},{20,12},{24,0},{28,4},{1,25},{... | collective-permute-start | bytes 98312 | tf_op jit(solution)/shard_map/ppermute | solution.py:33
  29.3 3.6 %collective-permute-start.4 = (f32[32,256]{1,0:T(8,128)S(1)}, f32[32,256]{1,0:T(8,128)S(1)}, u32[]{:S(2)}, u32[]{:S(2)}) collective-permute-start(f32[32,256]{1,0:T(8,128)S(1)} %fusion.5.refs_0_), channel_id=1, source_target_pairs={{0,8},{4,12},{8,0},{12,4},{16,24},{20,28},{24,16},{28,20},{1,9},{5... | collective-permute-start | bytes 98312 | tf_op jit(solution)/shard_map/ppermute | solution.py:33
  29.3 3.7 %collective-permute-start.5 = (f32[32,256]{1,0:T(8,128)S(1)}, f32[32,256]{1,0:T(8,128)S(1)}, u32[]{:S(2)}, u32[]{:S(2)}) collective-permute-start(f32[32,256]{1,0:T(8,128)S(1)} %fusion.5.refs_0_), channel_id=1, source_target_pairs={{0,16},{4,20},{8,24},{12,28},{16,0},{20,4},{24,8},{28,12},{1,17},{... | collective-permute-start | bytes 98312 | tf_op jit(solution)/shard_map/ppermute | solution.py:33
  30.0 4.6 %collective-permute-start.6 = (f32[32,256]{1,0:T(8,128)S(1)}, f32[32,256]{1,0:T(8,128)S(1)}, u32[]{:S(2)}, u32[]{:S(2)}) collective-permute-start(f32[32,256]{1,0:T(8,128)S(1)} %fusion.5.refs_0_), channel_id=1, source_target_pairs={{0,24},{4,28},{8,16},{12,20},{16,8},{20,12},{24,0},{28,4},{1,25},{... | collective-permute-start | bytes 98312 | tf_op jit(solution)/shard_map/ppermute | solution.py:33
  34.6 4.5 %collective-permute-start.7 = (f32[4,32,256]{2,1,0:T(8,128)S(1)}, f32[4,32,256]{2,1,0:T(8,128)S(1)}, u32[]{:S(2)}, u32[]{:S(2)}) collective-permute-start(f32[4,32,256]{2,1,0:T(8,128)S(1)} %stack.51.near_ref), channel_id=1, source_target_pairs={{0,4},{4,0},{8,12},{12,8},{16,20},{20,16},{24,28},{28,24},{1,5},{5... | collective-permute-start | bytes 393224 | tf_op jit(solution)/shard_map/ppermute | solution.py:33
  41.6 2.4 %collective-permute-start.10 = (bf16[4,1,32,3072]{3,2,1,0:T(8,128)(2,1)S(1)}, bf16[4,1,32,3072]{3,2,1,0:T(8,128)(2,1)S(1)}, u32[]{:S(2)}, u32[]{:S(2)}) collective-permute-start(bf16[4,1,32,3072]{3,2,1,0:T(8,128)(2,1)S(1)} %get-tuple-element.33), channel_id=1, source_target_pairs={{0,4},{4,0},{8,12},{12,8},{16,20},{20,16},{24,28},{28,24},{1,5},{5... | collective-permute-start | bytes 2359304 | tf_op jit(solution)/shard_map/ppermute | solution.py:33
  43.9 66.9 %slice-start = ((s8[9437184]{0:T(1024)(128)(4,1)}), s8[1048576]{0:T(1024)(128)(4,1)S(1)}, s32[]{:S(2)}) async-start(s8[9437184]{0:T(1024)(128)(4,1)} %bitcast.28), calls=%async_computation | async-start | bytes 2097152
  46.2 3.4 %collective-permute-start.14 = (bf16[256,96]{1,0:T(8,128)(2,1)}, bf16[256,96]{1,0:T(8,128)(2,1)}, u32[]{:S(2)}, u32[]{:S(2)}) collective-permute-start(bf16[256,96]{1,0:T(8,128)(2,1)} %get-tuple-element.38), channel_id=1, source_target_pairs={{0,1},{1,0},{2,3},{3,2},{4,5},{5,4},{6,7},{7,6},{8,9},{9,8},{10,11... | collective-permute-start | bytes 147464 | tf_op jit(solution)/shard_map/ppermute | solution.py:33
  46.4 14.1 %collective-permute-start.11 = (bf16[32,3072]{1,0:T(8,128)(2,1)}, bf16[32,3072]{1,0:T(8,128)(2,1)}, u32[]{:S(2)}, u32[]{:S(2)}) collective-permute-start(bf16[32,3072]{1,0:T(8,128)(2,1)} %get-tuple-element.35), channel_id=1, source_target_pairs={{0,1},{1,0},{2,3},{3,2},{4,5},{5,4},{6,7},{7,6},{8,9},{9,8},{10,11... | collective-permute-start | bytes 589832 | tf_op jit(solution)/shard_map/ppermute | solution.py:33
  47.7 12.9 %collective-permute-start.12 = (bf16[32,3072]{1,0:T(8,128)(2,1)}, bf16[32,3072]{1,0:T(8,128)(2,1)}, u32[]{:S(2)}, u32[]{:S(2)}) collective-permute-start(bf16[32,3072]{1,0:T(8,128)(2,1)} %get-tuple-element.36), channel_id=1, source_target_pairs={{0,2},{1,3},{2,0},{3,1},{4,6},{5,7},{6,4},{7,5},{8,10},{9,11},{10,... | collective-permute-start | bytes 589832 | tf_op jit(solution)/shard_map/ppermute | solution.py:33
  47.9 12.7 %collective-permute-start.13 = (bf16[32,3072]{1,0:T(8,128)(2,1)}, bf16[32,3072]{1,0:T(8,128)(2,1)}, u32[]{:S(2)}, u32[]{:S(2)}) collective-permute-start(bf16[32,3072]{1,0:T(8,128)(2,1)} %get-tuple-element.37), channel_id=1, source_target_pairs={{0,3},{1,2},{2,1},{3,0},{4,7},{5,6},{6,5},{7,4},{8,11},{9,10},{10,... | collective-permute-start | bytes 589832 | tf_op jit(solution)/shard_map/ppermute | solution.py:33
  49.1 6.6 %collective-permute-start.15 = (bf16[256,96]{1,0:T(8,128)(2,1)}, bf16[256,96]{1,0:T(8,128)(2,1)}, u32[]{:S(2)}, u32[]{:S(2)}) collective-permute-start(bf16[256,96]{1,0:T(8,128)(2,1)} %get-tuple-element.38), channel_id=1, source_target_pairs={{0,2},{1,3},{2,0},{3,1},{4,6},{5,7},{6,4},{7,5},{8,10},{9,11},{10,... | collective-permute-start | bytes 147464 | tf_op jit(solution)/shard_map/ppermute | solution.py:33
  49.6 10.0 %collective-permute-start.16 = (bf16[256,96]{1,0:T(8,128)(2,1)}, bf16[256,96]{1,0:T(8,128)(2,1)}, u32[]{:S(2)}, u32[]{:S(2)}) collective-permute-start(bf16[256,96]{1,0:T(8,128)(2,1)} %get-tuple-element.38), channel_id=1, source_target_pairs={{0,3},{1,2},{2,1},{3,0},{4,7},{5,6},{6,5},{7,4},{8,11},{9,10},{10,... | collective-permute-start | bytes 147464 | tf_op jit(solution)/shard_map/ppermute | solution.py:33
  63.4 31.2 %copy-start.9 = (f32[2688]{0:T(1024)S(1)}, f32[2688]{0:T(1024)}, u32[]{:S(2)}) copy-start(f32[2688]{0:T(1024)} %param.19) | copy-start | bytes 32260
  63.5 31.8 %copy-start.8 = (s32[8]{0:T(128)S(1)}, s32[8]{0:T(128)}, u32[]{:S(2)}) copy-start(s32[8]{0:T(128)} %owners.5) | copy-start | bytes 100
  63.5 15.6 %collective-permute-start.23 = (bf16[1,96,3072]{2,1,0:T(8,128)(2,1)S(1)}, bf16[1,96,3072]{2,1,0:T(8,128)(2,1)S(1)}, u32[]{:S(2)}, u32[]{:S(2)}) collective-permute-start(bf16[1,96,3072]{2,1,0:T(8,128)(2,1)S(1)} %get-tuple-element.43), channel_id=1, source_target_pairs={{0,2},{1,3},{2,0},{3,1},{4,6},{5,7},{6,4},{7,5},{8,10},{9,11},{10,... | collective-permute-start | bytes 1769480 | tf_op jit(solution)/shard_map/ppermute | solution.py:33
  64.7 14.4 %collective-permute-start.24 = (bf16[1,96,3072]{2,1,0:T(8,128)(2,1)S(1)}, bf16[1,96,3072]{2,1,0:T(8,128)(2,1)S(1)}, u32[]{:S(2)}, u32[]{:S(2)}) collective-permute-start(bf16[1,96,3072]{2,1,0:T(8,128)(2,1)S(1)} %get-tuple-element.44), channel_id=1, source_target_pairs={{0,1},{1,0},{2,3},{3,2},{4,5},{5,4},{6,7},{7,6},{8,9},{9,8},{10,11... | collective-permute-start | bytes 1769480 | tf_op jit(solution)/shard_map/ppermute | solution.py:33
  65.1 4.7 %collective-permute-start.19 = (bf16[32,768]{1,0:T(8,128)(2,1)S(1)}, bf16[32,768]{1,0:T(8,128)(2,1)S(1)}, u32[]{:S(2)}, u32[]{:S(2)}) collective-permute-start(bf16[32,768]{1,0:T(8,128)(2,1)S(1)} %get-tuple-element.42), channel_id=1, source_target_pairs={{0,24},{4,28},{8,16},{12,20},{16,8},{20,12},{24,0},{28,4},{1,25},{... | collective-permute-start | bytes 147464 | tf_op jit(solution)/shard_map/ppermute | solution.py:33
  68.2 4.7 %collective-permute-start.18 = (bf16[32,768]{1,0:T(8,128)(2,1)S(1)}, bf16[32,768]{1,0:T(8,128)(2,1)S(1)}, u32[]{:S(2)}, u32[]{:S(2)}) collective-permute-start(bf16[32,768]{1,0:T(8,128)(2,1)S(1)} %get-tuple-element.41), channel_id=1, source_target_pairs={{0,16},{4,20},{8,24},{12,28},{16,0},{20,4},{24,8},{28,12},{1,17},{... | collective-permute-start | bytes 147464 | tf_op jit(solution)/shard_map/ppermute | solution.py:33
  68.2 4.7 %collective-permute-start.17 = (bf16[32,768]{1,0:T(8,128)(2,1)S(1)}, bf16[32,768]{1,0:T(8,128)(2,1)S(1)}, u32[]{:S(2)}, u32[]{:S(2)}) collective-permute-start(bf16[32,768]{1,0:T(8,128)(2,1)S(1)} %get-tuple-element.40), channel_id=1, source_target_pairs={{0,8},{4,12},{8,0},{12,4},{16,24},{20,28},{24,16},{28,20},{1,9},{5... | collective-permute-start | bytes 147464 | tf_op jit(solution)/shard_map/ppermute | solution.py:33
  72.9 3.6 %collective-permute-start.20 = (bf16[32,768]{1,0:T(8,128)(2,1)S(1)}, bf16[32,768]{1,0:T(8,128)(2,1)S(1)}, u32[]{:S(2)}, u32[]{:S(2)}) collective-permute-start(bf16[32,768]{1,0:T(8,128)(2,1)S(1)} %add_convert_fusion.refs_0_), channel_id=1, source_target_pairs={{0,8},{4,12},{8,0},{12,4},{16,24},{20,28},{24,16},{28,20},{1,9},{5... | collective-permute-start | bytes 147464 | tf_op jit(solution)/shard_map/ppermute | solution.py:33
  73.0 3.9 %collective-permute-start.21 = (bf16[32,768]{1,0:T(8,128)(2,1)S(1)}, bf16[32,768]{1,0:T(8,128)(2,1)S(1)}, u32[]{:S(2)}, u32[]{:S(2)}) collective-permute-start(bf16[32,768]{1,0:T(8,128)(2,1)S(1)} %add_convert_fusion.refs_0_), channel_id=1, source_target_pairs={{0,16},{4,20},{8,24},{12,28},{16,0},{20,4},{24,8},{28,12},{1,17},{... | collective-permute-start | bytes 147464 | tf_op jit(solution)/shard_map/ppermute | solution.py:33
  74.3 4.8 %collective-permute-start.22 = (bf16[32,768]{1,0:T(8,128)(2,1)S(1)}, bf16[32,768]{1,0:T(8,128)(2,1)S(1)}, u32[]{:S(2)}, u32[]{:S(2)}) collective-permute-start(bf16[32,768]{1,0:T(8,128)(2,1)S(1)} %add_convert_fusion.refs_0_), channel_id=1, source_target_pairs={{0,24},{4,28},{8,16},{12,20},{16,8},{20,12},{24,0},{28,4},{1,25},{... | collective-permute-start | bytes 147464 | tf_op jit(solution)/shard_map/ppermute | solution.py:33
  79.7 4.6 %collective-permute-start.25 = (bf16[32,3072]{1,0:T(8,128)(2,1)S(1)}, bf16[32,3072]{1,0:T(8,128)(2,1)S(1)}, u32[]{:S(2)}, u32[]{:S(2)}) collective-permute-start(bf16[32,3072]{1,0:T(8,128)(2,1)S(1)} %column_gather.1.refs_0_), channel_id=1, source_target_pairs={{0,1},{1,0},{2,3},{3,2},{4,5},{5,4},{6,7},{7,6},{8,9},{9,8},{10,11... | collective-permute-start | bytes 589832 | tf_op jit(solution)/shard_map/ppermute | solution.py:33
  80.9 6.6 %collective-permute-start.26 = (bf16[32,3072]{1,0:T(8,128)(2,1)S(1)}, bf16[32,3072]{1,0:T(8,128)(2,1)S(1)}, u32[]{:S(2)}, u32[]{:S(2)}) collective-permute-start(bf16[32,3072]{1,0:T(8,128)(2,1)S(1)} %column_gather.1.refs_0_), channel_id=1, source_target_pairs={{0,2},{1,3},{2,0},{3,1},{4,6},{5,7},{6,4},{7,5},{8,10},{9,11},{10,... | collective-permute-start | bytes 589832 | tf_op jit(solution)/shard_map/ppermute | solution.py:33
  81.0 6.5 %collective-permute-start.27 = (bf16[32,3072]{1,0:T(8,128)(2,1)S(1)}, bf16[32,3072]{1,0:T(8,128)(2,1)S(1)}, u32[]{:S(2)}, u32[]{:S(2)}) collective-permute-start(bf16[32,3072]{1,0:T(8,128)(2,1)S(1)} %column_gather.1.refs_0_), channel_id=1, source_target_pairs={{0,3},{1,2},{2,1},{3,0},{4,7},{5,6},{6,5},{7,4},{8,11},{9,10},{10,... | collective-permute-start | bytes 589832 | tf_op jit(solution)/shard_map/ppermute | solution.py:33
  87.6 18.4 %collective-permute-start.28 = (bf16[4,1,32,3072]{3,2,1,0:T(8,128)(2,1)S(1)}, bf16[4,1,32,3072]{3,2,1,0:T(8,128)(2,1)S(1)}, u32[]{:S(2)}, u32[]{:S(2)}) collective-permute-start(bf16[4,1,32,3072]{3,2,1,0:T(8,128)(2,1)S(1)} %bitcast.30), channel_id=1, source_target_pairs={{0,4},{4,0},{8,12},{12,8},{16,20},{20,16},{24,28},{28,24},{1,5},{5... | collective-permute-start | bytes 2359304 | tf_op jit(solution)/shard_map/ppermute | solution.py:33
  (11 other events, 155.8 us)

commit v4 on v3

--- a/solution.py
+++ b/solution.py
@@ -8,14 +8,14 @@
 from jax.sharding import PartitionSpec as P
 
 CORES = 2
-LANES = 128
-VMEM_LIMIT = 24 * 1024 * 1024
+BASE_ROWS = 16
+COLUMNS = 512
 F32 = jnp.float32
 BF16 = jnp.bfloat16
 
 
-def params():
-    return pltpu.CompilerParams(vmem_limit_bytes=VMEM_LIMIT)
+def params(mib=12):
+    return pltpu.CompilerParams(vmem_limit_bytes=mib * 1024 * 1024)
 
 
 def cost(bytes_accessed=1000):
@@ -37,8 +37,7 @@
     k = pl.program_id(0)
     rows = g_ref.shape[2]
     rank = q_ref.shape[1]
-    group = LANES // rank
-    near, piece, _ = near_ref.shape
+    part = near_ref.shape[0]
 
     @pl.when(k == 0)
     def _():
@@ -49,29 +48,28 @@
             total[rows + i : rows + i + 1, :count] = vec_ref[:, first : first + count]
 
     comp = g_ref[0, 0] + f_ref[0, 0]
-    comp_ref[0] = comp
-    q = q_ref[0]
-    wide = jnp.concatenate([q] * group, axis=0)
-    member = lax.broadcasted_iota(jnp.int32, wide.shape, 0) // rank
-    wide = jnp.where(member == k % group, wide, jnp.zeros_like(wide))
-    terms = lax.dot_general(comp, wide, (((1,), (1,)), ((), ())), preferred_element_type=F32)
-    cols = pl.ds(pl.multiple_of((k // group) * LANES, LANES), LANES)
-    total[:rows, cols] += terms
+    comp_ref[k] = comp
+    terms = lax.dot_general(comp, q_ref[0], (((1,), (1,)), ((), ())), preferred_element_type=F32)
+    for i in range(total.shape[1] // rank):
+
+        @pl.when(k == i)
+        def _():
+            total[:rows, i * rank : (i + 1) * rank] = terms
 
     @pl.when(k == pl.num_programs(0) - 1)
     def _():
-        for s in range(near):
-            for out, slot in ((near_ref, s), (far_ref, s + near)):
-                out[s] = total[pl.ds(pl.multiple_of((slot ^ pos[3]) * piece, piece), piece), :]
-
-
-def left_terms(pos, gradients, feedback, right_t, vec, n_z):
+        for ref, core in ((near_ref, pos[2]), (far_ref, 1 - pos[2])):
+            ref[...] = total[pl.ds(pl.multiple_of(core * part, 16), part), :]
+
+
+def left_terms(pos, gradients, feedback, right_t, vec):
     _, nmat, rows, n = gradients.shape
     rank = right_t.shape[1]
     width = nmat * rank
     total = rows + -(-vec.shape[1] // width)
-    total += -total % (8 * CORES * n_z)
-    pieces = jax.ShapeDtypeStruct((n_z, total // (CORES * n_z), width), F32)
+    total += -total % (16 * CORES)
+    part = jax.ShapeDtypeStruct((total // CORES, width), F32)
+    vmem = pl.BlockSpec(memory_space=pltpu.VMEM)
     return pl.pallas_call(
         left_kernel,
         grid_spec=pltpu.PrefetchScalarGridSpec(
@@ -81,20 +79,34 @@
                 pl.BlockSpec((1, 1, rows, n), lambda k, pos: (0, k, 0, 0)),
                 pl.BlockSpec((1, 1, rows, n), lambda k, pos: (0, k, 0, 0)),
                 pl.BlockSpec((1, rank, n), lambda k, pos: (k, 0, 0)),
-                pl.BlockSpec(vec.shape, lambda k, pos: (0, 0)),
+                vmem,
             ],
-            out_specs=[
-                pl.BlockSpec((1, rows, n), lambda k, pos: (k, 0, 0)),
-                pl.BlockSpec(pieces.shape, lambda k, pos: (0, 0, 0)),
-                pl.BlockSpec(pieces.shape, lambda k, pos: (0, 0, 0)),
-            ],
+            out_specs=[vmem] * 3,
             scratch_shapes=[pltpu.VMEM((total, width), F32)],
         ),
-        out_shape=[jax.ShapeDtypeStruct((nmat, rows, n), BF16), pieces, pieces],
-        compiler_params=params(),
+        out_shape=[jax.ShapeDtypeStruct((nmat, rows, n), BF16), part, part],
+        compiler_params=params(16),
         cost_estimate=cost(),
         name="left_terms",
     )(pos, gradients, feedback, right_t, vec)
+
+
+def add_kernel(*refs):
+    out = refs[-1]
+    out[...] = tree_sum([ref[...].astype(F32) for ref in refs[:-1]]).astype(out.dtype)
+
+
+def add(parts, dtype):
+    vmem = pl.BlockSpec(memory_space=pltpu.VMEM)
+    return pl.pallas_call(
+        add_kernel,
+        in_specs=[vmem] * len(parts),
+        out_specs=vmem,
+        out_shape=jax.ShapeDtypeStruct(parts[0].shape, dtype),
+        compiler_params=params(),
+        cost_estimate=cost(),
+        name="add",
+    )(*parts)
 
 
 def send_kernel(half, pos, near_ref, far_ref, gram_ref, comp_ref, *refs):
@@ -105,10 +117,9 @@
 
     @pl.when(t == 0)
     def _():
-        near, piece, _ = near_ref.shape
-        for s in range(near):
-            for part, slot in ((near_ref, s), (far_ref, s + near)):
-                left[pl.ds(pl.multiple_of((slot ^ pos[3]) * piece, piece), piece), :] = part[s]
+        part = near_ref.shape[0]
+        for ref, core in ((near_ref, pos[2]), (far_ref, 1 - pos[2])):
+            left[pl.ds(pl.multiple_of(core * part, 16), part), :] = ref[...]
         vec_ref[...] = left[rows:, :]
         gram[...] = jnp.zeros(gram.shape, F32)
         for i in range(gram_ref.shape[0]):
@@ -125,7 +136,7 @@
     upm, unit = out_ref.shape[1], out_ref.shape[2]
     k = (pl.program_id(0) + start) ^ pos[0]
     rows = pl.ds(pl.multiple_of(k * upm * unit, upm * unit), upm * unit)
-    terms = jnp.dot(lt_ref[rows, :], comp_ref[0], preferred_element_type=F32)
+    terms = jnp.dot(lt_ref[rows, :], comp_ref[k], preferred_element_type=F32)
     for i in range(upm):
         out_ref[0, i ^ pos[1]] = terms[i * unit : (i + 1) * unit].astype(out_ref.dtype)
 
@@ -139,7 +150,7 @@
     rank = gram.shape[1]
     width = nmat * rank
     half = nmat // CORES
-    total = CORES * near.shape[0] * near.shape[1]
+    total = CORES * near.shape[0]
     shape = (half, upm, rank // upm, n)
     vmem = pl.BlockSpec(memory_space=pltpu.VMEM)
     out = pl.BlockSpec((1,) + shape[1:], lambda t, pos: (t, 0, 0, 0))
@@ -152,7 +163,7 @@
                 vmem,
                 vmem,
                 vmem,
-                pl.BlockSpec((1, rows, n), lambda t, pos: ((t + half) ^ pos[0], 0, 0)),
+                vmem,
             ]
             + [pl.BlockSpec(memory_space=pl.ANY)] * len(after),
             out_specs=[out, vmem, vmem],
@@ -172,7 +183,7 @@
         grid_spec=pltpu.PrefetchScalarGridSpec(
             num_scalar_prefetch=1,
             grid=(half,),
-            in_specs=[vmem, pl.BlockSpec((1, rows, n), lambda t, pos: (t ^ pos[0], 0, 0))],
+            in_specs=[vmem, vmem],
             out_specs=out,
         ),
         out_shape=jax.ShapeDtypeStruct(shape, F32),
@@ -183,26 +194,33 @@
     return send, keep, lt, vec
 
 
-def chip_kernel(pos, keep_ref, recv_ref, lt_ref, *refs):
+def chip_kernel(replica_rows, pos, keep_ref, recv_ref, lt_ref, own_ref, strip_ref, *sends):
     upm = keep_ref.shape[1]
-    for d, out in enumerate(refs[:-1]):
+    n = own_ref.shape[1]
+    left = lt_ref[...].astype(F32).T
+    strip = left[:replica_rows]
+    for i in range(1, left.shape[0] // replica_rows):
+        strip = jnp.where(pos[6] == i, left[i * replica_rows : (i + 1) * replica_rows], strip)
+    height = strip_ref.shape[0]
+    strip = jnp.concatenate(
+        [strip[i * height : (i + 1) * height] for i in range(replica_rows // height)], axis=1
+    )
+    strip_ref[...] = strip
+    own_ref[...] = keep_ref[0, 0] + recv_ref[0, 0].astype(F32)
+    for d, out in enumerate(sends, 1):
         j, i = d // upm, d % upm
-        out[...] = (keep_ref[j, i] + recv_ref[j, i].astype(F32)).astype(out.dtype)
-    strip_ref = refs[-1]
-    count = strip_ref.shape[1]
-    strip = lt_ref[:, :count]
-    for i in range(1, lt_ref.shape[1] // count):
-        strip = jnp.where(pos[6] == i, lt_ref[:, i * count : (i + 1) * count], strip)
-    strip_ref[...] = strip
+        terms = keep_ref[j, i] + recv_ref[j, i].astype(F32)
+        out[...] = jnp.concatenate([terms, strip], axis=0).astype(BF16)
 
 
 def chip_sum(pos, keep, recv, lt, replica_rows):
     half, upm, unit, n = keep.shape
-    vmem = pl.BlockSpec(memory_space=pltpu.VMEM)
-    outs = [jax.ShapeDtypeStruct((unit, n), BF16 if d else F32) for d in range(half * upm)]
-    outs.append(jax.ShapeDtypeStruct((lt.shape[0], replica_rows), BF16))
-    return pl.pallas_call(
-        chip_kernel,
+    height = lt.shape[0] * replica_rows // n
+    vmem = pl.BlockSpec(memory_space=pltpu.VMEM)
+    outs = [jax.ShapeDtypeStruct((unit, n), F32), jax.ShapeDtypeStruct((height, n), F32)]
+    outs += [jax.ShapeDtypeStruct((unit + height, n), BF16)] * (half * upm - 1)
+    return pl.pallas_call(
+        functools.partial(chip_kernel, replica_rows),
         grid_spec=pltpu.PrefetchScalarGridSpec(
             num_scalar_prefetch=1,
             grid=(1,),
@@ -241,36 +259,45 @@
     )(pos, *parts, *after)
 
 
-def plane_kernel(count, cuts, pos, *refs):
-    terms, wholes, outs = refs[:count], refs[count : count + len(cuts)], refs[count + len(cuts) + 1 :]
-    cols = outs[0].shape[1]
-    n_z = len(outs) - len(cuts)
-    for d, out in enumerate(outs[:n_z]):
+def plane_kernel(count, cuts, n_z, pos, own_ref, strip_ref, *refs):
+    terms, wholes, refs = refs[:count], refs[count : count + len(cuts)], refs[count + len(cuts) :]
+    outs, forwards, ltr_ref = refs[:n_z], refs[n_z:-1], refs[-1]
+    unit, n = own_ref.shape
+    cols = n // n_z
+    for d, out in enumerate(outs):
         block = pl.ds(pl.multiple_of((pos[4] ^ d) * cols, cols), cols)
-        out[...] = tree_sum([term[:, block].astype(F32) for term in terms]).astype(out.dtype)
-    for whole, out, first in zip(wholes, outs[n_z:], cuts):
+        parts = [own_ref[:, block]] + [term[:, block].astype(F32)[:unit] for term in terms]
+        out[...] = tree_sum(parts).astype(out.dtype)
+    strip = strip_ref[...]
+    for d, term in enumerate(terms, 1):
+        strip = jnp.where(pos[7] == d, term[...].astype(F32)[unit:], strip)
+    width = ltr_ref.shape[0]
+    rows = [strip[:, i * width : (i + 1) * width] for i in range(n // width)]
+    ltr_ref[...] = jnp.concatenate(rows, axis=0).T.astype(BF16)
+    for whole, out, first in zip(wholes, forwards, cuts):
         out[...] = whole[first : first + out.shape[0]]
 
 
-def plane_sum(pos, terms, n_z, wholes, cuts, after):
-    unit, n = terms[0].shape
+def plane_sum(pos, own, strip, terms, n_z, width, wholes, cuts):
+    unit, n = own.shape
     cols = n // n_z
     outs = [jax.ShapeDtypeStruct((unit, cols), BF16 if d else F32) for d in range(n_z)]
     outs += [jax.ShapeDtypeStruct((x.shape[0] // 2,) + x.shape[1:], x.dtype) for x in wholes]
-    vmem = pl.BlockSpec(memory_space=pltpu.VMEM)
-    return pl.pallas_call(
-        functools.partial(plane_kernel, len(terms), cuts),
+    outs.append(jax.ShapeDtypeStruct((width, strip.size // width), BF16))
+    vmem = pl.BlockSpec(memory_space=pltpu.VMEM)
+    return pl.pallas_call(
+        functools.partial(plane_kernel, len(terms), cuts, n_z),
         grid_spec=pltpu.PrefetchScalarGridSpec(
             num_scalar_prefetch=1,
             grid=(1,),
-            in_specs=[vmem] * (len(terms) + len(wholes)) + [pl.BlockSpec(memory_space=pl.ANY)],
+            in_specs=[vmem] * (2 + len(terms) + len(wholes)),
             out_specs=[vmem] * len(outs),
         ),
         out_shape=outs,
         compiler_params=params(),
         cost_estimate=cost(),
         name="plane_sum",
-    )(pos, *terms, *wholes, after)
+    )(pos, own, strip, *terms, *wholes)
 
 
 def matrix_of(right_ref, slot, sub):
@@ -321,10 +348,16 @@
     right = matrix_of(right_ref, j, pos[1])
     k = (j + start) ^ pos[0]
     rows = pl.ds(pl.multiple_of(k * rank, rank), rank)
-    feedback_ref[0, 0] = (comp_ref[0].astype(F32) - product(lt_ref[rows, :], right)).astype(BF16)
+    lt, ltr = lt_ref[rows, :], ltr_ref[rows, :]
     fetch(j, False)
-    base = held[lax.rem(j, 2)].astype(F32)
-    weights_ref[0] = (base - 0.1 * product(ltr_ref[rows, :], right)).astype(BF16)
+    buffer = lax.rem(j, 2)
+    n = right.shape[1]
+    for first in range(0, n, COLUMNS):
+        block = slice(first, first + COLUMNS)
+        approx = product(lt, right[:, block])
+        feedback_ref[0, 0, :, block] = (comp_ref[k, :, block].astype(F32) - approx).astype(BF16)
+        approx = product(ltr, right[:, block])
+        weights_ref[0, :, block] = (held[buffer, :, block].astype(F32) - 0.1 * approx).astype(BF16)
 
 
 def outputs(pos, owners, start, comp, right, lt, ltr, bases, places, earlier):
@@ -342,8 +375,7 @@
         grid_spec=pltpu.PrefetchScalarGridSpec(
             num_scalar_prefetch=2,
             grid=(half,),
-            in_specs=[pl.BlockSpec((1, rows, n), lambda j, pos, own: (matrix(j, pos), 0, 0))]
-            + [vmem] * 3
+            in_specs=[vmem] * 4
             + [any_spec] * (len(bases) + len(earlier)),
             out_specs=[
                 pl.BlockSpec((1, 1, rows, n), lambda j, pos, own: (0, matrix(j, pos), 0, 0)),
@@ -359,7 +391,7 @@
             jax.ShapeDtypeStruct((nmat, replica_rows, n), BF16),
         ],
         input_output_aliases={6 + len(bases) + i: i for i in range(len(earlier))},
-        compiler_params=params(),
+        compiler_params=params(16),
         cost_estimate=cost(),
         name="outputs",
     )(pos, owners, comp, right, lt, ltr, *bases, *earlier)
@@ -397,26 +429,43 @@
             out_specs=[state, state],
         ),
         out_shape=[jax.ShapeDtypeStruct(momentum.shape, F32)] * 2,
-        compiler_params=params(),
+        compiler_params=params(20),
         cost_estimate=cost(),
         name="owned",
     )(pos, owners, momentum, master, near, far, ltr)
 
 
-def base_kernel(momentum_ref, master_ref, out_ref):
-    out_ref[0] = (master_ref[0, 0] - 0.09 * momentum_ref[0, 0]).astype(BF16)
+def base_kernel(momentum_ref, master_ref, out_ref, momentum, master, sems):
+    capacity, rows, _ = out_ref.shape
+    blocks = [(c, first) for c in range(capacity) for first in range(0, rows, BASE_ROWS)]
+
+    def copies(i):
+        c, first = blocks[i]
+        part = pl.ds(first, BASE_ROWS)
+        return [
+            pltpu.make_async_copy(source.at[0, c, part], target.at[c, part], sems.at[j, i])
+            for j, (source, target) in enumerate(((momentum_ref, momentum), (master_ref, master)))
+        ]
+
+    for i in range(len(blocks)):
+        for copy in copies(i):
+            copy.start()
+    for i, (c, first) in enumerate(blocks):
+        for copy in copies(i):
+            copy.wait()
+        part = slice(first, first + BASE_ROWS)
+        out_ref[c, part] = (master[c, part] - 0.09 * momentum[c, part]).astype(BF16)
 
 
 def base_of(momentum, master):
     _, capacity, rows, n = momentum.shape
-    cuts = 2
-    state = pl.BlockSpec((1, 1, rows, n // cuts), lambda c, i: (0, c, 0, i))
+    state = pltpu.VMEM((capacity, rows, n), F32)
     return pl.pallas_call(
         base_kernel,
-        grid=(capacity, cuts),
-        in_specs=[state, state],
-        out_specs=pl.BlockSpec((1, rows, n // cuts), lambda c, i: (c, 0, i)),
+        in_specs=[pl.BlockSpec(memory_space=pl.ANY)] * 2,
+        out_specs=pl.BlockSpec(memory_space=pltpu.VMEM),
         out_shape=jax.ShapeDtypeStruct((capacity, rows, n), BF16),
+        scratch_shapes=[state, state, pltpu.SemaphoreType.DMA((2, capacity * rows // BASE_ROWS))],
         compiler_params=params(),
         cost_estimate=cost(),
         name="base",
@@ -465,12 +514,12 @@
     upm = CORES * n_mp // nmat
     half = nmat // CORES
     code = core * n_mp + p
-
-    pos = jnp.stack([code // upm, code % upm, core, core * n_z + z, z, p, r * replica_rows % rows // replica_rows]).astype(jnp.int32)
+    first = r * replica_rows
+
+    pos = jnp.stack([code // upm, code % upm, core, core * n_z + z, z, p, first % rows // replica_rows, first // rows ^ p]).astype(jnp.int32)
     in_hbm = lambda x: pltpu.with_memory_space_constraint(x, pltpu.HBM)
-    momentum, master_weights = in_hbm(momentum), in_hbm(master_weights)
-
-    base = base_of(momentum, master_weights)
+
+    base = base_of(in_hbm(momentum), in_hbm(master_weights))
     bases = [base] + [exchange(base, "mp", d) for d in range(1, 3 if n_mp == 4 else n_mp)]
     places = {(d, c): (d, c) for d in range(len(bases)) for c in range(capacity)}
     early, cuts = bases[1:], []
@@ -487,21 +536,18 @@
         in_hbm(feedback),
         in_hbm(jnp.swapaxes(right_init, 1, 2)),
         vector_grads,
-        n_z,
     )
-    chip = near + exchange(far, "replica", 1)
-    piece = tree_sum([chip[0]] + [exchange(chip[d], "replica", CORES * d) for d in range(1, n_z)])
-    near = stack([piece] + [exchange(piece, "replica", CORES * d) for d in range(1, n_z)])
+    chip = add([near, exchange(far, "replica", 1)], BF16)
+    near = add([chip] + [exchange(chip, "replica", CORES * d) for d in range(1, n_z)], F32)
     far = exchange(near, "replica", 1)
 
     send, keep, lt, vector_rows = right_terms(pos, near, far, gram_root, comp, upm, early)
     vector_total = vector_rows.reshape(-1)[:nvec]
-    *chip, strip = chip_sum(pos, keep, exchange(send, "replica", 1), lt, replica_rows)
-    plane = [chip[0]] + [exchange(chip[d], "mp", d) for d in range(1, n_mp)]
-    strips = jnp.stack([strip] + [exchange(strip, "mp", d) for d in range(1, n_mp)])
-    ltr = lax.dynamic_index_in_dim(strips, (r * replica_rows // rows) ^ p, 0, keepdims=False)
-    final = plane_sum(pos, plane, n_z, early[: len(cuts)], cuts, ltr)
-    late = [exchange(part, "mp", 2 - i) for i, part in enumerate(final[n_z:])]
+    own, strip, *chip = chip_sum(pos, keep, exchange(send, "replica", 1), lt, replica_rows)
+    plane = [exchange(part, "mp", d) for d, part in enumerate(chip, 1)]
+    final = plane_sum(pos, own, strip, plane, n_z, nmat * rank, early[: len(cuts)], cuts)
+    final, forwards, ltr = final[:n_z], final[n_z:-1], final[-1]
+    late = [exchange(part, "mp", 2 - i) for i, part in enumerate(forwards)]
     bases += late
     final = [final[0]] + [exchange(final[d], "replica", CORES * d).astype(F32) for d in range(1, n_z)]
     final = tree_sum(final).astype(BF16)

time: 116 us -> 98 us (0.84)
  starting transfers between devices: 39.3 us -> 32.8 us
  Pallas kernels: 40.3 us -> 34.1 us
  local copies, waits for them, and re-layouts: 5.59 us -> 0.14 us
    ppermute x29 -> x23, starting transfers between devices: 39.3 us -> 32.8 us  [exchange(): return lax.ppermute(x, axis, [(i, i ^ distance) for i in range(size)])]
    unnamed x29 -> x15, local copies, waits for them, and re-layouts: 5.5 us -> 0.05 us
    pallas_call x3 -> x5, Pallas kernels: 7.52 us -> 4.24 us  [the longest x1 2.65 us: base_of(): pl.pallas_call(base_kernel, in_specs=[pl.BlockSpec(memory_space=pl.ANY)]...]
    pallas_call x2, Pallas kernels: 12.6 us -> 11 us  [outputs(): pl.pallas_call(functools.partial(outputs_kernel, start, places), grid_spe...]
    pallas_call x1, Pallas kernels: 4.82 us -> 3.27 us  [owned(): pl.pallas_call(owned_kernel, grid_spec=pltpu.PrefetchScalarGridSpec(num_s...]
    ppermute x29 -> x23, waiting for transfers between devices: 28.7 us -> 29.3 us  [exchange(): return lax.ppermute(x, axis, [(i, i ^ distance) for i in range(size)])]
  transfers between devices with their start and end apart: 29 -> 23, of which waited for: 15 -> 14; matrix products, arithmetic and copies ran while one was open for 1% -> 1% of each run, Pallas kernels for 17% -> 19%
where the time goes in v4:
time: 98 us; the launch traced here: 97.8 us
  Pallas kernels  34.1 us (35%)
  starting transfers between devices  32.8 us (33%)
  waiting for transfers between devices  29.3 us (30%)
    ppermute x23, starting transfers between devices, exchange(): return lax.ppermute(x, axis, [(i, i ^ distance) for i in range(size)])  32.8 us
    ppermute x23, waiting for transfers between devices, exchange(): return lax.ppermute(x, axis, [(i, i ^ distance) for i in range(size)])  29.3 us
    pallas_call x2, Pallas kernels, outputs(): pl.pallas_call(functools.partial(outputs_kernel, start, places), grid_spe...  11 us
    pallas_call x1, Pallas kernels, left_terms(): pl.pallas_call(left_kernel, grid_spec=pltpu.PrefetchScalarGridSpec(num_sc...  10.8 us
    pallas_call x1, Pallas kernels, owned(): pl.pallas_call(owned_kernel, grid_spec=pltpu.PrefetchScalarGridSpec(num_s...  3.27 us
    pallas_call x1, Pallas kernels, base_of(): pl.pallas_call(base_kernel, in_specs=[pl.BlockSpec(memory_space=pl.ANY)]...  2.65 us
    pallas_call x1, Pallas kernels, right_terms(): pl.pallas_call(functools.partial(send_kernel, half), grid_spec=pltpu.Pref...  2.37 us
  transfers between devices with their start and end apart: 23, of which 14 were waited for; matrix products, arithmetic and copies ran while one was open for 1% of the time, Pallas kernels for 19%

profile of v4, /device:TPU:1, one launch (start us, length us, event | category | flops | bytes accessed | tf_op | source)
XLA Modules:
  0.0 97.8 jit_solution(5214084539516269731)
XLA Ops:
  0.6 2.6 %base.1.refs_0_ = bf16[2,96,3072]{2,1,0:T(8,128)(2,1)S(1)} custom-call(f32[1,2,96,3072]{3,2,1,0:T(8,128)} %momentum_ref.3, f32[1,2,96,3072]{3,2,1,0:T(8,128)} %master_ref.3), custom_call_target="tpu_custom_call" | custom-call | flops 1000 | bytes 1000 | tf_op jit(solution)/shard_map/base/pallas_call | solution.py:463
  3.3 2.1 %collective-permute-start.5 = (bf16[2,96,3072]{2,1,0:T(8,128)(2,1)S(1)}, bf16[2,96,3072]{2,1,0:T(8,128)(2,1)S(1)}, u32[]{:S(2)}, u32[]{:S(2)}) collective-permute-start(bf16[2,96,3072]{2,1,0:T(8,128)(2,1)S(1)} %base.1.refs_0_), channel_id=1, source_target_pairs={{0,1},{1,0},{2,3},{3,2},{4,5},{5,4},{6,7},{7,6},{8,9},{9,8},{10,11... | collective-permute-start | bytes 3538952 | tf_op jit(solution)/shard_map/ppermute | solution.py:33
  5.4 1.2 %collective-permute-start.6 = (bf16[2,96,3072]{2,1,0:T(8,128)(2,1)S(1)}, bf16[2,96,3072]{2,1,0:T(8,128)(2,1)S(1)}, u32[]{:S(2)}, u32[]{:S(2)}) collective-permute-start(bf16[2,96,3072]{2,1,0:T(8,128)(2,1)S(1)} %base.1.refs_0_), channel_id=1, source_target_pairs={{0,2},{1,3},{2,0},{3,1},{4,6},{5,7},{6,4},{7,5},{8,10},{9,11},{10,... | collective-permute-start | bytes 3538952 | tf_op jit(solution)/shard_map/ppermute | solution.py:33
  6.7 10.8 %left_terms.1 = (bf16[8,192,3072]{2,1,0:T(8,128)(2,1)S(1)}, f32[112,256]{1,0:T(8,128)S(1)}, f32[112,256]{1,0:T(8,128)S(1)}) custom-call(s32[8]{0:T(128)S(1)} %stack.33.pos, bf16[1,8,192,3072]{3,2,1,0:T(8,128)(2,1)} %g_ref.1, bf16[1,8,192,3072]{3,2,1,0:T(8,128)(2,1)} %f_ref.1, bf16[8,32,3072]{2,1,0:T(8,128)(2,1)} %bitcast.15, f32[1,2688]{1,0:T(1,128)S(1)} %copy-done.3), custom_call_target="tpu_custom_call" | custom-call | flops 1000 | bytes 1000 | tf_op jit(solution)/shard_map/left_terms/pallas_call | solution.py:73
  17.5 1.3 %collective-permute-start = (f32[112,256]{1,0:T(8,128)S(1)}, f32[112,256]{1,0:T(8,128)S(1)}, u32[]{:S(2)}, u32[]{:S(2)}) collective-permute-start(f32[112,256]{1,0:T(8,128)S(1)} %get-tuple-element.32), channel_id=1, source_target_pairs={{0,4},{4,0},{8,12},{12,8},{16,20},{20,16},{24,28},{28,24},{1,5},{5... | collective-permute-start | bytes 344072 | tf_op jit(solution)/shard_map/ppermute | solution.py:33
  19.8 1.4 %collective-permute-start.1 = (bf16[112,256]{1,0:T(8,128)(2,1)S(1)}, bf16[112,256]{1,0:T(8,128)(2,1)S(1)}, u32[]{:S(2)}, u32[]{:S(2)}) collective-permute-start(bf16[112,256]{1,0:T(8,128)(2,1)S(1)} %add.45.refs_0_), channel_id=1, source_target_pairs={{0,8},{4,12},{8,0},{12,4},{16,24},{20,28},{24,16},{28,20},{1,9},{5... | collective-permute-start | bytes 172040 | tf_op jit(solution)/shard_map/ppermute | solution.py:33
  21.2 2.3 %collective-permute-start.2 = (bf16[112,256]{1,0:T(8,128)(2,1)S(1)}, bf16[112,256]{1,0:T(8,128)(2,1)S(1)}, u32[]{:S(2)}, u32[]{:S(2)}) collective-permute-start(bf16[112,256]{1,0:T(8,128)(2,1)S(1)} %add.45.refs_0_), channel_id=1, source_target_pairs={{0,16},{4,20},{8,24},{12,28},{16,0},{20,4},{24,8},{28,12},{1,17},{... | collective-permute-start | bytes 172040 | tf_op jit(solution)/shard_map/ppermute | solution.py:33
  23.5 2.0 %collective-permute-done.2.refs_2_ = bf16[112,256]{1,0:T(8,128)(2,1)S(1)} collective-permute-done((bf16[112,256]{1,0:T(8,128)(2,1)S(1)}, bf16[112,256]{1,0:T(8,128)(2,1)S(1)}, u32[]{:S(2)}, u32[]{:S(2)}) %collective-permute-start.2) | collective-permute-done | bytes 57376 | tf_op jit(solution)/shard_map/ppermute | solution.py:33
  25.4 3.0 %collective-permute-done.3.refs_3_ = bf16[112,256]{1,0:T(8,128)(2,1)S(1)} collective-permute-done((bf16[112,256]{1,0:T(8,128)(2,1)S(1)}, bf16[112,256]{1,0:T(8,128)(2,1)S(1)}, u32[]{:S(2)}, u32[]{:S(2)}) %collective-permute-start.3) | collective-permute-done | bytes 57376 | tf_op jit(solution)/shard_map/ppermute | solution.py:33
  28.4 2.0 %collective-permute-start.4 = (f32[112,256]{1,0:T(8,128)S(1)}, f32[112,256]{1,0:T(8,128)S(1)}, u32[]{:S(2)}, u32[]{:S(2)}) collective-permute-start(f32[112,256]{1,0:T(8,128)S(1)} %add.46.near_ref), channel_id=1, source_target_pairs={{0,4},{4,0},{8,12},{12,8},{16,20},{20,16},{24,28},{28,24},{1,5},{5... | collective-permute-start | bytes 344072 | tf_op jit(solution)/shard_map/ppermute | solution.py:33
  31.9 2.4 %right_send.1 = (bf16[4,1,32,3072]{3,2,1,0:T(8,128)(2,1)S(1)}, bf16[256,192]{1,0:T(8,128)(2,1)S(1)}, f32[32,256]{1,0:T(8,128)S(1)}) custom-call(s32[8]{0:T(128)S(1)} %stack.33.pos, f32[112,256]{1,0:T(8,128)S(1)} %add.46.near_ref, f32[112,256]{1,0:T(8,128)S(1)} %collective-permute-done.4.far_ref, f32[8,32,32]{2,1,0:T(8,128)S(1)} %copy-done.2, ...), custom_call_target="tpu_custom_call" | custom-call | flops 1000 | bytes 1000 | tf_op jit(solution)/shard_map/right_send/pallas_call | solution.py:157
  34.3 1.9 %collective-permute-start.7 = (bf16[4,1,32,3072]{3,2,1,0:T(8,128)(2,1)S(1)}, bf16[4,1,32,3072]{3,2,1,0:T(8,128)(2,1)S(1)}, u32[]{:S(2)}, u32[]{:S(2)}) collective-permute-start(bf16[4,1,32,3072]{3,2,1,0:T(8,128)(2,1)S(1)} %get-tuple-element.34), channel_id=1, source_target_pairs={{0,4},{4,0},{8,12},{12,8},{16,20},{20,16},{24,28},{28,24},{1,5},{5... | collective-permute-start | bytes 2359304 | tf_op jit(solution)/shard_map/ppermute | solution.py:33
  36.2 1.9 %right_keep.1.keep_ref = f32[4,1,32,3072]{3,2,1,0:T(8,128)S(1)} custom-call(s32[8]{0:T(128)S(1)} %stack.33.pos, bf16[256,192]{1,0:T(8,128)(2,1)S(1)} %get-tuple-element.33.lt_ref, bf16[8,192,3072]{2,1,0:T(8,128)(2,1)S(1)} %get-tuple-element.30.comp_ref), custom_call_target="tpu_custom_call" | custom-call | flops 1000 | bytes 18874368 | tf_op jit(solution)/shard_map/right_keep/pallas_call | solution.py:181
  39.1 1.4 %collective-permute-start.9 = (bf16[40,3072]{1,0:T(8,128)(2,1)S(1)}, bf16[40,3072]{1,0:T(8,128)(2,1)S(1)}, u32[]{:S(2)}, u32[]{:S(2)}) collective-permute-start(bf16[40,3072]{1,0:T(8,128)(2,1)S(1)} %get-tuple-element.38), channel_id=1, source_target_pairs={{0,2},{1,3},{2,0},{3,1},{4,6},{5,7},{6,4},{7,5},{8,10},{9,11},{10,... | collective-permute-start | bytes 737288 | tf_op jit(solution)/shard_map/ppermute | solution.py:33
  40.5 1.2 %collective-permute-start.10 = (bf16[40,3072]{1,0:T(8,128)(2,1)S(1)}, bf16[40,3072]{1,0:T(8,128)(2,1)S(1)}, u32[]{:S(2)}, u32[]{:S(2)}) collective-permute-start(bf16[40,3072]{1,0:T(8,128)(2,1)S(1)} %get-tuple-element.39), channel_id=1, source_target_pairs={{0,3},{1,2},{2,1},{3,0},{4,7},{5,6},{6,5},{7,4},{8,11},{9,10},{10,... | collective-permute-start | bytes 737288 | tf_op jit(solution)/shard_map/ppermute | solution.py:33
  41.7 4.5 %collective-permute-done.8.refs_0_ = bf16[40,3072]{1,0:T(8,128)(2,1)S(1)} collective-permute-done((bf16[40,3072]{1,0:T(8,128)(2,1)S(1)}, bf16[40,3072]{1,0:T(8,128)(2,1)S(1)}, u32[]{:S(2)}, u32[]{:S(2)}) %collective-permute-start.8) | collective-permute-done | bytes 245792 | tf_op jit(solution)/shard_map/ppermute | solution.py:33
  46.2 6.2 %collective-permute-done.10.refs_2_ = bf16[40,3072]{1,0:T(8,128)(2,1)S(1)} collective-permute-done((bf16[40,3072]{1,0:T(8,128)(2,1)S(1)}, bf16[40,3072]{1,0:T(8,128)(2,1)S(1)}, u32[]{:S(2)}, u32[]{:S(2)}) %collective-permute-start.10) | collective-permute-done | bytes 245792 | tf_op jit(solution)/shard_map/ppermute | solution.py:33
  53.5 1.2 %collective-permute-start.18 = (bf16[1,96,3072]{2,1,0:T(8,128)(2,1)S(1)}, bf16[1,96,3072]{2,1,0:T(8,128)(2,1)S(1)}, u32[]{:S(2)}, u32[]{:S(2)}) collective-permute-start(bf16[1,96,3072]{2,1,0:T(8,128)(2,1)S(1)} %get-tuple-element.45), channel_id=1, source_target_pairs={{0,1},{1,0},{2,3},{3,2},{4,5},{5,4},{6,7},{7,6},{8,9},{9,8},{10,11... | collective-permute-start | bytes 1769480 | tf_op jit(solution)/shard_map/ppermute | solution.py:33
  54.7 3.3 %collective-permute-start.13 = (bf16[32,768]{1,0:T(8,128)(2,1)S(1)}, bf16[32,768]{1,0:T(8,128)(2,1)S(1)}, u32[]{:S(2)}, u32[]{:S(2)}) collective-permute-start(bf16[32,768]{1,0:T(8,128)(2,1)S(1)} %get-tuple-element.43), channel_id=1, source_target_pairs={{0,24},{4,28},{8,16},{12,20},{16,8},{20,12},{24,0},{28,4},{1,25},{... | collective-permute-start | bytes 147464 | tf_op jit(solution)/shard_map/ppermute | solution.py:33
  58.3 1.2 %collective-permute-done.13 = bf16[32,768]{1,0:T(8,128)(2,1)S(1)} collective-permute-done((bf16[32,768]{1,0:T(8,128)(2,1)S(1)}, bf16[32,768]{1,0:T(8,128)(2,1)S(1)}, u32[]{:S(2)}, u32[]{:S(2)}) %collective-permute-start.13) | collective-permute-done | bytes 49184 | tf_op jit(solution)/shard_map/ppermute | solution.py:33
  59.5 2.9 %collective-permute-done.12 = bf16[32,768]{1,0:T(8,128)(2,1)S(1)} collective-permute-done((bf16[32,768]{1,0:T(8,128)(2,1)S(1)}, bf16[32,768]{1,0:T(8,128)(2,1)S(1)}, u32[]{:S(2)}, u32[]{:S(2)}) %collective-permute-start.12) | collective-permute-done | bytes 49184 | tf_op jit(solution)/shard_map/ppermute | solution.py:33
  62.5 1.4 %collective-permute-start.15 = (bf16[32,768]{1,0:T(8,128)(2,1)S(1)}, bf16[32,768]{1,0:T(8,128)(2,1)S(1)}, u32[]{:S(2)}, u32[]{:S(2)}) collective-permute-start(bf16[32,768]{1,0:T(8,128)(2,1)S(1)} %add_convert_fusion.refs_0_), channel_id=1, source_target_pairs={{0,16},{4,20},{8,24},{12,28},{16,0},{20,4},{24,8},{28,12},{1,17},{... | collective-permute-start | bytes 147464 | tf_op jit(solution)/shard_map/ppermute | solution.py:33
  63.9 2.1 %collective-permute-start.16 = (bf16[32,768]{1,0:T(8,128)(2,1)S(1)}, bf16[32,768]{1,0:T(8,128)(2,1)S(1)}, u32[]{:S(2)}, u32[]{:S(2)}) collective-permute-start(bf16[32,768]{1,0:T(8,128)(2,1)S(1)} %add_convert_fusion.refs_0_), channel_id=1, source_target_pairs={{0,24},{4,28},{8,16},{12,20},{16,8},{20,12},{24,0},{28,4},{1,25},{... | collective-permute-start | bytes 147464 | tf_op jit(solution)/shard_map/ppermute | solution.py:33
  66.4 2.3 %collective-permute-done.16.refs_3_ = bf16[32,768]{1,0:T(8,128)(2,1)S(1)} collective-permute-done((bf16[32,768]{1,0:T(8,128)(2,1)S(1)}, bf16[32,768]{1,0:T(8,128)(2,1)S(1)}, u32[]{:S(2)}, u32[]{:S(2)}) %collective-permute-start.16) | collective-permute-done | bytes 49184 | tf_op jit(solution)/shard_map/ppermute | solution.py:33
  69.7 1.3 %collective-permute-start.20 = (bf16[32,3072]{1,0:T(8,128)(2,1)S(1)}, bf16[32,3072]{1,0:T(8,128)(2,1)S(1)}, u32[]{:S(2)}, u32[]{:S(2)}) collective-permute-start(bf16[32,3072]{1,0:T(8,128)(2,1)S(1)} %column_gather.1.refs_0_), channel_id=1, source_target_pairs={{0,2},{1,3},{2,0},{3,1},{4,6},{5,7},{6,4},{7,5},{8,10},{9,11},{10,... | collective-permute-start | bytes 589832 | tf_op jit(solution)/shard_map/ppermute | solution.py:33
  71.0 1.0 %collective-permute-start.21 = (bf16[32,3072]{1,0:T(8,128)(2,1)S(1)}, bf16[32,3072]{1,0:T(8,128)(2,1)S(1)}, u32[]{:S(2)}, u32[]{:S(2)}) collective-permute-start(bf16[32,3072]{1,0:T(8,128)(2,1)S(1)} %column_gather.1.refs_0_), channel_id=1, source_target_pairs={{0,3},{1,2},{2,1},{3,0},{4,7},{5,6},{6,5},{7,4},{8,11},{9,10},{10,... | collective-permute-start | bytes 589832 | tf_op jit(solution)/shard_map/ppermute | solution.py:33
  72.0 1.9 %collective-permute-done.19.refs_1_ = bf16[32,3072]{1,0:T(8,128)(2,1)S(1)} collective-permute-done((bf16[32,3072]{1,0:T(8,128)(2,1)S(1)}, bf16[32,3072]{1,0:T(8,128)(2,1)S(1)}, u32[]{:S(2)}, u32[]{:S(2)}) %collective-permute-start.19) | collective-permute-done | bytes 196640 | tf_op jit(solution)/shard_map/ppermute | solution.py:33
  73.9 1.8 %collective-permute-done.20.refs_2_ = bf16[32,3072]{1,0:T(8,128)(2,1)S(1)} collective-permute-done((bf16[32,3072]{1,0:T(8,128)(2,1)S(1)}, bf16[32,3072]{1,0:T(8,128)(2,1)S(1)}, u32[]{:S(2)}, u32[]{:S(2)}) %collective-permute-start.20) | collective-permute-done | bytes 196640 | tf_op jit(solution)/shard_map/ppermute | solution.py:33
  76.5 6.4 %collective-permute-start.22 = (bf16[4,1,32,3072]{3,2,1,0:T(8,128)(2,1)S(1)}, bf16[4,1,32,3072]{3,2,1,0:T(8,128)(2,1)S(1)}, u32[]{:S(2)}, u32[]{:S(2)}) collective-permute-start(bf16[4,1,32,3072]{3,2,1,0:T(8,128)(2,1)S(1)} %bitcast.11), channel_id=1, source_target_pairs={{0,4},{4,0},{8,12},{12,8},{16,20},{20,16},{24,28},{28,24},{1,5},{5... | collective-permute-start | bytes 2359304 | tf_op jit(solution)/shard_map/ppermute | solution.py:33
  83.5 5.5 %outputs.2 = (bf16[1,8,192,3072]{3,2,1,0:T(8,128)(2,1)}, bf16[8,96,3072]{2,1,0:T(8,128)(2,1)}) custom-call(s32[8]{0:T(128)S(1)} %stack.33.pos, s32[8]{0:T(128)S(1)} %copy-done.4, bf16[8,192,3072]{2,1,0:T(8,128)(2,1)S(1)} %get-tuple-element.30.comp_ref, bf16[4,1,32,3072]{3,2,1,0:T(8,128)(2,1)S(1)} %bitcast.12, bf16[256,192]{1,0:T(8,128)(2,1)S(1)} %get-tuple-element.33.lt_ref, ...), custom_call_target="tpu_custom_call" | custom-call | flops 1000 | bytes 1000 | tf_op jit(solution)/shard_map/outputs/pallas_call | solution.py:373
  89.1 3.3 %owned.1 = (f32[1,2,96,3072]{3,2,1,0:T(8,128)}, f32[1,2,96,3072]{3,2,1,0:T(8,128)}) custom-call(s32[8]{0:T(128)S(1)} %stack.33.pos, s32[8]{0:T(128)S(1)} %copy-done.4, f32[1,2,96,3072]{3,2,1,0:T(8,128)S(1)} %copy-done, f32[1,2,96,3072]{3,2,1,0:T(8,128)S(1)} %copy-done.1, bf16[4,1,32,3072]{3,2,1,0:T(8,128)(2,1)S(1)} %bitcast.13, ...), custom_call_target="tpu_custom_call" | custom-call | flops 1000 | bytes 1000 | tf_op jit(solution)/shard_map/owned/pallas_call | solution.py:423
  92.3 5.5 %outputs.3 = (bf16[1,8,192,3072]{3,2,1,0:T(8,128)(2,1)}, bf16[8,96,3072]{2,1,0:T(8,128)(2,1)}) custom-call(s32[8]{0:T(128)S(1)} %stack.33.pos, s32[8]{0:T(128)S(1)} %copy-done.4, bf16[8,192,3072]{2,1,0:T(8,128)(2,1)S(1)} %get-tuple-element.30.comp_ref, ...), custom_call_target="tpu_custom_call", output_to_operand_aliasing={{0}: (11, {}), {1}: (12, {})} | custom-call | flops 1000 | bytes 1000 | tf_op jit(solution)/shard_map/outputs/pallas_call | solution.py:373
  (45 shorter events, 7.7 us)
Async XLA Ops:
  0.6 6.1 %copy-start.3 = (f32[1,2688]{1,0:T(1,128)S(1)}, f32[1,2688]{1,0:T(1,128)}, u32[]{:S(2)}) copy-start(f32[1,2688]{1,0:T(1,128)} %vec_ref.1) | copy-start | bytes 32260
  3.3 28.1 %collective-permute-start.5 = (bf16[2,96,3072]{2,1,0:T(8,128)(2,1)S(1)}, bf16[2,96,3072]{2,1,0:T(8,128)(2,1)S(1)}, u32[]{:S(2)}, u32[]{:S(2)}) collective-permute-start(bf16[2,96,3072]{2,1,0:T(8,128)(2,1)S(1)} %base.1.refs_0_), channel_id=1, source_target_pairs={{0,1},{1,0},{2,3},{3,2},{4,5},{5,4},{6,7},{7,6},{8,9},{9,8},{10,11... | collective-permute-start | bytes 3538952 | tf_op jit(solution)/shard_map/ppermute | solution.py:33
  5.4 26.5 %collective-permute-start.6 = (bf16[2,96,3072]{2,1,0:T(8,128)(2,1)S(1)}, bf16[2,96,3072]{2,1,0:T(8,128)(2,1)S(1)}, u32[]{:S(2)}, u32[]{:S(2)}) collective-permute-start(bf16[2,96,3072]{2,1,0:T(8,128)(2,1)S(1)} %base.1.refs_0_), channel_id=1, source_target_pairs={{0,2},{1,3},{2,0},{3,1},{4,6},{5,7},{6,4},{7,5},{8,10},{9,11},{10,... | collective-permute-start | bytes 3538952 | tf_op jit(solution)/shard_map/ppermute | solution.py:33
  6.7 25.2 %copy-start.2 = (f32[8,32,32]{2,1,0:T(8,128)S(1)}, f32[8,32,32]{2,1,0:T(8,128)}, u32[]{:S(2)}) copy-start(f32[8,32,32]{2,1,0:T(8,128)} %gram_ref.1) | copy-start | bytes 98308
  17.5 2.3 %collective-permute-start = (f32[112,256]{1,0:T(8,128)S(1)}, f32[112,256]{1,0:T(8,128)S(1)}, u32[]{:S(2)}, u32[]{:S(2)}) collective-permute-start(f32[112,256]{1,0:T(8,128)S(1)} %get-tuple-element.32), channel_id=1, source_target_pairs={{0,4},{4,0},{8,12},{12,8},{16,20},{20,16},{24,28},{28,24},{1,5},{5... | collective-permute-start | bytes 344072 | tf_op jit(solution)/shard_map/ppermute | solution.py:33
  19.8 3.7 %collective-permute-start.1 = (bf16[112,256]{1,0:T(8,128)(2,1)S(1)}, bf16[112,256]{1,0:T(8,128)(2,1)S(1)}, u32[]{:S(2)}, u32[]{:S(2)}) collective-permute-start(bf16[112,256]{1,0:T(8,128)(2,1)S(1)} %add.45.refs_0_), channel_id=1, source_target_pairs={{0,8},{4,12},{8,0},{12,4},{16,24},{20,28},{24,16},{28,20},{1,9},{5... | collective-permute-start | bytes 172040 | tf_op jit(solution)/shard_map/ppermute | solution.py:33
  21.2 4.3 %collective-permute-start.2 = (bf16[112,256]{1,0:T(8,128)(2,1)S(1)}, bf16[112,256]{1,0:T(8,128)(2,1)S(1)}, u32[]{:S(2)}, u32[]{:S(2)}) collective-permute-start(bf16[112,256]{1,0:T(8,128)(2,1)S(1)} %add.45.refs_0_), channel_id=1, source_target_pairs={{0,16},{4,20},{8,24},{12,28},{16,0},{20,4},{24,8},{28,12},{1,17},{... | collective-permute-start | bytes 172040 | tf_op jit(solution)/shard_map/ppermute | solution.py:33
  23.5 4.9 %collective-permute-start.3 = (bf16[112,256]{1,0:T(8,128)(2,1)S(1)}, bf16[112,256]{1,0:T(8,128)(2,1)S(1)}, u32[]{:S(2)}, u32[]{:S(2)}) collective-permute-start(bf16[112,256]{1,0:T(8,128)(2,1)S(1)} %add.45.refs_0_), channel_id=1, source_target_pairs={{0,24},{4,28},{8,16},{12,20},{16,8},{20,12},{24,0},{28,4},{1,25},{... | collective-permute-start | bytes 172040 | tf_op jit(solution)/shard_map/ppermute | solution.py:33
  28.4 3.0 %collective-permute-start.4 = (f32[112,256]{1,0:T(8,128)S(1)}, f32[112,256]{1,0:T(8,128)S(1)}, u32[]{:S(2)}, u32[]{:S(2)}) collective-permute-start(f32[112,256]{1,0:T(8,128)S(1)} %add.46.near_ref), channel_id=1, source_target_pairs={{0,4},{4,0},{8,12},{12,8},{16,20},{20,16},{24,28},{28,24},{1,5},{5... | collective-permute-start | bytes 344072 | tf_op jit(solution)/shard_map/ppermute | solution.py:33
  34.3 3.8 %collective-permute-start.7 = (bf16[4,1,32,3072]{3,2,1,0:T(8,128)(2,1)S(1)}, bf16[4,1,32,3072]{3,2,1,0:T(8,128)(2,1)S(1)}, u32[]{:S(2)}, u32[]{:S(2)}) collective-permute-start(bf16[4,1,32,3072]{3,2,1,0:T(8,128)(2,1)S(1)} %get-tuple-element.34), channel_id=1, source_target_pairs={{0,4},{4,0},{8,12},{12,8},{16,20},{20,16},{24,28},{28,24},{1,5},{5... | collective-permute-start | bytes 2359304 | tf_op jit(solution)/shard_map/ppermute | solution.py:33
  38.9 7.2 %collective-permute-start.8 = (bf16[40,3072]{1,0:T(8,128)(2,1)S(1)}, bf16[40,3072]{1,0:T(8,128)(2,1)S(1)}, u32[]{:S(2)}, u32[]{:S(2)}) collective-permute-start(bf16[40,3072]{1,0:T(8,128)(2,1)S(1)} %get-tuple-element.37), channel_id=1, source_target_pairs={{0,1},{1,0},{2,3},{3,2},{4,5},{5,4},{6,7},{7,6},{8,9},{9,8},{10,11... | collective-permute-start | bytes 737288 | tf_op jit(solution)/shard_map/ppermute | solution.py:33
  39.1 7.1 %collective-permute-start.9 = (bf16[40,3072]{1,0:T(8,128)(2,1)S(1)}, bf16[40,3072]{1,0:T(8,128)(2,1)S(1)}, u32[]{:S(2)}, u32[]{:S(2)}) collective-permute-start(bf16[40,3072]{1,0:T(8,128)(2,1)S(1)} %get-tuple-element.38), channel_id=1, source_target_pairs={{0,2},{1,3},{2,0},{3,1},{4,6},{5,7},{6,4},{7,5},{8,10},{9,11},{10,... | collective-permute-start | bytes 737288 | tf_op jit(solution)/shard_map/ppermute | solution.py:33
  40.5 11.9 %collective-permute-start.10 = (bf16[40,3072]{1,0:T(8,128)(2,1)S(1)}, bf16[40,3072]{1,0:T(8,128)(2,1)S(1)}, u32[]{:S(2)}, u32[]{:S(2)}) collective-permute-start(bf16[40,3072]{1,0:T(8,128)(2,1)S(1)} %get-tuple-element.39), channel_id=1, source_target_pairs={{0,3},{1,2},{2,1},{3,0},{4,7},{5,6},{6,5},{7,4},{8,11},{9,10},{10,... | collective-permute-start | bytes 737288 | tf_op jit(solution)/shard_map/ppermute | solution.py:33
  53.1 29.8 %copy-start.5 = (f32[2688]{0:T(1024)S(1)}, f32[2688]{0:T(1024)}, u32[]{:S(2)}) copy-start(f32[2688]{0:T(1024)} %param.19) | copy-start | bytes 32260
  53.2 29.8 %copy-start.6 = (f32[2688]{0:T(1024)S(1)}, f32[2688]{0:T(1024)}, u32[]{:S(2)}) copy-start(f32[2688]{0:T(1024)} %param.18) | copy-start | bytes 32260
  53.2 30.4 %copy-start.4 = (s32[8]{0:T(128)S(1)}, s32[8]{0:T(128)}, u32[]{:S(2)}) copy-start(s32[8]{0:T(128)} %owners.5) | copy-start | bytes 100
  53.2 15.5 %collective-permute-start.17 = (bf16[1,96,3072]{2,1,0:T(8,128)(2,1)S(1)}, bf16[1,96,3072]{2,1,0:T(8,128)(2,1)S(1)}, u32[]{:S(2)}, u32[]{:S(2)}) collective-permute-start(bf16[1,96,3072]{2,1,0:T(8,128)(2,1)S(1)} %get-tuple-element.44), channel_id=1, source_target_pairs={{0,2},{1,3},{2,0},{3,1},{4,6},{5,7},{6,4},{7,5},{8,10},{9,11},{10,... | collective-permute-start | bytes 1769480 | tf_op jit(solution)/shard_map/ppermute | solution.py:33
  53.5 15.2 %collective-permute-start.18 = (bf16[1,96,3072]{2,1,0:T(8,128)(2,1)S(1)}, bf16[1,96,3072]{2,1,0:T(8,128)(2,1)S(1)}, u32[]{:S(2)}, u32[]{:S(2)}) collective-permute-start(bf16[1,96,3072]{2,1,0:T(8,128)(2,1)S(1)} %get-tuple-element.45), channel_id=1, source_target_pairs={{0,1},{1,0},{2,3},{3,2},{4,5},{5,4},{6,7},{7,6},{8,9},{9,8},{10,11... | collective-permute-start | bytes 1769480 | tf_op jit(solution)/shard_map/ppermute | solution.py:33
  54.7 4.8 %collective-permute-start.13 = (bf16[32,768]{1,0:T(8,128)(2,1)S(1)}, bf16[32,768]{1,0:T(8,128)(2,1)S(1)}, u32[]{:S(2)}, u32[]{:S(2)}) collective-permute-start(bf16[32,768]{1,0:T(8,128)(2,1)S(1)} %get-tuple-element.43), channel_id=1, source_target_pairs={{0,24},{4,28},{8,16},{12,20},{16,8},{20,12},{24,0},{28,4},{1,25},{... | collective-permute-start | bytes 147464 | tf_op jit(solution)/shard_map/ppermute | solution.py:33
  58.0 4.4 %collective-permute-start.12 = (bf16[32,768]{1,0:T(8,128)(2,1)S(1)}, bf16[32,768]{1,0:T(8,128)(2,1)S(1)}, u32[]{:S(2)}, u32[]{:S(2)}) collective-permute-start(bf16[32,768]{1,0:T(8,128)(2,1)S(1)} %get-tuple-element.42), channel_id=1, source_target_pairs={{0,16},{4,20},{8,24},{12,28},{16,0},{20,4},{24,8},{28,12},{1,17},{... | collective-permute-start | bytes 147464 | tf_op jit(solution)/shard_map/ppermute | solution.py:33
  58.0 4.4 %collective-permute-start.11 = (bf16[32,768]{1,0:T(8,128)(2,1)S(1)}, bf16[32,768]{1,0:T(8,128)(2,1)S(1)}, u32[]{:S(2)}, u32[]{:S(2)}) collective-permute-start(bf16[32,768]{1,0:T(8,128)(2,1)S(1)} %get-tuple-element.41), channel_id=1, source_target_pairs={{0,8},{4,12},{8,0},{12,4},{16,24},{20,28},{24,16},{28,20},{1,9},{5... | collective-permute-start | bytes 147464 | tf_op jit(solution)/shard_map/ppermute | solution.py:33
  62.4 3.6 %collective-permute-start.14 = (bf16[32,768]{1,0:T(8,128)(2,1)S(1)}, bf16[32,768]{1,0:T(8,128)(2,1)S(1)}, u32[]{:S(2)}, u32[]{:S(2)}) collective-permute-start(bf16[32,768]{1,0:T(8,128)(2,1)S(1)} %add_convert_fusion.refs_0_), channel_id=1, source_target_pairs={{0,8},{4,12},{8,0},{12,4},{16,24},{20,28},{24,16},{28,20},{1,9},{5... | collective-permute-start | bytes 147464 | tf_op jit(solution)/shard_map/ppermute | solution.py:33
  62.5 3.9 %collective-permute-start.15 = (bf16[32,768]{1,0:T(8,128)(2,1)S(1)}, bf16[32,768]{1,0:T(8,128)(2,1)S(1)}, u32[]{:S(2)}, u32[]{:S(2)}) collective-permute-start(bf16[32,768]{1,0:T(8,128)(2,1)S(1)} %add_convert_fusion.refs_0_), channel_id=1, source_target_pairs={{0,16},{4,20},{8,24},{12,28},{16,0},{20,4},{24,8},{28,12},{1,17},{... | collective-permute-start | bytes 147464 | tf_op jit(solution)/shard_map/ppermute | solution.py:33
  63.9 4.8 %collective-permute-start.16 = (bf16[32,768]{1,0:T(8,128)(2,1)S(1)}, bf16[32,768]{1,0:T(8,128)(2,1)S(1)}, u32[]{:S(2)}, u32[]{:S(2)}) collective-permute-start(bf16[32,768]{1,0:T(8,128)(2,1)S(1)} %add_convert_fusion.refs_0_), channel_id=1, source_target_pairs={{0,24},{4,28},{8,16},{12,20},{16,8},{20,12},{24,0},{28,4},{1,25},{... | collective-permute-start | bytes 147464 | tf_op jit(solution)/shard_map/ppermute | solution.py:33
  69.3 4.6 %collective-permute-start.19 = (bf16[32,3072]{1,0:T(8,128)(2,1)S(1)}, bf16[32,3072]{1,0:T(8,128)(2,1)S(1)}, u32[]{:S(2)}, u32[]{:S(2)}) collective-permute-start(bf16[32,3072]{1,0:T(8,128)(2,1)S(1)} %column_gather.1.refs_0_), channel_id=1, source_target_pairs={{0,1},{1,0},{2,3},{3,2},{4,5},{5,4},{6,7},{7,6},{8,9},{9,8},{10,11... | collective-permute-start | bytes 589832 | tf_op jit(solution)/shard_map/ppermute | solution.py:33
  69.7 6.0 %collective-permute-start.20 = (bf16[32,3072]{1,0:T(8,128)(2,1)S(1)}, bf16[32,3072]{1,0:T(8,128)(2,1)S(1)}, u32[]{:S(2)}, u32[]{:S(2)}) collective-permute-start(bf16[32,3072]{1,0:T(8,128)(2,1)S(1)} %column_gather.1.refs_0_), channel_id=1, source_target_pairs={{0,2},{1,3},{2,0},{3,1},{4,6},{5,7},{6,4},{7,5},{8,10},{9,11},{10,... | collective-permute-start | bytes 589832 | tf_op jit(solution)/shard_map/ppermute | solution.py:33
  71.0 5.4 %collective-permute-start.21 = (bf16[32,3072]{1,0:T(8,128)(2,1)S(1)}, bf16[32,3072]{1,0:T(8,128)(2,1)S(1)}, u32[]{:S(2)}, u32[]{:S(2)}) collective-permute-start(bf16[32,3072]{1,0:T(8,128)(2,1)S(1)} %column_gather.1.refs_0_), channel_id=1, source_target_pairs={{0,3},{1,2},{2,1},{3,0},{4,7},{5,6},{6,5},{7,4},{8,11},{9,10},{10,... | collective-permute-start | bytes 589832 | tf_op jit(solution)/shard_map/ppermute | solution.py:33
  76.5 12.6 %collective-permute-start.22 = (bf16[4,1,32,3072]{3,2,1,0:T(8,128)(2,1)S(1)}, bf16[4,1,32,3072]{3,2,1,0:T(8,128)(2,1)S(1)}, u32[]{:S(2)}, u32[]{:S(2)}) collective-permute-start(bf16[4,1,32,3072]{3,2,1,0:T(8,128)(2,1)S(1)} %bitcast.11), channel_id=1, source_target_pairs={{0,4},{4,0},{8,12},{12,8},{16,20},{20,16},{24,28},{28,24},{1,5},{5... | collective-permute-start | bytes 2359304 | tf_op jit(solution)/shard_map/ppermute | solution.py:33
  83.5 5.5 %copy-start = (f32[1,2,96,3072]{3,2,1,0:T(8,128)S(1)}, f32[1,2,96,3072]{3,2,1,0:T(8,128)}, u32[]{:S(2)}) copy-start(f32[1,2,96,3072]{3,2,1,0:T(8,128)} %momentum_ref.3) | copy-start | bytes 7077892
  83.5 5.5 %copy-start.1 = (f32[1,2,96,3072]{3,2,1,0:T(8,128)S(1)}, f32[1,2,96,3072]{3,2,1,0:T(8,128)}, u32[]{:S(2)}) copy-start(f32[1,2,96,3072]{3,2,1,0:T(8,128)} %master_ref.3) | copy-start | bytes 7077892

commit v5 on v4

v5 whole, which is shorter than its diff:
```python
import functools

import jax
import jax.numpy as jnp
from jax import lax
from jax.experimental import pallas as pl
from jax.experimental.pallas import tpu as pltpu
from jax.sharding import PartitionSpec as P

CORES = 2
AHEAD = 3
BASE_ROWS = 16
COLUMNS = 512
F32 = jnp.float32
BF16 = jnp.bfloat16


def params(mib=12):
    return pltpu.CompilerParams(vmem_limit_bytes=mib * 1024 * 1024)


def cost(bytes_accessed=1000):
    return pl.CostEstimate(flops=1000, bytes_accessed=bytes_accessed, transcendentals=0)


def tree_sum(terms):
    while len(terms) > 1:
        terms = [terms[i] + terms[i + 1] for i in range(0, len(terms), 2)]
    return terms[0]


def exchange(x, axis, distance):
    size = lax.axis_size(axis)
    return lax.ppermute(x, axis, [(i, i ^ distance) for i in range(size)])


def left_kernel(pos, g_ref, f_ref, q_ref, vec_ref, comp_ref, near_ref, far_ref, total, feedback, right, sems):
    nmat, rows, _ = comp_ref.shape
    rank = q_ref.shape[1]
    part = near_ref.shape[0]
    cut = rows // 2 if rows % 32 == 0 else rows

    def copies(k):
        out = [pltpu.make_async_copy(q_ref.at[k], right.at[k], sems.at[k, 4])]
        for i, first in enumerate(range(0, rows, cut)):
            block = pl.ds(first, cut)
            for j, (source, target) in enumerate(((g_ref, comp_ref), (f_ref, feedback))):
                source, target = source.at[0, k, block], target.at[k, block]
                out.append(pltpu.make_async_copy(source, target, sems.at[k, 2 * i + j]))
        return out

    for k in range(min(AHEAD, nmat)):
        for copy in copies(k):
            copy.start()
    total[...] = jnp.zeros(total.shape, F32)
    width, nvec = total.shape[1], vec_ref.shape[1]
    for i, first in enumerate(range(0, nvec, width)):
        count = min(width, nvec - first)
        total[rows + i : rows + i + 1, :count] = vec_ref[:, first : first + count]

    for k in range(nmat):
        for copy in copies(k):
            copy.wait()
        if k + AHEAD < nmat:
            for copy in copies(k + AHEAD):
                copy.start()
        comp = comp_ref[k] + feedback[k]
        comp_ref[k] = comp
        total[:rows, k * rank : (k + 1) * rank] = lax.dot_general(
            comp, right[k], (((1,), (1,)), ((), ())), preferred_element_type=F32
        )

    for ref, core in ((near_ref, pos[2]), (far_ref, 1 - pos[2])):
        ref[...] = total[pl.ds(pl.multiple_of(core * part, 16), part), :]


def left_terms(pos, gradients, feedback, right_t, vec):
    _, nmat, rows, n = gradients.shape
    rank = right_t.shape[1]
    width = nmat * rank
    total = rows + -(-vec.shape[1] // width)
    total += -total % (16 * CORES)
    part = jax.ShapeDtypeStruct((total // CORES, width), F32)
    vmem = pl.BlockSpec(memory_space=pltpu.VMEM)
    any_spec = pl.BlockSpec(memory_space=pl.ANY)
    return pl.pallas_call(
        left_kernel,
        grid_spec=pltpu.PrefetchScalarGridSpec(
            num_scalar_prefetch=1,
            grid=(1,),
            in_specs=[any_spec] * 3 + [vmem],
            out_specs=[vmem] * 3,
            scratch_shapes=[
                pltpu.VMEM((total, width), F32),
                pltpu.VMEM((nmat, rows, n), BF16),
                pltpu.VMEM((nmat, rank, n), BF16),
                pltpu.SemaphoreType.DMA((nmat, 5)),
            ],
        ),
        out_shape=[jax.ShapeDtypeStruct((nmat, rows, n), BF16), part, part],
        compiler_params=params(20),
        cost_estimate=cost(),
        name="left_terms",
    )(pos, gradients, feedback, right_t, vec)


def add_kernel(copies, *refs):
    out = refs[-1]
    parts = [ref[...].astype(F32) for ref in refs[:-1]]
    if len(parts) == 1:
        parts = [refs[0][i].astype(F32) for i in range(refs[0].shape[0])]
    total = tree_sum(parts).astype(out.dtype)
    if copies:
        for i in range(copies):
            out[i] = total
    else:
        out[...] = total


def add(parts, dtype, copies=0):
    vmem = pl.BlockSpec(memory_space=pltpu.VMEM)
    shape = parts[0].shape if len(parts) > 1 else parts[0].shape[1:]
    shape = (copies,) + shape if copies else shape
    return pl.pallas_call(
        functools.partial(add_kernel, copies),
        in_specs=[vmem] * len(parts),
        out_specs=vmem,
        out_shape=jax.ShapeDtypeStruct(shape, dtype),
        compiler_params=params(),
        cost_estimate=cost(),
        name="add",
    )(*parts)


def send_kernel(half, pos, near_ref, far_ref, gram_ref, comp_ref, *refs):
    send_ref, lt_ref, vec_ref, left, gram = refs[-5:]
    t = pl.program_id(0)
    rows = comp_ref.shape[1]
    rank = gram_ref.shape[1]

    @pl.when(t == 0)
    def _():
        part = near_ref.shape[0]
        for ref, core in ((near_ref, pos[2]), (far_ref, 1 - pos[2])):
            left[pl.ds(pl.multiple_of(core * part, 16), part), :] = ref[...]
        vec_ref[...] = left[rows:, :]
        gram[...] = jnp.zeros(gram.shape, F32)
        for i in range(gram_ref.shape[0]):
            gram[i * rank : (i + 1) * rank, i * rank : (i + 1) * rank] = gram_ref[i]
        hat = jnp.dot(
            left[:rows, :], gram[...], precision=lax.Precision.HIGHEST, preferred_element_type=F32
        )
        lt_ref[...] = hat.T.astype(BF16)

    right_rows((1 - pos[2]) * half, lt_ref, comp_ref, send_ref)


def right_rows(start, lt_ref, comp_ref, out_ref):
    upm, unit = out_ref.shape[1], out_ref.shape[2]
    k = pl.program_id(0) + start
    rows = pl.ds(pl.multiple_of(k * upm * unit, upm * unit), upm * unit)
    terms = jnp.dot(lt_ref[rows, :], comp_ref[k], preferred_element_type=F32)
    for i in range(upm):
        out_ref[0, i] = terms[i * unit : (i + 1) * unit].astype(out_ref.dtype)


def keep_kernel(half, pos, lt_ref, comp_ref, keep_ref):
    right_rows(pos[2] * half, lt_ref, comp_ref, keep_ref)


def right_terms(pos, near, far, gram, comp, upm):
    nmat, rows, n = comp.shape
    rank = gram.shape[1]
    width = nmat * rank
    half = nmat // CORES
    total = CORES * near.shape[0]
    shape = (half, upm, rank // upm, n)
    vmem = pl.BlockSpec(memory_space=pltpu.VMEM)
    out = pl.BlockSpec((1,) + shape[1:], lambda t, pos: (t, 0, 0, 0))
    send, lt, vec = pl.pallas_call(
        functools.partial(send_kernel, half),
        grid_spec=pltpu.PrefetchScalarGridSpec(
            num_scalar_prefetch=1,
            grid=(half,),
            in_specs=[
                vmem,
                vmem,
                vmem,
                vmem,
            ],
            out_specs=[out, vmem, vmem],
            scratch_shapes=[pltpu.VMEM((total, width), F32), pltpu.VMEM((width, width), F32)],
        ),
        out_shape=[
            jax.ShapeDtypeStruct(shape, BF16),
            jax.ShapeDtypeStruct((width, rows), BF16),
            jax.ShapeDtypeStruct((total - rows, width), F32),
        ],
        compiler_params=params(),
        cost_estimate=cost(),
        name="right_send",
    )(pos, near, far, gram, comp)
    keep = pl.pallas_call(
        functools.partial(keep_kernel, half),
        grid_spec=pltpu.PrefetchScalarGridSpec(
            num_scalar_prefetch=1,
            grid=(half,),
            in_specs=[vmem, vmem],
            out_specs=out,
        ),
        out_shape=jax.ShapeDtypeStruct(shape, F32),
        compiler_params=params(),
        cost_estimate=cost(4 * nmat * rows * n),
        name="right_keep",
    )(pos, lt, comp)
    return send, keep, lt, vec


def chip_kernel(replica_rows, pos, keep_ref, recv_ref, lt_ref, *refs):
    out_ref = refs[-1]
    upm = keep_ref.shape[1]
    count, height, n = out_ref.shape
    height -= keep_ref.shape[2]
    left = lt_ref[...].astype(F32).T
    strip = left[:replica_rows]
    for i in range(1, left.shape[0] // replica_rows):
        strip = jnp.where(pos[3] == i, left[i * replica_rows : (i + 1) * replica_rows], strip)
    strip = jnp.concatenate(
        [strip[i * height : (i + 1) * height] for i in range(replica_rows // height)], axis=1
    )
    for i in range(count):
        terms = keep_ref[i // upm, i % upm] + recv_ref[i // upm, i % upm].astype(F32)
        out_ref[i] = jnp.concatenate([terms, strip], axis=0).astype(BF16)


def chip_sum(pos, keep, recv, lt, replica_rows, after):
    half, upm, unit, n = keep.shape
    height = lt.shape[0] * replica_rows // n
    vmem = pl.BlockSpec(memory_space=pltpu.VMEM)
    return pl.pallas_call(
        functools.partial(chip_kernel, replica_rows),
        grid_spec=pltpu.PrefetchScalarGridSpec(
            num_scalar_prefetch=1,
            grid=(1,),
            in_specs=[vmem] * 3 + [pl.BlockSpec(memory_space=pl.ANY)] * len(after),
            out_specs=vmem,
        ),
        out_shape=jax.ShapeDtypeStruct((half * upm, unit + height, n), BF16),
        compiler_params=params(),
        cost_estimate=cost(),
        name="chip_sum",
    )(pos, keep, recv, lt, *after)


def plane_kernel(cuts, pos, terms_ref, *refs):
    wholes, (out_ref, ltr_ref, *forwards) = refs[: len(cuts)], refs[len(cuts) :]
    n_z, unit, cols = out_ref.shape
    for z in range(n_z):
        block = slice(z * cols, (z + 1) * cols)
        parts = [terms_ref[i, :, block].astype(F32)[:unit] for i in range(terms_ref.shape[0])]
        out_ref[z] = tree_sum(parts).astype(BF16)
    strip = terms_ref[pos[4]].astype(F32)[unit:]
    width = ltr_ref.shape[0]
    rows = [strip[:, i * width : (i + 1) * width] for i in range(strip.shape[1] // width)]
    ltr_ref[...] = jnp.concatenate(rows, axis=0).T.astype(BF16)
    for whole, out, first in zip(wholes, forwards, cuts):
        out[...] = whole[first : first + out.shape[0]]


def plane_sum(pos, terms, unit, n_z, width, wholes, cuts):
    _, height, n = terms.shape
    outs = [
        jax.ShapeDtypeStruct((n_z, unit, n // n_z), BF16),
        jax.ShapeDtypeStruct((width, (height - unit) * n // width), BF16),
    ]
    outs += [jax.ShapeDtypeStruct((x.shape[0] // 2,) + x.shape[1:], x.dtype) for x in wholes]
    vmem = pl.BlockSpec(memory_space=pltpu.VMEM)
    return pl.pallas_call(
        functools.partial(plane_kernel, cuts),
        grid_spec=pltpu.PrefetchScalarGridSpec(
            num_scalar_prefetch=1,
            grid=(1,),
            in_specs=[vmem] * (1 + len(wholes)),
            out_specs=[vmem] * len(outs),
        ),
        out_shape=outs,
        compiler_params=params(),
        cost_estimate=cost(),
        name="plane_sum",
    )(pos, terms, *wholes)


def column_kernel(parts_ref, *refs):
    out_ref = refs[-1]
    cols = parts_ref.shape[2]
    for z in range(parts_ref.shape[0]):
        part = parts_ref[z]
        for i in range(out_ref.shape[0]):
            out_ref[i, :, z * cols : (z + 1) * cols] = part


def column_gather(parts, copies, after):
    n_z, unit, cols = parts.shape
    vmem = pl.BlockSpec(memory_space=pltpu.VMEM)
    return pl.pallas_call(
        column_kernel,
        in_specs=[vmem] + [pl.BlockSpec(memory_space=pl.ANY)] * len(after),
        out_specs=vmem,
        out_shape=jax.ShapeDtypeStruct((copies, unit, cols * n_z), BF16),
        compiler_params=params(),
        cost_estimate=cost(),
        name="column_gather",
    )(parts, *after)


def matrix_of(right_ref, slot):
    parts = [right_ref[slot, i] for i in range(right_ref.shape[1])]
    return parts[0] if len(parts) == 1 else jnp.concatenate(parts, axis=0)


def product(lt, right):
    return lax.dot_general(lt, right, (((0,), (0,)), ((), ())), preferred_element_type=F32)


def rank_of(owners, k):
    count = jnp.int32(0)
    for j in range(owners.shape[0]):
        count += jnp.where((owners[j] == owners[k]) & (j < k), 1, 0)
    return count


def outputs_kernel(second, places, pos, owners, comp_ref, near_ref, lt_ref, ltr_ref, *refs):
    n_base = len({a for a, _ in places.values()})
    n_state = 2 if second else 0
    bases, refs = refs[:n_base], refs[n_base:]
    if second:
        far_ref, refs = refs[0], refs[1:]
        states, refs = refs[:n_state], refs[n_state + 2 :]
    outs, refs = refs[: 2 + n_state], refs[2 + n_state :]
    held, feedback, weights, fetch_sem, out_sem = refs[:5]
    half, rank = near_ref.shape[0], near_ref.shape[1] * near_ref.shape[2]
    rows, n = feedback.shape[1:]
    capacity = max(c for _, c in places) + 1
    core = 1 - pos[2] if second else pos[2]
    right_ref = far_ref if second else near_ref

    for j in range(half):
        k = core * half + j
        slot = (owners[k] ^ pos[5]) * capacity + rank_of(owners, k)
        for (d, c), (a, row) in places.items():

            @pl.when(slot == d * capacity + c)
            def _():
                pltpu.make_async_copy(bases[a].at[row], held.at[j], fetch_sem.at[j]).start()

    if second:
        scratch, state_in, state_out = refs[5:7], refs[7], refs[8]
        loads = [
            pltpu.make_async_copy(states[i].at[0, c], scratch[i].at[c], state_in.at[i, c])
            for c in range(capacity)
            for i in range(n_state)
        ]
        for load in loads:
            load.start()

    stores = []
    for j in range(half):
        k = core * half + j
        part = pl.ds(pl.multiple_of(k * rank, rank), rank)
        lt, ltr = lt_ref[part, :], ltr_ref[part, :]
        right = matrix_of(right_ref, j)
        pltpu.make_async_copy(bases[0].at[0], held.at[j], fetch_sem.at[j]).wait()
        for first in range(0, n, COLUMNS):
            block = slice(first, first + COLUMNS)
            approx = product(ltr, right[:, block])
            weights[j, :, block] = (held[j, :, block].astype(F32) - 0.1 * approx).astype(BF16)
        copies = [pltpu.make_async_copy(weights.at[j], outs[1].at[k], out_sem.at[j, 2])]
        copies[0].start()
        cut = rows // 2 if rows % 32 == 0 else rows
        for i, top in enumerate(range(0, rows, cut)):
            for first in range(0, n, COLUMNS):
                block = slice(first, first + COLUMNS)
                approx = product(lt[:, top : top + cut], right[:, block])
                wide = comp_ref[k, top : top + cut, block].astype(F32)
                feedback[j, top : top + cut, block] = (wide - approx).astype(BF16)
            source, target = feedback.at[j, pl.ds(top, cut)], outs[0].at[0, k, pl.ds(top, cut)]
            copies.append(pltpu.make_async_copy(source, target, out_sem.at[j, i]))
            copies[-1].start()
        stores += copies

    for c in range(capacity if second else 0):
        matrix = jnp.int32(-1)
        for k in range(owners.shape[0]):
            matrix = jnp.where((owners[k] == pos[5]) & (rank_of(owners, k) == c), k, matrix)
        safe = jnp.maximum(matrix, 0)
        inner = lax.rem(safe, half)
        is_far = safe // half == core
        right = jnp.where(is_far, matrix_of(far_ref, inner), matrix_of(near_ref, inner))
        ltr = ltr_ref[pl.ds(pl.multiple_of(safe * rank, rank), rank), :]
        for load in loads[c * n_state : (c + 1) * n_state]:
            load.wait()
        for first in range(0, n, COLUMNS):
            block = slice(first, first + COLUMNS)
            approx = jnp.where(matrix >= 0, product(ltr, right[:, block]), 0.0)
            momentum = 0.9 * scratch[0][c, :, block] + approx
            scratch[0][c, :, block] = momentum
            scratch[1][c, :, block] -= 0.1 * momentum
        for i in range(n_state):
            copy = pltpu.make_async_copy(scratch[i].at[c], outs[2 + i].at[0, c], state_out.at[i, c])
            copy.start()
            stores.append(copy)

    for copy in stores:
        copy.wait()


def outputs(pos, owners, comp, near, lt, ltr, bases, places, far=None, states=(), earlier=()):
    nmat, rows, n = comp.shape
    half = near.shape[0]
    capacity, replica_rows = bases[0].shape[:2]
    second = far is not None
    any_spec = pl.BlockSpec(memory_space=pl.ANY)
    vmem = pl.BlockSpec(memory_space=pltpu.VMEM)
    scratch = [
        pltpu.VMEM((half, replica_rows, n), BF16),
        pltpu.VMEM((half, rows, n), BF16),
        pltpu.VMEM((half, replica_rows, n), BF16),
        pltpu.SemaphoreType.DMA((half,)),
        pltpu.SemaphoreType.DMA((half, 3)),
    ]
    if second:
        scratch += [pltpu.VMEM((capacity, replica_rows, n), F32)] * 2
        scratch += [pltpu.SemaphoreType.DMA((2, capacity))] * 2
    outs = [
        jax.ShapeDtypeStruct((1, nmat, rows, n), BF16),
        jax.ShapeDtypeStruct((nmat, replica_rows, n), BF16),
    ] + [jax.ShapeDtypeStruct(x.shape, F32) for x in states]
    fars = [far] if second else []
    return pl.pallas_call(
        functools.partial(outputs_kernel, second, places),
        grid_spec=pltpu.PrefetchScalarGridSpec(
            num_scalar_prefetch=2,
            grid=(1,),
            in_specs=[vmem] * 4
            + [any_spec] * len(bases)
            + [vmem] * len(fars)
            + [any_spec] * (len(states) + len(earlier)),
            out_specs=[any_spec] * len(outs),
            scratch_shapes=scratch,
        ),
        out_shape=outs,
        input_output_aliases={
            6 + len(bases) + len(fars) + len(states) + i: i for i in range(len(earlier))
        },
        compiler_params=params(24),
        cost_estimate=cost(),
        name="outputs",
    )(pos, owners, comp, near, lt, ltr, *bases, *fars, *states, *earlier)


def base_kernel(momentum_ref, master_ref, out_ref, momentum, master, sems):
    capacity, rows, _ = out_ref.shape
    blocks = [(c, first) for c in range(capacity) for first in range(0, rows, BASE_ROWS)]

    def copies(i):
        c, first = blocks[i]
        part = pl.ds(first, BASE_ROWS)
        return [
            pltpu.make_async_copy(source.at[0, c, part], target.at[c, part], sems.at[j, i])
            for j, (source, target) in enumerate(((momentum_ref, momentum), (master_ref, master)))
        ]

    for i in range(len(blocks)):
        for copy in copies(i):
            copy.start()
    for i, (c, first) in enumerate(blocks):
        for copy in copies(i):
            copy.wait()
        part = slice(first, first + BASE_ROWS)
        out_ref[c, part] = (master[c, part] - 0.09 * momentum[c, part]).astype(BF16)


def base_of(momentum, master):
    _, capacity, rows, n = momentum.shape
    state = pltpu.VMEM((capacity, rows, n), F32)
    return pl.pallas_call(
        base_kernel,
        in_specs=[pl.BlockSpec(memory_space=pl.ANY)] * 2,
        out_specs=pl.BlockSpec(memory_space=pltpu.VMEM),
        out_shape=jax.ShapeDtypeStruct((capacity, rows, n), BF16),
        scratch_shapes=[state, state, pltpu.SemaphoreType.DMA((2, capacity * rows // BASE_ROWS))],
        compiler_params=params(),
        cost_estimate=cost(),
        name="base",
    )(momentum, master)


def per_device(
    gradients,
    feedback,
    right_init,
    gram_root,
    owners,
    momentum,
    master_weights,
    vector_grads,
    vector_momentum,
    vector_params,
):
    nmat, rows, n = gradients.shape[1:]
    rank = right_init.shape[2]
    n_mp = lax.axis_size("mp")
    n_z = lax.axis_size("replica") // CORES
    capacity, replica_rows = momentum.shape[1:3]
    p = lax.axis_index("mp")
    r = lax.axis_index("replica")
    core, z = r % CORES, r // CORES
    upm = CORES * n_mp // nmat
    half = nmat // CORES
    code = core * n_mp + p
    first = r * replica_rows

    pos = jnp.stack([p, z, core, first % rows // replica_rows, first // rows, p]).astype(jnp.int32)
    in_hbm = lambda x: pltpu.with_memory_space_constraint(x, pltpu.HBM)

    base = base_of(in_hbm(momentum), in_hbm(master_weights))
    bases = [base] + [exchange(base, "mp", d) for d in range(1, 3 if n_mp == 4 else n_mp)]
    places = {(d, c): (d, c) for d in range(len(bases)) for c in range(capacity)}
    early, cuts = bases[1:], []
    if n_mp == 4:
        cut = capacity // 2
        cuts = [0, cut]
        for c in range(capacity):
            places[3, c] = (3, c) if c < cut else (4, c - cut)

    nvec = vector_grads.shape[1]
    comp, near, far = left_terms(
        pos,
        in_hbm(gradients),
        in_hbm(feedback),
        in_hbm(jnp.swapaxes(right_init, 1, 2)),
        vector_grads,
    )
    columns = [[d * CORES + c for d in range(n_z)] for c in range(CORES)]
    along_z = lambda x: lax.all_to_all(x, "replica", 0, 0, axis_index_groups=columns, tiled=True)
    in_plane = lambda x: lax.all_to_all(x, "mp", 0, 0, tiled=True)
    chip = add([near, exchange(far, "replica", 1)], BF16, n_z)
    near = add([along_z(chip)], F32)
    far = exchange(near, "replica", 1)

    unit = rank // upm
    send, keep, lt, vector_rows = right_terms(pos, near, far, gram_root, comp, upm)
    vector_total = vector_rows.reshape(-1)[:nvec]
    chip = chip_sum(pos, keep, exchange(send, "replica", 1), lt, replica_rows, early)
    final, ltr, *forwards = plane_sum(
        pos, in_plane(chip), unit, n_z, nmat * rank, early[: len(cuts)], cuts
    )
    late = [exchange(part, "mp", 2 - i) for i, part in enumerate(forwards)]
    bases += late
    final = add([along_z(final)], BF16, n_z)

    whole = column_gather(along_z(final), n_mp, late)
    near = in_plane(whole).reshape(half, upm, unit, n)
    far = exchange(near, "replica", 1)

    done = outputs(pos, owners, comp, near, lt, ltr, bases, places)
    new_feedback, new_weights, new_momentum, new_master = outputs(
        pos, owners, comp, near, lt, ltr, bases, places, far, (momentum, master_weights), done
    )

    new_vector_momentum = 0.9 * vector_momentum + vector_total
    new_vector_params = vector_params - 0.1 * new_vector_momentum
    return new_feedback, new_momentum, new_master, new_weights, new_vector_momentum, new_vector_params


def solution(mesh):
    return jax.shard_map(
        per_device,
        mesh=mesh,
        in_specs=(
            P("replica", None, "mp", None),
            P("replica", None, "mp", None),
            P(),
            P(),
            P(),
            P("mp", None, "replica", None),
            P("mp", None, "replica", None),
            P("replica", "mp"),
            P("mp"),
            P("mp"),
        ),
        out_specs=(
            P("replica", None, "mp", None),
            P("mp", None, "replica", None),
            P("mp", None, "replica", None),
            P(None, "replica", None),
            P("mp"),
            P("mp"),
        ),
        check_vma=False,
    )
```

time: 98 us -> 126 us (1.29); the launches traced: 97.8 us -> 125 us
  blocking collectives: 0 us -> 31.9 us
  local copies, waits for them, and re-layouts: 0.14 us -> 16.4 us
  waiting for transfers between devices: 29.3 us -> 16.9 us
  starting transfers between devices: 32.8 us -> 24.4 us
  Pallas kernels: 34.1 us -> 32.7 us
    all_to_all x0 -> x3, blocking collectives: none -> 31.9 us  [the longest x2 23.4 us: per_device(): in_plane = lambda x: lax.all_to_all(x, 'mp', 0, 0, tiled=True)]
    ppermute x23 -> x8, starting transfers between devices: 32.8 us -> 14.5 us  [exchange(): return lax.ppermute(x, axis, [(i, i ^ distance) for i in range(size)])]
    ppermute x23 -> x8, waiting for transfers between devices: 29.3 us -> 11.7 us  [exchange(): return lax.ppermute(x, axis, [(i, i ^ distance) for i in range(size)])]
    unnamed x15 -> x35, local copies, waits for them, and re-layouts: 0.05 us -> 16.3 us
    all_to_all x0 -> x2, starting transfers between devices: none -> 9.92 us  [per_device(): lax.all_to_all(x, 'replica', 0, 0, axis_index_groups=columns, tiled=True)]
    all_to_all x0 -> x2, waiting for transfers between devices: none -> 5.21 us  [per_device(): lax.all_to_all(x, 'replica', 0, 0, axis_index_groups=columns, tiled=True)]
    pallas_call x1, Pallas kernels: 10.8 us -> 9.05 us  [left_terms(): pl.pallas_call(left_kernel, grid_spec=pltpu.PrefetchScalarGridSpec(num_sc...]
    pallas_call x9 -> x8, Pallas kernels: 17.5 us -> 17.9 us  [the longest x2 12.5 us: outputs(): pl.pallas_call(functools.partial(outputs_kernel, second, places), grid_sp...]
  transfers between devices with their start and end apart: 23 -> 10, of which waited for: 14 -> 6; matrix products, arithmetic and copies ran while one was open for 1% -> 1% of each run, Pallas kernels for 19% -> 11%
where the time goes in v5:
time: 126 us; the launch traced here: 125 us
  Pallas kernels  32.7 us (26%)
  blocking collectives  31.9 us (25%)
  starting transfers between devices  24.4 us (19%)
  waiting for transfers between devices  16.9 us (13%)
  local copies, waits for them, and re-layouts  16.4 us (13%)
  other arithmetic  1.33 us (1%)
    all_to_all x2, blocking collectives, per_device(): in_plane = lambda x: lax.all_to_all(x, 'mp', 0, 0, tiled=True)  23.4 us
    unnamed x35, local copies, waits for them, and re-layouts  16.3 us
    ppermute x8, starting transfers between devices, exchange(): return lax.ppermute(x, axis, [(i, i ^ distance) for i in range(size)])  14.5 us
    pallas_call x2, Pallas kernels, outputs(): pl.pallas_call(functools.partial(outputs_kernel, second, places), grid_sp...  12.5 us
    ppermute x8, waiting for transfers between devices, exchange(): return lax.ppermute(x, axis, [(i, i ^ distance) for i in range(size)])  11.7 us
    all_to_all x2, starting transfers between devices, per_device(): lax.all_to_all(x, 'replica', 0, 0, axis_index_groups=columns, tiled=True)  9.92 us
    pallas_call x1, Pallas kernels, left_terms(): pl.pallas_call(left_kernel, grid_spec=pltpu.PrefetchScalarGridSpec(num_sc...  9.05 us
    all_to_all x1, blocking collectives, per_device(): lax.all_to_all(x, 'replica', 0, 0, axis_index_groups=columns, tiled=True)  8.43 us
  transfers between devices with their start and end apart: 10, of which 6 were waited for; matrix products, arithmetic and copies ran while one was open for 1% of the time, Pallas kernels for 11%

profile of v5, /device:TPU:1, one launch (start us, length us, event | category | flops | bytes accessed | tf_op | source)
XLA Modules:
  0.0 124.5 jit_solution(4688955118873017057)
XLA Ops:
  1.5 9.0 %left_terms.1 = (bf16[8,192,3072]{2,1,0:T(8,128)(2,1)S(1)}, f32[112,256]{1,0:T(8,128)S(1)}, f32[112,256]{1,0:T(8,128)S(1)}) custom-call(s32[6]{0:T(128)S(1)} %stack.24.pos, bf16[1,8,192,3072]{3,2,1,0:T(8,128)(2,1)} %g_ref.1, bf16[1,8,192,3072]{3,2,1,0:T(8,128)(2,1)} %f_ref.1, bf16[8,32,3072]{2,1,0:T(8,128)(2,1)} %bitcast.13, f32[1,2688]{1,0:T(1,128)S(1)} %copy-done.13), custom_call_target="tpu_custom_call" | custom-call | flops 1000 | bytes 1000 | tf_op jit(solution)/shard_map/left_terms/pallas_call | solution.py:86
  10.6 3.7 %copy-done = bf16[8,192,3072]{2,1,0:T(8,128)(2,1)} copy-done((bf16[8,192,3072]{2,1,0:T(8,128)(2,1)}, bf16[8,192,3072]{2,1,0:T(8,128)(2,1)S(1)}, u32[]{:S(2)}) %copy-start) | copy-done | bytes 9437208
  14.3 1.3 %collective-permute-done.refs_1_ = f32[112,256]{1,0:T(8,128)S(1)} collective-permute-done((f32[112,256]{1,0:T(8,128)S(1)}, f32[112,256]{1,0:T(8,128)S(1)}, u32[]{:S(2)}, u32[]{:S(2)}) %collective-permute-start) | collective-permute-done | bytes 114720 | tf_op jit(solution)/shard_map/ppermute | solution.py:34
  16.3 5.7 %all-to-all-start = ((bf16[4,112,256]{2,1,0:T(8,128)(2,1)}), bf16[4,112,256]{2,1,0:T(8,128)(2,1)}, u32[]{:S(2)}, u32[]{:S(2)}) async-start(bf16[4,112,256]{2,1,0:T(8,128)(2,1)} %add.21), calls=%async_computation | async-start | bytes 458752 | tf_op jit(solution)/shard_map/all_to_all | solution.py:545
  22.1 2.6 %base.1.refs_0_ = bf16[2,96,3072]{2,1,0:T(8,128)(2,1)S(1)} custom-call(f32[1,2,96,3072]{3,2,1,0:T(8,128)} %refs_6_.1, f32[1,2,96,3072]{3,2,1,0:T(8,128)} %refs_7_.1), custom_call_target="tpu_custom_call" | custom-call | flops 1000 | bytes 1000 | tf_op jit(solution)/shard_map/base/pallas_call | solution.py:486
  24.7 1.3 %collective-permute-start.4 = (bf16[2,96,3072]{2,1,0:T(8,128)(2,1)S(1)}, bf16[2,96,3072]{2,1,0:T(8,128)(2,1)S(1)}, u32[]{:S(2)}, u32[]{:S(2)}) collective-permute-start(bf16[2,96,3072]{2,1,0:T(8,128)(2,1)S(1)} %base.1.refs_0_), channel_id=1, source_target_pairs={{0,2},{1,3},{2,0},{3,1},{4,6},{5,7},{6,4},{7,5},{8,10},{9,11},{10,... | collective-permute-start | bytes 3538952 | tf_op jit(solution)/shard_map/ppermute | solution.py:34
  26.0 1.2 collective-permute-start.3
  27.2 1.0 all-to-all-done.refs_0_
  28.2 1.0 add.22.near_ref
  29.1 3.2 %collective-permute-start.1 = (f32[112,256]{1,0:T(8,128)S(1)}, f32[112,256]{1,0:T(8,128)S(1)}, u32[]{:S(2)}, u32[]{:S(2)}) collective-permute-start(f32[112,256]{1,0:T(8,128)S(1)} %add.22.near_ref), channel_id=1, source_target_pairs={{0,4},{4,0},{8,12},{12,8},{16,20},{20,16},{24,28},{28,24},{1,5},{5... | collective-permute-start | bytes 344072 | tf_op jit(solution)/shard_map/ppermute | solution.py:34
  32.4 1.0 collective-permute-done.1.far_ref
  33.3 3.7 %copy-done.1 = bf16[8,192,3072]{2,1,0:T(8,128)(2,1)S(1)} copy-done((bf16[8,192,3072]{2,1,0:T(8,128)(2,1)S(1)}, bf16[8,192,3072]{2,1,0:T(8,128)(2,1)}, u32[]{:S(2)}) %copy-start.1) | copy-done | bytes 9437208
  37.0 0.9 copy-done.10
  37.9 2.4 %right_send.1 = (bf16[4,1,32,3072]{3,2,1,0:T(8,128)(2,1)S(1)}, bf16[256,192]{1,0:T(8,128)(2,1)S(1)}, f32[32,256]{1,0:T(8,128)S(1)}) custom-call(s32[6]{0:T(128)S(1)} %stack.24.pos, f32[112,256]{1,0:T(8,128)S(1)} %add.22.near_ref, f32[112,256]{1,0:T(8,128)S(1)} %collective-permute-done.1.far_ref, f32[8,32,32]{2,1,0:T(8,128)S(1)} %copy-done.10, ...), custom_call_target="tpu_custom_call" | custom-call | flops 1000 | bytes 1000 | tf_op jit(solution)/shard_map/right_send/pallas_call | solution.py:180
  41.3 1.9 %right_keep.1.keep_ref = f32[4,1,32,3072]{3,2,1,0:T(8,128)S(1)} custom-call(s32[6]{0:T(128)S(1)} %stack.24.pos, bf16[256,192]{1,0:T(8,128)(2,1)S(1)} %get-tuple-element.25.lt_ref, bf16[8,192,3072]{2,1,0:T(8,128)(2,1)S(1)} %copy-done.1), custom_call_target="tpu_custom_call" | custom-call | flops 1000 | bytes 18874368 | tf_op jit(solution)/shard_map/right_keep/pallas_call | solution.py:203
  43.2 8.5 %collective-permute-done.4.refs_1_.refs_2_ = bf16[2,96,3072]{2,1,0:T(8,128)(2,1)S(1)} collective-permute-done((bf16[2,96,3072]{2,1,0:T(8,128)(2,1)S(1)}, bf16[2,96,3072]{2,1,0:T(8,128)(2,1)S(1)}, u32[]{:S(2)}, u32[]{:S(2)}) %collective-permute-start.4) | collective-permute-done | bytes 1179680 | tf_op jit(solution)/shard_map/ppermute | solution.py:34
  51.6 0.9 collective-permute-done.3.refs_0_.refs_1_
  52.6 0.8 chip_sum.1
  53.4 13.6 %all_to_all.25.terms_ref = bf16[4,40,3072]{2,1,0:T(8,128)(2,1)S(1)} all-to-all(bf16[4,40,3072]{2,1,0:T(8,128)(2,1)S(1)} %chip_sum.1), channel_id=1, replica_groups=mesh['replica'=8,'mp'=4] {'mp'}, dimensions={0} | all-to-all | bytes 1966080 | tf_op jit(solution)/shard_map/all_to_all | solution.py:546
  69.1 0.8 copy-done.15
  69.9 0.8 copy-done.16
  70.7 4.2 %all-to-all-start.2 = ((bf16[4,32,768]{2,1,0:T(8,128)(2,1)}), bf16[4,32,768]{2,1,0:T(8,128)(2,1)}, u32[]{:S(2)}, u32[]{:S(2)}) async-start(bf16[4,32,768]{2,1,0:T(8,128)(2,1)} %copy-done.9), calls=%async_computation.2 | async-start | bytes 393216 | tf_op jit(solution)/shard_map/all_to_all | solution.py:545
  74.9 0.8 collective-permute-start.5
  75.9 4.3 %all-to-all-done.2.refs_0_ = bf16[4,32,768]{2,1,0:T(8,128)(2,1)} async-done(((bf16[4,32,768]{2,1,0:T(8,128)(2,1)}), bf16[4,32,768]{2,1,0:T(8,128)(2,1)}, u32[]{:S(2)}, u32[]{:S(2)}) %all-to-all-start.2) | async-done | bytes 196640 | tf_op jit(solution)/shard_map/all_to_all | solution.py:545
  80.1 1.0 add.23
  81.1 8.4 %all_to_all.26.parts_ref = bf16[4,32,768]{2,1,0:T(8,128)(2,1)S(1)} all-to-all(bf16[4,32,768]{2,1,0:T(8,128)(2,1)S(1)} %add.23), channel_id=1, replica_groups={{0,8,16,24},{4,12,20,28},{1,9,17,25},{5,13,21,29},{2,10,18,26},{6,14,22..., dimensions={0} | all-to-all | bytes 393216 | tf_op jit(solution)/shard_map/all_to_all | solution.py:545
  89.6 9.8 %all_to_all.27 = bf16[4,32,3072]{2,1,0:T(8,128)(2,1)S(1)} all-to-all(bf16[4,32,3072]{2,1,0:T(8,128)(2,1)S(1)} %column_gather.1), channel_id=1, replica_groups=mesh['replica'=8,'mp'=4] {'mp'}, dimensions={0} | all-to-all | bytes 1572864 | tf_op jit(solution)/shard_map/all_to_all | solution.py:546
  99.4 7.4 %collective-permute-start.7 = (bf16[4,1,32,3072]{3,2,1,0:T(8,128)(2,1)S(1)}, bf16[4,1,32,3072]{3,2,1,0:T(8,128)(2,1)S(1)}, u32[]{:S(2)}, u32[]{:S(2)}) collective-permute-start(bf16[4,1,32,3072]{3,2,1,0:T(8,128)(2,1)S(1)} %bitcast.9), channel_id=1, source_target_pairs={{0,4},{4,0},{8,12},{12,8},{16,20},{20,16},{24,28},{28,24},{1,5},{5... | collective-permute-start | bytes 2359304 | tf_op jit(solution)/shard_map/ppermute | solution.py:34
  106.8 1.3 %multiply_subtract_fusion = (f32[2688]{0:T(1024)}, f32[2688]{0:T(1024)}) fusion(f32[2688]{0:T(1024)} %param.19, f32[8192]{0:T(1024)S(1)} %bitcast.14, f32[2688]{0:T(1024)} %param.18), kind=kLoop, calls=%fused_computation.1 | loop fusion | flops 10752 | bytes 53760 | tf_op jit(solution)/shard_map/sub | solution.py:572
  108.1 3.7 %copy-done.2 = bf16[8,192,3072]{2,1,0:T(8,128)(2,1)S(1)} copy-done((bf16[8,192,3072]{2,1,0:T(8,128)(2,1)S(1)}, bf16[8,192,3072]{2,1,0:T(8,128)(2,1)}, u32[]{:S(2)}) %copy-start.2) | copy-done | bytes 9437208
  111.8 5.0 %outputs.2 = (bf16[1,8,192,3072]{3,2,1,0:T(8,128)(2,1)}, bf16[8,96,3072]{2,1,0:T(8,128)(2,1)}) custom-call(s32[6]{0:T(128)S(1)} %stack.24.pos, s32[8]{0:T(128)S(1)} %copy-done.14, bf16[8,192,3072]{2,1,0:T(8,128)(2,1)S(1)} %copy-done.2, bf16[4,1,32,3072]{3,2,1,0:T(8,128)(2,1)S(1)} %bitcast.10, bf16[256,192]{1,0:T(8,128)(2,1)S(1)} %copy-done.6, ...), custom_call_target="tpu_custom_call" | custom-call | flops 1000 | bytes 1000 | tf_op jit(solution)/shard_map/outputs/pallas_call | solution.py:439
  116.9 7.5 %outputs.3 = (bf16[1,8,192,3072]{3,2,1,0:T(8,128)(2,1)}, bf16[8,96,3072]{2,1,0:T(8,128)(2,1)}, f32[1,2,96,3072]{3,2,1,0:T(8,128)}, f32[1,2,96,3072]{3,2,1,0:T(8,128)}) custom-call(s32[6]{0:T(128)S(1)} %stack.24.pos, s32[8]{0:T(128)S(1)} %copy-done.14, bf16[8,192,3072]{2,1,0:T(8,128)(2,1)S(1)} %copy-done.2, ...), custom_call_target="tpu_custom_call", output_to_operand_aliasing={{0}: (14, {}), {1}: (15, {})} | custom-call | flops 1000 | bytes 1000 | tf_op jit(solution)/shard_map/outputs/pallas_call | solution.py:439
  (40 shorter events, 4.9 us)
Async XLA Ops:
  0.8 0.7 copy-start.13
  10.5 3.7 %copy-start = (bf16[8,192,3072]{2,1,0:T(8,128)(2,1)}, bf16[8,192,3072]{2,1,0:T(8,128)(2,1)S(1)}, u32[]{:S(2)}) copy-start(bf16[8,192,3072]{2,1,0:T(8,128)(2,1)S(1)} %get-tuple-element.22.comp_ref) | copy-start | bytes 28311556
  14.3 1.3 %collective-permute-start = (f32[112,256]{1,0:T(8,128)S(1)}, f32[112,256]{1,0:T(8,128)S(1)}, u32[]{:S(2)}, u32[]{:S(2)}) collective-permute-start(f32[112,256]{1,0:T(8,128)S(1)} %get-tuple-element.24), channel_id=1, source_target_pairs={{0,4},{4,0},{8,12},{12,8},{16,20},{20,16},{24,28},{28,24},{1,5},{5... | collective-permute-start | bytes 344072 | tf_op jit(solution)/shard_map/ppermute | solution.py:34
  16.3 11.9 %all-to-all-start = ((bf16[4,112,256]{2,1,0:T(8,128)(2,1)}), bf16[4,112,256]{2,1,0:T(8,128)(2,1)}, u32[]{:S(2)}, u32[]{:S(2)}) async-start(bf16[4,112,256]{2,1,0:T(8,128)(2,1)} %add.21), calls=%async_computation | async-start | bytes 458752 | tf_op jit(solution)/shard_map/all_to_all | solution.py:545
  24.7 26.9 %collective-permute-start.4 = (bf16[2,96,3072]{2,1,0:T(8,128)(2,1)S(1)}, bf16[2,96,3072]{2,1,0:T(8,128)(2,1)S(1)}, u32[]{:S(2)}, u32[]{:S(2)}) collective-permute-start(bf16[2,96,3072]{2,1,0:T(8,128)(2,1)S(1)} %base.1.refs_0_), channel_id=1, source_target_pairs={{0,2},{1,3},{2,0},{3,1},{4,6},{5,7},{6,4},{7,5},{8,10},{9,11},{10,... | collective-permute-start | bytes 3538952 | tf_op jit(solution)/shard_map/ppermute | solution.py:34
  26.0 26.6 %collective-permute-start.3 = (bf16[2,96,3072]{2,1,0:T(8,128)(2,1)S(1)}, bf16[2,96,3072]{2,1,0:T(8,128)(2,1)S(1)}, u32[]{:S(2)}, u32[]{:S(2)}) collective-permute-start(bf16[2,96,3072]{2,1,0:T(8,128)(2,1)S(1)} %base.1.refs_0_), channel_id=1, source_target_pairs={{0,1},{1,0},{2,3},{3,2},{4,5},{5,4},{6,7},{7,6},{8,9},{9,8},{10,11... | collective-permute-start | bytes 3538952 | tf_op jit(solution)/shard_map/ppermute | solution.py:34
  29.1 4.2 %collective-permute-start.1 = (f32[112,256]{1,0:T(8,128)S(1)}, f32[112,256]{1,0:T(8,128)S(1)}, u32[]{:S(2)}, u32[]{:S(2)}) collective-permute-start(f32[112,256]{1,0:T(8,128)S(1)} %add.22.near_ref), channel_id=1, source_target_pairs={{0,4},{4,0},{8,12},{12,8},{16,20},{20,16},{24,28},{28,24},{1,5},{5... | collective-permute-start | bytes 344072 | tf_op jit(solution)/shard_map/ppermute | solution.py:34
  33.3 3.7 %copy-start.1 = (bf16[8,192,3072]{2,1,0:T(8,128)(2,1)S(1)}, bf16[8,192,3072]{2,1,0:T(8,128)(2,1)}, u32[]{:S(2)}) copy-start(bf16[8,192,3072]{2,1,0:T(8,128)(2,1)} %copy-done) | copy-start | bytes 28311556
  37.0 0.9 copy-start.10
  40.3 0.6 copy-start.11
  40.9 11.7 %copy-start.5 = (bf16[256,192]{1,0:T(8,128)(2,1)}, bf16[256,192]{1,0:T(8,128)(2,1)S(1)}, u32[]{:S(2)}) copy-start(bf16[256,192]{1,0:T(8,128)(2,1)S(1)} %get-tuple-element.25.lt_ref) | copy-start | bytes 294916
  40.9 11.6 %collective-permute-start.2 = (bf16[4,1,32,3072]{3,2,1,0:T(8,128)(2,1)S(1)}, bf16[4,1,32,3072]{3,2,1,0:T(8,128)(2,1)S(1)}, u32[]{:S(2)}, u32[]{:S(2)}) collective-permute-start(bf16[4,1,32,3072]{3,2,1,0:T(8,128)(2,1)S(1)} %get-tuple-element.26), channel_id=1, source_target_pairs={{0,4},{4,0},{8,12},{12,8},{16,20},{20,16},{24,28},{28,24},{1,5},{5... | collective-permute-start | bytes 2359304 | tf_op jit(solution)/shard_map/ppermute | solution.py:34
  67.8 0.6 copy-start.7
  68.4 0.7 copy-start.9
  69.1 0.8 copy-start.15
  69.9 0.8 copy-start.16
  70.7 9.4 %all-to-all-start.2 = ((bf16[4,32,768]{2,1,0:T(8,128)(2,1)}), bf16[4,32,768]{2,1,0:T(8,128)(2,1)}, u32[]{:S(2)}, u32[]{:S(2)}) async-start(bf16[4,32,768]{2,1,0:T(8,128)(2,1)} %copy-done.9), calls=%async_computation.2 | async-start | bytes 393216 | tf_op jit(solution)/shard_map/all_to_all | solution.py:545
  74.9 33.2 %copy-start.14 = (s32[8]{0:T(128)S(1)}, s32[8]{0:T(128)}, u32[]{:S(2)}) copy-start(s32[8]{0:T(128)} %owners.3) | copy-start | bytes 100
  74.9 14.6 %collective-permute-start.5 = (bf16[1,96,3072]{2,1,0:T(8,128)(2,1)}, bf16[1,96,3072]{2,1,0:T(8,128)(2,1)}, u32[]{:S(2)}, u32[]{:S(2)}) collective-permute-start(bf16[1,96,3072]{2,1,0:T(8,128)(2,1)} %copy-done.16), channel_id=1, source_target_pairs={{0,2},{1,3},{2,0},{3,1},{4,6},{5,7},{6,4},{7,5},{8,10},{9,11},{10,... | collective-permute-start | bytes 1769480 | tf_op jit(solution)/shard_map/ppermute | solution.py:34
  75.7 13.9 %collective-permute-start.6 = (bf16[1,96,3072]{2,1,0:T(8,128)(2,1)}, bf16[1,96,3072]{2,1,0:T(8,128)(2,1)}, u32[]{:S(2)}, u32[]{:S(2)}) collective-permute-start(bf16[1,96,3072]{2,1,0:T(8,128)(2,1)} %copy-done.15), channel_id=1, source_target_pairs={{0,1},{1,0},{2,3},{3,2},{4,5},{5,4},{6,7},{7,6},{8,9},{9,8},{10,11... | collective-permute-start | bytes 1769480 | tf_op jit(solution)/shard_map/ppermute | solution.py:34
  80.1 26.6 %copy-start.12 = (f32[32,256]{1,0:T(8,128)S(1)}, f32[32,256]{1,0:T(8,128)}, u32[]{:S(2)}) copy-start(f32[32,256]{1,0:T(8,128)} %copy-done.11) | copy-start | bytes 98308
  80.1 28.0 %copy-start.6 = (bf16[256,192]{1,0:T(8,128)(2,1)S(1)}, bf16[256,192]{1,0:T(8,128)(2,1)}, u32[]{:S(2)}) copy-start(bf16[256,192]{1,0:T(8,128)(2,1)} %copy-done.5) | copy-start | bytes 294916
  80.1 28.0 %copy-start.8 = (bf16[256,96]{1,0:T(8,128)(2,1)S(1)}, bf16[256,96]{1,0:T(8,128)(2,1)}, u32[]{:S(2)}) copy-start(bf16[256,96]{1,0:T(8,128)(2,1)} %copy-done.7) | copy-start | bytes 147460
  99.4 17.4 %collective-permute-start.7 = (bf16[4,1,32,3072]{3,2,1,0:T(8,128)(2,1)S(1)}, bf16[4,1,32,3072]{3,2,1,0:T(8,128)(2,1)S(1)}, u32[]{:S(2)}, u32[]{:S(2)}) collective-permute-start(bf16[4,1,32,3072]{3,2,1,0:T(8,128)(2,1)S(1)} %bitcast.9), channel_id=1, source_target_pairs={{0,4},{4,0},{8,12},{12,8},{16,20},{20,16},{24,28},{28,24},{1,5},{5... | collective-permute-start | bytes 2359304 | tf_op jit(solution)/shard_map/ppermute | solution.py:34
  108.1 3.7 %copy-start.2 = (bf16[8,192,3072]{2,1,0:T(8,128)(2,1)S(1)}, bf16[8,192,3072]{2,1,0:T(8,128)(2,1)}, u32[]{:S(2)}) copy-start(bf16[8,192,3072]{2,1,0:T(8,128)(2,1)} %copy-done) | copy-start | bytes 28311556
  111.8 5.0 %copy-start.3 = (f32[1,2,96,3072]{3,2,1,0:T(8,128)S(1)}, f32[1,2,96,3072]{3,2,1,0:T(8,128)}, u32[]{:S(2)}) copy-start(f32[1,2,96,3072]{3,2,1,0:T(8,128)} %refs_6_.1) | copy-start | bytes 7077892
  111.8 5.0 %copy-start.4 = (f32[1,2,96,3072]{3,2,1,0:T(8,128)S(1)}, f32[1,2,96,3072]{3,2,1,0:T(8,128)}, u32[]{:S(2)}) copy-start(f32[1,2,96,3072]{3,2,1,0:T(8,128)} %refs_7_.1) | copy-start | bytes 7077892

commit v6 on v5

v6 whole, which is shorter than its diff:
```python
import functools

import jax
import jax.numpy as jnp
from jax import lax
from jax.experimental import pallas as pl
from jax.experimental.pallas import tpu as pltpu
from jax.sharding import PartitionSpec as P

CORES = 2
AHEAD = 4
BASE_ROWS = 16
COLUMNS = 256
F32 = jnp.float32
BF16 = jnp.bfloat16


def params(mib=12):
    return pltpu.CompilerParams(vmem_limit_bytes=mib * 1024 * 1024)


def cost(flops=1000, bytes_accessed=1000):
    return pl.CostEstimate(flops=flops, bytes_accessed=bytes_accessed, transcendentals=0)


def tree_sum(terms):
    while len(terms) > 1:
        terms = [terms[i] + terms[i + 1] for i in range(0, len(terms), 2)]
    return terms[0]


def exchange(x, axis, distance):
    size = lax.axis_size(axis)
    return lax.ppermute(x, axis, [(i, i ^ distance) for i in range(size)])


def left_kernel(pos, g_ref, f_ref, q_ref, vec_ref, comp_ref, near_ref, far_ref, total, feedback, right, sems):
    nmat, rows, _ = comp_ref.shape
    rank = q_ref.shape[1]
    part = near_ref.shape[0]
    cut = rows // 2 if rows % 32 == 0 else rows

    def copies(k):
        out = [pltpu.make_async_copy(q_ref.at[k], right.at[k], sems.at[k, 4])]
        for i, first in enumerate(range(0, rows, cut)):
            block = pl.ds(first, cut)
            for j, (source, target) in enumerate(((g_ref, comp_ref), (f_ref, feedback))):
                source, target = source.at[0, k, block], target.at[k, block]
                out.append(pltpu.make_async_copy(source, target, sems.at[k, 2 * i + j]))
        return out

    for k in range(min(AHEAD, nmat)):
        for copy in copies(k):
            copy.start()
    total[...] = jnp.zeros(total.shape, F32)
    width, nvec = total.shape[1], vec_ref.shape[1]
    for i, first in enumerate(range(0, nvec, width)):
        count = min(width, nvec - first)
        total[rows + i : rows + i + 1, :count] = vec_ref[:, first : first + count]

    for k in range(nmat):
        for copy in copies(k):
            copy.wait()
        if k + AHEAD < nmat:
            for copy in copies(k + AHEAD):
                copy.start()
        comp = comp_ref[k] + feedback[k]
        comp_ref[k] = comp
        total[:rows, k * rank : (k + 1) * rank] = lax.dot_general(
            comp, right[k], (((1,), (1,)), ((), ())), preferred_element_type=F32
        )

    for ref, core in ((near_ref, pos[2]), (far_ref, 1 - pos[2])):
        ref[...] = total[pl.ds(pl.multiple_of(core * part, 16), part), :]


def left_terms(pos, gradients, feedback, right_t, vec):
    _, nmat, rows, n = gradients.shape
    rank = right_t.shape[1]
    width = nmat * rank
    total = rows + -(-vec.shape[1] // width)
    total += -total % (16 * CORES)
    part = jax.ShapeDtypeStruct((total // CORES, width), F32)
    vmem = pl.BlockSpec(memory_space=pltpu.VMEM)
    any_spec = pl.BlockSpec(memory_space=pl.ANY)
    return pl.pallas_call(
        left_kernel,
        grid_spec=pltpu.PrefetchScalarGridSpec(
            num_scalar_prefetch=1,
            grid=(1,),
            in_specs=[any_spec] * 3 + [vmem],
            out_specs=[vmem] * 3,
            scratch_shapes=[
                pltpu.VMEM((total, width), F32),
                pltpu.VMEM((nmat, rows, n), BF16),
                pltpu.VMEM((nmat, rank, n), BF16),
                pltpu.SemaphoreType.DMA((nmat, 5)),
            ],
        ),
        out_shape=[jax.ShapeDtypeStruct((nmat, rows, n), BF16), part, part],
        compiler_params=params(20),
        cost_estimate=cost(),
        name="left_terms",
    )(pos, gradients, feedback, right_t, vec)


def add_kernel(*refs):
    out = refs[-1]
    out[...] = tree_sum([ref[...].astype(F32) for ref in refs[:-1]]).astype(out.dtype)


def add(parts, dtype):
    vmem = pl.BlockSpec(memory_space=pltpu.VMEM)
    return pl.pallas_call(
        add_kernel,
        in_specs=[vmem] * len(parts),
        out_specs=vmem,
        out_shape=jax.ShapeDtypeStruct(parts[0].shape, dtype),
        compiler_params=params(),
        cost_estimate=cost(),
        name="add",
    )(*parts)


def send_kernel(half, pos, near_ref, far_ref, gram_ref, comp_ref, *refs):
    send_ref, lt_ref, left_ref, vec_ref, left, gram = refs
    t = pl.program_id(0)
    rows = comp_ref.shape[1]
    rank = gram_ref.shape[1]

    @pl.when(t == 0)
    def _():
        part = near_ref.shape[0]
        for ref, core in ((near_ref, pos[2]), (far_ref, 1 - pos[2])):
            left[pl.ds(pl.multiple_of(core * part, 16), part), :] = ref[...]
        vec_ref[...] = left[rows:, :]
        gram[...] = jnp.zeros(gram.shape, F32)
        for i in range(gram_ref.shape[0]):
            gram[i * rank : (i + 1) * rank, i * rank : (i + 1) * rank] = gram_ref[i]
        hat = jnp.dot(
            left[:rows, :], gram[...], precision=lax.Precision.HIGHEST, preferred_element_type=F32
        )
        lt_ref[...] = hat.T.astype(BF16)
        for i in range(gram_ref.shape[0]):
            left_ref[i] = hat[:, i * rank : (i + 1) * rank].astype(BF16)

    right_rows(half, pos, lt_ref, comp_ref, send_ref)


def right_rows(start, pos, lt_ref, comp_ref, out_ref):
    upm, unit = out_ref.shape[1], out_ref.shape[2]
    k = (pl.program_id(0) + start) ^ pos[0]
    rows = pl.ds(pl.multiple_of(k * upm * unit, upm * unit), upm * unit)
    terms = jnp.dot(lt_ref[rows, :], comp_ref[k], preferred_element_type=F32)
    for i in range(upm):
        out_ref[0, i ^ pos[1]] = terms[i * unit : (i + 1) * unit].astype(out_ref.dtype)


def keep_kernel(pos, lt_ref, comp_ref, *refs):
    right_rows(0, pos, lt_ref, comp_ref, refs[-1])


def right_terms(pos, near, far, gram, comp, upm, after):
    nmat, rows, n = comp.shape
    rank = gram.shape[1]
    width = nmat * rank
    half = nmat // CORES
    total = CORES * near.shape[0]
    shape = (half, upm, rank // upm, n)
    vmem = pl.BlockSpec(memory_space=pltpu.VMEM)
    out = pl.BlockSpec((1,) + shape[1:], lambda t, pos: (t, 0, 0, 0))
    send, lt, left, vec = pl.pallas_call(
        functools.partial(send_kernel, half),
        grid_spec=pltpu.PrefetchScalarGridSpec(
            num_scalar_prefetch=1,
            grid=(half,),
            in_specs=[
                vmem,
                vmem,
                vmem,
                vmem,
            ],
            out_specs=[out, vmem, vmem, vmem],
            scratch_shapes=[pltpu.VMEM((total, width), F32), pltpu.VMEM((width, width), F32)],
        ),
        out_shape=[
            jax.ShapeDtypeStruct(shape, BF16),
            jax.ShapeDtypeStruct((width, rows), BF16),
            jax.ShapeDtypeStruct((nmat, rows, rank), BF16),
            jax.ShapeDtypeStruct((total - rows, width), F32),
        ],
        compiler_params=params(),
        cost_estimate=cost(),
        name="right_send",
    )(pos, near, far, gram, comp)
    keep = pl.pallas_call(
        keep_kernel,
        grid_spec=pltpu.PrefetchScalarGridSpec(
            num_scalar_prefetch=1,
            grid=(half,),
            in_specs=[vmem, vmem] + [pl.BlockSpec(memory_space=pl.ANY)] * len(after),
            out_specs=out,
        ),
        out_shape=jax.ShapeDtypeStruct(shape, F32),
        compiler_params=params(),
        cost_estimate=cost(2000 * nmat * rows * n),
        name="right_keep",
    )(pos, lt, comp, *after)
    return send, keep, lt, left, vec


def chip_kernel(replica_rows, pos, keep_ref, recv_ref, lt_ref, own_ref, strip_ref, *sends):
    upm = keep_ref.shape[1]
    n = own_ref.shape[1]
    left = lt_ref[...].astype(F32).T
    strip = left[:replica_rows]
    for i in range(1, left.shape[0] // replica_rows):
        strip = jnp.where(pos[6] == i, left[i * replica_rows : (i + 1) * replica_rows], strip)
    height = strip_ref.shape[0]
    strip = jnp.concatenate(
        [strip[i * height : (i + 1) * height] for i in range(replica_rows // height)], axis=1
    )
    strip_ref[...] = strip
    own_ref[...] = keep_ref[0, 0] + recv_ref[0, 0].astype(F32)
    for d, out in enumerate(sends, 1):
        j, i = d // upm, d % upm
        terms = keep_ref[j, i] + recv_ref[j, i].astype(F32)
        out[...] = jnp.concatenate([terms, strip], axis=0).astype(BF16)


def chip_sum(pos, keep, recv, lt, replica_rows):
    half, upm, unit, n = keep.shape
    height = lt.shape[0] * replica_rows // n
    vmem = pl.BlockSpec(memory_space=pltpu.VMEM)
    outs = [jax.ShapeDtypeStruct((unit, n), F32), jax.ShapeDtypeStruct((height, n), F32)]
    outs += [jax.ShapeDtypeStruct((unit + height, n), BF16)] * (half * upm - 1)
    return pl.pallas_call(
        functools.partial(chip_kernel, replica_rows),
        grid_spec=pltpu.PrefetchScalarGridSpec(
            num_scalar_prefetch=1,
            grid=(1,),
            in_specs=[vmem] * 3,
            out_specs=[vmem] * len(outs),
        ),
        out_shape=outs,
        compiler_params=params(),
        cost_estimate=cost(),
        name="chip_sum",
    )(pos, keep, recv, lt)


def column_kernel(n_z, pos, *refs):
    out = refs[-1]
    cols = out.shape[1] // n_z
    for d in range(n_z):
        out[:, pl.ds(pl.multiple_of((pos[4] ^ d) * cols, cols), cols)] = refs[d][...]


def column_gather(pos, parts, after):
    unit, cols = parts[0].shape
    vmem = pl.BlockSpec(memory_space=pltpu.VMEM)
    return pl.pallas_call(
        functools.partial(column_kernel, len(parts)),
        grid_spec=pltpu.PrefetchScalarGridSpec(
            num_scalar_prefetch=1,
            grid=(1,),
            in_specs=[vmem] * len(parts) + [pl.BlockSpec(memory_space=pl.ANY)] * len(after),
            out_specs=vmem,
        ),
        out_shape=jax.ShapeDtypeStruct((unit, cols * len(parts)), BF16),
        compiler_params=params(),
        cost_estimate=cost(),
        name="column_gather",
    )(pos, *parts, *after)


def plane_kernel(pos, own_ref, strip_ref, *refs):
    n_z = own_ref.shape[1] // refs[-2].shape[1]
    terms, outs, ltr_ref = refs[: -n_z - 1], refs[-n_z - 1 : -1], refs[-1]
    unit, n = own_ref.shape
    cols = n // n_z
    for d, out in enumerate(outs):
        block = pl.ds(pl.multiple_of((pos[4] ^ d) * cols, cols), cols)
        parts = [own_ref[:, block]] + [term[:, block].astype(F32)[:unit] for term in terms]
        out[...] = tree_sum(parts).astype(out.dtype)
    strip = strip_ref[...]
    for d, term in enumerate(terms, 1):
        strip = jnp.where(pos[7] == d, term[...].astype(F32)[unit:], strip)
    nmat, _, rank = ltr_ref.shape
    width = nmat * rank
    rows = [strip[:, i * width : (i + 1) * width] for i in range(n // width)]
    rows = jnp.concatenate(rows, axis=0)
    for i in range(nmat):
        ltr_ref[i] = rows[:, i * rank : (i + 1) * rank].astype(BF16)


def plane_sum(pos, own, strip, terms, n_z, nmat, rank):
    unit, n = own.shape
    outs = [jax.ShapeDtypeStruct((unit, n // n_z), BF16 if d else F32) for d in range(n_z)]
    outs.append(jax.ShapeDtypeStruct((nmat, strip.size // (nmat * rank), rank), BF16))
    vmem = pl.BlockSpec(memory_space=pltpu.VMEM)
    return pl.pallas_call(
        plane_kernel,
        grid_spec=pltpu.PrefetchScalarGridSpec(
            num_scalar_prefetch=1,
            grid=(1,),
            in_specs=[vmem] * (2 + len(terms)),
            out_specs=[vmem] * len(outs),
        ),
        out_shape=outs,
        compiler_params=params(),
        cost_estimate=cost(),
        name="plane_sum",
    )(pos, own, strip, *terms)


def forward_kernel(cuts, *refs):
    for whole, out, first in zip(refs, refs[-len(cuts) :], cuts):
        out[...] = whole[first : first + out.shape[0]]


def forward(wholes, cuts, count, after):
    vmem = pl.BlockSpec(memory_space=pltpu.VMEM)
    shapes = [(count,) + x.shape[1:] for x in wholes]
    return pl.pallas_call(
        functools.partial(forward_kernel, cuts),
        in_specs=[vmem] * len(wholes) + [pl.BlockSpec(memory_space=pl.ANY)],
        out_specs=[vmem] * len(wholes),
        out_shape=[jax.ShapeDtypeStruct(shape, BF16) for shape in shapes],
        compiler_params=params(),
        cost_estimate=cost(20000 * wholes[0].size),
        name="forward",
    )(*wholes, after)


def rank_of(owners, k):
    count = jnp.int32(0)
    for j in range(owners.shape[0]):
        count += jnp.where((owners[j] == owners[k]) & (j < k), 1, 0)
    return count


def outputs_kernel(jobs, upm, places, n_state, pos, owners, comp_ref, left_ref, ltr_ref, *refs):
    n_base = len({a for a, _ in places.values()})
    half = comp_ref.shape[0] // CORES
    n_right = CORES * half * upm if n_state else len(jobs) * upm
    bases, rights, states = refs[:n_base], refs[n_base:][:n_right], refs[n_base + n_right :][:n_state]
    refs = refs[len(refs) - (3 + n_state) - 6 - (4 if n_state else 0) :]
    outs, token, refs = refs[: 2 + n_state], refs[2 + n_state], refs[3 + n_state :]
    token[...] = jnp.zeros(token.shape, F32)
    held, feedback, weights, gathered, fetch_sem, out_sem = refs[:6]
    rows, n = feedback.shape[1:]
    capacity = max(c for _, c in places) + 1

    def matrix(other, j):
        core = 1 - pos[2] if other else pos[2]
        return core * half + (lax.rem(pos[0], half) ^ j)

    def right_of(i):
        if upm == 1:
            return rights[i][...]
        for u in range(upm):
            gathered[u ^ pos[1]] = rights[i * upm + u][...]
        return jnp.concatenate([gathered[u] for u in range(upm)], axis=0)

    for i, job in enumerate(jobs):
        k = matrix(*job)
        slot = (owners[k] ^ pos[5]) * capacity + rank_of(owners, k)
        for (d, c), (a, row) in places.items():

            @pl.when(slot == d * capacity + c)
            def _():
                pltpu.make_async_copy(bases[a].at[row], held.at[i], fetch_sem.at[i]).start()

    if n_state:
        scratch, state_in, state_out = refs[6:8], refs[8], refs[9]
        loads = [
            pltpu.make_async_copy(states[i].at[0, c], scratch[i].at[c], state_in.at[i, c])
            for c in range(capacity)
            for i in range(n_state)
        ]
        for load in loads:
            load.start()

    stores = []
    for i, (other, j) in enumerate(jobs):
        k = matrix(other, j)
        right = right_of(other * half + j if n_state else i)
        left, ltr = left_ref[k], ltr_ref[k]
        pltpu.make_async_copy(bases[0].at[0], held.at[i], fetch_sem.at[i]).wait()
        for first in range(0, n, COLUMNS):
            block = slice(first, first + COLUMNS)
            approx = jnp.dot(ltr, right[:, block], preferred_element_type=F32)
            weights[i, :, block] = (held[i, :, block].astype(F32) - 0.1 * approx).astype(BF16)
        stores.append(pltpu.make_async_copy(weights.at[i], outs[1].at[k], out_sem.at[i, 1]))
        stores[-1].start()
        for first in range(0, n, COLUMNS):
            block = slice(first, first + COLUMNS)
            approx = jnp.dot(left, right[:, block], preferred_element_type=F32)
            feedback[i, :, block] = (comp_ref[k, :, block].astype(F32) - approx).astype(BF16)
        stores.append(pltpu.make_async_copy(feedback.at[i], outs[0].at[0, k], out_sem.at[i, 0]))
        stores[-1].start()

    for c in range(capacity if n_state else 0):
        mine = jnp.int32(-1)
        for k in range(owners.shape[0]):
            mine = jnp.where((owners[k] == pos[5]) & (rank_of(owners, k) == c), k, mine)
        for other in range(CORES):
            for j in range(half):

                @pl.when(jnp.maximum(mine, 0) == matrix(other, j))
                def _():
                    for u in range(upm):
                        unit = rights[(other * half + j) * upm + u][...]
                        gathered[u ^ pos[1] if upm > 1 else 0] = unit

        right = jnp.concatenate([gathered[u] for u in range(upm)], axis=0)
        ltr = ltr_ref[jnp.maximum(mine, 0)]
        for load in loads[c * n_state : (c + 1) * n_state]:
            load.wait()
        for first in range(0, n, COLUMNS):
            block = slice(first, first + COLUMNS)
            approx = jnp.dot(ltr, right[:, block], preferred_element_type=F32)
            momentum = 0.9 * scratch[0][c, :, block] + jnp.where(mine >= 0, approx, 0.0)
            scratch[0][c, :, block] = momentum
            scratch[1][c, :, block] -= 0.1 * momentum
        for i in range(n_state):
            copy = pltpu.make_async_copy(scratch[i].at[c], outs[2 + i].at[0, c], state_out.at[i, c])
            copy.start()
            stores.append(copy)

    for copy in stores:
        copy.wait()


def outputs(pos, owners, comp, left, ltr, bases, places, jobs, rights, upm, states=(), earlier=()):
    nmat, rows, n = comp.shape
    capacity, replica_rows = bases[0].shape[:2]
    any_spec = pl.BlockSpec(memory_space=pl.ANY)
    vmem = pl.BlockSpec(memory_space=pltpu.VMEM)
    count = len(jobs)
    scratch = [
        pltpu.VMEM((count, replica_rows, n), BF16),
        pltpu.VMEM((count, rows, n), BF16),
        pltpu.VMEM((count, replica_rows, n), BF16),
        pltpu.VMEM((upm,) + rights[0].shape, BF16),
        pltpu.SemaphoreType.DMA((count,)),
        pltpu.SemaphoreType.DMA((count, 2)),
    ]
    if states:
        scratch += [pltpu.VMEM((capacity, replica_rows, n), F32)] * 2
        scratch += [pltpu.SemaphoreType.DMA((2, capacity))] * 2
    outs = [
        jax.ShapeDtypeStruct((1, nmat, rows, n), BF16),
        jax.ShapeDtypeStruct((nmat, replica_rows, n), BF16),
    ] + [jax.ShapeDtypeStruct(x.shape, F32) for x in states]
    token = jax.ShapeDtypeStruct((8, 128), F32)
    first = 5 + len(bases) + len(rights) + len(states)
    return pl.pallas_call(
        functools.partial(outputs_kernel, jobs, upm, places, len(states)),
        grid_spec=pltpu.PrefetchScalarGridSpec(
            num_scalar_prefetch=2,
            grid=(1,),
            in_specs=[vmem] * 3
            + [any_spec] * len(bases)
            + [vmem] * len(rights)
            + [any_spec] * (len(states) + len(earlier)),
            out_specs=[any_spec] * len(outs) + [vmem],
            scratch_shapes=scratch,
        ),
        out_shape=outs + [token],
        input_output_aliases={first + i: i for i in range(len(earlier))},
        compiler_params=params(20),
        cost_estimate=cost(20000 * len(jobs) * rows * n),
        name="outputs",
    )(pos, owners, comp, left, ltr, *bases, *rights, *states, *earlier)


def base_kernel(momentum_ref, master_ref, out_ref, momentum, master, sems):
    capacity, rows, _ = out_ref.shape
    blocks = [(c, first) for c in range(capacity) for first in range(0, rows, BASE_ROWS)]

    def copies(i):
        c, first = blocks[i]
        part = pl.ds(first, BASE_ROWS)
        return [
            pltpu.make_async_copy(source.at[0, c, part], target.at[c, part], sems.at[j, i])
            for j, (source, target) in enumerate(((momentum_ref, momentum), (master_ref, master)))
        ]

    for i in range(len(blocks)):
        for copy in copies(i):
            copy.start()
    for i, (c, first) in enumerate(blocks):
        for copy in copies(i):
            copy.wait()
        part = slice(first, first + BASE_ROWS)
        out_ref[c, part] = (master[c, part] - 0.09 * momentum[c, part]).astype(BF16)


def base_of(momentum, master):
    _, capacity, rows, n = momentum.shape
    state = pltpu.VMEM((capacity, rows, n), F32)
    return pl.pallas_call(
        base_kernel,
        in_specs=[pl.BlockSpec(memory_space=pl.ANY)] * 2,
        out_specs=pl.BlockSpec(memory_space=pltpu.VMEM),
        out_shape=jax.ShapeDtypeStruct((capacity, rows, n), BF16),
        scratch_shapes=[state, state, pltpu.SemaphoreType.DMA((2, capacity * rows // BASE_ROWS))],
        compiler_params=params(),
        cost_estimate=cost(),
        name="base",
    )(momentum, master)


def per_device(
    gradients,
    feedback,
    right_init,
    gram_root,
    owners,
    momentum,
    master_weights,
    vector_grads,
    vector_momentum,
    vector_params,
):
    nmat, rows, n = gradients.shape[1:]
    rank = right_init.shape[2]
    unit = rank * nmat // (CORES * lax.axis_size("mp"))
    n_mp = lax.axis_size("mp")
    n_z = lax.axis_size("replica") // CORES
    capacity, replica_rows = momentum.shape[1:3]
    p = lax.axis_index("mp")
    r = lax.axis_index("replica")
    core, z = r % CORES, r // CORES
    upm = CORES * n_mp // nmat
    half = nmat // CORES
    code = core * n_mp + p
    first = r * replica_rows

    places_of = [code // upm, code % upm, core, r, z, p, first % rows // replica_rows, first // rows ^ p]
    pos = jnp.stack(places_of).astype(jnp.int32)
    in_hbm = lambda x: pltpu.with_memory_space_constraint(x, pltpu.HBM)

    base = base_of(in_hbm(momentum), in_hbm(master_weights))
    bases = [base] + [exchange(base, "mp", d) for d in range(1, 3 if n_mp == 4 else n_mp)]
    places = {(d, c): (d, c) for d in range(len(bases)) for c in range(capacity)}
    early, cuts = bases[1:], []
    if n_mp == 4:
        cut = capacity // 2
        cuts = [0, cut]
        for c in range(capacity):
            places[3, c] = (3, c) if c < cut else (4, c - cut)

    nvec = vector_grads.shape[1]
    comp, near, far = left_terms(
        pos,
        in_hbm(gradients),
        in_hbm(feedback),
        in_hbm(jnp.swapaxes(right_init, 1, 2)),
        vector_grads,
    )
    chip = add([near, exchange(far, "replica", 1)], BF16)
    near = add([chip] + [exchange(chip, "replica", CORES * d) for d in range(1, n_z)], F32)
    far = exchange(near, "replica", 1)

    send, keep, lt, left, vector_rows = right_terms(pos, near, far, gram_root, comp, upm, early)
    vector_total = vector_rows.reshape(-1)[:nvec]
    own, strip, *chip = chip_sum(pos, keep, exchange(send, "replica", 1), lt, replica_rows)
    plane = [exchange(part, "mp", d) for d, part in enumerate(chip, 1)]
    *final, ltr = plane_sum(pos, own, strip, plane, n_z, nmat, rank)
    arrived = [exchange(final[d], "replica", CORES * d) for d in range(1, n_z)]
    if cuts:
        forwards = forward(early, cuts, capacity // 2, ltr)
        bases += [exchange(part, "mp", 2 - i) for i, part in enumerate(forwards)]
    final = tree_sum([final[0]] + [part.astype(F32) for part in arrived]).astype(BF16)

    final = [final] + [exchange(final, "replica", CORES * d) for d in range(1, n_z)]
    whole = column_gather(pos, final, ())
    near = [whole] + [exchange(whole, "mp", d) for d in range(1, n_mp)]
    far, groups, done = [], [], ()
    for j in range(half):
        group = near[j * upm : (j + 1) * upm]
        sent = forward(group, [0] * upm, unit, token) if j else group
        groups.append([group, [exchange(part, "replica", 1) for part in sent]])
        far += groups[-1][1]
        jobs = [(0, j)] + ([(1, j - 1)] if j else [])
        rights = sum((groups[i][other] for other, i in jobs), [])
        *done, token = outputs(
            pos, owners, comp, left, ltr, bases, places, jobs, rights, upm, earlier=done
        )
    new_feedback, new_weights, new_momentum, new_master, _ = outputs(
        pos,
        owners,
        comp,
        left,
        ltr,
        bases,
        places,
        [(1, half - 1)],
        near + far,
        upm,
        (momentum, master_weights),
        done,
    )

    new_vector_momentum = 0.9 * vector_momentum + vector_total
    new_vector_params = vector_params - 0.1 * new_vector_momentum
    return new_feedback, new_momentum, new_master, new_weights, new_vector_momentum, new_vector_params


def solution(mesh):
    return jax.shard_map(
        per_device,
        mesh=mesh,
        in_specs=(
            P("replica", None, "mp", None),
            P("replica", None, "mp", None),
            P(),
            P(),
            P(),
            P("mp", None, "replica", None),
            P("mp", None, "replica", None),
            P("replica", "mp"),
            P("mp"),
            P("mp"),
        ),
        out_specs=(
            P("replica", None, "mp", None),
            P("mp", None, "replica", None),
            P("mp", None, "replica", None),
            P(None, "replica", None),
            P("mp"),
            P("mp"),
        ),
        check_vma=False,
    )
```

time: 126 us -> 98.7 us (0.78); the launches traced: 125 us -> 98.5 us
  blocking collectives: 31.9 us -> 0 us
  local copies, waits for them, and re-layouts: 16.4 us -> 0.14 us
  waiting for transfers between devices: 16.9 us -> 28.2 us
  starting transfers between devices: 24.4 us -> 31.9 us
  Pallas kernels: 32.7 us -> 36.6 us
    all_to_all x3 -> x0, blocking collectives: 31.9 us -> none  [the longest x2 23.4 us: per_device(): in_plane = lambda x: lax.all_to_all(x, 'mp', 0, 0, tiled=True)]
    ppermute x8 -> x26, starting transfers between devices: 14.5 us -> 31.9 us  [exchange(): return lax.ppermute(x, axis, [(i, i ^ distance) for i in range(size)])]
    ppermute x8 -> x26, waiting for transfers between devices: 11.7 us -> 28.2 us  [exchange(): return lax.ppermute(x, axis, [(i, i ^ distance) for i in range(size)])]
    unnamed x35 -> x15, local copies, waits for them, and re-layouts: 16.3 us -> 0.05 us
    all_to_all x2 -> x0, starting transfers between devices: 9.92 us -> none  [per_device(): lax.all_to_all(x, 'replica', 0, 0, axis_index_groups=columns, tiled=True)]
    all_to_all x2 -> x0, waiting for transfers between devices: 5.21 us -> none  [per_device(): lax.all_to_all(x, 'replica', 0, 0, axis_index_groups=columns, tiled=True)]
    pallas_call x8 -> x14, Pallas kernels: 17.9 us -> 21.6 us  [the longest x5 18.3 us: outputs(): pl.pallas_call(functools.partial(outputs_kernel, jobs, upm, places, len(s...]
  transfers between devices with their start and end apart: 10 -> 26, of which waited for: 6 -> 13; matrix products, arithmetic and copies ran while one was open for 1% -> 1% of each run, Pallas kernels for 11% -> 27%
where the time goes in v6:
time: 98.7 us; the launch traced here: 98.5 us
  Pallas kernels  36.6 us (37%)
  starting transfers between devices  31.9 us (32%)
  waiting for transfers between devices  28.2 us (29%)
  between operations  1.03 us (1%)
    ppermute x26, starting transfers between devices, exchange(): return lax.ppermute(x, axis, [(i, i ^ distance) for i in range(size)])  31.9 us
    ppermute x26, waiting for transfers between devices, exchange(): return lax.ppermute(x, axis, [(i, i ^ distance) for i in range(size)])  28.2 us
    pallas_call x5, Pallas kernels, outputs(): pl.pallas_call(functools.partial(outputs_kernel, jobs, upm, places, len(s...  18.3 us
    pallas_call x1, Pallas kernels, left_terms(): pl.pallas_call(left_kernel, grid_spec=pltpu.PrefetchScalarGridSpec(num_sc...  9.03 us
    pallas_call x1, Pallas kernels, base_of(): pl.pallas_call(base_kernel, in_specs=[pl.BlockSpec(memory_space=pl.ANY)]...  2.65 us
    pallas_call x1, Pallas kernels, right_terms(): pl.pallas_call(functools.partial(send_kernel, half), grid_spec=pltpu.Pref...  2.52 us
  transfers between devices with their start and end apart: 26, of which 13 were waited for; matrix products, arithmetic and copies ran while one was open for 1% of the time, Pallas kernels for 27%

profile of v6, /device:TPU:1, one launch (start us, length us, event | category | flops | bytes accessed | tf_op | source)
XLA Modules:
  0.0 98.5 jit_solution(14200542522351832749)
XLA Ops:
  0.6 2.6 %base.1.refs_0_ = bf16[2,96,3072]{2,1,0:T(8,128)(2,1)S(1)} custom-call(f32[1,2,96,3072]{3,2,1,0:T(8,128)} %refs_13_.1, f32[1,2,96,3072]{3,2,1,0:T(8,128)} %refs_14_.1), custom_call_target="tpu_custom_call" | custom-call | flops 1000 | bytes 1000 | tf_op jit(solution)/shard_map/base/pallas_call | solution.py:504
  3.3 2.1 %collective-permute-start.6 = (bf16[2,96,3072]{2,1,0:T(8,128)(2,1)S(1)}, bf16[2,96,3072]{2,1,0:T(8,128)(2,1)S(1)}, u32[]{:S(2)}, u32[]{:S(2)}) collective-permute-start(bf16[2,96,3072]{2,1,0:T(8,128)(2,1)S(1)} %base.1.refs_0_), channel_id=1, source_target_pairs={{0,2},{1,3},{2,0},{3,1},{4,6},{5,7},{6,4},{7,5},{8,10},{9,11},{10,... | collective-permute-start | bytes 3538952 | tf_op jit(solution)/shard_map/ppermute | solution.py:34
  5.4 1.2 %collective-permute-start.5 = (bf16[2,96,3072]{2,1,0:T(8,128)(2,1)S(1)}, bf16[2,96,3072]{2,1,0:T(8,128)(2,1)S(1)}, u32[]{:S(2)}, u32[]{:S(2)}) collective-permute-start(bf16[2,96,3072]{2,1,0:T(8,128)(2,1)S(1)} %base.1.refs_0_), channel_id=1, source_target_pairs={{0,1},{1,0},{2,3},{3,2},{4,5},{5,4},{6,7},{7,6},{8,9},{9,8},{10,11... | collective-permute-start | bytes 3538952 | tf_op jit(solution)/shard_map/ppermute | solution.py:34
  6.7 9.0 %left_terms.1 = (bf16[8,192,3072]{2,1,0:T(8,128)(2,1)S(1)}, f32[112,256]{1,0:T(8,128)S(1)}, f32[112,256]{1,0:T(8,128)S(1)}) custom-call(s32[8]{0:T(128)S(1)} %stack.32.pos, bf16[1,8,192,3072]{3,2,1,0:T(8,128)(2,1)} %g_ref.1, bf16[1,8,192,3072]{3,2,1,0:T(8,128)(2,1)} %f_ref.1, bf16[8,32,3072]{2,1,0:T(8,128)(2,1)} %bitcast.11, f32[1,2688]{1,0:T(1,128)S(1)} %copy-done.3), custom_call_target="tpu_custom_call" | custom-call | flops 1000 | bytes 1000 | tf_op jit(solution)/shard_map/left_terms/pallas_call | solution.py:86
  15.8 1.3 %collective-permute-start = (f32[112,256]{1,0:T(8,128)S(1)}, f32[112,256]{1,0:T(8,128)S(1)}, u32[]{:S(2)}, u32[]{:S(2)}) collective-permute-start(f32[112,256]{1,0:T(8,128)S(1)} %get-tuple-element.42), channel_id=1, source_target_pairs={{0,4},{4,0},{8,12},{12,8},{16,20},{20,16},{24,28},{28,24},{1,5},{5... | collective-permute-start | bytes 344072 | tf_op jit(solution)/shard_map/ppermute | solution.py:34
  17.1 1.0 collective-permute-done.refs_1_
  18.1 3.4 %collective-permute-start.3 = (bf16[112,256]{1,0:T(8,128)(2,1)S(1)}, bf16[112,256]{1,0:T(8,128)(2,1)S(1)}, u32[]{:S(2)}, u32[]{:S(2)}) collective-permute-start(bf16[112,256]{1,0:T(8,128)(2,1)S(1)} %add.41.refs_0_), channel_id=1, source_target_pairs={{0,24},{4,28},{8,16},{12,20},{16,8},{20,12},{24,0},{28,4},{1,25},{... | collective-permute-start | bytes 172040 | tf_op jit(solution)/shard_map/ppermute | solution.py:34
  21.8 1.3 %collective-permute-done.3.refs_3_ = bf16[112,256]{1,0:T(8,128)(2,1)S(1)} collective-permute-done((bf16[112,256]{1,0:T(8,128)(2,1)S(1)}, bf16[112,256]{1,0:T(8,128)(2,1)S(1)}, u32[]{:S(2)}, u32[]{:S(2)}) %collective-permute-start.3) | collective-permute-done | bytes 57376 | tf_op jit(solution)/shard_map/ppermute | solution.py:34
  23.1 3.4 %collective-permute-done.2.refs_2_ = bf16[112,256]{1,0:T(8,128)(2,1)S(1)} collective-permute-done((bf16[112,256]{1,0:T(8,128)(2,1)S(1)}, bf16[112,256]{1,0:T(8,128)(2,1)S(1)}, u32[]{:S(2)}, u32[]{:S(2)}) %collective-permute-start.2) | collective-permute-done | bytes 57376 | tf_op jit(solution)/shard_map/ppermute | solution.py:34
  26.6 1.0 %collective-permute-start.4 = (f32[112,256]{1,0:T(8,128)S(1)}, f32[112,256]{1,0:T(8,128)S(1)}, u32[]{:S(2)}, u32[]{:S(2)}) collective-permute-start(f32[112,256]{1,0:T(8,128)S(1)} %add.42.near_ref), channel_id=1, source_target_pairs={{0,4},{4,0},{8,12},{12,8},{16,20},{20,16},{24,28},{28,24},{1,5},{5... | collective-permute-start | bytes 344072 | tf_op jit(solution)/shard_map/ppermute | solution.py:34
  27.6 1.0 collective-permute-done.4.far_ref
  28.5 2.5 %right_send.1 = (bf16[4,1,32,3072]{3,2,1,0:T(8,128)(2,1)S(1)}, bf16[256,192]{1,0:T(8,128)(2,1)S(1)}, bf16[8,192,32]{2,1,0:T(8,128)(2,1)S(1)}, f32[32,256]{1,0:T(8,128)S(1)}) custom-call(s32[8]{0:T(128)S(1)} %stack.32.pos, f32[112,256]{1,0:T(8,128)S(1)} %add.42.near_ref, f32[112,256]{1,0:T(8,128)S(1)} %collective-permute-done.4.far_ref, ...), custom_call_target="tpu_custom_call" | custom-call | flops 1000 | bytes 1000 | tf_op jit(solution)/shard_map/right_send/pallas_call | solution.py:172
  31.9 1.9 %right_keep.1.keep_ref = f32[4,1,32,3072]{3,2,1,0:T(8,128)S(1)} custom-call(s32[8]{0:T(128)S(1)} %stack.32.pos, bf16[256,192]{1,0:T(8,128)(2,1)S(1)} %get-tuple-element.44.lt_ref, bf16[8,192,3072]{2,1,0:T(8,128)(2,1)S(1)} %get-tuple-element.40.comp_ref, bf16[2,96,3072]{2,1,0:T(8,128)(2,1)S(1)} %collective-permute-done.5.refs_0_.refs_1_, ...), custom_call_target="tpu_custom_call" | custom-call | flops 9437184000 | bytes 1000 | tf_op jit(solution)/shard_map/right_keep/pallas_call | solution.py:196
  34.6 1.3 %collective-permute-start.8 = (bf16[40,3072]{1,0:T(8,128)(2,1)S(1)}, bf16[40,3072]{1,0:T(8,128)(2,1)S(1)}, u32[]{:S(2)}, u32[]{:S(2)}) collective-permute-start(bf16[40,3072]{1,0:T(8,128)(2,1)S(1)} %get-tuple-element.48), channel_id=1, source_target_pairs={{0,1},{1,0},{2,3},{3,2},{4,5},{5,4},{6,7},{7,6},{8,9},{9,8},{10,11... | collective-permute-start | bytes 737288 | tf_op jit(solution)/shard_map/ppermute | solution.py:34
  36.2 1.1 %collective-permute-start.10 = (bf16[40,3072]{1,0:T(8,128)(2,1)S(1)}, bf16[40,3072]{1,0:T(8,128)(2,1)S(1)}, u32[]{:S(2)}, u32[]{:S(2)}) collective-permute-start(bf16[40,3072]{1,0:T(8,128)(2,1)S(1)} %get-tuple-element.50), channel_id=1, source_target_pairs={{0,3},{1,2},{2,1},{3,0},{4,7},{5,6},{6,5},{7,4},{8,11},{9,10},{10,... | collective-permute-start | bytes 737288 | tf_op jit(solution)/shard_map/ppermute | solution.py:34
  37.4 2.9 %collective-permute-done.8.refs_0_ = bf16[40,3072]{1,0:T(8,128)(2,1)S(1)} collective-permute-done((bf16[40,3072]{1,0:T(8,128)(2,1)S(1)}, bf16[40,3072]{1,0:T(8,128)(2,1)S(1)}, u32[]{:S(2)}, u32[]{:S(2)}) %collective-permute-start.8) | collective-permute-done | bytes 245792 | tf_op jit(solution)/shard_map/ppermute | solution.py:34
  40.3 1.9 %collective-permute-done.9.refs_1_ = bf16[40,3072]{1,0:T(8,128)(2,1)S(1)} collective-permute-done((bf16[40,3072]{1,0:T(8,128)(2,1)S(1)}, bf16[40,3072]{1,0:T(8,128)(2,1)S(1)}, u32[]{:S(2)}, u32[]{:S(2)}) %collective-permute-start.9) | collective-permute-done | bytes 245792 | tf_op jit(solution)/shard_map/ppermute | solution.py:34
  42.2 3.8 %collective-permute-done.10.refs_2_ = bf16[40,3072]{1,0:T(8,128)(2,1)S(1)} collective-permute-done((bf16[40,3072]{1,0:T(8,128)(2,1)S(1)}, bf16[40,3072]{1,0:T(8,128)(2,1)S(1)}, u32[]{:S(2)}, u32[]{:S(2)}) %collective-permute-start.10) | collective-permute-done | bytes 245792 | tf_op jit(solution)/shard_map/ppermute | solution.py:34
  47.7 1.2 %collective-permute-start.12 = (bf16[1,96,3072]{2,1,0:T(8,128)(2,1)S(1)}, bf16[1,96,3072]{2,1,0:T(8,128)(2,1)S(1)}, u32[]{:S(2)}, u32[]{:S(2)}) collective-permute-start(bf16[1,96,3072]{2,1,0:T(8,128)(2,1)S(1)} %get-tuple-element.53), channel_id=1, source_target_pairs={{0,1},{1,0},{2,3},{3,2},{4,5},{5,4},{6,7},{7,6},{8,9},{9,8},{10,11... | collective-permute-start | bytes 1769480 | tf_op jit(solution)/shard_map/ppermute | solution.py:34
  48.9 1.3 %collective-permute-start.13 = (bf16[32,768]{1,0:T(8,128)(2,1)S(1)}, bf16[32,768]{1,0:T(8,128)(2,1)S(1)}, u32[]{:S(2)}, u32[]{:S(2)}) collective-permute-start(bf16[32,768]{1,0:T(8,128)(2,1)S(1)} %get-tuple-element.55), channel_id=1, source_target_pairs={{0,8},{4,12},{8,0},{12,4},{16,24},{20,28},{24,16},{28,20},{1,9},{5... | collective-permute-start | bytes 147464 | tf_op jit(solution)/shard_map/ppermute | solution.py:34
  50.2 2.3 %collective-permute-start.14 = (bf16[32,768]{1,0:T(8,128)(2,1)S(1)}, bf16[32,768]{1,0:T(8,128)(2,1)S(1)}, u32[]{:S(2)}, u32[]{:S(2)}) collective-permute-start(bf16[32,768]{1,0:T(8,128)(2,1)S(1)} %get-tuple-element.56), channel_id=1, source_target_pairs={{0,16},{4,20},{8,24},{12,28},{16,0},{20,4},{24,8},{28,12},{1,17},{... | collective-permute-start | bytes 147464 | tf_op jit(solution)/shard_map/ppermute | solution.py:34
  52.5 2.0 %collective-permute-done.14 = bf16[32,768]{1,0:T(8,128)(2,1)S(1)} collective-permute-done((bf16[32,768]{1,0:T(8,128)(2,1)S(1)}, bf16[32,768]{1,0:T(8,128)(2,1)S(1)}, u32[]{:S(2)}, u32[]{:S(2)}) %collective-permute-start.14) | collective-permute-done | bytes 49184 | tf_op jit(solution)/shard_map/ppermute | solution.py:34
  54.5 2.9 %collective-permute-done.15 = bf16[32,768]{1,0:T(8,128)(2,1)S(1)} collective-permute-done((bf16[32,768]{1,0:T(8,128)(2,1)S(1)}, bf16[32,768]{1,0:T(8,128)(2,1)S(1)}, u32[]{:S(2)}, u32[]{:S(2)}) %collective-permute-start.15) | collective-permute-done | bytes 49184 | tf_op jit(solution)/shard_map/ppermute | solution.py:34
  57.9 3.2 %collective-permute-start.16 = (bf16[32,768]{1,0:T(8,128)(2,1)S(1)}, bf16[32,768]{1,0:T(8,128)(2,1)S(1)}, u32[]{:S(2)}, u32[]{:S(2)}) collective-permute-start(bf16[32,768]{1,0:T(8,128)(2,1)S(1)} %add_convert_fusion.refs_0_), channel_id=1, source_target_pairs={{0,8},{4,12},{8,0},{12,4},{16,24},{20,28},{24,16},{28,20},{1,9},{5... | collective-permute-start | bytes 147464 | tf_op jit(solution)/shard_map/ppermute | solution.py:34
  63.7 6.0 %collective-permute-start.22 = (bf16[32,3072]{1,0:T(8,128)(2,1)S(1)}, bf16[32,3072]{1,0:T(8,128)(2,1)S(1)}, u32[]{:S(2)}, u32[]{:S(2)}) collective-permute-start(bf16[32,3072]{1,0:T(8,128)(2,1)S(1)} %column_gather.1.refs_5_), channel_id=1, source_target_pairs={{0,4},{4,0},{8,12},{12,8},{16,20},{20,16},{24,28},{28,24},{1,5},{5... | collective-permute-start | bytes 589832 | tf_op jit(solution)/shard_map/ppermute | solution.py:34
  69.7 2.2 %collective-permute-start.21 = (bf16[32,3072]{1,0:T(8,128)(2,1)S(1)}, bf16[32,3072]{1,0:T(8,128)(2,1)S(1)}, u32[]{:S(2)}, u32[]{:S(2)}) collective-permute-start(bf16[32,3072]{1,0:T(8,128)(2,1)S(1)} %column_gather.1.refs_5_), channel_id=1, source_target_pairs={{0,3},{1,2},{2,1},{3,0},{4,7},{5,6},{6,5},{7,4},{8,11},{9,10},{10,... | collective-permute-start | bytes 589832 | tf_op jit(solution)/shard_map/ppermute | solution.py:34
  72.4 2.4 %outputs.5 = (bf16[1,8,192,3072]{3,2,1,0:T(8,128)(2,1)}, bf16[8,96,3072]{2,1,0:T(8,128)(2,1)}, f32[8,128]{1,0:T(8,128)S(1)}) custom-call(s32[8]{0:T(128)S(1)} %stack.32.pos, s32[8]{0:T(128)S(1)} %copy-done.4, bf16[8,192,3072]{2,1,0:T(8,128)(2,1)S(1)} %get-tuple-element.40.comp_ref, bf16[8,192,32]{2,1,0:T(8,128)(2,1)S(1)} %get-tuple-element.43.left_ref, ...), custom_call_target="tpu_custom_call" | custom-call | flops 11796480000 | bytes 1000 | tf_op jit(solution)/shard_map/outputs/pallas_call | solution.py:459
  74.7 6.0 %collective-permute-done.19.refs_0_.refs_5_.refs_6_ = bf16[32,3072]{1,0:T(8,128)(2,1)S(1)} collective-permute-done((bf16[32,3072]{1,0:T(8,128)(2,1)S(1)}, bf16[32,3072]{1,0:T(8,128)(2,1)S(1)}, u32[]{:S(2)}, u32[]{:S(2)}) %collective-permute-start.19) | collective-permute-done | bytes 196640 | tf_op jit(solution)/shard_map/ppermute | solution.py:34
  81.7 3.2 %outputs.6 = (bf16[1,8,192,3072]{3,2,1,0:T(8,128)(2,1)}, bf16[8,96,3072]{2,1,0:T(8,128)(2,1)}, f32[8,128]{1,0:T(8,128)S(1)}) custom-call(s32[8]{0:T(128)S(1)} %stack.32.pos, s32[8]{0:T(128)S(1)} %copy-done.4, bf16[8,192,3072]{2,1,0:T(8,128)(2,1)S(1)} %get-tuple-element.40.comp_ref, ...), custom_call_target="tpu_custom_call", output_to_operand_aliasing={{0}: (12, {}), {1}: (13, {})} | custom-call | flops 23592960000 | bytes 1000 | tf_op jit(solution)/shard_map/outputs/pallas_call | solution.py:459
  85.0 3.4 %outputs.7 = (bf16[1,8,192,3072]{3,2,1,0:T(8,128)(2,1)}, bf16[8,96,3072]{2,1,0:T(8,128)(2,1)}, f32[8,128]{1,0:T(8,128)S(1)}) custom-call(s32[8]{0:T(128)S(1)} %stack.32.pos, s32[8]{0:T(128)S(1)} %copy-done.4, bf16[8,192,3072]{2,1,0:T(8,128)(2,1)S(1)} %get-tuple-element.40.comp_ref, ...), custom_call_target="tpu_custom_call", output_to_operand_aliasing={{0}: (12, {}), {1}: (13, {})} | custom-call | flops 23592960000 | bytes 1000 | tf_op jit(solution)/shard_map/outputs/pallas_call | solution.py:459
  88.9 3.8 %outputs.8 = (bf16[1,8,192,3072]{3,2,1,0:T(8,128)(2,1)}, bf16[8,96,3072]{2,1,0:T(8,128)(2,1)}, f32[8,128]{1,0:T(8,128)}) custom-call(s32[8]{0:T(128)S(1)} %stack.32.pos, s32[8]{0:T(128)S(1)} %copy-done.4, bf16[8,192,3072]{2,1,0:T(8,128)(2,1)S(1)} %get-tuple-element.40.comp_ref, ...), custom_call_target="tpu_custom_call", output_to_operand_aliasing={{0}: (12, {}), {1}: (13, {})} | custom-call | flops 23592960000 | bytes 1000 | tf_op jit(solution)/shard_map/outputs/pallas_call | solution.py:459
  92.7 5.6 %outputs.9 = (bf16[1,8,192,3072]{3,2,1,0:T(8,128)(2,1)}, bf16[8,96,3072]{2,1,0:T(8,128)(2,1)}, f32[1,2,96,3072]{3,2,1,0:T(8,128)}, f32[1,2,96,3072]{3,2,1,0:T(8,128)}, f32[8,128]{1,0:T(8,128)}) custom-call(s32[8]{0:T(128)S(1)} %stack.32.pos, s32[8]{0:T(128)S(1)} %copy-done.4, ...), custom_call_target="tpu_custom_call", output_to_operand_aliasing={{0}: (20, {}), {1}: (21, {})} | custom-call | flops 11796480000 | bytes 1000 | tf_op jit(solution)/shard_map/outputs/pallas_call | solution.py:459
  (56 shorter events, 9.3 us)
Async XLA Ops:
  0.6 6.1 %copy-start.3 = (f32[1,2688]{1,0:T(1,128)S(1)}, f32[1,2688]{1,0:T(1,128)}, u32[]{:S(2)}) copy-start(f32[1,2688]{1,0:T(1,128)} %vec_ref.1) | copy-start | bytes 32260
  3.3 28.2 %collective-permute-start.6 = (bf16[2,96,3072]{2,1,0:T(8,128)(2,1)S(1)}, bf16[2,96,3072]{2,1,0:T(8,128)(2,1)S(1)}, u32[]{:S(2)}, u32[]{:S(2)}) collective-permute-start(bf16[2,96,3072]{2,1,0:T(8,128)(2,1)S(1)} %base.1.refs_0_), channel_id=1, source_target_pairs={{0,2},{1,3},{2,0},{3,1},{4,6},{5,7},{6,4},{7,5},{8,10},{9,11},{10,... | collective-permute-start | bytes 3538952 | tf_op jit(solution)/shard_map/ppermute | solution.py:34
  5.4 26.5 %collective-permute-start.5 = (bf16[2,96,3072]{2,1,0:T(8,128)(2,1)S(1)}, bf16[2,96,3072]{2,1,0:T(8,128)(2,1)S(1)}, u32[]{:S(2)}, u32[]{:S(2)}) collective-permute-start(bf16[2,96,3072]{2,1,0:T(8,128)(2,1)S(1)} %base.1.refs_0_), channel_id=1, source_target_pairs={{0,1},{1,0},{2,3},{3,2},{4,5},{5,4},{6,7},{7,6},{8,9},{9,8},{10,11... | collective-permute-start | bytes 3538952 | tf_op jit(solution)/shard_map/ppermute | solution.py:34
  6.7 21.8 %copy-start.2 = (f32[8,32,32]{2,1,0:T(8,128)S(1)}, f32[8,32,32]{2,1,0:T(8,128)}, u32[]{:S(2)}) copy-start(f32[8,32,32]{2,1,0:T(8,128)} %gram_ref.1) | copy-start | bytes 98308
  15.8 2.3 %collective-permute-start = (f32[112,256]{1,0:T(8,128)S(1)}, f32[112,256]{1,0:T(8,128)S(1)}, u32[]{:S(2)}, u32[]{:S(2)}) collective-permute-start(f32[112,256]{1,0:T(8,128)S(1)} %get-tuple-element.42), channel_id=1, source_target_pairs={{0,4},{4,0},{8,12},{12,8},{16,20},{20,16},{24,28},{28,24},{1,5},{5... | collective-permute-start | bytes 344072 | tf_op jit(solution)/shard_map/ppermute | solution.py:34
  18.1 5.1 %collective-permute-start.3 = (bf16[112,256]{1,0:T(8,128)(2,1)S(1)}, bf16[112,256]{1,0:T(8,128)(2,1)S(1)}, u32[]{:S(2)}, u32[]{:S(2)}) collective-permute-start(bf16[112,256]{1,0:T(8,128)(2,1)S(1)} %add.41.refs_0_), channel_id=1, source_target_pairs={{0,24},{4,28},{8,16},{12,20},{16,8},{20,12},{24,0},{28,4},{1,25},{... | collective-permute-start | bytes 172040 | tf_op jit(solution)/shard_map/ppermute | solution.py:34
  21.4 5.1 %collective-permute-start.2 = (bf16[112,256]{1,0:T(8,128)(2,1)S(1)}, bf16[112,256]{1,0:T(8,128)(2,1)S(1)}, u32[]{:S(2)}, u32[]{:S(2)}) collective-permute-start(bf16[112,256]{1,0:T(8,128)(2,1)S(1)} %add.41.refs_0_), channel_id=1, source_target_pairs={{0,16},{4,20},{8,24},{12,28},{16,0},{20,4},{24,8},{28,12},{1,17},{... | collective-permute-start | bytes 172040 | tf_op jit(solution)/shard_map/ppermute | solution.py:34
  21.4 5.1 %collective-permute-start.1 = (bf16[112,256]{1,0:T(8,128)(2,1)S(1)}, bf16[112,256]{1,0:T(8,128)(2,1)S(1)}, u32[]{:S(2)}, u32[]{:S(2)}) collective-permute-start(bf16[112,256]{1,0:T(8,128)(2,1)S(1)} %add.41.refs_0_), channel_id=1, source_target_pairs={{0,8},{4,12},{8,0},{12,4},{16,24},{20,28},{24,16},{28,20},{1,9},{5... | collective-permute-start | bytes 172040 | tf_op jit(solution)/shard_map/ppermute | solution.py:34
  26.6 2.0 %collective-permute-start.4 = (f32[112,256]{1,0:T(8,128)S(1)}, f32[112,256]{1,0:T(8,128)S(1)}, u32[]{:S(2)}, u32[]{:S(2)}) collective-permute-start(f32[112,256]{1,0:T(8,128)S(1)} %add.42.near_ref), channel_id=1, source_target_pairs={{0,4},{4,0},{8,12},{12,8},{16,20},{20,16},{24,28},{28,24},{1,5},{5... | collective-permute-start | bytes 344072 | tf_op jit(solution)/shard_map/ppermute | solution.py:34
  31.1 2.8 %collective-permute-start.7 = (bf16[4,1,32,3072]{3,2,1,0:T(8,128)(2,1)S(1)}, bf16[4,1,32,3072]{3,2,1,0:T(8,128)(2,1)S(1)}, u32[]{:S(2)}, u32[]{:S(2)}) collective-permute-start(bf16[4,1,32,3072]{3,2,1,0:T(8,128)(2,1)S(1)} %get-tuple-element.45), channel_id=1, source_target_pairs={{0,4},{4,0},{8,12},{12,8},{16,20},{20,16},{24,28},{28,24},{1,5},{5... | collective-permute-start | bytes 2359304 | tf_op jit(solution)/shard_map/ppermute | solution.py:34
  34.6 5.6 %collective-permute-start.8 = (bf16[40,3072]{1,0:T(8,128)(2,1)S(1)}, bf16[40,3072]{1,0:T(8,128)(2,1)S(1)}, u32[]{:S(2)}, u32[]{:S(2)}) collective-permute-start(bf16[40,3072]{1,0:T(8,128)(2,1)S(1)} %get-tuple-element.48), channel_id=1, source_target_pairs={{0,1},{1,0},{2,3},{3,2},{4,5},{5,4},{6,7},{7,6},{8,9},{9,8},{10,11... | collective-permute-start | bytes 737288 | tf_op jit(solution)/shard_map/ppermute | solution.py:34
  35.9 6.3 %collective-permute-start.9 = (bf16[40,3072]{1,0:T(8,128)(2,1)S(1)}, bf16[40,3072]{1,0:T(8,128)(2,1)S(1)}, u32[]{:S(2)}, u32[]{:S(2)}) collective-permute-start(bf16[40,3072]{1,0:T(8,128)(2,1)S(1)} %get-tuple-element.49), channel_id=1, source_target_pairs={{0,2},{1,3},{2,0},{3,1},{4,6},{5,7},{6,4},{7,5},{8,10},{9,11},{10,... | collective-permute-start | bytes 737288 | tf_op jit(solution)/shard_map/ppermute | solution.py:34
  36.2 9.8 %collective-permute-start.10 = (bf16[40,3072]{1,0:T(8,128)(2,1)S(1)}, bf16[40,3072]{1,0:T(8,128)(2,1)S(1)}, u32[]{:S(2)}, u32[]{:S(2)}) collective-permute-start(bf16[40,3072]{1,0:T(8,128)(2,1)S(1)} %get-tuple-element.50), channel_id=1, source_target_pairs={{0,3},{1,2},{2,1},{3,0},{4,7},{5,6},{6,5},{7,4},{8,11},{9,10},{10,... | collective-permute-start | bytes 737288 | tf_op jit(solution)/shard_map/ppermute | solution.py:34
  46.8 14.3 %copy-start.5 = (f32[2688]{0:T(1024)S(1)}, f32[2688]{0:T(1024)}, u32[]{:S(2)}) copy-start(f32[2688]{0:T(1024)} %param.19) | copy-start | bytes 32260
  46.8 14.3 %copy-start.6 = (f32[2688]{0:T(1024)S(1)}, f32[2688]{0:T(1024)}, u32[]{:S(2)}) copy-start(f32[2688]{0:T(1024)} %param.18) | copy-start | bytes 32260
  46.8 25.6 %copy-start.4 = (s32[8]{0:T(128)S(1)}, s32[8]{0:T(128)}, u32[]{:S(2)}) copy-start(s32[8]{0:T(128)} %owners.9) | copy-start | bytes 100
  46.9 25.0 %collective-permute-start.11 = (bf16[1,96,3072]{2,1,0:T(8,128)(2,1)S(1)}, bf16[1,96,3072]{2,1,0:T(8,128)(2,1)S(1)}, u32[]{:S(2)}, u32[]{:S(2)}) collective-permute-start(bf16[1,96,3072]{2,1,0:T(8,128)(2,1)S(1)} %get-tuple-element.52), channel_id=1, source_target_pairs={{0,2},{1,3},{2,0},{3,1},{4,6},{5,7},{6,4},{7,5},{8,10},{9,11},{10,... | collective-permute-start | bytes 1769480 | tf_op jit(solution)/shard_map/ppermute | solution.py:34
  47.7 24.7 %collective-permute-start.12 = (bf16[1,96,3072]{2,1,0:T(8,128)(2,1)S(1)}, bf16[1,96,3072]{2,1,0:T(8,128)(2,1)S(1)}, u32[]{:S(2)}, u32[]{:S(2)}) collective-permute-start(bf16[1,96,3072]{2,1,0:T(8,128)(2,1)S(1)} %get-tuple-element.53), channel_id=1, source_target_pairs={{0,1},{1,0},{2,3},{3,2},{4,5},{5,4},{6,7},{7,6},{8,9},{9,8},{10,11... | collective-permute-start | bytes 1769480 | tf_op jit(solution)/shard_map/ppermute | solution.py:34
  48.9 3.6 %collective-permute-start.13 = (bf16[32,768]{1,0:T(8,128)(2,1)S(1)}, bf16[32,768]{1,0:T(8,128)(2,1)S(1)}, u32[]{:S(2)}, u32[]{:S(2)}) collective-permute-start(bf16[32,768]{1,0:T(8,128)(2,1)S(1)} %get-tuple-element.55), channel_id=1, source_target_pairs={{0,8},{4,12},{8,0},{12,4},{16,24},{20,28},{24,16},{28,20},{1,9},{5... | collective-permute-start | bytes 147464 | tf_op jit(solution)/shard_map/ppermute | solution.py:34
  50.2 4.4 %collective-permute-start.14 = (bf16[32,768]{1,0:T(8,128)(2,1)S(1)}, bf16[32,768]{1,0:T(8,128)(2,1)S(1)}, u32[]{:S(2)}, u32[]{:S(2)}) collective-permute-start(bf16[32,768]{1,0:T(8,128)(2,1)S(1)} %get-tuple-element.56), channel_id=1, source_target_pairs={{0,16},{4,20},{8,24},{12,28},{16,0},{20,4},{24,8},{28,12},{1,17},{... | collective-permute-start | bytes 147464 | tf_op jit(solution)/shard_map/ppermute | solution.py:34
  52.5 4.9 %collective-permute-start.15 = (bf16[32,768]{1,0:T(8,128)(2,1)S(1)}, bf16[32,768]{1,0:T(8,128)(2,1)S(1)}, u32[]{:S(2)}, u32[]{:S(2)}) collective-permute-start(bf16[32,768]{1,0:T(8,128)(2,1)S(1)} %get-tuple-element.57), channel_id=1, source_target_pairs={{0,24},{4,28},{8,16},{12,20},{16,8},{20,12},{24,0},{28,4},{1,25},{... | collective-permute-start | bytes 147464 | tf_op jit(solution)/shard_map/ppermute | solution.py:34
  57.4 4.8 %collective-permute-start.18 = (bf16[32,768]{1,0:T(8,128)(2,1)S(1)}, bf16[32,768]{1,0:T(8,128)(2,1)S(1)}, u32[]{:S(2)}, u32[]{:S(2)}) collective-permute-start(bf16[32,768]{1,0:T(8,128)(2,1)S(1)} %add_convert_fusion.refs_0_), channel_id=1, source_target_pairs={{0,24},{4,28},{8,16},{12,20},{16,8},{20,12},{24,0},{28,4},{1,25},{... | collective-permute-start | bytes 147464 | tf_op jit(solution)/shard_map/ppermute | solution.py:34
  57.9 5.3 %collective-permute-start.17 = (bf16[32,768]{1,0:T(8,128)(2,1)S(1)}, bf16[32,768]{1,0:T(8,128)(2,1)S(1)}, u32[]{:S(2)}, u32[]{:S(2)}) collective-permute-start(bf16[32,768]{1,0:T(8,128)(2,1)S(1)} %add_convert_fusion.refs_0_), channel_id=1, source_target_pairs={{0,16},{4,20},{8,24},{12,28},{16,0},{20,4},{24,8},{28,12},{1,17},{... | collective-permute-start | bytes 147464 | tf_op jit(solution)/shard_map/ppermute | solution.py:34
  57.9 5.3 %collective-permute-start.16 = (bf16[32,768]{1,0:T(8,128)(2,1)S(1)}, bf16[32,768]{1,0:T(8,128)(2,1)S(1)}, u32[]{:S(2)}, u32[]{:S(2)}) collective-permute-start(bf16[32,768]{1,0:T(8,128)(2,1)S(1)} %add_convert_fusion.refs_0_), channel_id=1, source_target_pairs={{0,8},{4,12},{8,0},{12,4},{16,24},{20,28},{24,16},{28,20},{1,9},{5... | collective-permute-start | bytes 147464 | tf_op jit(solution)/shard_map/ppermute | solution.py:34
  63.7 17.9 %collective-permute-start.22 = (bf16[32,3072]{1,0:T(8,128)(2,1)S(1)}, bf16[32,3072]{1,0:T(8,128)(2,1)S(1)}, u32[]{:S(2)}, u32[]{:S(2)}) collective-permute-start(bf16[32,3072]{1,0:T(8,128)(2,1)S(1)} %column_gather.1.refs_5_), channel_id=1, source_target_pairs={{0,4},{4,0},{8,12},{12,8},{16,20},{20,16},{24,28},{28,24},{1,5},{5... | collective-permute-start | bytes 589832 | tf_op jit(solution)/shard_map/ppermute | solution.py:34
  69.7 18.7 %collective-permute-start.21 = (bf16[32,3072]{1,0:T(8,128)(2,1)S(1)}, bf16[32,3072]{1,0:T(8,128)(2,1)S(1)}, u32[]{:S(2)}, u32[]{:S(2)}) collective-permute-start(bf16[32,3072]{1,0:T(8,128)(2,1)S(1)} %column_gather.1.refs_5_), channel_id=1, source_target_pairs={{0,3},{1,2},{2,1},{3,0},{4,7},{5,6},{6,5},{7,4},{8,11},{9,10},{10,... | collective-permute-start | bytes 589832 | tf_op jit(solution)/shard_map/ppermute | solution.py:34
  71.9 12.9 %collective-permute-start.20 = (bf16[32,3072]{1,0:T(8,128)(2,1)S(1)}, bf16[32,3072]{1,0:T(8,128)(2,1)S(1)}, u32[]{:S(2)}, u32[]{:S(2)}) collective-permute-start(bf16[32,3072]{1,0:T(8,128)(2,1)S(1)} %column_gather.1.refs_5_), channel_id=1, source_target_pairs={{0,2},{1,3},{2,0},{3,1},{4,6},{5,7},{6,4},{7,5},{8,10},{9,11},{10,... | collective-permute-start | bytes 589832 | tf_op jit(solution)/shard_map/ppermute | solution.py:34
  71.9 8.8 %collective-permute-start.19 = (bf16[32,3072]{1,0:T(8,128)(2,1)S(1)}, bf16[32,3072]{1,0:T(8,128)(2,1)S(1)}, u32[]{:S(2)}, u32[]{:S(2)}) collective-permute-start(bf16[32,3072]{1,0:T(8,128)(2,1)S(1)} %column_gather.1.refs_5_), channel_id=1, source_target_pairs={{0,1},{1,0},{2,3},{3,2},{4,5},{5,4},{6,7},{7,6},{8,9},{9,8},{10,11... | collective-permute-start | bytes 589832 | tf_op jit(solution)/shard_map/ppermute | solution.py:34
  80.7 4.2 %collective-permute-start.23 = (bf16[32,3072]{1,0:T(8,128)(2,1)S(1)}, bf16[32,3072]{1,0:T(8,128)(2,1)S(1)}, u32[]{:S(2)}, u32[]{:S(2)}) collective-permute-start(bf16[32,3072]{1,0:T(8,128)(2,1)S(1)} %forward.5), channel_id=1, source_target_pairs={{0,4},{4,0},{8,12},{12,8},{16,20},{20,16},{24,28},{28,24},{1,5},{5... | collective-permute-start | bytes 589832 | tf_op jit(solution)/shard_map/ppermute | solution.py:34
  84.9 4.0 %collective-permute-start.24 = (bf16[32,3072]{1,0:T(8,128)(2,1)S(1)}, bf16[32,3072]{1,0:T(8,128)(2,1)S(1)}, u32[]{:S(2)}, u32[]{:S(2)}) collective-permute-start(bf16[32,3072]{1,0:T(8,128)(2,1)S(1)} %forward.6), channel_id=1, source_target_pairs={{0,4},{4,0},{8,12},{12,8},{16,20},{20,16},{24,28},{28,24},{1,5},{5... | collective-permute-start | bytes 589832 | tf_op jit(solution)/shard_map/ppermute | solution.py:34
  88.4 4.3 %collective-permute-start.25 = (bf16[32,3072]{1,0:T(8,128)(2,1)S(1)}, bf16[32,3072]{1,0:T(8,128)(2,1)S(1)}, u32[]{:S(2)}, u32[]{:S(2)}) collective-permute-start(bf16[32,3072]{1,0:T(8,128)(2,1)S(1)} %forward.7), channel_id=1, source_target_pairs={{0,4},{4,0},{8,12},{12,8},{16,20},{20,16},{24,28},{28,24},{1,5},{5... | collective-permute-start | bytes 589832 | tf_op jit(solution)/shard_map/ppermute | solution.py:34
  88.9 3.8 %copy-start.1 = (f32[1,2,96,3072]{3,2,1,0:T(8,128)S(1)}, f32[1,2,96,3072]{3,2,1,0:T(8,128)}, u32[]{:S(2)}) copy-start(f32[1,2,96,3072]{3,2,1,0:T(8,128)} %refs_14_.1) | copy-start | bytes 7077892
  (1 other events, 3.8 us)

commit v7 on v6

v7 whole, which is shorter than its diff:
```python
import functools

import jax
import jax.numpy as jnp
from jax import lax
from jax.experimental import pallas as pl
from jax.experimental.pallas import tpu as pltpu
from jax.sharding import PartitionSpec as P

CORES = 2
AHEAD = 4
BASE_ROWS = 16
COLUMNS = 256
F32 = jnp.float32
BF16 = jnp.bfloat16


def params(mib=12):
    return pltpu.CompilerParams(vmem_limit_bytes=mib * 1024 * 1024)


def cost(flops=1000, bytes_accessed=1000):
    return pl.CostEstimate(flops=flops, bytes_accessed=bytes_accessed, transcendentals=0)


def tree_sum(terms):
    while len(terms) > 1:
        terms = [terms[i] + terms[i + 1] for i in range(0, len(terms), 2)]
    return terms[0]


def exchange(x, axis, distance):
    size = lax.axis_size(axis)
    return lax.ppermute(x, axis, [(i, i ^ distance) for i in range(size)])


def left_kernel(pos, g_ref, f_ref, q_ref, vec_ref, comp_ref, near_ref, far_ref, total, feedback, right, sems):
    nmat, rows, _ = comp_ref.shape
    rank = q_ref.shape[1]
    part = near_ref.shape[0]
    cut = rows // 2 if rows % 32 == 0 else rows

    def copies(k):
        out = [pltpu.make_async_copy(q_ref.at[k], right.at[k], sems.at[k, 4])]
        for i, first in enumerate(range(0, rows, cut)):
            block = pl.ds(first, cut)
            for j, (source, target) in enumerate(((g_ref, comp_ref), (f_ref, feedback))):
                source, target = source.at[0, k, block], target.at[k, block]
                out.append(pltpu.make_async_copy(source, target, sems.at[k, 2 * i + j]))
        return out

    for k in range(min(AHEAD, nmat)):
        for copy in copies(k):
            copy.start()
    total[...] = jnp.zeros(total.shape, F32)
    width, nvec = total.shape[1], vec_ref.shape[1]
    for i, first in enumerate(range(0, nvec, width)):
        count = min(width, nvec - first)
        total[rows + i : rows + i + 1, :count] = vec_ref[:, first : first + count]

    for k in range(nmat):
        for copy in copies(k):
            copy.wait()
        if k + AHEAD < nmat:
            for copy in copies(k + AHEAD):
                copy.start()
        comp = comp_ref[k] + feedback[k]
        comp_ref[k] = comp
        total[:rows, k * rank : (k + 1) * rank] = lax.dot_general(
            comp, right[k], (((1,), (1,)), ((), ())), preferred_element_type=F32
        )

    for ref, core in ((near_ref, pos[2]), (far_ref, 1 - pos[2])):
        ref[...] = total[pl.ds(pl.multiple_of(core * part, 16), part), :]


def left_terms(pos, gradients, feedback, right_t, vec):
    _, nmat, rows, n = gradients.shape
    rank = right_t.shape[1]
    width = nmat * rank
    total = rows + -(-vec.shape[1] // width)
    total += -total % (16 * CORES)
    part = jax.ShapeDtypeStruct((total // CORES, width), F32)
    vmem = pl.BlockSpec(memory_space=pltpu.VMEM)
    any_spec = pl.BlockSpec(memory_space=pl.ANY)
    return pl.pallas_call(
        left_kernel,
        grid_spec=pltpu.PrefetchScalarGridSpec(
            num_scalar_prefetch=1,
            grid=(1,),
            in_specs=[any_spec] * 3 + [vmem],
            out_specs=[vmem] * 3,
            scratch_shapes=[
                pltpu.VMEM((total, width), F32),
                pltpu.VMEM((nmat, rows, n), BF16),
                pltpu.VMEM((nmat, rank, n), BF16),
                pltpu.SemaphoreType.DMA((nmat, 5)),
            ],
        ),
        out_shape=[jax.ShapeDtypeStruct((nmat, rows, n), BF16), part, part],
        compiler_params=params(20),
        cost_estimate=cost(),
        name="left_terms",
    )(pos, gradients, feedback, right_t, vec)


def add_kernel(one_ref, other_ref, *refs):
    out = refs[-1]
    out[...] = (one_ref[...].astype(F32) + other_ref[...].astype(F32)).astype(out.dtype)


def add(parts, dtype, after=()):
    vmem = pl.BlockSpec(memory_space=pltpu.VMEM)
    return pl.pallas_call(
        add_kernel,
        in_specs=[vmem] * 2 + [pl.BlockSpec(memory_space=pl.ANY)] * len(after),
        out_specs=vmem,
        out_shape=jax.ShapeDtypeStruct(parts[0].shape, dtype),
        compiler_params=params(),
        cost_estimate=cost(),
        name="add",
    )(*parts, *after)


def send_kernel(half, pos, near_ref, far_ref, gram_ref, comp_ref, send_ref, lt_ref, mix_ref, vec_ref, left, gram):
    nmat, rows, _ = comp_ref.shape
    rank = gram_ref.shape[1]
    part = near_ref.shape[0]
    for ref, core in ((near_ref, pos[2]), (far_ref, 1 - pos[2])):
        left[pl.ds(pl.multiple_of(core * part, 16), part), :] = ref[...]
    vec_ref[...] = left[rows:, :]
    gram[...] = jnp.zeros(gram.shape, F32)
    for i in range(nmat):
        gram[i * rank : (i + 1) * rank, i * rank : (i + 1) * rank] = gram_ref[i]
    hat = jnp.dot(
        left[:rows, :], gram[...], precision=lax.Precision.HIGHEST, preferred_element_type=F32
    )
    lt_ref[...] = hat.T.astype(BF16)
    mix_ref[:, :, :rows] = jnp.broadcast_to(unit_matrix(rows), (nmat, rows, rows))
    for i in range(nmat):
        mix_ref[i, :, rows:] = -hat[:, i * rank : (i + 1) * rank].astype(BF16)
    right_rows(half, pos, lt_ref, comp_ref, send_ref)


def unit_matrix(size):
    row = lax.broadcasted_iota(jnp.int32, (size, size), 0)
    col = lax.broadcasted_iota(jnp.int32, (size, size), 1)
    return jnp.where(row == col, 1.0, 0.0).astype(BF16)


def right_rows(start, pos, lt_ref, comp_ref, out_ref):
    half, upm, unit, _ = out_ref.shape
    for t in range(half):
        k = (t + start) ^ pos[0]
        rows = pl.ds(pl.multiple_of(k * upm * unit, upm * unit), upm * unit)
        terms = jnp.dot(lt_ref[rows, :], comp_ref[k], preferred_element_type=F32)
        for i in range(upm):
            out_ref[t, i ^ pos[1]] = terms[i * unit : (i + 1) * unit].astype(out_ref.dtype)


def keep_kernel(pos, lt_ref, comp_ref, *refs):
    right_rows(0, pos, lt_ref, comp_ref, refs[-1])


def right_terms(pos, near, far, gram, comp, upm, after):
    nmat, rows, n = comp.shape
    rank = gram.shape[1]
    width = nmat * rank
    half = nmat // CORES
    total = CORES * near.shape[0]
    shape = (half, upm, rank // upm, n)
    vmem = pl.BlockSpec(memory_space=pltpu.VMEM)
    send, lt, mix, vec = pl.pallas_call(
        functools.partial(send_kernel, half),
        grid_spec=pltpu.PrefetchScalarGridSpec(
            num_scalar_prefetch=1,
            grid=(1,),
            in_specs=[vmem] * 4,
            out_specs=[vmem] * 4,
            scratch_shapes=[pltpu.VMEM((total, width), F32), pltpu.VMEM((width, width), F32)],
        ),
        out_shape=[
            jax.ShapeDtypeStruct(shape, BF16),
            jax.ShapeDtypeStruct((width, rows), BF16),
            jax.ShapeDtypeStruct((nmat, rows, rows + rank), BF16),
            jax.ShapeDtypeStruct((total - rows, width), F32),
        ],
        compiler_params=params(),
        cost_estimate=cost(),
        name="right_send",
    )(pos, near, far, gram, comp)
    keep = pl.pallas_call(
        keep_kernel,
        grid_spec=pltpu.PrefetchScalarGridSpec(
            num_scalar_prefetch=1,
            grid=(1,),
            in_specs=[vmem, vmem] + [pl.BlockSpec(memory_space=pl.ANY)] * len(after),
            out_specs=vmem,
        ),
        out_shape=jax.ShapeDtypeStruct(shape, F32),
        compiler_params=params(),
        cost_estimate=cost(2000 * nmat * rows * n),
        name="right_keep",
    )(pos, lt, comp, *after)
    return send, keep, lt, mix, vec


def chip_kernel(replica_rows, pos, keep_ref, recv_ref, lt_ref, *refs):
    upm = keep_ref.shape[1]
    own_ref, strip_ref, *sends = refs[-(keep_ref.shape[0] * upm + 1) :]
    left = lt_ref[...].astype(F32).T
    strip = left[:replica_rows]
    for i in range(1, left.shape[0] // replica_rows):
        strip = jnp.where(pos[6] == i, left[i * replica_rows : (i + 1) * replica_rows], strip)
    height = strip_ref.shape[0]
    strip = jnp.concatenate(
        [strip[i * height : (i + 1) * height] for i in range(replica_rows // height)], axis=1
    )
    strip_ref[...] = strip
    own_ref[...] = keep_ref[0, 0] + recv_ref[0, 0].astype(F32)
    for d, out in enumerate(sends, 1):
        j, i = d // upm, d % upm
        terms = keep_ref[j, i] + recv_ref[j, i].astype(F32)
        out[...] = jnp.concatenate([terms, strip], axis=0).astype(BF16)


def chip_sum(pos, keep, recv, lt, replica_rows, after):
    half, upm, unit, n = keep.shape
    height = lt.shape[0] * replica_rows // n
    vmem = pl.BlockSpec(memory_space=pltpu.VMEM)
    outs = [jax.ShapeDtypeStruct((unit, n), F32), jax.ShapeDtypeStruct((height, n), F32)]
    outs += [jax.ShapeDtypeStruct((unit + height, n), BF16)] * (half * upm - 1)
    return pl.pallas_call(
        functools.partial(chip_kernel, replica_rows),
        grid_spec=pltpu.PrefetchScalarGridSpec(
            num_scalar_prefetch=1,
            grid=(1,),
            in_specs=[vmem] * 3 + [pl.BlockSpec(memory_space=pl.ANY)] * len(after),
            out_specs=[vmem] * len(outs),
        ),
        out_shape=outs,
        compiler_params=params(),
        cost_estimate=cost(),
        name="chip_sum",
    )(pos, keep, recv, lt, *after)


def column_kernel(places, pos, *refs):
    out = refs[-1]
    for ref, relative in zip(refs, places):
        for i, d in enumerate(relative):
            cols = ref.shape[2]
            out[:, pl.ds(pl.multiple_of((pos[4] ^ d) * cols, cols), cols)] = ref[i]


def column_gather(pos, parts, places, after):
    unit, cols = parts[0].shape[1:]
    vmem = pl.BlockSpec(memory_space=pltpu.VMEM)
    count = sum(part.shape[0] for part in parts)
    return pl.pallas_call(
        functools.partial(column_kernel, places),
        grid_spec=pltpu.PrefetchScalarGridSpec(
            num_scalar_prefetch=1,
            grid=(1,),
            in_specs=[vmem] * len(parts) + [pl.BlockSpec(memory_space=pl.ANY)] * len(after),
            out_specs=vmem,
        ),
        out_shape=jax.ShapeDtypeStruct((unit, cols * count), BF16),
        compiler_params=params(),
        cost_estimate=cost(),
        name="column_gather",
    )(pos, *parts, *after)


def halve_kernel(keep_ref, recv_ref, *outs):
    for i in range(keep_ref.shape[0]):
        out = outs[i % len(outs)]
        out[i // len(outs)] = (keep_ref[i] + recv_ref[i].astype(F32)).astype(out.dtype)


def halve(keep, recv):
    count, unit, cols = keep.shape
    vmem = pl.BlockSpec(memory_space=pltpu.VMEM)
    shape = (max(count // 2, 1), unit, cols)
    kinds = [F32, BF16] if count > 1 else [BF16]
    return pl.pallas_call(
        halve_kernel,
        in_specs=[vmem] * 2,
        out_specs=[vmem] * len(kinds),
        out_shape=[jax.ShapeDtypeStruct(shape, kind) for kind in kinds],
        compiler_params=params(),
        cost_estimate=cost(),
        name="halve",
    )(keep, recv)


def plane_kernel(pos, own_ref, strip_ref, *refs):
    terms, (keep_ref, send_ref, mix_ref) = refs[:-3], refs[-3:]
    unit, n = own_ref.shape
    cols = keep_ref.shape[2]
    for d in range(n // cols):
        block = pl.ds(pl.multiple_of((pos[4] ^ d) * cols, cols), cols)
        parts = [own_ref[:, block]] + [term[:, block].astype(F32)[:unit] for term in terms]
        out = send_ref if d % 2 else keep_ref
        out[d // 2] = tree_sum(parts).astype(out.dtype)
    strip = strip_ref[...]
    for d, term in enumerate(terms, 1):
        strip = jnp.where(pos[7] == d, term[...].astype(F32)[unit:], strip)
    nmat, count, depth = mix_ref.shape
    rank = (depth - count) // 2
    width = nmat * rank
    rows = [strip[:, i * width : (i + 1) * width] for i in range(n // width)]
    rows = -0.1 * jnp.concatenate(rows, axis=0)
    high = rows.astype(BF16)
    low = (rows - high.astype(F32)).astype(BF16)
    mix_ref[:, :, :count] = jnp.broadcast_to(unit_matrix(count), (nmat, count, count))
    for i in range(nmat):
        mix_ref[i, :, count : count + rank] = high[:, i * rank : (i + 1) * rank]
        mix_ref[i, :, count + rank :] = low[:, i * rank : (i + 1) * rank]


def plane_sum(pos, own, strip, terms, n_z, nmat, rank):
    unit, n = own.shape
    count = strip.size // (nmat * rank)
    shape = (n_z // 2, unit, n // n_z)
    outs = [
        jax.ShapeDtypeStruct(shape, F32),
        jax.ShapeDtypeStruct(shape, BF16),
        jax.ShapeDtypeStruct((nmat, count, count + 2 * rank), BF16),
    ]
    vmem = pl.BlockSpec(memory_space=pltpu.VMEM)
    return pl.pallas_call(
        plane_kernel,
        grid_spec=pltpu.PrefetchScalarGridSpec(
            num_scalar_prefetch=1,
            grid=(1,),
            in_specs=[vmem] * (2 + len(terms)),
            out_specs=[vmem] * len(outs),
        ),
        out_shape=outs,
        compiler_params=params(),
        cost_estimate=cost(),
        name="plane_sum",
    )(pos, own, strip, *terms)


def stack_kernel(*refs):
    out, first = refs[-1], 0
    for part in refs[:-1]:
        out[first : first + part.shape[0]] = part[...]
        first += part.shape[0]


def stack(parts):
    vmem = pl.BlockSpec(memory_space=pltpu.VMEM)
    count = sum(part.shape[0] for part in parts)
    return pl.pallas_call(
        stack_kernel,
        in_specs=[vmem] * len(parts),
        out_specs=vmem,
        out_shape=jax.ShapeDtypeStruct((count,) + parts[0].shape[1:], parts[0].dtype),
        compiler_params=params(),
        cost_estimate=cost(),
        name="stack",
    )(*parts)


def forward_kernel(*refs):
    count = len(refs) // 2
    for source, out in zip(refs, refs[-count:]):
        out[...] = source[...]


def forward(parts, after):
    vmem = pl.BlockSpec(memory_space=pltpu.VMEM)
    return pl.pallas_call(
        forward_kernel,
        in_specs=[vmem] * len(parts) + [pl.BlockSpec(memory_space=pl.ANY)],
        out_specs=[vmem] * len(parts),
        out_shape=[jax.ShapeDtypeStruct(part.shape, part.dtype) for part in parts],
        compiler_params=params(),
        cost_estimate=cost(),
        name="forward",
    )(*parts, after)


def rank_of(owners, k):
    count = jnp.int32(0)
    for j in range(owners.shape[0]):
        count += jnp.where((owners[j] == owners[k]) & (j < k), 1, 0)
    return count


def outputs_kernel(second, places, pos, owners, comp_ref, mix_ref, mixr_ref, near_ref, *refs):
    n_base = len(places)
    n_state = 2 if second else 0
    bases, refs = refs[:n_base], refs[n_base:]
    if second:
        far_ref, states, refs = refs[0], refs[1 : 1 + n_state], refs[1 + n_state + 2 :]
    outs, refs = refs[: 2 + n_state], refs[2 + n_state :]
    held, feedback, weights, fetch_sem, out_sem = refs[:5]
    half, upm, unit, n = near_ref.shape
    rows, count = feedback.shape[1], held.shape[1]
    capacity = max(c for _, c in places) + 1

    def right_of(ref, j):
        parts = [ref[j, i ^ pos[1]] for i in range(upm)]
        return parts[0] if upm == 1 else jnp.concatenate(parts, axis=0)

    matrices = [(j + (half if second else 0)) ^ pos[0] for j in range(half)]
    for j, k in enumerate(matrices):
        slot = (owners[k] ^ pos[5]) * capacity + rank_of(owners, k)
        for a, (d, c) in enumerate(places):

            @pl.when(slot == d * capacity + c)
            def _():
                pltpu.make_async_copy(bases[a].at[0], held.at[j], fetch_sem.at[j]).start()

    if second:
        scratch, state_in, state_out = refs[5:7], refs[7], refs[8]
        loads = [
            pltpu.make_async_copy(states[i].at[0, c], scratch[i].at[c], state_in.at[i, c])
            for c in range(capacity)
            for i in range(n_state)
        ]
        for load in loads:
            load.start()

    stores = []
    for j, k in enumerate(matrices):
        right = right_of(far_ref if second else near_ref, j)
        mix, mixr = mix_ref[k], mixr_ref[k]
        pltpu.make_async_copy(bases[0].at[0], held.at[j], fetch_sem.at[j]).wait()
        for first in range(0, n, COLUMNS):
            block = slice(first, first + COLUMNS)
            part = right[:, block]
            both = jnp.concatenate([comp_ref[k, :, block], part], axis=0)
            feedback[j, :, block] = jnp.dot(mix, both, preferred_element_type=F32).astype(BF16)
            both = jnp.concatenate([held[j, :, block], part, part], axis=0)
            weights[j, :, block] = jnp.dot(mixr, both, preferred_element_type=F32).astype(BF16)
        for source, target, i in ((feedback, outs[0].at[0, k], 0), (weights, outs[1].at[k], 1)):
            stores.append(pltpu.make_async_copy(source.at[j], target, out_sem.at[j, i]))
            stores[-1].start()

    for c in range(capacity if second else 0):
        matrix = jnp.int32(-1)
        for k in range(owners.shape[0]):
            matrix = jnp.where((owners[k] == pos[5]) & (rank_of(owners, k) == c), k, matrix)
        safe = jnp.maximum(matrix, 0)
        slot = safe ^ pos[0]
        inner = lax.rem(slot, half)
        right = jnp.where(slot < half, right_of(near_ref, inner), right_of(far_ref, inner))
        both = jnp.concatenate([right, right], axis=0)
        mixr = mixr_ref[safe][:, count:]
        for load in loads[c * n_state : (c + 1) * n_state]:
            load.wait()
        for first in range(0, n, COLUMNS):
            block = slice(first, first + COLUMNS)
            change = jnp.dot(mixr, both[:, block], preferred_element_type=F32)
            momentum = 0.9 * scratch[0][c, :, block] - jnp.where(matrix >= 0, 10.0 * change, 0.0)
            scratch[0][c, :, block] = momentum
            scratch[1][c, :, block] -= 0.1 * momentum
        for i in range(n_state):
            copy = pltpu.make_async_copy(scratch[i].at[c], outs[2 + i].at[0, c], state_out.at[i, c])
            copy.start()
            stores.append(copy)

    for copy in stores:
        copy.wait()


def outputs(pos, owners, comp, mix, mixr, near, bases, places, far=None, states=(), earlier=()):
    nmat, rows, n = comp.shape
    half = near.shape[0]
    capacity = max(c for _, c in places) + 1
    replica_rows = bases[0].shape[1]
    second = far is not None
    any_spec = pl.BlockSpec(memory_space=pl.ANY)
    vmem = pl.BlockSpec(memory_space=pltpu.VMEM)
    scratch = [
        pltpu.VMEM((half, replica_rows, n), BF16),
        pltpu.VMEM((half, rows, n), BF16),
        pltpu.VMEM((half, replica_rows, n), BF16),
        pltpu.SemaphoreType.DMA((half,)),
        pltpu.SemaphoreType.DMA((half, 2)),
    ]
    if second:
        scratch += [pltpu.VMEM((capacity, replica_rows, n), F32)] * 2
        scratch += [pltpu.SemaphoreType.DMA((2, capacity))] * 2
    outs = [
        jax.ShapeDtypeStruct((1, nmat, rows, n), BF16),
        jax.ShapeDtypeStruct((nmat, replica_rows, n), BF16),
    ] + [jax.ShapeDtypeStruct(x.shape, F32) for x in states]
    fars = [far] if second else []
    first = 6 + len(bases) + len(fars) + len(states)
    return pl.pallas_call(
        functools.partial(outputs_kernel, second, places),
        grid_spec=pltpu.PrefetchScalarGridSpec(
            num_scalar_prefetch=2,
            grid=(1,),
            in_specs=[vmem] * 4
            + [any_spec] * len(bases)
            + [vmem] * len(fars)
            + [any_spec] * (len(states) + len(earlier)),
            out_specs=[any_spec] * len(outs),
            scratch_shapes=scratch,
        ),
        out_shape=outs,
        input_output_aliases={first + i: i for i in range(len(earlier))},
        compiler_params=params(24),
        cost_estimate=cost(),
        name="outputs",
    )(pos, owners, comp, mix, mixr, near, *bases, *fars, *states, *earlier)


def base_kernel(momentum_ref, master_ref, *refs):
    outs, (momentum, master, sems) = refs[:-3], refs[-3:]
    rows = outs[0].shape[1]
    blocks = [(c, first) for c in range(len(outs)) for first in range(0, rows, BASE_ROWS)]

    def copies(i):
        c, first = blocks[i]
        part = pl.ds(first, BASE_ROWS)
        return [
            pltpu.make_async_copy(source.at[0, c, part], target.at[c, part], sems.at[j, i])
            for j, (source, target) in enumerate(((momentum_ref, momentum), (master_ref, master)))
        ]

    for i in range(len(blocks)):
        for copy in copies(i):
            copy.start()
    for i, (c, first) in enumerate(blocks):
        for copy in copies(i):
            copy.wait()
        part = slice(first, first + BASE_ROWS)
        outs[c][0, part] = (master[c, part] - 0.09 * momentum[c, part]).astype(BF16)


def base_of(momentum, master):
    _, capacity, rows, n = momentum.shape
    return pl.pallas_call(
        base_kernel,
        in_specs=[pl.BlockSpec(memory_space=pl.ANY)] * 2,
        out_specs=[pl.BlockSpec(memory_space=pltpu.VMEM)] * capacity,
        out_shape=[jax.ShapeDtypeStruct((1, rows, n), BF16)] * capacity,
        scratch_shapes=[pltpu.VMEM((capacity, rows, n), F32)] * 2
        + [pltpu.SemaphoreType.DMA((2, capacity * rows // BASE_ROWS))],
        compiler_params=params(),
        cost_estimate=cost(),
        name="base",
    )(momentum, master)


def per_device(
    gradients,
    feedback,
    right_init,
    gram_root,
    owners,
    momentum,
    master_weights,
    vector_grads,
    vector_momentum,
    vector_params,
):
    nmat, rows, n = gradients.shape[1:]
    rank = right_init.shape[2]
    unit = rank * nmat // (CORES * lax.axis_size("mp"))
    n_mp = lax.axis_size("mp")
    n_z = lax.axis_size("replica") // CORES
    capacity, replica_rows = momentum.shape[1:3]
    p = lax.axis_index("mp")
    r = lax.axis_index("replica")
    core, z = r % CORES, r // CORES
    upm = CORES * n_mp // nmat
    half = nmat // CORES
    code = core * n_mp + p
    first = r * replica_rows

    places_of = [code // upm, code % upm, core, r, z, p, first % rows // replica_rows, first // rows ^ p]
    pos = jnp.stack(places_of).astype(jnp.int32)
    in_hbm = lambda x: pltpu.with_memory_space_constraint(x, pltpu.HBM)

    square = n_mp == 4 and capacity == 2
    near_owners = range(1, 3 if square else n_mp)
    states = in_hbm(momentum), in_hbm(master_weights)
    held = {(0, c): part for c, part in enumerate(base_of(*states))}
    for c in range(capacity):
        for d in near_owners:
            held[d, c] = exchange(held[0, c], "mp", d)

    nvec = vector_grads.shape[1]
    comp, near, far = left_terms(
        pos,
        in_hbm(gradients),
        in_hbm(feedback),
        in_hbm(jnp.swapaxes(right_init, 1, 2)),
        vector_grads,
    )
    piece = add([near, exchange(far, "replica", 1)], BF16)
    early = [held[d, 0] for d in near_owners]
    middle = [held[d, c] for c in range(1, capacity) for d in near_owners]
    steps = [1 << i for i in range(n_z.bit_length() - 1)]
    for d in steps:
        last = d == steps[-1]
        recv = exchange(piece, "replica", CORES * d)
        piece = add([piece, recv], F32 if last else BF16, ())
    near, far = piece, exchange(piece, "replica", 1)

    send, keep, lt, mix, vector_rows = right_terms(pos, near, far, gram_root, comp, upm, early + middle)
    vector_total = vector_rows.reshape(-1)[:nvec]
    recv = exchange(send, "replica", 1)
    own, strip, *chip = chip_sum(pos, keep, recv, lt, replica_rows, [])
    plane = [exchange(part, "mp", d) for d, part in enumerate(chip, 1)]
    kept, *sent, mixr = plane_sum(pos, own, strip, plane, n_z, nmat, rank)
    late = []
    if square:
        late = forward([held[1, 0], held[2, 1]], mixr)
        late = [exchange(late[0], "mp", 2), exchange(late[1], "mp", 1)]
        held[3, 0], held[3, 1] = late
    for d in steps:
        kept, *sent = halve(kept, exchange(sent[0], "replica", CORES * d))

    parts, relative = [kept], [[0]]
    for d in reversed(steps):
        have = stack(parts) if len(parts) > 1 else parts[0]
        order = sum(relative, [])
        parts = [have, exchange(have, "replica", CORES * d)]
        relative = [order, [i ^ d for i in order]]
    whole = column_gather(pos, parts, relative, late)[None]
    near = stack([whole] + [exchange(whole, "mp", d) for d in range(1, n_mp)])
    near = near.reshape(half, upm, unit, n)
    far = exchange(near, "replica", 1)

    places, bases = list(held), list(held.values())
    done = outputs(pos, owners, comp, mix, mixr, near, bases, places)
    new_feedback, new_weights, new_momentum, new_master = outputs(
        pos, owners, comp, mix, mixr, near, bases, places, far, (momentum, master_weights), done
    )

    new_vector_momentum = 0.9 * vector_momentum + vector_total
    new_vector_params = vector_params - 0.1 * new_vector_momentum
    return new_feedback, new_momentum, new_master, new_weights, new_vector_momentum, new_vector_params


def solution(mesh):
    return jax.shard_map(
        per_device,
        mesh=mesh,
        in_specs=(
            P("replica", None, "mp", None),
            P("replica", None, "mp", None),
            P(),
            P(),
            P(),
            P("mp", None, "replica", None),
            P("mp", None, "replica", None),
            P("replica", "mp"),
            P("mp"),
            P("mp"),
        ),
        out_specs=(
            P("replica", None, "mp", None),
            P("mp", None, "replica", None),
            P("mp", None, "replica", None),
            P(None, "replica", None),
            P("mp"),
            P("mp"),
        ),
        check_vma=False,
    )
```

time: 98.7 us -> 97.1 us (0.984)
  Pallas kernels: 36.6 us -> 30.9 us
  waiting for transfers between devices: 28.2 us -> 30.5 us
  starting transfers between devices: 31.9 us -> 33.9 us
    pallas_call x12 -> x11, Pallas kernels: 19 us -> 13.9 us  [the longest x2 13.1 us: outputs(): pl.pallas_call(functools.partial(outputs_kernel, second, places), grid_sp...]
    ppermute x26 -> x22, waiting for transfers between devices: 28.2 us -> 30.5 us  [exchange(): return lax.ppermute(x, axis, [(i, i ^ distance) for i in range(size)])]
    ppermute x26 -> x22, starting transfers between devices: 31.9 us -> 33.9 us  [exchange(): return lax.ppermute(x, axis, [(i, i ^ distance) for i in range(size)])]
  transfers between devices with their start and end apart: 26 -> 22, of which waited for: 13 -> 15; matrix products, arithmetic and copies ran while one was open for 1% -> 1% of each run, Pallas kernels for 27% -> 19%
where the time goes in v7:
time: 97.1 us; the launch traced here: 97 us
  starting transfers between devices  33.9 us (35%)
  Pallas kernels  30.9 us (32%)
  waiting for transfers between devices  30.5 us (31%)
    ppermute x22, starting transfers between devices, exchange(): return lax.ppermute(x, axis, [(i, i ^ distance) for i in range(size)])  33.9 us
    ppermute x22, waiting for transfers between devices, exchange(): return lax.ppermute(x, axis, [(i, i ^ distance) for i in range(size)])  30.5 us
    pallas_call x2, Pallas kernels, outputs(): pl.pallas_call(functools.partial(outputs_kernel, second, places), grid_sp...  13.1 us
    pallas_call x1, Pallas kernels, left_terms(): pl.pallas_call(left_kernel, grid_spec=pltpu.PrefetchScalarGridSpec(num_sc...  9.01 us
    pallas_call x1, Pallas kernels, base_of(): pl.pallas_call(base_kernel, in_specs=[pl.BlockSpec(memory_space=pl.ANY)]...  2.65 us
    pallas_call x1, Pallas kernels, right_terms(): pl.pallas_call(functools.partial(send_kernel, half), grid_spec=pltpu.Pref...  2.22 us
  transfers between devices with their start and end apart: 22, of which 15 were waited for; matrix products, arithmetic and copies ran while one was open for 1% of the time, Pallas kernels for 19%

profile of v7, /device:TPU:1, one launch (start us, length us, event | category | flops | bytes accessed | tf_op | source)
XLA Modules:
  0.0 97.0 jit_solution(7228899218020760894)
XLA Ops:
  0.6 2.6 %base.1 = (bf16[1,96,3072]{2,1,0:T(8,128)(2,1)S(1)}, bf16[1,96,3072]{2,1,0:T(8,128)(2,1)S(1)}) custom-call(f32[1,2,96,3072]{3,2,1,0:T(8,128)} %refs_9_.1, f32[1,2,96,3072]{3,2,1,0:T(8,128)} %refs_10_.1), custom_call_target="tpu_custom_call" | custom-call | flops 1000 | bytes 1000 | tf_op jit(solution)/shard_map/base/pallas_call | solution.py:541
  3.3 2.1 %collective-permute-start.5 = (bf16[1,96,3072]{2,1,0:T(8,128)(2,1)S(1)}, bf16[1,96,3072]{2,1,0:T(8,128)(2,1)S(1)}, u32[]{:S(2)}, u32[]{:S(2)}) collective-permute-start(bf16[1,96,3072]{2,1,0:T(8,128)(2,1)S(1)} %get-tuple-element.38.refs_0_), channel_id=1, source_target_pairs={{0,2},{1,3},{2,0},{3,1},{4,6},{5,7},{6,4},{7,5},{8,10},{9,11},{10,... | collective-permute-start | bytes 1769480 | tf_op jit(solution)/shard_map/ppermute | solution.py:34
  5.4 1.2 %collective-permute-start.4 = (bf16[1,96,3072]{2,1,0:T(8,128)(2,1)S(1)}, bf16[1,96,3072]{2,1,0:T(8,128)(2,1)S(1)}, u32[]{:S(2)}, u32[]{:S(2)}) collective-permute-start(bf16[1,96,3072]{2,1,0:T(8,128)(2,1)S(1)} %get-tuple-element.38.refs_0_), channel_id=1, source_target_pairs={{0,1},{1,0},{2,3},{3,2},{4,5},{5,4},{6,7},{7,6},{8,9},{9,8},{10,11... | collective-permute-start | bytes 1769480 | tf_op jit(solution)/shard_map/ppermute | solution.py:34
  7.1 9.0 %left_terms.1 = (bf16[8,192,3072]{2,1,0:T(8,128)(2,1)S(1)}, f32[112,256]{1,0:T(8,128)S(1)}, f32[112,256]{1,0:T(8,128)S(1)}) custom-call(s32[8]{0:T(128)S(1)} %stack.34.pos, bf16[1,8,192,3072]{3,2,1,0:T(8,128)(2,1)} %g_ref.1, bf16[1,8,192,3072]{3,2,1,0:T(8,128)(2,1)} %f_ref.1, bf16[8,32,3072]{2,1,0:T(8,128)(2,1)} %bitcast.20, f32[1,2688]{1,0:T(1,128)S(1)} %copy-done.3), custom_call_target="tpu_custom_call" | custom-call | flops 1000 | bytes 1000 | tf_op jit(solution)/shard_map/left_terms/pallas_call | solution.py:86
  16.1 1.6 %collective-permute-start = (f32[112,256]{1,0:T(8,128)S(1)}, f32[112,256]{1,0:T(8,128)S(1)}, u32[]{:S(2)}, u32[]{:S(2)}) collective-permute-start(f32[112,256]{1,0:T(8,128)S(1)} %get-tuple-element.35), channel_id=1, source_target_pairs={{0,4},{4,0},{8,12},{12,8},{16,20},{20,16},{24,28},{28,24},{1,5},{5... | collective-permute-start | bytes 344072 | tf_op jit(solution)/shard_map/ppermute | solution.py:34
  18.6 1.8 %collective-permute-start.1 = (bf16[112,256]{1,0:T(8,128)(2,1)S(1)}, bf16[112,256]{1,0:T(8,128)(2,1)S(1)}, u32[]{:S(2)}, u32[]{:S(2)}) collective-permute-start(bf16[112,256]{1,0:T(8,128)(2,1)S(1)} %add.27.one_ref), channel_id=1, source_target_pairs={{0,8},{4,12},{8,0},{12,4},{16,24},{20,28},{24,16},{28,20},{1,9},{5... | collective-permute-start | bytes 172040 | tf_op jit(solution)/shard_map/ppermute | solution.py:34
  20.4 2.0 %collective-permute-done.1.other_ref = bf16[112,256]{1,0:T(8,128)(2,1)S(1)} collective-permute-done((bf16[112,256]{1,0:T(8,128)(2,1)S(1)}, bf16[112,256]{1,0:T(8,128)(2,1)S(1)}, u32[]{:S(2)}, u32[]{:S(2)}) %collective-permute-start.1) | collective-permute-done | bytes 57376 | tf_op jit(solution)/shard_map/ppermute | solution.py:34
  22.4 2.4 %collective-permute-start.2 = (bf16[112,256]{1,0:T(8,128)(2,1)S(1)}, bf16[112,256]{1,0:T(8,128)(2,1)S(1)}, u32[]{:S(2)}, u32[]{:S(2)}) collective-permute-start(bf16[112,256]{1,0:T(8,128)(2,1)S(1)} %add.28.one_ref), channel_id=1, source_target_pairs={{0,16},{4,20},{8,24},{12,28},{16,0},{20,4},{24,8},{28,12},{1,17},{... | collective-permute-start | bytes 172040 | tf_op jit(solution)/shard_map/ppermute | solution.py:34
  24.9 1.6 %collective-permute-done.2.other_ref = bf16[112,256]{1,0:T(8,128)(2,1)S(1)} collective-permute-done((bf16[112,256]{1,0:T(8,128)(2,1)S(1)}, bf16[112,256]{1,0:T(8,128)(2,1)S(1)}, u32[]{:S(2)}, u32[]{:S(2)}) %collective-permute-start.2) | collective-permute-done | bytes 57376 | tf_op jit(solution)/shard_map/ppermute | solution.py:34
  26.5 2.4 %collective-permute-start.3 = (f32[112,256]{1,0:T(8,128)S(1)}, f32[112,256]{1,0:T(8,128)S(1)}, u32[]{:S(2)}, u32[]{:S(2)}) collective-permute-start(f32[112,256]{1,0:T(8,128)S(1)} %add.29.near_ref), channel_id=1, source_target_pairs={{0,4},{4,0},{8,12},{12,8},{16,20},{20,16},{24,28},{28,24},{1,5},{5... | collective-permute-start | bytes 344072 | tf_op jit(solution)/shard_map/ppermute | solution.py:34
  29.8 2.2 %right_send.1 = (bf16[4,1,32,3072]{3,2,1,0:T(8,128)(2,1)S(1)}, bf16[256,192]{1,0:T(8,128)(2,1)S(1)}, bf16[8,192,224]{2,1,0:T(8,128)(2,1)S(1)}, f32[32,256]{1,0:T(8,128)S(1)}) custom-call(s32[8]{0:T(128)S(1)} %stack.34.pos, f32[112,256]{1,0:T(8,128)S(1)} %add.29.near_ref, f32[112,256]{1,0:T(8,128)S(1)} %collective-permute-done.3.far_ref, ...), custom_call_target="tpu_custom_call" | custom-call | flops 1000 | bytes 1000 | tf_op jit(solution)/shard_map/right_send/pallas_call | solution.py:173
  32.5 1.5 %right_keep.1.keep_ref = f32[4,1,32,3072]{3,2,1,0:T(8,128)S(1)} custom-call(s32[8]{0:T(128)S(1)} %stack.34.pos, bf16[256,192]{1,0:T(8,128)(2,1)S(1)} %get-tuple-element.37.lt_ref, bf16[8,192,3072]{2,1,0:T(8,128)(2,1)S(1)} %get-tuple-element.33.comp_ref, bf16[1,96,3072]{2,1,0:T(8,128)(2,1)S(1)} %collective-permute-done.4.refs_0_.refs_2_, ...), custom_call_target="tpu_custom_call" | custom-call | flops 9437184000 | bytes 1000 | tf_op jit(solution)/shard_map/right_keep/pallas_call | solution.py:192
  35.2 1.3 %collective-permute-start.9 = (bf16[40,3072]{1,0:T(8,128)(2,1)S(1)}, bf16[40,3072]{1,0:T(8,128)(2,1)S(1)}, u32[]{:S(2)}, u32[]{:S(2)}) collective-permute-start(bf16[40,3072]{1,0:T(8,128)(2,1)S(1)} %get-tuple-element.43), channel_id=1, source_target_pairs={{0,1},{1,0},{2,3},{3,2},{4,5},{5,4},{6,7},{7,6},{8,9},{9,8},{10,11... | collective-permute-start | bytes 737288 | tf_op jit(solution)/shard_map/ppermute | solution.py:34
  36.5 1.2 %collective-permute-start.10 = (bf16[40,3072]{1,0:T(8,128)(2,1)S(1)}, bf16[40,3072]{1,0:T(8,128)(2,1)S(1)}, u32[]{:S(2)}, u32[]{:S(2)}) collective-permute-start(bf16[40,3072]{1,0:T(8,128)(2,1)S(1)} %get-tuple-element.44), channel_id=1, source_target_pairs={{0,2},{1,3},{2,0},{3,1},{4,6},{5,7},{6,4},{7,5},{8,10},{9,11},{10,... | collective-permute-start | bytes 737288 | tf_op jit(solution)/shard_map/ppermute | solution.py:34
  37.9 3.9 %collective-permute-done.9.refs_0_ = bf16[40,3072]{1,0:T(8,128)(2,1)S(1)} collective-permute-done((bf16[40,3072]{1,0:T(8,128)(2,1)S(1)}, bf16[40,3072]{1,0:T(8,128)(2,1)S(1)}, u32[]{:S(2)}, u32[]{:S(2)}) %collective-permute-start.9) | collective-permute-done | bytes 245792 | tf_op jit(solution)/shard_map/ppermute | solution.py:34
  41.8 1.9 %collective-permute-done.10.refs_1_ = bf16[40,3072]{1,0:T(8,128)(2,1)S(1)} collective-permute-done((bf16[40,3072]{1,0:T(8,128)(2,1)S(1)}, bf16[40,3072]{1,0:T(8,128)(2,1)S(1)}, u32[]{:S(2)}, u32[]{:S(2)}) %collective-permute-start.10) | collective-permute-done | bytes 245792 | tf_op jit(solution)/shard_map/ppermute | solution.py:34
  43.6 5.1 %collective-permute-done.11.refs_2_ = bf16[40,3072]{1,0:T(8,128)(2,1)S(1)} collective-permute-done((bf16[40,3072]{1,0:T(8,128)(2,1)S(1)}, bf16[40,3072]{1,0:T(8,128)(2,1)S(1)}, u32[]{:S(2)}, u32[]{:S(2)}) %collective-permute-start.11) | collective-permute-done | bytes 245792 | tf_op jit(solution)/shard_map/ppermute | solution.py:34
  49.7 1.2 %collective-permute-start.16 = (bf16[1,96,3072]{2,1,0:T(8,128)(2,1)S(1)}, bf16[1,96,3072]{2,1,0:T(8,128)(2,1)S(1)}, u32[]{:S(2)}, u32[]{:S(2)}) collective-permute-start(bf16[1,96,3072]{2,1,0:T(8,128)(2,1)S(1)} %get-tuple-element.51), channel_id=1, source_target_pairs={{0,2},{1,3},{2,0},{3,1},{4,6},{5,7},{6,4},{7,5},{8,10},{9,11},{10,... | collective-permute-start | bytes 1769480 | tf_op jit(solution)/shard_map/ppermute | solution.py:34
  51.0 1.3 %collective-permute-start.12 = (bf16[2,32,768]{2,1,0:T(8,128)(2,1)S(1)}, bf16[2,32,768]{2,1,0:T(8,128)(2,1)S(1)}, u32[]{:S(2)}, u32[]{:S(2)}) collective-permute-start(bf16[2,32,768]{2,1,0:T(8,128)(2,1)S(1)} %get-tuple-element.48), channel_id=1, source_target_pairs={{0,8},{4,12},{8,0},{12,4},{16,24},{20,28},{24,16},{28,20},{1,9},{5... | collective-permute-start | bytes 294920 | tf_op jit(solution)/shard_map/ppermute | solution.py:34
  52.3 2.5 %collective-permute-done.12.recv_ref = bf16[2,32,768]{2,1,0:T(8,128)(2,1)S(1)} collective-permute-done((bf16[2,32,768]{2,1,0:T(8,128)(2,1)S(1)}, bf16[2,32,768]{2,1,0:T(8,128)(2,1)S(1)}, u32[]{:S(2)}, u32[]{:S(2)}) %collective-permute-start.12) | collective-permute-done | bytes 98336 | tf_op jit(solution)/shard_map/ppermute | solution.py:34
  54.8 2.8 %collective-permute-start.13 = (bf16[1,32,768]{2,1,0:T(8,128)(2,1)S(1)}, bf16[1,32,768]{2,1,0:T(8,128)(2,1)S(1)}, u32[]{:S(2)}, u32[]{:S(2)}) collective-permute-start(bf16[1,32,768]{2,1,0:T(8,128)(2,1)S(1)} %get-tuple-element.50), channel_id=1, source_target_pairs={{0,16},{4,20},{8,24},{12,28},{16,0},{20,4},{24,8},{28,12},{1,17},{... | collective-permute-start | bytes 147464 | tf_op jit(solution)/shard_map/ppermute | solution.py:34
  57.7 1.5 %collective-permute-done.13.recv_ref = bf16[1,32,768]{2,1,0:T(8,128)(2,1)S(1)} collective-permute-done((bf16[1,32,768]{2,1,0:T(8,128)(2,1)S(1)}, bf16[1,32,768]{2,1,0:T(8,128)(2,1)S(1)}, u32[]{:S(2)}, u32[]{:S(2)}) %collective-permute-start.13) | collective-permute-done | bytes 49184 | tf_op jit(solution)/shard_map/ppermute | solution.py:34
  59.2 2.4 %collective-permute-start.14 = (bf16[1,32,768]{2,1,0:T(8,128)(2,1)S(1)}, bf16[1,32,768]{2,1,0:T(8,128)(2,1)S(1)}, u32[]{:S(2)}, u32[]{:S(2)}) collective-permute-start(bf16[1,32,768]{2,1,0:T(8,128)(2,1)S(1)} %halve.3.refs_0_), channel_id=1, source_target_pairs={{0,16},{4,20},{8,24},{12,28},{16,0},{20,4},{24,8},{28,12},{1,17},{... | collective-permute-start | bytes 147464 | tf_op jit(solution)/shard_map/ppermute | solution.py:34
  61.6 2.0 %collective-permute-done.14.refs_1_ = bf16[1,32,768]{2,1,0:T(8,128)(2,1)S(1)} collective-permute-done((bf16[1,32,768]{2,1,0:T(8,128)(2,1)S(1)}, bf16[1,32,768]{2,1,0:T(8,128)(2,1)S(1)}, u32[]{:S(2)}, u32[]{:S(2)}) %collective-permute-start.14) | collective-permute-done | bytes 49184 | tf_op jit(solution)/shard_map/ppermute | solution.py:34
  63.6 1.2 %collective-permute-start.15 = (bf16[2,32,768]{2,1,0:T(8,128)(2,1)S(1)}, bf16[2,32,768]{2,1,0:T(8,128)(2,1)S(1)}, u32[]{:S(2)}, u32[]{:S(2)}) collective-permute-start(bf16[2,32,768]{2,1,0:T(8,128)(2,1)S(1)} %stack.35.refs_0_), channel_id=1, source_target_pairs={{0,8},{4,12},{8,0},{12,4},{16,24},{20,28},{24,16},{28,20},{1,9},{5... | collective-permute-start | bytes 294920 | tf_op jit(solution)/shard_map/ppermute | solution.py:34
  64.8 2.8 %collective-permute-done.15.refs_1_ = bf16[2,32,768]{2,1,0:T(8,128)(2,1)S(1)} collective-permute-done((bf16[2,32,768]{2,1,0:T(8,128)(2,1)S(1)}, bf16[2,32,768]{2,1,0:T(8,128)(2,1)S(1)}, u32[]{:S(2)}, u32[]{:S(2)}) %collective-permute-start.15) | collective-permute-done | bytes 98336 | tf_op jit(solution)/shard_map/ppermute | solution.py:34
  68.3 1.3 %collective-permute-start.20 = (bf16[1,32,3072]{2,1,0:T(8,128)(2,1)S(1)}, bf16[1,32,3072]{2,1,0:T(8,128)(2,1)S(1)}, u32[]{:S(2)}, u32[]{:S(2)}) collective-permute-start(bf16[1,32,3072]{2,1,0:T(8,128)(2,1)S(1)} %bitcast.15), channel_id=1, source_target_pairs={{0,3},{1,2},{2,1},{3,0},{4,7},{5,6},{6,5},{7,4},{8,11},{9,10},{10,... | collective-permute-start | bytes 589832 | tf_op jit(solution)/shard_map/ppermute | solution.py:34
  71.0 2.9 %collective-permute-done.20.refs_3_ = bf16[1,32,3072]{2,1,0:T(8,128)(2,1)S(1)} collective-permute-done((bf16[1,32,3072]{2,1,0:T(8,128)(2,1)S(1)}, bf16[1,32,3072]{2,1,0:T(8,128)(2,1)S(1)}, u32[]{:S(2)}, u32[]{:S(2)}) %collective-permute-start.20) | collective-permute-done | bytes 196640 | tf_op jit(solution)/shard_map/ppermute | solution.py:34
  73.8 2.0 %collective-permute-done.19.refs_2_ = bf16[1,32,3072]{2,1,0:T(8,128)(2,1)S(1)} collective-permute-done((bf16[1,32,3072]{2,1,0:T(8,128)(2,1)S(1)}, bf16[1,32,3072]{2,1,0:T(8,128)(2,1)S(1)}, u32[]{:S(2)}, u32[]{:S(2)}) %collective-permute-start.19) | collective-permute-done | bytes 196640 | tf_op jit(solution)/shard_map/ppermute | solution.py:34
  76.0 7.0 %collective-permute-start.21 = (bf16[4,1,32,3072]{3,2,1,0:T(8,128)(2,1)S(1)}, bf16[4,1,32,3072]{3,2,1,0:T(8,128)(2,1)S(1)}, u32[]{:S(2)}, u32[]{:S(2)}) collective-permute-start(bf16[4,1,32,3072]{3,2,1,0:T(8,128)(2,1)S(1)} %bitcast.12), channel_id=1, source_target_pairs={{0,4},{4,0},{8,12},{12,8},{16,20},{20,16},{24,28},{28,24},{1,5},{5... | collective-permute-start | bytes 2359304 | tf_op jit(solution)/shard_map/ppermute | solution.py:34
  83.7 5.4 %outputs.2 = (bf16[1,8,192,3072]{3,2,1,0:T(8,128)(2,1)}, bf16[8,96,3072]{2,1,0:T(8,128)(2,1)}) custom-call(s32[8]{0:T(128)S(1)} %stack.34.pos, s32[8]{0:T(128)S(1)} %copy-done.4, bf16[8,192,3072]{2,1,0:T(8,128)(2,1)S(1)} %get-tuple-element.33.comp_ref, bf16[8,192,224]{2,1,0:T(8,128)(2,1)S(1)} %get-tuple-element.36.mix_ref, ...), custom_call_target="tpu_custom_call" | custom-call | flops 1000 | bytes 1000 | tf_op jit(solution)/shard_map/outputs/pallas_call | solution.py:496
  89.1 7.7 %outputs.3 = (bf16[1,8,192,3072]{3,2,1,0:T(8,128)(2,1)}, bf16[8,96,3072]{2,1,0:T(8,128)(2,1)}, f32[1,2,96,3072]{3,2,1,0:T(8,128)}, f32[1,2,96,3072]{3,2,1,0:T(8,128)}) custom-call(s32[8]{0:T(128)S(1)} %stack.34.pos, s32[8]{0:T(128)S(1)} %copy-done.4, ...), custom_call_target="tpu_custom_call", output_to_operand_aliasing={{0}: (17, {}), {1}: (18, {})} | custom-call | flops 1000 | bytes 1000 | tf_op jit(solution)/shard_map/outputs/pallas_call | solution.py:496
  (46 shorter events, 7.9 us)
Async XLA Ops:
  0.6 6.4 %copy-start.3 = (f32[1,2688]{1,0:T(1,128)S(1)}, f32[1,2688]{1,0:T(1,128)}, u32[]{:S(2)}) copy-start(f32[1,2688]{1,0:T(1,128)} %vec_ref.1) | copy-start | bytes 32260
  3.3 29.2 %collective-permute-start.5 = (bf16[1,96,3072]{2,1,0:T(8,128)(2,1)S(1)}, bf16[1,96,3072]{2,1,0:T(8,128)(2,1)S(1)}, u32[]{:S(2)}, u32[]{:S(2)}) collective-permute-start(bf16[1,96,3072]{2,1,0:T(8,128)(2,1)S(1)} %get-tuple-element.38.refs_0_), channel_id=1, source_target_pairs={{0,2},{1,3},{2,0},{3,1},{4,6},{5,7},{6,4},{7,5},{8,10},{9,11},{10,... | collective-permute-start | bytes 1769480 | tf_op jit(solution)/shard_map/ppermute | solution.py:34
  5.4 27.1 %collective-permute-start.4 = (bf16[1,96,3072]{2,1,0:T(8,128)(2,1)S(1)}, bf16[1,96,3072]{2,1,0:T(8,128)(2,1)S(1)}, u32[]{:S(2)}, u32[]{:S(2)}) collective-permute-start(bf16[1,96,3072]{2,1,0:T(8,128)(2,1)S(1)} %get-tuple-element.38.refs_0_), channel_id=1, source_target_pairs={{0,1},{1,0},{2,3},{3,2},{4,5},{5,4},{6,7},{7,6},{8,9},{9,8},{10,11... | collective-permute-start | bytes 1769480 | tf_op jit(solution)/shard_map/ppermute | solution.py:34
  6.6 25.9 %collective-permute-start.7 = (bf16[1,96,3072]{2,1,0:T(8,128)(2,1)S(1)}, bf16[1,96,3072]{2,1,0:T(8,128)(2,1)S(1)}, u32[]{:S(2)}, u32[]{:S(2)}) collective-permute-start(bf16[1,96,3072]{2,1,0:T(8,128)(2,1)S(1)} %get-tuple-element.39.refs_1_), channel_id=1, source_target_pairs={{0,2},{1,3},{2,0},{3,1},{4,6},{5,7},{6,4},{7,5},{8,10},{9,11},{10,... | collective-permute-start | bytes 1769480 | tf_op jit(solution)/shard_map/ppermute | solution.py:34
  6.9 25.6 %collective-permute-start.6 = (bf16[1,96,3072]{2,1,0:T(8,128)(2,1)S(1)}, bf16[1,96,3072]{2,1,0:T(8,128)(2,1)S(1)}, u32[]{:S(2)}, u32[]{:S(2)}) collective-permute-start(bf16[1,96,3072]{2,1,0:T(8,128)(2,1)S(1)} %get-tuple-element.39.refs_1_), channel_id=1, source_target_pairs={{0,1},{1,0},{2,3},{3,2},{4,5},{5,4},{6,7},{7,6},{8,9},{9,8},{10,11... | collective-permute-start | bytes 1769480 | tf_op jit(solution)/shard_map/ppermute | solution.py:34
  7.1 22.8 %copy-start.2 = (f32[8,32,32]{2,1,0:T(8,128)S(1)}, f32[8,32,32]{2,1,0:T(8,128)}, u32[]{:S(2)}) copy-start(f32[8,32,32]{2,1,0:T(8,128)} %gram_ref.1) | copy-start | bytes 98308
  16.1 2.5 %collective-permute-start = (f32[112,256]{1,0:T(8,128)S(1)}, f32[112,256]{1,0:T(8,128)S(1)}, u32[]{:S(2)}, u32[]{:S(2)}) collective-permute-start(f32[112,256]{1,0:T(8,128)S(1)} %get-tuple-element.35), channel_id=1, source_target_pairs={{0,4},{4,0},{8,12},{12,8},{16,20},{20,16},{24,28},{28,24},{1,5},{5... | collective-permute-start | bytes 344072 | tf_op jit(solution)/shard_map/ppermute | solution.py:34
  18.6 3.8 %collective-permute-start.1 = (bf16[112,256]{1,0:T(8,128)(2,1)S(1)}, bf16[112,256]{1,0:T(8,128)(2,1)S(1)}, u32[]{:S(2)}, u32[]{:S(2)}) collective-permute-start(bf16[112,256]{1,0:T(8,128)(2,1)S(1)} %add.27.one_ref), channel_id=1, source_target_pairs={{0,8},{4,12},{8,0},{12,4},{16,24},{20,28},{24,16},{28,20},{1,9},{5... | collective-permute-start | bytes 172040 | tf_op jit(solution)/shard_map/ppermute | solution.py:34
  22.4 4.0 %collective-permute-start.2 = (bf16[112,256]{1,0:T(8,128)(2,1)S(1)}, bf16[112,256]{1,0:T(8,128)(2,1)S(1)}, u32[]{:S(2)}, u32[]{:S(2)}) collective-permute-start(bf16[112,256]{1,0:T(8,128)(2,1)S(1)} %add.28.one_ref), channel_id=1, source_target_pairs={{0,16},{4,20},{8,24},{12,28},{16,0},{20,4},{24,8},{28,12},{1,17},{... | collective-permute-start | bytes 172040 | tf_op jit(solution)/shard_map/ppermute | solution.py:34
  26.5 3.4 %collective-permute-start.3 = (f32[112,256]{1,0:T(8,128)S(1)}, f32[112,256]{1,0:T(8,128)S(1)}, u32[]{:S(2)}, u32[]{:S(2)}) collective-permute-start(f32[112,256]{1,0:T(8,128)S(1)} %add.29.near_ref), channel_id=1, source_target_pairs={{0,4},{4,0},{8,12},{12,8},{16,20},{20,16},{24,28},{28,24},{1,5},{5... | collective-permute-start | bytes 344072 | tf_op jit(solution)/shard_map/ppermute | solution.py:34
  32.1 2.4 %collective-permute-start.8 = (bf16[4,1,32,3072]{3,2,1,0:T(8,128)(2,1)S(1)}, bf16[4,1,32,3072]{3,2,1,0:T(8,128)(2,1)S(1)}, u32[]{:S(2)}, u32[]{:S(2)}) collective-permute-start(bf16[4,1,32,3072]{3,2,1,0:T(8,128)(2,1)S(1)} %get-tuple-element.40), channel_id=1, source_target_pairs={{0,4},{4,0},{8,12},{12,8},{16,20},{20,16},{24,28},{28,24},{1,5},{5... | collective-permute-start | bytes 2359304 | tf_op jit(solution)/shard_map/ppermute | solution.py:34
  34.1 49.0 %copy-start.5 = (f32[2688]{0:T(1024)S(1)}, f32[2688]{0:T(1024)}, u32[]{:S(2)}) copy-start(f32[2688]{0:T(1024)} %param.19) | copy-start | bytes 32260
  34.1 49.0 %copy-start.6 = (f32[2688]{0:T(1024)S(1)}, f32[2688]{0:T(1024)}, u32[]{:S(2)}) copy-start(f32[2688]{0:T(1024)} %param.18) | copy-start | bytes 32260
  34.1 49.6 %copy-start.4 = (s32[8]{0:T(128)S(1)}, s32[8]{0:T(128)}, u32[]{:S(2)}) copy-start(s32[8]{0:T(128)} %owners.3) | copy-start | bytes 100
  35.2 6.6 %collective-permute-start.9 = (bf16[40,3072]{1,0:T(8,128)(2,1)S(1)}, bf16[40,3072]{1,0:T(8,128)(2,1)S(1)}, u32[]{:S(2)}, u32[]{:S(2)}) collective-permute-start(bf16[40,3072]{1,0:T(8,128)(2,1)S(1)} %get-tuple-element.43), channel_id=1, source_target_pairs={{0,1},{1,0},{2,3},{3,2},{4,5},{5,4},{6,7},{7,6},{8,9},{9,8},{10,11... | collective-permute-start | bytes 737288 | tf_op jit(solution)/shard_map/ppermute | solution.py:34
  36.5 7.1 %collective-permute-start.10 = (bf16[40,3072]{1,0:T(8,128)(2,1)S(1)}, bf16[40,3072]{1,0:T(8,128)(2,1)S(1)}, u32[]{:S(2)}, u32[]{:S(2)}) collective-permute-start(bf16[40,3072]{1,0:T(8,128)(2,1)S(1)} %get-tuple-element.44), channel_id=1, source_target_pairs={{0,2},{1,3},{2,0},{3,1},{4,6},{5,7},{6,4},{7,5},{8,10},{9,11},{10,... | collective-permute-start | bytes 737288 | tf_op jit(solution)/shard_map/ppermute | solution.py:34
  37.8 11.0 %collective-permute-start.11 = (bf16[40,3072]{1,0:T(8,128)(2,1)S(1)}, bf16[40,3072]{1,0:T(8,128)(2,1)S(1)}, u32[]{:S(2)}, u32[]{:S(2)}) collective-permute-start(bf16[40,3072]{1,0:T(8,128)(2,1)S(1)} %get-tuple-element.45), channel_id=1, source_target_pairs={{0,3},{1,2},{2,1},{3,0},{4,7},{5,6},{6,5},{7,4},{8,11},{9,10},{10,... | collective-permute-start | bytes 737288 | tf_op jit(solution)/shard_map/ppermute | solution.py:34
  49.7 18.0 %collective-permute-start.16 = (bf16[1,96,3072]{2,1,0:T(8,128)(2,1)S(1)}, bf16[1,96,3072]{2,1,0:T(8,128)(2,1)S(1)}, u32[]{:S(2)}, u32[]{:S(2)}) collective-permute-start(bf16[1,96,3072]{2,1,0:T(8,128)(2,1)S(1)} %get-tuple-element.51), channel_id=1, source_target_pairs={{0,2},{1,3},{2,0},{3,1},{4,6},{5,7},{6,4},{7,5},{8,10},{9,11},{10,... | collective-permute-start | bytes 1769480 | tf_op jit(solution)/shard_map/ppermute | solution.py:34
  50.9 16.8 %collective-permute-start.17 = (bf16[1,96,3072]{2,1,0:T(8,128)(2,1)S(1)}, bf16[1,96,3072]{2,1,0:T(8,128)(2,1)S(1)}, u32[]{:S(2)}, u32[]{:S(2)}) collective-permute-start(bf16[1,96,3072]{2,1,0:T(8,128)(2,1)S(1)} %get-tuple-element.52), channel_id=1, source_target_pairs={{0,1},{1,0},{2,3},{3,2},{4,5},{5,4},{6,7},{7,6},{8,9},{9,8},{10,11... | collective-permute-start | bytes 1769480 | tf_op jit(solution)/shard_map/ppermute | solution.py:34
  51.0 3.8 %collective-permute-start.12 = (bf16[2,32,768]{2,1,0:T(8,128)(2,1)S(1)}, bf16[2,32,768]{2,1,0:T(8,128)(2,1)S(1)}, u32[]{:S(2)}, u32[]{:S(2)}) collective-permute-start(bf16[2,32,768]{2,1,0:T(8,128)(2,1)S(1)} %get-tuple-element.48), channel_id=1, source_target_pairs={{0,8},{4,12},{8,0},{12,4},{16,24},{20,28},{24,16},{28,20},{1,9},{5... | collective-permute-start | bytes 294920 | tf_op jit(solution)/shard_map/ppermute | solution.py:34
  54.8 4.3 %collective-permute-start.13 = (bf16[1,32,768]{2,1,0:T(8,128)(2,1)S(1)}, bf16[1,32,768]{2,1,0:T(8,128)(2,1)S(1)}, u32[]{:S(2)}, u32[]{:S(2)}) collective-permute-start(bf16[1,32,768]{2,1,0:T(8,128)(2,1)S(1)} %get-tuple-element.50), channel_id=1, source_target_pairs={{0,16},{4,20},{8,24},{12,28},{16,0},{20,4},{24,8},{28,12},{1,17},{... | collective-permute-start | bytes 147464 | tf_op jit(solution)/shard_map/ppermute | solution.py:34
  59.2 4.5 %collective-permute-start.14 = (bf16[1,32,768]{2,1,0:T(8,128)(2,1)S(1)}, bf16[1,32,768]{2,1,0:T(8,128)(2,1)S(1)}, u32[]{:S(2)}, u32[]{:S(2)}) collective-permute-start(bf16[1,32,768]{2,1,0:T(8,128)(2,1)S(1)} %halve.3.refs_0_), channel_id=1, source_target_pairs={{0,16},{4,20},{8,24},{12,28},{16,0},{20,4},{24,8},{28,12},{1,17},{... | collective-permute-start | bytes 147464 | tf_op jit(solution)/shard_map/ppermute | solution.py:34
  63.6 4.1 %collective-permute-start.15 = (bf16[2,32,768]{2,1,0:T(8,128)(2,1)S(1)}, bf16[2,32,768]{2,1,0:T(8,128)(2,1)S(1)}, u32[]{:S(2)}, u32[]{:S(2)}) collective-permute-start(bf16[2,32,768]{2,1,0:T(8,128)(2,1)S(1)} %stack.35.refs_0_), channel_id=1, source_target_pairs={{0,8},{4,12},{8,0},{12,4},{16,24},{20,28},{24,16},{28,20},{1,9},{5... | collective-permute-start | bytes 294920 | tf_op jit(solution)/shard_map/ppermute | solution.py:34
  68.3 5.6 %collective-permute-start.20 = (bf16[1,32,3072]{2,1,0:T(8,128)(2,1)S(1)}, bf16[1,32,3072]{2,1,0:T(8,128)(2,1)S(1)}, u32[]{:S(2)}, u32[]{:S(2)}) collective-permute-start(bf16[1,32,3072]{2,1,0:T(8,128)(2,1)S(1)} %bitcast.15), channel_id=1, source_target_pairs={{0,3},{1,2},{2,1},{3,0},{4,7},{5,6},{6,5},{7,4},{8,11},{9,10},{10,... | collective-permute-start | bytes 589832 | tf_op jit(solution)/shard_map/ppermute | solution.py:34
  69.6 6.3 %collective-permute-start.19 = (bf16[1,32,3072]{2,1,0:T(8,128)(2,1)S(1)}, bf16[1,32,3072]{2,1,0:T(8,128)(2,1)S(1)}, u32[]{:S(2)}, u32[]{:S(2)}) collective-permute-start(bf16[1,32,3072]{2,1,0:T(8,128)(2,1)S(1)} %bitcast.16), channel_id=1, source_target_pairs={{0,2},{1,3},{2,0},{3,1},{4,6},{5,7},{6,4},{7,5},{8,10},{9,11},{10,... | collective-permute-start | bytes 589832 | tf_op jit(solution)/shard_map/ppermute | solution.py:34
  70.7 5.2 %collective-permute-start.18 = (bf16[1,32,3072]{2,1,0:T(8,128)(2,1)S(1)}, bf16[1,32,3072]{2,1,0:T(8,128)(2,1)S(1)}, u32[]{:S(2)}, u32[]{:S(2)}) collective-permute-start(bf16[1,32,3072]{2,1,0:T(8,128)(2,1)S(1)} %bitcast.17), channel_id=1, source_target_pairs={{0,1},{1,0},{2,3},{3,2},{4,5},{5,4},{6,7},{7,6},{8,9},{9,8},{10,11... | collective-permute-start | bytes 589832 | tf_op jit(solution)/shard_map/ppermute | solution.py:34
  76.0 13.1 %collective-permute-start.21 = (bf16[4,1,32,3072]{3,2,1,0:T(8,128)(2,1)S(1)}, bf16[4,1,32,3072]{3,2,1,0:T(8,128)(2,1)S(1)}, u32[]{:S(2)}, u32[]{:S(2)}) collective-permute-start(bf16[4,1,32,3072]{3,2,1,0:T(8,128)(2,1)S(1)} %bitcast.12), channel_id=1, source_target_pairs={{0,4},{4,0},{8,12},{12,8},{16,20},{20,16},{24,28},{28,24},{1,5},{5... | collective-permute-start | bytes 2359304 | tf_op jit(solution)/shard_map/ppermute | solution.py:34
  83.7 5.4 %copy-start = (f32[1,2,96,3072]{3,2,1,0:T(8,128)S(1)}, f32[1,2,96,3072]{3,2,1,0:T(8,128)}, u32[]{:S(2)}) copy-start(f32[1,2,96,3072]{3,2,1,0:T(8,128)} %refs_9_.1) | copy-start | bytes 7077892
  83.7 5.4 %copy-start.1 = (f32[1,2,96,3072]{3,2,1,0:T(8,128)S(1)}, f32[1,2,96,3072]{3,2,1,0:T(8,128)}, u32[]{:S(2)}) copy-start(f32[1,2,96,3072]{3,2,1,0:T(8,128)} %refs_10_.1) | copy-start | bytes 7077892

commit v8 on v7

--- a/solution.py
+++ b/solution.py
@@ -10,7 +10,7 @@
 CORES = 2
 AHEAD = 4
 BASE_ROWS = 16
-COLUMNS = 256
+COLUMNS = 384
 F32 = jnp.float32
 BF16 = jnp.bfloat16
 
@@ -104,22 +104,22 @@
     )(pos, gradients, feedback, right_t, vec)
 
 
-def add_kernel(one_ref, other_ref, *refs):
+def add_kernel(*refs):
     out = refs[-1]
-    out[...] = (one_ref[...].astype(F32) + other_ref[...].astype(F32)).astype(out.dtype)
-
-
-def add(parts, dtype, after=()):
+    out[...] = tree_sum([ref[...].astype(F32) for ref in refs[:-1]]).astype(out.dtype)
+
+
+def add(parts, dtype):
     vmem = pl.BlockSpec(memory_space=pltpu.VMEM)
     return pl.pallas_call(
         add_kernel,
-        in_specs=[vmem] * 2 + [pl.BlockSpec(memory_space=pl.ANY)] * len(after),
+        in_specs=[vmem] * len(parts),
         out_specs=vmem,
         out_shape=jax.ShapeDtypeStruct(parts[0].shape, dtype),
         compiler_params=params(),
         cost_estimate=cost(),
         name="add",
-    )(*parts, *after)
+    )(*parts)
 
 
 def send_kernel(half, pos, near_ref, far_ref, gram_ref, comp_ref, send_ref, lt_ref, mix_ref, vec_ref, left, gram):
@@ -245,64 +245,15 @@
     )(pos, keep, recv, lt, *after)
 
 
-def column_kernel(places, pos, *refs):
-    out = refs[-1]
-    for ref, relative in zip(refs, places):
-        for i, d in enumerate(relative):
-            cols = ref.shape[2]
-            out[:, pl.ds(pl.multiple_of((pos[4] ^ d) * cols, cols), cols)] = ref[i]
-
-
-def column_gather(pos, parts, places, after):
-    unit, cols = parts[0].shape[1:]
-    vmem = pl.BlockSpec(memory_space=pltpu.VMEM)
-    count = sum(part.shape[0] for part in parts)
-    return pl.pallas_call(
-        functools.partial(column_kernel, places),
-        grid_spec=pltpu.PrefetchScalarGridSpec(
-            num_scalar_prefetch=1,
-            grid=(1,),
-            in_specs=[vmem] * len(parts) + [pl.BlockSpec(memory_space=pl.ANY)] * len(after),
-            out_specs=vmem,
-        ),
-        out_shape=jax.ShapeDtypeStruct((unit, cols * count), BF16),
-        compiler_params=params(),
-        cost_estimate=cost(),
-        name="column_gather",
-    )(pos, *parts, *after)
-
-
-def halve_kernel(keep_ref, recv_ref, *outs):
-    for i in range(keep_ref.shape[0]):
-        out = outs[i % len(outs)]
-        out[i // len(outs)] = (keep_ref[i] + recv_ref[i].astype(F32)).astype(out.dtype)
-
-
-def halve(keep, recv):
-    count, unit, cols = keep.shape
-    vmem = pl.BlockSpec(memory_space=pltpu.VMEM)
-    shape = (max(count // 2, 1), unit, cols)
-    kinds = [F32, BF16] if count > 1 else [BF16]
-    return pl.pallas_call(
-        halve_kernel,
-        in_specs=[vmem] * 2,
-        out_specs=[vmem] * len(kinds),
-        out_shape=[jax.ShapeDtypeStruct(shape, kind) for kind in kinds],
-        compiler_params=params(),
-        cost_estimate=cost(),
-        name="halve",
-    )(keep, recv)
-
-
 def plane_kernel(pos, own_ref, strip_ref, *refs):
-    terms, (keep_ref, send_ref, mix_ref) = refs[:-3], refs[-3:]
+    n_z = own_ref.shape[1] // refs[-2].shape[1]
+    terms, outs, mix_ref = refs[: -n_z - 1], refs[-n_z - 1 : -1], refs[-1]
     unit, n = own_ref.shape
-    cols = keep_ref.shape[2]
-    for d in range(n // cols):
+    cols = n // n_z
+    for d, out in enumerate(outs):
         block = pl.ds(pl.multiple_of((pos[4] ^ d) * cols, cols), cols)
         parts = [own_ref[:, block]] + [term[:, block].astype(F32)[:unit] for term in terms]
-        out = send_ref if d % 2 else keep_ref
-        out[d // 2] = tree_sum(parts).astype(out.dtype)
+        out[...] = tree_sum(parts).astype(out.dtype)
     strip = strip_ref[...]
     for d, term in enumerate(terms, 1):
         strip = jnp.where(pos[7] == d, term[...].astype(F32)[unit:], strip)
@@ -322,12 +273,8 @@
 def plane_sum(pos, own, strip, terms, n_z, nmat, rank):
     unit, n = own.shape
     count = strip.size // (nmat * rank)
-    shape = (n_z // 2, unit, n // n_z)
-    outs = [
-        jax.ShapeDtypeStruct(shape, F32),
-        jax.ShapeDtypeStruct(shape, BF16),
-        jax.ShapeDtypeStruct((nmat, count, count + 2 * rank), BF16),
-    ]
+    outs = [jax.ShapeDtypeStruct((unit, n // n_z), BF16 if d else F32) for d in range(n_z)]
+    outs.append(jax.ShapeDtypeStruct((nmat, count, count + 2 * rank), BF16))
     vmem = pl.BlockSpec(memory_space=pltpu.VMEM)
     return pl.pallas_call(
         plane_kernel,
@@ -344,40 +291,36 @@
     )(pos, own, strip, *terms)
 
 
-def stack_kernel(*refs):
-    out, first = refs[-1], 0
-    for part in refs[:-1]:
-        out[first : first + part.shape[0]] = part[...]
-        first += part.shape[0]
-
-
-def stack(parts):
-    vmem = pl.BlockSpec(memory_space=pltpu.VMEM)
-    count = sum(part.shape[0] for part in parts)
+def stack_kernel(count, *refs):
+    for i in range(count):
+        refs[-1][i] = refs[i][...]
+
+
+def stack(parts, after=()):
+    vmem = pl.BlockSpec(memory_space=pltpu.VMEM)
     return pl.pallas_call(
-        stack_kernel,
-        in_specs=[vmem] * len(parts),
+        functools.partial(stack_kernel, len(parts)),
+        in_specs=[vmem] * len(parts) + [pl.BlockSpec(memory_space=pl.ANY)] * len(after),
         out_specs=vmem,
-        out_shape=jax.ShapeDtypeStruct((count,) + parts[0].shape[1:], parts[0].dtype),
+        out_shape=jax.ShapeDtypeStruct((len(parts),) + parts[0].shape, parts[0].dtype),
         compiler_params=params(),
         cost_estimate=cost(),
         name="stack",
-    )(*parts)
-
-
-def forward_kernel(*refs):
-    count = len(refs) // 2
-    for source, out in zip(refs, refs[-count:]):
-        out[...] = source[...]
-
-
-def forward(parts, after):
+    )(*parts, *after)
+
+
+def forward_kernel(cuts, *refs):
+    for source, out, first in zip(refs, refs[-len(cuts) :], cuts):
+        out[...] = source[first : first + out.shape[0]]
+
+
+def forward(parts, cuts, count, after):
     vmem = pl.BlockSpec(memory_space=pltpu.VMEM)
     return pl.pallas_call(
-        forward_kernel,
+        functools.partial(forward_kernel, cuts),
         in_specs=[vmem] * len(parts) + [pl.BlockSpec(memory_space=pl.ANY)],
         out_specs=[vmem] * len(parts),
-        out_shape=[jax.ShapeDtypeStruct(part.shape, part.dtype) for part in parts],
+        out_shape=[jax.ShapeDtypeStruct((count,) + part.shape[1:], part.dtype) for part in parts],
         compiler_params=params(),
         cost_estimate=cost(),
         name="forward",
@@ -392,78 +335,90 @@
 
 
 def outputs_kernel(second, places, pos, owners, comp_ref, mix_ref, mixr_ref, near_ref, *refs):
-    n_base = len(places)
-    n_state = 2 if second else 0
+    n_base = len({a for a, _ in places.values()})
     bases, refs = refs[:n_base], refs[n_base:]
     if second:
-        far_ref, states, refs = refs[0], refs[1 : 1 + n_state], refs[1 + n_state + 2 :]
-    outs, refs = refs[: 2 + n_state], refs[2 + n_state :]
+        far_ref, momentum_ref, master_ref, refs = refs[0], refs[1], refs[2], refs[5:]
+    n_out = 4 if second else 2
+    outs, refs = refs[:n_out], refs[n_out:]
     held, feedback, weights, fetch_sem, out_sem = refs[:5]
-    half, upm, unit, n = near_ref.shape
-    rows, count = feedback.shape[1], held.shape[1]
+    half, upm, n_z, unit, cols = near_ref.shape
+    count = held.shape[1]
     capacity = max(c for _, c in places) + 1
 
-    def right_of(ref, j):
-        parts = [ref[j, i ^ pos[1]] for i in range(upm)]
+    def right_of(ref, j, d, block):
+        parts = [ref[j, i ^ pos[1], d, :, block] for i in range(upm)]
         return parts[0] if upm == 1 else jnp.concatenate(parts, axis=0)
 
+    def columns(d, first=0, size=cols):
+        return pl.ds(pl.multiple_of((pos[4] ^ d) * cols + first, 128), size)
+
+    pieces = [slice(first, first + COLUMNS) for first in range(0, cols, COLUMNS)]
     matrices = [(j + (half if second else 0)) ^ pos[0] for j in range(half)]
     for j, k in enumerate(matrices):
         slot = (owners[k] ^ pos[5]) * capacity + rank_of(owners, k)
-        for a, (d, c) in enumerate(places):
+        for (d, c), (a, row) in places.items():
 
             @pl.when(slot == d * capacity + c)
             def _():
-                pltpu.make_async_copy(bases[a].at[0], held.at[j], fetch_sem.at[j]).start()
+                pltpu.make_async_copy(bases[a].at[row], held.at[j], fetch_sem.at[j]).start()
+
+    stores = []
+
+    def store(source, target, sem):
+        stores.append(pltpu.make_async_copy(source, target, sem))
+        stores[-1].start()
 
     if second:
-        scratch, state_in, state_out = refs[5:7], refs[7], refs[8]
-        loads = [
-            pltpu.make_async_copy(states[i].at[0, c], scratch[i].at[c], state_in.at[i, c])
-            for c in range(capacity)
-            for i in range(n_state)
-        ]
-        for load in loads:
-            load.start()
-
-    stores = []
+        new_momentum, new_master, state_sem = refs[5:8]
+        for c in range(capacity):
+            matrix = jnp.int32(-1)
+            for k in range(owners.shape[0]):
+                matrix = jnp.where((owners[k] == pos[5]) & (rank_of(owners, k) == c), k, matrix)
+            safe = jnp.maximum(matrix, 0)
+            slot = safe ^ pos[0]
+            inner = lax.rem(slot, half)
+            mixr = mixr_ref[safe][:, count:]
+            for d in range(n_z):
+                for block in pieces:
+                    right = jnp.where(
+                        slot < half,
+                        right_of(near_ref, inner, d, block),
+                        right_of(far_ref, inner, d, block),
+                    )
+                    both = jnp.concatenate([right, right], axis=0)
+                    change = jnp.dot(mixr, both, preferred_element_type=F32)
+                    change = jnp.where(matrix >= 0, 10.0 * change, 0.0)
+                    place = columns(d, block.start, COLUMNS)
+                    momentum = 0.9 * momentum_ref[c, :, place] - change
+                    new_momentum[c, :, place] = momentum
+                    new_master[c, :, place] = master_ref[c, :, place] - 0.1 * momentum
+                place = columns(d)
+                for i, new in enumerate((new_momentum, new_master)):
+                    store(
+                        new.at[c, :, place], outs[2 + i].at[0, c, :, place], state_sem.at[i, c, d]
+                    )
+
     for j, k in enumerate(matrices):
-        right = right_of(far_ref if second else near_ref, j)
+        ref = far_ref if second else near_ref
         mix, mixr = mix_ref[k], mixr_ref[k]
+        for d in range(n_z):
+            for block in pieces:
+                right = right_of(ref, j, d, block)
+                place = columns(d, block.start, COLUMNS)
+                both = jnp.concatenate([comp_ref[k, :, place], right], axis=0)
+                feedback[j, :, place] = jnp.dot(mix, both, preferred_element_type=F32).astype(BF16)
+            place = columns(d)
+            store(feedback.at[j, :, place], outs[0].at[0, k, :, place], out_sem.at[j, d, 0])
         pltpu.make_async_copy(bases[0].at[0], held.at[j], fetch_sem.at[j]).wait()
-        for first in range(0, n, COLUMNS):
-            block = slice(first, first + COLUMNS)
-            part = right[:, block]
-            both = jnp.concatenate([comp_ref[k, :, block], part], axis=0)
-            feedback[j, :, block] = jnp.dot(mix, both, preferred_element_type=F32).astype(BF16)
-            both = jnp.concatenate([held[j, :, block], part, part], axis=0)
-            weights[j, :, block] = jnp.dot(mixr, both, preferred_element_type=F32).astype(BF16)
-        for source, target, i in ((feedback, outs[0].at[0, k], 0), (weights, outs[1].at[k], 1)):
-            stores.append(pltpu.make_async_copy(source.at[j], target, out_sem.at[j, i]))
-            stores[-1].start()
-
-    for c in range(capacity if second else 0):
-        matrix = jnp.int32(-1)
-        for k in range(owners.shape[0]):
-            matrix = jnp.where((owners[k] == pos[5]) & (rank_of(owners, k) == c), k, matrix)
-        safe = jnp.maximum(matrix, 0)
-        slot = safe ^ pos[0]
-        inner = lax.rem(slot, half)
-        right = jnp.where(slot < half, right_of(near_ref, inner), right_of(far_ref, inner))
-        both = jnp.concatenate([right, right], axis=0)
-        mixr = mixr_ref[safe][:, count:]
-        for load in loads[c * n_state : (c + 1) * n_state]:
-            load.wait()
-        for first in range(0, n, COLUMNS):
-            block = slice(first, first + COLUMNS)
-            change = jnp.dot(mixr, both[:, block], preferred_element_type=F32)
-            momentum = 0.9 * scratch[0][c, :, block] - jnp.where(matrix >= 0, 10.0 * change, 0.0)
-            scratch[0][c, :, block] = momentum
-            scratch[1][c, :, block] -= 0.1 * momentum
-        for i in range(n_state):
-            copy = pltpu.make_async_copy(scratch[i].at[c], outs[2 + i].at[0, c], state_out.at[i, c])
-            copy.start()
-            stores.append(copy)
+        for d in range(n_z):
+            for block in pieces:
+                right = right_of(ref, j, d, block)
+                place = columns(d, block.start, COLUMNS)
+                both = jnp.concatenate([held[j, :, place], right, right], axis=0)
+                weights[j, :, place] = jnp.dot(mixr, both, preferred_element_type=F32).astype(BF16)
+            place = columns(d)
+            store(weights.at[j, :, place], outs[1].at[k, :, place], out_sem.at[j, d, 1])
 
     for copy in stores:
         copy.wait()
@@ -471,7 +426,7 @@
 
 def outputs(pos, owners, comp, mix, mixr, near, bases, places, far=None, states=(), earlier=()):
     nmat, rows, n = comp.shape
-    half = near.shape[0]
+    half, _, n_z = near.shape[:3]
     capacity = max(c for _, c in places) + 1
     replica_rows = bases[0].shape[1]
     second = far is not None
@@ -482,15 +437,15 @@
         pltpu.VMEM((half, rows, n), BF16),
         pltpu.VMEM((half, replica_rows, n), BF16),
         pltpu.SemaphoreType.DMA((half,)),
-        pltpu.SemaphoreType.DMA((half, 2)),
+        pltpu.SemaphoreType.DMA((half, n_z, 2)),
     ]
     if second:
         scratch += [pltpu.VMEM((capacity, replica_rows, n), F32)] * 2
-        scratch += [pltpu.SemaphoreType.DMA((2, capacity))] * 2
+        scratch += [pltpu.SemaphoreType.DMA((2, capacity, n_z))]
     outs = [
         jax.ShapeDtypeStruct((1, nmat, rows, n), BF16),
         jax.ShapeDtypeStruct((nmat, replica_rows, n), BF16),
-    ] + [jax.ShapeDtypeStruct(x.shape, F32) for x in states]
+    ] + [jax.ShapeDtypeStruct((1,) + x.shape, F32) for x in states]
     fars = [far] if second else []
     first = 6 + len(bases) + len(fars) + len(states)
     return pl.pallas_call(
@@ -500,8 +455,8 @@
             grid=(1,),
             in_specs=[vmem] * 4
             + [any_spec] * len(bases)
-            + [vmem] * len(fars)
-            + [any_spec] * (len(states) + len(earlier)),
+            + [vmem] * (len(fars) + len(states))
+            + [any_spec] * len(earlier),
             out_specs=[any_spec] * len(outs),
             scratch_shapes=scratch,
         ),
@@ -514,9 +469,9 @@
 
 
 def base_kernel(momentum_ref, master_ref, *refs):
-    outs, (momentum, master, sems) = refs[:-3], refs[-3:]
-    rows = outs[0].shape[1]
-    blocks = [(c, first) for c in range(len(outs)) for first in range(0, rows, BASE_ROWS)]
+    out_ref, momentum, master, sems = refs
+    capacity, rows, _ = out_ref.shape
+    blocks = [(c, first) for c in range(capacity) for first in range(0, rows, BASE_ROWS)]
 
     def copies(i):
         c, first = blocks[i]
@@ -533,22 +488,23 @@
         for copy in copies(i):
             copy.wait()
         part = slice(first, first + BASE_ROWS)
-        outs[c][0, part] = (master[c, part] - 0.09 * momentum[c, part]).astype(BF16)
+        out_ref[c, part] = (master[c, part] - 0.09 * momentum[c, part]).astype(BF16)
 
 
 def base_of(momentum, master):
     _, capacity, rows, n = momentum.shape
-    return pl.pallas_call(
+    state = jax.ShapeDtypeStruct((capacity, rows, n), F32)
+    base, momentum, master = pl.pallas_call(
         base_kernel,
         in_specs=[pl.BlockSpec(memory_space=pl.ANY)] * 2,
-        out_specs=[pl.BlockSpec(memory_space=pltpu.VMEM)] * capacity,
-        out_shape=[jax.ShapeDtypeStruct((1, rows, n), BF16)] * capacity,
-        scratch_shapes=[pltpu.VMEM((capacity, rows, n), F32)] * 2
-        + [pltpu.SemaphoreType.DMA((2, capacity * rows // BASE_ROWS))],
+        out_specs=[pl.BlockSpec(memory_space=pltpu.VMEM)] * 3,
+        out_shape=[jax.ShapeDtypeStruct((capacity, rows, n), BF16), state, state],
+        scratch_shapes=[pltpu.SemaphoreType.DMA((2, capacity * rows // BASE_ROWS))],
         compiler_params=params(),
         cost_estimate=cost(),
         name="base",
     )(momentum, master)
+    return base, (momentum, master)
 
 
 def per_device(
@@ -582,12 +538,10 @@
     in_hbm = lambda x: pltpu.with_memory_space_constraint(x, pltpu.HBM)
 
     square = n_mp == 4 and capacity == 2
-    near_owners = range(1, 3 if square else n_mp)
-    states = in_hbm(momentum), in_hbm(master_weights)
-    held = {(0, c): part for c, part in enumerate(base_of(*states))}
-    for c in range(capacity):
-        for d in near_owners:
-            held[d, c] = exchange(held[0, c], "mp", d)
+    base, states = base_of(in_hbm(momentum), in_hbm(master_weights))
+    early = [exchange(base, "mp", d) for d in range(1, 3 if square else n_mp)]
+    bases = [base] + early
+    places = {(d, c): (d, c) for d in range(len(bases)) for c in range(capacity)}
 
     nvec = vector_grads.shape[1]
     comp, near, far = left_terms(
@@ -598,48 +552,38 @@
         vector_grads,
     )
     piece = add([near, exchange(far, "replica", 1)], BF16)
-    early = [held[d, 0] for d in near_owners]
-    middle = [held[d, c] for c in range(1, capacity) for d in near_owners]
-    steps = [1 << i for i in range(n_z.bit_length() - 1)]
-    for d in steps:
-        last = d == steps[-1]
-        recv = exchange(piece, "replica", CORES * d)
-        piece = add([piece, recv], F32 if last else BF16, ())
+    piece = add([near, exchange(far, "replica", 1)], BF16)
+    along_z = lambda x: [exchange(x, "replica", CORES * d) for d in range(1, n_z)]
+    piece = add([piece] + along_z(piece), F32)
     near, far = piece, exchange(piece, "replica", 1)
 
-    send, keep, lt, mix, vector_rows = right_terms(pos, near, far, gram_root, comp, upm, early + middle)
+    send, keep, lt, mix, vector_rows = right_terms(pos, near, far, gram_root, comp, upm, early)
     vector_total = vector_rows.reshape(-1)[:nvec]
     recv = exchange(send, "replica", 1)
     own, strip, *chip = chip_sum(pos, keep, recv, lt, replica_rows, [])
     plane = [exchange(part, "mp", d) for d, part in enumerate(chip, 1)]
-    kept, *sent, mixr = plane_sum(pos, own, strip, plane, n_z, nmat, rank)
+    *final, mixr = plane_sum(pos, own, strip, plane, n_z, nmat, rank)
     late = []
     if square:
-        late = forward([held[1, 0], held[2, 1]], mixr)
-        late = [exchange(late[0], "mp", 2), exchange(late[1], "mp", 1)]
-        held[3, 0], held[3, 1] = late
-    for d in steps:
-        kept, *sent = halve(kept, exchange(sent[0], "replica", CORES * d))
-
-    parts, relative = [kept], [[0]]
-    for d in reversed(steps):
-        have = stack(parts) if len(parts) > 1 else parts[0]
-        order = sum(relative, [])
-        parts = [have, exchange(have, "replica", CORES * d)]
-        relative = [order, [i ^ d for i in order]]
-    whole = column_gather(pos, parts, relative, late)[None]
+        parts = forward(early, [0, 1], 1, mixr)
+        late = [exchange(part, "mp", 2 - i) for i, part in enumerate(parts)]
+        bases = bases + late
+        places[3, 0], places[3, 1] = (3, 0), (4, 0)
+    final = [final[0]] + [exchange(final[d], "replica", CORES * d) for d in range(1, n_z)]
+    final = add(final, BF16)
+    new_vector_momentum = 0.9 * vector_momentum + vector_total
+    new_vector_params = vector_params - 0.1 * new_vector_momentum
+
+    whole = stack([final] + along_z(final), late + [new_vector_params])
     near = stack([whole] + [exchange(whole, "mp", d) for d in range(1, n_mp)])
-    near = near.reshape(half, upm, unit, n)
+    near = near.reshape((half, upm) + whole.shape)
     far = exchange(near, "replica", 1)
 
-    places, bases = list(held), list(held.values())
     done = outputs(pos, owners, comp, mix, mixr, near, bases, places)
     new_feedback, new_weights, new_momentum, new_master = outputs(
-        pos, owners, comp, mix, mixr, near, bases, places, far, (momentum, master_weights), done
+        pos, owners, comp, mix, mixr, near, bases, places, far, states, done
     )
 
-    new_vector_momentum = 0.9 * vector_momentum + vector_total
-    new_vector_params = vector_params - 0.1 * new_vector_momentum
     return new_feedback, new_momentum, new_master, new_weights, new_vector_momentum, new_vector_params
 
 

time: 97.1 us -> 93.2 us (0.960)
  waiting for transfers between devices: 30.5 us -> 27.1 us
  local copies, waits for them, and re-layouts: 0.13 us -> 2.94 us
  starting transfers between devices: 33.9 us -> 31.7 us
  Pallas kernels: 30.9 us -> 29.7 us
    ppermute x22 -> x23, waiting for transfers between devices: 30.5 us -> 27.1 us  [exchange(): return lax.ppermute(x, axis, [(i, i ^ distance) for i in range(size)])]
    unnamed x15 -> x21, local copies, waits for them, and re-layouts: 0.05 us -> 2.86 us
    ppermute x22 -> x23, starting transfers between devices: 33.9 us -> 31.7 us  [exchange(): return lax.ppermute(x, axis, [(i, i ^ distance) for i in range(size)])]
  transfers between devices with their start and end apart: 22 -> 23, of which waited for: 15 -> 14; matrix products, arithmetic and copies ran while one was open for 1% -> 1% of each run, Pallas kernels for 19% -> 20%
where the time goes in v8:
time: 93.2 us; the launch traced here: 93.1 us
  starting transfers between devices  31.7 us (34%)
  Pallas kernels  29.7 us (32%)
  waiting for transfers between devices  27.1 us (29%)
  local copies, waits for them, and re-layouts  2.94 us (3%)
  between operations  0.98 us (1%)
    ppermute x23, starting transfers between devices, exchange(): return lax.ppermute(x, axis, [(i, i ^ distance) for i in range(size)])  31.7 us
    ppermute x23, waiting for transfers between devices, exchange(): return lax.ppermute(x, axis, [(i, i ^ distance) for i in range(size)])  27.1 us
    pallas_call x2, Pallas kernels, outputs(): pl.pallas_call(functools.partial(outputs_kernel, second, places), grid_sp...  12.4 us
    pallas_call x1, Pallas kernels, left_terms(): pl.pallas_call(left_kernel, grid_spec=pltpu.PrefetchScalarGridSpec(num_sc...  9.01 us
    unnamed x21, local copies, waits for them, and re-layouts  2.86 us
    pallas_call x1, Pallas kernels, base_of(): pl.pallas_call(base_kernel, in_specs=[pl.BlockSpec(memory_space=pl.ANY)]...  2.65 us
    pallas_call x1, Pallas kernels, right_terms(): pl.pallas_call(functools.partial(send_kernel, half), grid_spec=pltpu.Pref...  2.22 us
  transfers between devices with their start and end apart: 23, of which 14 were waited for; matrix products, arithmetic and copies ran while one was open for 1% of the time, Pallas kernels for 20%

profile of v8, /device:TPU:1, one launch (start us, length us, event | category | flops | bytes accessed | tf_op | source)
XLA Modules:
  0.0 93.1 jit_solution(16463737522817840821)
XLA Ops:
  0.6 2.6 %base.1 = (bf16[2,96,3072]{2,1,0:T(8,128)(2,1)S(1)}, f32[2,96,3072]{2,1,0:T(8,128)S(1)}, f32[2,96,3072]{2,1,0:T(8,128)S(1)}) custom-call(f32[1,2,96,3072]{3,2,1,0:T(8,128)} %momentum_ref.1, f32[1,2,96,3072]{3,2,1,0:T(8,128)} %master_ref.1), custom_call_target="tpu_custom_call" | custom-call | flops 1000 | bytes 1000 | tf_op jit(solution)/shard_map/base/pallas_call | solution.py:497
  3.3 1.4 %copy-done = f32[2,96,3072]{2,1,0:T(8,128)} copy-done((f32[2,96,3072]{2,1,0:T(8,128)}, f32[2,96,3072]{2,1,0:T(8,128)S(1)}, u32[]{:S(2)}) %copy-start) | copy-done | bytes 2359320
  4.7 1.4 %copy-done.2 = f32[2,96,3072]{2,1,0:T(8,128)} copy-done((f32[2,96,3072]{2,1,0:T(8,128)}, f32[2,96,3072]{2,1,0:T(8,128)S(1)}, u32[]{:S(2)}) %copy-start.2) | copy-done | bytes 2359320
  6.1 2.1 %collective-permute-start.6 = (bf16[2,96,3072]{2,1,0:T(8,128)(2,1)S(1)}, bf16[2,96,3072]{2,1,0:T(8,128)(2,1)S(1)}, u32[]{:S(2)}, u32[]{:S(2)}) collective-permute-start(bf16[2,96,3072]{2,1,0:T(8,128)(2,1)S(1)} %get-tuple-element.39.refs_0_), channel_id=1, source_target_pairs={{0,2},{1,3},{2,0},{3,1},{4,6},{5,7},{6,4},{7,5},{8,10},{9,11},{10,... | collective-permute-start | bytes 3538952 | tf_op jit(solution)/shard_map/ppermute | solution.py:34
  8.2 1.2 %collective-permute-start.5 = (bf16[2,96,3072]{2,1,0:T(8,128)(2,1)S(1)}, bf16[2,96,3072]{2,1,0:T(8,128)(2,1)S(1)}, u32[]{:S(2)}, u32[]{:S(2)}) collective-permute-start(bf16[2,96,3072]{2,1,0:T(8,128)(2,1)S(1)} %get-tuple-element.39.refs_0_), channel_id=1, source_target_pairs={{0,1},{1,0},{2,3},{3,2},{4,5},{5,4},{6,7},{7,6},{8,9},{9,8},{10,11... | collective-permute-start | bytes 3538952 | tf_op jit(solution)/shard_map/ppermute | solution.py:34
  9.5 9.0 %left_terms.1 = (bf16[8,192,3072]{2,1,0:T(8,128)(2,1)S(1)}, f32[112,256]{1,0:T(8,128)S(1)}, f32[112,256]{1,0:T(8,128)S(1)}) custom-call(s32[8]{0:T(128)S(1)} %stack.34.pos, bf16[1,8,192,3072]{3,2,1,0:T(8,128)(2,1)} %g_ref.1, bf16[1,8,192,3072]{3,2,1,0:T(8,128)(2,1)} %f_ref.1, bf16[8,32,3072]{2,1,0:T(8,128)(2,1)} %bitcast.15, f32[1,2688]{1,0:T(1,128)S(1)} %copy-done.6), custom_call_target="tpu_custom_call" | custom-call | flops 1000 | bytes 1000 | tf_op jit(solution)/shard_map/left_terms/pallas_call | solution.py:86
  18.5 1.3 %collective-permute-start = (f32[112,256]{1,0:T(8,128)S(1)}, f32[112,256]{1,0:T(8,128)S(1)}, u32[]{:S(2)}, u32[]{:S(2)}) collective-permute-start(f32[112,256]{1,0:T(8,128)S(1)} %get-tuple-element.36), channel_id=1, source_target_pairs={{0,4},{4,0},{8,12},{12,8},{16,20},{20,16},{24,28},{28,24},{1,5},{5... | collective-permute-start | bytes 344072 | tf_op jit(solution)/shard_map/ppermute | solution.py:34
  19.8 1.0 %collective-permute-done.refs_1_ = f32[112,256]{1,0:T(8,128)S(1)} collective-permute-done((f32[112,256]{1,0:T(8,128)S(1)}, f32[112,256]{1,0:T(8,128)S(1)}, u32[]{:S(2)}, u32[]{:S(2)}) %collective-permute-start) | collective-permute-done | bytes 114720 | tf_op jit(solution)/shard_map/ppermute | solution.py:34
  20.8 3.4 %collective-permute-start.3 = (bf16[112,256]{1,0:T(8,128)(2,1)S(1)}, bf16[112,256]{1,0:T(8,128)(2,1)S(1)}, u32[]{:S(2)}, u32[]{:S(2)}) collective-permute-start(bf16[112,256]{1,0:T(8,128)(2,1)S(1)} %add.27.refs_0_), channel_id=1, source_target_pairs={{0,24},{4,28},{8,16},{12,20},{16,8},{20,12},{24,0},{28,4},{1,25},{... | collective-permute-start | bytes 172040 | tf_op jit(solution)/shard_map/ppermute | solution.py:34
  24.5 1.3 %collective-permute-done.3.refs_3_ = bf16[112,256]{1,0:T(8,128)(2,1)S(1)} collective-permute-done((bf16[112,256]{1,0:T(8,128)(2,1)S(1)}, bf16[112,256]{1,0:T(8,128)(2,1)S(1)}, u32[]{:S(2)}, u32[]{:S(2)}) %collective-permute-start.3) | collective-permute-done | bytes 57376 | tf_op jit(solution)/shard_map/ppermute | solution.py:34
  25.8 3.4 %collective-permute-done.2.refs_2_ = bf16[112,256]{1,0:T(8,128)(2,1)S(1)} collective-permute-done((bf16[112,256]{1,0:T(8,128)(2,1)S(1)}, bf16[112,256]{1,0:T(8,128)(2,1)S(1)}, u32[]{:S(2)}, u32[]{:S(2)}) %collective-permute-start.2) | collective-permute-done | bytes 57376 | tf_op jit(solution)/shard_map/ppermute | solution.py:34
  29.3 1.0 %collective-permute-start.4 = (f32[112,256]{1,0:T(8,128)S(1)}, f32[112,256]{1,0:T(8,128)S(1)}, u32[]{:S(2)}, u32[]{:S(2)}) collective-permute-start(f32[112,256]{1,0:T(8,128)S(1)} %add.28.near_ref), channel_id=1, source_target_pairs={{0,4},{4,0},{8,12},{12,8},{16,20},{20,16},{24,28},{28,24},{1,5},{5... | collective-permute-start | bytes 344072 | tf_op jit(solution)/shard_map/ppermute | solution.py:34
  30.3 1.0 %collective-permute-done.4.far_ref = f32[112,256]{1,0:T(8,128)S(1)} collective-permute-done((f32[112,256]{1,0:T(8,128)S(1)}, f32[112,256]{1,0:T(8,128)S(1)}, u32[]{:S(2)}, u32[]{:S(2)}) %collective-permute-start.4) | collective-permute-done | bytes 114720 | tf_op jit(solution)/shard_map/ppermute | solution.py:34
  31.3 2.2 %right_send.1 = (bf16[4,1,32,3072]{3,2,1,0:T(8,128)(2,1)S(1)}, bf16[256,192]{1,0:T(8,128)(2,1)S(1)}, bf16[8,192,224]{2,1,0:T(8,128)(2,1)S(1)}, f32[32,256]{1,0:T(8,128)S(1)}) custom-call(s32[8]{0:T(128)S(1)} %stack.34.pos, f32[112,256]{1,0:T(8,128)S(1)} %add.28.near_ref, f32[112,256]{1,0:T(8,128)S(1)} %collective-permute-done.4.far_ref, ...), custom_call_target="tpu_custom_call" | custom-call | flops 1000 | bytes 1000 | tf_op jit(solution)/shard_map/right_send/pallas_call | solution.py:173
  34.7 1.5 %right_keep.1.keep_ref = f32[4,1,32,3072]{3,2,1,0:T(8,128)S(1)} custom-call(s32[8]{0:T(128)S(1)} %stack.34.pos, bf16[256,192]{1,0:T(8,128)(2,1)S(1)} %get-tuple-element.38.lt_ref, bf16[8,192,3072]{2,1,0:T(8,128)(2,1)S(1)} %get-tuple-element.34.comp_ref, bf16[2,96,3072]{2,1,0:T(8,128)(2,1)S(1)} %collective-permute-done.5.refs_0_.refs_1_, ...), custom_call_target="tpu_custom_call" | custom-call | flops 9437184000 | bytes 1000 | tf_op jit(solution)/shard_map/right_keep/pallas_call | solution.py:192
  37.1 1.3 %collective-permute-start.8 = (bf16[40,3072]{1,0:T(8,128)(2,1)S(1)}, bf16[40,3072]{1,0:T(8,128)(2,1)S(1)}, u32[]{:S(2)}, u32[]{:S(2)}) collective-permute-start(bf16[40,3072]{1,0:T(8,128)(2,1)S(1)} %get-tuple-element.43), channel_id=1, source_target_pairs={{0,1},{1,0},{2,3},{3,2},{4,5},{5,4},{6,7},{7,6},{8,9},{9,8},{10,11... | collective-permute-start | bytes 737288 | tf_op jit(solution)/shard_map/ppermute | solution.py:34
  38.7 1.1 %collective-permute-start.10 = (bf16[40,3072]{1,0:T(8,128)(2,1)S(1)}, bf16[40,3072]{1,0:T(8,128)(2,1)S(1)}, u32[]{:S(2)}, u32[]{:S(2)}) collective-permute-start(bf16[40,3072]{1,0:T(8,128)(2,1)S(1)} %get-tuple-element.45), channel_id=1, source_target_pairs={{0,3},{1,2},{2,1},{3,0},{4,7},{5,6},{6,5},{7,4},{8,11},{9,10},{10,... | collective-permute-start | bytes 737288 | tf_op jit(solution)/shard_map/ppermute | solution.py:34
  39.8 2.9 %collective-permute-done.8.refs_0_ = bf16[40,3072]{1,0:T(8,128)(2,1)S(1)} collective-permute-done((bf16[40,3072]{1,0:T(8,128)(2,1)S(1)}, bf16[40,3072]{1,0:T(8,128)(2,1)S(1)}, u32[]{:S(2)}, u32[]{:S(2)}) %collective-permute-start.8) | collective-permute-done | bytes 245792 | tf_op jit(solution)/shard_map/ppermute | solution.py:34
  42.7 2.1 %collective-permute-done.9.refs_1_ = bf16[40,3072]{1,0:T(8,128)(2,1)S(1)} collective-permute-done((bf16[40,3072]{1,0:T(8,128)(2,1)S(1)}, bf16[40,3072]{1,0:T(8,128)(2,1)S(1)}, u32[]{:S(2)}, u32[]{:S(2)}) %collective-permute-start.9) | collective-permute-done | bytes 245792 | tf_op jit(solution)/shard_map/ppermute | solution.py:34
  44.8 3.6 %collective-permute-done.10.refs_2_ = bf16[40,3072]{1,0:T(8,128)(2,1)S(1)} collective-permute-done((bf16[40,3072]{1,0:T(8,128)(2,1)S(1)}, bf16[40,3072]{1,0:T(8,128)(2,1)S(1)}, u32[]{:S(2)}, u32[]{:S(2)}) %collective-permute-start.10) | collective-permute-done | bytes 245792 | tf_op jit(solution)/shard_map/ppermute | solution.py:34
  50.2 1.2 %collective-permute-start.18 = (bf16[1,96,3072]{2,1,0:T(8,128)(2,1)S(1)}, bf16[1,96,3072]{2,1,0:T(8,128)(2,1)S(1)}, u32[]{:S(2)}, u32[]{:S(2)}) collective-permute-start(bf16[1,96,3072]{2,1,0:T(8,128)(2,1)S(1)} %get-tuple-element.52), channel_id=1, source_target_pairs={{0,1},{1,0},{2,3},{3,2},{4,5},{5,4},{6,7},{7,6},{8,9},{9,8},{10,11... | collective-permute-start | bytes 1769480 | tf_op jit(solution)/shard_map/ppermute | solution.py:34
  51.4 1.3 %collective-permute-start.11 = (bf16[32,768]{1,0:T(8,128)(2,1)S(1)}, bf16[32,768]{1,0:T(8,128)(2,1)S(1)}, u32[]{:S(2)}, u32[]{:S(2)}) collective-permute-start(bf16[32,768]{1,0:T(8,128)(2,1)S(1)} %get-tuple-element.48), channel_id=1, source_target_pairs={{0,8},{4,12},{8,0},{12,4},{16,24},{20,28},{24,16},{28,20},{1,9},{5... | collective-permute-start | bytes 147464 | tf_op jit(solution)/shard_map/ppermute | solution.py:34
  52.7 2.3 %collective-permute-start.12 = (bf16[32,768]{1,0:T(8,128)(2,1)S(1)}, bf16[32,768]{1,0:T(8,128)(2,1)S(1)}, u32[]{:S(2)}, u32[]{:S(2)}) collective-permute-start(bf16[32,768]{1,0:T(8,128)(2,1)S(1)} %get-tuple-element.49), channel_id=1, source_target_pairs={{0,16},{4,20},{8,24},{12,28},{16,0},{20,4},{24,8},{28,12},{1,17},{... | collective-permute-start | bytes 147464 | tf_op jit(solution)/shard_map/ppermute | solution.py:34
  55.0 2.0 %collective-permute-done.12.refs_2_ = bf16[32,768]{1,0:T(8,128)(2,1)S(1)} collective-permute-done((bf16[32,768]{1,0:T(8,128)(2,1)S(1)}, bf16[32,768]{1,0:T(8,128)(2,1)S(1)}, u32[]{:S(2)}, u32[]{:S(2)}) %collective-permute-start.12) | collective-permute-done | bytes 49184 | tf_op jit(solution)/shard_map/ppermute | solution.py:34
  57.0 2.9 %collective-permute-done.13.refs_3_ = bf16[32,768]{1,0:T(8,128)(2,1)S(1)} collective-permute-done((bf16[32,768]{1,0:T(8,128)(2,1)S(1)}, bf16[32,768]{1,0:T(8,128)(2,1)S(1)}, u32[]{:S(2)}, u32[]{:S(2)}) %collective-permute-start.13) | collective-permute-done | bytes 49184 | tf_op jit(solution)/shard_map/ppermute | solution.py:34
  60.4 3.2 %collective-permute-start.14 = (bf16[32,768]{1,0:T(8,128)(2,1)S(1)}, bf16[32,768]{1,0:T(8,128)(2,1)S(1)}, u32[]{:S(2)}, u32[]{:S(2)}) collective-permute-start(bf16[32,768]{1,0:T(8,128)(2,1)S(1)} %add.29.refs_0_), channel_id=1, source_target_pairs={{0,8},{4,12},{8,0},{12,4},{16,24},{20,28},{24,16},{28,20},{1,9},{5... | collective-permute-start | bytes 147464 | tf_op jit(solution)/shard_map/ppermute | solution.py:34
  67.4 1.0 %collective-permute-start.19 = (bf16[4,32,768]{2,1,0:T(8,128)(2,1)S(1)}, bf16[4,32,768]{2,1,0:T(8,128)(2,1)S(1)}, u32[]{:S(2)}, u32[]{:S(2)}) collective-permute-start(bf16[4,32,768]{2,1,0:T(8,128)(2,1)S(1)} %stack.35.refs_0_), channel_id=1, source_target_pairs={{0,1},{1,0},{2,3},{3,2},{4,5},{5,4},{6,7},{7,6},{8,9},{9,8},{10,11... | collective-permute-start | bytes 589832 | tf_op jit(solution)/shard_map/ppermute | solution.py:34
  68.4 2.9 %collective-permute-done.21.refs_3_ = bf16[4,32,768]{2,1,0:T(8,128)(2,1)S(1)} collective-permute-done((bf16[4,32,768]{2,1,0:T(8,128)(2,1)S(1)}, bf16[4,32,768]{2,1,0:T(8,128)(2,1)S(1)}, u32[]{:S(2)}, u32[]{:S(2)}) %collective-permute-start.21) | collective-permute-done | bytes 196640 | tf_op jit(solution)/shard_map/ppermute | solution.py:34
  71.3 1.8 %collective-permute-done.20.refs_2_ = bf16[4,32,768]{2,1,0:T(8,128)(2,1)S(1)} collective-permute-done((bf16[4,32,768]{2,1,0:T(8,128)(2,1)S(1)}, bf16[4,32,768]{2,1,0:T(8,128)(2,1)S(1)}, u32[]{:S(2)}, u32[]{:S(2)}) %collective-permute-start.20) | collective-permute-done | bytes 196640 | tf_op jit(solution)/shard_map/ppermute | solution.py:34
  73.2 7.3 %collective-permute-start.22 = (bf16[4,1,4,32,768]{4,3,2,1,0:T(8,128)(2,1)S(1)}, bf16[4,1,4,32,768]{4,3,2,1,0:T(8,128)(2,1)S(1)}, u32[]{:S(2)}, u32[]{:S(2)}) collective-permute-start(bf16[4,1,4,32,768]{4,3,2,1,0:T(8,128)(2,1)S(1)} %bitcast.11), channel_id=1, source_target_pairs={{0,4},{4,0},{8,12},{12,8},{16,20},{20,16},{24,28},{28,24},{1,5},{5... | collective-permute-start | bytes 2359304 | tf_op jit(solution)/shard_map/ppermute | solution.py:34
  80.5 5.8 %outputs.2 = (bf16[1,8,192,3072]{3,2,1,0:T(8,128)(2,1)}, bf16[8,96,3072]{2,1,0:T(8,128)(2,1)}) custom-call(s32[8]{0:T(128)S(1)} %stack.34.pos, s32[8]{0:T(128)S(1)} %copy-done.7, bf16[8,192,3072]{2,1,0:T(8,128)(2,1)S(1)} %get-tuple-element.34.comp_ref, bf16[8,192,224]{2,1,0:T(8,128)(2,1)S(1)} %get-tuple-element.37.mix_ref, ...), custom_call_target="tpu_custom_call" | custom-call | flops 1000 | bytes 1000 | tf_op jit(solution)/shard_map/outputs/pallas_call | solution.py:451
  86.3 6.6 %outputs.3 = (bf16[1,8,192,3072]{3,2,1,0:T(8,128)(2,1)}, bf16[8,96,3072]{2,1,0:T(8,128)(2,1)}, f32[1,2,96,3072]{3,2,1,0:T(8,128)}, f32[1,2,96,3072]{3,2,1,0:T(8,128)}) custom-call(s32[8]{0:T(128)S(1)} %stack.34.pos, s32[8]{0:T(128)S(1)} %copy-done.7, ...), custom_call_target="tpu_custom_call", output_to_operand_aliasing={{0}: (14, {}), {1}: (15, {})} | custom-call | flops 1000 | bytes 1000 | tf_op jit(solution)/shard_map/outputs/pallas_call | solution.py:451
  (51 shorter events, 9.0 us)
Async XLA Ops:
  0.6 8.8 %copy-start.6 = (f32[1,2688]{1,0:T(1,128)S(1)}, f32[1,2688]{1,0:T(1,128)}, u32[]{:S(2)}) copy-start(f32[1,2688]{1,0:T(1,128)} %vec_ref.1) | copy-start | bytes 32260
  3.3 1.4 %copy-start = (f32[2,96,3072]{2,1,0:T(8,128)}, f32[2,96,3072]{2,1,0:T(8,128)S(1)}, u32[]{:S(2)}) copy-start(f32[2,96,3072]{2,1,0:T(8,128)S(1)} %get-tuple-element.54.refs_6_) | copy-start | bytes 7077892
  6.1 27.8 %collective-permute-start.6 = (bf16[2,96,3072]{2,1,0:T(8,128)(2,1)S(1)}, bf16[2,96,3072]{2,1,0:T(8,128)(2,1)S(1)}, u32[]{:S(2)}, u32[]{:S(2)}) collective-permute-start(bf16[2,96,3072]{2,1,0:T(8,128)(2,1)S(1)} %get-tuple-element.39.refs_0_), channel_id=1, source_target_pairs={{0,2},{1,3},{2,0},{3,1},{4,6},{5,7},{6,4},{7,5},{8,10},{9,11},{10,... | collective-permute-start | bytes 3538952 | tf_op jit(solution)/shard_map/ppermute | solution.py:34
  8.2 26.5 %collective-permute-start.5 = (bf16[2,96,3072]{2,1,0:T(8,128)(2,1)S(1)}, bf16[2,96,3072]{2,1,0:T(8,128)(2,1)S(1)}, u32[]{:S(2)}, u32[]{:S(2)}) collective-permute-start(bf16[2,96,3072]{2,1,0:T(8,128)(2,1)S(1)} %get-tuple-element.39.refs_0_), channel_id=1, source_target_pairs={{0,1},{1,0},{2,3},{3,2},{4,5},{5,4},{6,7},{7,6},{8,9},{9,8},{10,11... | collective-permute-start | bytes 3538952 | tf_op jit(solution)/shard_map/ppermute | solution.py:34
  9.5 21.8 %copy-start.4 = (f32[8,32,32]{2,1,0:T(8,128)S(1)}, f32[8,32,32]{2,1,0:T(8,128)}, u32[]{:S(2)}) copy-start(f32[8,32,32]{2,1,0:T(8,128)} %gram_ref.1) | copy-start | bytes 98308
  18.5 2.3 %collective-permute-start = (f32[112,256]{1,0:T(8,128)S(1)}, f32[112,256]{1,0:T(8,128)S(1)}, u32[]{:S(2)}, u32[]{:S(2)}) collective-permute-start(f32[112,256]{1,0:T(8,128)S(1)} %get-tuple-element.36), channel_id=1, source_target_pairs={{0,4},{4,0},{8,12},{12,8},{16,20},{20,16},{24,28},{28,24},{1,5},{5... | collective-permute-start | bytes 344072 | tf_op jit(solution)/shard_map/ppermute | solution.py:34
  20.8 5.1 %collective-permute-start.3 = (bf16[112,256]{1,0:T(8,128)(2,1)S(1)}, bf16[112,256]{1,0:T(8,128)(2,1)S(1)}, u32[]{:S(2)}, u32[]{:S(2)}) collective-permute-start(bf16[112,256]{1,0:T(8,128)(2,1)S(1)} %add.27.refs_0_), channel_id=1, source_target_pairs={{0,24},{4,28},{8,16},{12,20},{16,8},{20,12},{24,0},{28,4},{1,25},{... | collective-permute-start | bytes 172040 | tf_op jit(solution)/shard_map/ppermute | solution.py:34
  24.2 5.1 %collective-permute-start.2 = (bf16[112,256]{1,0:T(8,128)(2,1)S(1)}, bf16[112,256]{1,0:T(8,128)(2,1)S(1)}, u32[]{:S(2)}, u32[]{:S(2)}) collective-permute-start(bf16[112,256]{1,0:T(8,128)(2,1)S(1)} %add.27.refs_0_), channel_id=1, source_target_pairs={{0,16},{4,20},{8,24},{12,28},{16,0},{20,4},{24,8},{28,12},{1,17},{... | collective-permute-start | bytes 172040 | tf_op jit(solution)/shard_map/ppermute | solution.py:34
  24.2 5.1 %collective-permute-start.1 = (bf16[112,256]{1,0:T(8,128)(2,1)S(1)}, bf16[112,256]{1,0:T(8,128)(2,1)S(1)}, u32[]{:S(2)}, u32[]{:S(2)}) collective-permute-start(bf16[112,256]{1,0:T(8,128)(2,1)S(1)} %add.27.refs_0_), channel_id=1, source_target_pairs={{0,8},{4,12},{8,0},{12,4},{16,24},{20,28},{24,16},{28,20},{1,9},{5... | collective-permute-start | bytes 172040 | tf_op jit(solution)/shard_map/ppermute | solution.py:34
  29.3 2.0 %collective-permute-start.4 = (f32[112,256]{1,0:T(8,128)S(1)}, f32[112,256]{1,0:T(8,128)S(1)}, u32[]{:S(2)}, u32[]{:S(2)}) collective-permute-start(f32[112,256]{1,0:T(8,128)S(1)} %add.28.near_ref), channel_id=1, source_target_pairs={{0,4},{4,0},{8,12},{12,8},{16,20},{20,16},{24,28},{28,24},{1,5},{5... | collective-permute-start | bytes 344072 | tf_op jit(solution)/shard_map/ppermute | solution.py:34
  33.5 2.7 %collective-permute-start.7 = (bf16[4,1,32,3072]{3,2,1,0:T(8,128)(2,1)S(1)}, bf16[4,1,32,3072]{3,2,1,0:T(8,128)(2,1)S(1)}, u32[]{:S(2)}, u32[]{:S(2)}) collective-permute-start(bf16[4,1,32,3072]{3,2,1,0:T(8,128)(2,1)S(1)} %get-tuple-element.40), channel_id=1, source_target_pairs={{0,4},{4,0},{8,12},{12,8},{16,20},{20,16},{24,28},{28,24},{1,5},{5... | collective-permute-start | bytes 2359304 | tf_op jit(solution)/shard_map/ppermute | solution.py:34
  37.0 26.5 %copy-start.8 = (f32[2688]{0:T(1024)S(1)}, f32[2688]{0:T(1024)}, u32[]{:S(2)}) copy-start(f32[2688]{0:T(1024)} %param.19) | copy-start | bytes 32260
  37.1 26.5 %copy-start.9 = (f32[2688]{0:T(1024)S(1)}, f32[2688]{0:T(1024)}, u32[]{:S(2)}) copy-start(f32[2688]{0:T(1024)} %param.18) | copy-start | bytes 32260
  37.1 5.6 %collective-permute-start.8 = (bf16[40,3072]{1,0:T(8,128)(2,1)S(1)}, bf16[40,3072]{1,0:T(8,128)(2,1)S(1)}, u32[]{:S(2)}, u32[]{:S(2)}) collective-permute-start(bf16[40,3072]{1,0:T(8,128)(2,1)S(1)} %get-tuple-element.43), channel_id=1, source_target_pairs={{0,1},{1,0},{2,3},{3,2},{4,5},{5,4},{6,7},{7,6},{8,9},{9,8},{10,11... | collective-permute-start | bytes 737288 | tf_op jit(solution)/shard_map/ppermute | solution.py:34
  38.4 6.5 %collective-permute-start.9 = (bf16[40,3072]{1,0:T(8,128)(2,1)S(1)}, bf16[40,3072]{1,0:T(8,128)(2,1)S(1)}, u32[]{:S(2)}, u32[]{:S(2)}) collective-permute-start(bf16[40,3072]{1,0:T(8,128)(2,1)S(1)} %get-tuple-element.44), channel_id=1, source_target_pairs={{0,2},{1,3},{2,0},{3,1},{4,6},{5,7},{6,4},{7,5},{8,10},{9,11},{10,... | collective-permute-start | bytes 737288 | tf_op jit(solution)/shard_map/ppermute | solution.py:34
  38.7 9.7 %collective-permute-start.10 = (bf16[40,3072]{1,0:T(8,128)(2,1)S(1)}, bf16[40,3072]{1,0:T(8,128)(2,1)S(1)}, u32[]{:S(2)}, u32[]{:S(2)}) collective-permute-start(bf16[40,3072]{1,0:T(8,128)(2,1)S(1)} %get-tuple-element.45), channel_id=1, source_target_pairs={{0,3},{1,2},{2,1},{3,0},{4,7},{5,6},{6,5},{7,4},{8,11},{9,10},{10,... | collective-permute-start | bytes 737288 | tf_op jit(solution)/shard_map/ppermute | solution.py:34
  49.3 31.2 %copy-start.7 = (s32[8]{0:T(128)S(1)}, s32[8]{0:T(128)}, u32[]{:S(2)}) copy-start(s32[8]{0:T(128)} %owners.3) | copy-start | bytes 100
  49.3 16.4 %collective-permute-start.17 = (bf16[1,96,3072]{2,1,0:T(8,128)(2,1)S(1)}, bf16[1,96,3072]{2,1,0:T(8,128)(2,1)S(1)}, u32[]{:S(2)}, u32[]{:S(2)}) collective-permute-start(bf16[1,96,3072]{2,1,0:T(8,128)(2,1)S(1)} %get-tuple-element.51), channel_id=1, source_target_pairs={{0,2},{1,3},{2,0},{3,1},{4,6},{5,7},{6,4},{7,5},{8,10},{9,11},{10,... | collective-permute-start | bytes 1769480 | tf_op jit(solution)/shard_map/ppermute | solution.py:34
  50.2 15.5 %collective-permute-start.18 = (bf16[1,96,3072]{2,1,0:T(8,128)(2,1)S(1)}, bf16[1,96,3072]{2,1,0:T(8,128)(2,1)S(1)}, u32[]{:S(2)}, u32[]{:S(2)}) collective-permute-start(bf16[1,96,3072]{2,1,0:T(8,128)(2,1)S(1)} %get-tuple-element.52), channel_id=1, source_target_pairs={{0,1},{1,0},{2,3},{3,2},{4,5},{5,4},{6,7},{7,6},{8,9},{9,8},{10,11... | collective-permute-start | bytes 1769480 | tf_op jit(solution)/shard_map/ppermute | solution.py:34
  51.4 3.6 %collective-permute-start.11 = (bf16[32,768]{1,0:T(8,128)(2,1)S(1)}, bf16[32,768]{1,0:T(8,128)(2,1)S(1)}, u32[]{:S(2)}, u32[]{:S(2)}) collective-permute-start(bf16[32,768]{1,0:T(8,128)(2,1)S(1)} %get-tuple-element.48), channel_id=1, source_target_pairs={{0,8},{4,12},{8,0},{12,4},{16,24},{20,28},{24,16},{28,20},{1,9},{5... | collective-permute-start | bytes 147464 | tf_op jit(solution)/shard_map/ppermute | solution.py:34
  52.7 4.4 %collective-permute-start.12 = (bf16[32,768]{1,0:T(8,128)(2,1)S(1)}, bf16[32,768]{1,0:T(8,128)(2,1)S(1)}, u32[]{:S(2)}, u32[]{:S(2)}) collective-permute-start(bf16[32,768]{1,0:T(8,128)(2,1)S(1)} %get-tuple-element.49), channel_id=1, source_target_pairs={{0,16},{4,20},{8,24},{12,28},{16,0},{20,4},{24,8},{28,12},{1,17},{... | collective-permute-start | bytes 147464 | tf_op jit(solution)/shard_map/ppermute | solution.py:34
  55.0 4.9 %collective-permute-start.13 = (bf16[32,768]{1,0:T(8,128)(2,1)S(1)}, bf16[32,768]{1,0:T(8,128)(2,1)S(1)}, u32[]{:S(2)}, u32[]{:S(2)}) collective-permute-start(bf16[32,768]{1,0:T(8,128)(2,1)S(1)} %get-tuple-element.50), channel_id=1, source_target_pairs={{0,24},{4,28},{8,16},{12,20},{16,8},{20,12},{24,0},{28,4},{1,25},{... | collective-permute-start | bytes 147464 | tf_op jit(solution)/shard_map/ppermute | solution.py:34
  59.9 4.8 %collective-permute-start.16 = (bf16[32,768]{1,0:T(8,128)(2,1)S(1)}, bf16[32,768]{1,0:T(8,128)(2,1)S(1)}, u32[]{:S(2)}, u32[]{:S(2)}) collective-permute-start(bf16[32,768]{1,0:T(8,128)(2,1)S(1)} %add.29.refs_0_), channel_id=1, source_target_pairs={{0,24},{4,28},{8,16},{12,20},{16,8},{20,12},{24,0},{28,4},{1,25},{... | collective-permute-start | bytes 147464 | tf_op jit(solution)/shard_map/ppermute | solution.py:34
  60.4 5.3 %collective-permute-start.15 = (bf16[32,768]{1,0:T(8,128)(2,1)S(1)}, bf16[32,768]{1,0:T(8,128)(2,1)S(1)}, u32[]{:S(2)}, u32[]{:S(2)}) collective-permute-start(bf16[32,768]{1,0:T(8,128)(2,1)S(1)} %add.29.refs_0_), channel_id=1, source_target_pairs={{0,16},{4,20},{8,24},{12,28},{16,0},{20,4},{24,8},{28,12},{1,17},{... | collective-permute-start | bytes 147464 | tf_op jit(solution)/shard_map/ppermute | solution.py:34
  60.4 5.3 %collective-permute-start.14 = (bf16[32,768]{1,0:T(8,128)(2,1)S(1)}, bf16[32,768]{1,0:T(8,128)(2,1)S(1)}, u32[]{:S(2)}, u32[]{:S(2)}) collective-permute-start(bf16[32,768]{1,0:T(8,128)(2,1)S(1)} %add.29.refs_0_), channel_id=1, source_target_pairs={{0,8},{4,12},{8,0},{12,4},{16,24},{20,28},{24,16},{28,20},{1,9},{5... | collective-permute-start | bytes 147464 | tf_op jit(solution)/shard_map/ppermute | solution.py:34
  64.2 22.1 %copy-start.5 = (f32[2688]{0:T(1024)}, f32[2688]{0:T(1024)S(1)}, u32[]{:S(2)}) copy-start(f32[2688]{0:T(1024)S(1)} %get-tuple-element.62.refs_6_) | copy-start | bytes 32260
  65.7 5.6 %collective-permute-start.21 = (bf16[4,32,768]{2,1,0:T(8,128)(2,1)S(1)}, bf16[4,32,768]{2,1,0:T(8,128)(2,1)S(1)}, u32[]{:S(2)}, u32[]{:S(2)}) collective-permute-start(bf16[4,32,768]{2,1,0:T(8,128)(2,1)S(1)} %stack.35.refs_0_), channel_id=1, source_target_pairs={{0,3},{1,2},{2,1},{3,0},{4,7},{5,6},{6,5},{7,4},{8,11},{9,10},{10,... | collective-permute-start | bytes 589832 | tf_op jit(solution)/shard_map/ppermute | solution.py:34
  66.5 6.6 %collective-permute-start.20 = (bf16[4,32,768]{2,1,0:T(8,128)(2,1)S(1)}, bf16[4,32,768]{2,1,0:T(8,128)(2,1)S(1)}, u32[]{:S(2)}, u32[]{:S(2)}) collective-permute-start(bf16[4,32,768]{2,1,0:T(8,128)(2,1)S(1)} %stack.35.refs_0_), channel_id=1, source_target_pairs={{0,2},{1,3},{2,0},{3,1},{4,6},{5,7},{6,4},{7,5},{8,10},{9,11},{10,... | collective-permute-start | bytes 589832 | tf_op jit(solution)/shard_map/ppermute | solution.py:34
  67.4 5.7 %collective-permute-start.19 = (bf16[4,32,768]{2,1,0:T(8,128)(2,1)S(1)}, bf16[4,32,768]{2,1,0:T(8,128)(2,1)S(1)}, u32[]{:S(2)}, u32[]{:S(2)}) collective-permute-start(bf16[4,32,768]{2,1,0:T(8,128)(2,1)S(1)} %stack.35.refs_0_), channel_id=1, source_target_pairs={{0,1},{1,0},{2,3},{3,2},{4,5},{5,4},{6,7},{7,6},{8,9},{9,8},{10,11... | collective-permute-start | bytes 589832 | tf_op jit(solution)/shard_map/ppermute | solution.py:34
  73.2 13.1 %collective-permute-start.22 = (bf16[4,1,4,32,768]{4,3,2,1,0:T(8,128)(2,1)S(1)}, bf16[4,1,4,32,768]{4,3,2,1,0:T(8,128)(2,1)S(1)}, u32[]{:S(2)}, u32[]{:S(2)}) collective-permute-start(bf16[4,1,4,32,768]{4,3,2,1,0:T(8,128)(2,1)S(1)} %bitcast.11), channel_id=1, source_target_pairs={{0,4},{4,0},{8,12},{12,8},{16,20},{20,16},{24,28},{28,24},{1,5},{5... | collective-permute-start | bytes 2359304 | tf_op jit(solution)/shard_map/ppermute | solution.py:34
  80.5 5.8 %copy-start.1 = (f32[2,96,3072]{2,1,0:T(8,128)S(1)}, f32[2,96,3072]{2,1,0:T(8,128)}, u32[]{:S(2)}) copy-start(f32[2,96,3072]{2,1,0:T(8,128)} %copy-done) | copy-start | bytes 7077892
  80.5 5.8 %copy-start.3 = (f32[2,96,3072]{2,1,0:T(8,128)S(1)}, f32[2,96,3072]{2,1,0:T(8,128)}, u32[]{:S(2)}) copy-start(f32[2,96,3072]{2,1,0:T(8,128)} %copy-done.2) | copy-start | bytes 7077892
  (1 other events, 1.4 us)

commit v9 on v8

--- a/solution.py
+++ b/solution.py
@@ -199,7 +199,7 @@
         ),
         out_shape=jax.ShapeDtypeStruct(shape, F32),
         compiler_params=params(),
-        cost_estimate=cost(2000 * nmat * rows * n),
+        cost_estimate=cost(),
         name="right_keep",
     )(pos, lt, comp, *after)
     return send, keep, lt, mix, vec
@@ -307,6 +307,22 @@
         cost_estimate=cost(),
         name="stack",
     )(*parts, *after)
+
+
+def token_kernel(*refs):
+    refs[-1][...] = jnp.zeros(refs[-1].shape, F32)
+
+
+def token(after):
+    return pl.pallas_call(
+        token_kernel,
+        in_specs=[pl.BlockSpec(memory_space=pl.ANY)] * len(after),
+        out_specs=pl.BlockSpec(memory_space=pltpu.VMEM),
+        out_shape=jax.ShapeDtypeStruct((8, 128), F32),
+        compiler_params=params(),
+        cost_estimate=cost(),
+        name="token",
+    )(*after)
 
 
 def forward_kernel(cuts, *refs):
@@ -468,7 +484,7 @@
     )(pos, owners, comp, mix, mixr, near, *bases, *fars, *states, *earlier)
 
 
-def base_kernel(momentum_ref, master_ref, *refs):
+def base_kernel(pos, momentum_ref, master_ref, *refs):
     out_ref, momentum, master, sems = refs
     capacity, rows, _ = out_ref.shape
     blocks = [(c, first) for c in range(capacity) for first in range(0, rows, BASE_ROWS)]
@@ -491,19 +507,23 @@
         out_ref[c, part] = (master[c, part] - 0.09 * momentum[c, part]).astype(BF16)
 
 
-def base_of(momentum, master):
+def base_of(pos, momentum, master):
     _, capacity, rows, n = momentum.shape
     state = jax.ShapeDtypeStruct((capacity, rows, n), F32)
     base, momentum, master = pl.pallas_call(
         base_kernel,
-        in_specs=[pl.BlockSpec(memory_space=pl.ANY)] * 2,
-        out_specs=[pl.BlockSpec(memory_space=pltpu.VMEM)] * 3,
+        grid_spec=pltpu.PrefetchScalarGridSpec(
+            num_scalar_prefetch=1,
+            grid=(1,),
+            in_specs=[pl.BlockSpec(memory_space=pl.ANY)] * 2,
+            out_specs=[pl.BlockSpec(memory_space=pltpu.VMEM)] * 3,
+            scratch_shapes=[pltpu.SemaphoreType.DMA((2, capacity * rows // BASE_ROWS))],
+        ),
         out_shape=[jax.ShapeDtypeStruct((capacity, rows, n), BF16), state, state],
-        scratch_shapes=[pltpu.SemaphoreType.DMA((2, capacity * rows // BASE_ROWS))],
         compiler_params=params(),
         cost_estimate=cost(),
         name="base",
-    )(momentum, master)
+    )(pos, momentum, master)
     return base, (momentum, master)
 
 
@@ -538,7 +558,7 @@
     in_hbm = lambda x: pltpu.with_memory_space_constraint(x, pltpu.HBM)
 
     square = n_mp == 4 and capacity == 2
-    base, states = base_of(in_hbm(momentum), in_hbm(master_weights))
+    base, states = base_of(pos, in_hbm(momentum), in_hbm(master_weights))
     early = [exchange(base, "mp", d) for d in range(1, 3 if square else n_mp)]
     bases = [base] + early
     places = {(d, c): (d, c) for d in range(len(bases)) for c in range(capacity)}
@@ -552,15 +572,14 @@
         vector_grads,
     )
     piece = add([near, exchange(far, "replica", 1)], BF16)
-    piece = add([near, exchange(far, "replica", 1)], BF16)
     along_z = lambda x: [exchange(x, "replica", CORES * d) for d in range(1, n_z)]
     piece = add([piece] + along_z(piece), F32)
     near, far = piece, exchange(piece, "replica", 1)
 
-    send, keep, lt, mix, vector_rows = right_terms(pos, near, far, gram_root, comp, upm, early)
+    send, keep, lt, mix, vector_rows = right_terms(pos, near, far, gram_root, comp, upm, [])
     vector_total = vector_rows.reshape(-1)[:nvec]
     recv = exchange(send, "replica", 1)
-    own, strip, *chip = chip_sum(pos, keep, recv, lt, replica_rows, [])
+    own, strip, *chip = chip_sum(pos, keep, recv, lt, replica_rows, [token([keep] + early)])
     plane = [exchange(part, "mp", d) for d, part in enumerate(chip, 1)]
     *final, mixr = plane_sum(pos, own, strip, plane, n_z, nmat, rank)
     late = []

time: 93.2 us -> 89.6 us (0.961)
  local copies, waits for them, and re-layouts: 2.94 us -> 0.13 us
  starting transfers between devices: 31.7 us -> 30.6 us
    unnamed x21 -> x13, local copies, waits for them, and re-layouts: 2.86 us -> 0.05 us
    ppermute x23, starting transfers between devices: 31.7 us -> 30.6 us  [exchange(): return lax.ppermute(x, axis, [(i, i ^ distance) for i in range(size)])]
    pallas_call x1 -> x2, Pallas kernels: 2.65 us -> 3.19 us  [the longest x1 3.18 us: base_of(): pl.pallas_call(base_kernel, grid_spec=pltpu.PrefetchScalarGridSpec(num_sc...]
  transfers between devices with their start and end apart: 23 -> 23, of which waited for: 14 -> 13; matrix products, arithmetic and copies ran while one was open for 1% -> 1% of each run, Pallas kernels for 20% -> 21%
where the time goes in v9:
time: 89.6 us; the launch traced here: 89.4 us
  starting transfers between devices  30.6 us (34%)
  Pallas kernels  30.2 us (34%)
  waiting for transfers between devices  26.9 us (30%)
  between operations  1.03 us (1%)
    ppermute x23, starting transfers between devices, exchange(): return lax.ppermute(x, axis, [(i, i ^ distance) for i in range(size)])  30.6 us
    ppermute x23, waiting for transfers between devices, exchange(): return lax.ppermute(x, axis, [(i, i ^ distance) for i in range(size)])  26.9 us
    pallas_call x2, Pallas kernels, outputs(): pl.pallas_call(functools.partial(outputs_kernel, second, places), grid_sp...  12.4 us
    pallas_call x1, Pallas kernels, left_terms(): pl.pallas_call(left_kernel, grid_spec=pltpu.PrefetchScalarGridSpec(num_sc...  9 us
    pallas_call x1, Pallas kernels, base_of(): pl.pallas_call(base_kernel, grid_spec=pltpu.PrefetchScalarGridSpec(num_sc...  3.18 us
    pallas_call x1, Pallas kernels, right_terms(): pl.pallas_call(functools.partial(send_kernel, half), grid_spec=pltpu.Pref...  2.22 us
  transfers between devices with their start and end apart: 23, of which 13 were waited for; matrix products, arithmetic and copies ran while one was open for 1% of the time, Pallas kernels for 21%

profile of v9, /device:TPU:1, one launch (start us, length us, event | category | flops | bytes accessed | tf_op | source)
XLA Modules:
  0.0 89.4 jit_solution(9313269567607722190)
XLA Ops:
  0.8 3.2 %base.1 = (bf16[2,96,3072]{2,1,0:T(8,128)(2,1)S(1)}, f32[2,96,3072]{2,1,0:T(8,128)S(1)}, f32[2,96,3072]{2,1,0:T(8,128)S(1)}) custom-call(s32[8]{0:T(128)S(1)} %stack.34.pos, f32[1,2,96,3072]{3,2,1,0:T(8,128)} %momentum_ref.1, f32[1,2,96,3072]{3,2,1,0:T(8,128)} %master_ref.1), custom_call_target="tpu_custom_call" | custom-call | flops 1000 | bytes 1000 | tf_op jit(solution)/shard_map/base/pallas_call | solution.py:513
  4.0 2.1 %collective-permute-start.7 = (bf16[2,96,3072]{2,1,0:T(8,128)(2,1)S(1)}, bf16[2,96,3072]{2,1,0:T(8,128)(2,1)S(1)}, u32[]{:S(2)}, u32[]{:S(2)}) collective-permute-start(bf16[2,96,3072]{2,1,0:T(8,128)(2,1)S(1)} %get-tuple-element.40.refs_0_), channel_id=1, source_target_pairs={{0,2},{1,3},{2,0},{3,1},{4,6},{5,7},{6,4},{7,5},{8,10},{9,11},{10,... | collective-permute-start | bytes 3538952 | tf_op jit(solution)/shard_map/ppermute | solution.py:34
  6.1 1.2 %collective-permute-start.6 = (bf16[2,96,3072]{2,1,0:T(8,128)(2,1)S(1)}, bf16[2,96,3072]{2,1,0:T(8,128)(2,1)S(1)}, u32[]{:S(2)}, u32[]{:S(2)}) collective-permute-start(bf16[2,96,3072]{2,1,0:T(8,128)(2,1)S(1)} %get-tuple-element.40.refs_0_), channel_id=1, source_target_pairs={{0,1},{1,0},{2,3},{3,2},{4,5},{5,4},{6,7},{7,6},{8,9},{9,8},{10,11... | collective-permute-start | bytes 3538952 | tf_op jit(solution)/shard_map/ppermute | solution.py:34
  7.3 9.0 %left_terms.1 = (bf16[8,192,3072]{2,1,0:T(8,128)(2,1)S(1)}, f32[112,256]{1,0:T(8,128)S(1)}, f32[112,256]{1,0:T(8,128)S(1)}) custom-call(s32[8]{0:T(128)S(1)} %stack.34.pos, bf16[1,8,192,3072]{3,2,1,0:T(8,128)(2,1)} %g_ref.1, bf16[1,8,192,3072]{3,2,1,0:T(8,128)(2,1)} %f_ref.1, bf16[8,32,3072]{2,1,0:T(8,128)(2,1)} %bitcast.15, f32[1,2688]{1,0:T(1,128)S(1)} %copy-done.2), custom_call_target="tpu_custom_call" | custom-call | flops 1000 | bytes 1000 | tf_op jit(solution)/shard_map/left_terms/pallas_call | solution.py:86
  16.3 1.3 %collective-permute-start = (f32[112,256]{1,0:T(8,128)S(1)}, f32[112,256]{1,0:T(8,128)S(1)}, u32[]{:S(2)}, u32[]{:S(2)}) collective-permute-start(f32[112,256]{1,0:T(8,128)S(1)} %get-tuple-element.36), channel_id=1, source_target_pairs={{0,4},{4,0},{8,12},{12,8},{16,20},{20,16},{24,28},{28,24},{1,5},{5... | collective-permute-start | bytes 344072 | tf_op jit(solution)/shard_map/ppermute | solution.py:34
  17.6 1.0 %collective-permute-done.refs_1_ = f32[112,256]{1,0:T(8,128)S(1)} collective-permute-done((f32[112,256]{1,0:T(8,128)S(1)}, f32[112,256]{1,0:T(8,128)S(1)}, u32[]{:S(2)}, u32[]{:S(2)}) %collective-permute-start) | collective-permute-done | bytes 114720 | tf_op jit(solution)/shard_map/ppermute | solution.py:34
  18.6 3.4 %collective-permute-start.3 = (bf16[112,256]{1,0:T(8,128)(2,1)S(1)}, bf16[112,256]{1,0:T(8,128)(2,1)S(1)}, u32[]{:S(2)}, u32[]{:S(2)}) collective-permute-start(bf16[112,256]{1,0:T(8,128)(2,1)S(1)} %add.27.refs_0_), channel_id=1, source_target_pairs={{0,24},{4,28},{8,16},{12,20},{16,8},{20,12},{24,0},{28,4},{1,25},{... | collective-permute-start | bytes 172040 | tf_op jit(solution)/shard_map/ppermute | solution.py:34
  22.4 1.3 %collective-permute-done.3.refs_3_ = bf16[112,256]{1,0:T(8,128)(2,1)S(1)} collective-permute-done((bf16[112,256]{1,0:T(8,128)(2,1)S(1)}, bf16[112,256]{1,0:T(8,128)(2,1)S(1)}, u32[]{:S(2)}, u32[]{:S(2)}) %collective-permute-start.3) | collective-permute-done | bytes 57376 | tf_op jit(solution)/shard_map/ppermute | solution.py:34
  23.7 3.4 %collective-permute-done.2.refs_2_ = bf16[112,256]{1,0:T(8,128)(2,1)S(1)} collective-permute-done((bf16[112,256]{1,0:T(8,128)(2,1)S(1)}, bf16[112,256]{1,0:T(8,128)(2,1)S(1)}, u32[]{:S(2)}, u32[]{:S(2)}) %collective-permute-start.2) | collective-permute-done | bytes 57376 | tf_op jit(solution)/shard_map/ppermute | solution.py:34
  27.1 1.0 %collective-permute-start.4 = (f32[112,256]{1,0:T(8,128)S(1)}, f32[112,256]{1,0:T(8,128)S(1)}, u32[]{:S(2)}, u32[]{:S(2)}) collective-permute-start(f32[112,256]{1,0:T(8,128)S(1)} %add.28.near_ref), channel_id=1, source_target_pairs={{0,4},{4,0},{8,12},{12,8},{16,20},{20,16},{24,28},{28,24},{1,5},{5... | collective-permute-start | bytes 344072 | tf_op jit(solution)/shard_map/ppermute | solution.py:34
  28.1 1.0 %collective-permute-done.4.far_ref = f32[112,256]{1,0:T(8,128)S(1)} collective-permute-done((f32[112,256]{1,0:T(8,128)S(1)}, f32[112,256]{1,0:T(8,128)S(1)}, u32[]{:S(2)}, u32[]{:S(2)}) %collective-permute-start.4) | collective-permute-done | bytes 114720 | tf_op jit(solution)/shard_map/ppermute | solution.py:34
  29.1 2.2 %right_send.1 = (bf16[4,1,32,3072]{3,2,1,0:T(8,128)(2,1)S(1)}, bf16[256,192]{1,0:T(8,128)(2,1)S(1)}, bf16[8,192,224]{2,1,0:T(8,128)(2,1)S(1)}, f32[32,256]{1,0:T(8,128)S(1)}) custom-call(s32[8]{0:T(128)S(1)} %stack.34.pos, f32[112,256]{1,0:T(8,128)S(1)} %add.28.near_ref, f32[112,256]{1,0:T(8,128)S(1)} %collective-permute-done.4.far_ref, ...), custom_call_target="tpu_custom_call" | custom-call | flops 1000 | bytes 1000 | tf_op jit(solution)/shard_map/right_send/pallas_call | solution.py:173
  31.8 1.5 %right_keep.1.refs_0_.keep_ref = f32[4,1,32,3072]{3,2,1,0:T(8,128)S(1)} custom-call(s32[8]{0:T(128)S(1)} %stack.34.pos, bf16[256,192]{1,0:T(8,128)(2,1)S(1)} %get-tuple-element.38.lt_ref, bf16[8,192,3072]{2,1,0:T(8,128)(2,1)S(1)} %get-tuple-element.34.comp_ref), custom_call_target="tpu_custom_call" | custom-call | flops 1000 | bytes 1000 | tf_op jit(solution)/shard_map/right_keep/pallas_call | solution.py:192
  33.7 0.8 chip_sum.1
  35.1 2.2 %collective-permute-start.10 = (bf16[40,3072]{1,0:T(8,128)(2,1)S(1)}, bf16[40,3072]{1,0:T(8,128)(2,1)S(1)}, u32[]{:S(2)}, u32[]{:S(2)}) collective-permute-start(bf16[40,3072]{1,0:T(8,128)(2,1)S(1)} %get-tuple-element.45), channel_id=1, source_target_pairs={{0,3},{1,2},{2,1},{3,0},{4,7},{5,6},{6,5},{7,4},{8,11},{9,10},{10,... | collective-permute-start | bytes 737288 | tf_op jit(solution)/shard_map/ppermute | solution.py:34
  37.2 4.0 %collective-permute-done.8.refs_0_ = bf16[40,3072]{1,0:T(8,128)(2,1)S(1)} collective-permute-done((bf16[40,3072]{1,0:T(8,128)(2,1)S(1)}, bf16[40,3072]{1,0:T(8,128)(2,1)S(1)}, u32[]{:S(2)}, u32[]{:S(2)}) %collective-permute-start.8) | collective-permute-done | bytes 245792 | tf_op jit(solution)/shard_map/ppermute | solution.py:34
  41.2 5.4 %collective-permute-done.10.refs_2_ = bf16[40,3072]{1,0:T(8,128)(2,1)S(1)} collective-permute-done((bf16[40,3072]{1,0:T(8,128)(2,1)S(1)}, bf16[40,3072]{1,0:T(8,128)(2,1)S(1)}, u32[]{:S(2)}, u32[]{:S(2)}) %collective-permute-start.10) | collective-permute-done | bytes 245792 | tf_op jit(solution)/shard_map/ppermute | solution.py:34
  46.7 0.8 plane_sum.1
  47.6 1.1 %collective-permute-start.17 = (bf16[1,96,3072]{2,1,0:T(8,128)(2,1)S(1)}, bf16[1,96,3072]{2,1,0:T(8,128)(2,1)S(1)}, u32[]{:S(2)}, u32[]{:S(2)}) collective-permute-start(bf16[1,96,3072]{2,1,0:T(8,128)(2,1)S(1)} %get-tuple-element.51), channel_id=1, source_target_pairs={{0,2},{1,3},{2,0},{3,1},{4,6},{5,7},{6,4},{7,5},{8,10},{9,11},{10,... | collective-permute-start | bytes 1769480 | tf_op jit(solution)/shard_map/ppermute | solution.py:34
  49.1 2.3 %collective-permute-start.12 = (bf16[32,768]{1,0:T(8,128)(2,1)S(1)}, bf16[32,768]{1,0:T(8,128)(2,1)S(1)}, u32[]{:S(2)}, u32[]{:S(2)}) collective-permute-start(bf16[32,768]{1,0:T(8,128)(2,1)S(1)} %get-tuple-element.49), channel_id=1, source_target_pairs={{0,16},{4,20},{8,24},{12,28},{16,0},{20,4},{24,8},{28,12},{1,17},{... | collective-permute-start | bytes 147464 | tf_op jit(solution)/shard_map/ppermute | solution.py:34
  51.4 0.8 collective-permute-start.13
  52.9 3.4 %collective-permute-done.13.refs_3_ = bf16[32,768]{1,0:T(8,128)(2,1)S(1)} collective-permute-done((bf16[32,768]{1,0:T(8,128)(2,1)S(1)}, bf16[32,768]{1,0:T(8,128)(2,1)S(1)}, u32[]{:S(2)}, u32[]{:S(2)}) %collective-permute-start.13) | collective-permute-done | bytes 49184 | tf_op jit(solution)/shard_map/ppermute | solution.py:34
  56.3 0.7 collective-permute-start.16
  57.1 2.9 %collective-permute-start.14 = (bf16[32,768]{1,0:T(8,128)(2,1)S(1)}, bf16[32,768]{1,0:T(8,128)(2,1)S(1)}, u32[]{:S(2)}, u32[]{:S(2)}) collective-permute-start(bf16[32,768]{1,0:T(8,128)(2,1)S(1)} %add.29.refs_0_), channel_id=1, source_target_pairs={{0,8},{4,12},{8,0},{12,4},{16,24},{20,28},{24,16},{28,20},{1,9},{5... | collective-permute-start | bytes 147464 | tf_op jit(solution)/shard_map/ppermute | solution.py:34
  61.2 0.9 %collective-permute-done.15.refs_2_ = bf16[32,768]{1,0:T(8,128)(2,1)S(1)} collective-permute-done((bf16[32,768]{1,0:T(8,128)(2,1)S(1)}, bf16[32,768]{1,0:T(8,128)(2,1)S(1)}, u32[]{:S(2)}, u32[]{:S(2)}) %collective-permute-start.15) | collective-permute-done | bytes 49184 | tf_op jit(solution)/shard_map/ppermute | solution.py:34
  62.1 1.0 %collective-permute-start.21 = (bf16[4,32,768]{2,1,0:T(8,128)(2,1)S(1)}, bf16[4,32,768]{2,1,0:T(8,128)(2,1)S(1)}, u32[]{:S(2)}, u32[]{:S(2)}) collective-permute-start(bf16[4,32,768]{2,1,0:T(8,128)(2,1)S(1)} %stack.35.refs_0_), channel_id=1, source_target_pairs={{0,3},{1,2},{2,1},{3,0},{4,7},{5,6},{6,5},{7,4},{8,11},{9,10},{10,... | collective-permute-start | bytes 589832 | tf_op jit(solution)/shard_map/ppermute | solution.py:34
  63.1 1.1 %collective-permute-start.20 = (bf16[4,32,768]{2,1,0:T(8,128)(2,1)S(1)}, bf16[4,32,768]{2,1,0:T(8,128)(2,1)S(1)}, u32[]{:S(2)}, u32[]{:S(2)}) collective-permute-start(bf16[4,32,768]{2,1,0:T(8,128)(2,1)S(1)} %stack.35.refs_0_), channel_id=1, source_target_pairs={{0,2},{1,3},{2,0},{3,1},{4,6},{5,7},{6,4},{7,5},{8,10},{9,11},{10,... | collective-permute-start | bytes 589832 | tf_op jit(solution)/shard_map/ppermute | solution.py:34
  64.8 2.9 %collective-permute-done.21.refs_3_ = bf16[4,32,768]{2,1,0:T(8,128)(2,1)S(1)} collective-permute-done((bf16[4,32,768]{2,1,0:T(8,128)(2,1)S(1)}, bf16[4,32,768]{2,1,0:T(8,128)(2,1)S(1)}, u32[]{:S(2)}, u32[]{:S(2)}) %collective-permute-start.21) | collective-permute-done | bytes 196640 | tf_op jit(solution)/shard_map/ppermute | solution.py:34
  67.7 2.0 %collective-permute-done.20.refs_2_ = bf16[4,32,768]{2,1,0:T(8,128)(2,1)S(1)} collective-permute-done((bf16[4,32,768]{2,1,0:T(8,128)(2,1)S(1)}, bf16[4,32,768]{2,1,0:T(8,128)(2,1)S(1)}, u32[]{:S(2)}, u32[]{:S(2)}) %collective-permute-start.20) | collective-permute-done | bytes 196640 | tf_op jit(solution)/shard_map/ppermute | solution.py:34
  69.8 7.1 %collective-permute-start.22 = (bf16[4,1,4,32,768]{4,3,2,1,0:T(8,128)(2,1)S(1)}, bf16[4,1,4,32,768]{4,3,2,1,0:T(8,128)(2,1)S(1)}, u32[]{:S(2)}, u32[]{:S(2)}) collective-permute-start(bf16[4,1,4,32,768]{4,3,2,1,0:T(8,128)(2,1)S(1)} %bitcast.11), channel_id=1, source_target_pairs={{0,4},{4,0},{8,12},{12,8},{16,20},{20,16},{24,28},{28,24},{1,5},{5... | collective-permute-start | bytes 2359304 | tf_op jit(solution)/shard_map/ppermute | solution.py:34
  76.9 5.8 %outputs.2 = (bf16[1,8,192,3072]{3,2,1,0:T(8,128)(2,1)}, bf16[8,96,3072]{2,1,0:T(8,128)(2,1)}) custom-call(s32[8]{0:T(128)S(1)} %stack.34.pos, s32[8]{0:T(128)S(1)} %copy-done.3, bf16[8,192,3072]{2,1,0:T(8,128)(2,1)S(1)} %get-tuple-element.34.comp_ref, bf16[8,192,224]{2,1,0:T(8,128)(2,1)S(1)} %get-tuple-element.37.mix_ref, ...), custom_call_target="tpu_custom_call" | custom-call | flops 1000 | bytes 1000 | tf_op jit(solution)/shard_map/outputs/pallas_call | solution.py:467
  82.6 6.6 %outputs.3 = (bf16[1,8,192,3072]{3,2,1,0:T(8,128)(2,1)}, bf16[8,96,3072]{2,1,0:T(8,128)(2,1)}, f32[1,2,96,3072]{3,2,1,0:T(8,128)}, f32[1,2,96,3072]{3,2,1,0:T(8,128)}) custom-call(s32[8]{0:T(128)S(1)} %stack.34.pos, s32[8]{0:T(128)S(1)} %copy-done.3, ...), custom_call_target="tpu_custom_call", output_to_operand_aliasing={{0}: (14, {}), {1}: (15, {})} | custom-call | flops 1000 | bytes 1000 | tf_op jit(solution)/shard_map/outputs/pallas_call | solution.py:467
  (44 shorter events, 5.0 us)
Async XLA Ops:
  0.8 6.5 %copy-start.2 = (f32[1,2688]{1,0:T(1,128)S(1)}, f32[1,2688]{1,0:T(1,128)}, u32[]{:S(2)}) copy-start(f32[1,2688]{1,0:T(1,128)} %vec_ref.1) | copy-start | bytes 32260
  4.0 29.3 %collective-permute-start.7 = (bf16[2,96,3072]{2,1,0:T(8,128)(2,1)S(1)}, bf16[2,96,3072]{2,1,0:T(8,128)(2,1)S(1)}, u32[]{:S(2)}, u32[]{:S(2)}) collective-permute-start(bf16[2,96,3072]{2,1,0:T(8,128)(2,1)S(1)} %get-tuple-element.40.refs_0_), channel_id=1, source_target_pairs={{0,2},{1,3},{2,0},{3,1},{4,6},{5,7},{6,4},{7,5},{8,10},{9,11},{10,... | collective-permute-start | bytes 3538952 | tf_op jit(solution)/shard_map/ppermute | solution.py:34
  6.1 27.2 %collective-permute-start.6 = (bf16[2,96,3072]{2,1,0:T(8,128)(2,1)S(1)}, bf16[2,96,3072]{2,1,0:T(8,128)(2,1)S(1)}, u32[]{:S(2)}, u32[]{:S(2)}) collective-permute-start(bf16[2,96,3072]{2,1,0:T(8,128)(2,1)S(1)} %get-tuple-element.40.refs_0_), channel_id=1, source_target_pairs={{0,1},{1,0},{2,3},{3,2},{4,5},{5,4},{6,7},{7,6},{8,9},{9,8},{10,11... | collective-permute-start | bytes 3538952 | tf_op jit(solution)/shard_map/ppermute | solution.py:34
  7.3 21.8 %copy-start = (f32[8,32,32]{2,1,0:T(8,128)S(1)}, f32[8,32,32]{2,1,0:T(8,128)}, u32[]{:S(2)}) copy-start(f32[8,32,32]{2,1,0:T(8,128)} %gram_ref.1) | copy-start | bytes 98308
  16.3 2.3 %collective-permute-start = (f32[112,256]{1,0:T(8,128)S(1)}, f32[112,256]{1,0:T(8,128)S(1)}, u32[]{:S(2)}, u32[]{:S(2)}) collective-permute-start(f32[112,256]{1,0:T(8,128)S(1)} %get-tuple-element.36), channel_id=1, source_target_pairs={{0,4},{4,0},{8,12},{12,8},{16,20},{20,16},{24,28},{28,24},{1,5},{5... | collective-permute-start | bytes 344072 | tf_op jit(solution)/shard_map/ppermute | solution.py:34
  18.6 5.1 %collective-permute-start.3 = (bf16[112,256]{1,0:T(8,128)(2,1)S(1)}, bf16[112,256]{1,0:T(8,128)(2,1)S(1)}, u32[]{:S(2)}, u32[]{:S(2)}) collective-permute-start(bf16[112,256]{1,0:T(8,128)(2,1)S(1)} %add.27.refs_0_), channel_id=1, source_target_pairs={{0,24},{4,28},{8,16},{12,20},{16,8},{20,12},{24,0},{28,4},{1,25},{... | collective-permute-start | bytes 172040 | tf_op jit(solution)/shard_map/ppermute | solution.py:34
  22.0 5.1 %collective-permute-start.2 = (bf16[112,256]{1,0:T(8,128)(2,1)S(1)}, bf16[112,256]{1,0:T(8,128)(2,1)S(1)}, u32[]{:S(2)}, u32[]{:S(2)}) collective-permute-start(bf16[112,256]{1,0:T(8,128)(2,1)S(1)} %add.27.refs_0_), channel_id=1, source_target_pairs={{0,16},{4,20},{8,24},{12,28},{16,0},{20,4},{24,8},{28,12},{1,17},{... | collective-permute-start | bytes 172040 | tf_op jit(solution)/shard_map/ppermute | solution.py:34
  22.0 5.1 %collective-permute-start.1 = (bf16[112,256]{1,0:T(8,128)(2,1)S(1)}, bf16[112,256]{1,0:T(8,128)(2,1)S(1)}, u32[]{:S(2)}, u32[]{:S(2)}) collective-permute-start(bf16[112,256]{1,0:T(8,128)(2,1)S(1)} %add.27.refs_0_), channel_id=1, source_target_pairs={{0,8},{4,12},{8,0},{12,4},{16,24},{20,28},{24,16},{28,20},{1,9},{5... | collective-permute-start | bytes 172040 | tf_op jit(solution)/shard_map/ppermute | solution.py:34
  27.1 2.0 %collective-permute-start.4 = (f32[112,256]{1,0:T(8,128)S(1)}, f32[112,256]{1,0:T(8,128)S(1)}, u32[]{:S(2)}, u32[]{:S(2)}) collective-permute-start(f32[112,256]{1,0:T(8,128)S(1)} %add.28.near_ref), channel_id=1, source_target_pairs={{0,4},{4,0},{8,12},{12,8},{16,20},{20,16},{24,28},{28,24},{1,5},{5... | collective-permute-start | bytes 344072 | tf_op jit(solution)/shard_map/ppermute | solution.py:34
  31.3 2.4 %collective-permute-start.5 = (bf16[4,1,32,3072]{3,2,1,0:T(8,128)(2,1)S(1)}, bf16[4,1,32,3072]{3,2,1,0:T(8,128)(2,1)S(1)}, u32[]{:S(2)}, u32[]{:S(2)}) collective-permute-start(bf16[4,1,32,3072]{3,2,1,0:T(8,128)(2,1)S(1)} %get-tuple-element.39), channel_id=1, source_target_pairs={{0,4},{4,0},{8,12},{12,8},{16,20},{20,16},{24,28},{28,24},{1,5},{5... | collective-permute-start | bytes 2359304 | tf_op jit(solution)/shard_map/ppermute | solution.py:34
  34.5 25.5 %copy-start.4 = (f32[2688]{0:T(1024)S(1)}, f32[2688]{0:T(1024)}, u32[]{:S(2)}) copy-start(f32[2688]{0:T(1024)} %param.19) | copy-start | bytes 32260
  34.5 25.5 %copy-start.5 = (f32[2688]{0:T(1024)S(1)}, f32[2688]{0:T(1024)}, u32[]{:S(2)}) copy-start(f32[2688]{0:T(1024)} %param.18) | copy-start | bytes 32260
  34.5 6.7 %collective-permute-start.8 = (bf16[40,3072]{1,0:T(8,128)(2,1)S(1)}, bf16[40,3072]{1,0:T(8,128)(2,1)S(1)}, u32[]{:S(2)}, u32[]{:S(2)}) collective-permute-start(bf16[40,3072]{1,0:T(8,128)(2,1)S(1)} %get-tuple-element.43), channel_id=1, source_target_pairs={{0,1},{1,0},{2,3},{3,2},{4,5},{5,4},{6,7},{7,6},{8,9},{9,8},{10,11... | collective-permute-start | bytes 737288 | tf_op jit(solution)/shard_map/ppermute | solution.py:34
  34.8 6.4 %collective-permute-start.9 = (bf16[40,3072]{1,0:T(8,128)(2,1)S(1)}, bf16[40,3072]{1,0:T(8,128)(2,1)S(1)}, u32[]{:S(2)}, u32[]{:S(2)}) collective-permute-start(bf16[40,3072]{1,0:T(8,128)(2,1)S(1)} %get-tuple-element.44), channel_id=1, source_target_pairs={{0,2},{1,3},{2,0},{3,1},{4,6},{5,7},{6,4},{7,5},{8,10},{9,11},{10,... | collective-permute-start | bytes 737288 | tf_op jit(solution)/shard_map/ppermute | solution.py:34
  35.1 11.6 %collective-permute-start.10 = (bf16[40,3072]{1,0:T(8,128)(2,1)S(1)}, bf16[40,3072]{1,0:T(8,128)(2,1)S(1)}, u32[]{:S(2)}, u32[]{:S(2)}) collective-permute-start(bf16[40,3072]{1,0:T(8,128)(2,1)S(1)} %get-tuple-element.45), channel_id=1, source_target_pairs={{0,3},{1,2},{2,1},{3,0},{4,7},{5,6},{6,5},{7,4},{8,11},{9,10},{10,... | collective-permute-start | bytes 737288 | tf_op jit(solution)/shard_map/ppermute | solution.py:34
  47.6 29.3 %copy-start.3 = (s32[8]{0:T(128)S(1)}, s32[8]{0:T(128)}, u32[]{:S(2)}) copy-start(s32[8]{0:T(128)} %owners.3) | copy-start | bytes 100
  47.6 14.5 %collective-permute-start.17 = (bf16[1,96,3072]{2,1,0:T(8,128)(2,1)S(1)}, bf16[1,96,3072]{2,1,0:T(8,128)(2,1)S(1)}, u32[]{:S(2)}, u32[]{:S(2)}) collective-permute-start(bf16[1,96,3072]{2,1,0:T(8,128)(2,1)S(1)} %get-tuple-element.51), channel_id=1, source_target_pairs={{0,2},{1,3},{2,0},{3,1},{4,6},{5,7},{6,4},{7,5},{8,10},{9,11},{10,... | collective-permute-start | bytes 1769480 | tf_op jit(solution)/shard_map/ppermute | solution.py:34
  48.7 13.4 %collective-permute-start.18 = (bf16[1,96,3072]{2,1,0:T(8,128)(2,1)S(1)}, bf16[1,96,3072]{2,1,0:T(8,128)(2,1)S(1)}, u32[]{:S(2)}, u32[]{:S(2)}) collective-permute-start(bf16[1,96,3072]{2,1,0:T(8,128)(2,1)S(1)} %get-tuple-element.52), channel_id=1, source_target_pairs={{0,1},{1,0},{2,3},{3,2},{4,5},{5,4},{6,7},{7,6},{8,9},{9,8},{10,11... | collective-permute-start | bytes 1769480 | tf_op jit(solution)/shard_map/ppermute | solution.py:34
  48.7 3.6 %collective-permute-start.11 = (bf16[32,768]{1,0:T(8,128)(2,1)S(1)}, bf16[32,768]{1,0:T(8,128)(2,1)S(1)}, u32[]{:S(2)}, u32[]{:S(2)}) collective-permute-start(bf16[32,768]{1,0:T(8,128)(2,1)S(1)} %get-tuple-element.48), channel_id=1, source_target_pairs={{0,8},{4,12},{8,0},{12,4},{16,24},{20,28},{24,16},{28,20},{1,9},{5... | collective-permute-start | bytes 147464 | tf_op jit(solution)/shard_map/ppermute | solution.py:34
  49.1 3.8 %collective-permute-start.12 = (bf16[32,768]{1,0:T(8,128)(2,1)S(1)}, bf16[32,768]{1,0:T(8,128)(2,1)S(1)}, u32[]{:S(2)}, u32[]{:S(2)}) collective-permute-start(bf16[32,768]{1,0:T(8,128)(2,1)S(1)} %get-tuple-element.49), channel_id=1, source_target_pairs={{0,16},{4,20},{8,24},{12,28},{16,0},{20,4},{24,8},{28,12},{1,17},{... | collective-permute-start | bytes 147464 | tf_op jit(solution)/shard_map/ppermute | solution.py:34
  51.4 4.9 %collective-permute-start.13 = (bf16[32,768]{1,0:T(8,128)(2,1)S(1)}, bf16[32,768]{1,0:T(8,128)(2,1)S(1)}, u32[]{:S(2)}, u32[]{:S(2)}) collective-permute-start(bf16[32,768]{1,0:T(8,128)(2,1)S(1)} %get-tuple-element.50), channel_id=1, source_target_pairs={{0,24},{4,28},{8,16},{12,20},{16,8},{20,12},{24,0},{28,4},{1,25},{... | collective-permute-start | bytes 147464 | tf_op jit(solution)/shard_map/ppermute | solution.py:34
  56.3 4.8 %collective-permute-start.16 = (bf16[32,768]{1,0:T(8,128)(2,1)S(1)}, bf16[32,768]{1,0:T(8,128)(2,1)S(1)}, u32[]{:S(2)}, u32[]{:S(2)}) collective-permute-start(bf16[32,768]{1,0:T(8,128)(2,1)S(1)} %add.29.refs_0_), channel_id=1, source_target_pairs={{0,24},{4,28},{8,16},{12,20},{16,8},{20,12},{24,0},{28,4},{1,25},{... | collective-permute-start | bytes 147464 | tf_op jit(solution)/shard_map/ppermute | solution.py:34
  57.1 5.0 %collective-permute-start.15 = (bf16[32,768]{1,0:T(8,128)(2,1)S(1)}, bf16[32,768]{1,0:T(8,128)(2,1)S(1)}, u32[]{:S(2)}, u32[]{:S(2)}) collective-permute-start(bf16[32,768]{1,0:T(8,128)(2,1)S(1)} %add.29.refs_0_), channel_id=1, source_target_pairs={{0,16},{4,20},{8,24},{12,28},{16,0},{20,4},{24,8},{28,12},{1,17},{... | collective-permute-start | bytes 147464 | tf_op jit(solution)/shard_map/ppermute | solution.py:34
  57.1 5.0 %collective-permute-start.14 = (bf16[32,768]{1,0:T(8,128)(2,1)S(1)}, bf16[32,768]{1,0:T(8,128)(2,1)S(1)}, u32[]{:S(2)}, u32[]{:S(2)}) collective-permute-start(bf16[32,768]{1,0:T(8,128)(2,1)S(1)} %add.29.refs_0_), channel_id=1, source_target_pairs={{0,8},{4,12},{8,0},{12,4},{16,24},{20,28},{24,16},{28,20},{1,9},{5... | collective-permute-start | bytes 147464 | tf_op jit(solution)/shard_map/ppermute | solution.py:34
  60.6 22.1 %copy-start.1 = (f32[2688]{0:T(1024)}, f32[2688]{0:T(1024)S(1)}, u32[]{:S(2)}) copy-start(f32[2688]{0:T(1024)S(1)} %get-tuple-element.62.refs_6_) | copy-start | bytes 32260
  62.1 5.6 %collective-permute-start.21 = (bf16[4,32,768]{2,1,0:T(8,128)(2,1)S(1)}, bf16[4,32,768]{2,1,0:T(8,128)(2,1)S(1)}, u32[]{:S(2)}, u32[]{:S(2)}) collective-permute-start(bf16[4,32,768]{2,1,0:T(8,128)(2,1)S(1)} %stack.35.refs_0_), channel_id=1, source_target_pairs={{0,3},{1,2},{2,1},{3,0},{4,7},{5,6},{6,5},{7,4},{8,11},{9,10},{10,... | collective-permute-start | bytes 589832 | tf_op jit(solution)/shard_map/ppermute | solution.py:34
  63.1 6.6 %collective-permute-start.20 = (bf16[4,32,768]{2,1,0:T(8,128)(2,1)S(1)}, bf16[4,32,768]{2,1,0:T(8,128)(2,1)S(1)}, u32[]{:S(2)}, u32[]{:S(2)}) collective-permute-start(bf16[4,32,768]{2,1,0:T(8,128)(2,1)S(1)} %stack.35.refs_0_), channel_id=1, source_target_pairs={{0,2},{1,3},{2,0},{3,1},{4,6},{5,7},{6,4},{7,5},{8,10},{9,11},{10,... | collective-permute-start | bytes 589832 | tf_op jit(solution)/shard_map/ppermute | solution.py:34
  64.2 5.5 %collective-permute-start.19 = (bf16[4,32,768]{2,1,0:T(8,128)(2,1)S(1)}, bf16[4,32,768]{2,1,0:T(8,128)(2,1)S(1)}, u32[]{:S(2)}, u32[]{:S(2)}) collective-permute-start(bf16[4,32,768]{2,1,0:T(8,128)(2,1)S(1)} %stack.35.refs_0_), channel_id=1, source_target_pairs={{0,1},{1,0},{2,3},{3,2},{4,5},{5,4},{6,7},{7,6},{8,9},{9,8},{10,11... | collective-permute-start | bytes 589832 | tf_op jit(solution)/shard_map/ppermute | solution.py:34
  69.8 12.9 %collective-permute-start.22 = (bf16[4,1,4,32,768]{4,3,2,1,0:T(8,128)(2,1)S(1)}, bf16[4,1,4,32,768]{4,3,2,1,0:T(8,128)(2,1)S(1)}, u32[]{:S(2)}, u32[]{:S(2)}) collective-permute-start(bf16[4,1,4,32,768]{4,3,2,1,0:T(8,128)(2,1)S(1)} %bitcast.11), channel_id=1, source_target_pairs={{0,4},{4,0},{8,12},{12,8},{16,20},{20,16},{24,28},{28,24},{1,5},{5... | collective-permute-start | bytes 2359304 | tf_op jit(solution)/shard_map/ppermute | solution.py:34

commit v10 on v9

--- a/solution.py
+++ b/solution.py
@@ -8,8 +8,8 @@
 from jax.sharding import PartitionSpec as P
 
 CORES = 2
-AHEAD = 4
-BASE_ROWS = 16
+AHEAD = 8
+BASE_ROWS = 48
 COLUMNS = 384
 F32 = jnp.float32
 BF16 = jnp.bfloat16
@@ -38,16 +38,13 @@
     nmat, rows, _ = comp_ref.shape
     rank = q_ref.shape[1]
     part = near_ref.shape[0]
-    cut = rows // 2 if rows % 32 == 0 else rows
 
     def copies(k):
-        out = [pltpu.make_async_copy(q_ref.at[k], right.at[k], sems.at[k, 4])]
-        for i, first in enumerate(range(0, rows, cut)):
-            block = pl.ds(first, cut)
-            for j, (source, target) in enumerate(((g_ref, comp_ref), (f_ref, feedback))):
-                source, target = source.at[0, k, block], target.at[k, block]
-                out.append(pltpu.make_async_copy(source, target, sems.at[k, 2 * i + j]))
-        return out
+        return [
+            pltpu.make_async_copy(g_ref.at[0, k], comp_ref.at[k], sems.at[k, 0]),
+            pltpu.make_async_copy(f_ref.at[0, k], feedback.at[k], sems.at[k, 1]),
+            pltpu.make_async_copy(q_ref.at[k], right.at[k], sems.at[k, 2]),
+        ]
 
     for k in range(min(AHEAD, nmat)):
         for copy in copies(k):
@@ -94,7 +91,7 @@
                 pltpu.VMEM((total, width), F32),
                 pltpu.VMEM((nmat, rows, n), BF16),
                 pltpu.VMEM((nmat, rank, n), BF16),
-                pltpu.SemaphoreType.DMA((nmat, 5)),
+                pltpu.SemaphoreType.DMA((nmat, 3)),
             ],
         ),
         out_shape=[jax.ShapeDtypeStruct((nmat, rows, n), BF16), part, part],
@@ -350,61 +347,72 @@
     return count
 
 
-def outputs_kernel(second, places, pos, owners, comp_ref, mix_ref, mixr_ref, near_ref, *refs):
-    n_base = len({a for a, _ in places.values()})
-    bases, refs = refs[:n_base], refs[n_base:]
-    if second:
-        far_ref, momentum_ref, master_ref, refs = refs[0], refs[1], refs[2], refs[5:]
-    n_out = 4 if second else 2
-    outs, refs = refs[:n_out], refs[n_out:]
-    held, feedback, weights, fetch_sem, out_sem = refs[:5]
-    half, upm, n_z, unit, cols = near_ref.shape
-    count = held.shape[1]
-    capacity = max(c for _, c in places) + 1
-
-    def right_of(ref, j, d, block):
-        parts = [ref[j, i ^ pos[1], d, :, block] for i in range(upm)]
+def collect_kernel(places, *refs):
+    for i, (a, row) in enumerate(places):
+        refs[-1][i] = refs[a][row]
+
+
+def collect(bases, places):
+    vmem = pl.BlockSpec(memory_space=pltpu.VMEM)
+    return pl.pallas_call(
+        functools.partial(collect_kernel, places),
+        in_specs=[vmem] * len(bases),
+        out_specs=vmem,
+        out_shape=jax.ShapeDtypeStruct((len(places),) + bases[0].shape[1:], BF16),
+        compiler_params=params(),
+        cost_estimate=cost(),
+        name="collect",
+    )(*bases)
+
+
+def outputs_kernel(jobs, where, capacity, pos, owners, comp_ref, mix_ref, mixr_ref, base_ref, *refs):
+    n_right = 1 + max(a for a, _ in (where or jobs).values())
+    rights, refs = refs[:n_right], refs[n_right:]
+    n_scratch = 6 if where else 3
+    scratch = refs[-n_scratch:]
+    feedback, weights, out_sem = scratch[:3]
+    refs = refs[:-n_scratch]
+    token_ref, outs = refs[-1], refs[-5:-1] if where else refs[-3:-1]
+    token_ref[...] = jnp.zeros(token_ref.shape, F32)
+    _, upm, n_z, _, cols = rights[0].shape
+    half = comp_ref.shape[0] // CORES
+    count = weights.shape[1]
+
+    def right_of(place, d, block):
+        a, entry = place
+        parts = [rights[a][entry, i ^ pos[1], d, :, block] for i in range(upm)]
         return parts[0] if upm == 1 else jnp.concatenate(parts, axis=0)
 
     def columns(d, first=0, size=cols):
         return pl.ds(pl.multiple_of((pos[4] ^ d) * cols + first, 128), size)
 
+    def matrix(other, j):
+        return (j + half * other) ^ pos[0]
+
     pieces = [slice(first, first + COLUMNS) for first in range(0, cols, COLUMNS)]
-    matrices = [(j + (half if second else 0)) ^ pos[0] for j in range(half)]
-    for j, k in enumerate(matrices):
-        slot = (owners[k] ^ pos[5]) * capacity + rank_of(owners, k)
-        for (d, c), (a, row) in places.items():
-
-            @pl.when(slot == d * capacity + c)
-            def _():
-                pltpu.make_async_copy(bases[a].at[row], held.at[j], fetch_sem.at[j]).start()
-
     stores = []
 
     def store(source, target, sem):
         stores.append(pltpu.make_async_copy(source, target, sem))
         stores[-1].start()
 
-    if second:
-        new_momentum, new_master, state_sem = refs[5:8]
+    if where:
+        momentum_ref, master_ref = refs[:2]
+        new_momentum, new_master, state_sem = scratch[3:]
         for c in range(capacity):
-            matrix = jnp.int32(-1)
+            mine = jnp.int32(-1)
             for k in range(owners.shape[0]):
-                matrix = jnp.where((owners[k] == pos[5]) & (rank_of(owners, k) == c), k, matrix)
-            safe = jnp.maximum(matrix, 0)
-            slot = safe ^ pos[0]
-            inner = lax.rem(slot, half)
+                mine = jnp.where((owners[k] == pos[5]) & (rank_of(owners, k) == c), k, mine)
+            safe = jnp.maximum(mine, 0)
             mixr = mixr_ref[safe][:, count:]
             for d in range(n_z):
                 for block in pieces:
-                    right = jnp.where(
-                        slot < half,
-                        right_of(near_ref, inner, d, block),
-                        right_of(far_ref, inner, d, block),
-                    )
+                    right = jnp.zeros((mixr.shape[1] // 2, COLUMNS), BF16)
+                    for job, place in where.items():
+                        right = jnp.where(safe == matrix(*job), right_of(place, d, block), right)
                     both = jnp.concatenate([right, right], axis=0)
                     change = jnp.dot(mixr, both, preferred_element_type=F32)
-                    change = jnp.where(matrix >= 0, 10.0 * change, 0.0)
+                    change = jnp.where(mine >= 0, 10.0 * change, 0.0)
                     place = columns(d, block.start, COLUMNS)
                     momentum = 0.9 * momentum_ref[c, :, place] - change
                     new_momentum[c, :, place] = momentum
@@ -415,73 +423,60 @@
                         new.at[c, :, place], outs[2 + i].at[0, c, :, place], state_sem.at[i, c, d]
                     )
 
-    for j, k in enumerate(matrices):
-        ref = far_ref if second else near_ref
+    for i, (job, where_right) in enumerate(jobs.items()):
+        k = matrix(*job)
+        slot = (owners[k] ^ pos[5]) * capacity + rank_of(owners, k)
         mix, mixr = mix_ref[k], mixr_ref[k]
         for d in range(n_z):
             for block in pieces:
-                right = right_of(ref, j, d, block)
+                right = right_of(where_right, d, block)
                 place = columns(d, block.start, COLUMNS)
                 both = jnp.concatenate([comp_ref[k, :, place], right], axis=0)
-                feedback[j, :, place] = jnp.dot(mix, both, preferred_element_type=F32).astype(BF16)
+                feedback[i, :, place] = jnp.dot(mix, both, preferred_element_type=F32).astype(BF16)
+                both = jnp.concatenate([base_ref[slot, :, place], right, right], axis=0)
+                weights[i, :, place] = jnp.dot(mixr, both, preferred_element_type=F32).astype(BF16)
             place = columns(d)
-            store(feedback.at[j, :, place], outs[0].at[0, k, :, place], out_sem.at[j, d, 0])
-        pltpu.make_async_copy(bases[0].at[0], held.at[j], fetch_sem.at[j]).wait()
-        for d in range(n_z):
-            for block in pieces:
-                right = right_of(ref, j, d, block)
-                place = columns(d, block.start, COLUMNS)
-                both = jnp.concatenate([held[j, :, place], right, right], axis=0)
-                weights[j, :, place] = jnp.dot(mixr, both, preferred_element_type=F32).astype(BF16)
-            place = columns(d)
-            store(weights.at[j, :, place], outs[1].at[k, :, place], out_sem.at[j, d, 1])
+            store(feedback.at[i, :, place], outs[0].at[0, k, :, place], out_sem.at[i, d, 0])
+            store(weights.at[i, :, place], outs[1].at[k, :, place], out_sem.at[i, d, 1])
 
     for copy in stores:
         copy.wait()
 
 
-def outputs(pos, owners, comp, mix, mixr, near, bases, places, far=None, states=(), earlier=()):
+def outputs(pos, owners, comp, mix, mixr, base, capacity, rights, jobs, where=None, states=(), earlier=()):
     nmat, rows, n = comp.shape
-    half, _, n_z = near.shape[:3]
-    capacity = max(c for _, c in places) + 1
-    replica_rows = bases[0].shape[1]
-    second = far is not None
+    n_z = rights[0].shape[2]
+    replica_rows = base.shape[1]
     any_spec = pl.BlockSpec(memory_space=pl.ANY)
     vmem = pl.BlockSpec(memory_space=pltpu.VMEM)
     scratch = [
-        pltpu.VMEM((half, replica_rows, n), BF16),
-        pltpu.VMEM((half, rows, n), BF16),
-        pltpu.VMEM((half, replica_rows, n), BF16),
-        pltpu.SemaphoreType.DMA((half,)),
-        pltpu.SemaphoreType.DMA((half, n_z, 2)),
+        pltpu.VMEM((len(jobs), rows, n), BF16),
+        pltpu.VMEM((len(jobs), replica_rows, n), BF16),
+        pltpu.SemaphoreType.DMA((len(jobs), n_z, 2)),
     ]
-    if second:
+    if states:
         scratch += [pltpu.VMEM((capacity, replica_rows, n), F32)] * 2
         scratch += [pltpu.SemaphoreType.DMA((2, capacity, n_z))]
     outs = [
         jax.ShapeDtypeStruct((1, nmat, rows, n), BF16),
         jax.ShapeDtypeStruct((nmat, replica_rows, n), BF16),
     ] + [jax.ShapeDtypeStruct((1,) + x.shape, F32) for x in states]
-    fars = [far] if second else []
-    first = 6 + len(bases) + len(fars) + len(states)
-    return pl.pallas_call(
-        functools.partial(outputs_kernel, second, places),
+    first = 6 + len(rights) + len(states)
+    return pl.pallas_call(
+        functools.partial(outputs_kernel, jobs, where, capacity),
         grid_spec=pltpu.PrefetchScalarGridSpec(
             num_scalar_prefetch=2,
             grid=(1,),
-            in_specs=[vmem] * 4
-            + [any_spec] * len(bases)
-            + [vmem] * (len(fars) + len(states))
-            + [any_spec] * len(earlier),
-            out_specs=[any_spec] * len(outs),
+            in_specs=[vmem] * (4 + len(rights) + len(states)) + [any_spec] * len(earlier),
+            out_specs=[any_spec] * len(outs) + [vmem],
             scratch_shapes=scratch,
         ),
-        out_shape=outs,
+        out_shape=outs + [jax.ShapeDtypeStruct((8, 128), F32)],
         input_output_aliases={first + i: i for i in range(len(earlier))},
         compiler_params=params(24),
         cost_estimate=cost(),
         name="outputs",
-    )(pos, owners, comp, mix, mixr, near, *bases, *fars, *states, *earlier)
+    )(pos, owners, comp, mix, mixr, base, *rights, *states, *earlier)
 
 
 def base_kernel(pos, momentum_ref, master_ref, *refs):
@@ -594,15 +589,23 @@
     new_vector_params = vector_params - 0.1 * new_vector_momentum
 
     whole = stack([final] + along_z(final), late + [new_vector_params])
-    near = stack([whole] + [exchange(whole, "mp", d) for d in range(1, n_mp)])
-    near = near.reshape((half, upm) + whole.shape)
+    others = [exchange(whole, "mp", d) for d in range(1, n_mp)]
+    slots = collect(bases, [places[d, c] for d in range(n_mp) for c in range(capacity)])
+    common = (pos, owners, comp, mix, mixr, slots, capacity)
+    shape = (half, upm) + whole.shape
+    done, near_jobs, after = (), {(0, j): (0, j) for j in range(half)}, [slots]
+    if upm == 1:
+        *done, after = outputs(*common, [whole[None, None]], {(0, 0): (0, 0)})
+        after = [after]
+        del near_jobs[0, 0]
+    near = stack([whole] + others, after).reshape(shape)
     far = exchange(near, "replica", 1)
-
-    done = outputs(pos, owners, comp, mix, mixr, near, bases, places)
-    new_feedback, new_weights, new_momentum, new_master = outputs(
-        pos, owners, comp, mix, mixr, near, bases, places, far, states, done
+    far_jobs = {(1, j): (1, j) for j in range(half)}
+    where = {(0, j): (0, j) for j in range(half)} | far_jobs
+    *done, _ = outputs(*common, [near], near_jobs, earlier=done)
+    new_feedback, new_weights, new_momentum, new_master, _ = outputs(
+        *common, [near, far], far_jobs, where, states, done
     )
-
     return new_feedback, new_momentum, new_master, new_weights, new_vector_momentum, new_vector_params
 
 

time: 89.6 us -> 87.7 us (0.979)
  waiting for transfers between devices: 26.9 us -> 24.6 us
    ppermute x23, waiting for transfers between devices: 26.9 us -> 24.6 us  [exchange(): return lax.ppermute(x, axis, [(i, i ^ distance) for i in range(size)])]
    pallas_call x2 -> x4, Pallas kernels: 12.4 us -> 13.1 us  [the longest x3 12.8 us: outputs(): pl.pallas_call(functools.partial(outputs_kernel, jobs, where, capacity),...]
  transfers between devices with their start and end apart: 23 -> 23, of which waited for: 13 -> 13; matrix products, arithmetic and copies ran while one was open for 1% -> 1% of each run, Pallas kernels for 21% -> 22%
where the time goes in v10:
time: 87.7 us; the launch traced here: 87.5 us
  starting transfers between devices  30.7 us (35%)
  Pallas kernels  30.5 us (35%)
  waiting for transfers between devices  24.6 us (28%)
  between operations  1.04 us (1%)
    ppermute x23, starting transfers between devices, exchange(): return lax.ppermute(x, axis, [(i, i ^ distance) for i in range(size)])  30.7 us
    ppermute x23, waiting for transfers between devices, exchange(): return lax.ppermute(x, axis, [(i, i ^ distance) for i in range(size)])  24.6 us
    pallas_call x3, Pallas kernels, outputs(): pl.pallas_call(functools.partial(outputs_kernel, jobs, where, capacity),...  12.8 us
    pallas_call x1, Pallas kernels, left_terms(): pl.pallas_call(left_kernel, grid_spec=pltpu.PrefetchScalarGridSpec(num_sc...  8.78 us
    pallas_call x1, Pallas kernels, base_of(): pl.pallas_call(base_kernel, grid_spec=pltpu.PrefetchScalarGridSpec(num_sc...  2.99 us
    pallas_call x1, Pallas kernels, right_terms(): pl.pallas_call(functools.partial(send_kernel, half), grid_spec=pltpu.Pref...  2.22 us
  transfers between devices with their start and end apart: 23, of which 13 were waited for; matrix products, arithmetic and copies ran while one was open for 1% of the time, Pallas kernels for 22%

profile of v10, /device:TPU:1, one launch (start us, length us, event | category | flops | bytes accessed | tf_op | source)
XLA Modules:
  0.0 87.5 jit_solution(16416639717826902409)
XLA Ops:
  0.8 3.0 %base.1 = (bf16[2,96,3072]{2,1,0:T(8,128)(2,1)S(1)}, f32[2,96,3072]{2,1,0:T(8,128)S(1)}, f32[2,96,3072]{2,1,0:T(8,128)S(1)}) custom-call(s32[8]{0:T(128)S(1)} %stack.34.pos, f32[1,2,96,3072]{3,2,1,0:T(8,128)} %momentum_ref.1, f32[1,2,96,3072]{3,2,1,0:T(8,128)} %master_ref.1), custom_call_target="tpu_custom_call" | custom-call | flops 1000 | bytes 1000 | tf_op jit(solution)/shard_map/base/pallas_call | solution.py:508
  3.8 2.1 %collective-permute-start.7 = (bf16[2,96,3072]{2,1,0:T(8,128)(2,1)S(1)}, bf16[2,96,3072]{2,1,0:T(8,128)(2,1)S(1)}, u32[]{:S(2)}, u32[]{:S(2)}) collective-permute-start(bf16[2,96,3072]{2,1,0:T(8,128)(2,1)S(1)} %get-tuple-element.43.refs_0_), channel_id=1, source_target_pairs={{0,2},{1,3},{2,0},{3,1},{4,6},{5,7},{6,4},{7,5},{8,10},{9,11},{10,... | collective-permute-start | bytes 3538952 | tf_op jit(solution)/shard_map/ppermute | solution.py:34
  5.9 1.2 %collective-permute-start.6 = (bf16[2,96,3072]{2,1,0:T(8,128)(2,1)S(1)}, bf16[2,96,3072]{2,1,0:T(8,128)(2,1)S(1)}, u32[]{:S(2)}, u32[]{:S(2)}) collective-permute-start(bf16[2,96,3072]{2,1,0:T(8,128)(2,1)S(1)} %get-tuple-element.43.refs_0_), channel_id=1, source_target_pairs={{0,1},{1,0},{2,3},{3,2},{4,5},{5,4},{6,7},{7,6},{8,9},{9,8},{10,11... | collective-permute-start | bytes 3538952 | tf_op jit(solution)/shard_map/ppermute | solution.py:34
  7.1 8.8 %left_terms.1 = (bf16[8,192,3072]{2,1,0:T(8,128)(2,1)S(1)}, f32[112,256]{1,0:T(8,128)S(1)}, f32[112,256]{1,0:T(8,128)S(1)}) custom-call(s32[8]{0:T(128)S(1)} %stack.34.pos, bf16[1,8,192,3072]{3,2,1,0:T(8,128)(2,1)} %g_ref.1, bf16[1,8,192,3072]{3,2,1,0:T(8,128)(2,1)} %f_ref.1, bf16[8,32,3072]{2,1,0:T(8,128)(2,1)} %bitcast.17, f32[1,2688]{1,0:T(1,128)S(1)} %copy-done.2), custom_call_target="tpu_custom_call" | custom-call | flops 1000 | bytes 1000 | tf_op jit(solution)/shard_map/left_terms/pallas_call | solution.py:83
  15.9 1.3 %collective-permute-start = (f32[112,256]{1,0:T(8,128)S(1)}, f32[112,256]{1,0:T(8,128)S(1)}, u32[]{:S(2)}, u32[]{:S(2)}) collective-permute-start(f32[112,256]{1,0:T(8,128)S(1)} %get-tuple-element.39), channel_id=1, source_target_pairs={{0,4},{4,0},{8,12},{12,8},{16,20},{20,16},{24,28},{28,24},{1,5},{5... | collective-permute-start | bytes 344072 | tf_op jit(solution)/shard_map/ppermute | solution.py:34
  17.2 1.0 %collective-permute-done.refs_1_ = f32[112,256]{1,0:T(8,128)S(1)} collective-permute-done((f32[112,256]{1,0:T(8,128)S(1)}, f32[112,256]{1,0:T(8,128)S(1)}, u32[]{:S(2)}, u32[]{:S(2)}) %collective-permute-start) | collective-permute-done | bytes 114720 | tf_op jit(solution)/shard_map/ppermute | solution.py:34
  18.2 3.4 %collective-permute-start.3 = (bf16[112,256]{1,0:T(8,128)(2,1)S(1)}, bf16[112,256]{1,0:T(8,128)(2,1)S(1)}, u32[]{:S(2)}, u32[]{:S(2)}) collective-permute-start(bf16[112,256]{1,0:T(8,128)(2,1)S(1)} %add.27.refs_0_), channel_id=1, source_target_pairs={{0,24},{4,28},{8,16},{12,20},{16,8},{20,12},{24,0},{28,4},{1,25},{... | collective-permute-start | bytes 172040 | tf_op jit(solution)/shard_map/ppermute | solution.py:34
  22.0 1.3 %collective-permute-done.3.refs_3_ = bf16[112,256]{1,0:T(8,128)(2,1)S(1)} collective-permute-done((bf16[112,256]{1,0:T(8,128)(2,1)S(1)}, bf16[112,256]{1,0:T(8,128)(2,1)S(1)}, u32[]{:S(2)}, u32[]{:S(2)}) %collective-permute-start.3) | collective-permute-done | bytes 57376 | tf_op jit(solution)/shard_map/ppermute | solution.py:34
  23.3 3.4 %collective-permute-done.2.refs_2_ = bf16[112,256]{1,0:T(8,128)(2,1)S(1)} collective-permute-done((bf16[112,256]{1,0:T(8,128)(2,1)S(1)}, bf16[112,256]{1,0:T(8,128)(2,1)S(1)}, u32[]{:S(2)}, u32[]{:S(2)}) %collective-permute-start.2) | collective-permute-done | bytes 57376 | tf_op jit(solution)/shard_map/ppermute | solution.py:34
  26.7 1.0 %collective-permute-start.4 = (f32[112,256]{1,0:T(8,128)S(1)}, f32[112,256]{1,0:T(8,128)S(1)}, u32[]{:S(2)}, u32[]{:S(2)}) collective-permute-start(f32[112,256]{1,0:T(8,128)S(1)} %add.28.near_ref), channel_id=1, source_target_pairs={{0,4},{4,0},{8,12},{12,8},{16,20},{20,16},{24,28},{28,24},{1,5},{5... | collective-permute-start | bytes 344072 | tf_op jit(solution)/shard_map/ppermute | solution.py:34
  27.7 1.0 %collective-permute-done.4.far_ref = f32[112,256]{1,0:T(8,128)S(1)} collective-permute-done((f32[112,256]{1,0:T(8,128)S(1)}, f32[112,256]{1,0:T(8,128)S(1)}, u32[]{:S(2)}, u32[]{:S(2)}) %collective-permute-start.4) | collective-permute-done | bytes 114720 | tf_op jit(solution)/shard_map/ppermute | solution.py:34
  28.7 2.2 %right_send.1 = (bf16[4,1,32,3072]{3,2,1,0:T(8,128)(2,1)S(1)}, bf16[256,192]{1,0:T(8,128)(2,1)S(1)}, bf16[8,192,224]{2,1,0:T(8,128)(2,1)S(1)}, f32[32,256]{1,0:T(8,128)S(1)}) custom-call(s32[8]{0:T(128)S(1)} %stack.34.pos, f32[112,256]{1,0:T(8,128)S(1)} %add.28.near_ref, f32[112,256]{1,0:T(8,128)S(1)} %collective-permute-done.4.far_ref, ...), custom_call_target="tpu_custom_call" | custom-call | flops 1000 | bytes 1000 | tf_op jit(solution)/shard_map/right_send/pallas_call | solution.py:170
  31.3 1.5 %right_keep.1.refs_0_.keep_ref = f32[4,1,32,3072]{3,2,1,0:T(8,128)S(1)} custom-call(s32[8]{0:T(128)S(1)} %stack.34.pos, bf16[256,192]{1,0:T(8,128)(2,1)S(1)} %get-tuple-element.41.lt_ref, bf16[8,192,3072]{2,1,0:T(8,128)(2,1)S(1)} %get-tuple-element.37.comp_ref), custom_call_target="tpu_custom_call" | custom-call | flops 1000 | bytes 1000 | tf_op jit(solution)/shard_map/right_keep/pallas_call | solution.py:189
  34.9 1.9 %collective-permute-start.10 = (bf16[40,3072]{1,0:T(8,128)(2,1)S(1)}, bf16[40,3072]{1,0:T(8,128)(2,1)S(1)}, u32[]{:S(2)}, u32[]{:S(2)}) collective-permute-start(bf16[40,3072]{1,0:T(8,128)(2,1)S(1)} %get-tuple-element.48), channel_id=1, source_target_pairs={{0,3},{1,2},{2,1},{3,0},{4,7},{5,6},{6,5},{7,4},{8,11},{9,10},{10,... | collective-permute-start | bytes 737288 | tf_op jit(solution)/shard_map/ppermute | solution.py:34
  36.8 3.8 %collective-permute-done.8.refs_0_ = bf16[40,3072]{1,0:T(8,128)(2,1)S(1)} collective-permute-done((bf16[40,3072]{1,0:T(8,128)(2,1)S(1)}, bf16[40,3072]{1,0:T(8,128)(2,1)S(1)}, u32[]{:S(2)}, u32[]{:S(2)}) %collective-permute-start.8) | collective-permute-done | bytes 245792 | tf_op jit(solution)/shard_map/ppermute | solution.py:34
  40.6 5.4 %collective-permute-done.10.refs_2_ = bf16[40,3072]{1,0:T(8,128)(2,1)S(1)} collective-permute-done((bf16[40,3072]{1,0:T(8,128)(2,1)S(1)}, bf16[40,3072]{1,0:T(8,128)(2,1)S(1)}, u32[]{:S(2)}, u32[]{:S(2)}) %collective-permute-start.10) | collective-permute-done | bytes 245792 | tf_op jit(solution)/shard_map/ppermute | solution.py:34
  46.0 0.8 plane_sum.1
  46.9 1.1 %collective-permute-start.11 = (bf16[1,96,3072]{2,1,0:T(8,128)(2,1)S(1)}, bf16[1,96,3072]{2,1,0:T(8,128)(2,1)S(1)}, u32[]{:S(2)}, u32[]{:S(2)}) collective-permute-start(bf16[1,96,3072]{2,1,0:T(8,128)(2,1)S(1)} %get-tuple-element.50), channel_id=1, source_target_pairs={{0,2},{1,3},{2,0},{3,1},{4,6},{5,7},{6,4},{7,5},{8,10},{9,11},{10,... | collective-permute-start | bytes 1769480 | tf_op jit(solution)/shard_map/ppermute | solution.py:34
  48.0 0.8 collective-permute-start.13
  48.9 2.3 %collective-permute-start.14 = (bf16[32,768]{1,0:T(8,128)(2,1)S(1)}, bf16[32,768]{1,0:T(8,128)(2,1)S(1)}, u32[]{:S(2)}, u32[]{:S(2)}) collective-permute-start(bf16[32,768]{1,0:T(8,128)(2,1)S(1)} %get-tuple-element.54), channel_id=1, source_target_pairs={{0,16},{4,20},{8,24},{12,28},{16,0},{20,4},{24,8},{28,12},{1,17},{... | collective-permute-start | bytes 147464 | tf_op jit(solution)/shard_map/ppermute | solution.py:34
  51.6 1.6 %collective-permute-done.14.refs_2_ = bf16[32,768]{1,0:T(8,128)(2,1)S(1)} collective-permute-done((bf16[32,768]{1,0:T(8,128)(2,1)S(1)}, bf16[32,768]{1,0:T(8,128)(2,1)S(1)}, u32[]{:S(2)}, u32[]{:S(2)}) %collective-permute-start.14) | collective-permute-done | bytes 49184 | tf_op jit(solution)/shard_map/ppermute | solution.py:34
  53.2 2.9 %collective-permute-done.15.refs_3_ = bf16[32,768]{1,0:T(8,128)(2,1)S(1)} collective-permute-done((bf16[32,768]{1,0:T(8,128)(2,1)S(1)}, bf16[32,768]{1,0:T(8,128)(2,1)S(1)}, u32[]{:S(2)}, u32[]{:S(2)}) %collective-permute-start.15) | collective-permute-done | bytes 49184 | tf_op jit(solution)/shard_map/ppermute | solution.py:34
  56.6 3.2 %collective-permute-start.16 = (bf16[32,768]{1,0:T(8,128)(2,1)S(1)}, bf16[32,768]{1,0:T(8,128)(2,1)S(1)}, u32[]{:S(2)}, u32[]{:S(2)}) collective-permute-start(bf16[32,768]{1,0:T(8,128)(2,1)S(1)} %add.29.refs_0_), channel_id=1, source_target_pairs={{0,8},{4,12},{8,0},{12,4},{16,24},{20,28},{24,16},{28,20},{1,9},{5... | collective-permute-start | bytes 147464 | tf_op jit(solution)/shard_map/ppermute | solution.py:34
  61.0 0.9 %collective-permute-done.17.refs_2_ = bf16[32,768]{1,0:T(8,128)(2,1)S(1)} collective-permute-done((bf16[32,768]{1,0:T(8,128)(2,1)S(1)}, bf16[32,768]{1,0:T(8,128)(2,1)S(1)}, u32[]{:S(2)}, u32[]{:S(2)}) %collective-permute-start.17) | collective-permute-done | bytes 49184 | tf_op jit(solution)/shard_map/ppermute | solution.py:34
  61.9 0.9 %collective-permute-start.21 = (bf16[4,32,768]{2,1,0:T(8,128)(2,1)S(1)}, bf16[4,32,768]{2,1,0:T(8,128)(2,1)S(1)}, u32[]{:S(2)}, u32[]{:S(2)}) collective-permute-start(bf16[4,32,768]{2,1,0:T(8,128)(2,1)S(1)} %stack.35.refs_0_), channel_id=1, source_target_pairs={{0,3},{1,2},{2,1},{3,0},{4,7},{5,6},{6,5},{7,4},{8,11},{9,10},{10,... | collective-permute-start | bytes 589832 | tf_op jit(solution)/shard_map/ppermute | solution.py:34
  62.9 0.9 %collective-permute-start.20 = (bf16[4,32,768]{2,1,0:T(8,128)(2,1)S(1)}, bf16[4,32,768]{2,1,0:T(8,128)(2,1)S(1)}, u32[]{:S(2)}, u32[]{:S(2)}) collective-permute-start(bf16[4,32,768]{2,1,0:T(8,128)(2,1)S(1)} %stack.35.refs_0_), channel_id=1, source_target_pairs={{0,2},{1,3},{2,0},{3,1},{4,6},{5,7},{6,4},{7,5},{8,10},{9,11},{10,... | collective-permute-start | bytes 589832 | tf_op jit(solution)/shard_map/ppermute | solution.py:34
  63.8 0.9 collective-permute-start.19
  65.0 2.2 %outputs.3 = (bf16[1,8,192,3072]{3,2,1,0:T(8,128)(2,1)}, bf16[8,96,3072]{2,1,0:T(8,128)(2,1)}, f32[8,128]{1,0:T(8,128)S(1)}) custom-call(s32[8]{0:T(128)S(1)} %stack.34.pos, s32[8]{0:T(128)S(1)} %copy-done.3, bf16[8,192,3072]{2,1,0:T(8,128)(2,1)S(1)} %get-tuple-element.37.comp_ref, bf16[8,192,224]{2,1,0:T(8,128)(2,1)S(1)} %get-tuple-element.40.mix_ref, ...), custom_call_target="tpu_custom_call" | custom-call | flops 1000 | bytes 1000 | tf_op jit(solution)/shard_map/outputs/pallas_call | solution.py:465
  67.5 2.0 %collective-permute-done.20.refs_2_ = bf16[4,32,768]{2,1,0:T(8,128)(2,1)S(1)} collective-permute-done((bf16[4,32,768]{2,1,0:T(8,128)(2,1)S(1)}, bf16[4,32,768]{2,1,0:T(8,128)(2,1)S(1)}, u32[]{:S(2)}, u32[]{:S(2)}) %collective-permute-start.20) | collective-permute-done | bytes 196640 | tf_op jit(solution)/shard_map/ppermute | solution.py:34
  69.5 7.2 %collective-permute-start.22 = (bf16[4,1,4,32,768]{4,3,2,1,0:T(8,128)(2,1)S(1)}, bf16[4,1,4,32,768]{4,3,2,1,0:T(8,128)(2,1)S(1)}, u32[]{:S(2)}, u32[]{:S(2)}) collective-permute-start(bf16[4,1,4,32,768]{4,3,2,1,0:T(8,128)(2,1)S(1)} %bitcast.12), channel_id=1, source_target_pairs={{0,4},{4,0},{8,12},{12,8},{16,20},{20,16},{24,28},{28,24},{1,5},{5... | collective-permute-start | bytes 2359304 | tf_op jit(solution)/shard_map/ppermute | solution.py:34
  76.7 4.4 %outputs.4 = (bf16[1,8,192,3072]{3,2,1,0:T(8,128)(2,1)}, bf16[8,96,3072]{2,1,0:T(8,128)(2,1)}, f32[8,128]{1,0:T(8,128)}) custom-call(s32[8]{0:T(128)S(1)} %stack.34.pos, s32[8]{0:T(128)S(1)} %copy-done.3, bf16[8,192,3072]{2,1,0:T(8,128)(2,1)S(1)} %get-tuple-element.37.comp_ref, ...), custom_call_target="tpu_custom_call", output_to_operand_aliasing={{0}: (7, {}), {1}: (8, {})} | custom-call | flops 1000 | bytes 1000 | tf_op jit(solution)/shard_map/outputs/pallas_call | solution.py:465
  81.1 6.3 %outputs.5 = (bf16[1,8,192,3072]{3,2,1,0:T(8,128)(2,1)}, bf16[8,96,3072]{2,1,0:T(8,128)(2,1)}, f32[1,2,96,3072]{3,2,1,0:T(8,128)}, f32[1,2,96,3072]{3,2,1,0:T(8,128)}, f32[8,128]{1,0:T(8,128)}) custom-call(s32[8]{0:T(128)S(1)} %stack.34.pos, s32[8]{0:T(128)S(1)} %copy-done.3, ...), custom_call_target="tpu_custom_call", output_to_operand_aliasing={{0}: (10, {}), {1}: (11, {})} | custom-call | flops 1000 | bytes 1000 | tf_op jit(solution)/shard_map/outputs/pallas_call | solution.py:465
  (46 shorter events, 5.9 us)
Async XLA Ops:
  0.8 6.3 %copy-start.2 = (f32[1,2688]{1,0:T(1,128)S(1)}, f32[1,2688]{1,0:T(1,128)}, u32[]{:S(2)}) copy-start(f32[1,2688]{1,0:T(1,128)} %vec_ref.1) | copy-start | bytes 32260
  3.8 29.1 %collective-permute-start.7 = (bf16[2,96,3072]{2,1,0:T(8,128)(2,1)S(1)}, bf16[2,96,3072]{2,1,0:T(8,128)(2,1)S(1)}, u32[]{:S(2)}, u32[]{:S(2)}) collective-permute-start(bf16[2,96,3072]{2,1,0:T(8,128)(2,1)S(1)} %get-tuple-element.43.refs_0_), channel_id=1, source_target_pairs={{0,2},{1,3},{2,0},{3,1},{4,6},{5,7},{6,4},{7,5},{8,10},{9,11},{10,... | collective-permute-start | bytes 3538952 | tf_op jit(solution)/shard_map/ppermute | solution.py:34
  5.9 27.0 %collective-permute-start.6 = (bf16[2,96,3072]{2,1,0:T(8,128)(2,1)S(1)}, bf16[2,96,3072]{2,1,0:T(8,128)(2,1)S(1)}, u32[]{:S(2)}, u32[]{:S(2)}) collective-permute-start(bf16[2,96,3072]{2,1,0:T(8,128)(2,1)S(1)} %get-tuple-element.43.refs_0_), channel_id=1, source_target_pairs={{0,1},{1,0},{2,3},{3,2},{4,5},{5,4},{6,7},{7,6},{8,9},{9,8},{10,11... | collective-permute-start | bytes 3538952 | tf_op jit(solution)/shard_map/ppermute | solution.py:34
  7.1 21.6 %copy-start = (f32[8,32,32]{2,1,0:T(8,128)S(1)}, f32[8,32,32]{2,1,0:T(8,128)}, u32[]{:S(2)}) copy-start(f32[8,32,32]{2,1,0:T(8,128)} %gram_ref.1) | copy-start | bytes 98308
  15.9 2.3 %collective-permute-start = (f32[112,256]{1,0:T(8,128)S(1)}, f32[112,256]{1,0:T(8,128)S(1)}, u32[]{:S(2)}, u32[]{:S(2)}) collective-permute-start(f32[112,256]{1,0:T(8,128)S(1)} %get-tuple-element.39), channel_id=1, source_target_pairs={{0,4},{4,0},{8,12},{12,8},{16,20},{20,16},{24,28},{28,24},{1,5},{5... | collective-permute-start | bytes 344072 | tf_op jit(solution)/shard_map/ppermute | solution.py:34
  18.2 5.1 %collective-permute-start.3 = (bf16[112,256]{1,0:T(8,128)(2,1)S(1)}, bf16[112,256]{1,0:T(8,128)(2,1)S(1)}, u32[]{:S(2)}, u32[]{:S(2)}) collective-permute-start(bf16[112,256]{1,0:T(8,128)(2,1)S(1)} %add.27.refs_0_), channel_id=1, source_target_pairs={{0,24},{4,28},{8,16},{12,20},{16,8},{20,12},{24,0},{28,4},{1,25},{... | collective-permute-start | bytes 172040 | tf_op jit(solution)/shard_map/ppermute | solution.py:34
  21.6 5.1 %collective-permute-start.2 = (bf16[112,256]{1,0:T(8,128)(2,1)S(1)}, bf16[112,256]{1,0:T(8,128)(2,1)S(1)}, u32[]{:S(2)}, u32[]{:S(2)}) collective-permute-start(bf16[112,256]{1,0:T(8,128)(2,1)S(1)} %add.27.refs_0_), channel_id=1, source_target_pairs={{0,16},{4,20},{8,24},{12,28},{16,0},{20,4},{24,8},{28,12},{1,17},{... | collective-permute-start | bytes 172040 | tf_op jit(solution)/shard_map/ppermute | solution.py:34
  21.6 5.1 %collective-permute-start.1 = (bf16[112,256]{1,0:T(8,128)(2,1)S(1)}, bf16[112,256]{1,0:T(8,128)(2,1)S(1)}, u32[]{:S(2)}, u32[]{:S(2)}) collective-permute-start(bf16[112,256]{1,0:T(8,128)(2,1)S(1)} %add.27.refs_0_), channel_id=1, source_target_pairs={{0,8},{4,12},{8,0},{12,4},{16,24},{20,28},{24,16},{28,20},{1,9},{5... | collective-permute-start | bytes 172040 | tf_op jit(solution)/shard_map/ppermute | solution.py:34
  26.7 2.0 %collective-permute-start.4 = (f32[112,256]{1,0:T(8,128)S(1)}, f32[112,256]{1,0:T(8,128)S(1)}, u32[]{:S(2)}, u32[]{:S(2)}) collective-permute-start(f32[112,256]{1,0:T(8,128)S(1)} %add.28.near_ref), channel_id=1, source_target_pairs={{0,4},{4,0},{8,12},{12,8},{16,20},{20,16},{24,28},{28,24},{1,5},{5... | collective-permute-start | bytes 344072 | tf_op jit(solution)/shard_map/ppermute | solution.py:34
  30.9 2.4 %collective-permute-start.5 = (bf16[4,1,32,3072]{3,2,1,0:T(8,128)(2,1)S(1)}, bf16[4,1,32,3072]{3,2,1,0:T(8,128)(2,1)S(1)}, u32[]{:S(2)}, u32[]{:S(2)}) collective-permute-start(bf16[4,1,32,3072]{3,2,1,0:T(8,128)(2,1)S(1)} %get-tuple-element.42), channel_id=1, source_target_pairs={{0,4},{4,0},{8,12},{12,8},{16,20},{20,16},{24,28},{28,24},{1,5},{5... | collective-permute-start | bytes 2359304 | tf_op jit(solution)/shard_map/ppermute | solution.py:34
  34.1 25.7 %copy-start.4 = (f32[2688]{0:T(1024)S(1)}, f32[2688]{0:T(1024)}, u32[]{:S(2)}) copy-start(f32[2688]{0:T(1024)} %param.19) | copy-start | bytes 32260
  34.1 25.7 %copy-start.5 = (f32[2688]{0:T(1024)S(1)}, f32[2688]{0:T(1024)}, u32[]{:S(2)}) copy-start(f32[2688]{0:T(1024)} %param.18) | copy-start | bytes 32260
  34.1 6.5 %collective-permute-start.8 = (bf16[40,3072]{1,0:T(8,128)(2,1)S(1)}, bf16[40,3072]{1,0:T(8,128)(2,1)S(1)}, u32[]{:S(2)}, u32[]{:S(2)}) collective-permute-start(bf16[40,3072]{1,0:T(8,128)(2,1)S(1)} %get-tuple-element.46), channel_id=1, source_target_pairs={{0,1},{1,0},{2,3},{3,2},{4,5},{5,4},{6,7},{7,6},{8,9},{9,8},{10,11... | collective-permute-start | bytes 737288 | tf_op jit(solution)/shard_map/ppermute | solution.py:34
  34.6 6.0 %collective-permute-start.9 = (bf16[40,3072]{1,0:T(8,128)(2,1)S(1)}, bf16[40,3072]{1,0:T(8,128)(2,1)S(1)}, u32[]{:S(2)}, u32[]{:S(2)}) collective-permute-start(bf16[40,3072]{1,0:T(8,128)(2,1)S(1)} %get-tuple-element.47), channel_id=1, source_target_pairs={{0,2},{1,3},{2,0},{3,1},{4,6},{5,7},{6,4},{7,5},{8,10},{9,11},{10,... | collective-permute-start | bytes 737288 | tf_op jit(solution)/shard_map/ppermute | solution.py:34
  34.9 11.1 %collective-permute-start.10 = (bf16[40,3072]{1,0:T(8,128)(2,1)S(1)}, bf16[40,3072]{1,0:T(8,128)(2,1)S(1)}, u32[]{:S(2)}, u32[]{:S(2)}) collective-permute-start(bf16[40,3072]{1,0:T(8,128)(2,1)S(1)} %get-tuple-element.48), channel_id=1, source_target_pairs={{0,3},{1,2},{2,1},{3,0},{4,7},{5,6},{6,5},{7,4},{8,11},{9,10},{10,... | collective-permute-start | bytes 737288 | tf_op jit(solution)/shard_map/ppermute | solution.py:34
  46.9 14.9 %collective-permute-start.11 = (bf16[1,96,3072]{2,1,0:T(8,128)(2,1)S(1)}, bf16[1,96,3072]{2,1,0:T(8,128)(2,1)S(1)}, u32[]{:S(2)}, u32[]{:S(2)}) collective-permute-start(bf16[1,96,3072]{2,1,0:T(8,128)(2,1)S(1)} %get-tuple-element.50), channel_id=1, source_target_pairs={{0,2},{1,3},{2,0},{3,1},{4,6},{5,7},{6,4},{7,5},{8,10},{9,11},{10,... | collective-permute-start | bytes 1769480 | tf_op jit(solution)/shard_map/ppermute | solution.py:34
  48.0 13.9 %collective-permute-start.12 = (bf16[1,96,3072]{2,1,0:T(8,128)(2,1)S(1)}, bf16[1,96,3072]{2,1,0:T(8,128)(2,1)S(1)}, u32[]{:S(2)}, u32[]{:S(2)}) collective-permute-start(bf16[1,96,3072]{2,1,0:T(8,128)(2,1)S(1)} %get-tuple-element.51), channel_id=1, source_target_pairs={{0,1},{1,0},{2,3},{3,2},{4,5},{5,4},{6,7},{7,6},{8,9},{9,8},{10,11... | collective-permute-start | bytes 1769480 | tf_op jit(solution)/shard_map/ppermute | solution.py:34
  48.0 3.6 %collective-permute-start.13 = (bf16[32,768]{1,0:T(8,128)(2,1)S(1)}, bf16[32,768]{1,0:T(8,128)(2,1)S(1)}, u32[]{:S(2)}, u32[]{:S(2)}) collective-permute-start(bf16[32,768]{1,0:T(8,128)(2,1)S(1)} %get-tuple-element.53), channel_id=1, source_target_pairs={{0,8},{4,12},{8,0},{12,4},{16,24},{20,28},{24,16},{28,20},{1,9},{5... | collective-permute-start | bytes 147464 | tf_op jit(solution)/shard_map/ppermute | solution.py:34
  48.9 4.4 %collective-permute-start.14 = (bf16[32,768]{1,0:T(8,128)(2,1)S(1)}, bf16[32,768]{1,0:T(8,128)(2,1)S(1)}, u32[]{:S(2)}, u32[]{:S(2)}) collective-permute-start(bf16[32,768]{1,0:T(8,128)(2,1)S(1)} %get-tuple-element.54), channel_id=1, source_target_pairs={{0,16},{4,20},{8,24},{12,28},{16,0},{20,4},{24,8},{28,12},{1,17},{... | collective-permute-start | bytes 147464 | tf_op jit(solution)/shard_map/ppermute | solution.py:34
  51.2 4.9 %collective-permute-start.15 = (bf16[32,768]{1,0:T(8,128)(2,1)S(1)}, bf16[32,768]{1,0:T(8,128)(2,1)S(1)}, u32[]{:S(2)}, u32[]{:S(2)}) collective-permute-start(bf16[32,768]{1,0:T(8,128)(2,1)S(1)} %get-tuple-element.55), channel_id=1, source_target_pairs={{0,24},{4,28},{8,16},{12,20},{16,8},{20,12},{24,0},{28,4},{1,25},{... | collective-permute-start | bytes 147464 | tf_op jit(solution)/shard_map/ppermute | solution.py:34
  56.1 4.8 %collective-permute-start.18 = (bf16[32,768]{1,0:T(8,128)(2,1)S(1)}, bf16[32,768]{1,0:T(8,128)(2,1)S(1)}, u32[]{:S(2)}, u32[]{:S(2)}) collective-permute-start(bf16[32,768]{1,0:T(8,128)(2,1)S(1)} %add.29.refs_0_), channel_id=1, source_target_pairs={{0,24},{4,28},{8,16},{12,20},{16,8},{20,12},{24,0},{28,4},{1,25},{... | collective-permute-start | bytes 147464 | tf_op jit(solution)/shard_map/ppermute | solution.py:34
  56.6 5.3 %collective-permute-start.17 = (bf16[32,768]{1,0:T(8,128)(2,1)S(1)}, bf16[32,768]{1,0:T(8,128)(2,1)S(1)}, u32[]{:S(2)}, u32[]{:S(2)}) collective-permute-start(bf16[32,768]{1,0:T(8,128)(2,1)S(1)} %add.29.refs_0_), channel_id=1, source_target_pairs={{0,16},{4,20},{8,24},{12,28},{16,0},{20,4},{24,8},{28,12},{1,17},{... | collective-permute-start | bytes 147464 | tf_op jit(solution)/shard_map/ppermute | solution.py:34
  56.6 5.3 %collective-permute-start.16 = (bf16[32,768]{1,0:T(8,128)(2,1)S(1)}, bf16[32,768]{1,0:T(8,128)(2,1)S(1)}, u32[]{:S(2)}, u32[]{:S(2)}) collective-permute-start(bf16[32,768]{1,0:T(8,128)(2,1)S(1)} %add.29.refs_0_), channel_id=1, source_target_pairs={{0,8},{4,12},{8,0},{12,4},{16,24},{20,28},{24,16},{28,20},{1,9},{5... | collective-permute-start | bytes 147464 | tf_op jit(solution)/shard_map/ppermute | solution.py:34
  60.4 4.6 %copy-start.1 = (f32[2688]{0:T(1024)}, f32[2688]{0:T(1024)S(1)}, u32[]{:S(2)}) copy-start(f32[2688]{0:T(1024)S(1)} %get-tuple-element.68.refs_6_) | copy-start | bytes 32260
  61.9 3.0 %copy-start.3 = (s32[8]{0:T(128)S(1)}, s32[8]{0:T(128)}, u32[]{:S(2)}) copy-start(s32[8]{0:T(128)} %owners.5) | copy-start | bytes 100
  61.9 5.6 %collective-permute-start.21 = (bf16[4,32,768]{2,1,0:T(8,128)(2,1)S(1)}, bf16[4,32,768]{2,1,0:T(8,128)(2,1)S(1)}, u32[]{:S(2)}, u32[]{:S(2)}) collective-permute-start(bf16[4,32,768]{2,1,0:T(8,128)(2,1)S(1)} %stack.35.refs_0_), channel_id=1, source_target_pairs={{0,3},{1,2},{2,1},{3,0},{4,7},{5,6},{6,5},{7,4},{8,11},{9,10},{10,... | collective-permute-start | bytes 589832 | tf_op jit(solution)/shard_map/ppermute | solution.py:34
  62.9 6.6 %collective-permute-start.20 = (bf16[4,32,768]{2,1,0:T(8,128)(2,1)S(1)}, bf16[4,32,768]{2,1,0:T(8,128)(2,1)S(1)}, u32[]{:S(2)}, u32[]{:S(2)}) collective-permute-start(bf16[4,32,768]{2,1,0:T(8,128)(2,1)S(1)} %stack.35.refs_0_), channel_id=1, source_target_pairs={{0,2},{1,3},{2,0},{3,1},{4,6},{5,7},{6,4},{7,5},{8,10},{9,11},{10,... | collective-permute-start | bytes 589832 | tf_op jit(solution)/shard_map/ppermute | solution.py:34
  63.8 5.7 %collective-permute-start.19 = (bf16[4,32,768]{2,1,0:T(8,128)(2,1)S(1)}, bf16[4,32,768]{2,1,0:T(8,128)(2,1)S(1)}, u32[]{:S(2)}, u32[]{:S(2)}) collective-permute-start(bf16[4,32,768]{2,1,0:T(8,128)(2,1)S(1)} %stack.35.refs_0_), channel_id=1, source_target_pairs={{0,1},{1,0},{2,3},{3,2},{4,5},{5,4},{6,7},{7,6},{8,9},{9,8},{10,11... | collective-permute-start | bytes 589832 | tf_op jit(solution)/shard_map/ppermute | solution.py:34
  69.5 11.6 %collective-permute-start.22 = (bf16[4,1,4,32,768]{4,3,2,1,0:T(8,128)(2,1)S(1)}, bf16[4,1,4,32,768]{4,3,2,1,0:T(8,128)(2,1)S(1)}, u32[]{:S(2)}, u32[]{:S(2)}) collective-permute-start(bf16[4,1,4,32,768]{4,3,2,1,0:T(8,128)(2,1)S(1)} %bitcast.12), channel_id=1, source_target_pairs={{0,4},{4,0},{8,12},{12,8},{16,20},{20,16},{24,28},{28,24},{1,5},{5... | collective-permute-start | bytes 2359304 | tf_op jit(solution)/shard_map/ppermute | solution.py:34

commit v11 on v10

--- a/solution.py
+++ b/solution.py
@@ -10,7 +10,6 @@
 CORES = 2
 AHEAD = 8
 BASE_ROWS = 48
-COLUMNS = 384
 F32 = jnp.float32
 BF16 = jnp.bfloat16
 
@@ -119,7 +118,7 @@
     )(*parts)
 
 
-def send_kernel(half, pos, near_ref, far_ref, gram_ref, comp_ref, send_ref, lt_ref, mix_ref, vec_ref, left, gram):
+def send_kernel(half, pos, near_ref, far_ref, gram_ref, comp_ref, send_ref, lt_ref, left_ref, vec_ref, left, gram):
     nmat, rows, _ = comp_ref.shape
     rank = gram_ref.shape[1]
     part = near_ref.shape[0]
@@ -133,16 +132,9 @@
         left[:rows, :], gram[...], precision=lax.Precision.HIGHEST, preferred_element_type=F32
     )
     lt_ref[...] = hat.T.astype(BF16)
-    mix_ref[:, :, :rows] = jnp.broadcast_to(unit_matrix(rows), (nmat, rows, rows))
     for i in range(nmat):
-        mix_ref[i, :, rows:] = -hat[:, i * rank : (i + 1) * rank].astype(BF16)
+        left_ref[i] = hat[:, i * rank : (i + 1) * rank].astype(BF16)
     right_rows(half, pos, lt_ref, comp_ref, send_ref)
-
-
-def unit_matrix(size):
-    row = lax.broadcasted_iota(jnp.int32, (size, size), 0)
-    col = lax.broadcasted_iota(jnp.int32, (size, size), 1)
-    return jnp.where(row == col, 1.0, 0.0).astype(BF16)
 
 
 def right_rows(start, pos, lt_ref, comp_ref, out_ref):
@@ -167,7 +159,7 @@
     total = CORES * near.shape[0]
     shape = (half, upm, rank // upm, n)
     vmem = pl.BlockSpec(memory_space=pltpu.VMEM)
-    send, lt, mix, vec = pl.pallas_call(
+    send, lt, left, vec = pl.pallas_call(
         functools.partial(send_kernel, half),
         grid_spec=pltpu.PrefetchScalarGridSpec(
             num_scalar_prefetch=1,
@@ -179,7 +171,7 @@
         out_shape=[
             jax.ShapeDtypeStruct(shape, BF16),
             jax.ShapeDtypeStruct((width, rows), BF16),
-            jax.ShapeDtypeStruct((nmat, rows, rows + rank), BF16),
+            jax.ShapeDtypeStruct((nmat, rows, rank), BF16),
             jax.ShapeDtypeStruct((total - rows, width), F32),
         ],
         compiler_params=params(),
@@ -199,7 +191,7 @@
         cost_estimate=cost(),
         name="right_keep",
     )(pos, lt, comp, *after)
-    return send, keep, lt, mix, vec
+    return send, keep, lt, left, vec
 
 
 def chip_kernel(replica_rows, pos, keep_ref, recv_ref, lt_ref, *refs):
@@ -244,7 +236,7 @@
 
 def plane_kernel(pos, own_ref, strip_ref, *refs):
     n_z = own_ref.shape[1] // refs[-2].shape[1]
-    terms, outs, mix_ref = refs[: -n_z - 1], refs[-n_z - 1 : -1], refs[-1]
+    terms, outs, left_ref = refs[: -n_z - 1], refs[-n_z - 1 : -1], refs[-1]
     unit, n = own_ref.shape
     cols = n // n_z
     for d, out in enumerate(outs):
@@ -254,24 +246,19 @@
     strip = strip_ref[...]
     for d, term in enumerate(terms, 1):
         strip = jnp.where(pos[7] == d, term[...].astype(F32)[unit:], strip)
-    nmat, count, depth = mix_ref.shape
-    rank = (depth - count) // 2
+    nmat, _, rank = left_ref.shape
     width = nmat * rank
     rows = [strip[:, i * width : (i + 1) * width] for i in range(n // width)]
-    rows = -0.1 * jnp.concatenate(rows, axis=0)
-    high = rows.astype(BF16)
-    low = (rows - high.astype(F32)).astype(BF16)
-    mix_ref[:, :, :count] = jnp.broadcast_to(unit_matrix(count), (nmat, count, count))
+    rows = jnp.concatenate(rows, axis=0).astype(BF16)
     for i in range(nmat):
-        mix_ref[i, :, count : count + rank] = high[:, i * rank : (i + 1) * rank]
-        mix_ref[i, :, count + rank :] = low[:, i * rank : (i + 1) * rank]
+        left_ref[i] = rows[:, i * rank : (i + 1) * rank]
 
 
 def plane_sum(pos, own, strip, terms, n_z, nmat, rank):
     unit, n = own.shape
     count = strip.size // (nmat * rank)
     outs = [jax.ShapeDtypeStruct((unit, n // n_z), BF16 if d else F32) for d in range(n_z)]
-    outs.append(jax.ShapeDtypeStruct((nmat, count, count + 2 * rank), BF16))
+    outs.append(jax.ShapeDtypeStruct((nmat, count, rank), BF16))
     vmem = pl.BlockSpec(memory_space=pltpu.VMEM)
     return pl.pallas_call(
         plane_kernel,
@@ -365,7 +352,7 @@
     )(*bases)
 
 
-def outputs_kernel(jobs, where, capacity, pos, owners, comp_ref, mix_ref, mixr_ref, base_ref, *refs):
+def outputs_kernel(jobs, where, capacity, pos, owners, comp_ref, left_ref, strip_ref, base_ref, *refs):
     n_right = 1 + max(a for a, _ in (where or jobs).values())
     rights, refs = refs[:n_right], refs[n_right:]
     n_scratch = 6 if where else 3
@@ -376,7 +363,6 @@
     token_ref[...] = jnp.zeros(token_ref.shape, F32)
     _, upm, n_z, _, cols = rights[0].shape
     half = comp_ref.shape[0] // CORES
-    count = weights.shape[1]
 
     def right_of(place, d, block):
         a, entry = place
@@ -389,7 +375,8 @@
     def matrix(other, j):
         return (j + half * other) ^ pos[0]
 
-    pieces = [slice(first, first + COLUMNS) for first in range(0, cols, COLUMNS)]
+    step = 256 if cols % 256 == 0 else 128
+    pieces = [slice(first, first + step) for first in range(0, cols, step)]
     stores = []
 
     def store(source, target, sem):
@@ -404,17 +391,16 @@
             for k in range(owners.shape[0]):
                 mine = jnp.where((owners[k] == pos[5]) & (rank_of(owners, k) == c), k, mine)
             safe = jnp.maximum(mine, 0)
-            mixr = mixr_ref[safe][:, count:]
+            strip = strip_ref[safe]
             for d in range(n_z):
                 for block in pieces:
-                    right = jnp.zeros((mixr.shape[1] // 2, COLUMNS), BF16)
+                    right = jnp.zeros((strip.shape[1], step), BF16)
                     for job, place in where.items():
                         right = jnp.where(safe == matrix(*job), right_of(place, d, block), right)
-                    both = jnp.concatenate([right, right], axis=0)
-                    change = jnp.dot(mixr, both, preferred_element_type=F32)
-                    change = jnp.where(mine >= 0, 10.0 * change, 0.0)
-                    place = columns(d, block.start, COLUMNS)
-                    momentum = 0.9 * momentum_ref[c, :, place] - change
+                    approx = jnp.dot(strip, right, preferred_element_type=F32)
+                    approx = jnp.where(mine >= 0, approx, 0.0)
+                    place = columns(d, block.start, step)
+                    momentum = 0.9 * momentum_ref[c, :, place] + approx
                     new_momentum[c, :, place] = momentum
                     new_master[c, :, place] = master_ref[c, :, place] - 0.1 * momentum
                 place = columns(d)
@@ -426,15 +412,16 @@
     for i, (job, where_right) in enumerate(jobs.items()):
         k = matrix(*job)
         slot = (owners[k] ^ pos[5]) * capacity + rank_of(owners, k)
-        mix, mixr = mix_ref[k], mixr_ref[k]
+        left, strip = left_ref[k], strip_ref[k]
         for d in range(n_z):
             for block in pieces:
                 right = right_of(where_right, d, block)
-                place = columns(d, block.start, COLUMNS)
-                both = jnp.concatenate([comp_ref[k, :, place], right], axis=0)
-                feedback[i, :, place] = jnp.dot(mix, both, preferred_element_type=F32).astype(BF16)
-                both = jnp.concatenate([base_ref[slot, :, place], right, right], axis=0)
-                weights[i, :, place] = jnp.dot(mixr, both, preferred_element_type=F32).astype(BF16)
+                place = columns(d, block.start, step)
+                approx = jnp.dot(left, right, preferred_element_type=F32)
+                feedback[i, :, place] = (comp_ref[k, :, place].astype(F32) - approx).astype(BF16)
+                approx = jnp.dot(strip, right, preferred_element_type=F32)
+                base = base_ref[slot, :, place].astype(F32)
+                weights[i, :, place] = (base - 0.1 * approx).astype(BF16)
             place = columns(d)
             store(feedback.at[i, :, place], outs[0].at[0, k, :, place], out_sem.at[i, d, 0])
             store(weights.at[i, :, place], outs[1].at[k, :, place], out_sem.at[i, d, 1])
@@ -443,7 +430,7 @@
         copy.wait()
 
 
-def outputs(pos, owners, comp, mix, mixr, base, capacity, rights, jobs, where=None, states=(), earlier=()):
+def outputs(pos, owners, comp, left, strip, base, capacity, rights, jobs, where=None, states=(), earlier=()):
     nmat, rows, n = comp.shape
     n_z = rights[0].shape[2]
     replica_rows = base.shape[1]
@@ -476,7 +463,7 @@
         compiler_params=params(24),
         cost_estimate=cost(),
         name="outputs",
-    )(pos, owners, comp, mix, mixr, base, *rights, *states, *earlier)
+    )(pos, owners, comp, left, strip, base, *rights, *states, *earlier)
 
 
 def base_kernel(pos, momentum_ref, master_ref, *refs):
@@ -571,15 +558,15 @@
     piece = add([piece] + along_z(piece), F32)
     near, far = piece, exchange(piece, "replica", 1)
 
-    send, keep, lt, mix, vector_rows = right_terms(pos, near, far, gram_root, comp, upm, [])
+    send, keep, lt, left, vector_rows = right_terms(pos, near, far, gram_root, comp, upm, [])
     vector_total = vector_rows.reshape(-1)[:nvec]
     recv = exchange(send, "replica", 1)
     own, strip, *chip = chip_sum(pos, keep, recv, lt, replica_rows, [token([keep] + early)])
     plane = [exchange(part, "mp", d) for d, part in enumerate(chip, 1)]
-    *final, mixr = plane_sum(pos, own, strip, plane, n_z, nmat, rank)
+    *final, mine = plane_sum(pos, own, strip, plane, n_z, nmat, rank)
     late = []
     if square:
-        parts = forward(early, [0, 1], 1, mixr)
+        parts = forward(early, [0, 1], 1, mine)
         late = [exchange(part, "mp", 2 - i) for i, part in enumerate(parts)]
         bases = bases + late
         places[3, 0], places[3, 1] = (3, 0), (4, 0)
@@ -591,7 +578,7 @@
     whole = stack([final] + along_z(final), late + [new_vector_params])
     others = [exchange(whole, "mp", d) for d in range(1, n_mp)]
     slots = collect(bases, [places[d, c] for d in range(n_mp) for c in range(capacity)])
-    common = (pos, owners, comp, mix, mixr, slots, capacity)
+    common = (pos, owners, comp, left, mine, slots, capacity)
     shape = (half, upm) + whole.shape
     done, near_jobs, after = (), {(0, j): (0, j) for j in range(half)}, [slots]
     if upm == 1:

time: 87.7 us -> 86.9 us (level)
  no operation moved by 1% of the time
where the time goes in v11:
time: 86.9 us; the launch traced here: 86.8 us
  starting transfers between devices  30.7 us (35%)
  Pallas kernels  29.8 us (34%)
  waiting for transfers between devices  24.7 us (28%)
  between operations  0.88 us (1%)
    ppermute x23, starting transfers between devices, exchange(): return lax.ppermute(x, axis, [(i, i ^ distance) for i in range(size)])  30.7 us
    ppermute x23, waiting for transfers between devices, exchange(): return lax.ppermute(x, axis, [(i, i ^ distance) for i in range(size)])  24.7 us
    pallas_call x3, Pallas kernels, outputs(): pl.pallas_call(functools.partial(outputs_kernel, jobs, where, capacity),...  12.2 us
    pallas_call x1, Pallas kernels, left_terms(): pl.pallas_call(left_kernel, grid_spec=pltpu.PrefetchScalarGridSpec(num_sc...  8.78 us
    pallas_call x1, Pallas kernels, base_of(): pl.pallas_call(base_kernel, grid_spec=pltpu.PrefetchScalarGridSpec(num_sc...  2.99 us
    pallas_call x1, Pallas kernels, right_terms(): pl.pallas_call(functools.partial(send_kernel, half), grid_spec=pltpu.Pref...  2.22 us
  transfers between devices with their start and end apart: 23, of which 13 were waited for; matrix products, arithmetic and copies ran while one was open for 1% of the time, Pallas kernels for 22%

profile of v11, /device:TPU:1, one launch (start us, length us, event | category | flops | bytes accessed | tf_op | source)
XLA Modules:
  0.0 86.8 jit_solution(2071132606777471004)
XLA Ops:
  0.8 3.0 %base.1 = (bf16[2,96,3072]{2,1,0:T(8,128)(2,1)S(1)}, f32[2,96,3072]{2,1,0:T(8,128)S(1)}, f32[2,96,3072]{2,1,0:T(8,128)S(1)}) custom-call(s32[8]{0:T(128)S(1)} %stack.34.pos, f32[1,2,96,3072]{3,2,1,0:T(8,128)} %momentum_ref.1, f32[1,2,96,3072]{3,2,1,0:T(8,128)} %master_ref.1), custom_call_target="tpu_custom_call" | custom-call | flops 1000 | bytes 1000 | tf_op jit(solution)/shard_map/base/pallas_call | solution.py:495
  3.8 2.1 %collective-permute-start.7 = (bf16[2,96,3072]{2,1,0:T(8,128)(2,1)S(1)}, bf16[2,96,3072]{2,1,0:T(8,128)(2,1)S(1)}, u32[]{:S(2)}, u32[]{:S(2)}) collective-permute-start(bf16[2,96,3072]{2,1,0:T(8,128)(2,1)S(1)} %get-tuple-element.43.refs_0_), channel_id=1, source_target_pairs={{0,2},{1,3},{2,0},{3,1},{4,6},{5,7},{6,4},{7,5},{8,10},{9,11},{10,... | collective-permute-start | bytes 3538952 | tf_op jit(solution)/shard_map/ppermute | solution.py:33
  5.9 1.2 %collective-permute-start.6 = (bf16[2,96,3072]{2,1,0:T(8,128)(2,1)S(1)}, bf16[2,96,3072]{2,1,0:T(8,128)(2,1)S(1)}, u32[]{:S(2)}, u32[]{:S(2)}) collective-permute-start(bf16[2,96,3072]{2,1,0:T(8,128)(2,1)S(1)} %get-tuple-element.43.refs_0_), channel_id=1, source_target_pairs={{0,1},{1,0},{2,3},{3,2},{4,5},{5,4},{6,7},{7,6},{8,9},{9,8},{10,11... | collective-permute-start | bytes 3538952 | tf_op jit(solution)/shard_map/ppermute | solution.py:33
  7.1 8.8 %left_terms.1 = (bf16[8,192,3072]{2,1,0:T(8,128)(2,1)S(1)}, f32[112,256]{1,0:T(8,128)S(1)}, f32[112,256]{1,0:T(8,128)S(1)}) custom-call(s32[8]{0:T(128)S(1)} %stack.34.pos, bf16[1,8,192,3072]{3,2,1,0:T(8,128)(2,1)} %g_ref.1, bf16[1,8,192,3072]{3,2,1,0:T(8,128)(2,1)} %f_ref.1, bf16[8,32,3072]{2,1,0:T(8,128)(2,1)} %bitcast.17, f32[1,2688]{1,0:T(1,128)S(1)} %copy-done.2), custom_call_target="tpu_custom_call" | custom-call | flops 1000 | bytes 1000 | tf_op jit(solution)/shard_map/left_terms/pallas_call | solution.py:82
  15.9 1.3 %collective-permute-start = (f32[112,256]{1,0:T(8,128)S(1)}, f32[112,256]{1,0:T(8,128)S(1)}, u32[]{:S(2)}, u32[]{:S(2)}) collective-permute-start(f32[112,256]{1,0:T(8,128)S(1)} %get-tuple-element.39), channel_id=1, source_target_pairs={{0,4},{4,0},{8,12},{12,8},{16,20},{20,16},{24,28},{28,24},{1,5},{5... | collective-permute-start | bytes 344072 | tf_op jit(solution)/shard_map/ppermute | solution.py:33
  17.2 1.0 %collective-permute-done.refs_1_ = f32[112,256]{1,0:T(8,128)S(1)} collective-permute-done((f32[112,256]{1,0:T(8,128)S(1)}, f32[112,256]{1,0:T(8,128)S(1)}, u32[]{:S(2)}, u32[]{:S(2)}) %collective-permute-start) | collective-permute-done | bytes 114720 | tf_op jit(solution)/shard_map/ppermute | solution.py:33
  18.2 3.4 %collective-permute-start.3 = (bf16[112,256]{1,0:T(8,128)(2,1)S(1)}, bf16[112,256]{1,0:T(8,128)(2,1)S(1)}, u32[]{:S(2)}, u32[]{:S(2)}) collective-permute-start(bf16[112,256]{1,0:T(8,128)(2,1)S(1)} %add.27.refs_0_), channel_id=1, source_target_pairs={{0,24},{4,28},{8,16},{12,20},{16,8},{20,12},{24,0},{28,4},{1,25},{... | collective-permute-start | bytes 172040 | tf_op jit(solution)/shard_map/ppermute | solution.py:33
  22.0 1.3 %collective-permute-done.3.refs_3_ = bf16[112,256]{1,0:T(8,128)(2,1)S(1)} collective-permute-done((bf16[112,256]{1,0:T(8,128)(2,1)S(1)}, bf16[112,256]{1,0:T(8,128)(2,1)S(1)}, u32[]{:S(2)}, u32[]{:S(2)}) %collective-permute-start.3) | collective-permute-done | bytes 57376 | tf_op jit(solution)/shard_map/ppermute | solution.py:33
  23.3 3.4 %collective-permute-done.2.refs_2_ = bf16[112,256]{1,0:T(8,128)(2,1)S(1)} collective-permute-done((bf16[112,256]{1,0:T(8,128)(2,1)S(1)}, bf16[112,256]{1,0:T(8,128)(2,1)S(1)}, u32[]{:S(2)}, u32[]{:S(2)}) %collective-permute-start.2) | collective-permute-done | bytes 57376 | tf_op jit(solution)/shard_map/ppermute | solution.py:33
  26.7 1.0 %collective-permute-start.4 = (f32[112,256]{1,0:T(8,128)S(1)}, f32[112,256]{1,0:T(8,128)S(1)}, u32[]{:S(2)}, u32[]{:S(2)}) collective-permute-start(f32[112,256]{1,0:T(8,128)S(1)} %add.28.near_ref), channel_id=1, source_target_pairs={{0,4},{4,0},{8,12},{12,8},{16,20},{20,16},{24,28},{28,24},{1,5},{5... | collective-permute-start | bytes 344072 | tf_op jit(solution)/shard_map/ppermute | solution.py:33
  27.7 1.0 %collective-permute-done.4.far_ref = f32[112,256]{1,0:T(8,128)S(1)} collective-permute-done((f32[112,256]{1,0:T(8,128)S(1)}, f32[112,256]{1,0:T(8,128)S(1)}, u32[]{:S(2)}, u32[]{:S(2)}) %collective-permute-start.4) | collective-permute-done | bytes 114720 | tf_op jit(solution)/shard_map/ppermute | solution.py:33
  28.7 2.2 %right_send.1 = (bf16[4,1,32,3072]{3,2,1,0:T(8,128)(2,1)S(1)}, bf16[256,192]{1,0:T(8,128)(2,1)S(1)}, bf16[8,192,32]{2,1,0:T(8,128)(2,1)S(1)}, f32[32,256]{1,0:T(8,128)S(1)}) custom-call(s32[8]{0:T(128)S(1)} %stack.34.pos, f32[112,256]{1,0:T(8,128)S(1)} %add.28.near_ref, f32[112,256]{1,0:T(8,128)S(1)} %collective-permute-done.4.far_ref, ...), custom_call_target="tpu_custom_call" | custom-call | flops 1000 | bytes 1000 | tf_op jit(solution)/shard_map/right_send/pallas_call | solution.py:162
  31.3 1.5 %right_keep.1.refs_0_.keep_ref = f32[4,1,32,3072]{3,2,1,0:T(8,128)S(1)} custom-call(s32[8]{0:T(128)S(1)} %stack.34.pos, bf16[256,192]{1,0:T(8,128)(2,1)S(1)} %get-tuple-element.41.lt_ref, bf16[8,192,3072]{2,1,0:T(8,128)(2,1)S(1)} %get-tuple-element.37.comp_ref), custom_call_target="tpu_custom_call" | custom-call | flops 1000 | bytes 1000 | tf_op jit(solution)/shard_map/right_keep/pallas_call | solution.py:181
  33.3 0.8 chip_sum.1
  34.9 1.9 %collective-permute-start.10 = (bf16[40,3072]{1,0:T(8,128)(2,1)S(1)}, bf16[40,3072]{1,0:T(8,128)(2,1)S(1)}, u32[]{:S(2)}, u32[]{:S(2)}) collective-permute-start(bf16[40,3072]{1,0:T(8,128)(2,1)S(1)} %get-tuple-element.48), channel_id=1, source_target_pairs={{0,3},{1,2},{2,1},{3,0},{4,7},{5,6},{6,5},{7,4},{8,11},{9,10},{10,... | collective-permute-start | bytes 737288 | tf_op jit(solution)/shard_map/ppermute | solution.py:33
  36.8 3.8 %collective-permute-done.8.refs_0_ = bf16[40,3072]{1,0:T(8,128)(2,1)S(1)} collective-permute-done((bf16[40,3072]{1,0:T(8,128)(2,1)S(1)}, bf16[40,3072]{1,0:T(8,128)(2,1)S(1)}, u32[]{:S(2)}, u32[]{:S(2)}) %collective-permute-start.8) | collective-permute-done | bytes 245792 | tf_op jit(solution)/shard_map/ppermute | solution.py:33
  40.6 5.4 %collective-permute-done.10.refs_2_ = bf16[40,3072]{1,0:T(8,128)(2,1)S(1)} collective-permute-done((bf16[40,3072]{1,0:T(8,128)(2,1)S(1)}, bf16[40,3072]{1,0:T(8,128)(2,1)S(1)}, u32[]{:S(2)}, u32[]{:S(2)}) %collective-permute-start.10) | collective-permute-done | bytes 245792 | tf_op jit(solution)/shard_map/ppermute | solution.py:33
  46.8 1.1 %collective-permute-start.11 = (bf16[1,96,3072]{2,1,0:T(8,128)(2,1)S(1)}, bf16[1,96,3072]{2,1,0:T(8,128)(2,1)S(1)}, u32[]{:S(2)}, u32[]{:S(2)}) collective-permute-start(bf16[1,96,3072]{2,1,0:T(8,128)(2,1)S(1)} %get-tuple-element.50), channel_id=1, source_target_pairs={{0,2},{1,3},{2,0},{3,1},{4,6},{5,7},{6,4},{7,5},{8,10},{9,11},{10,... | collective-permute-start | bytes 1769480 | tf_op jit(solution)/shard_map/ppermute | solution.py:33
  47.9 0.9 collective-permute-start.13
  48.8 2.3 %collective-permute-start.14 = (bf16[32,768]{1,0:T(8,128)(2,1)S(1)}, bf16[32,768]{1,0:T(8,128)(2,1)S(1)}, u32[]{:S(2)}, u32[]{:S(2)}) collective-permute-start(bf16[32,768]{1,0:T(8,128)(2,1)S(1)} %get-tuple-element.54), channel_id=1, source_target_pairs={{0,16},{4,20},{8,24},{12,28},{16,0},{20,4},{24,8},{28,12},{1,17},{... | collective-permute-start | bytes 147464 | tf_op jit(solution)/shard_map/ppermute | solution.py:33
  51.5 1.6 %collective-permute-done.14.refs_2_ = bf16[32,768]{1,0:T(8,128)(2,1)S(1)} collective-permute-done((bf16[32,768]{1,0:T(8,128)(2,1)S(1)}, bf16[32,768]{1,0:T(8,128)(2,1)S(1)}, u32[]{:S(2)}, u32[]{:S(2)}) %collective-permute-start.14) | collective-permute-done | bytes 49184 | tf_op jit(solution)/shard_map/ppermute | solution.py:33
  53.1 2.9 %collective-permute-done.15.refs_3_ = bf16[32,768]{1,0:T(8,128)(2,1)S(1)} collective-permute-done((bf16[32,768]{1,0:T(8,128)(2,1)S(1)}, bf16[32,768]{1,0:T(8,128)(2,1)S(1)}, u32[]{:S(2)}, u32[]{:S(2)}) %collective-permute-start.15) | collective-permute-done | bytes 49184 | tf_op jit(solution)/shard_map/ppermute | solution.py:33
  56.5 3.2 %collective-permute-start.16 = (bf16[32,768]{1,0:T(8,128)(2,1)S(1)}, bf16[32,768]{1,0:T(8,128)(2,1)S(1)}, u32[]{:S(2)}, u32[]{:S(2)}) collective-permute-start(bf16[32,768]{1,0:T(8,128)(2,1)S(1)} %add.29.refs_0_), channel_id=1, source_target_pairs={{0,8},{4,12},{8,0},{12,4},{16,24},{20,28},{24,16},{28,20},{1,9},{5... | collective-permute-start | bytes 147464 | tf_op jit(solution)/shard_map/ppermute | solution.py:33
  60.9 0.9 %collective-permute-done.17.refs_2_ = bf16[32,768]{1,0:T(8,128)(2,1)S(1)} collective-permute-done((bf16[32,768]{1,0:T(8,128)(2,1)S(1)}, bf16[32,768]{1,0:T(8,128)(2,1)S(1)}, u32[]{:S(2)}, u32[]{:S(2)}) %collective-permute-start.17) | collective-permute-done | bytes 49184 | tf_op jit(solution)/shard_map/ppermute | solution.py:33
  61.8 0.9 %collective-permute-start.21 = (bf16[4,32,768]{2,1,0:T(8,128)(2,1)S(1)}, bf16[4,32,768]{2,1,0:T(8,128)(2,1)S(1)}, u32[]{:S(2)}, u32[]{:S(2)}) collective-permute-start(bf16[4,32,768]{2,1,0:T(8,128)(2,1)S(1)} %stack.35.refs_0_), channel_id=1, source_target_pairs={{0,3},{1,2},{2,1},{3,0},{4,7},{5,6},{6,5},{7,4},{8,11},{9,10},{10,... | collective-permute-start | bytes 589832 | tf_op jit(solution)/shard_map/ppermute | solution.py:33
  62.8 0.9 %collective-permute-start.20 = (bf16[4,32,768]{2,1,0:T(8,128)(2,1)S(1)}, bf16[4,32,768]{2,1,0:T(8,128)(2,1)S(1)}, u32[]{:S(2)}, u32[]{:S(2)}) collective-permute-start(bf16[4,32,768]{2,1,0:T(8,128)(2,1)S(1)} %stack.35.refs_0_), channel_id=1, source_target_pairs={{0,2},{1,3},{2,0},{3,1},{4,6},{5,7},{6,4},{7,5},{8,10},{9,11},{10,... | collective-permute-start | bytes 589832 | tf_op jit(solution)/shard_map/ppermute | solution.py:33
  63.7 0.9 collective-permute-start.19
  64.9 2.1 %outputs.3 = (bf16[1,8,192,3072]{3,2,1,0:T(8,128)(2,1)}, bf16[8,96,3072]{2,1,0:T(8,128)(2,1)}, f32[8,128]{1,0:T(8,128)S(1)}) custom-call(s32[8]{0:T(128)S(1)} %stack.34.pos, s32[8]{0:T(128)S(1)} %copy-done.3, bf16[8,192,3072]{2,1,0:T(8,128)(2,1)S(1)} %get-tuple-element.37.comp_ref, bf16[8,192,32]{2,1,0:T(8,128)(2,1)S(1)} %get-tuple-element.40.left_ref, ...), custom_call_target="tpu_custom_call" | custom-call | flops 1000 | bytes 1000 | tf_op jit(solution)/shard_map/outputs/pallas_call | solution.py:452
  67.4 2.0 %collective-permute-done.20.refs_2_ = bf16[4,32,768]{2,1,0:T(8,128)(2,1)S(1)} collective-permute-done((bf16[4,32,768]{2,1,0:T(8,128)(2,1)S(1)}, bf16[4,32,768]{2,1,0:T(8,128)(2,1)S(1)}, u32[]{:S(2)}, u32[]{:S(2)}) %collective-permute-start.20) | collective-permute-done | bytes 196640 | tf_op jit(solution)/shard_map/ppermute | solution.py:33
  69.4 7.2 %collective-permute-start.22 = (bf16[4,1,4,32,768]{4,3,2,1,0:T(8,128)(2,1)S(1)}, bf16[4,1,4,32,768]{4,3,2,1,0:T(8,128)(2,1)S(1)}, u32[]{:S(2)}, u32[]{:S(2)}) collective-permute-start(bf16[4,1,4,32,768]{4,3,2,1,0:T(8,128)(2,1)S(1)} %bitcast.12), channel_id=1, source_target_pairs={{0,4},{4,0},{8,12},{12,8},{16,20},{20,16},{24,28},{28,24},{1,5},{5... | collective-permute-start | bytes 2359304 | tf_op jit(solution)/shard_map/ppermute | solution.py:33
  76.6 3.9 %outputs.4 = (bf16[1,8,192,3072]{3,2,1,0:T(8,128)(2,1)}, bf16[8,96,3072]{2,1,0:T(8,128)(2,1)}, f32[8,128]{1,0:T(8,128)}) custom-call(s32[8]{0:T(128)S(1)} %stack.34.pos, s32[8]{0:T(128)S(1)} %copy-done.3, bf16[8,192,3072]{2,1,0:T(8,128)(2,1)S(1)} %get-tuple-element.37.comp_ref, ...), custom_call_target="tpu_custom_call", output_to_operand_aliasing={{0}: (7, {}), {1}: (8, {})} | custom-call | flops 1000 | bytes 1000 | tf_op jit(solution)/shard_map/outputs/pallas_call | solution.py:452
  80.6 6.2 %outputs.5 = (bf16[1,8,192,3072]{3,2,1,0:T(8,128)(2,1)}, bf16[8,96,3072]{2,1,0:T(8,128)(2,1)}, f32[1,2,96,3072]{3,2,1,0:T(8,128)}, f32[1,2,96,3072]{3,2,1,0:T(8,128)}, f32[8,128]{1,0:T(8,128)}) custom-call(s32[8]{0:T(128)S(1)} %stack.34.pos, s32[8]{0:T(128)S(1)} %copy-done.3, ...), custom_call_target="tpu_custom_call", output_to_operand_aliasing={{0}: (10, {}), {1}: (11, {})} | custom-call | flops 1000 | bytes 1000 | tf_op jit(solution)/shard_map/outputs/pallas_call | solution.py:452
  (46 shorter events, 5.9 us)
Async XLA Ops:
  0.8 6.4 %copy-start.2 = (f32[1,2688]{1,0:T(1,128)S(1)}, f32[1,2688]{1,0:T(1,128)}, u32[]{:S(2)}) copy-start(f32[1,2688]{1,0:T(1,128)} %vec_ref.1) | copy-start | bytes 32260
  3.8 29.1 %collective-permute-start.7 = (bf16[2,96,3072]{2,1,0:T(8,128)(2,1)S(1)}, bf16[2,96,3072]{2,1,0:T(8,128)(2,1)S(1)}, u32[]{:S(2)}, u32[]{:S(2)}) collective-permute-start(bf16[2,96,3072]{2,1,0:T(8,128)(2,1)S(1)} %get-tuple-element.43.refs_0_), channel_id=1, source_target_pairs={{0,2},{1,3},{2,0},{3,1},{4,6},{5,7},{6,4},{7,5},{8,10},{9,11},{10,... | collective-permute-start | bytes 3538952 | tf_op jit(solution)/shard_map/ppermute | solution.py:33
  5.9 27.0 %collective-permute-start.6 = (bf16[2,96,3072]{2,1,0:T(8,128)(2,1)S(1)}, bf16[2,96,3072]{2,1,0:T(8,128)(2,1)S(1)}, u32[]{:S(2)}, u32[]{:S(2)}) collective-permute-start(bf16[2,96,3072]{2,1,0:T(8,128)(2,1)S(1)} %get-tuple-element.43.refs_0_), channel_id=1, source_target_pairs={{0,1},{1,0},{2,3},{3,2},{4,5},{5,4},{6,7},{7,6},{8,9},{9,8},{10,11... | collective-permute-start | bytes 3538952 | tf_op jit(solution)/shard_map/ppermute | solution.py:33
  7.1 21.6 %copy-start = (f32[8,32,32]{2,1,0:T(8,128)S(1)}, f32[8,32,32]{2,1,0:T(8,128)}, u32[]{:S(2)}) copy-start(f32[8,32,32]{2,1,0:T(8,128)} %gram_ref.1) | copy-start | bytes 98308
  15.9 2.3 %collective-permute-start = (f32[112,256]{1,0:T(8,128)S(1)}, f32[112,256]{1,0:T(8,128)S(1)}, u32[]{:S(2)}, u32[]{:S(2)}) collective-permute-start(f32[112,256]{1,0:T(8,128)S(1)} %get-tuple-element.39), channel_id=1, source_target_pairs={{0,4},{4,0},{8,12},{12,8},{16,20},{20,16},{24,28},{28,24},{1,5},{5... | collective-permute-start | bytes 344072 | tf_op jit(solution)/shard_map/ppermute | solution.py:33
  18.2 5.1 %collective-permute-start.3 = (bf16[112,256]{1,0:T(8,128)(2,1)S(1)}, bf16[112,256]{1,0:T(8,128)(2,1)S(1)}, u32[]{:S(2)}, u32[]{:S(2)}) collective-permute-start(bf16[112,256]{1,0:T(8,128)(2,1)S(1)} %add.27.refs_0_), channel_id=1, source_target_pairs={{0,24},{4,28},{8,16},{12,20},{16,8},{20,12},{24,0},{28,4},{1,25},{... | collective-permute-start | bytes 172040 | tf_op jit(solution)/shard_map/ppermute | solution.py:33
  21.6 5.1 %collective-permute-start.2 = (bf16[112,256]{1,0:T(8,128)(2,1)S(1)}, bf16[112,256]{1,0:T(8,128)(2,1)S(1)}, u32[]{:S(2)}, u32[]{:S(2)}) collective-permute-start(bf16[112,256]{1,0:T(8,128)(2,1)S(1)} %add.27.refs_0_), channel_id=1, source_target_pairs={{0,16},{4,20},{8,24},{12,28},{16,0},{20,4},{24,8},{28,12},{1,17},{... | collective-permute-start | bytes 172040 | tf_op jit(solution)/shard_map/ppermute | solution.py:33
  21.6 5.1 %collective-permute-start.1 = (bf16[112,256]{1,0:T(8,128)(2,1)S(1)}, bf16[112,256]{1,0:T(8,128)(2,1)S(1)}, u32[]{:S(2)}, u32[]{:S(2)}) collective-permute-start(bf16[112,256]{1,0:T(8,128)(2,1)S(1)} %add.27.refs_0_), channel_id=1, source_target_pairs={{0,8},{4,12},{8,0},{12,4},{16,24},{20,28},{24,16},{28,20},{1,9},{5... | collective-permute-start | bytes 172040 | tf_op jit(solution)/shard_map/ppermute | solution.py:33
  26.7 2.0 %collective-permute-start.4 = (f32[112,256]{1,0:T(8,128)S(1)}, f32[112,256]{1,0:T(8,128)S(1)}, u32[]{:S(2)}, u32[]{:S(2)}) collective-permute-start(f32[112,256]{1,0:T(8,128)S(1)} %add.28.near_ref), channel_id=1, source_target_pairs={{0,4},{4,0},{8,12},{12,8},{16,20},{20,16},{24,28},{28,24},{1,5},{5... | collective-permute-start | bytes 344072 | tf_op jit(solution)/shard_map/ppermute | solution.py:33
  30.9 2.4 %collective-permute-start.5 = (bf16[4,1,32,3072]{3,2,1,0:T(8,128)(2,1)S(1)}, bf16[4,1,32,3072]{3,2,1,0:T(8,128)(2,1)S(1)}, u32[]{:S(2)}, u32[]{:S(2)}) collective-permute-start(bf16[4,1,32,3072]{3,2,1,0:T(8,128)(2,1)S(1)} %get-tuple-element.42), channel_id=1, source_target_pairs={{0,4},{4,0},{8,12},{12,8},{16,20},{20,16},{24,28},{28,24},{1,5},{5... | collective-permute-start | bytes 2359304 | tf_op jit(solution)/shard_map/ppermute | solution.py:33
  34.1 25.6 %copy-start.4 = (f32[2688]{0:T(1024)S(1)}, f32[2688]{0:T(1024)}, u32[]{:S(2)}) copy-start(f32[2688]{0:T(1024)} %param.19) | copy-start | bytes 32260
  34.1 25.6 %copy-start.5 = (f32[2688]{0:T(1024)S(1)}, f32[2688]{0:T(1024)}, u32[]{:S(2)}) copy-start(f32[2688]{0:T(1024)} %param.18) | copy-start | bytes 32260
  34.1 6.5 %collective-permute-start.8 = (bf16[40,3072]{1,0:T(8,128)(2,1)S(1)}, bf16[40,3072]{1,0:T(8,128)(2,1)S(1)}, u32[]{:S(2)}, u32[]{:S(2)}) collective-permute-start(bf16[40,3072]{1,0:T(8,128)(2,1)S(1)} %get-tuple-element.46), channel_id=1, source_target_pairs={{0,1},{1,0},{2,3},{3,2},{4,5},{5,4},{6,7},{7,6},{8,9},{9,8},{10,11... | collective-permute-start | bytes 737288 | tf_op jit(solution)/shard_map/ppermute | solution.py:33
  34.6 6.0 %collective-permute-start.9 = (bf16[40,3072]{1,0:T(8,128)(2,1)S(1)}, bf16[40,3072]{1,0:T(8,128)(2,1)S(1)}, u32[]{:S(2)}, u32[]{:S(2)}) collective-permute-start(bf16[40,3072]{1,0:T(8,128)(2,1)S(1)} %get-tuple-element.47), channel_id=1, source_target_pairs={{0,2},{1,3},{2,0},{3,1},{4,6},{5,7},{6,4},{7,5},{8,10},{9,11},{10,... | collective-permute-start | bytes 737288 | tf_op jit(solution)/shard_map/ppermute | solution.py:33
  34.9 11.1 %collective-permute-start.10 = (bf16[40,3072]{1,0:T(8,128)(2,1)S(1)}, bf16[40,3072]{1,0:T(8,128)(2,1)S(1)}, u32[]{:S(2)}, u32[]{:S(2)}) collective-permute-start(bf16[40,3072]{1,0:T(8,128)(2,1)S(1)} %get-tuple-element.48), channel_id=1, source_target_pairs={{0,3},{1,2},{2,1},{3,0},{4,7},{5,6},{6,5},{7,4},{8,11},{9,10},{10,... | collective-permute-start | bytes 737288 | tf_op jit(solution)/shard_map/ppermute | solution.py:33
  46.8 15.0 %collective-permute-start.11 = (bf16[1,96,3072]{2,1,0:T(8,128)(2,1)S(1)}, bf16[1,96,3072]{2,1,0:T(8,128)(2,1)S(1)}, u32[]{:S(2)}, u32[]{:S(2)}) collective-permute-start(bf16[1,96,3072]{2,1,0:T(8,128)(2,1)S(1)} %get-tuple-element.50), channel_id=1, source_target_pairs={{0,2},{1,3},{2,0},{3,1},{4,6},{5,7},{6,4},{7,5},{8,10},{9,11},{10,... | collective-permute-start | bytes 1769480 | tf_op jit(solution)/shard_map/ppermute | solution.py:33
  47.9 13.9 %collective-permute-start.12 = (bf16[1,96,3072]{2,1,0:T(8,128)(2,1)S(1)}, bf16[1,96,3072]{2,1,0:T(8,128)(2,1)S(1)}, u32[]{:S(2)}, u32[]{:S(2)}) collective-permute-start(bf16[1,96,3072]{2,1,0:T(8,128)(2,1)S(1)} %get-tuple-element.51), channel_id=1, source_target_pairs={{0,1},{1,0},{2,3},{3,2},{4,5},{5,4},{6,7},{7,6},{8,9},{9,8},{10,11... | collective-permute-start | bytes 1769480 | tf_op jit(solution)/shard_map/ppermute | solution.py:33
  47.9 3.6 %collective-permute-start.13 = (bf16[32,768]{1,0:T(8,128)(2,1)S(1)}, bf16[32,768]{1,0:T(8,128)(2,1)S(1)}, u32[]{:S(2)}, u32[]{:S(2)}) collective-permute-start(bf16[32,768]{1,0:T(8,128)(2,1)S(1)} %get-tuple-element.53), channel_id=1, source_target_pairs={{0,8},{4,12},{8,0},{12,4},{16,24},{20,28},{24,16},{28,20},{1,9},{5... | collective-permute-start | bytes 147464 | tf_op jit(solution)/shard_map/ppermute | solution.py:33
  48.8 4.4 %collective-permute-start.14 = (bf16[32,768]{1,0:T(8,128)(2,1)S(1)}, bf16[32,768]{1,0:T(8,128)(2,1)S(1)}, u32[]{:S(2)}, u32[]{:S(2)}) collective-permute-start(bf16[32,768]{1,0:T(8,128)(2,1)S(1)} %get-tuple-element.54), channel_id=1, source_target_pairs={{0,16},{4,20},{8,24},{12,28},{16,0},{20,4},{24,8},{28,12},{1,17},{... | collective-permute-start | bytes 147464 | tf_op jit(solution)/shard_map/ppermute | solution.py:33
  51.1 4.9 %collective-permute-start.15 = (bf16[32,768]{1,0:T(8,128)(2,1)S(1)}, bf16[32,768]{1,0:T(8,128)(2,1)S(1)}, u32[]{:S(2)}, u32[]{:S(2)}) collective-permute-start(bf16[32,768]{1,0:T(8,128)(2,1)S(1)} %get-tuple-element.55), channel_id=1, source_target_pairs={{0,24},{4,28},{8,16},{12,20},{16,8},{20,12},{24,0},{28,4},{1,25},{... | collective-permute-start | bytes 147464 | tf_op jit(solution)/shard_map/ppermute | solution.py:33
  56.0 4.8 %collective-permute-start.18 = (bf16[32,768]{1,0:T(8,128)(2,1)S(1)}, bf16[32,768]{1,0:T(8,128)(2,1)S(1)}, u32[]{:S(2)}, u32[]{:S(2)}) collective-permute-start(bf16[32,768]{1,0:T(8,128)(2,1)S(1)} %add.29.refs_0_), channel_id=1, source_target_pairs={{0,24},{4,28},{8,16},{12,20},{16,8},{20,12},{24,0},{28,4},{1,25},{... | collective-permute-start | bytes 147464 | tf_op jit(solution)/shard_map/ppermute | solution.py:33
  56.5 5.3 %collective-permute-start.17 = (bf16[32,768]{1,0:T(8,128)(2,1)S(1)}, bf16[32,768]{1,0:T(8,128)(2,1)S(1)}, u32[]{:S(2)}, u32[]{:S(2)}) collective-permute-start(bf16[32,768]{1,0:T(8,128)(2,1)S(1)} %add.29.refs_0_), channel_id=1, source_target_pairs={{0,16},{4,20},{8,24},{12,28},{16,0},{20,4},{24,8},{28,12},{1,17},{... | collective-permute-start | bytes 147464 | tf_op jit(solution)/shard_map/ppermute | solution.py:33
  56.5 5.3 %collective-permute-start.16 = (bf16[32,768]{1,0:T(8,128)(2,1)S(1)}, bf16[32,768]{1,0:T(8,128)(2,1)S(1)}, u32[]{:S(2)}, u32[]{:S(2)}) collective-permute-start(bf16[32,768]{1,0:T(8,128)(2,1)S(1)} %add.29.refs_0_), channel_id=1, source_target_pairs={{0,8},{4,12},{8,0},{12,4},{16,24},{20,28},{24,16},{28,20},{1,9},{5... | collective-permute-start | bytes 147464 | tf_op jit(solution)/shard_map/ppermute | solution.py:33
  60.3 4.6 %copy-start.1 = (f32[2688]{0:T(1024)}, f32[2688]{0:T(1024)S(1)}, u32[]{:S(2)}) copy-start(f32[2688]{0:T(1024)S(1)} %get-tuple-element.68.refs_6_) | copy-start | bytes 32260
  61.8 3.0 %copy-start.3 = (s32[8]{0:T(128)S(1)}, s32[8]{0:T(128)}, u32[]{:S(2)}) copy-start(s32[8]{0:T(128)} %owners.5) | copy-start | bytes 100
  61.8 5.6 %collective-permute-start.21 = (bf16[4,32,768]{2,1,0:T(8,128)(2,1)S(1)}, bf16[4,32,768]{2,1,0:T(8,128)(2,1)S(1)}, u32[]{:S(2)}, u32[]{:S(2)}) collective-permute-start(bf16[4,32,768]{2,1,0:T(8,128)(2,1)S(1)} %stack.35.refs_0_), channel_id=1, source_target_pairs={{0,3},{1,2},{2,1},{3,0},{4,7},{5,6},{6,5},{7,4},{8,11},{9,10},{10,... | collective-permute-start | bytes 589832 | tf_op jit(solution)/shard_map/ppermute | solution.py:33
  62.8 6.6 %collective-permute-start.20 = (bf16[4,32,768]{2,1,0:T(8,128)(2,1)S(1)}, bf16[4,32,768]{2,1,0:T(8,128)(2,1)S(1)}, u32[]{:S(2)}, u32[]{:S(2)}) collective-permute-start(bf16[4,32,768]{2,1,0:T(8,128)(2,1)S(1)} %stack.35.refs_0_), channel_id=1, source_target_pairs={{0,2},{1,3},{2,0},{3,1},{4,6},{5,7},{6,4},{7,5},{8,10},{9,11},{10,... | collective-permute-start | bytes 589832 | tf_op jit(solution)/shard_map/ppermute | solution.py:33
  63.7 5.7 %collective-permute-start.19 = (bf16[4,32,768]{2,1,0:T(8,128)(2,1)S(1)}, bf16[4,32,768]{2,1,0:T(8,128)(2,1)S(1)}, u32[]{:S(2)}, u32[]{:S(2)}) collective-permute-start(bf16[4,32,768]{2,1,0:T(8,128)(2,1)S(1)} %stack.35.refs_0_), channel_id=1, source_target_pairs={{0,1},{1,0},{2,3},{3,2},{4,5},{5,4},{6,7},{7,6},{8,9},{9,8},{10,11... | collective-permute-start | bytes 589832 | tf_op jit(solution)/shard_map/ppermute | solution.py:33
  69.4 11.1 %collective-permute-start.22 = (bf16[4,1,4,32,768]{4,3,2,1,0:T(8,128)(2,1)S(1)}, bf16[4,1,4,32,768]{4,3,2,1,0:T(8,128)(2,1)S(1)}, u32[]{:S(2)}, u32[]{:S(2)}) collective-permute-start(bf16[4,1,4,32,768]{4,3,2,1,0:T(8,128)(2,1)S(1)} %bitcast.12), channel_id=1, source_target_pairs={{0,4},{4,0},{8,12},{12,8},{16,20},{20,16},{24,28},{28,24},{1,5},{5... | collective-permute-start | bytes 2359304 | tf_op jit(solution)/shard_map/ppermute | solution.py:33

commit v12 on v11

--- a/solution.py
+++ b/solution.py
@@ -36,7 +36,7 @@
 def left_kernel(pos, g_ref, f_ref, q_ref, vec_ref, comp_ref, near_ref, far_ref, total, feedback, right, sems):
     nmat, rows, _ = comp_ref.shape
     rank = q_ref.shape[1]
-    part = near_ref.shape[0]
+    part = near_ref.shape[1]
 
     def copies(k):
         return [
@@ -66,8 +66,8 @@
             comp, right[k], (((1,), (1,)), ((), ())), preferred_element_type=F32
         )
 
-    for ref, core in ((near_ref, pos[2]), (far_ref, 1 - pos[2])):
-        ref[...] = total[pl.ds(pl.multiple_of(core * part, 16), part), :]
+    for ref, core in ((near_ref, 1 - pos[2]), (far_ref, pos[2])):
+        ref[...] = total[:, pl.ds(pl.multiple_of(core * part, 128), part)]
 
 
 def left_terms(pos, gradients, feedback, right_t, vec):
@@ -75,8 +75,8 @@
     rank = right_t.shape[1]
     width = nmat * rank
     total = rows + -(-vec.shape[1] // width)
-    total += -total % (16 * CORES)
-    part = jax.ShapeDtypeStruct((total // CORES, width), F32)
+    total += -total % 16
+    part = jax.ShapeDtypeStruct((total, width // CORES), F32)
     vmem = pl.BlockSpec(memory_space=pltpu.VMEM)
     any_spec = pl.BlockSpec(memory_space=pl.ANY)
     return pl.pallas_call(
@@ -118,90 +118,104 @@
     )(*parts)
 
 
-def send_kernel(half, pos, near_ref, far_ref, gram_ref, comp_ref, send_ref, lt_ref, left_ref, vec_ref, left, gram):
-    nmat, rows, _ = comp_ref.shape
-    rank = gram_ref.shape[1]
-    part = near_ref.shape[0]
-    for ref, core in ((near_ref, pos[2]), (far_ref, 1 - pos[2])):
-        left[pl.ds(pl.multiple_of(core * part, 16), part), :] = ref[...]
-    vec_ref[...] = left[rows:, :]
+def right_kernel(other, pos, sums_ref, gram_ref, comp_ref, *refs):
+    out_ref, hat_ref, left_ref, lt, gram = refs[-5:]
+    rows = comp_ref.shape[1]
+    half, upm, unit, _ = out_ref.shape
+    rank = upm * unit
+    core = 1 - pos[2] if other else pos[2]
     gram[...] = jnp.zeros(gram.shape, F32)
-    for i in range(nmat):
-        gram[i * rank : (i + 1) * rank, i * rank : (i + 1) * rank] = gram_ref[i]
+    for i in range(half):
+        part = slice(i * rank, (i + 1) * rank)
+        gram[part, part] = gram_ref[core * half + i]
     hat = jnp.dot(
-        left[:rows, :], gram[...], precision=lax.Precision.HIGHEST, preferred_element_type=F32
+        sums_ref[:rows, :], gram[...], precision=lax.Precision.HIGHEST, preferred_element_type=F32
     )
-    lt_ref[...] = hat.T.astype(BF16)
-    for i in range(nmat):
-        left_ref[i] = hat[:, i * rank : (i + 1) * rank].astype(BF16)
-    right_rows(half, pos, lt_ref, comp_ref, send_ref)
-
-
-def right_rows(start, pos, lt_ref, comp_ref, out_ref):
+    lt[...] = hat.T.astype(BF16)
+    hat = hat.astype(BF16)
+    hat_ref[...] = hat
+    for i in range(half):
+        left_ref[i] = hat[:, i * rank : (i + 1) * rank]
+    if not other:
+        others_ref, vec_ref = refs[0], refs[-6]
+        width = sums_ref.shape[1]
+        for ref, place in ((sums_ref, core), (others_ref, 1 - core)):
+            vec_ref[:, pl.ds(pl.multiple_of(place * width, 128), width)] = ref[rows:, :]
+    right_rows(other, range(half // 2 if other else half), pos, lt, comp_ref, out_ref)
+
+
+def right_rows(other, entries, pos, lt, comp_ref, out_ref):
     half, upm, unit, _ = out_ref.shape
-    for t in range(half):
-        k = (t + start) ^ pos[0]
-        rows = pl.ds(pl.multiple_of(k * upm * unit, upm * unit), upm * unit)
-        terms = jnp.dot(lt_ref[rows, :], comp_ref[k], preferred_element_type=F32)
+    rank = upm * unit
+    for t in entries:
+        k = (t + half * other) ^ pos[0]
+        part = pl.ds(pl.multiple_of(lax.rem(k, half) * rank, rank), rank)
+        terms = jnp.dot(lt[part, :], comp_ref[k], preferred_element_type=F32)
         for i in range(upm):
             out_ref[t, i ^ pos[1]] = terms[i * unit : (i + 1) * unit].astype(out_ref.dtype)
 
 
-def keep_kernel(pos, lt_ref, comp_ref, *refs):
-    right_rows(0, pos, lt_ref, comp_ref, refs[-1])
-
-
-def right_terms(pos, near, far, gram, comp, upm, after):
-    nmat, rows, n = comp.shape
-    rank = gram.shape[1]
-    width = nmat * rank
-    half = nmat // CORES
-    total = CORES * near.shape[0]
-    shape = (half, upm, rank // upm, n)
-    vmem = pl.BlockSpec(memory_space=pltpu.VMEM)
-    send, lt, left, vec = pl.pallas_call(
-        functools.partial(send_kernel, half),
+def more_kernel(pos, lt_ref, comp_ref, *refs):
+    out_ref = refs[-1]
+    half = out_ref.shape[0]
+    right_rows(1, range(half // 2, half), pos, lt_ref, comp_ref, out_ref)
+
+
+def right_more(pos, lt, comp, send, after):
+    vmem = pl.BlockSpec(memory_space=pltpu.VMEM)
+    return pl.pallas_call(
+        more_kernel,
         grid_spec=pltpu.PrefetchScalarGridSpec(
             num_scalar_prefetch=1,
             grid=(1,),
-            in_specs=[vmem] * 4,
-            out_specs=[vmem] * 4,
-            scratch_shapes=[pltpu.VMEM((total, width), F32), pltpu.VMEM((width, width), F32)],
-        ),
-        out_shape=[
-            jax.ShapeDtypeStruct(shape, BF16),
-            jax.ShapeDtypeStruct((width, rows), BF16),
-            jax.ShapeDtypeStruct((nmat, rows, rank), BF16),
-            jax.ShapeDtypeStruct((total - rows, width), F32),
-        ],
-        compiler_params=params(),
-        cost_estimate=cost(),
-        name="right_send",
-    )(pos, near, far, gram, comp)
-    keep = pl.pallas_call(
-        keep_kernel,
+            in_specs=[vmem] * 3 + [pl.BlockSpec(memory_space=pl.ANY)] * len(after),
+            out_specs=vmem,
+        ),
+        out_shape=jax.ShapeDtypeStruct(send.shape, send.dtype),
+        input_output_aliases={3: 0},
+        compiler_params=params(),
+        cost_estimate=cost(),
+        name="right_more",
+    )(pos, lt, comp, send, *after)
+
+
+def right_terms(pos, sums, gram, comp, upm, others=None, after=()):
+    nmat, rows, n = comp.shape
+    rank = gram.shape[1]
+    total, width = sums.shape
+    half = nmat // CORES
+    vmem = pl.BlockSpec(memory_space=pltpu.VMEM)
+    own = others is not None
+    outs = [
+        jax.ShapeDtypeStruct((half, upm, rank // upm, n), F32 if own else BF16),
+        jax.ShapeDtypeStruct((rows, width), BF16),
+        jax.ShapeDtypeStruct((half, rows, rank), BF16),
+        jax.ShapeDtypeStruct((width, rows), BF16),
+    ]
+    if own:
+        outs = [jax.ShapeDtypeStruct((total - rows, CORES * width), F32)] + outs
+    return pl.pallas_call(
+        functools.partial(right_kernel, 0 if own else 1),
         grid_spec=pltpu.PrefetchScalarGridSpec(
             num_scalar_prefetch=1,
             grid=(1,),
-            in_specs=[vmem, vmem] + [pl.BlockSpec(memory_space=pl.ANY)] * len(after),
-            out_specs=vmem,
-        ),
-        out_shape=jax.ShapeDtypeStruct(shape, F32),
-        compiler_params=params(),
-        cost_estimate=cost(),
-        name="right_keep",
-    )(pos, lt, comp, *after)
-    return send, keep, lt, left, vec
-
-
-def chip_kernel(replica_rows, pos, keep_ref, recv_ref, lt_ref, *refs):
+            in_specs=[vmem] * (4 if own else 3) + [pl.BlockSpec(memory_space=pl.ANY)] * len(after),
+            out_specs=[vmem] * len(outs),
+            scratch_shapes=[pltpu.VMEM((width, width), F32)],
+        ),
+        out_shape=outs,
+        compiler_params=params(),
+        cost_estimate=cost(),
+        name="right_keep" if own else "right_send",
+    )(pos, sums, gram, comp, *([others] if own else []), *after)
+
+
+def chip_kernel(replica_rows, pos, keep_ref, recv_ref, far_ref, near_ref, *refs):
     upm = keep_ref.shape[1]
     own_ref, strip_ref, *sends = refs[-(keep_ref.shape[0] * upm + 1) :]
-    left = lt_ref[...].astype(F32).T
-    strip = left[:replica_rows]
-    for i in range(1, left.shape[0] // replica_rows):
-        strip = jnp.where(pos[6] == i, left[i * replica_rows : (i + 1) * replica_rows], strip)
     height = strip_ref.shape[0]
+    part = pl.ds(pl.multiple_of(pos[6] * replica_rows, 16), replica_rows)
+    strip = jnp.concatenate([ref[part, :].astype(F32) for ref in (far_ref, near_ref)], axis=1)
     strip = jnp.concatenate(
         [strip[i * height : (i + 1) * height] for i in range(replica_rows // height)], axis=1
     )
@@ -213,9 +227,9 @@
         out[...] = jnp.concatenate([terms, strip], axis=0).astype(BF16)
 
 
-def chip_sum(pos, keep, recv, lt, replica_rows, after):
+def chip_sum(pos, keep, recv, hats, replica_rows):
     half, upm, unit, n = keep.shape
-    height = lt.shape[0] * replica_rows // n
+    height = CORES * hats[0].shape[1] * replica_rows // n
     vmem = pl.BlockSpec(memory_space=pltpu.VMEM)
     outs = [jax.ShapeDtypeStruct((unit, n), F32), jax.ShapeDtypeStruct((height, n), F32)]
     outs += [jax.ShapeDtypeStruct((unit + height, n), BF16)] * (half * upm - 1)
@@ -224,14 +238,14 @@
         grid_spec=pltpu.PrefetchScalarGridSpec(
             num_scalar_prefetch=1,
             grid=(1,),
-            in_specs=[vmem] * 3 + [pl.BlockSpec(memory_space=pl.ANY)] * len(after),
+            in_specs=[vmem] * 4,
             out_specs=[vmem] * len(outs),
         ),
         out_shape=outs,
         compiler_params=params(),
         cost_estimate=cost(),
         name="chip_sum",
-    )(pos, keep, recv, lt, *after)
+    )(pos, keep, recv, *hats)
 
 
 def plane_kernel(pos, own_ref, strip_ref, *refs):
@@ -293,38 +307,26 @@
     )(*parts, *after)
 
 
-def token_kernel(*refs):
-    refs[-1][...] = jnp.zeros(refs[-1].shape, F32)
-
-
-def token(after):
-    return pl.pallas_call(
-        token_kernel,
-        in_specs=[pl.BlockSpec(memory_space=pl.ANY)] * len(after),
-        out_specs=pl.BlockSpec(memory_space=pltpu.VMEM),
-        out_shape=jax.ShapeDtypeStruct((8, 128), F32),
-        compiler_params=params(),
-        cost_estimate=cost(),
-        name="token",
-    )(*after)
-
-
-def forward_kernel(cuts, *refs):
-    for source, out, first in zip(refs, refs[-len(cuts) :], cuts):
-        out[...] = source[first : first + out.shape[0]]
-
-
-def forward(parts, cuts, count, after):
-    vmem = pl.BlockSpec(memory_space=pltpu.VMEM)
-    return pl.pallas_call(
-        functools.partial(forward_kernel, cuts),
-        in_specs=[vmem] * len(parts) + [pl.BlockSpec(memory_space=pl.ANY)],
-        out_specs=[vmem] * len(parts),
-        out_shape=[jax.ShapeDtypeStruct((count,) + part.shape[1:], part.dtype) for part in parts],
+def forward_kernel(later, x_ref, y_ref, base_ref, after_ref, *outs):
+    rows = base_ref.shape[1]
+    for source, slot, out in ((y_ref, 1, outs[0]), (x_ref, 0, outs[1])):
+        out[:rows] = source[:rows]
+        out[rows:] = base_ref[slot, rows - later :]
+
+
+def forward(x, y, base, after):
+    _, rows, n = base.shape
+    later = 2 * rows - x.shape[0]
+    vmem = pl.BlockSpec(memory_space=pltpu.VMEM)
+    return pl.pallas_call(
+        functools.partial(forward_kernel, later),
+        in_specs=[vmem] * 3 + [pl.BlockSpec(memory_space=pl.ANY)],
+        out_specs=[vmem] * 2,
+        out_shape=[jax.ShapeDtypeStruct((rows + later, n), BF16)] * 2,
         compiler_params=params(),
         cost_estimate=cost(),
         name="forward",
-    )(*parts, after)
+    )(x, y, base, after)
 
 
 def rank_of(owners, k):
@@ -334,25 +336,39 @@
     return count
 
 
-def collect_kernel(places, *refs):
-    for i, (a, row) in enumerate(places):
-        refs[-1][i] = refs[a][row]
-
-
-def collect(bases, places):
-    vmem = pl.BlockSpec(memory_space=pltpu.VMEM)
-    return pl.pallas_call(
-        functools.partial(collect_kernel, places),
-        in_specs=[vmem] * len(bases),
+def collect_kernel(square, base_ref, *refs):
+    out = refs[-1]
+    capacity, rows, _ = base_ref.shape
+    out[:capacity] = base_ref[...]
+    if not square:
+        for d, ref in enumerate(refs[:-1], 1):
+            out[d * capacity : (d + 1) * capacity] = ref[...]
+        return
+    x, y, more_x, more_y = refs[:-1]
+    early = x.shape[0] - rows
+    for d, slot, first, second in ((1, 0, x, more_x), (2, 1, y, more_y)):
+        out[d * capacity + slot] = first[:rows]
+        out[d * capacity + 1 - slot, :early] = first[rows:]
+        out[d * capacity + 1 - slot, early:] = second[rows:]
+    out[3 * capacity] = more_y[:rows]
+    out[3 * capacity + 1] = more_x[:rows]
+
+
+def collect(square, n_mp, base, parts):
+    capacity, rows, n = base.shape
+    vmem = pl.BlockSpec(memory_space=pltpu.VMEM)
+    return pl.pallas_call(
+        functools.partial(collect_kernel, square),
+        in_specs=[vmem] * (1 + len(parts)),
         out_specs=vmem,
-        out_shape=jax.ShapeDtypeStruct((len(places),) + bases[0].shape[1:], BF16),
+        out_shape=jax.ShapeDtypeStruct((n_mp * capacity, rows, n), BF16),
         compiler_params=params(),
         cost_estimate=cost(),
         name="collect",
-    )(*bases)
-
-
-def outputs_kernel(jobs, where, capacity, pos, owners, comp_ref, left_ref, strip_ref, base_ref, *refs):
+    )(base, *parts)
+
+
+def outputs_kernel(jobs, where, capacity, pos, owners, comp_ref, near_ref, far_ref, strip_ref, base_ref, *refs):
     n_right = 1 + max(a for a, _ in (where or jobs).values())
     rights, refs = refs[:n_right], refs[n_right:]
     n_scratch = 6 if where else 3
@@ -362,7 +378,8 @@
     token_ref, outs = refs[-1], refs[-5:-1] if where else refs[-3:-1]
     token_ref[...] = jnp.zeros(token_ref.shape, F32)
     _, upm, n_z, _, cols = rights[0].shape
-    half = comp_ref.shape[0] // CORES
+    half = near_ref.shape[0]
+    turn = (1 - pos[2]) * half
 
     def right_of(place, d, block):
         a, entry = place
@@ -391,7 +408,7 @@
             for k in range(owners.shape[0]):
                 mine = jnp.where((owners[k] == pos[5]) & (rank_of(owners, k) == c), k, mine)
             safe = jnp.maximum(mine, 0)
-            strip = strip_ref[safe]
+            strip = strip_ref[safe ^ turn]
             for d in range(n_z):
                 for block in pieces:
                     right = jnp.zeros((strip.shape[1], step), BF16)
@@ -412,7 +429,8 @@
     for i, (job, where_right) in enumerate(jobs.items()):
         k = matrix(*job)
         slot = (owners[k] ^ pos[5]) * capacity + rank_of(owners, k)
-        left, strip = left_ref[k], strip_ref[k]
+        left = (far_ref if job[0] else near_ref)[lax.rem(k, half)]
+        strip = strip_ref[k ^ turn]
         for d in range(n_z):
             for block in pieces:
                 right = right_of(where_right, d, block)
@@ -430,7 +448,7 @@
         copy.wait()
 
 
-def outputs(pos, owners, comp, left, strip, base, capacity, rights, jobs, where=None, states=(), earlier=()):
+def outputs(pos, owners, comp, near, far, strip, base, capacity, rights, jobs, where=None, states=(), earlier=()):
     nmat, rows, n = comp.shape
     n_z = rights[0].shape[2]
     replica_rows = base.shape[1]
@@ -448,13 +466,13 @@
         jax.ShapeDtypeStruct((1, nmat, rows, n), BF16),
         jax.ShapeDtypeStruct((nmat, replica_rows, n), BF16),
     ] + [jax.ShapeDtypeStruct((1,) + x.shape, F32) for x in states]
-    first = 6 + len(rights) + len(states)
+    first = 7 + len(rights) + len(states)
     return pl.pallas_call(
         functools.partial(outputs_kernel, jobs, where, capacity),
         grid_spec=pltpu.PrefetchScalarGridSpec(
             num_scalar_prefetch=2,
             grid=(1,),
-            in_specs=[vmem] * (4 + len(rights) + len(states)) + [any_spec] * len(earlier),
+            in_specs=[vmem] * (5 + len(rights) + len(states)) + [any_spec] * len(earlier),
             out_specs=[any_spec] * len(outs) + [vmem],
             scratch_shapes=scratch,
         ),
@@ -463,11 +481,11 @@
         compiler_params=params(24),
         cost_estimate=cost(),
         name="outputs",
-    )(pos, owners, comp, left, strip, base, *rights, *states, *earlier)
-
-
-def base_kernel(pos, momentum_ref, master_ref, *refs):
-    out_ref, momentum, master, sems = refs
+    )(pos, owners, comp, near, far, strip, base, *rights, *states, *earlier)
+
+
+def base_kernel(pos, momentum_ref, master_ref, out_ref, momentum, master, *refs):
+    firsts, sems = refs[:-1], refs[-1]
     capacity, rows, _ = out_ref.shape
     blocks = [(c, first) for c in range(capacity) for first in range(0, rows, BASE_ROWS)]
 
@@ -487,26 +505,31 @@
             copy.wait()
         part = slice(first, first + BASE_ROWS)
         out_ref[c, part] = (master[c, part] - 0.09 * momentum[c, part]).astype(BF16)
-
-
-def base_of(pos, momentum, master):
+    for slot, ref in enumerate(firsts):
+        ref[:rows] = out_ref[slot]
+        ref[rows:] = out_ref[1 - slot, : ref.shape[0] - rows]
+
+
+def base_of(pos, momentum, master, square):
     _, capacity, rows, n = momentum.shape
     state = jax.ShapeDtypeStruct((capacity, rows, n), F32)
-    base, momentum, master = pl.pallas_call(
+    base = jax.ShapeDtypeStruct((capacity, rows, n), BF16)
+    firsts = [jax.ShapeDtypeStruct((rows + 2 * rows // 3, n), BF16)] * (2 if square else 0)
+    base, momentum, master, *firsts = pl.pallas_call(
         base_kernel,
         grid_spec=pltpu.PrefetchScalarGridSpec(
             num_scalar_prefetch=1,
             grid=(1,),
             in_specs=[pl.BlockSpec(memory_space=pl.ANY)] * 2,
-            out_specs=[pl.BlockSpec(memory_space=pltpu.VMEM)] * 3,
+            out_specs=[pl.BlockSpec(memory_space=pltpu.VMEM)] * (3 + len(firsts)),
             scratch_shapes=[pltpu.SemaphoreType.DMA((2, capacity * rows // BASE_ROWS))],
         ),
-        out_shape=[jax.ShapeDtypeStruct((capacity, rows, n), BF16), state, state],
+        out_shape=[base, state, state] + firsts,
         compiler_params=params(),
         cost_estimate=cost(),
         name="base",
     )(pos, momentum, master)
-    return base, (momentum, master)
+    return base, (momentum, master), firsts
 
 
 def per_device(
@@ -539,11 +562,10 @@
     pos = jnp.stack(places_of).astype(jnp.int32)
     in_hbm = lambda x: pltpu.with_memory_space_constraint(x, pltpu.HBM)
 
-    square = n_mp == 4 and capacity == 2
-    base, states = base_of(pos, in_hbm(momentum), in_hbm(master_weights))
-    early = [exchange(base, "mp", d) for d in range(1, 3 if square else n_mp)]
-    bases = [base] + early
-    places = {(d, c): (d, c) for d in range(len(bases)) for c in range(capacity)}
+    square = n_mp == 4 and capacity == 2 and replica_rows % 48 == 0
+    base, states, firsts = base_of(pos, in_hbm(momentum), in_hbm(master_weights), square)
+    firsts = firsts or [base] * (n_mp - 1)
+    early = [exchange(part, "mp", d) for d, part in enumerate(firsts, 1)]
 
     nvec = vector_grads.shape[1]
     comp, near, far = left_terms(
@@ -556,29 +578,29 @@
     piece = add([near, exchange(far, "replica", 1)], BF16)
     along_z = lambda x: [exchange(x, "replica", CORES * d) for d in range(1, n_z)]
     piece = add([piece] + along_z(piece), F32)
-    near, far = piece, exchange(piece, "replica", 1)
-
-    send, keep, lt, left, vector_rows = right_terms(pos, near, far, gram_root, comp, upm, [])
+
+    mine = exchange(piece, "replica", 1)
+    send, far_hat, far_left, lt = right_terms(pos, piece, gram_root, comp, upm)
+    recv = exchange(right_more(pos, lt, comp, send, [mine] + early), "replica", 1)
+    vector_rows, keep, near_hat, near_left, _ = right_terms(
+        pos, mine, gram_root, comp, upm, piece
+    )
     vector_total = vector_rows.reshape(-1)[:nvec]
-    recv = exchange(send, "replica", 1)
-    own, strip, *chip = chip_sum(pos, keep, recv, lt, replica_rows, [token([keep] + early)])
+    own, strip, *chip = chip_sum(pos, keep, recv, [far_hat, near_hat], replica_rows)
     plane = [exchange(part, "mp", d) for d, part in enumerate(chip, 1)]
-    *final, mine = plane_sum(pos, own, strip, plane, n_z, nmat, rank)
+    *final, strips = plane_sum(pos, own, strip, plane, n_z, nmat, rank)
     late = []
     if square:
-        parts = forward(early, [0, 1], 1, mine)
-        late = [exchange(part, "mp", 2 - i) for i, part in enumerate(parts)]
-        bases = bases + late
-        places[3, 0], places[3, 1] = (3, 0), (4, 0)
+        late = [exchange(part, "mp", d) for d, part in enumerate(forward(*early, base, strips), 1)]
     final = [final[0]] + [exchange(final[d], "replica", CORES * d) for d in range(1, n_z)]
     final = add(final, BF16)
     new_vector_momentum = 0.9 * vector_momentum + vector_total
     new_vector_params = vector_params - 0.1 * new_vector_momentum
 
-    whole = stack([final] + along_z(final), late + [new_vector_params])
+    whole = stack([final] + along_z(final), [new_vector_params])
     others = [exchange(whole, "mp", d) for d in range(1, n_mp)]
-    slots = collect(bases, [places[d, c] for d in range(n_mp) for c in range(capacity)])
-    common = (pos, owners, comp, left, mine, slots, capacity)
+    slots = collect(square, n_mp, base, early + late)
+    common = (pos, owners, comp, near_left, far_left, strips, slots, capacity)
     shape = (half, upm) + whole.shape
     done, near_jobs, after = (), {(0, j): (0, j) for j in range(half)}, [slots]
     if upm == 1:

time: 86.9 us -> 88 us (1.013)
  starting transfers between devices: 30.7 us -> 28.2 us
  waiting for transfers between devices: 24.7 us -> 27.2 us
  Pallas kernels: 29.8 us -> 30.9 us
    ppermute x23, waiting for transfers between devices: 24.7 us -> 27.2 us  [exchange(): return lax.ppermute(x, axis, [(i, i ^ distance) for i in range(size)])]
    ppermute x23, starting transfers between devices: 30.7 us -> 28.2 us  [exchange(): return lax.ppermute(x, axis, [(i, i ^ distance) for i in range(size)])]
    pallas_call x5, Pallas kernels: 4.13 us -> 5.18 us  [the longest x2 3.68 us: right_terms(): pl.pallas_call(functools.partial(right_kernel, 0 if own else 1), grid_spe...]
  transfers between devices with their start and end apart: 23 -> 23, of which waited for: 13 -> 11; matrix products, arithmetic and copies ran while one was open for 1% -> 1% of each run, Pallas kernels for 22% -> 21%
where the time goes in v12:
time: 88 us; the launch traced here: 87.9 us
  Pallas kernels  30.9 us (35%)
  starting transfers between devices  28.2 us (32%)
  waiting for transfers between devices  27.2 us (31%)
  between operations  0.88 us (1%)
    ppermute x23, starting transfers between devices, exchange(): return lax.ppermute(x, axis, [(i, i ^ distance) for i in range(size)])  28.2 us
    ppermute x23, waiting for transfers between devices, exchange(): return lax.ppermute(x, axis, [(i, i ^ distance) for i in range(size)])  27.2 us
    pallas_call x3, Pallas kernels, outputs(): pl.pallas_call(functools.partial(outputs_kernel, jobs, where, capacity),...  12.2 us
    pallas_call x1, Pallas kernels, left_terms(): pl.pallas_call(left_kernel, grid_spec=pltpu.PrefetchScalarGridSpec(num_sc...  8.78 us
    pallas_call x2, Pallas kernels, right_terms(): pl.pallas_call(functools.partial(right_kernel, 0 if own else 1), grid_spe...  3.68 us
    pallas_call x1, Pallas kernels, base_of(): pl.pallas_call(base_kernel, grid_spec=pltpu.PrefetchScalarGridSpec(num_sc...  3.13 us
  transfers between devices with their start and end apart: 23, of which 11 were waited for; matrix products, arithmetic and copies ran while one was open for 1% of the time, Pallas kernels for 21%

profile of v12, /device:TPU:1, one launch (start us, length us, event | category | flops | bytes accessed | tf_op | source)
XLA Modules:
  0.0 87.9 jit_solution(5288592727061218155)
XLA Ops:
  0.8 3.1 %base.1 = (bf16[2,96,3072]{2,1,0:T(8,128)(2,1)S(1)}, f32[2,96,3072]{2,1,0:T(8,128)S(1)}, f32[2,96,3072]{2,1,0:T(8,128)S(1)}, bf16[160,3072]{1,0:T(8,128)(2,1)S(1)}, bf16[160,3072]{1,0:T(8,128)(2,1)S(1)}) custom-call(s32[8]{0:T(128)S(1)} %stack.34.pos, f32[1,2,96,3072]{3,2,1,0:T(8,128)} %momentum_ref.1, f32[1,2,96,3072]{3,2,1,0:T(8,128)} %master_ref.1), custom_call_target="tpu_custom_call" | custom-call | flops 1000 | bytes 1000 | tf_op jit(solution)/shard_map/base/pallas_call | solution.py:518
  3.9 2.1 %collective-permute-start.5 = (bf16[160,3072]{1,0:T(8,128)(2,1)S(1)}, bf16[160,3072]{1,0:T(8,128)(2,1)S(1)}, u32[]{:S(2)}, u32[]{:S(2)}) collective-permute-start(bf16[160,3072]{1,0:T(8,128)(2,1)S(1)} %get-tuple-element.51), channel_id=1, source_target_pairs={{0,1},{1,0},{2,3},{3,2},{4,5},{5,4},{6,7},{7,6},{8,9},{9,8},{10,11... | collective-permute-start | bytes 2949128 | tf_op jit(solution)/shard_map/ppermute | solution.py:33
  6.0 1.2 %collective-permute-start.6 = (bf16[160,3072]{1,0:T(8,128)(2,1)S(1)}, bf16[160,3072]{1,0:T(8,128)(2,1)S(1)}, u32[]{:S(2)}, u32[]{:S(2)}) collective-permute-start(bf16[160,3072]{1,0:T(8,128)(2,1)S(1)} %get-tuple-element.52), channel_id=1, source_target_pairs={{0,2},{1,3},{2,0},{3,1},{4,6},{5,7},{6,4},{7,5},{8,10},{9,11},{10,... | collective-permute-start | bytes 2949128 | tf_op jit(solution)/shard_map/ppermute | solution.py:33
  7.3 8.8 %left_terms.1 = (bf16[8,192,3072]{2,1,0:T(8,128)(2,1)S(1)}, f32[208,128]{1,0:T(8,128)S(1)}, f32[208,128]{1,0:T(8,128)S(1)}) custom-call(s32[8]{0:T(128)S(1)} %stack.34.pos, bf16[1,8,192,3072]{3,2,1,0:T(8,128)(2,1)} %g_ref.1, bf16[1,8,192,3072]{3,2,1,0:T(8,128)(2,1)} %f_ref.1, bf16[8,32,3072]{2,1,0:T(8,128)(2,1)} %bitcast.17, f32[1,2688]{1,0:T(1,128)S(1)} %copy-done.2), custom_call_target="tpu_custom_call" | custom-call | flops 1000 | bytes 1000 | tf_op jit(solution)/shard_map/left_terms/pallas_call | solution.py:82
  16.1 1.3 %collective-permute-start = (f32[208,128]{1,0:T(8,128)S(1)}, f32[208,128]{1,0:T(8,128)S(1)}, u32[]{:S(2)}, u32[]{:S(2)}) collective-permute-start(f32[208,128]{1,0:T(8,128)S(1)} %get-tuple-element.45), channel_id=1, source_target_pairs={{0,4},{4,0},{8,12},{12,8},{16,20},{20,16},{24,28},{28,24},{1,5},{5... | collective-permute-start | bytes 319496 | tf_op jit(solution)/shard_map/ppermute | solution.py:33
  17.4 1.0 %collective-permute-done.refs_1_ = f32[208,128]{1,0:T(8,128)S(1)} collective-permute-done((f32[208,128]{1,0:T(8,128)S(1)}, f32[208,128]{1,0:T(8,128)S(1)}, u32[]{:S(2)}, u32[]{:S(2)}) %collective-permute-start) | collective-permute-done | bytes 106528 | tf_op jit(solution)/shard_map/ppermute | solution.py:33
  18.4 3.4 %collective-permute-start.3 = (bf16[208,128]{1,0:T(8,128)(2,1)S(1)}, bf16[208,128]{1,0:T(8,128)(2,1)S(1)}, u32[]{:S(2)}, u32[]{:S(2)}) collective-permute-start(bf16[208,128]{1,0:T(8,128)(2,1)S(1)} %add.27.refs_0_), channel_id=1, source_target_pairs={{0,24},{4,28},{8,16},{12,20},{16,8},{20,12},{24,0},{28,4},{1,25},{... | collective-permute-start | bytes 159752 | tf_op jit(solution)/shard_map/ppermute | solution.py:33
  22.1 1.3 %collective-permute-done.3.refs_3_ = bf16[208,128]{1,0:T(8,128)(2,1)S(1)} collective-permute-done((bf16[208,128]{1,0:T(8,128)(2,1)S(1)}, bf16[208,128]{1,0:T(8,128)(2,1)S(1)}, u32[]{:S(2)}, u32[]{:S(2)}) %collective-permute-start.3) | collective-permute-done | bytes 53280 | tf_op jit(solution)/shard_map/ppermute | solution.py:33
  23.4 3.1 %collective-permute-done.2.refs_2_ = bf16[208,128]{1,0:T(8,128)(2,1)S(1)} collective-permute-done((bf16[208,128]{1,0:T(8,128)(2,1)S(1)}, bf16[208,128]{1,0:T(8,128)(2,1)S(1)}, u32[]{:S(2)}, u32[]{:S(2)}) %collective-permute-start.2) | collective-permute-done | bytes 53280 | tf_op jit(solution)/shard_map/ppermute | solution.py:33
  26.6 1.0 %collective-permute-start.4 = (f32[208,128]{1,0:T(8,128)S(1)}, f32[208,128]{1,0:T(8,128)S(1)}, u32[]{:S(2)}, u32[]{:S(2)}) collective-permute-start(f32[208,128]{1,0:T(8,128)S(1)} %add.28.refs_0_.sums_ref), channel_id=1, source_target_pairs={{0,4},{4,0},{8,12},{12,8},{16,20},{20,16},{24,28},{28,24},{1,5},{5... | collective-permute-start | bytes 319496 | tf_op jit(solution)/shard_map/ppermute | solution.py:33
  27.6 1.6 %right_send.1 = (bf16[4,1,32,3072]{3,2,1,0:T(8,128)(2,1)S(1)}, bf16[192,128]{1,0:T(8,128)(2,1)S(1)}, bf16[4,192,32]{2,1,0:T(8,128)(2,1)S(1)}, bf16[128,192]{1,0:T(8,128)(2,1)S(1)}) custom-call(s32[8]{0:T(128)S(1)} %stack.34.pos, f32[208,128]{1,0:T(8,128)S(1)} %add.28.refs_0_.sums_ref, f32[8,32,32]{2,1,0:T(8,128)S(1)} %copy-done, ...), custom_call_target="tpu_custom_call" | custom-call | flops 1000 | bytes 1000 | tf_op jit(solution)/shard_map/right_send/pallas_call | solution.py:197
  29.2 1.1 %right_more.1 = bf16[4,1,32,3072]{3,2,1,0:T(8,128)(2,1)S(1)} custom-call(s32[8]{0:T(128)S(1)} %stack.34.pos, bf16[128,192]{1,0:T(8,128)(2,1)S(1)} %get-tuple-element.49.lt_ref, bf16[8,192,3072]{2,1,0:T(8,128)(2,1)S(1)} %get-tuple-element.43.comp_ref, bf16[4,1,32,3072]{3,2,1,0:T(8,128)(2,1)S(1)} %get-tuple-element.50.refs_0_, ...), custom_call_target="tpu_custom_call", output_to_operand_aliasing={{}: (3, {})} | custom-call | flops 1000 | bytes 1000 | tf_op jit(solution)/shard_map/right_more/pallas_call | solution.py:166
  30.3 1.1 %collective-permute-start.7 = (bf16[4,1,32,3072]{3,2,1,0:T(8,128)(2,1)S(1)}, bf16[4,1,32,3072]{3,2,1,0:T(8,128)(2,1)S(1)}, u32[]{:S(2)}, u32[]{:S(2)}) collective-permute-start(bf16[4,1,32,3072]{3,2,1,0:T(8,128)(2,1)S(1)} %right_more.1), channel_id=1, source_target_pairs={{0,4},{4,0},{8,12},{12,8},{16,20},{20,16},{24,28},{28,24},{1,5},{5... | collective-permute-start | bytes 2359304 | tf_op jit(solution)/shard_map/ppermute | solution.py:33
  31.4 2.1 %right_keep.1 = (f32[16,256]{1,0:T(8,128)S(1)}, f32[4,1,32,3072]{3,2,1,0:T(8,128)S(1)}, bf16[192,128]{1,0:T(8,128)(2,1)S(1)}, bf16[4,192,32]{2,1,0:T(8,128)(2,1)S(1)}, bf16[128,192]{1,0:T(8,128)(2,1)}) custom-call(s32[8]{0:T(128)S(1)} %stack.34.pos, f32[208,128]{1,0:T(8,128)S(1)} %collective-permute-done.4.sums_ref.refs_1_, f32[8,32,32]{2,1,0:T(8,128)S(1)} %copy-done, ...), custom_call_target="tpu_custom_call" | custom-call | flops 1000 | bytes 1000 | tf_op jit(solution)/shard_map/right_keep/pallas_call | solution.py:197
  34.3 1.4 %collective-permute-start.9 = (bf16[40,3072]{1,0:T(8,128)(2,1)S(1)}, bf16[40,3072]{1,0:T(8,128)(2,1)S(1)}, u32[]{:S(2)}, u32[]{:S(2)}) collective-permute-start(bf16[40,3072]{1,0:T(8,128)(2,1)S(1)} %get-tuple-element.58), channel_id=1, source_target_pairs={{0,2},{1,3},{2,0},{3,1},{4,6},{5,7},{6,4},{7,5},{8,10},{9,11},{10,... | collective-permute-start | bytes 737288 | tf_op jit(solution)/shard_map/ppermute | solution.py:33
  35.8 1.2 %collective-permute-start.10 = (bf16[40,3072]{1,0:T(8,128)(2,1)S(1)}, bf16[40,3072]{1,0:T(8,128)(2,1)S(1)}, u32[]{:S(2)}, u32[]{:S(2)}) collective-permute-start(bf16[40,3072]{1,0:T(8,128)(2,1)S(1)} %get-tuple-element.59), channel_id=1, source_target_pairs={{0,3},{1,2},{2,1},{3,0},{4,7},{5,6},{6,5},{7,4},{8,11},{9,10},{10,... | collective-permute-start | bytes 737288 | tf_op jit(solution)/shard_map/ppermute | solution.py:33
  36.9 4.8 %collective-permute-done.8.refs_0_ = bf16[40,3072]{1,0:T(8,128)(2,1)S(1)} collective-permute-done((bf16[40,3072]{1,0:T(8,128)(2,1)S(1)}, bf16[40,3072]{1,0:T(8,128)(2,1)S(1)}, u32[]{:S(2)}, u32[]{:S(2)}) %collective-permute-start.8) | collective-permute-done | bytes 245792 | tf_op jit(solution)/shard_map/ppermute | solution.py:33
  41.7 6.2 %collective-permute-done.10.refs_2_ = bf16[40,3072]{1,0:T(8,128)(2,1)S(1)} collective-permute-done((bf16[40,3072]{1,0:T(8,128)(2,1)S(1)}, bf16[40,3072]{1,0:T(8,128)(2,1)S(1)}, u32[]{:S(2)}, u32[]{:S(2)}) %collective-permute-start.10) | collective-permute-done | bytes 245792 | tf_op jit(solution)/shard_map/ppermute | solution.py:33
  49.1 1.1 %collective-permute-start.12 = (bf16[128,3072]{1,0:T(8,128)(2,1)S(1)}, bf16[128,3072]{1,0:T(8,128)(2,1)S(1)}, u32[]{:S(2)}, u32[]{:S(2)}) collective-permute-start(bf16[128,3072]{1,0:T(8,128)(2,1)S(1)} %get-tuple-element.63), channel_id=1, source_target_pairs={{0,2},{1,3},{2,0},{3,1},{4,6},{5,7},{6,4},{7,5},{8,10},{9,11},{10,... | collective-permute-start | bytes 2359304 | tf_op jit(solution)/shard_map/ppermute | solution.py:33
  50.2 1.3 %collective-permute-start.13 = (bf16[32,768]{1,0:T(8,128)(2,1)S(1)}, bf16[32,768]{1,0:T(8,128)(2,1)S(1)}, u32[]{:S(2)}, u32[]{:S(2)}) collective-permute-start(bf16[32,768]{1,0:T(8,128)(2,1)S(1)} %get-tuple-element.65), channel_id=1, source_target_pairs={{0,8},{4,12},{8,0},{12,4},{16,24},{20,28},{24,16},{28,20},{1,9},{5... | collective-permute-start | bytes 147464 | tf_op jit(solution)/shard_map/ppermute | solution.py:33
  51.5 2.3 %collective-permute-start.14 = (bf16[32,768]{1,0:T(8,128)(2,1)S(1)}, bf16[32,768]{1,0:T(8,128)(2,1)S(1)}, u32[]{:S(2)}, u32[]{:S(2)}) collective-permute-start(bf16[32,768]{1,0:T(8,128)(2,1)S(1)} %get-tuple-element.66), channel_id=1, source_target_pairs={{0,16},{4,20},{8,24},{12,28},{16,0},{20,4},{24,8},{28,12},{1,17},{... | collective-permute-start | bytes 147464 | tf_op jit(solution)/shard_map/ppermute | solution.py:33
  53.9 2.0 %collective-permute-done.14.refs_2_ = bf16[32,768]{1,0:T(8,128)(2,1)S(1)} collective-permute-done((bf16[32,768]{1,0:T(8,128)(2,1)S(1)}, bf16[32,768]{1,0:T(8,128)(2,1)S(1)}, u32[]{:S(2)}, u32[]{:S(2)}) %collective-permute-start.14) | collective-permute-done | bytes 49184 | tf_op jit(solution)/shard_map/ppermute | solution.py:33
  55.9 2.8 %collective-permute-done.15.refs_3_ = bf16[32,768]{1,0:T(8,128)(2,1)S(1)} collective-permute-done((bf16[32,768]{1,0:T(8,128)(2,1)S(1)}, bf16[32,768]{1,0:T(8,128)(2,1)S(1)}, u32[]{:S(2)}, u32[]{:S(2)}) %collective-permute-start.15) | collective-permute-done | bytes 49184 | tf_op jit(solution)/shard_map/ppermute | solution.py:33
  58.7 1.0 %collective-permute-start.18 = (bf16[32,768]{1,0:T(8,128)(2,1)S(1)}, bf16[32,768]{1,0:T(8,128)(2,1)S(1)}, u32[]{:S(2)}, u32[]{:S(2)}) collective-permute-start(bf16[32,768]{1,0:T(8,128)(2,1)S(1)} %add.29.refs_0_), channel_id=1, source_target_pairs={{0,24},{4,28},{8,16},{12,20},{16,8},{20,12},{24,0},{28,4},{1,25},{... | collective-permute-start | bytes 147464 | tf_op jit(solution)/shard_map/ppermute | solution.py:33
  59.7 2.6 %collective-permute-start.16 = (bf16[32,768]{1,0:T(8,128)(2,1)S(1)}, bf16[32,768]{1,0:T(8,128)(2,1)S(1)}, u32[]{:S(2)}, u32[]{:S(2)}) collective-permute-start(bf16[32,768]{1,0:T(8,128)(2,1)S(1)} %add.29.refs_0_), channel_id=1, source_target_pairs={{0,8},{4,12},{8,0},{12,4},{16,24},{20,28},{24,16},{28,20},{1,9},{5... | collective-permute-start | bytes 147464 | tf_op jit(solution)/shard_map/ppermute | solution.py:33
  63.6 1.5 %collective-permute-done.17.refs_2_ = bf16[32,768]{1,0:T(8,128)(2,1)S(1)} collective-permute-done((bf16[32,768]{1,0:T(8,128)(2,1)S(1)}, bf16[32,768]{1,0:T(8,128)(2,1)S(1)}, u32[]{:S(2)}, u32[]{:S(2)}) %collective-permute-start.17) | collective-permute-done | bytes 49184 | tf_op jit(solution)/shard_map/ppermute | solution.py:33
  66.6 1.2 %collective-permute-start.19 = (bf16[4,32,768]{2,1,0:T(8,128)(2,1)S(1)}, bf16[4,32,768]{2,1,0:T(8,128)(2,1)S(1)}, u32[]{:S(2)}, u32[]{:S(2)}) collective-permute-start(bf16[4,32,768]{2,1,0:T(8,128)(2,1)S(1)} %stack.35.refs_0_), channel_id=1, source_target_pairs={{0,1},{1,0},{2,3},{3,2},{4,5},{5,4},{6,7},{7,6},{8,9},{9,8},{10,11... | collective-permute-start | bytes 589832 | tf_op jit(solution)/shard_map/ppermute | solution.py:33
  68.2 2.1 %outputs.3 = (bf16[1,8,192,3072]{3,2,1,0:T(8,128)(2,1)}, bf16[8,96,3072]{2,1,0:T(8,128)(2,1)}, f32[8,128]{1,0:T(8,128)S(1)}) custom-call(s32[8]{0:T(128)S(1)} %stack.34.pos, s32[8]{0:T(128)S(1)} %copy-done.3, bf16[8,192,3072]{2,1,0:T(8,128)(2,1)S(1)} %get-tuple-element.43.comp_ref, bf16[4,192,32]{2,1,0:T(8,128)(2,1)S(1)} %get-tuple-element.46.near_ref, ...), custom_call_target="tpu_custom_call" | custom-call | flops 1000 | bytes 1000 | tf_op jit(solution)/shard_map/outputs/pallas_call | solution.py:470
  70.7 3.5 %collective-permute-done.20.refs_2_ = bf16[4,32,768]{2,1,0:T(8,128)(2,1)S(1)} collective-permute-done((bf16[4,32,768]{2,1,0:T(8,128)(2,1)S(1)}, bf16[4,32,768]{2,1,0:T(8,128)(2,1)S(1)}, u32[]{:S(2)}, u32[]{:S(2)}) %collective-permute-start.20) | collective-permute-done | bytes 196640 | tf_op jit(solution)/shard_map/ppermute | solution.py:33
  74.2 3.6 %collective-permute-start.22 = (bf16[4,1,4,32,768]{4,3,2,1,0:T(8,128)(2,1)S(1)}, bf16[4,1,4,32,768]{4,3,2,1,0:T(8,128)(2,1)S(1)}, u32[]{:S(2)}, u32[]{:S(2)}) collective-permute-start(bf16[4,1,4,32,768]{4,3,2,1,0:T(8,128)(2,1)S(1)} %bitcast.12), channel_id=1, source_target_pairs={{0,4},{4,0},{8,12},{12,8},{16,20},{20,16},{24,28},{28,24},{1,5},{5... | collective-permute-start | bytes 2359304 | tf_op jit(solution)/shard_map/ppermute | solution.py:33
  77.8 3.9 %outputs.4 = (bf16[1,8,192,3072]{3,2,1,0:T(8,128)(2,1)}, bf16[8,96,3072]{2,1,0:T(8,128)(2,1)}, f32[8,128]{1,0:T(8,128)}) custom-call(s32[8]{0:T(128)S(1)} %stack.34.pos, s32[8]{0:T(128)S(1)} %copy-done.3, bf16[8,192,3072]{2,1,0:T(8,128)(2,1)S(1)} %get-tuple-element.43.comp_ref, ...), custom_call_target="tpu_custom_call", output_to_operand_aliasing={{0}: (8, {}), {1}: (9, {})} | custom-call | flops 1000 | bytes 1000 | tf_op jit(solution)/shard_map/outputs/pallas_call | solution.py:470
  81.7 6.2 %outputs.5 = (bf16[1,8,192,3072]{3,2,1,0:T(8,128)(2,1)}, bf16[8,96,3072]{2,1,0:T(8,128)(2,1)}, f32[1,2,96,3072]{3,2,1,0:T(8,128)}, f32[1,2,96,3072]{3,2,1,0:T(8,128)}, f32[8,128]{1,0:T(8,128)}) custom-call(s32[8]{0:T(128)S(1)} %stack.34.pos, s32[8]{0:T(128)S(1)} %copy-done.3, ...), custom_call_target="tpu_custom_call", output_to_operand_aliasing={{0}: (11, {}), {1}: (12, {})} | custom-call | flops 1000 | bytes 1000 | tf_op jit(solution)/shard_map/outputs/pallas_call | solution.py:470
  (46 shorter events, 6.2 us)
Async XLA Ops:
  0.6 6.7 %copy-start.2 = (f32[1,2688]{1,0:T(1,128)S(1)}, f32[1,2688]{1,0:T(1,128)}, u32[]{:S(2)}) copy-start(f32[1,2688]{1,0:T(1,128)} %vec_ref.1) | copy-start | bytes 32260
  3.9 25.2 %collective-permute-start.5 = (bf16[160,3072]{1,0:T(8,128)(2,1)S(1)}, bf16[160,3072]{1,0:T(8,128)(2,1)S(1)}, u32[]{:S(2)}, u32[]{:S(2)}) collective-permute-start(bf16[160,3072]{1,0:T(8,128)(2,1)S(1)} %get-tuple-element.51), channel_id=1, source_target_pairs={{0,1},{1,0},{2,3},{3,2},{4,5},{5,4},{6,7},{7,6},{8,9},{9,8},{10,11... | collective-permute-start | bytes 2949128 | tf_op jit(solution)/shard_map/ppermute | solution.py:33
  6.0 23.1 %collective-permute-start.6 = (bf16[160,3072]{1,0:T(8,128)(2,1)S(1)}, bf16[160,3072]{1,0:T(8,128)(2,1)S(1)}, u32[]{:S(2)}, u32[]{:S(2)}) collective-permute-start(bf16[160,3072]{1,0:T(8,128)(2,1)S(1)} %get-tuple-element.52), channel_id=1, source_target_pairs={{0,2},{1,3},{2,0},{3,1},{4,6},{5,7},{6,4},{7,5},{8,10},{9,11},{10,... | collective-permute-start | bytes 2949128 | tf_op jit(solution)/shard_map/ppermute | solution.py:33
  7.3 20.3 %copy-start = (f32[8,32,32]{2,1,0:T(8,128)S(1)}, f32[8,32,32]{2,1,0:T(8,128)}, u32[]{:S(2)}) copy-start(f32[8,32,32]{2,1,0:T(8,128)} %gram_ref.3) | copy-start | bytes 98308
  16.1 2.3 %collective-permute-start = (f32[208,128]{1,0:T(8,128)S(1)}, f32[208,128]{1,0:T(8,128)S(1)}, u32[]{:S(2)}, u32[]{:S(2)}) collective-permute-start(f32[208,128]{1,0:T(8,128)S(1)} %get-tuple-element.45), channel_id=1, source_target_pairs={{0,4},{4,0},{8,12},{12,8},{16,20},{20,16},{24,28},{28,24},{1,5},{5... | collective-permute-start | bytes 319496 | tf_op jit(solution)/shard_map/ppermute | solution.py:33
  18.4 5.0 %collective-permute-start.3 = (bf16[208,128]{1,0:T(8,128)(2,1)S(1)}, bf16[208,128]{1,0:T(8,128)(2,1)S(1)}, u32[]{:S(2)}, u32[]{:S(2)}) collective-permute-start(bf16[208,128]{1,0:T(8,128)(2,1)S(1)} %add.27.refs_0_), channel_id=1, source_target_pairs={{0,24},{4,28},{8,16},{12,20},{16,8},{20,12},{24,0},{28,4},{1,25},{... | collective-permute-start | bytes 159752 | tf_op jit(solution)/shard_map/ppermute | solution.py:33
  21.7 4.8 %collective-permute-start.2 = (bf16[208,128]{1,0:T(8,128)(2,1)S(1)}, bf16[208,128]{1,0:T(8,128)(2,1)S(1)}, u32[]{:S(2)}, u32[]{:S(2)}) collective-permute-start(bf16[208,128]{1,0:T(8,128)(2,1)S(1)} %add.27.refs_0_), channel_id=1, source_target_pairs={{0,16},{4,20},{8,24},{12,28},{16,0},{20,4},{24,8},{28,12},{1,17},{... | collective-permute-start | bytes 159752 | tf_op jit(solution)/shard_map/ppermute | solution.py:33
  21.7 4.8 %collective-permute-start.1 = (bf16[208,128]{1,0:T(8,128)(2,1)S(1)}, bf16[208,128]{1,0:T(8,128)(2,1)S(1)}, u32[]{:S(2)}, u32[]{:S(2)}) collective-permute-start(bf16[208,128]{1,0:T(8,128)(2,1)S(1)} %add.27.refs_0_), channel_id=1, source_target_pairs={{0,8},{4,12},{8,0},{12,4},{16,24},{20,28},{24,16},{28,20},{1,9},{5... | collective-permute-start | bytes 159752 | tf_op jit(solution)/shard_map/ppermute | solution.py:33
  26.6 2.6 %collective-permute-start.4 = (f32[208,128]{1,0:T(8,128)S(1)}, f32[208,128]{1,0:T(8,128)S(1)}, u32[]{:S(2)}, u32[]{:S(2)}) collective-permute-start(f32[208,128]{1,0:T(8,128)S(1)} %add.28.refs_0_.sums_ref), channel_id=1, source_target_pairs={{0,4},{4,0},{8,12},{12,8},{16,20},{20,16},{24,28},{28,24},{1,5},{5... | collective-permute-start | bytes 319496 | tf_op jit(solution)/shard_map/ppermute | solution.py:33
  30.3 3.2 %collective-permute-start.7 = (bf16[4,1,32,3072]{3,2,1,0:T(8,128)(2,1)S(1)}, bf16[4,1,32,3072]{3,2,1,0:T(8,128)(2,1)S(1)}, u32[]{:S(2)}, u32[]{:S(2)}) collective-permute-start(bf16[4,1,32,3072]{3,2,1,0:T(8,128)(2,1)S(1)} %right_more.1), channel_id=1, source_target_pairs={{0,4},{4,0},{8,12},{12,8},{16,20},{20,16},{24,28},{28,24},{1,5},{5... | collective-permute-start | bytes 2359304 | tf_op jit(solution)/shard_map/ppermute | solution.py:33
  33.5 28.8 %copy-start.4 = (f32[2688]{0:T(1024)S(1)}, f32[2688]{0:T(1024)}, u32[]{:S(2)}) copy-start(f32[2688]{0:T(1024)} %param.19) | copy-start | bytes 32260
  33.5 28.8 %copy-start.5 = (f32[2688]{0:T(1024)S(1)}, f32[2688]{0:T(1024)}, u32[]{:S(2)}) copy-start(f32[2688]{0:T(1024)} %param.18) | copy-start | bytes 32260
  34.2 7.5 %collective-permute-start.8 = (bf16[40,3072]{1,0:T(8,128)(2,1)S(1)}, bf16[40,3072]{1,0:T(8,128)(2,1)S(1)}, u32[]{:S(2)}, u32[]{:S(2)}) collective-permute-start(bf16[40,3072]{1,0:T(8,128)(2,1)S(1)} %get-tuple-element.57), channel_id=1, source_target_pairs={{0,1},{1,0},{2,3},{3,2},{4,5},{5,4},{6,7},{7,6},{8,9},{9,8},{10,11... | collective-permute-start | bytes 737288 | tf_op jit(solution)/shard_map/ppermute | solution.py:33
  34.3 7.3 %collective-permute-start.9 = (bf16[40,3072]{1,0:T(8,128)(2,1)S(1)}, bf16[40,3072]{1,0:T(8,128)(2,1)S(1)}, u32[]{:S(2)}, u32[]{:S(2)}) collective-permute-start(bf16[40,3072]{1,0:T(8,128)(2,1)S(1)} %get-tuple-element.58), channel_id=1, source_target_pairs={{0,2},{1,3},{2,0},{3,1},{4,6},{5,7},{6,4},{7,5},{8,10},{9,11},{10,... | collective-permute-start | bytes 737288 | tf_op jit(solution)/shard_map/ppermute | solution.py:33
  35.8 12.1 %collective-permute-start.10 = (bf16[40,3072]{1,0:T(8,128)(2,1)S(1)}, bf16[40,3072]{1,0:T(8,128)(2,1)S(1)}, u32[]{:S(2)}, u32[]{:S(2)}) collective-permute-start(bf16[40,3072]{1,0:T(8,128)(2,1)S(1)} %get-tuple-element.59), channel_id=1, source_target_pairs={{0,3},{1,2},{2,1},{3,0},{4,7},{5,6},{6,5},{7,4},{8,11},{9,10},{10,... | collective-permute-start | bytes 737288 | tf_op jit(solution)/shard_map/ppermute | solution.py:33
  48.7 19.1 %collective-permute-start.11 = (bf16[128,3072]{1,0:T(8,128)(2,1)S(1)}, bf16[128,3072]{1,0:T(8,128)(2,1)S(1)}, u32[]{:S(2)}, u32[]{:S(2)}) collective-permute-start(bf16[128,3072]{1,0:T(8,128)(2,1)S(1)} %get-tuple-element.62), channel_id=1, source_target_pairs={{0,1},{1,0},{2,3},{3,2},{4,5},{5,4},{6,7},{7,6},{8,9},{9,8},{10,11... | collective-permute-start | bytes 2359304 | tf_op jit(solution)/shard_map/ppermute | solution.py:33
  49.1 18.7 %collective-permute-start.12 = (bf16[128,3072]{1,0:T(8,128)(2,1)S(1)}, bf16[128,3072]{1,0:T(8,128)(2,1)S(1)}, u32[]{:S(2)}, u32[]{:S(2)}) collective-permute-start(bf16[128,3072]{1,0:T(8,128)(2,1)S(1)} %get-tuple-element.63), channel_id=1, source_target_pairs={{0,2},{1,3},{2,0},{3,1},{4,6},{5,7},{6,4},{7,5},{8,10},{9,11},{10,... | collective-permute-start | bytes 2359304 | tf_op jit(solution)/shard_map/ppermute | solution.py:33
  50.2 3.6 %collective-permute-start.13 = (bf16[32,768]{1,0:T(8,128)(2,1)S(1)}, bf16[32,768]{1,0:T(8,128)(2,1)S(1)}, u32[]{:S(2)}, u32[]{:S(2)}) collective-permute-start(bf16[32,768]{1,0:T(8,128)(2,1)S(1)} %get-tuple-element.65), channel_id=1, source_target_pairs={{0,8},{4,12},{8,0},{12,4},{16,24},{20,28},{24,16},{28,20},{1,9},{5... | collective-permute-start | bytes 147464 | tf_op jit(solution)/shard_map/ppermute | solution.py:33
  51.5 4.4 %collective-permute-start.14 = (bf16[32,768]{1,0:T(8,128)(2,1)S(1)}, bf16[32,768]{1,0:T(8,128)(2,1)S(1)}, u32[]{:S(2)}, u32[]{:S(2)}) collective-permute-start(bf16[32,768]{1,0:T(8,128)(2,1)S(1)} %get-tuple-element.66), channel_id=1, source_target_pairs={{0,16},{4,20},{8,24},{12,28},{16,0},{20,4},{24,8},{28,12},{1,17},{... | collective-permute-start | bytes 147464 | tf_op jit(solution)/shard_map/ppermute | solution.py:33
  53.9 4.8 %collective-permute-start.15 = (bf16[32,768]{1,0:T(8,128)(2,1)S(1)}, bf16[32,768]{1,0:T(8,128)(2,1)S(1)}, u32[]{:S(2)}, u32[]{:S(2)}) collective-permute-start(bf16[32,768]{1,0:T(8,128)(2,1)S(1)} %get-tuple-element.67), channel_id=1, source_target_pairs={{0,24},{4,28},{8,16},{12,20},{16,8},{20,12},{24,0},{28,4},{1,25},{... | collective-permute-start | bytes 147464 | tf_op jit(solution)/shard_map/ppermute | solution.py:33
  58.7 4.9 %collective-permute-start.18 = (bf16[32,768]{1,0:T(8,128)(2,1)S(1)}, bf16[32,768]{1,0:T(8,128)(2,1)S(1)}, u32[]{:S(2)}, u32[]{:S(2)}) collective-permute-start(bf16[32,768]{1,0:T(8,128)(2,1)S(1)} %add.29.refs_0_), channel_id=1, source_target_pairs={{0,24},{4,28},{8,16},{12,20},{16,8},{20,12},{24,0},{28,4},{1,25},{... | collective-permute-start | bytes 147464 | tf_op jit(solution)/shard_map/ppermute | solution.py:33
  59.7 5.3 %collective-permute-start.17 = (bf16[32,768]{1,0:T(8,128)(2,1)S(1)}, bf16[32,768]{1,0:T(8,128)(2,1)S(1)}, u32[]{:S(2)}, u32[]{:S(2)}) collective-permute-start(bf16[32,768]{1,0:T(8,128)(2,1)S(1)} %add.29.refs_0_), channel_id=1, source_target_pairs={{0,16},{4,20},{8,24},{12,28},{16,0},{20,4},{24,8},{28,12},{1,17},{... | collective-permute-start | bytes 147464 | tf_op jit(solution)/shard_map/ppermute | solution.py:33
  59.7 5.3 %collective-permute-start.16 = (bf16[32,768]{1,0:T(8,128)(2,1)S(1)}, bf16[32,768]{1,0:T(8,128)(2,1)S(1)}, u32[]{:S(2)}, u32[]{:S(2)}) collective-permute-start(bf16[32,768]{1,0:T(8,128)(2,1)S(1)} %add.29.refs_0_), channel_id=1, source_target_pairs={{0,8},{4,12},{8,0},{12,4},{16,24},{20,28},{24,16},{28,20},{1,9},{5... | collective-permute-start | bytes 147464 | tf_op jit(solution)/shard_map/ppermute | solution.py:33
  62.9 5.2 %copy-start.1 = (f32[2688]{0:T(1024)}, f32[2688]{0:T(1024)S(1)}, u32[]{:S(2)}) copy-start(f32[2688]{0:T(1024)S(1)} %get-tuple-element.80.refs_4_) | copy-start | bytes 32260
  65.1 3.1 %copy-start.3 = (s32[8]{0:T(128)S(1)}, s32[8]{0:T(128)}, u32[]{:S(2)}) copy-start(s32[8]{0:T(128)} %owners.5) | copy-start | bytes 100
  65.1 5.6 %collective-permute-start.21 = (bf16[4,32,768]{2,1,0:T(8,128)(2,1)S(1)}, bf16[4,32,768]{2,1,0:T(8,128)(2,1)S(1)}, u32[]{:S(2)}, u32[]{:S(2)}) collective-permute-start(bf16[4,32,768]{2,1,0:T(8,128)(2,1)S(1)} %stack.35.refs_0_), channel_id=1, source_target_pairs={{0,3},{1,2},{2,1},{3,0},{4,7},{5,6},{6,5},{7,4},{8,11},{9,10},{10,... | collective-permute-start | bytes 589832 | tf_op jit(solution)/shard_map/ppermute | solution.py:33
  66.0 8.2 %collective-permute-start.20 = (bf16[4,32,768]{2,1,0:T(8,128)(2,1)S(1)}, bf16[4,32,768]{2,1,0:T(8,128)(2,1)S(1)}, u32[]{:S(2)}, u32[]{:S(2)}) collective-permute-start(bf16[4,32,768]{2,1,0:T(8,128)(2,1)S(1)} %stack.35.refs_0_), channel_id=1, source_target_pairs={{0,2},{1,3},{2,0},{3,1},{4,6},{5,7},{6,4},{7,5},{8,10},{9,11},{10,... | collective-permute-start | bytes 589832 | tf_op jit(solution)/shard_map/ppermute | solution.py:33
  66.6 7.5 %collective-permute-start.19 = (bf16[4,32,768]{2,1,0:T(8,128)(2,1)S(1)}, bf16[4,32,768]{2,1,0:T(8,128)(2,1)S(1)}, u32[]{:S(2)}, u32[]{:S(2)}) collective-permute-start(bf16[4,32,768]{2,1,0:T(8,128)(2,1)S(1)} %stack.35.refs_0_), channel_id=1, source_target_pairs={{0,1},{1,0},{2,3},{3,2},{4,5},{5,4},{6,7},{7,6},{8,9},{9,8},{10,11... | collective-permute-start | bytes 589832 | tf_op jit(solution)/shard_map/ppermute | solution.py:33
  74.2 7.5 %collective-permute-start.22 = (bf16[4,1,4,32,768]{4,3,2,1,0:T(8,128)(2,1)S(1)}, bf16[4,1,4,32,768]{4,3,2,1,0:T(8,128)(2,1)S(1)}, u32[]{:S(2)}, u32[]{:S(2)}) collective-permute-start(bf16[4,1,4,32,768]{4,3,2,1,0:T(8,128)(2,1)S(1)} %bitcast.12), channel_id=1, source_target_pairs={{0,4},{4,0},{8,12},{12,8},{16,20},{20,16},{24,28},{28,24},{1,5},{5... | collective-permute-start | bytes 2359304 | tf_op jit(solution)/shard_map/ppermute | solution.py:33

commit v13 on v11

--- a/solution.py
+++ b/solution.py
@@ -309,22 +309,26 @@
     )(*after)
 
 
-def forward_kernel(cuts, *refs):
-    for source, out, first in zip(refs, refs[-len(cuts) :], cuts):
-        out[...] = source[first : first + out.shape[0]]
-
-
-def forward(parts, cuts, count, after):
-    vmem = pl.BlockSpec(memory_space=pltpu.VMEM)
-    return pl.pallas_call(
-        functools.partial(forward_kernel, cuts),
-        in_specs=[vmem] * len(parts) + [pl.BlockSpec(memory_space=pl.ANY)],
-        out_specs=[vmem] * len(parts),
-        out_shape=[jax.ShapeDtypeStruct((count,) + part.shape[1:], part.dtype) for part in parts],
+def forward_kernel(later, x_ref, y_ref, base_ref, after_ref, *outs):
+    rows = base_ref.shape[1]
+    for source, slot, out in ((y_ref, 1, outs[0]), (x_ref, 0, outs[1])):
+        out[:rows] = source[:rows]
+        out[rows:] = base_ref[slot, rows - later :]
+
+
+def forward(x, y, base, after):
+    _, rows, n = base.shape
+    later = 2 * rows - x.shape[0]
+    vmem = pl.BlockSpec(memory_space=pltpu.VMEM)
+    return pl.pallas_call(
+        functools.partial(forward_kernel, later),
+        in_specs=[vmem] * 3 + [pl.BlockSpec(memory_space=pl.ANY)],
+        out_specs=[vmem] * 2,
+        out_shape=[jax.ShapeDtypeStruct((rows + later, n), BF16)] * 2,
         compiler_params=params(),
         cost_estimate=cost(),
         name="forward",
-    )(*parts, after)
+    )(x, y, base, after)
 
 
 def rank_of(owners, k):
@@ -334,22 +338,36 @@
     return count
 
 
-def collect_kernel(places, *refs):
-    for i, (a, row) in enumerate(places):
-        refs[-1][i] = refs[a][row]
-
-
-def collect(bases, places):
-    vmem = pl.BlockSpec(memory_space=pltpu.VMEM)
-    return pl.pallas_call(
-        functools.partial(collect_kernel, places),
-        in_specs=[vmem] * len(bases),
+def collect_kernel(square, base_ref, *refs):
+    out = refs[-1]
+    capacity, rows, _ = base_ref.shape
+    out[:capacity] = base_ref[...]
+    if not square:
+        for d, ref in enumerate(refs[:-1], 1):
+            out[d * capacity : (d + 1) * capacity] = ref[...]
+        return
+    x, y, more_x, more_y = refs[:-1]
+    early = x.shape[0] - rows
+    for d, slot, first, second in ((1, 0, x, more_x), (2, 1, y, more_y)):
+        out[d * capacity + slot] = first[:rows]
+        out[d * capacity + 1 - slot, :early] = first[rows:]
+        out[d * capacity + 1 - slot, early:] = second[rows:]
+    out[3 * capacity] = more_y[:rows]
+    out[3 * capacity + 1] = more_x[:rows]
+
+
+def collect(square, n_mp, base, parts):
+    capacity, rows, n = base.shape
+    vmem = pl.BlockSpec(memory_space=pltpu.VMEM)
+    return pl.pallas_call(
+        functools.partial(collect_kernel, square),
+        in_specs=[vmem] * (1 + len(parts)),
         out_specs=vmem,
-        out_shape=jax.ShapeDtypeStruct((len(places),) + bases[0].shape[1:], BF16),
+        out_shape=jax.ShapeDtypeStruct((n_mp * capacity, rows, n), BF16),
         compiler_params=params(),
         cost_estimate=cost(),
         name="collect",
-    )(*bases)
+    )(base, *parts)
 
 
 def outputs_kernel(jobs, where, capacity, pos, owners, comp_ref, left_ref, strip_ref, base_ref, *refs):
@@ -466,8 +484,8 @@
     )(pos, owners, comp, left, strip, base, *rights, *states, *earlier)
 
 
-def base_kernel(pos, momentum_ref, master_ref, *refs):
-    out_ref, momentum, master, sems = refs
+def base_kernel(pos, momentum_ref, master_ref, out_ref, momentum, master, *refs):
+    firsts, sems = refs[:-1], refs[-1]
     capacity, rows, _ = out_ref.shape
     blocks = [(c, first) for c in range(capacity) for first in range(0, rows, BASE_ROWS)]
 
@@ -487,26 +505,31 @@
             copy.wait()
         part = slice(first, first + BASE_ROWS)
         out_ref[c, part] = (master[c, part] - 0.09 * momentum[c, part]).astype(BF16)
-
-
-def base_of(pos, momentum, master):
+    for slot, ref in enumerate(firsts):
+        ref[:rows] = out_ref[slot]
+        ref[rows:] = out_ref[1 - slot, : ref.shape[0] - rows]
+
+
+def base_of(pos, momentum, master, square):
     _, capacity, rows, n = momentum.shape
     state = jax.ShapeDtypeStruct((capacity, rows, n), F32)
-    base, momentum, master = pl.pallas_call(
+    base = jax.ShapeDtypeStruct((capacity, rows, n), BF16)
+    firsts = [jax.ShapeDtypeStruct((rows + 5 * rows // 6, n), BF16)] * (2 if square else 0)
+    base, momentum, master, *firsts = pl.pallas_call(
         base_kernel,
         grid_spec=pltpu.PrefetchScalarGridSpec(
             num_scalar_prefetch=1,
             grid=(1,),
             in_specs=[pl.BlockSpec(memory_space=pl.ANY)] * 2,
-            out_specs=[pl.BlockSpec(memory_space=pltpu.VMEM)] * 3,
+            out_specs=[pl.BlockSpec(memory_space=pltpu.VMEM)] * (3 + len(firsts)),
             scratch_shapes=[pltpu.SemaphoreType.DMA((2, capacity * rows // BASE_ROWS))],
         ),
-        out_shape=[jax.ShapeDtypeStruct((capacity, rows, n), BF16), state, state],
+        out_shape=[base, state, state] + firsts,
         compiler_params=params(),
         cost_estimate=cost(),
         name="base",
     )(pos, momentum, master)
-    return base, (momentum, master)
+    return base, (momentum, master), firsts
 
 
 def per_device(
@@ -539,11 +562,10 @@
     pos = jnp.stack(places_of).astype(jnp.int32)
     in_hbm = lambda x: pltpu.with_memory_space_constraint(x, pltpu.HBM)
 
-    square = n_mp == 4 and capacity == 2
-    base, states = base_of(pos, in_hbm(momentum), in_hbm(master_weights))
-    early = [exchange(base, "mp", d) for d in range(1, 3 if square else n_mp)]
-    bases = [base] + early
-    places = {(d, c): (d, c) for d in range(len(bases)) for c in range(capacity)}
+    square = n_mp == 4 and capacity == 2 and replica_rows % 96 == 0
+    base, states, firsts = base_of(pos, in_hbm(momentum), in_hbm(master_weights), square)
+    firsts = firsts or [base] * (n_mp - 1)
+    early = [exchange(part, "mp", d) for d, part in enumerate(firsts, 1)]
 
     nvec = vector_grads.shape[1]
     comp, near, far = left_terms(
@@ -566,10 +588,7 @@
     *final, mine = plane_sum(pos, own, strip, plane, n_z, nmat, rank)
     late = []
     if square:
-        parts = forward(early, [0, 1], 1, mine)
-        late = [exchange(part, "mp", 2 - i) for i, part in enumerate(parts)]
-        bases = bases + late
-        places[3, 0], places[3, 1] = (3, 0), (4, 0)
+        late = [exchange(part, "mp", d) for d, part in enumerate(forward(*early, base, mine), 1)]
     final = [final[0]] + [exchange(final[d], "replica", CORES * d) for d in range(1, n_z)]
     final = add(final, BF16)
     new_vector_momentum = 0.9 * vector_momentum + vector_total
@@ -577,7 +596,7 @@
 
     whole = stack([final] + along_z(final), late + [new_vector_params])
     others = [exchange(whole, "mp", d) for d in range(1, n_mp)]
-    slots = collect(bases, [places[d, c] for d in range(n_mp) for c in range(capacity)])
+    slots = collect(square, n_mp, base, early + late)
     common = (pos, owners, comp, left, mine, slots, capacity)
     shape = (half, upm) + whole.shape
     done, near_jobs, after = (), {(0, j): (0, j) for j in range(half)}, [slots]

time: 86.9 us -> 86.9 us (level)
  starting transfers between devices: 30.7 us -> 26.2 us
  waiting for transfers between devices: 24.7 us -> 29 us
    ppermute x23, starting transfers between devices: 30.7 us -> 26.2 us  [exchange(): return lax.ppermute(x, axis, [(i, i ^ distance) for i in range(size)])]
    ppermute x23, waiting for transfers between devices: 24.7 us -> 29 us  [exchange(): return lax.ppermute(x, axis, [(i, i ^ distance) for i in range(size)])]
  transfers between devices with their start and end apart: 23 -> 23, of which waited for: 13 -> 15; matrix products, arithmetic and copies ran while one was open for 1% -> 1% of each run, Pallas kernels for 22% -> 22%
where the time goes in v13:
time: 86.9 us; the launch traced here: 86.8 us
  Pallas kernels  30 us (35%)
  waiting for transfers between devices  29 us (33%)
  starting transfers between devices  26.2 us (30%)
    ppermute x23, waiting for transfers between devices, exchange(): return lax.ppermute(x, axis, [(i, i ^ distance) for i in range(size)])  29 us
    ppermute x23, starting transfers between devices, exchange(): return lax.ppermute(x, axis, [(i, i ^ distance) for i in range(size)])  26.2 us
    pallas_call x3, Pallas kernels, outputs(): pl.pallas_call(functools.partial(outputs_kernel, jobs, where, capacity),...  12.2 us
    pallas_call x1, Pallas kernels, left_terms(): pl.pallas_call(left_kernel, grid_spec=pltpu.PrefetchScalarGridSpec(num_sc...  8.78 us
    pallas_call x1, Pallas kernels, base_of(): pl.pallas_call(base_kernel, grid_spec=pltpu.PrefetchScalarGridSpec(num_sc...  3.16 us
    pallas_call x1, Pallas kernels, right_terms(): pl.pallas_call(functools.partial(send_kernel, half), grid_spec=pltpu.Pref...  2.22 us
  transfers between devices with their start and end apart: 23, of which 15 were waited for; matrix products, arithmetic and copies ran while one was open for 1% of the time, Pallas kernels for 22%

profile of v13, /device:TPU:1, one launch (start us, length us, event | category | flops | bytes accessed | tf_op | source)
XLA Modules:
  0.0 86.8 jit_solution(8375458181959532428)
XLA Ops:
  0.8 3.2 %base.1 = (bf16[2,96,3072]{2,1,0:T(8,128)(2,1)S(1)}, f32[2,96,3072]{2,1,0:T(8,128)S(1)}, f32[2,96,3072]{2,1,0:T(8,128)S(1)}, bf16[176,3072]{1,0:T(8,128)(2,1)S(1)}, bf16[176,3072]{1,0:T(8,128)(2,1)S(1)}) custom-call(s32[8]{0:T(128)S(1)} %stack.34.pos, f32[1,2,96,3072]{3,2,1,0:T(8,128)} %momentum_ref.1, f32[1,2,96,3072]{3,2,1,0:T(8,128)} %master_ref.1), custom_call_target="tpu_custom_call" | custom-call | flops 1000 | bytes 1000 | tf_op jit(solution)/shard_map/base/pallas_call | solution.py:518
  4.0 2.1 %collective-permute-start.6 = (bf16[176,3072]{1,0:T(8,128)(2,1)S(1)}, bf16[176,3072]{1,0:T(8,128)(2,1)S(1)}, u32[]{:S(2)}, u32[]{:S(2)}) collective-permute-start(bf16[176,3072]{1,0:T(8,128)(2,1)S(1)} %get-tuple-element.45), channel_id=1, source_target_pairs={{0,1},{1,0},{2,3},{3,2},{4,5},{5,4},{6,7},{7,6},{8,9},{9,8},{10,11... | collective-permute-start | bytes 3244040 | tf_op jit(solution)/shard_map/ppermute | solution.py:33
  6.1 1.2 %collective-permute-start.7 = (bf16[176,3072]{1,0:T(8,128)(2,1)S(1)}, bf16[176,3072]{1,0:T(8,128)(2,1)S(1)}, u32[]{:S(2)}, u32[]{:S(2)}) collective-permute-start(bf16[176,3072]{1,0:T(8,128)(2,1)S(1)} %get-tuple-element.46), channel_id=1, source_target_pairs={{0,2},{1,3},{2,0},{3,1},{4,6},{5,7},{6,4},{7,5},{8,10},{9,11},{10,... | collective-permute-start | bytes 3244040 | tf_op jit(solution)/shard_map/ppermute | solution.py:33
  7.3 8.8 %left_terms.1 = (bf16[8,192,3072]{2,1,0:T(8,128)(2,1)S(1)}, f32[112,256]{1,0:T(8,128)S(1)}, f32[112,256]{1,0:T(8,128)S(1)}) custom-call(s32[8]{0:T(128)S(1)} %stack.34.pos, bf16[1,8,192,3072]{3,2,1,0:T(8,128)(2,1)} %g_ref.1, bf16[1,8,192,3072]{3,2,1,0:T(8,128)(2,1)} %f_ref.1, bf16[8,32,3072]{2,1,0:T(8,128)(2,1)} %bitcast.17, f32[1,2688]{1,0:T(1,128)S(1)} %copy-done.2), custom_call_target="tpu_custom_call" | custom-call | flops 1000 | bytes 1000 | tf_op jit(solution)/shard_map/left_terms/pallas_call | solution.py:82
  16.1 1.3 %collective-permute-start = (f32[112,256]{1,0:T(8,128)S(1)}, f32[112,256]{1,0:T(8,128)S(1)}, u32[]{:S(2)}, u32[]{:S(2)}) collective-permute-start(f32[112,256]{1,0:T(8,128)S(1)} %get-tuple-element.41), channel_id=1, source_target_pairs={{0,4},{4,0},{8,12},{12,8},{16,20},{20,16},{24,28},{28,24},{1,5},{5... | collective-permute-start | bytes 344072 | tf_op jit(solution)/shard_map/ppermute | solution.py:33
  17.4 1.0 %collective-permute-done.refs_1_ = f32[112,256]{1,0:T(8,128)S(1)} collective-permute-done((f32[112,256]{1,0:T(8,128)S(1)}, f32[112,256]{1,0:T(8,128)S(1)}, u32[]{:S(2)}, u32[]{:S(2)}) %collective-permute-start) | collective-permute-done | bytes 114720 | tf_op jit(solution)/shard_map/ppermute | solution.py:33
  18.4 3.4 %collective-permute-start.3 = (bf16[112,256]{1,0:T(8,128)(2,1)S(1)}, bf16[112,256]{1,0:T(8,128)(2,1)S(1)}, u32[]{:S(2)}, u32[]{:S(2)}) collective-permute-start(bf16[112,256]{1,0:T(8,128)(2,1)S(1)} %add.27.refs_0_), channel_id=1, source_target_pairs={{0,24},{4,28},{8,16},{12,20},{16,8},{20,12},{24,0},{28,4},{1,25},{... | collective-permute-start | bytes 172040 | tf_op jit(solution)/shard_map/ppermute | solution.py:33
  22.1 1.3 %collective-permute-done.3.refs_3_ = bf16[112,256]{1,0:T(8,128)(2,1)S(1)} collective-permute-done((bf16[112,256]{1,0:T(8,128)(2,1)S(1)}, bf16[112,256]{1,0:T(8,128)(2,1)S(1)}, u32[]{:S(2)}, u32[]{:S(2)}) %collective-permute-start.3) | collective-permute-done | bytes 57376 | tf_op jit(solution)/shard_map/ppermute | solution.py:33
  23.4 3.4 %collective-permute-done.2.refs_2_ = bf16[112,256]{1,0:T(8,128)(2,1)S(1)} collective-permute-done((bf16[112,256]{1,0:T(8,128)(2,1)S(1)}, bf16[112,256]{1,0:T(8,128)(2,1)S(1)}, u32[]{:S(2)}, u32[]{:S(2)}) %collective-permute-start.2) | collective-permute-done | bytes 57376 | tf_op jit(solution)/shard_map/ppermute | solution.py:33
  26.9 1.0 %collective-permute-start.4 = (f32[112,256]{1,0:T(8,128)S(1)}, f32[112,256]{1,0:T(8,128)S(1)}, u32[]{:S(2)}, u32[]{:S(2)}) collective-permute-start(f32[112,256]{1,0:T(8,128)S(1)} %add.28.near_ref), channel_id=1, source_target_pairs={{0,4},{4,0},{8,12},{12,8},{16,20},{20,16},{24,28},{28,24},{1,5},{5... | collective-permute-start | bytes 344072 | tf_op jit(solution)/shard_map/ppermute | solution.py:33
  27.9 1.0 %collective-permute-done.4.far_ref = f32[112,256]{1,0:T(8,128)S(1)} collective-permute-done((f32[112,256]{1,0:T(8,128)S(1)}, f32[112,256]{1,0:T(8,128)S(1)}, u32[]{:S(2)}, u32[]{:S(2)}) %collective-permute-start.4) | collective-permute-done | bytes 114720 | tf_op jit(solution)/shard_map/ppermute | solution.py:33
  28.9 2.2 %right_send.1 = (bf16[4,1,32,3072]{3,2,1,0:T(8,128)(2,1)S(1)}, bf16[256,192]{1,0:T(8,128)(2,1)S(1)}, bf16[8,192,32]{2,1,0:T(8,128)(2,1)S(1)}, f32[32,256]{1,0:T(8,128)S(1)}) custom-call(s32[8]{0:T(128)S(1)} %stack.34.pos, f32[112,256]{1,0:T(8,128)S(1)} %add.28.near_ref, f32[112,256]{1,0:T(8,128)S(1)} %collective-permute-done.4.far_ref, ...), custom_call_target="tpu_custom_call" | custom-call | flops 1000 | bytes 1000 | tf_op jit(solution)/shard_map/right_send/pallas_call | solution.py:162
  31.5 1.5 %right_keep.1.refs_0_.keep_ref = f32[4,1,32,3072]{3,2,1,0:T(8,128)S(1)} custom-call(s32[8]{0:T(128)S(1)} %stack.34.pos, bf16[256,192]{1,0:T(8,128)(2,1)S(1)} %get-tuple-element.43.lt_ref, bf16[8,192,3072]{2,1,0:T(8,128)(2,1)S(1)} %get-tuple-element.39.comp_ref), custom_call_target="tpu_custom_call" | custom-call | flops 1000 | bytes 1000 | tf_op jit(solution)/shard_map/right_keep/pallas_call | solution.py:181
  34.8 2.2 %collective-permute-start.10 = (bf16[40,3072]{1,0:T(8,128)(2,1)S(1)}, bf16[40,3072]{1,0:T(8,128)(2,1)S(1)}, u32[]{:S(2)}, u32[]{:S(2)}) collective-permute-start(bf16[40,3072]{1,0:T(8,128)(2,1)S(1)} %get-tuple-element.51), channel_id=1, source_target_pairs={{0,3},{1,2},{2,1},{3,0},{4,7},{5,6},{6,5},{7,4},{8,11},{9,10},{10,... | collective-permute-start | bytes 737288 | tf_op jit(solution)/shard_map/ppermute | solution.py:33
  37.0 4.5 %collective-permute-done.8.refs_0_ = bf16[40,3072]{1,0:T(8,128)(2,1)S(1)} collective-permute-done((bf16[40,3072]{1,0:T(8,128)(2,1)S(1)}, bf16[40,3072]{1,0:T(8,128)(2,1)S(1)}, u32[]{:S(2)}, u32[]{:S(2)}) %collective-permute-start.8) | collective-permute-done | bytes 245792 | tf_op jit(solution)/shard_map/ppermute | solution.py:33
  41.5 5.3 %collective-permute-done.10.refs_2_ = bf16[40,3072]{1,0:T(8,128)(2,1)S(1)} collective-permute-done((bf16[40,3072]{1,0:T(8,128)(2,1)S(1)}, bf16[40,3072]{1,0:T(8,128)(2,1)S(1)}, u32[]{:S(2)}, u32[]{:S(2)}) %collective-permute-start.10) | collective-permute-done | bytes 245792 | tf_op jit(solution)/shard_map/ppermute | solution.py:33
  47.6 1.2 %collective-permute-start.11 = (bf16[112,3072]{1,0:T(8,128)(2,1)S(1)}, bf16[112,3072]{1,0:T(8,128)(2,1)S(1)}, u32[]{:S(2)}, u32[]{:S(2)}) collective-permute-start(bf16[112,3072]{1,0:T(8,128)(2,1)S(1)} %get-tuple-element.54), channel_id=1, source_target_pairs={{0,1},{1,0},{2,3},{3,2},{4,5},{5,4},{6,7},{7,6},{8,9},{9,8},{10,11... | collective-permute-start | bytes 2064392 | tf_op jit(solution)/shard_map/ppermute | solution.py:33
  50.0 1.6 %collective-permute-start.14 = (bf16[32,768]{1,0:T(8,128)(2,1)S(1)}, bf16[32,768]{1,0:T(8,128)(2,1)S(1)}, u32[]{:S(2)}, u32[]{:S(2)}) collective-permute-start(bf16[32,768]{1,0:T(8,128)(2,1)S(1)} %get-tuple-element.58), channel_id=1, source_target_pairs={{0,16},{4,20},{8,24},{12,28},{16,0},{20,4},{24,8},{28,12},{1,17},{... | collective-permute-start | bytes 147464 | tf_op jit(solution)/shard_map/ppermute | solution.py:33
  51.5 1.2 %collective-permute-start.15 = (bf16[32,768]{1,0:T(8,128)(2,1)S(1)}, bf16[32,768]{1,0:T(8,128)(2,1)S(1)}, u32[]{:S(2)}, u32[]{:S(2)}) collective-permute-start(bf16[32,768]{1,0:T(8,128)(2,1)S(1)} %get-tuple-element.59), channel_id=1, source_target_pairs={{0,24},{4,28},{8,16},{12,20},{16,8},{20,12},{24,0},{28,4},{1,25},{... | collective-permute-start | bytes 147464 | tf_op jit(solution)/shard_map/ppermute | solution.py:33
  52.7 1.7 %collective-permute-done.14.refs_2_ = bf16[32,768]{1,0:T(8,128)(2,1)S(1)} collective-permute-done((bf16[32,768]{1,0:T(8,128)(2,1)S(1)}, bf16[32,768]{1,0:T(8,128)(2,1)S(1)}, u32[]{:S(2)}, u32[]{:S(2)}) %collective-permute-start.14) | collective-permute-done | bytes 49184 | tf_op jit(solution)/shard_map/ppermute | solution.py:33
  54.4 1.9 %collective-permute-done.15.refs_3_ = bf16[32,768]{1,0:T(8,128)(2,1)S(1)} collective-permute-done((bf16[32,768]{1,0:T(8,128)(2,1)S(1)}, bf16[32,768]{1,0:T(8,128)(2,1)S(1)}, u32[]{:S(2)}, u32[]{:S(2)}) %collective-permute-start.15) | collective-permute-done | bytes 49184 | tf_op jit(solution)/shard_map/ppermute | solution.py:33
  56.3 1.4 %collective-permute-start.18 = (bf16[32,768]{1,0:T(8,128)(2,1)S(1)}, bf16[32,768]{1,0:T(8,128)(2,1)S(1)}, u32[]{:S(2)}, u32[]{:S(2)}) collective-permute-start(bf16[32,768]{1,0:T(8,128)(2,1)S(1)} %add.29.refs_0_), channel_id=1, source_target_pairs={{0,24},{4,28},{8,16},{12,20},{16,8},{20,12},{24,0},{28,4},{1,25},{... | collective-permute-start | bytes 147464 | tf_op jit(solution)/shard_map/ppermute | solution.py:33
  57.8 2.2 %collective-permute-start.16 = (bf16[32,768]{1,0:T(8,128)(2,1)S(1)}, bf16[32,768]{1,0:T(8,128)(2,1)S(1)}, u32[]{:S(2)}, u32[]{:S(2)}) collective-permute-start(bf16[32,768]{1,0:T(8,128)(2,1)S(1)} %add.29.refs_0_), channel_id=1, source_target_pairs={{0,8},{4,12},{8,0},{12,4},{16,24},{20,28},{24,16},{28,20},{1,9},{5... | collective-permute-start | bytes 147464 | tf_op jit(solution)/shard_map/ppermute | solution.py:33
  61.2 1.5 %collective-permute-done.17.refs_2_ = bf16[32,768]{1,0:T(8,128)(2,1)S(1)} collective-permute-done((bf16[32,768]{1,0:T(8,128)(2,1)S(1)}, bf16[32,768]{1,0:T(8,128)(2,1)S(1)}, u32[]{:S(2)}, u32[]{:S(2)}) %collective-permute-start.17) | collective-permute-done | bytes 49184 | tf_op jit(solution)/shard_map/ppermute | solution.py:33
  63.1 0.8 collective-permute-done.12.refs_3_.refs_5_
  64.0 1.6 %collective-permute-start.21 = (bf16[4,32,768]{2,1,0:T(8,128)(2,1)S(1)}, bf16[4,32,768]{2,1,0:T(8,128)(2,1)S(1)}, u32[]{:S(2)}, u32[]{:S(2)}) collective-permute-start(bf16[4,32,768]{2,1,0:T(8,128)(2,1)S(1)} %stack.35.refs_0_), channel_id=1, source_target_pairs={{0,3},{1,2},{2,1},{3,0},{4,7},{5,6},{6,5},{7,4},{8,11},{9,10},{10,... | collective-permute-start | bytes 589832 | tf_op jit(solution)/shard_map/ppermute | solution.py:33
  65.6 1.1 %collective-permute-start.19 = (bf16[4,32,768]{2,1,0:T(8,128)(2,1)S(1)}, bf16[4,32,768]{2,1,0:T(8,128)(2,1)S(1)}, u32[]{:S(2)}, u32[]{:S(2)}) collective-permute-start(bf16[4,32,768]{2,1,0:T(8,128)(2,1)S(1)} %stack.35.refs_0_), channel_id=1, source_target_pairs={{0,1},{1,0},{2,3},{3,2},{4,5},{5,4},{6,7},{7,6},{8,9},{9,8},{10,11... | collective-permute-start | bytes 589832 | tf_op jit(solution)/shard_map/ppermute | solution.py:33
  67.0 2.1 %outputs.3 = (bf16[1,8,192,3072]{3,2,1,0:T(8,128)(2,1)}, bf16[8,96,3072]{2,1,0:T(8,128)(2,1)}, f32[8,128]{1,0:T(8,128)S(1)}) custom-call(s32[8]{0:T(128)S(1)} %stack.34.pos, s32[8]{0:T(128)S(1)} %copy-done.3, bf16[8,192,3072]{2,1,0:T(8,128)(2,1)S(1)} %get-tuple-element.39.comp_ref, bf16[8,192,32]{2,1,0:T(8,128)(2,1)S(1)} %get-tuple-element.42.left_ref, ...), custom_call_target="tpu_custom_call" | custom-call | flops 1000 | bytes 1000 | tf_op jit(solution)/shard_map/outputs/pallas_call | solution.py:470
  69.6 4.7 %collective-permute-done.20.refs_2_ = bf16[4,32,768]{2,1,0:T(8,128)(2,1)S(1)} collective-permute-done((bf16[4,32,768]{2,1,0:T(8,128)(2,1)S(1)}, bf16[4,32,768]{2,1,0:T(8,128)(2,1)S(1)}, u32[]{:S(2)}, u32[]{:S(2)}) %collective-permute-start.20) | collective-permute-done | bytes 196640 | tf_op jit(solution)/shard_map/ppermute | solution.py:33
  74.3 2.3 %collective-permute-start.22 = (bf16[4,1,4,32,768]{4,3,2,1,0:T(8,128)(2,1)S(1)}, bf16[4,1,4,32,768]{4,3,2,1,0:T(8,128)(2,1)S(1)}, u32[]{:S(2)}, u32[]{:S(2)}) collective-permute-start(bf16[4,1,4,32,768]{4,3,2,1,0:T(8,128)(2,1)S(1)} %bitcast.12), channel_id=1, source_target_pairs={{0,4},{4,0},{8,12},{12,8},{16,20},{20,16},{24,28},{28,24},{1,5},{5... | collective-permute-start | bytes 2359304 | tf_op jit(solution)/shard_map/ppermute | solution.py:33
  76.6 3.9 %outputs.4 = (bf16[1,8,192,3072]{3,2,1,0:T(8,128)(2,1)}, bf16[8,96,3072]{2,1,0:T(8,128)(2,1)}, f32[8,128]{1,0:T(8,128)}) custom-call(s32[8]{0:T(128)S(1)} %stack.34.pos, s32[8]{0:T(128)S(1)} %copy-done.3, bf16[8,192,3072]{2,1,0:T(8,128)(2,1)S(1)} %get-tuple-element.39.comp_ref, ...), custom_call_target="tpu_custom_call", output_to_operand_aliasing={{0}: (7, {}), {1}: (8, {})} | custom-call | flops 1000 | bytes 1000 | tf_op jit(solution)/shard_map/outputs/pallas_call | solution.py:470
  80.6 6.2 %outputs.5 = (bf16[1,8,192,3072]{3,2,1,0:T(8,128)(2,1)}, bf16[8,96,3072]{2,1,0:T(8,128)(2,1)}, f32[1,2,96,3072]{3,2,1,0:T(8,128)}, f32[1,2,96,3072]{3,2,1,0:T(8,128)}, f32[8,128]{1,0:T(8,128)}) custom-call(s32[8]{0:T(128)S(1)} %stack.34.pos, s32[8]{0:T(128)S(1)} %copy-done.3, ...), custom_call_target="tpu_custom_call", output_to_operand_aliasing={{0}: (10, {}), {1}: (11, {})} | custom-call | flops 1000 | bytes 1000 | tf_op jit(solution)/shard_map/outputs/pallas_call | solution.py:470
  (46 shorter events, 7.2 us)
Async XLA Ops:
  0.8 6.5 %copy-start.2 = (f32[1,2688]{1,0:T(1,128)S(1)}, f32[1,2688]{1,0:T(1,128)}, u32[]{:S(2)}) copy-start(f32[1,2688]{1,0:T(1,128)} %vec_ref.1) | copy-start | bytes 32260
  4.0 29.1 %collective-permute-start.6 = (bf16[176,3072]{1,0:T(8,128)(2,1)S(1)}, bf16[176,3072]{1,0:T(8,128)(2,1)S(1)}, u32[]{:S(2)}, u32[]{:S(2)}) collective-permute-start(bf16[176,3072]{1,0:T(8,128)(2,1)S(1)} %get-tuple-element.45), channel_id=1, source_target_pairs={{0,1},{1,0},{2,3},{3,2},{4,5},{5,4},{6,7},{7,6},{8,9},{9,8},{10,11... | collective-permute-start | bytes 3244040 | tf_op jit(solution)/shard_map/ppermute | solution.py:33
  6.1 27.0 %collective-permute-start.7 = (bf16[176,3072]{1,0:T(8,128)(2,1)S(1)}, bf16[176,3072]{1,0:T(8,128)(2,1)S(1)}, u32[]{:S(2)}, u32[]{:S(2)}) collective-permute-start(bf16[176,3072]{1,0:T(8,128)(2,1)S(1)} %get-tuple-element.46), channel_id=1, source_target_pairs={{0,2},{1,3},{2,0},{3,1},{4,6},{5,7},{6,4},{7,5},{8,10},{9,11},{10,... | collective-permute-start | bytes 3244040 | tf_op jit(solution)/shard_map/ppermute | solution.py:33
  7.3 21.6 %copy-start = (f32[8,32,32]{2,1,0:T(8,128)S(1)}, f32[8,32,32]{2,1,0:T(8,128)}, u32[]{:S(2)}) copy-start(f32[8,32,32]{2,1,0:T(8,128)} %gram_ref.1) | copy-start | bytes 98308
  16.1 2.3 %collective-permute-start = (f32[112,256]{1,0:T(8,128)S(1)}, f32[112,256]{1,0:T(8,128)S(1)}, u32[]{:S(2)}, u32[]{:S(2)}) collective-permute-start(f32[112,256]{1,0:T(8,128)S(1)} %get-tuple-element.41), channel_id=1, source_target_pairs={{0,4},{4,0},{8,12},{12,8},{16,20},{20,16},{24,28},{28,24},{1,5},{5... | collective-permute-start | bytes 344072 | tf_op jit(solution)/shard_map/ppermute | solution.py:33
  18.4 5.1 %collective-permute-start.3 = (bf16[112,256]{1,0:T(8,128)(2,1)S(1)}, bf16[112,256]{1,0:T(8,128)(2,1)S(1)}, u32[]{:S(2)}, u32[]{:S(2)}) collective-permute-start(bf16[112,256]{1,0:T(8,128)(2,1)S(1)} %add.27.refs_0_), channel_id=1, source_target_pairs={{0,24},{4,28},{8,16},{12,20},{16,8},{20,12},{24,0},{28,4},{1,25},{... | collective-permute-start | bytes 172040 | tf_op jit(solution)/shard_map/ppermute | solution.py:33
  21.8 5.1 %collective-permute-start.2 = (bf16[112,256]{1,0:T(8,128)(2,1)S(1)}, bf16[112,256]{1,0:T(8,128)(2,1)S(1)}, u32[]{:S(2)}, u32[]{:S(2)}) collective-permute-start(bf16[112,256]{1,0:T(8,128)(2,1)S(1)} %add.27.refs_0_), channel_id=1, source_target_pairs={{0,16},{4,20},{8,24},{12,28},{16,0},{20,4},{24,8},{28,12},{1,17},{... | collective-permute-start | bytes 172040 | tf_op jit(solution)/shard_map/ppermute | solution.py:33
  21.8 5.1 %collective-permute-start.1 = (bf16[112,256]{1,0:T(8,128)(2,1)S(1)}, bf16[112,256]{1,0:T(8,128)(2,1)S(1)}, u32[]{:S(2)}, u32[]{:S(2)}) collective-permute-start(bf16[112,256]{1,0:T(8,128)(2,1)S(1)} %add.27.refs_0_), channel_id=1, source_target_pairs={{0,8},{4,12},{8,0},{12,4},{16,24},{20,28},{24,16},{28,20},{1,9},{5... | collective-permute-start | bytes 172040 | tf_op jit(solution)/shard_map/ppermute | solution.py:33
  26.9 2.0 %collective-permute-start.4 = (f32[112,256]{1,0:T(8,128)S(1)}, f32[112,256]{1,0:T(8,128)S(1)}, u32[]{:S(2)}, u32[]{:S(2)}) collective-permute-start(f32[112,256]{1,0:T(8,128)S(1)} %add.28.near_ref), channel_id=1, source_target_pairs={{0,4},{4,0},{8,12},{12,8},{16,20},{20,16},{24,28},{28,24},{1,5},{5... | collective-permute-start | bytes 344072 | tf_op jit(solution)/shard_map/ppermute | solution.py:33
  31.1 2.4 %collective-permute-start.5 = (bf16[4,1,32,3072]{3,2,1,0:T(8,128)(2,1)S(1)}, bf16[4,1,32,3072]{3,2,1,0:T(8,128)(2,1)S(1)}, u32[]{:S(2)}, u32[]{:S(2)}) collective-permute-start(bf16[4,1,32,3072]{3,2,1,0:T(8,128)(2,1)S(1)} %get-tuple-element.44), channel_id=1, source_target_pairs={{0,4},{4,0},{8,12},{12,8},{16,20},{20,16},{24,28},{28,24},{1,5},{5... | collective-permute-start | bytes 2359304 | tf_op jit(solution)/shard_map/ppermute | solution.py:33
  34.3 7.2 %collective-permute-start.8 = (bf16[40,3072]{1,0:T(8,128)(2,1)S(1)}, bf16[40,3072]{1,0:T(8,128)(2,1)S(1)}, u32[]{:S(2)}, u32[]{:S(2)}) collective-permute-start(bf16[40,3072]{1,0:T(8,128)(2,1)S(1)} %get-tuple-element.49), channel_id=1, source_target_pairs={{0,1},{1,0},{2,3},{3,2},{4,5},{5,4},{6,7},{7,6},{8,9},{9,8},{10,11... | collective-permute-start | bytes 737288 | tf_op jit(solution)/shard_map/ppermute | solution.py:33
  34.6 6.9 %collective-permute-start.9 = (bf16[40,3072]{1,0:T(8,128)(2,1)S(1)}, bf16[40,3072]{1,0:T(8,128)(2,1)S(1)}, u32[]{:S(2)}, u32[]{:S(2)}) collective-permute-start(bf16[40,3072]{1,0:T(8,128)(2,1)S(1)} %get-tuple-element.50), channel_id=1, source_target_pairs={{0,2},{1,3},{2,0},{3,1},{4,6},{5,7},{6,4},{7,5},{8,10},{9,11},{10,... | collective-permute-start | bytes 737288 | tf_op jit(solution)/shard_map/ppermute | solution.py:33
  34.8 12.0 %collective-permute-start.10 = (bf16[40,3072]{1,0:T(8,128)(2,1)S(1)}, bf16[40,3072]{1,0:T(8,128)(2,1)S(1)}, u32[]{:S(2)}, u32[]{:S(2)}) collective-permute-start(bf16[40,3072]{1,0:T(8,128)(2,1)S(1)} %get-tuple-element.51), channel_id=1, source_target_pairs={{0,3},{1,2},{2,1},{3,0},{4,7},{5,6},{6,5},{7,4},{8,11},{9,10},{10,... | collective-permute-start | bytes 737288 | tf_op jit(solution)/shard_map/ppermute | solution.py:33
  46.8 13.2 %copy-start.4 = (f32[2688]{0:T(1024)S(1)}, f32[2688]{0:T(1024)}, u32[]{:S(2)}) copy-start(f32[2688]{0:T(1024)} %param.19) | copy-start | bytes 32260
  46.8 13.2 %copy-start.5 = (f32[2688]{0:T(1024)S(1)}, f32[2688]{0:T(1024)}, u32[]{:S(2)}) copy-start(f32[2688]{0:T(1024)} %param.18) | copy-start | bytes 32260
  47.6 15.5 %collective-permute-start.11 = (bf16[112,3072]{1,0:T(8,128)(2,1)S(1)}, bf16[112,3072]{1,0:T(8,128)(2,1)S(1)}, u32[]{:S(2)}, u32[]{:S(2)}) collective-permute-start(bf16[112,3072]{1,0:T(8,128)(2,1)S(1)} %get-tuple-element.54), channel_id=1, source_target_pairs={{0,1},{1,0},{2,3},{3,2},{4,5},{5,4},{6,7},{7,6},{8,9},{9,8},{10,11... | collective-permute-start | bytes 2064392 | tf_op jit(solution)/shard_map/ppermute | solution.py:33
  48.8 15.1 %collective-permute-start.12 = (bf16[112,3072]{1,0:T(8,128)(2,1)S(1)}, bf16[112,3072]{1,0:T(8,128)(2,1)S(1)}, u32[]{:S(2)}, u32[]{:S(2)}) collective-permute-start(bf16[112,3072]{1,0:T(8,128)(2,1)S(1)} %get-tuple-element.55), channel_id=1, source_target_pairs={{0,2},{1,3},{2,0},{3,1},{4,6},{5,7},{6,4},{7,5},{8,10},{9,11},{10,... | collective-permute-start | bytes 2064392 | tf_op jit(solution)/shard_map/ppermute | solution.py:33
  49.1 3.6 %collective-permute-start.13 = (bf16[32,768]{1,0:T(8,128)(2,1)S(1)}, bf16[32,768]{1,0:T(8,128)(2,1)S(1)}, u32[]{:S(2)}, u32[]{:S(2)}) collective-permute-start(bf16[32,768]{1,0:T(8,128)(2,1)S(1)} %get-tuple-element.57), channel_id=1, source_target_pairs={{0,8},{4,12},{8,0},{12,4},{16,24},{20,28},{24,16},{28,20},{1,9},{5... | collective-permute-start | bytes 147464 | tf_op jit(solution)/shard_map/ppermute | solution.py:33
  50.0 4.5 %collective-permute-start.14 = (bf16[32,768]{1,0:T(8,128)(2,1)S(1)}, bf16[32,768]{1,0:T(8,128)(2,1)S(1)}, u32[]{:S(2)}, u32[]{:S(2)}) collective-permute-start(bf16[32,768]{1,0:T(8,128)(2,1)S(1)} %get-tuple-element.58), channel_id=1, source_target_pairs={{0,16},{4,20},{8,24},{12,28},{16,0},{20,4},{24,8},{28,12},{1,17},{... | collective-permute-start | bytes 147464 | tf_op jit(solution)/shard_map/ppermute | solution.py:33
  51.5 4.8 %collective-permute-start.15 = (bf16[32,768]{1,0:T(8,128)(2,1)S(1)}, bf16[32,768]{1,0:T(8,128)(2,1)S(1)}, u32[]{:S(2)}, u32[]{:S(2)}) collective-permute-start(bf16[32,768]{1,0:T(8,128)(2,1)S(1)} %get-tuple-element.59), channel_id=1, source_target_pairs={{0,24},{4,28},{8,16},{12,20},{16,8},{20,12},{24,0},{28,4},{1,25},{... | collective-permute-start | bytes 147464 | tf_op jit(solution)/shard_map/ppermute | solution.py:33
  56.3 4.8 %collective-permute-start.18 = (bf16[32,768]{1,0:T(8,128)(2,1)S(1)}, bf16[32,768]{1,0:T(8,128)(2,1)S(1)}, u32[]{:S(2)}, u32[]{:S(2)}) collective-permute-start(bf16[32,768]{1,0:T(8,128)(2,1)S(1)} %add.29.refs_0_), channel_id=1, source_target_pairs={{0,24},{4,28},{8,16},{12,20},{16,8},{20,12},{24,0},{28,4},{1,25},{... | collective-permute-start | bytes 147464 | tf_op jit(solution)/shard_map/ppermute | solution.py:33
  57.8 4.9 %collective-permute-start.17 = (bf16[32,768]{1,0:T(8,128)(2,1)S(1)}, bf16[32,768]{1,0:T(8,128)(2,1)S(1)}, u32[]{:S(2)}, u32[]{:S(2)}) collective-permute-start(bf16[32,768]{1,0:T(8,128)(2,1)S(1)} %add.29.refs_0_), channel_id=1, source_target_pairs={{0,16},{4,20},{8,24},{12,28},{16,0},{20,4},{24,8},{28,12},{1,17},{... | collective-permute-start | bytes 147464 | tf_op jit(solution)/shard_map/ppermute | solution.py:33
  57.8 4.9 %collective-permute-start.16 = (bf16[32,768]{1,0:T(8,128)(2,1)S(1)}, bf16[32,768]{1,0:T(8,128)(2,1)S(1)}, u32[]{:S(2)}, u32[]{:S(2)}) collective-permute-start(bf16[32,768]{1,0:T(8,128)(2,1)S(1)} %add.29.refs_0_), channel_id=1, source_target_pairs={{0,8},{4,12},{8,0},{12,4},{16,24},{20,28},{24,16},{28,20},{1,9},{5... | collective-permute-start | bytes 147464 | tf_op jit(solution)/shard_map/ppermute | solution.py:33
  60.6 6.5 %copy-start.1 = (f32[2688]{0:T(1024)}, f32[2688]{0:T(1024)S(1)}, u32[]{:S(2)}) copy-start(f32[2688]{0:T(1024)S(1)} %get-tuple-element.72.refs_6_) | copy-start | bytes 32260
  64.0 3.0 %copy-start.3 = (s32[8]{0:T(128)S(1)}, s32[8]{0:T(128)}, u32[]{:S(2)}) copy-start(s32[8]{0:T(128)} %owners.5) | copy-start | bytes 100
  64.0 5.6 %collective-permute-start.21 = (bf16[4,32,768]{2,1,0:T(8,128)(2,1)S(1)}, bf16[4,32,768]{2,1,0:T(8,128)(2,1)S(1)}, u32[]{:S(2)}, u32[]{:S(2)}) collective-permute-start(bf16[4,32,768]{2,1,0:T(8,128)(2,1)S(1)} %stack.35.refs_0_), channel_id=1, source_target_pairs={{0,3},{1,2},{2,1},{3,0},{4,7},{5,6},{6,5},{7,4},{8,11},{9,10},{10,... | collective-permute-start | bytes 589832 | tf_op jit(solution)/shard_map/ppermute | solution.py:33
  65.6 8.7 %collective-permute-start.20 = (bf16[4,32,768]{2,1,0:T(8,128)(2,1)S(1)}, bf16[4,32,768]{2,1,0:T(8,128)(2,1)S(1)}, u32[]{:S(2)}, u32[]{:S(2)}) collective-permute-start(bf16[4,32,768]{2,1,0:T(8,128)(2,1)S(1)} %stack.35.refs_0_), channel_id=1, source_target_pairs={{0,2},{1,3},{2,0},{3,1},{4,6},{5,7},{6,4},{7,5},{8,10},{9,11},{10,... | collective-permute-start | bytes 589832 | tf_op jit(solution)/shard_map/ppermute | solution.py:33
  65.6 8.7 %collective-permute-start.19 = (bf16[4,32,768]{2,1,0:T(8,128)(2,1)S(1)}, bf16[4,32,768]{2,1,0:T(8,128)(2,1)S(1)}, u32[]{:S(2)}, u32[]{:S(2)}) collective-permute-start(bf16[4,32,768]{2,1,0:T(8,128)(2,1)S(1)} %stack.35.refs_0_), channel_id=1, source_target_pairs={{0,1},{1,0},{2,3},{3,2},{4,5},{5,4},{6,7},{7,6},{8,9},{9,8},{10,11... | collective-permute-start | bytes 589832 | tf_op jit(solution)/shard_map/ppermute | solution.py:33
  74.3 6.2 %collective-permute-start.22 = (bf16[4,1,4,32,768]{4,3,2,1,0:T(8,128)(2,1)S(1)}, bf16[4,1,4,32,768]{4,3,2,1,0:T(8,128)(2,1)S(1)}, u32[]{:S(2)}, u32[]{:S(2)}) collective-permute-start(bf16[4,1,4,32,768]{4,3,2,1,0:T(8,128)(2,1)S(1)} %bitcast.12), channel_id=1, source_target_pairs={{0,4},{4,0},{8,12},{12,8},{16,20},{20,16},{24,28},{28,24},{1,5},{5... | collective-permute-start | bytes 2359304 | tf_op jit(solution)/shard_map/ppermute | solution.py:33

commit v14 on v13

--- a/solution.py
+++ b/solution.py
@@ -8,7 +8,6 @@
 from jax.sharding import PartitionSpec as P
 
 CORES = 2
-AHEAD = 8
 BASE_ROWS = 48
 F32 = jnp.float32
 BF16 = jnp.bfloat16
@@ -33,7 +32,7 @@
     return lax.ppermute(x, axis, [(i, i ^ distance) for i in range(size)])
 
 
-def left_kernel(pos, g_ref, f_ref, q_ref, vec_ref, comp_ref, near_ref, far_ref, total, feedback, right, sems):
+def left_kernel(pos, g_ref, f_ref, q_ref, vec_ref, comp_ref, near_ref, far_ref, total, feedback, right, terms, sems):
     nmat, rows, _ = comp_ref.shape
     rank = q_ref.shape[1]
     part = near_ref.shape[0]
@@ -45,27 +44,29 @@
             pltpu.make_async_copy(q_ref.at[k], right.at[k], sems.at[k, 2]),
         ]
 
-    for k in range(min(AHEAD, nmat)):
+    @pl.loop(0, nmat)
+    def _(k):
         for copy in copies(k):
             copy.start()
+
     total[...] = jnp.zeros(total.shape, F32)
     width, nvec = total.shape[1], vec_ref.shape[1]
     for i, first in enumerate(range(0, nvec, width)):
         count = min(width, nvec - first)
         total[rows + i : rows + i + 1, :count] = vec_ref[:, first : first + count]
 
-    for k in range(nmat):
+    @pl.loop(0, nmat)
+    def _(k):
         for copy in copies(k):
             copy.wait()
-        if k + AHEAD < nmat:
-            for copy in copies(k + AHEAD):
-                copy.start()
         comp = comp_ref[k] + feedback[k]
         comp_ref[k] = comp
-        total[:rows, k * rank : (k + 1) * rank] = lax.dot_general(
+        terms[k] = lax.dot_general(
             comp, right[k], (((1,), (1,)), ((), ())), preferred_element_type=F32
         )
 
+    for k in range(nmat):
+        total[:rows, k * rank : (k + 1) * rank] = terms[k]
     for ref, core in ((near_ref, pos[2]), (far_ref, 1 - pos[2])):
         ref[...] = total[pl.ds(pl.multiple_of(core * part, 16), part), :]
 
@@ -90,6 +91,7 @@
                 pltpu.VMEM((total, width), F32),
                 pltpu.VMEM((nmat, rows, n), BF16),
                 pltpu.VMEM((nmat, rank, n), BF16),
+                pltpu.VMEM((nmat, rows, rank), F32),
                 pltpu.SemaphoreType.DMA((nmat, 3)),
             ],
         ),
@@ -394,58 +396,90 @@
         return (j + half * other) ^ pos[0]
 
     step = 256 if cols % 256 == 0 else 128
-    pieces = [slice(first, first + step) for first in range(0, cols, step)]
-    stores = []
-
-    def store(source, target, sem):
-        stores.append(pltpu.make_async_copy(source, target, sem))
-        stores[-1].start()
+    pieces = cols // step
+
+    def block_of(b):
+        d, first = b // pieces, lax.rem(b, pieces) * step
+        return d, pl.ds(pl.multiple_of(first, 128), step), columns(d, first, step)
 
     if where:
         momentum_ref, master_ref = refs[:2]
         new_momentum, new_master, state_sem = scratch[3:]
-        for c in range(capacity):
+
+        def state_copies(c):
+            return [
+                pltpu.make_async_copy(new.at[c], outs[2 + i].at[0, c], state_sem.at[i, c])
+                for i, new in enumerate((new_momentum, new_master))
+            ]
+
+        @pl.loop(0, capacity)
+        def _(c):
             mine = jnp.int32(-1)
             for k in range(owners.shape[0]):
                 mine = jnp.where((owners[k] == pos[5]) & (rank_of(owners, k) == c), k, mine)
             safe = jnp.maximum(mine, 0)
             strip = strip_ref[safe]
-            for d in range(n_z):
-                for block in pieces:
-                    right = jnp.zeros((strip.shape[1], step), BF16)
-                    for job, place in where.items():
-                        right = jnp.where(safe == matrix(*job), right_of(place, d, block), right)
-                    approx = jnp.dot(strip, right, preferred_element_type=F32)
-                    approx = jnp.where(mine >= 0, approx, 0.0)
-                    place = columns(d, block.start, step)
-                    momentum = 0.9 * momentum_ref[c, :, place] + approx
-                    new_momentum[c, :, place] = momentum
-                    new_master[c, :, place] = master_ref[c, :, place] - 0.1 * momentum
-                place = columns(d)
-                for i, new in enumerate((new_momentum, new_master)):
-                    store(
-                        new.at[c, :, place], outs[2 + i].at[0, c, :, place], state_sem.at[i, c, d]
-                    )
-
-    for i, (job, where_right) in enumerate(jobs.items()):
-        k = matrix(*job)
+
+            @pl.loop(0, n_z * pieces)
+            def _(b):
+                d, block, place = block_of(b)
+                right = jnp.zeros((strip.shape[1], step), BF16)
+                for job, entry in where.items():
+                    right = jnp.where(safe == matrix(*job), right_of(entry, d, block), right)
+                approx = jnp.dot(strip, right, preferred_element_type=F32)
+                approx = jnp.where(mine >= 0, approx, 0.0)
+                momentum = 0.9 * momentum_ref[c, :, place] + approx
+                new_momentum[c, :, place] = momentum
+                new_master[c, :, place] = master_ref[c, :, place] - 0.1 * momentum
+
+            for copy in state_copies(c):
+                copy.start()
+
+    (other, start), (a, entry) = next(iter(jobs.items()))
+
+    def copies(i, d):
+        k, place = matrix(other, start + i), columns(d)
+        return [
+            pltpu.make_async_copy(
+                feedback.at[i, :, place], outs[0].at[0, k, :, place], out_sem.at[i, d, 0]
+            ),
+            pltpu.make_async_copy(
+                weights.at[i, :, place], outs[1].at[k, :, place], out_sem.at[i, d, 1]
+            ),
+        ]
+
+    @pl.loop(0, len(jobs))
+    def _(i):
+        k = matrix(other, start + i)
         slot = (owners[k] ^ pos[5]) * capacity + rank_of(owners, k)
         left, strip = left_ref[k], strip_ref[k]
-        for d in range(n_z):
-            for block in pieces:
-                right = right_of(where_right, d, block)
-                place = columns(d, block.start, step)
+
+        @pl.loop(0, n_z)
+        def _(d):
+            for first in range(0, cols, step):
+                right = right_of((a, entry + i), d, slice(first, first + step))
+                place = columns(d, first, step)
                 approx = jnp.dot(left, right, preferred_element_type=F32)
                 feedback[i, :, place] = (comp_ref[k, :, place].astype(F32) - approx).astype(BF16)
                 approx = jnp.dot(strip, right, preferred_element_type=F32)
                 base = base_ref[slot, :, place].astype(F32)
                 weights[i, :, place] = (base - 0.1 * approx).astype(BF16)
-            place = columns(d)
-            store(feedback.at[i, :, place], outs[0].at[0, k, :, place], out_sem.at[i, d, 0])
-            store(weights.at[i, :, place], outs[1].at[k, :, place], out_sem.at[i, d, 1])
-
-    for copy in stores:
-        copy.wait()
+            for copy in copies(i, d):
+                copy.start()
+
+    @pl.loop(0, len(jobs))
+    def _(i):
+        @pl.loop(0, n_z)
+        def _(d):
+            for copy in copies(i, d):
+                copy.wait()
+
+    if where:
+
+        @pl.loop(0, capacity)
+        def _(c):
+            for copy in state_copies(c):
+                copy.wait()
 
 
 def outputs(pos, owners, comp, left, strip, base, capacity, rights, jobs, where=None, states=(), earlier=()):
@@ -461,7 +495,7 @@
     ]
     if states:
         scratch += [pltpu.VMEM((capacity, replica_rows, n), F32)] * 2
-        scratch += [pltpu.SemaphoreType.DMA((2, capacity, n_z))]
+        scratch += [pltpu.SemaphoreType.DMA((2, capacity))]
     outs = [
         jax.ShapeDtypeStruct((1, nmat, rows, n), BF16),
         jax.ShapeDtypeStruct((nmat, replica_rows, n), BF16),

time: 86.9 us -> 91.8 us (1.056)
  Pallas kernels: 30 us -> 35.3 us
    pallas_call x3, Pallas kernels: 12.2 us -> 18 us  [outputs(): pl.pallas_call(functools.partial(outputs_kernel, jobs, where, capacity),...]
where the time goes in v14:
time: 91.8 us; the launch traced here: 91.7 us
  Pallas kernels  35.3 us (38%)
  waiting for transfers between devices  28.5 us (31%)
  starting transfers between devices  26.3 us (29%)
    ppermute x23, waiting for transfers between devices, exchange(): return lax.ppermute(x, axis, [(i, i ^ distance) for i in range(size)])  28.5 us
    ppermute x23, starting transfers between devices, exchange(): return lax.ppermute(x, axis, [(i, i ^ distance) for i in range(size)])  26.3 us
    pallas_call x3, Pallas kernels, outputs(): pl.pallas_call(functools.partial(outputs_kernel, jobs, where, capacity),...  18 us
    pallas_call x1, Pallas kernels, left_terms(): pl.pallas_call(left_kernel, grid_spec=pltpu.PrefetchScalarGridSpec(num_sc...  8.26 us
    pallas_call x1, Pallas kernels, base_of(): pl.pallas_call(base_kernel, grid_spec=pltpu.PrefetchScalarGridSpec(num_sc...  3.16 us
    pallas_call x1, Pallas kernels, right_terms(): pl.pallas_call(functools.partial(send_kernel, half), grid_spec=pltpu.Pref...  2.22 us
  transfers between devices with their start and end apart: 23, of which 15 were waited for; matrix products, arithmetic and copies ran while one was open for 1% of the time, Pallas kernels for 22%

profile of v14, /device:TPU:1, one launch (start us, length us, event | category | flops | bytes accessed | tf_op | source)
XLA Modules:
  0.0 91.7 jit_solution(15565717090964826734)
XLA Ops:
  0.8 3.2 %base.1 = (bf16[2,96,3072]{2,1,0:T(8,128)(2,1)S(1)}, f32[2,96,3072]{2,1,0:T(8,128)S(1)}, f32[2,96,3072]{2,1,0:T(8,128)S(1)}, bf16[176,3072]{1,0:T(8,128)(2,1)S(1)}, bf16[176,3072]{1,0:T(8,128)(2,1)S(1)}) custom-call(s32[8]{0:T(128)S(1)} %stack.34.pos, f32[1,2,96,3072]{3,2,1,0:T(8,128)} %momentum_ref.1, f32[1,2,96,3072]{3,2,1,0:T(8,128)} %master_ref.1), custom_call_target="tpu_custom_call" | custom-call | flops 1000 | bytes 1000 | tf_op jit(solution)/shard_map/base/pallas_call | solution.py:552
  4.0 2.1 %collective-permute-start.6 = (bf16[176,3072]{1,0:T(8,128)(2,1)S(1)}, bf16[176,3072]{1,0:T(8,128)(2,1)S(1)}, u32[]{:S(2)}, u32[]{:S(2)}) collective-permute-start(bf16[176,3072]{1,0:T(8,128)(2,1)S(1)} %get-tuple-element.45), channel_id=1, source_target_pairs={{0,1},{1,0},{2,3},{3,2},{4,5},{5,4},{6,7},{7,6},{8,9},{9,8},{10,11... | collective-permute-start | bytes 3244040 | tf_op jit(solution)/shard_map/ppermute | solution.py:32
  6.1 1.2 %collective-permute-start.7 = (bf16[176,3072]{1,0:T(8,128)(2,1)S(1)}, bf16[176,3072]{1,0:T(8,128)(2,1)S(1)}, u32[]{:S(2)}, u32[]{:S(2)}) collective-permute-start(bf16[176,3072]{1,0:T(8,128)(2,1)S(1)} %get-tuple-element.46), channel_id=1, source_target_pairs={{0,2},{1,3},{2,0},{3,1},{4,6},{5,7},{6,4},{7,5},{8,10},{9,11},{10,... | collective-permute-start | bytes 3244040 | tf_op jit(solution)/shard_map/ppermute | solution.py:32
  7.3 8.3 %left_terms.1 = (bf16[8,192,3072]{2,1,0:T(8,128)(2,1)S(1)}, f32[112,256]{1,0:T(8,128)S(1)}, f32[112,256]{1,0:T(8,128)S(1)}) custom-call(s32[8]{0:T(128)S(1)} %stack.34.pos, bf16[1,8,192,3072]{3,2,1,0:T(8,128)(2,1)} %g_ref.1, bf16[1,8,192,3072]{3,2,1,0:T(8,128)(2,1)} %f_ref.1, bf16[8,32,3072]{2,1,0:T(8,128)(2,1)} %bitcast.17, f32[1,2688]{1,0:T(1,128)S(1)} %copy-done.2), custom_call_target="tpu_custom_call" | custom-call | flops 1000 | bytes 1000 | tf_op jit(solution)/shard_map/left_terms/pallas_call | solution.py:83
  15.6 1.3 %collective-permute-start = (f32[112,256]{1,0:T(8,128)S(1)}, f32[112,256]{1,0:T(8,128)S(1)}, u32[]{:S(2)}, u32[]{:S(2)}) collective-permute-start(f32[112,256]{1,0:T(8,128)S(1)} %get-tuple-element.41), channel_id=1, source_target_pairs={{0,4},{4,0},{8,12},{12,8},{16,20},{20,16},{24,28},{28,24},{1,5},{5... | collective-permute-start | bytes 344072 | tf_op jit(solution)/shard_map/ppermute | solution.py:32
  16.9 1.0 %collective-permute-done.refs_1_ = f32[112,256]{1,0:T(8,128)S(1)} collective-permute-done((f32[112,256]{1,0:T(8,128)S(1)}, f32[112,256]{1,0:T(8,128)S(1)}, u32[]{:S(2)}, u32[]{:S(2)}) %collective-permute-start) | collective-permute-done | bytes 114720 | tf_op jit(solution)/shard_map/ppermute | solution.py:32
  17.9 3.4 %collective-permute-start.3 = (bf16[112,256]{1,0:T(8,128)(2,1)S(1)}, bf16[112,256]{1,0:T(8,128)(2,1)S(1)}, u32[]{:S(2)}, u32[]{:S(2)}) collective-permute-start(bf16[112,256]{1,0:T(8,128)(2,1)S(1)} %add.27.refs_0_), channel_id=1, source_target_pairs={{0,24},{4,28},{8,16},{12,20},{16,8},{20,12},{24,0},{28,4},{1,25},{... | collective-permute-start | bytes 172040 | tf_op jit(solution)/shard_map/ppermute | solution.py:32
  21.6 1.3 %collective-permute-done.3.refs_3_ = bf16[112,256]{1,0:T(8,128)(2,1)S(1)} collective-permute-done((bf16[112,256]{1,0:T(8,128)(2,1)S(1)}, bf16[112,256]{1,0:T(8,128)(2,1)S(1)}, u32[]{:S(2)}, u32[]{:S(2)}) %collective-permute-start.3) | collective-permute-done | bytes 57376 | tf_op jit(solution)/shard_map/ppermute | solution.py:32
  22.9 3.4 %collective-permute-done.2.refs_2_ = bf16[112,256]{1,0:T(8,128)(2,1)S(1)} collective-permute-done((bf16[112,256]{1,0:T(8,128)(2,1)S(1)}, bf16[112,256]{1,0:T(8,128)(2,1)S(1)}, u32[]{:S(2)}, u32[]{:S(2)}) %collective-permute-start.2) | collective-permute-done | bytes 57376 | tf_op jit(solution)/shard_map/ppermute | solution.py:32
  26.4 1.0 %collective-permute-start.4 = (f32[112,256]{1,0:T(8,128)S(1)}, f32[112,256]{1,0:T(8,128)S(1)}, u32[]{:S(2)}, u32[]{:S(2)}) collective-permute-start(f32[112,256]{1,0:T(8,128)S(1)} %add.28.near_ref), channel_id=1, source_target_pairs={{0,4},{4,0},{8,12},{12,8},{16,20},{20,16},{24,28},{28,24},{1,5},{5... | collective-permute-start | bytes 344072 | tf_op jit(solution)/shard_map/ppermute | solution.py:32
  27.4 1.0 %collective-permute-done.4.far_ref = f32[112,256]{1,0:T(8,128)S(1)} collective-permute-done((f32[112,256]{1,0:T(8,128)S(1)}, f32[112,256]{1,0:T(8,128)S(1)}, u32[]{:S(2)}, u32[]{:S(2)}) %collective-permute-start.4) | collective-permute-done | bytes 114720 | tf_op jit(solution)/shard_map/ppermute | solution.py:32
  28.3 2.2 %right_send.1 = (bf16[4,1,32,3072]{3,2,1,0:T(8,128)(2,1)S(1)}, bf16[256,192]{1,0:T(8,128)(2,1)S(1)}, bf16[8,192,32]{2,1,0:T(8,128)(2,1)S(1)}, f32[32,256]{1,0:T(8,128)S(1)}) custom-call(s32[8]{0:T(128)S(1)} %stack.34.pos, f32[112,256]{1,0:T(8,128)S(1)} %add.28.near_ref, f32[112,256]{1,0:T(8,128)S(1)} %collective-permute-done.4.far_ref, ...), custom_call_target="tpu_custom_call" | custom-call | flops 1000 | bytes 1000 | tf_op jit(solution)/shard_map/right_send/pallas_call | solution.py:164
  31.0 1.5 %right_keep.1.refs_0_.keep_ref = f32[4,1,32,3072]{3,2,1,0:T(8,128)S(1)} custom-call(s32[8]{0:T(128)S(1)} %stack.34.pos, bf16[256,192]{1,0:T(8,128)(2,1)S(1)} %get-tuple-element.43.lt_ref, bf16[8,192,3072]{2,1,0:T(8,128)(2,1)S(1)} %get-tuple-element.39.comp_ref), custom_call_target="tpu_custom_call" | custom-call | flops 1000 | bytes 1000 | tf_op jit(solution)/shard_map/right_keep/pallas_call | solution.py:183
  34.3 2.2 %collective-permute-start.10 = (bf16[40,3072]{1,0:T(8,128)(2,1)S(1)}, bf16[40,3072]{1,0:T(8,128)(2,1)S(1)}, u32[]{:S(2)}, u32[]{:S(2)}) collective-permute-start(bf16[40,3072]{1,0:T(8,128)(2,1)S(1)} %get-tuple-element.51), channel_id=1, source_target_pairs={{0,3},{1,2},{2,1},{3,0},{4,7},{5,6},{6,5},{7,4},{8,11},{9,10},{10,... | collective-permute-start | bytes 737288 | tf_op jit(solution)/shard_map/ppermute | solution.py:32
  36.4 4.5 %collective-permute-done.8.refs_0_ = bf16[40,3072]{1,0:T(8,128)(2,1)S(1)} collective-permute-done((bf16[40,3072]{1,0:T(8,128)(2,1)S(1)}, bf16[40,3072]{1,0:T(8,128)(2,1)S(1)}, u32[]{:S(2)}, u32[]{:S(2)}) %collective-permute-start.8) | collective-permute-done | bytes 245792 | tf_op jit(solution)/shard_map/ppermute | solution.py:32
  41.0 5.2 %collective-permute-done.10.refs_2_ = bf16[40,3072]{1,0:T(8,128)(2,1)S(1)} collective-permute-done((bf16[40,3072]{1,0:T(8,128)(2,1)S(1)}, bf16[40,3072]{1,0:T(8,128)(2,1)S(1)}, u32[]{:S(2)}, u32[]{:S(2)}) %collective-permute-start.10) | collective-permute-done | bytes 245792 | tf_op jit(solution)/shard_map/ppermute | solution.py:32
  47.0 1.3 %collective-permute-start.11 = (bf16[112,3072]{1,0:T(8,128)(2,1)S(1)}, bf16[112,3072]{1,0:T(8,128)(2,1)S(1)}, u32[]{:S(2)}, u32[]{:S(2)}) collective-permute-start(bf16[112,3072]{1,0:T(8,128)(2,1)S(1)} %get-tuple-element.54), channel_id=1, source_target_pairs={{0,1},{1,0},{2,3},{3,2},{4,5},{5,4},{6,7},{7,6},{8,9},{9,8},{10,11... | collective-permute-start | bytes 2064392 | tf_op jit(solution)/shard_map/ppermute | solution.py:32
  49.4 1.2 %collective-permute-start.14 = (bf16[32,768]{1,0:T(8,128)(2,1)S(1)}, bf16[32,768]{1,0:T(8,128)(2,1)S(1)}, u32[]{:S(2)}, u32[]{:S(2)}) collective-permute-start(bf16[32,768]{1,0:T(8,128)(2,1)S(1)} %get-tuple-element.58), channel_id=1, source_target_pairs={{0,16},{4,20},{8,24},{12,28},{16,0},{20,4},{24,8},{28,12},{1,17},{... | collective-permute-start | bytes 147464 | tf_op jit(solution)/shard_map/ppermute | solution.py:32
  50.6 1.5 %collective-permute-start.15 = (bf16[32,768]{1,0:T(8,128)(2,1)S(1)}, bf16[32,768]{1,0:T(8,128)(2,1)S(1)}, u32[]{:S(2)}, u32[]{:S(2)}) collective-permute-start(bf16[32,768]{1,0:T(8,128)(2,1)S(1)} %get-tuple-element.59), channel_id=1, source_target_pairs={{0,24},{4,28},{8,16},{12,20},{16,8},{20,12},{24,0},{28,4},{1,25},{... | collective-permute-start | bytes 147464 | tf_op jit(solution)/shard_map/ppermute | solution.py:32
  52.2 1.7 %collective-permute-done.14.refs_2_ = bf16[32,768]{1,0:T(8,128)(2,1)S(1)} collective-permute-done((bf16[32,768]{1,0:T(8,128)(2,1)S(1)}, bf16[32,768]{1,0:T(8,128)(2,1)S(1)}, u32[]{:S(2)}, u32[]{:S(2)}) %collective-permute-start.14) | collective-permute-done | bytes 49184 | tf_op jit(solution)/shard_map/ppermute | solution.py:32
  53.9 1.8 %collective-permute-done.15.refs_3_ = bf16[32,768]{1,0:T(8,128)(2,1)S(1)} collective-permute-done((bf16[32,768]{1,0:T(8,128)(2,1)S(1)}, bf16[32,768]{1,0:T(8,128)(2,1)S(1)}, u32[]{:S(2)}, u32[]{:S(2)}) %collective-permute-start.15) | collective-permute-done | bytes 49184 | tf_op jit(solution)/shard_map/ppermute | solution.py:32
  55.7 1.5 %collective-permute-start.18 = (bf16[32,768]{1,0:T(8,128)(2,1)S(1)}, bf16[32,768]{1,0:T(8,128)(2,1)S(1)}, u32[]{:S(2)}, u32[]{:S(2)}) collective-permute-start(bf16[32,768]{1,0:T(8,128)(2,1)S(1)} %add.29.refs_0_), channel_id=1, source_target_pairs={{0,24},{4,28},{8,16},{12,20},{16,8},{20,12},{24,0},{28,4},{1,25},{... | collective-permute-start | bytes 147464 | tf_op jit(solution)/shard_map/ppermute | solution.py:32
  57.2 2.1 %collective-permute-start.16 = (bf16[32,768]{1,0:T(8,128)(2,1)S(1)}, bf16[32,768]{1,0:T(8,128)(2,1)S(1)}, u32[]{:S(2)}, u32[]{:S(2)}) collective-permute-start(bf16[32,768]{1,0:T(8,128)(2,1)S(1)} %add.29.refs_0_), channel_id=1, source_target_pairs={{0,8},{4,12},{8,0},{12,4},{16,24},{20,28},{24,16},{28,20},{1,9},{5... | collective-permute-start | bytes 147464 | tf_op jit(solution)/shard_map/ppermute | solution.py:32
  60.6 1.5 %collective-permute-done.17.refs_2_ = bf16[32,768]{1,0:T(8,128)(2,1)S(1)} collective-permute-done((bf16[32,768]{1,0:T(8,128)(2,1)S(1)}, bf16[32,768]{1,0:T(8,128)(2,1)S(1)}, u32[]{:S(2)}, u32[]{:S(2)}) %collective-permute-start.17) | collective-permute-done | bytes 49184 | tf_op jit(solution)/shard_map/ppermute | solution.py:32
  62.4 1.0 %collective-permute-done.12.refs_3_.refs_5_ = bf16[112,3072]{1,0:T(8,128)(2,1)S(1)} collective-permute-done((bf16[112,3072]{1,0:T(8,128)(2,1)S(1)}, bf16[112,3072]{1,0:T(8,128)(2,1)S(1)}, u32[]{:S(2)}, u32[]{:S(2)}) %collective-permute-start.12) | collective-permute-done | bytes 688160 | tf_op jit(solution)/shard_map/ppermute | solution.py:32
  63.5 1.6 %collective-permute-start.21 = (bf16[4,32,768]{2,1,0:T(8,128)(2,1)S(1)}, bf16[4,32,768]{2,1,0:T(8,128)(2,1)S(1)}, u32[]{:S(2)}, u32[]{:S(2)}) collective-permute-start(bf16[4,32,768]{2,1,0:T(8,128)(2,1)S(1)} %stack.35.refs_0_), channel_id=1, source_target_pairs={{0,3},{1,2},{2,1},{3,0},{4,7},{5,6},{6,5},{7,4},{8,11},{9,10},{10,... | collective-permute-start | bytes 589832 | tf_op jit(solution)/shard_map/ppermute | solution.py:32
  65.1 1.1 %collective-permute-start.19 = (bf16[4,32,768]{2,1,0:T(8,128)(2,1)S(1)}, bf16[4,32,768]{2,1,0:T(8,128)(2,1)S(1)}, u32[]{:S(2)}, u32[]{:S(2)}) collective-permute-start(bf16[4,32,768]{2,1,0:T(8,128)(2,1)S(1)} %stack.35.refs_0_), channel_id=1, source_target_pairs={{0,1},{1,0},{2,3},{3,2},{4,5},{5,4},{6,7},{7,6},{8,9},{9,8},{10,11... | collective-permute-start | bytes 589832 | tf_op jit(solution)/shard_map/ppermute | solution.py:32
  66.5 2.4 %outputs.3 = (bf16[1,8,192,3072]{3,2,1,0:T(8,128)(2,1)}, bf16[8,96,3072]{2,1,0:T(8,128)(2,1)}, f32[8,128]{1,0:T(8,128)S(1)}) custom-call(s32[8]{0:T(128)S(1)} %stack.34.pos, s32[8]{0:T(128)S(1)} %copy-done.3, bf16[8,192,3072]{2,1,0:T(8,128)(2,1)S(1)} %get-tuple-element.39.comp_ref, bf16[8,192,32]{2,1,0:T(8,128)(2,1)S(1)} %get-tuple-element.42.left_ref, ...), custom_call_target="tpu_custom_call" | custom-call | flops 1000 | bytes 1000 | tf_op jit(solution)/shard_map/outputs/pallas_call | solution.py:504
  69.1 4.7 %collective-permute-done.20.refs_2_ = bf16[4,32,768]{2,1,0:T(8,128)(2,1)S(1)} collective-permute-done((bf16[4,32,768]{2,1,0:T(8,128)(2,1)S(1)}, bf16[4,32,768]{2,1,0:T(8,128)(2,1)S(1)}, u32[]{:S(2)}, u32[]{:S(2)}) %collective-permute-start.20) | collective-permute-done | bytes 196640 | tf_op jit(solution)/shard_map/ppermute | solution.py:32
  73.8 2.3 %collective-permute-start.22 = (bf16[4,1,4,32,768]{4,3,2,1,0:T(8,128)(2,1)S(1)}, bf16[4,1,4,32,768]{4,3,2,1,0:T(8,128)(2,1)S(1)}, u32[]{:S(2)}, u32[]{:S(2)}) collective-permute-start(bf16[4,1,4,32,768]{4,3,2,1,0:T(8,128)(2,1)S(1)} %bitcast.12), channel_id=1, source_target_pairs={{0,4},{4,0},{8,12},{12,8},{16,20},{20,16},{24,28},{28,24},{1,5},{5... | collective-permute-start | bytes 2359304 | tf_op jit(solution)/shard_map/ppermute | solution.py:32
  76.1 5.3 %outputs.4 = (bf16[1,8,192,3072]{3,2,1,0:T(8,128)(2,1)}, bf16[8,96,3072]{2,1,0:T(8,128)(2,1)}, f32[8,128]{1,0:T(8,128)}) custom-call(s32[8]{0:T(128)S(1)} %stack.34.pos, s32[8]{0:T(128)S(1)} %copy-done.3, bf16[8,192,3072]{2,1,0:T(8,128)(2,1)S(1)} %get-tuple-element.39.comp_ref, ...), custom_call_target="tpu_custom_call", output_to_operand_aliasing={{0}: (7, {}), {1}: (8, {})} | custom-call | flops 1000 | bytes 1000 | tf_op jit(solution)/shard_map/outputs/pallas_call | solution.py:504
  81.4 10.3 %outputs.5 = (bf16[1,8,192,3072]{3,2,1,0:T(8,128)(2,1)}, bf16[8,96,3072]{2,1,0:T(8,128)(2,1)}, f32[1,2,96,3072]{3,2,1,0:T(8,128)}, f32[1,2,96,3072]{3,2,1,0:T(8,128)}, f32[8,128]{1,0:T(8,128)}) custom-call(s32[8]{0:T(128)S(1)} %stack.34.pos, s32[8]{0:T(128)S(1)} %copy-done.3, ...), custom_call_target="tpu_custom_call", output_to_operand_aliasing={{0}: (10, {}), {1}: (11, {})} | custom-call | flops 1000 | bytes 1000 | tf_op jit(solution)/shard_map/outputs/pallas_call | solution.py:504
  (46 shorter events, 6.7 us)
Async XLA Ops:
  0.8 6.5 %copy-start.2 = (f32[1,2688]{1,0:T(1,128)S(1)}, f32[1,2688]{1,0:T(1,128)}, u32[]{:S(2)}) copy-start(f32[1,2688]{1,0:T(1,128)} %vec_ref.1) | copy-start | bytes 32260
  4.0 28.6 %collective-permute-start.6 = (bf16[176,3072]{1,0:T(8,128)(2,1)S(1)}, bf16[176,3072]{1,0:T(8,128)(2,1)S(1)}, u32[]{:S(2)}, u32[]{:S(2)}) collective-permute-start(bf16[176,3072]{1,0:T(8,128)(2,1)S(1)} %get-tuple-element.45), channel_id=1, source_target_pairs={{0,1},{1,0},{2,3},{3,2},{4,5},{5,4},{6,7},{7,6},{8,9},{9,8},{10,11... | collective-permute-start | bytes 3244040 | tf_op jit(solution)/shard_map/ppermute | solution.py:32
  6.1 26.5 %collective-permute-start.7 = (bf16[176,3072]{1,0:T(8,128)(2,1)S(1)}, bf16[176,3072]{1,0:T(8,128)(2,1)S(1)}, u32[]{:S(2)}, u32[]{:S(2)}) collective-permute-start(bf16[176,3072]{1,0:T(8,128)(2,1)S(1)} %get-tuple-element.46), channel_id=1, source_target_pairs={{0,2},{1,3},{2,0},{3,1},{4,6},{5,7},{6,4},{7,5},{8,10},{9,11},{10,... | collective-permute-start | bytes 3244040 | tf_op jit(solution)/shard_map/ppermute | solution.py:32
  7.3 21.0 %copy-start = (f32[8,32,32]{2,1,0:T(8,128)S(1)}, f32[8,32,32]{2,1,0:T(8,128)}, u32[]{:S(2)}) copy-start(f32[8,32,32]{2,1,0:T(8,128)} %gram_ref.1) | copy-start | bytes 98308
  15.6 2.3 %collective-permute-start = (f32[112,256]{1,0:T(8,128)S(1)}, f32[112,256]{1,0:T(8,128)S(1)}, u32[]{:S(2)}, u32[]{:S(2)}) collective-permute-start(f32[112,256]{1,0:T(8,128)S(1)} %get-tuple-element.41), channel_id=1, source_target_pairs={{0,4},{4,0},{8,12},{12,8},{16,20},{20,16},{24,28},{28,24},{1,5},{5... | collective-permute-start | bytes 344072 | tf_op jit(solution)/shard_map/ppermute | solution.py:32
  17.9 5.1 %collective-permute-start.3 = (bf16[112,256]{1,0:T(8,128)(2,1)S(1)}, bf16[112,256]{1,0:T(8,128)(2,1)S(1)}, u32[]{:S(2)}, u32[]{:S(2)}) collective-permute-start(bf16[112,256]{1,0:T(8,128)(2,1)S(1)} %add.27.refs_0_), channel_id=1, source_target_pairs={{0,24},{4,28},{8,16},{12,20},{16,8},{20,12},{24,0},{28,4},{1,25},{... | collective-permute-start | bytes 172040 | tf_op jit(solution)/shard_map/ppermute | solution.py:32
  21.2 5.1 %collective-permute-start.2 = (bf16[112,256]{1,0:T(8,128)(2,1)S(1)}, bf16[112,256]{1,0:T(8,128)(2,1)S(1)}, u32[]{:S(2)}, u32[]{:S(2)}) collective-permute-start(bf16[112,256]{1,0:T(8,128)(2,1)S(1)} %add.27.refs_0_), channel_id=1, source_target_pairs={{0,16},{4,20},{8,24},{12,28},{16,0},{20,4},{24,8},{28,12},{1,17},{... | collective-permute-start | bytes 172040 | tf_op jit(solution)/shard_map/ppermute | solution.py:32
  21.2 5.1 %collective-permute-start.1 = (bf16[112,256]{1,0:T(8,128)(2,1)S(1)}, bf16[112,256]{1,0:T(8,128)(2,1)S(1)}, u32[]{:S(2)}, u32[]{:S(2)}) collective-permute-start(bf16[112,256]{1,0:T(8,128)(2,1)S(1)} %add.27.refs_0_), channel_id=1, source_target_pairs={{0,8},{4,12},{8,0},{12,4},{16,24},{20,28},{24,16},{28,20},{1,9},{5... | collective-permute-start | bytes 172040 | tf_op jit(solution)/shard_map/ppermute | solution.py:32
  26.4 2.0 %collective-permute-start.4 = (f32[112,256]{1,0:T(8,128)S(1)}, f32[112,256]{1,0:T(8,128)S(1)}, u32[]{:S(2)}, u32[]{:S(2)}) collective-permute-start(f32[112,256]{1,0:T(8,128)S(1)} %add.28.near_ref), channel_id=1, source_target_pairs={{0,4},{4,0},{8,12},{12,8},{16,20},{20,16},{24,28},{28,24},{1,5},{5... | collective-permute-start | bytes 344072 | tf_op jit(solution)/shard_map/ppermute | solution.py:32
  30.6 2.4 %collective-permute-start.5 = (bf16[4,1,32,3072]{3,2,1,0:T(8,128)(2,1)S(1)}, bf16[4,1,32,3072]{3,2,1,0:T(8,128)(2,1)S(1)}, u32[]{:S(2)}, u32[]{:S(2)}) collective-permute-start(bf16[4,1,32,3072]{3,2,1,0:T(8,128)(2,1)S(1)} %get-tuple-element.44), channel_id=1, source_target_pairs={{0,4},{4,0},{8,12},{12,8},{16,20},{20,16},{24,28},{28,24},{1,5},{5... | collective-permute-start | bytes 2359304 | tf_op jit(solution)/shard_map/ppermute | solution.py:32
  33.7 7.2 %collective-permute-start.8 = (bf16[40,3072]{1,0:T(8,128)(2,1)S(1)}, bf16[40,3072]{1,0:T(8,128)(2,1)S(1)}, u32[]{:S(2)}, u32[]{:S(2)}) collective-permute-start(bf16[40,3072]{1,0:T(8,128)(2,1)S(1)} %get-tuple-element.49), channel_id=1, source_target_pairs={{0,1},{1,0},{2,3},{3,2},{4,5},{5,4},{6,7},{7,6},{8,9},{9,8},{10,11... | collective-permute-start | bytes 737288 | tf_op jit(solution)/shard_map/ppermute | solution.py:32
  34.0 6.9 %collective-permute-start.9 = (bf16[40,3072]{1,0:T(8,128)(2,1)S(1)}, bf16[40,3072]{1,0:T(8,128)(2,1)S(1)}, u32[]{:S(2)}, u32[]{:S(2)}) collective-permute-start(bf16[40,3072]{1,0:T(8,128)(2,1)S(1)} %get-tuple-element.50), channel_id=1, source_target_pairs={{0,2},{1,3},{2,0},{3,1},{4,6},{5,7},{6,4},{7,5},{8,10},{9,11},{10,... | collective-permute-start | bytes 737288 | tf_op jit(solution)/shard_map/ppermute | solution.py:32
  34.3 11.9 %collective-permute-start.10 = (bf16[40,3072]{1,0:T(8,128)(2,1)S(1)}, bf16[40,3072]{1,0:T(8,128)(2,1)S(1)}, u32[]{:S(2)}, u32[]{:S(2)}) collective-permute-start(bf16[40,3072]{1,0:T(8,128)(2,1)S(1)} %get-tuple-element.51), channel_id=1, source_target_pairs={{0,3},{1,2},{2,1},{3,0},{4,7},{5,6},{6,5},{7,4},{8,11},{9,10},{10,... | collective-permute-start | bytes 737288 | tf_op jit(solution)/shard_map/ppermute | solution.py:32
  46.1 13.2 %copy-start.4 = (f32[2688]{0:T(1024)S(1)}, f32[2688]{0:T(1024)}, u32[]{:S(2)}) copy-start(f32[2688]{0:T(1024)} %param.19) | copy-start | bytes 32260
  46.1 13.2 %copy-start.5 = (f32[2688]{0:T(1024)S(1)}, f32[2688]{0:T(1024)}, u32[]{:S(2)}) copy-start(f32[2688]{0:T(1024)} %param.18) | copy-start | bytes 32260
  47.0 15.4 %collective-permute-start.11 = (bf16[112,3072]{1,0:T(8,128)(2,1)S(1)}, bf16[112,3072]{1,0:T(8,128)(2,1)S(1)}, u32[]{:S(2)}, u32[]{:S(2)}) collective-permute-start(bf16[112,3072]{1,0:T(8,128)(2,1)S(1)} %get-tuple-element.54), channel_id=1, source_target_pairs={{0,1},{1,0},{2,3},{3,2},{4,5},{5,4},{6,7},{7,6},{8,9},{9,8},{10,11... | collective-permute-start | bytes 2064392 | tf_op jit(solution)/shard_map/ppermute | solution.py:32
  48.3 15.1 %collective-permute-start.12 = (bf16[112,3072]{1,0:T(8,128)(2,1)S(1)}, bf16[112,3072]{1,0:T(8,128)(2,1)S(1)}, u32[]{:S(2)}, u32[]{:S(2)}) collective-permute-start(bf16[112,3072]{1,0:T(8,128)(2,1)S(1)} %get-tuple-element.55), channel_id=1, source_target_pairs={{0,2},{1,3},{2,0},{3,1},{4,6},{5,7},{6,4},{7,5},{8,10},{9,11},{10,... | collective-permute-start | bytes 2064392 | tf_op jit(solution)/shard_map/ppermute | solution.py:32
  48.6 3.6 %collective-permute-start.13 = (bf16[32,768]{1,0:T(8,128)(2,1)S(1)}, bf16[32,768]{1,0:T(8,128)(2,1)S(1)}, u32[]{:S(2)}, u32[]{:S(2)}) collective-permute-start(bf16[32,768]{1,0:T(8,128)(2,1)S(1)} %get-tuple-element.57), channel_id=1, source_target_pairs={{0,8},{4,12},{8,0},{12,4},{16,24},{20,28},{24,16},{28,20},{1,9},{5... | collective-permute-start | bytes 147464 | tf_op jit(solution)/shard_map/ppermute | solution.py:32
  49.4 4.5 %collective-permute-start.14 = (bf16[32,768]{1,0:T(8,128)(2,1)S(1)}, bf16[32,768]{1,0:T(8,128)(2,1)S(1)}, u32[]{:S(2)}, u32[]{:S(2)}) collective-permute-start(bf16[32,768]{1,0:T(8,128)(2,1)S(1)} %get-tuple-element.58), channel_id=1, source_target_pairs={{0,16},{4,20},{8,24},{12,28},{16,0},{20,4},{24,8},{28,12},{1,17},{... | collective-permute-start | bytes 147464 | tf_op jit(solution)/shard_map/ppermute | solution.py:32
  50.6 5.0 %collective-permute-start.15 = (bf16[32,768]{1,0:T(8,128)(2,1)S(1)}, bf16[32,768]{1,0:T(8,128)(2,1)S(1)}, u32[]{:S(2)}, u32[]{:S(2)}) collective-permute-start(bf16[32,768]{1,0:T(8,128)(2,1)S(1)} %get-tuple-element.59), channel_id=1, source_target_pairs={{0,24},{4,28},{8,16},{12,20},{16,8},{20,12},{24,0},{28,4},{1,25},{... | collective-permute-start | bytes 147464 | tf_op jit(solution)/shard_map/ppermute | solution.py:32
  55.7 4.8 %collective-permute-start.18 = (bf16[32,768]{1,0:T(8,128)(2,1)S(1)}, bf16[32,768]{1,0:T(8,128)(2,1)S(1)}, u32[]{:S(2)}, u32[]{:S(2)}) collective-permute-start(bf16[32,768]{1,0:T(8,128)(2,1)S(1)} %add.29.refs_0_), channel_id=1, source_target_pairs={{0,24},{4,28},{8,16},{12,20},{16,8},{20,12},{24,0},{28,4},{1,25},{... | collective-permute-start | bytes 147464 | tf_op jit(solution)/shard_map/ppermute | solution.py:32
  57.2 4.8 %collective-permute-start.17 = (bf16[32,768]{1,0:T(8,128)(2,1)S(1)}, bf16[32,768]{1,0:T(8,128)(2,1)S(1)}, u32[]{:S(2)}, u32[]{:S(2)}) collective-permute-start(bf16[32,768]{1,0:T(8,128)(2,1)S(1)} %add.29.refs_0_), channel_id=1, source_target_pairs={{0,16},{4,20},{8,24},{12,28},{16,0},{20,4},{24,8},{28,12},{1,17},{... | collective-permute-start | bytes 147464 | tf_op jit(solution)/shard_map/ppermute | solution.py:32
  57.2 4.8 %collective-permute-start.16 = (bf16[32,768]{1,0:T(8,128)(2,1)S(1)}, bf16[32,768]{1,0:T(8,128)(2,1)S(1)}, u32[]{:S(2)}, u32[]{:S(2)}) collective-permute-start(bf16[32,768]{1,0:T(8,128)(2,1)S(1)} %add.29.refs_0_), channel_id=1, source_target_pairs={{0,8},{4,12},{8,0},{12,4},{16,24},{20,28},{24,16},{28,20},{1,9},{5... | collective-permute-start | bytes 147464 | tf_op jit(solution)/shard_map/ppermute | solution.py:32
  59.9 6.5 %copy-start.1 = (f32[2688]{0:T(1024)}, f32[2688]{0:T(1024)S(1)}, u32[]{:S(2)}) copy-start(f32[2688]{0:T(1024)S(1)} %get-tuple-element.72.refs_6_) | copy-start | bytes 32260
  63.5 3.0 %copy-start.3 = (s32[8]{0:T(128)S(1)}, s32[8]{0:T(128)}, u32[]{:S(2)}) copy-start(s32[8]{0:T(128)} %owners.5) | copy-start | bytes 100
  63.5 5.6 %collective-permute-start.21 = (bf16[4,32,768]{2,1,0:T(8,128)(2,1)S(1)}, bf16[4,32,768]{2,1,0:T(8,128)(2,1)S(1)}, u32[]{:S(2)}, u32[]{:S(2)}) collective-permute-start(bf16[4,32,768]{2,1,0:T(8,128)(2,1)S(1)} %stack.35.refs_0_), channel_id=1, source_target_pairs={{0,3},{1,2},{2,1},{3,0},{4,7},{5,6},{6,5},{7,4},{8,11},{9,10},{10,... | collective-permute-start | bytes 589832 | tf_op jit(solution)/shard_map/ppermute | solution.py:32
  65.1 8.7 %collective-permute-start.20 = (bf16[4,32,768]{2,1,0:T(8,128)(2,1)S(1)}, bf16[4,32,768]{2,1,0:T(8,128)(2,1)S(1)}, u32[]{:S(2)}, u32[]{:S(2)}) collective-permute-start(bf16[4,32,768]{2,1,0:T(8,128)(2,1)S(1)} %stack.35.refs_0_), channel_id=1, source_target_pairs={{0,2},{1,3},{2,0},{3,1},{4,6},{5,7},{6,4},{7,5},{8,10},{9,11},{10,... | collective-permute-start | bytes 589832 | tf_op jit(solution)/shard_map/ppermute | solution.py:32
  65.1 8.7 %collective-permute-start.19 = (bf16[4,32,768]{2,1,0:T(8,128)(2,1)S(1)}, bf16[4,32,768]{2,1,0:T(8,128)(2,1)S(1)}, u32[]{:S(2)}, u32[]{:S(2)}) collective-permute-start(bf16[4,32,768]{2,1,0:T(8,128)(2,1)S(1)} %stack.35.refs_0_), channel_id=1, source_target_pairs={{0,1},{1,0},{2,3},{3,2},{4,5},{5,4},{6,7},{7,6},{8,9},{9,8},{10,11... | collective-permute-start | bytes 589832 | tf_op jit(solution)/shard_map/ppermute | solution.py:32
  73.8 7.6 %collective-permute-start.22 = (bf16[4,1,4,32,768]{4,3,2,1,0:T(8,128)(2,1)S(1)}, bf16[4,1,4,32,768]{4,3,2,1,0:T(8,128)(2,1)S(1)}, u32[]{:S(2)}, u32[]{:S(2)}) collective-permute-start(bf16[4,1,4,32,768]{4,3,2,1,0:T(8,128)(2,1)S(1)} %bitcast.12), channel_id=1, source_target_pairs={{0,4},{4,0},{8,12},{12,8},{16,20},{20,16},{24,28},{28,24},{1,5},{5... | collective-permute-start | bytes 2359304 | tf_op jit(solution)/shard_map/ppermute | solution.py:32

commit v15 on v13

--- a/solution.py
+++ b/solution.py
@@ -8,7 +8,6 @@
 from jax.sharding import PartitionSpec as P
 
 CORES = 2
-AHEAD = 8
 BASE_ROWS = 48
 F32 = jnp.float32
 BF16 = jnp.bfloat16
@@ -33,7 +32,7 @@
     return lax.ppermute(x, axis, [(i, i ^ distance) for i in range(size)])
 
 
-def left_kernel(pos, g_ref, f_ref, q_ref, vec_ref, comp_ref, near_ref, far_ref, total, feedback, right, sems):
+def left_kernel(pos, g_ref, f_ref, q_ref, vec_ref, comp_ref, near_ref, far_ref, total, feedback, right, terms, sems):
     nmat, rows, _ = comp_ref.shape
     rank = q_ref.shape[1]
     part = near_ref.shape[0]
@@ -45,27 +44,29 @@
             pltpu.make_async_copy(q_ref.at[k], right.at[k], sems.at[k, 2]),
         ]
 
-    for k in range(min(AHEAD, nmat)):
+    @pl.loop(0, nmat)
+    def _(k):
         for copy in copies(k):
             copy.start()
+
     total[...] = jnp.zeros(total.shape, F32)
     width, nvec = total.shape[1], vec_ref.shape[1]
     for i, first in enumerate(range(0, nvec, width)):
         count = min(width, nvec - first)
         total[rows + i : rows + i + 1, :count] = vec_ref[:, first : first + count]
 
-    for k in range(nmat):
+    @pl.loop(0, nmat)
+    def _(k):
         for copy in copies(k):
             copy.wait()
-        if k + AHEAD < nmat:
-            for copy in copies(k + AHEAD):
-                copy.start()
         comp = comp_ref[k] + feedback[k]
         comp_ref[k] = comp
-        total[:rows, k * rank : (k + 1) * rank] = lax.dot_general(
+        terms[k] = lax.dot_general(
             comp, right[k], (((1,), (1,)), ((), ())), preferred_element_type=F32
         )
 
+    for k in range(nmat):
+        total[:rows, k * rank : (k + 1) * rank] = terms[k]
     for ref, core in ((near_ref, pos[2]), (far_ref, 1 - pos[2])):
         ref[...] = total[pl.ds(pl.multiple_of(core * part, 16), part), :]
 
@@ -90,6 +91,7 @@
                 pltpu.VMEM((total, width), F32),
                 pltpu.VMEM((nmat, rows, n), BF16),
                 pltpu.VMEM((nmat, rank, n), BF16),
+                pltpu.VMEM((nmat, rows, rank), F32),
                 pltpu.SemaphoreType.DMA((nmat, 3)),
             ],
         ),
@@ -430,16 +432,16 @@
     for i, (job, where_right) in enumerate(jobs.items()):
         k = matrix(*job)
         slot = (owners[k] ^ pos[5]) * capacity + rank_of(owners, k)
-        left, strip = left_ref[k], strip_ref[k]
+        left = jnp.concatenate([left_ref[k], strip_ref[k]], axis=0)
+        rows = left_ref.shape[1]
         for d in range(n_z):
             for block in pieces:
                 right = right_of(where_right, d, block)
                 place = columns(d, block.start, step)
                 approx = jnp.dot(left, right, preferred_element_type=F32)
-                feedback[i, :, place] = (comp_ref[k, :, place].astype(F32) - approx).astype(BF16)
-                approx = jnp.dot(strip, right, preferred_element_type=F32)
-                base = base_ref[slot, :, place].astype(F32)
-                weights[i, :, place] = (base - 0.1 * approx).astype(BF16)
+                comp, base = comp_ref[k, :, place].astype(F32), base_ref[slot, :, place].astype(F32)
+                feedback[i, :, place] = (comp - approx[:rows]).astype(BF16)
+                weights[i, :, place] = (base - 0.1 * approx[rows:]).astype(BF16)
             place = columns(d)
             store(feedback.at[i, :, place], outs[0].at[0, k, :, place], out_sem.at[i, d, 0])
             store(weights.at[i, :, place], outs[1].at[k, :, place], out_sem.at[i, d, 1])

time: 86.9 us -> 86.4 us (level)
  transfers between devices with their start and end apart: 23 -> 23, of which waited for: 15 -> 15; matrix products, arithmetic and copies ran while one was open for 1% -> 1% of each run, Pallas kernels for 22% -> 21%
where the time goes in v15:
time: 86.4 us; the launch traced here: 86.2 us
  Pallas kernels  29.5 us (34%)
  waiting for transfers between devices  28.8 us (33%)
  starting transfers between devices  26.3 us (30%)
    ppermute x23, waiting for transfers between devices, exchange(): return lax.ppermute(x, axis, [(i, i ^ distance) for i in range(size)])  28.8 us
    ppermute x23, starting transfers between devices, exchange(): return lax.ppermute(x, axis, [(i, i ^ distance) for i in range(size)])  26.3 us
    pallas_call x3, Pallas kernels, outputs(): pl.pallas_call(functools.partial(outputs_kernel, jobs, where, capacity),...  12.2 us
    pallas_call x1, Pallas kernels, left_terms(): pl.pallas_call(left_kernel, grid_spec=pltpu.PrefetchScalarGridSpec(num_sc...  8.26 us
    pallas_call x1, Pallas kernels, base_of(): pl.pallas_call(base_kernel, grid_spec=pltpu.PrefetchScalarGridSpec(num_sc...  3.16 us
    pallas_call x1, Pallas kernels, right_terms(): pl.pallas_call(functools.partial(send_kernel, half), grid_spec=pltpu.Pref...  2.22 us
  transfers between devices with their start and end apart: 23, of which 15 were waited for; matrix products, arithmetic and copies ran while one was open for 1% of the time, Pallas kernels for 21%

profile of v15, /device:TPU:1, one launch (start us, length us, event | category | flops | bytes accessed | tf_op | source)
XLA Modules:
  0.0 86.2 jit_solution(11186363327272452429)
XLA Ops:
  0.8 3.2 %base.1 = (bf16[2,96,3072]{2,1,0:T(8,128)(2,1)S(1)}, f32[2,96,3072]{2,1,0:T(8,128)S(1)}, f32[2,96,3072]{2,1,0:T(8,128)S(1)}, bf16[176,3072]{1,0:T(8,128)(2,1)S(1)}, bf16[176,3072]{1,0:T(8,128)(2,1)S(1)}) custom-call(s32[8]{0:T(128)S(1)} %stack.34.pos, f32[1,2,96,3072]{3,2,1,0:T(8,128)} %momentum_ref.1, f32[1,2,96,3072]{3,2,1,0:T(8,128)} %master_ref.1), custom_call_target="tpu_custom_call" | custom-call | flops 1000 | bytes 1000 | tf_op jit(solution)/shard_map/base/pallas_call | solution.py:520
  4.0 2.1 %collective-permute-start.6 = (bf16[176,3072]{1,0:T(8,128)(2,1)S(1)}, bf16[176,3072]{1,0:T(8,128)(2,1)S(1)}, u32[]{:S(2)}, u32[]{:S(2)}) collective-permute-start(bf16[176,3072]{1,0:T(8,128)(2,1)S(1)} %get-tuple-element.45), channel_id=1, source_target_pairs={{0,1},{1,0},{2,3},{3,2},{4,5},{5,4},{6,7},{7,6},{8,9},{9,8},{10,11... | collective-permute-start | bytes 3244040 | tf_op jit(solution)/shard_map/ppermute | solution.py:32
  6.1 1.2 %collective-permute-start.7 = (bf16[176,3072]{1,0:T(8,128)(2,1)S(1)}, bf16[176,3072]{1,0:T(8,128)(2,1)S(1)}, u32[]{:S(2)}, u32[]{:S(2)}) collective-permute-start(bf16[176,3072]{1,0:T(8,128)(2,1)S(1)} %get-tuple-element.46), channel_id=1, source_target_pairs={{0,2},{1,3},{2,0},{3,1},{4,6},{5,7},{6,4},{7,5},{8,10},{9,11},{10,... | collective-permute-start | bytes 3244040 | tf_op jit(solution)/shard_map/ppermute | solution.py:32
  7.3 8.3 %left_terms.1 = (bf16[8,192,3072]{2,1,0:T(8,128)(2,1)S(1)}, f32[112,256]{1,0:T(8,128)S(1)}, f32[112,256]{1,0:T(8,128)S(1)}) custom-call(s32[8]{0:T(128)S(1)} %stack.34.pos, bf16[1,8,192,3072]{3,2,1,0:T(8,128)(2,1)} %g_ref.1, bf16[1,8,192,3072]{3,2,1,0:T(8,128)(2,1)} %f_ref.1, bf16[8,32,3072]{2,1,0:T(8,128)(2,1)} %bitcast.17, f32[1,2688]{1,0:T(1,128)S(1)} %copy-done.2), custom_call_target="tpu_custom_call" | custom-call | flops 1000 | bytes 1000 | tf_op jit(solution)/shard_map/left_terms/pallas_call | solution.py:83
  15.6 1.3 %collective-permute-start = (f32[112,256]{1,0:T(8,128)S(1)}, f32[112,256]{1,0:T(8,128)S(1)}, u32[]{:S(2)}, u32[]{:S(2)}) collective-permute-start(f32[112,256]{1,0:T(8,128)S(1)} %get-tuple-element.41), channel_id=1, source_target_pairs={{0,4},{4,0},{8,12},{12,8},{16,20},{20,16},{24,28},{28,24},{1,5},{5... | collective-permute-start | bytes 344072 | tf_op jit(solution)/shard_map/ppermute | solution.py:32
  16.9 1.0 %collective-permute-done.refs_1_ = f32[112,256]{1,0:T(8,128)S(1)} collective-permute-done((f32[112,256]{1,0:T(8,128)S(1)}, f32[112,256]{1,0:T(8,128)S(1)}, u32[]{:S(2)}, u32[]{:S(2)}) %collective-permute-start) | collective-permute-done | bytes 114720 | tf_op jit(solution)/shard_map/ppermute | solution.py:32
  17.9 3.4 %collective-permute-start.3 = (bf16[112,256]{1,0:T(8,128)(2,1)S(1)}, bf16[112,256]{1,0:T(8,128)(2,1)S(1)}, u32[]{:S(2)}, u32[]{:S(2)}) collective-permute-start(bf16[112,256]{1,0:T(8,128)(2,1)S(1)} %add.27.refs_0_), channel_id=1, source_target_pairs={{0,24},{4,28},{8,16},{12,20},{16,8},{20,12},{24,0},{28,4},{1,25},{... | collective-permute-start | bytes 172040 | tf_op jit(solution)/shard_map/ppermute | solution.py:32
  21.6 1.3 %collective-permute-done.3.refs_3_ = bf16[112,256]{1,0:T(8,128)(2,1)S(1)} collective-permute-done((bf16[112,256]{1,0:T(8,128)(2,1)S(1)}, bf16[112,256]{1,0:T(8,128)(2,1)S(1)}, u32[]{:S(2)}, u32[]{:S(2)}) %collective-permute-start.3) | collective-permute-done | bytes 57376 | tf_op jit(solution)/shard_map/ppermute | solution.py:32
  22.9 3.4 %collective-permute-done.2.refs_2_ = bf16[112,256]{1,0:T(8,128)(2,1)S(1)} collective-permute-done((bf16[112,256]{1,0:T(8,128)(2,1)S(1)}, bf16[112,256]{1,0:T(8,128)(2,1)S(1)}, u32[]{:S(2)}, u32[]{:S(2)}) %collective-permute-start.2) | collective-permute-done | bytes 57376 | tf_op jit(solution)/shard_map/ppermute | solution.py:32
  26.4 1.0 %collective-permute-start.4 = (f32[112,256]{1,0:T(8,128)S(1)}, f32[112,256]{1,0:T(8,128)S(1)}, u32[]{:S(2)}, u32[]{:S(2)}) collective-permute-start(f32[112,256]{1,0:T(8,128)S(1)} %add.28.near_ref), channel_id=1, source_target_pairs={{0,4},{4,0},{8,12},{12,8},{16,20},{20,16},{24,28},{28,24},{1,5},{5... | collective-permute-start | bytes 344072 | tf_op jit(solution)/shard_map/ppermute | solution.py:32
  27.4 1.0 %collective-permute-done.4.far_ref = f32[112,256]{1,0:T(8,128)S(1)} collective-permute-done((f32[112,256]{1,0:T(8,128)S(1)}, f32[112,256]{1,0:T(8,128)S(1)}, u32[]{:S(2)}, u32[]{:S(2)}) %collective-permute-start.4) | collective-permute-done | bytes 114720 | tf_op jit(solution)/shard_map/ppermute | solution.py:32
  28.3 2.2 %right_send.1 = (bf16[4,1,32,3072]{3,2,1,0:T(8,128)(2,1)S(1)}, bf16[256,192]{1,0:T(8,128)(2,1)S(1)}, bf16[8,192,32]{2,1,0:T(8,128)(2,1)S(1)}, f32[32,256]{1,0:T(8,128)S(1)}) custom-call(s32[8]{0:T(128)S(1)} %stack.34.pos, f32[112,256]{1,0:T(8,128)S(1)} %add.28.near_ref, f32[112,256]{1,0:T(8,128)S(1)} %collective-permute-done.4.far_ref, ...), custom_call_target="tpu_custom_call" | custom-call | flops 1000 | bytes 1000 | tf_op jit(solution)/shard_map/right_send/pallas_call | solution.py:164
  31.0 1.5 %right_keep.1.refs_0_.keep_ref = f32[4,1,32,3072]{3,2,1,0:T(8,128)S(1)} custom-call(s32[8]{0:T(128)S(1)} %stack.34.pos, bf16[256,192]{1,0:T(8,128)(2,1)S(1)} %get-tuple-element.43.lt_ref, bf16[8,192,3072]{2,1,0:T(8,128)(2,1)S(1)} %get-tuple-element.39.comp_ref), custom_call_target="tpu_custom_call" | custom-call | flops 1000 | bytes 1000 | tf_op jit(solution)/shard_map/right_keep/pallas_call | solution.py:183
  34.3 2.2 %collective-permute-start.10 = (bf16[40,3072]{1,0:T(8,128)(2,1)S(1)}, bf16[40,3072]{1,0:T(8,128)(2,1)S(1)}, u32[]{:S(2)}, u32[]{:S(2)}) collective-permute-start(bf16[40,3072]{1,0:T(8,128)(2,1)S(1)} %get-tuple-element.51), channel_id=1, source_target_pairs={{0,3},{1,2},{2,1},{3,0},{4,7},{5,6},{6,5},{7,4},{8,11},{9,10},{10,... | collective-permute-start | bytes 737288 | tf_op jit(solution)/shard_map/ppermute | solution.py:32
  36.4 4.5 %collective-permute-done.8.refs_0_ = bf16[40,3072]{1,0:T(8,128)(2,1)S(1)} collective-permute-done((bf16[40,3072]{1,0:T(8,128)(2,1)S(1)}, bf16[40,3072]{1,0:T(8,128)(2,1)S(1)}, u32[]{:S(2)}, u32[]{:S(2)}) %collective-permute-start.8) | collective-permute-done | bytes 245792 | tf_op jit(solution)/shard_map/ppermute | solution.py:32
  41.0 5.2 %collective-permute-done.10.refs_2_ = bf16[40,3072]{1,0:T(8,128)(2,1)S(1)} collective-permute-done((bf16[40,3072]{1,0:T(8,128)(2,1)S(1)}, bf16[40,3072]{1,0:T(8,128)(2,1)S(1)}, u32[]{:S(2)}, u32[]{:S(2)}) %collective-permute-start.10) | collective-permute-done | bytes 245792 | tf_op jit(solution)/shard_map/ppermute | solution.py:32
  47.0 1.3 %collective-permute-start.11 = (bf16[112,3072]{1,0:T(8,128)(2,1)S(1)}, bf16[112,3072]{1,0:T(8,128)(2,1)S(1)}, u32[]{:S(2)}, u32[]{:S(2)}) collective-permute-start(bf16[112,3072]{1,0:T(8,128)(2,1)S(1)} %get-tuple-element.54), channel_id=1, source_target_pairs={{0,1},{1,0},{2,3},{3,2},{4,5},{5,4},{6,7},{7,6},{8,9},{9,8},{10,11... | collective-permute-start | bytes 2064392 | tf_op jit(solution)/shard_map/ppermute | solution.py:32
  49.4 1.2 %collective-permute-start.14 = (bf16[32,768]{1,0:T(8,128)(2,1)S(1)}, bf16[32,768]{1,0:T(8,128)(2,1)S(1)}, u32[]{:S(2)}, u32[]{:S(2)}) collective-permute-start(bf16[32,768]{1,0:T(8,128)(2,1)S(1)} %get-tuple-element.58), channel_id=1, source_target_pairs={{0,16},{4,20},{8,24},{12,28},{16,0},{20,4},{24,8},{28,12},{1,17},{... | collective-permute-start | bytes 147464 | tf_op jit(solution)/shard_map/ppermute | solution.py:32
  50.6 1.5 %collective-permute-start.15 = (bf16[32,768]{1,0:T(8,128)(2,1)S(1)}, bf16[32,768]{1,0:T(8,128)(2,1)S(1)}, u32[]{:S(2)}, u32[]{:S(2)}) collective-permute-start(bf16[32,768]{1,0:T(8,128)(2,1)S(1)} %get-tuple-element.59), channel_id=1, source_target_pairs={{0,24},{4,28},{8,16},{12,20},{16,8},{20,12},{24,0},{28,4},{1,25},{... | collective-permute-start | bytes 147464 | tf_op jit(solution)/shard_map/ppermute | solution.py:32
  52.2 1.7 %collective-permute-done.14.refs_2_ = bf16[32,768]{1,0:T(8,128)(2,1)S(1)} collective-permute-done((bf16[32,768]{1,0:T(8,128)(2,1)S(1)}, bf16[32,768]{1,0:T(8,128)(2,1)S(1)}, u32[]{:S(2)}, u32[]{:S(2)}) %collective-permute-start.14) | collective-permute-done | bytes 49184 | tf_op jit(solution)/shard_map/ppermute | solution.py:32
  53.9 1.8 %collective-permute-done.15.refs_3_ = bf16[32,768]{1,0:T(8,128)(2,1)S(1)} collective-permute-done((bf16[32,768]{1,0:T(8,128)(2,1)S(1)}, bf16[32,768]{1,0:T(8,128)(2,1)S(1)}, u32[]{:S(2)}, u32[]{:S(2)}) %collective-permute-start.15) | collective-permute-done | bytes 49184 | tf_op jit(solution)/shard_map/ppermute | solution.py:32
  55.7 1.5 %collective-permute-start.18 = (bf16[32,768]{1,0:T(8,128)(2,1)S(1)}, bf16[32,768]{1,0:T(8,128)(2,1)S(1)}, u32[]{:S(2)}, u32[]{:S(2)}) collective-permute-start(bf16[32,768]{1,0:T(8,128)(2,1)S(1)} %add.29.refs_0_), channel_id=1, source_target_pairs={{0,24},{4,28},{8,16},{12,20},{16,8},{20,12},{24,0},{28,4},{1,25},{... | collective-permute-start | bytes 147464 | tf_op jit(solution)/shard_map/ppermute | solution.py:32
  57.2 2.1 %collective-permute-start.16 = (bf16[32,768]{1,0:T(8,128)(2,1)S(1)}, bf16[32,768]{1,0:T(8,128)(2,1)S(1)}, u32[]{:S(2)}, u32[]{:S(2)}) collective-permute-start(bf16[32,768]{1,0:T(8,128)(2,1)S(1)} %add.29.refs_0_), channel_id=1, source_target_pairs={{0,8},{4,12},{8,0},{12,4},{16,24},{20,28},{24,16},{28,20},{1,9},{5... | collective-permute-start | bytes 147464 | tf_op jit(solution)/shard_map/ppermute | solution.py:32
  60.6 1.5 %collective-permute-done.17.refs_2_ = bf16[32,768]{1,0:T(8,128)(2,1)S(1)} collective-permute-done((bf16[32,768]{1,0:T(8,128)(2,1)S(1)}, bf16[32,768]{1,0:T(8,128)(2,1)S(1)}, u32[]{:S(2)}, u32[]{:S(2)}) %collective-permute-start.17) | collective-permute-done | bytes 49184 | tf_op jit(solution)/shard_map/ppermute | solution.py:32
  62.4 1.0 %collective-permute-done.12.refs_3_.refs_5_ = bf16[112,3072]{1,0:T(8,128)(2,1)S(1)} collective-permute-done((bf16[112,3072]{1,0:T(8,128)(2,1)S(1)}, bf16[112,3072]{1,0:T(8,128)(2,1)S(1)}, u32[]{:S(2)}, u32[]{:S(2)}) %collective-permute-start.12) | collective-permute-done | bytes 688160 | tf_op jit(solution)/shard_map/ppermute | solution.py:32
  63.5 1.6 %collective-permute-start.21 = (bf16[4,32,768]{2,1,0:T(8,128)(2,1)S(1)}, bf16[4,32,768]{2,1,0:T(8,128)(2,1)S(1)}, u32[]{:S(2)}, u32[]{:S(2)}) collective-permute-start(bf16[4,32,768]{2,1,0:T(8,128)(2,1)S(1)} %stack.35.refs_0_), channel_id=1, source_target_pairs={{0,3},{1,2},{2,1},{3,0},{4,7},{5,6},{6,5},{7,4},{8,11},{9,10},{10,... | collective-permute-start | bytes 589832 | tf_op jit(solution)/shard_map/ppermute | solution.py:32
  65.1 1.1 %collective-permute-start.19 = (bf16[4,32,768]{2,1,0:T(8,128)(2,1)S(1)}, bf16[4,32,768]{2,1,0:T(8,128)(2,1)S(1)}, u32[]{:S(2)}, u32[]{:S(2)}) collective-permute-start(bf16[4,32,768]{2,1,0:T(8,128)(2,1)S(1)} %stack.35.refs_0_), channel_id=1, source_target_pairs={{0,1},{1,0},{2,3},{3,2},{4,5},{5,4},{6,7},{7,6},{8,9},{9,8},{10,11... | collective-permute-start | bytes 589832 | tf_op jit(solution)/shard_map/ppermute | solution.py:32
  66.5 2.1 %outputs.3 = (bf16[1,8,192,3072]{3,2,1,0:T(8,128)(2,1)}, bf16[8,96,3072]{2,1,0:T(8,128)(2,1)}, f32[8,128]{1,0:T(8,128)S(1)}) custom-call(s32[8]{0:T(128)S(1)} %stack.34.pos, s32[8]{0:T(128)S(1)} %copy-done.3, bf16[8,192,3072]{2,1,0:T(8,128)(2,1)S(1)} %get-tuple-element.39.comp_ref, bf16[8,192,32]{2,1,0:T(8,128)(2,1)S(1)} %get-tuple-element.42.left_ref, ...), custom_call_target="tpu_custom_call" | custom-call | flops 1000 | bytes 1000 | tf_op jit(solution)/shard_map/outputs/pallas_call | solution.py:472
  69.1 4.7 %collective-permute-done.20.refs_2_ = bf16[4,32,768]{2,1,0:T(8,128)(2,1)S(1)} collective-permute-done((bf16[4,32,768]{2,1,0:T(8,128)(2,1)S(1)}, bf16[4,32,768]{2,1,0:T(8,128)(2,1)S(1)}, u32[]{:S(2)}, u32[]{:S(2)}) %collective-permute-start.20) | collective-permute-done | bytes 196640 | tf_op jit(solution)/shard_map/ppermute | solution.py:32
  73.8 2.3 %collective-permute-start.22 = (bf16[4,1,4,32,768]{4,3,2,1,0:T(8,128)(2,1)S(1)}, bf16[4,1,4,32,768]{4,3,2,1,0:T(8,128)(2,1)S(1)}, u32[]{:S(2)}, u32[]{:S(2)}) collective-permute-start(bf16[4,1,4,32,768]{4,3,2,1,0:T(8,128)(2,1)S(1)} %bitcast.12), channel_id=1, source_target_pairs={{0,4},{4,0},{8,12},{12,8},{16,20},{20,16},{24,28},{28,24},{1,5},{5... | collective-permute-start | bytes 2359304 | tf_op jit(solution)/shard_map/ppermute | solution.py:32
  76.1 4.0 %outputs.4 = (bf16[1,8,192,3072]{3,2,1,0:T(8,128)(2,1)}, bf16[8,96,3072]{2,1,0:T(8,128)(2,1)}, f32[8,128]{1,0:T(8,128)}) custom-call(s32[8]{0:T(128)S(1)} %stack.34.pos, s32[8]{0:T(128)S(1)} %copy-done.3, bf16[8,192,3072]{2,1,0:T(8,128)(2,1)S(1)} %get-tuple-element.39.comp_ref, ...), custom_call_target="tpu_custom_call", output_to_operand_aliasing={{0}: (7, {}), {1}: (8, {})} | custom-call | flops 1000 | bytes 1000 | tf_op jit(solution)/shard_map/outputs/pallas_call | solution.py:472
  80.1 6.2 %outputs.5 = (bf16[1,8,192,3072]{3,2,1,0:T(8,128)(2,1)}, bf16[8,96,3072]{2,1,0:T(8,128)(2,1)}, f32[1,2,96,3072]{3,2,1,0:T(8,128)}, f32[1,2,96,3072]{3,2,1,0:T(8,128)}, f32[8,128]{1,0:T(8,128)}) custom-call(s32[8]{0:T(128)S(1)} %stack.34.pos, s32[8]{0:T(128)S(1)} %copy-done.3, ...), custom_call_target="tpu_custom_call", output_to_operand_aliasing={{0}: (10, {}), {1}: (11, {})} | custom-call | flops 1000 | bytes 1000 | tf_op jit(solution)/shard_map/outputs/pallas_call | solution.py:472
  (46 shorter events, 7.1 us)
Async XLA Ops:
  0.8 6.5 %copy-start.2 = (f32[1,2688]{1,0:T(1,128)S(1)}, f32[1,2688]{1,0:T(1,128)}, u32[]{:S(2)}) copy-start(f32[1,2688]{1,0:T(1,128)} %vec_ref.1) | copy-start | bytes 32260
  4.0 28.6 %collective-permute-start.6 = (bf16[176,3072]{1,0:T(8,128)(2,1)S(1)}, bf16[176,3072]{1,0:T(8,128)(2,1)S(1)}, u32[]{:S(2)}, u32[]{:S(2)}) collective-permute-start(bf16[176,3072]{1,0:T(8,128)(2,1)S(1)} %get-tuple-element.45), channel_id=1, source_target_pairs={{0,1},{1,0},{2,3},{3,2},{4,5},{5,4},{6,7},{7,6},{8,9},{9,8},{10,11... | collective-permute-start | bytes 3244040 | tf_op jit(solution)/shard_map/ppermute | solution.py:32
  6.1 26.5 %collective-permute-start.7 = (bf16[176,3072]{1,0:T(8,128)(2,1)S(1)}, bf16[176,3072]{1,0:T(8,128)(2,1)S(1)}, u32[]{:S(2)}, u32[]{:S(2)}) collective-permute-start(bf16[176,3072]{1,0:T(8,128)(2,1)S(1)} %get-tuple-element.46), channel_id=1, source_target_pairs={{0,2},{1,3},{2,0},{3,1},{4,6},{5,7},{6,4},{7,5},{8,10},{9,11},{10,... | collective-permute-start | bytes 3244040 | tf_op jit(solution)/shard_map/ppermute | solution.py:32
  7.3 21.0 %copy-start = (f32[8,32,32]{2,1,0:T(8,128)S(1)}, f32[8,32,32]{2,1,0:T(8,128)}, u32[]{:S(2)}) copy-start(f32[8,32,32]{2,1,0:T(8,128)} %gram_ref.1) | copy-start | bytes 98308
  15.6 2.3 %collective-permute-start = (f32[112,256]{1,0:T(8,128)S(1)}, f32[112,256]{1,0:T(8,128)S(1)}, u32[]{:S(2)}, u32[]{:S(2)}) collective-permute-start(f32[112,256]{1,0:T(8,128)S(1)} %get-tuple-element.41), channel_id=1, source_target_pairs={{0,4},{4,0},{8,12},{12,8},{16,20},{20,16},{24,28},{28,24},{1,5},{5... | collective-permute-start | bytes 344072 | tf_op jit(solution)/shard_map/ppermute | solution.py:32
  17.9 5.1 %collective-permute-start.3 = (bf16[112,256]{1,0:T(8,128)(2,1)S(1)}, bf16[112,256]{1,0:T(8,128)(2,1)S(1)}, u32[]{:S(2)}, u32[]{:S(2)}) collective-permute-start(bf16[112,256]{1,0:T(8,128)(2,1)S(1)} %add.27.refs_0_), channel_id=1, source_target_pairs={{0,24},{4,28},{8,16},{12,20},{16,8},{20,12},{24,0},{28,4},{1,25},{... | collective-permute-start | bytes 172040 | tf_op jit(solution)/shard_map/ppermute | solution.py:32
  21.2 5.1 %collective-permute-start.2 = (bf16[112,256]{1,0:T(8,128)(2,1)S(1)}, bf16[112,256]{1,0:T(8,128)(2,1)S(1)}, u32[]{:S(2)}, u32[]{:S(2)}) collective-permute-start(bf16[112,256]{1,0:T(8,128)(2,1)S(1)} %add.27.refs_0_), channel_id=1, source_target_pairs={{0,16},{4,20},{8,24},{12,28},{16,0},{20,4},{24,8},{28,12},{1,17},{... | collective-permute-start | bytes 172040 | tf_op jit(solution)/shard_map/ppermute | solution.py:32
  21.2 5.1 %collective-permute-start.1 = (bf16[112,256]{1,0:T(8,128)(2,1)S(1)}, bf16[112,256]{1,0:T(8,128)(2,1)S(1)}, u32[]{:S(2)}, u32[]{:S(2)}) collective-permute-start(bf16[112,256]{1,0:T(8,128)(2,1)S(1)} %add.27.refs_0_), channel_id=1, source_target_pairs={{0,8},{4,12},{8,0},{12,4},{16,24},{20,28},{24,16},{28,20},{1,9},{5... | collective-permute-start | bytes 172040 | tf_op jit(solution)/shard_map/ppermute | solution.py:32
  26.4 2.0 %collective-permute-start.4 = (f32[112,256]{1,0:T(8,128)S(1)}, f32[112,256]{1,0:T(8,128)S(1)}, u32[]{:S(2)}, u32[]{:S(2)}) collective-permute-start(f32[112,256]{1,0:T(8,128)S(1)} %add.28.near_ref), channel_id=1, source_target_pairs={{0,4},{4,0},{8,12},{12,8},{16,20},{20,16},{24,28},{28,24},{1,5},{5... | collective-permute-start | bytes 344072 | tf_op jit(solution)/shard_map/ppermute | solution.py:32
  30.6 2.4 %collective-permute-start.5 = (bf16[4,1,32,3072]{3,2,1,0:T(8,128)(2,1)S(1)}, bf16[4,1,32,3072]{3,2,1,0:T(8,128)(2,1)S(1)}, u32[]{:S(2)}, u32[]{:S(2)}) collective-permute-start(bf16[4,1,32,3072]{3,2,1,0:T(8,128)(2,1)S(1)} %get-tuple-element.44), channel_id=1, source_target_pairs={{0,4},{4,0},{8,12},{12,8},{16,20},{20,16},{24,28},{28,24},{1,5},{5... | collective-permute-start | bytes 2359304 | tf_op jit(solution)/shard_map/ppermute | solution.py:32
  33.7 7.2 %collective-permute-start.8 = (bf16[40,3072]{1,0:T(8,128)(2,1)S(1)}, bf16[40,3072]{1,0:T(8,128)(2,1)S(1)}, u32[]{:S(2)}, u32[]{:S(2)}) collective-permute-start(bf16[40,3072]{1,0:T(8,128)(2,1)S(1)} %get-tuple-element.49), channel_id=1, source_target_pairs={{0,1},{1,0},{2,3},{3,2},{4,5},{5,4},{6,7},{7,6},{8,9},{9,8},{10,11... | collective-permute-start | bytes 737288 | tf_op jit(solution)/shard_map/ppermute | solution.py:32
  34.0 6.9 %collective-permute-start.9 = (bf16[40,3072]{1,0:T(8,128)(2,1)S(1)}, bf16[40,3072]{1,0:T(8,128)(2,1)S(1)}, u32[]{:S(2)}, u32[]{:S(2)}) collective-permute-start(bf16[40,3072]{1,0:T(8,128)(2,1)S(1)} %get-tuple-element.50), channel_id=1, source_target_pairs={{0,2},{1,3},{2,0},{3,1},{4,6},{5,7},{6,4},{7,5},{8,10},{9,11},{10,... | collective-permute-start | bytes 737288 | tf_op jit(solution)/shard_map/ppermute | solution.py:32
  34.3 11.9 %collective-permute-start.10 = (bf16[40,3072]{1,0:T(8,128)(2,1)S(1)}, bf16[40,3072]{1,0:T(8,128)(2,1)S(1)}, u32[]{:S(2)}, u32[]{:S(2)}) collective-permute-start(bf16[40,3072]{1,0:T(8,128)(2,1)S(1)} %get-tuple-element.51), channel_id=1, source_target_pairs={{0,3},{1,2},{2,1},{3,0},{4,7},{5,6},{6,5},{7,4},{8,11},{9,10},{10,... | collective-permute-start | bytes 737288 | tf_op jit(solution)/shard_map/ppermute | solution.py:32
  46.1 13.2 %copy-start.4 = (f32[2688]{0:T(1024)S(1)}, f32[2688]{0:T(1024)}, u32[]{:S(2)}) copy-start(f32[2688]{0:T(1024)} %param.19) | copy-start | bytes 32260
  46.1 13.2 %copy-start.5 = (f32[2688]{0:T(1024)S(1)}, f32[2688]{0:T(1024)}, u32[]{:S(2)}) copy-start(f32[2688]{0:T(1024)} %param.18) | copy-start | bytes 32260
  47.0 15.4 %collective-permute-start.11 = (bf16[112,3072]{1,0:T(8,128)(2,1)S(1)}, bf16[112,3072]{1,0:T(8,128)(2,1)S(1)}, u32[]{:S(2)}, u32[]{:S(2)}) collective-permute-start(bf16[112,3072]{1,0:T(8,128)(2,1)S(1)} %get-tuple-element.54), channel_id=1, source_target_pairs={{0,1},{1,0},{2,3},{3,2},{4,5},{5,4},{6,7},{7,6},{8,9},{9,8},{10,11... | collective-permute-start | bytes 2064392 | tf_op jit(solution)/shard_map/ppermute | solution.py:32
  48.3 15.1 %collective-permute-start.12 = (bf16[112,3072]{1,0:T(8,128)(2,1)S(1)}, bf16[112,3072]{1,0:T(8,128)(2,1)S(1)}, u32[]{:S(2)}, u32[]{:S(2)}) collective-permute-start(bf16[112,3072]{1,0:T(8,128)(2,1)S(1)} %get-tuple-element.55), channel_id=1, source_target_pairs={{0,2},{1,3},{2,0},{3,1},{4,6},{5,7},{6,4},{7,5},{8,10},{9,11},{10,... | collective-permute-start | bytes 2064392 | tf_op jit(solution)/shard_map/ppermute | solution.py:32
  48.6 3.6 %collective-permute-start.13 = (bf16[32,768]{1,0:T(8,128)(2,1)S(1)}, bf16[32,768]{1,0:T(8,128)(2,1)S(1)}, u32[]{:S(2)}, u32[]{:S(2)}) collective-permute-start(bf16[32,768]{1,0:T(8,128)(2,1)S(1)} %get-tuple-element.57), channel_id=1, source_target_pairs={{0,8},{4,12},{8,0},{12,4},{16,24},{20,28},{24,16},{28,20},{1,9},{5... | collective-permute-start | bytes 147464 | tf_op jit(solution)/shard_map/ppermute | solution.py:32
  49.4 4.5 %collective-permute-start.14 = (bf16[32,768]{1,0:T(8,128)(2,1)S(1)}, bf16[32,768]{1,0:T(8,128)(2,1)S(1)}, u32[]{:S(2)}, u32[]{:S(2)}) collective-permute-start(bf16[32,768]{1,0:T(8,128)(2,1)S(1)} %get-tuple-element.58), channel_id=1, source_target_pairs={{0,16},{4,20},{8,24},{12,28},{16,0},{20,4},{24,8},{28,12},{1,17},{... | collective-permute-start | bytes 147464 | tf_op jit(solution)/shard_map/ppermute | solution.py:32
  50.6 5.0 %collective-permute-start.15 = (bf16[32,768]{1,0:T(8,128)(2,1)S(1)}, bf16[32,768]{1,0:T(8,128)(2,1)S(1)}, u32[]{:S(2)}, u32[]{:S(2)}) collective-permute-start(bf16[32,768]{1,0:T(8,128)(2,1)S(1)} %get-tuple-element.59), channel_id=1, source_target_pairs={{0,24},{4,28},{8,16},{12,20},{16,8},{20,12},{24,0},{28,4},{1,25},{... | collective-permute-start | bytes 147464 | tf_op jit(solution)/shard_map/ppermute | solution.py:32
  55.7 4.8 %collective-permute-start.18 = (bf16[32,768]{1,0:T(8,128)(2,1)S(1)}, bf16[32,768]{1,0:T(8,128)(2,1)S(1)}, u32[]{:S(2)}, u32[]{:S(2)}) collective-permute-start(bf16[32,768]{1,0:T(8,128)(2,1)S(1)} %add.29.refs_0_), channel_id=1, source_target_pairs={{0,24},{4,28},{8,16},{12,20},{16,8},{20,12},{24,0},{28,4},{1,25},{... | collective-permute-start | bytes 147464 | tf_op jit(solution)/shard_map/ppermute | solution.py:32
  57.2 4.8 %collective-permute-start.17 = (bf16[32,768]{1,0:T(8,128)(2,1)S(1)}, bf16[32,768]{1,0:T(8,128)(2,1)S(1)}, u32[]{:S(2)}, u32[]{:S(2)}) collective-permute-start(bf16[32,768]{1,0:T(8,128)(2,1)S(1)} %add.29.refs_0_), channel_id=1, source_target_pairs={{0,16},{4,20},{8,24},{12,28},{16,0},{20,4},{24,8},{28,12},{1,17},{... | collective-permute-start | bytes 147464 | tf_op jit(solution)/shard_map/ppermute | solution.py:32
  57.2 4.8 %collective-permute-start.16 = (bf16[32,768]{1,0:T(8,128)(2,1)S(1)}, bf16[32,768]{1,0:T(8,128)(2,1)S(1)}, u32[]{:S(2)}, u32[]{:S(2)}) collective-permute-start(bf16[32,768]{1,0:T(8,128)(2,1)S(1)} %add.29.refs_0_), channel_id=1, source_target_pairs={{0,8},{4,12},{8,0},{12,4},{16,24},{20,28},{24,16},{28,20},{1,9},{5... | collective-permute-start | bytes 147464 | tf_op jit(solution)/shard_map/ppermute | solution.py:32
  59.9 6.5 %copy-start.1 = (f32[2688]{0:T(1024)}, f32[2688]{0:T(1024)S(1)}, u32[]{:S(2)}) copy-start(f32[2688]{0:T(1024)S(1)} %get-tuple-element.72.refs_6_) | copy-start | bytes 32260
  63.5 3.0 %copy-start.3 = (s32[8]{0:T(128)S(1)}, s32[8]{0:T(128)}, u32[]{:S(2)}) copy-start(s32[8]{0:T(128)} %owners.5) | copy-start | bytes 100
  63.5 5.6 %collective-permute-start.21 = (bf16[4,32,768]{2,1,0:T(8,128)(2,1)S(1)}, bf16[4,32,768]{2,1,0:T(8,128)(2,1)S(1)}, u32[]{:S(2)}, u32[]{:S(2)}) collective-permute-start(bf16[4,32,768]{2,1,0:T(8,128)(2,1)S(1)} %stack.35.refs_0_), channel_id=1, source_target_pairs={{0,3},{1,2},{2,1},{3,0},{4,7},{5,6},{6,5},{7,4},{8,11},{9,10},{10,... | collective-permute-start | bytes 589832 | tf_op jit(solution)/shard_map/ppermute | solution.py:32
  65.1 8.7 %collective-permute-start.20 = (bf16[4,32,768]{2,1,0:T(8,128)(2,1)S(1)}, bf16[4,32,768]{2,1,0:T(8,128)(2,1)S(1)}, u32[]{:S(2)}, u32[]{:S(2)}) collective-permute-start(bf16[4,32,768]{2,1,0:T(8,128)(2,1)S(1)} %stack.35.refs_0_), channel_id=1, source_target_pairs={{0,2},{1,3},{2,0},{3,1},{4,6},{5,7},{6,4},{7,5},{8,10},{9,11},{10,... | collective-permute-start | bytes 589832 | tf_op jit(solution)/shard_map/ppermute | solution.py:32
  65.1 8.7 %collective-permute-start.19 = (bf16[4,32,768]{2,1,0:T(8,128)(2,1)S(1)}, bf16[4,32,768]{2,1,0:T(8,128)(2,1)S(1)}, u32[]{:S(2)}, u32[]{:S(2)}) collective-permute-start(bf16[4,32,768]{2,1,0:T(8,128)(2,1)S(1)} %stack.35.refs_0_), channel_id=1, source_target_pairs={{0,1},{1,0},{2,3},{3,2},{4,5},{5,4},{6,7},{7,6},{8,9},{9,8},{10,11... | collective-permute-start | bytes 589832 | tf_op jit(solution)/shard_map/ppermute | solution.py:32
  73.8 6.3 %collective-permute-start.22 = (bf16[4,1,4,32,768]{4,3,2,1,0:T(8,128)(2,1)S(1)}, bf16[4,1,4,32,768]{4,3,2,1,0:T(8,128)(2,1)S(1)}, u32[]{:S(2)}, u32[]{:S(2)}) collective-permute-start(bf16[4,1,4,32,768]{4,3,2,1,0:T(8,128)(2,1)S(1)} %bitcast.12), channel_id=1, source_target_pairs={{0,4},{4,0},{8,12},{12,8},{16,20},{20,16},{24,28},{28,24},{1,5},{5... | collective-permute-start | bytes 2359304 | tf_op jit(solution)/shard_map/ppermute | solution.py:32

commit v16 on v15

--- a/solution.py
+++ b/solution.py
@@ -603,9 +603,12 @@
     shape = (half, upm) + whole.shape
     done, near_jobs, after = (), {(0, j): (0, j) for j in range(half)}, [slots]
     if upm == 1:
-        *done, after = outputs(*common, [whole[None, None]], {(0, 0): (0, 0)})
+        *done, _ = outputs(*common, [whole[None, None]], {(0, 0): (0, 0)})
+        *done, after = outputs(
+            *common, [others[-1][None, None]], {(0, half - 1): (0, 0)}, earlier=done
+        )
         after = [after]
-        del near_jobs[0, 0]
+        del near_jobs[0, 0], near_jobs[0, half - 1]
     near = stack([whole] + others, after).reshape(shape)
     far = exchange(near, "replica", 1)
     far_jobs = {(1, j): (1, j) for j in range(half)}

time: 86.4 us -> 85.9 us (level)
  waiting for transfers between devices: 28.8 us -> 26.2 us
  Pallas kernels: 29.5 us -> 31.5 us
    ppermute x23, waiting for transfers between devices: 28.8 us -> 26.2 us  [exchange(): return lax.ppermute(x, axis, [(i, i ^ distance) for i in range(size)])]
    pallas_call x3 -> x4, Pallas kernels: 12.2 us -> 14.2 us  [outputs(): pl.pallas_call(functools.partial(outputs_kernel, jobs, where, capacity),...]
  transfers between devices with their start and end apart: 23 -> 23, of which waited for: 15 -> 14; matrix products, arithmetic and copies ran while one was open for 1% -> 1% of each run, Pallas kernels for 21% -> 24%
where the time goes in v16:
time: 85.9 us; the launch traced here: 85.7 us
  Pallas kernels  31.5 us (37%)
  starting transfers between devices  26.4 us (31%)
  waiting for transfers between devices  26.2 us (31%)
  between operations  0.88 us (1%)
    ppermute x23, starting transfers between devices, exchange(): return lax.ppermute(x, axis, [(i, i ^ distance) for i in range(size)])  26.4 us
    ppermute x23, waiting for transfers between devices, exchange(): return lax.ppermute(x, axis, [(i, i ^ distance) for i in range(size)])  26.2 us
    pallas_call x4, Pallas kernels, outputs(): pl.pallas_call(functools.partial(outputs_kernel, jobs, where, capacity),...  14.2 us
    pallas_call x1, Pallas kernels, left_terms(): pl.pallas_call(left_kernel, grid_spec=pltpu.PrefetchScalarGridSpec(num_sc...  8.26 us
    pallas_call x1, Pallas kernels, base_of(): pl.pallas_call(base_kernel, grid_spec=pltpu.PrefetchScalarGridSpec(num_sc...  3.17 us
    pallas_call x1, Pallas kernels, right_terms(): pl.pallas_call(functools.partial(send_kernel, half), grid_spec=pltpu.Pref...  2.23 us
  transfers between devices with their start and end apart: 23, of which 14 were waited for; matrix products, arithmetic and copies ran while one was open for 1% of the time, Pallas kernels for 24%

profile of v16, /device:TPU:1, one launch (start us, length us, event | category | flops | bytes accessed | tf_op | source)
XLA Modules:
  0.0 85.7 jit_solution(16183313293773178117)
XLA Ops:
  0.8 3.2 %base.1 = (bf16[2,96,3072]{2,1,0:T(8,128)(2,1)S(1)}, f32[2,96,3072]{2,1,0:T(8,128)S(1)}, f32[2,96,3072]{2,1,0:T(8,128)S(1)}, bf16[176,3072]{1,0:T(8,128)(2,1)S(1)}, bf16[176,3072]{1,0:T(8,128)(2,1)S(1)}) custom-call(s32[8]{0:T(128)S(1)} %stack.34.pos, f32[1,2,96,3072]{3,2,1,0:T(8,128)} %momentum_ref.1, f32[1,2,96,3072]{3,2,1,0:T(8,128)} %master_ref.1), custom_call_target="tpu_custom_call" | custom-call | flops 1000 | bytes 1000 | tf_op jit(solution)/shard_map/base/pallas_call | solution.py:520
  4.0 2.1 %collective-permute-start.6 = (bf16[176,3072]{1,0:T(8,128)(2,1)S(1)}, bf16[176,3072]{1,0:T(8,128)(2,1)S(1)}, u32[]{:S(2)}, u32[]{:S(2)}) collective-permute-start(bf16[176,3072]{1,0:T(8,128)(2,1)S(1)} %get-tuple-element.47), channel_id=1, source_target_pairs={{0,1},{1,0},{2,3},{3,2},{4,5},{5,4},{6,7},{7,6},{8,9},{9,8},{10,11... | collective-permute-start | bytes 3244040 | tf_op jit(solution)/shard_map/ppermute | solution.py:32
  6.1 1.2 %collective-permute-start.7 = (bf16[176,3072]{1,0:T(8,128)(2,1)S(1)}, bf16[176,3072]{1,0:T(8,128)(2,1)S(1)}, u32[]{:S(2)}, u32[]{:S(2)}) collective-permute-start(bf16[176,3072]{1,0:T(8,128)(2,1)S(1)} %get-tuple-element.48), channel_id=1, source_target_pairs={{0,2},{1,3},{2,0},{3,1},{4,6},{5,7},{6,4},{7,5},{8,10},{9,11},{10,... | collective-permute-start | bytes 3244040 | tf_op jit(solution)/shard_map/ppermute | solution.py:32
  7.3 8.3 %left_terms.1 = (bf16[8,192,3072]{2,1,0:T(8,128)(2,1)S(1)}, f32[112,256]{1,0:T(8,128)S(1)}, f32[112,256]{1,0:T(8,128)S(1)}) custom-call(s32[8]{0:T(128)S(1)} %stack.34.pos, bf16[1,8,192,3072]{3,2,1,0:T(8,128)(2,1)} %g_ref.1, bf16[1,8,192,3072]{3,2,1,0:T(8,128)(2,1)} %f_ref.1, bf16[8,32,3072]{2,1,0:T(8,128)(2,1)} %bitcast.19, f32[1,2688]{1,0:T(1,128)S(1)} %copy-done.2), custom_call_target="tpu_custom_call" | custom-call | flops 1000 | bytes 1000 | tf_op jit(solution)/shard_map/left_terms/pallas_call | solution.py:83
  15.6 1.3 %collective-permute-start = (f32[112,256]{1,0:T(8,128)S(1)}, f32[112,256]{1,0:T(8,128)S(1)}, u32[]{:S(2)}, u32[]{:S(2)}) collective-permute-start(f32[112,256]{1,0:T(8,128)S(1)} %get-tuple-element.43), channel_id=1, source_target_pairs={{0,4},{4,0},{8,12},{12,8},{16,20},{20,16},{24,28},{28,24},{1,5},{5... | collective-permute-start | bytes 344072 | tf_op jit(solution)/shard_map/ppermute | solution.py:32
  16.9 1.0 %collective-permute-done.refs_1_ = f32[112,256]{1,0:T(8,128)S(1)} collective-permute-done((f32[112,256]{1,0:T(8,128)S(1)}, f32[112,256]{1,0:T(8,128)S(1)}, u32[]{:S(2)}, u32[]{:S(2)}) %collective-permute-start) | collective-permute-done | bytes 114720 | tf_op jit(solution)/shard_map/ppermute | solution.py:32
  17.9 3.4 %collective-permute-start.3 = (bf16[112,256]{1,0:T(8,128)(2,1)S(1)}, bf16[112,256]{1,0:T(8,128)(2,1)S(1)}, u32[]{:S(2)}, u32[]{:S(2)}) collective-permute-start(bf16[112,256]{1,0:T(8,128)(2,1)S(1)} %add.27.refs_0_), channel_id=1, source_target_pairs={{0,24},{4,28},{8,16},{12,20},{16,8},{20,12},{24,0},{28,4},{1,25},{... | collective-permute-start | bytes 172040 | tf_op jit(solution)/shard_map/ppermute | solution.py:32
  21.6 1.3 %collective-permute-done.3.refs_3_ = bf16[112,256]{1,0:T(8,128)(2,1)S(1)} collective-permute-done((bf16[112,256]{1,0:T(8,128)(2,1)S(1)}, bf16[112,256]{1,0:T(8,128)(2,1)S(1)}, u32[]{:S(2)}, u32[]{:S(2)}) %collective-permute-start.3) | collective-permute-done | bytes 57376 | tf_op jit(solution)/shard_map/ppermute | solution.py:32
  22.9 3.4 %collective-permute-done.2.refs_2_ = bf16[112,256]{1,0:T(8,128)(2,1)S(1)} collective-permute-done((bf16[112,256]{1,0:T(8,128)(2,1)S(1)}, bf16[112,256]{1,0:T(8,128)(2,1)S(1)}, u32[]{:S(2)}, u32[]{:S(2)}) %collective-permute-start.2) | collective-permute-done | bytes 57376 | tf_op jit(solution)/shard_map/ppermute | solution.py:32
  26.4 1.0 %collective-permute-start.4 = (f32[112,256]{1,0:T(8,128)S(1)}, f32[112,256]{1,0:T(8,128)S(1)}, u32[]{:S(2)}, u32[]{:S(2)}) collective-permute-start(f32[112,256]{1,0:T(8,128)S(1)} %add.28.near_ref), channel_id=1, source_target_pairs={{0,4},{4,0},{8,12},{12,8},{16,20},{20,16},{24,28},{28,24},{1,5},{5... | collective-permute-start | bytes 344072 | tf_op jit(solution)/shard_map/ppermute | solution.py:32
  28.4 2.2 %right_send.1 = (bf16[4,1,32,3072]{3,2,1,0:T(8,128)(2,1)S(1)}, bf16[256,192]{1,0:T(8,128)(2,1)S(1)}, bf16[8,192,32]{2,1,0:T(8,128)(2,1)S(1)}, f32[32,256]{1,0:T(8,128)S(1)}) custom-call(s32[8]{0:T(128)S(1)} %stack.34.pos, f32[112,256]{1,0:T(8,128)S(1)} %add.28.near_ref, f32[112,256]{1,0:T(8,128)S(1)} %collective-permute-done.4.far_ref, ...), custom_call_target="tpu_custom_call" | custom-call | flops 1000 | bytes 1000 | tf_op jit(solution)/shard_map/right_send/pallas_call | solution.py:164
  31.0 1.5 %right_keep.1.refs_0_.keep_ref = f32[4,1,32,3072]{3,2,1,0:T(8,128)S(1)} custom-call(s32[8]{0:T(128)S(1)} %stack.34.pos, bf16[256,192]{1,0:T(8,128)(2,1)S(1)} %get-tuple-element.45.lt_ref, bf16[8,192,3072]{2,1,0:T(8,128)(2,1)S(1)} %get-tuple-element.41.comp_ref), custom_call_target="tpu_custom_call" | custom-call | flops 1000 | bytes 1000 | tf_op jit(solution)/shard_map/right_keep/pallas_call | solution.py:183
  34.3 2.2 %collective-permute-start.10 = (bf16[40,3072]{1,0:T(8,128)(2,1)S(1)}, bf16[40,3072]{1,0:T(8,128)(2,1)S(1)}, u32[]{:S(2)}, u32[]{:S(2)}) collective-permute-start(bf16[40,3072]{1,0:T(8,128)(2,1)S(1)} %get-tuple-element.53), channel_id=1, source_target_pairs={{0,3},{1,2},{2,1},{3,0},{4,7},{5,6},{6,5},{7,4},{8,11},{9,10},{10,... | collective-permute-start | bytes 737288 | tf_op jit(solution)/shard_map/ppermute | solution.py:32
  36.5 4.5 %collective-permute-done.8.refs_0_ = bf16[40,3072]{1,0:T(8,128)(2,1)S(1)} collective-permute-done((bf16[40,3072]{1,0:T(8,128)(2,1)S(1)}, bf16[40,3072]{1,0:T(8,128)(2,1)S(1)}, u32[]{:S(2)}, u32[]{:S(2)}) %collective-permute-start.8) | collective-permute-done | bytes 245792 | tf_op jit(solution)/shard_map/ppermute | solution.py:32
  41.0 5.2 %collective-permute-done.10.refs_2_ = bf16[40,3072]{1,0:T(8,128)(2,1)S(1)} collective-permute-done((bf16[40,3072]{1,0:T(8,128)(2,1)S(1)}, bf16[40,3072]{1,0:T(8,128)(2,1)S(1)}, u32[]{:S(2)}, u32[]{:S(2)}) %collective-permute-start.10) | collective-permute-done | bytes 245792 | tf_op jit(solution)/shard_map/ppermute | solution.py:32
  47.0 1.3 %collective-permute-start.11 = (bf16[112,3072]{1,0:T(8,128)(2,1)S(1)}, bf16[112,3072]{1,0:T(8,128)(2,1)S(1)}, u32[]{:S(2)}, u32[]{:S(2)}) collective-permute-start(bf16[112,3072]{1,0:T(8,128)(2,1)S(1)} %get-tuple-element.56), channel_id=1, source_target_pairs={{0,1},{1,0},{2,3},{3,2},{4,5},{5,4},{6,7},{7,6},{8,9},{9,8},{10,11... | collective-permute-start | bytes 2064392 | tf_op jit(solution)/shard_map/ppermute | solution.py:32
  49.5 1.2 %collective-permute-start.14 = (bf16[32,768]{1,0:T(8,128)(2,1)S(1)}, bf16[32,768]{1,0:T(8,128)(2,1)S(1)}, u32[]{:S(2)}, u32[]{:S(2)}) collective-permute-start(bf16[32,768]{1,0:T(8,128)(2,1)S(1)} %get-tuple-element.60), channel_id=1, source_target_pairs={{0,16},{4,20},{8,24},{12,28},{16,0},{20,4},{24,8},{28,12},{1,17},{... | collective-permute-start | bytes 147464 | tf_op jit(solution)/shard_map/ppermute | solution.py:32
  50.7 1.5 %collective-permute-start.15 = (bf16[32,768]{1,0:T(8,128)(2,1)S(1)}, bf16[32,768]{1,0:T(8,128)(2,1)S(1)}, u32[]{:S(2)}, u32[]{:S(2)}) collective-permute-start(bf16[32,768]{1,0:T(8,128)(2,1)S(1)} %get-tuple-element.61), channel_id=1, source_target_pairs={{0,24},{4,28},{8,16},{12,20},{16,8},{20,12},{24,0},{28,4},{1,25},{... | collective-permute-start | bytes 147464 | tf_op jit(solution)/shard_map/ppermute | solution.py:32
  52.2 1.7 %collective-permute-done.14.refs_2_ = bf16[32,768]{1,0:T(8,128)(2,1)S(1)} collective-permute-done((bf16[32,768]{1,0:T(8,128)(2,1)S(1)}, bf16[32,768]{1,0:T(8,128)(2,1)S(1)}, u32[]{:S(2)}, u32[]{:S(2)}) %collective-permute-start.14) | collective-permute-done | bytes 49184 | tf_op jit(solution)/shard_map/ppermute | solution.py:32
  53.9 1.8 %collective-permute-done.15.refs_3_ = bf16[32,768]{1,0:T(8,128)(2,1)S(1)} collective-permute-done((bf16[32,768]{1,0:T(8,128)(2,1)S(1)}, bf16[32,768]{1,0:T(8,128)(2,1)S(1)}, u32[]{:S(2)}, u32[]{:S(2)}) %collective-permute-start.15) | collective-permute-done | bytes 49184 | tf_op jit(solution)/shard_map/ppermute | solution.py:32
  55.7 1.5 %collective-permute-start.18 = (bf16[32,768]{1,0:T(8,128)(2,1)S(1)}, bf16[32,768]{1,0:T(8,128)(2,1)S(1)}, u32[]{:S(2)}, u32[]{:S(2)}) collective-permute-start(bf16[32,768]{1,0:T(8,128)(2,1)S(1)} %add.29.refs_0_), channel_id=1, source_target_pairs={{0,24},{4,28},{8,16},{12,20},{16,8},{20,12},{24,0},{28,4},{1,25},{... | collective-permute-start | bytes 147464 | tf_op jit(solution)/shard_map/ppermute | solution.py:32
  57.2 2.1 %collective-permute-start.16 = (bf16[32,768]{1,0:T(8,128)(2,1)S(1)}, bf16[32,768]{1,0:T(8,128)(2,1)S(1)}, u32[]{:S(2)}, u32[]{:S(2)}) collective-permute-start(bf16[32,768]{1,0:T(8,128)(2,1)S(1)} %add.29.refs_0_), channel_id=1, source_target_pairs={{0,8},{4,12},{8,0},{12,4},{16,24},{20,28},{24,16},{28,20},{1,9},{5... | collective-permute-start | bytes 147464 | tf_op jit(solution)/shard_map/ppermute | solution.py:32
  60.6 1.5 %collective-permute-done.17.refs_2_ = bf16[32,768]{1,0:T(8,128)(2,1)S(1)} collective-permute-done((bf16[32,768]{1,0:T(8,128)(2,1)S(1)}, bf16[32,768]{1,0:T(8,128)(2,1)S(1)}, u32[]{:S(2)}, u32[]{:S(2)}) %collective-permute-start.17) | collective-permute-done | bytes 49184 | tf_op jit(solution)/shard_map/ppermute | solution.py:32
  62.5 1.0 %collective-permute-done.12.refs_3_.refs_5_ = bf16[112,3072]{1,0:T(8,128)(2,1)S(1)} collective-permute-done((bf16[112,3072]{1,0:T(8,128)(2,1)S(1)}, bf16[112,3072]{1,0:T(8,128)(2,1)S(1)}, u32[]{:S(2)}, u32[]{:S(2)}) %collective-permute-start.12) | collective-permute-done | bytes 688160 | tf_op jit(solution)/shard_map/ppermute | solution.py:32
  63.5 1.6 %collective-permute-start.21 = (bf16[4,32,768]{2,1,0:T(8,128)(2,1)S(1)}, bf16[4,32,768]{2,1,0:T(8,128)(2,1)S(1)}, u32[]{:S(2)}, u32[]{:S(2)}) collective-permute-start(bf16[4,32,768]{2,1,0:T(8,128)(2,1)S(1)} %stack.35.refs_0_), channel_id=1, source_target_pairs={{0,3},{1,2},{2,1},{3,0},{4,7},{5,6},{6,5},{7,4},{8,11},{9,10},{10,... | collective-permute-start | bytes 589832 | tf_op jit(solution)/shard_map/ppermute | solution.py:32
  65.1 1.1 %collective-permute-start.19 = (bf16[4,32,768]{2,1,0:T(8,128)(2,1)S(1)}, bf16[4,32,768]{2,1,0:T(8,128)(2,1)S(1)}, u32[]{:S(2)}, u32[]{:S(2)}) collective-permute-start(bf16[4,32,768]{2,1,0:T(8,128)(2,1)S(1)} %stack.35.refs_0_), channel_id=1, source_target_pairs={{0,1},{1,0},{2,3},{3,2},{4,5},{5,4},{6,7},{7,6},{8,9},{9,8},{10,11... | collective-permute-start | bytes 589832 | tf_op jit(solution)/shard_map/ppermute | solution.py:32
  66.5 2.7 %outputs.4 = (bf16[1,8,192,3072]{3,2,1,0:T(8,128)(2,1)}, bf16[8,96,3072]{2,1,0:T(8,128)(2,1)}, f32[8,128]{1,0:T(8,128)}) custom-call(s32[8]{0:T(128)S(1)} %stack.34.pos, s32[8]{0:T(128)S(1)} %copy-done.3, bf16[8,192,3072]{2,1,0:T(8,128)(2,1)S(1)} %get-tuple-element.41.comp_ref, bf16[8,192,32]{2,1,0:T(8,128)(2,1)S(1)} %get-tuple-element.44.left_ref, ...), custom_call_target="tpu_custom_call" | custom-call | flops 1000 | bytes 1000 | tf_op jit(solution)/shard_map/outputs/pallas_call | solution.py:472
  69.2 2.1 %outputs.5 = (bf16[1,8,192,3072]{3,2,1,0:T(8,128)(2,1)}, bf16[8,96,3072]{2,1,0:T(8,128)(2,1)}, f32[8,128]{1,0:T(8,128)S(1)}) custom-call(s32[8]{0:T(128)S(1)} %stack.34.pos, s32[8]{0:T(128)S(1)} %copy-done.3, bf16[8,192,3072]{2,1,0:T(8,128)(2,1)S(1)} %get-tuple-element.41.comp_ref, ...), custom_call_target="tpu_custom_call", output_to_operand_aliasing={{0}: (7, {}), {1}: (8, {})} | custom-call | flops 1000 | bytes 1000 | tf_op jit(solution)/shard_map/outputs/pallas_call | solution.py:472
  71.3 2.4 %collective-permute-done.20.refs_2_ = bf16[4,32,768]{2,1,0:T(8,128)(2,1)S(1)} collective-permute-done((bf16[4,32,768]{2,1,0:T(8,128)(2,1)S(1)}, bf16[4,32,768]{2,1,0:T(8,128)(2,1)S(1)}, u32[]{:S(2)}, u32[]{:S(2)}) %collective-permute-start.20) | collective-permute-done | bytes 196640 | tf_op jit(solution)/shard_map/ppermute | solution.py:32
  73.8 2.4 %collective-permute-start.22 = (bf16[4,1,4,32,768]{4,3,2,1,0:T(8,128)(2,1)S(1)}, bf16[4,1,4,32,768]{4,3,2,1,0:T(8,128)(2,1)S(1)}, u32[]{:S(2)}, u32[]{:S(2)}) collective-permute-start(bf16[4,1,4,32,768]{4,3,2,1,0:T(8,128)(2,1)S(1)} %bitcast.13), channel_id=1, source_target_pairs={{0,4},{4,0},{8,12},{12,8},{16,20},{20,16},{24,28},{28,24},{1,5},{5... | collective-permute-start | bytes 2359304 | tf_op jit(solution)/shard_map/ppermute | solution.py:32
  76.2 3.3 %outputs.6 = (bf16[1,8,192,3072]{3,2,1,0:T(8,128)(2,1)}, bf16[8,96,3072]{2,1,0:T(8,128)(2,1)}, f32[8,128]{1,0:T(8,128)}) custom-call(s32[8]{0:T(128)S(1)} %stack.34.pos, s32[8]{0:T(128)S(1)} %copy-done.3, bf16[8,192,3072]{2,1,0:T(8,128)(2,1)S(1)} %get-tuple-element.41.comp_ref, ...), custom_call_target="tpu_custom_call", output_to_operand_aliasing={{0}: (7, {}), {1}: (8, {})} | custom-call | flops 1000 | bytes 1000 | tf_op jit(solution)/shard_map/outputs/pallas_call | solution.py:472
  79.5 6.2 %outputs.7 = (bf16[1,8,192,3072]{3,2,1,0:T(8,128)(2,1)}, bf16[8,96,3072]{2,1,0:T(8,128)(2,1)}, f32[1,2,96,3072]{3,2,1,0:T(8,128)}, f32[1,2,96,3072]{3,2,1,0:T(8,128)}, f32[8,128]{1,0:T(8,128)}) custom-call(s32[8]{0:T(128)S(1)} %stack.34.pos, s32[8]{0:T(128)S(1)} %copy-done.3, ...), custom_call_target="tpu_custom_call", output_to_operand_aliasing={{0}: (10, {}), {1}: (11, {})} | custom-call | flops 1000 | bytes 1000 | tf_op jit(solution)/shard_map/outputs/pallas_call | solution.py:472
  (47 shorter events, 7.6 us)
Async XLA Ops:
  0.8 6.5 %copy-start.2 = (f32[1,2688]{1,0:T(1,128)S(1)}, f32[1,2688]{1,0:T(1,128)}, u32[]{:S(2)}) copy-start(f32[1,2688]{1,0:T(1,128)} %vec_ref.1) | copy-start | bytes 32260
  4.0 28.6 %collective-permute-start.6 = (bf16[176,3072]{1,0:T(8,128)(2,1)S(1)}, bf16[176,3072]{1,0:T(8,128)(2,1)S(1)}, u32[]{:S(2)}, u32[]{:S(2)}) collective-permute-start(bf16[176,3072]{1,0:T(8,128)(2,1)S(1)} %get-tuple-element.47), channel_id=1, source_target_pairs={{0,1},{1,0},{2,3},{3,2},{4,5},{5,4},{6,7},{7,6},{8,9},{9,8},{10,11... | collective-permute-start | bytes 3244040 | tf_op jit(solution)/shard_map/ppermute | solution.py:32
  6.1 26.5 %collective-permute-start.7 = (bf16[176,3072]{1,0:T(8,128)(2,1)S(1)}, bf16[176,3072]{1,0:T(8,128)(2,1)S(1)}, u32[]{:S(2)}, u32[]{:S(2)}) collective-permute-start(bf16[176,3072]{1,0:T(8,128)(2,1)S(1)} %get-tuple-element.48), channel_id=1, source_target_pairs={{0,2},{1,3},{2,0},{3,1},{4,6},{5,7},{6,4},{7,5},{8,10},{9,11},{10,... | collective-permute-start | bytes 3244040 | tf_op jit(solution)/shard_map/ppermute | solution.py:32
  7.3 21.0 %copy-start = (f32[8,32,32]{2,1,0:T(8,128)S(1)}, f32[8,32,32]{2,1,0:T(8,128)}, u32[]{:S(2)}) copy-start(f32[8,32,32]{2,1,0:T(8,128)} %gram_ref.1) | copy-start | bytes 98308
  15.6 2.3 %collective-permute-start = (f32[112,256]{1,0:T(8,128)S(1)}, f32[112,256]{1,0:T(8,128)S(1)}, u32[]{:S(2)}, u32[]{:S(2)}) collective-permute-start(f32[112,256]{1,0:T(8,128)S(1)} %get-tuple-element.43), channel_id=1, source_target_pairs={{0,4},{4,0},{8,12},{12,8},{16,20},{20,16},{24,28},{28,24},{1,5},{5... | collective-permute-start | bytes 344072 | tf_op jit(solution)/shard_map/ppermute | solution.py:32
  17.9 5.1 %collective-permute-start.3 = (bf16[112,256]{1,0:T(8,128)(2,1)S(1)}, bf16[112,256]{1,0:T(8,128)(2,1)S(1)}, u32[]{:S(2)}, u32[]{:S(2)}) collective-permute-start(bf16[112,256]{1,0:T(8,128)(2,1)S(1)} %add.27.refs_0_), channel_id=1, source_target_pairs={{0,24},{4,28},{8,16},{12,20},{16,8},{20,12},{24,0},{28,4},{1,25},{... | collective-permute-start | bytes 172040 | tf_op jit(solution)/shard_map/ppermute | solution.py:32
  21.3 5.1 %collective-permute-start.2 = (bf16[112,256]{1,0:T(8,128)(2,1)S(1)}, bf16[112,256]{1,0:T(8,128)(2,1)S(1)}, u32[]{:S(2)}, u32[]{:S(2)}) collective-permute-start(bf16[112,256]{1,0:T(8,128)(2,1)S(1)} %add.27.refs_0_), channel_id=1, source_target_pairs={{0,16},{4,20},{8,24},{12,28},{16,0},{20,4},{24,8},{28,12},{1,17},{... | collective-permute-start | bytes 172040 | tf_op jit(solution)/shard_map/ppermute | solution.py:32
  21.3 5.1 %collective-permute-start.1 = (bf16[112,256]{1,0:T(8,128)(2,1)S(1)}, bf16[112,256]{1,0:T(8,128)(2,1)S(1)}, u32[]{:S(2)}, u32[]{:S(2)}) collective-permute-start(bf16[112,256]{1,0:T(8,128)(2,1)S(1)} %add.27.refs_0_), channel_id=1, source_target_pairs={{0,8},{4,12},{8,0},{12,4},{16,24},{20,28},{24,16},{28,20},{1,9},{5... | collective-permute-start | bytes 172040 | tf_op jit(solution)/shard_map/ppermute | solution.py:32
  26.4 2.0 %collective-permute-start.4 = (f32[112,256]{1,0:T(8,128)S(1)}, f32[112,256]{1,0:T(8,128)S(1)}, u32[]{:S(2)}, u32[]{:S(2)}) collective-permute-start(f32[112,256]{1,0:T(8,128)S(1)} %add.28.near_ref), channel_id=1, source_target_pairs={{0,4},{4,0},{8,12},{12,8},{16,20},{20,16},{24,28},{28,24},{1,5},{5... | collective-permute-start | bytes 344072 | tf_op jit(solution)/shard_map/ppermute | solution.py:32
  30.6 2.4 %collective-permute-start.5 = (bf16[4,1,32,3072]{3,2,1,0:T(8,128)(2,1)S(1)}, bf16[4,1,32,3072]{3,2,1,0:T(8,128)(2,1)S(1)}, u32[]{:S(2)}, u32[]{:S(2)}) collective-permute-start(bf16[4,1,32,3072]{3,2,1,0:T(8,128)(2,1)S(1)} %get-tuple-element.46), channel_id=1, source_target_pairs={{0,4},{4,0},{8,12},{12,8},{16,20},{20,16},{24,28},{28,24},{1,5},{5... | collective-permute-start | bytes 2359304 | tf_op jit(solution)/shard_map/ppermute | solution.py:32
  33.7 7.2 %collective-permute-start.8 = (bf16[40,3072]{1,0:T(8,128)(2,1)S(1)}, bf16[40,3072]{1,0:T(8,128)(2,1)S(1)}, u32[]{:S(2)}, u32[]{:S(2)}) collective-permute-start(bf16[40,3072]{1,0:T(8,128)(2,1)S(1)} %get-tuple-element.51), channel_id=1, source_target_pairs={{0,1},{1,0},{2,3},{3,2},{4,5},{5,4},{6,7},{7,6},{8,9},{9,8},{10,11... | collective-permute-start | bytes 737288 | tf_op jit(solution)/shard_map/ppermute | solution.py:32
  34.1 6.9 %collective-permute-start.9 = (bf16[40,3072]{1,0:T(8,128)(2,1)S(1)}, bf16[40,3072]{1,0:T(8,128)(2,1)S(1)}, u32[]{:S(2)}, u32[]{:S(2)}) collective-permute-start(bf16[40,3072]{1,0:T(8,128)(2,1)S(1)} %get-tuple-element.52), channel_id=1, source_target_pairs={{0,2},{1,3},{2,0},{3,1},{4,6},{5,7},{6,4},{7,5},{8,10},{9,11},{10,... | collective-permute-start | bytes 737288 | tf_op jit(solution)/shard_map/ppermute | solution.py:32
  34.3 11.9 %collective-permute-start.10 = (bf16[40,3072]{1,0:T(8,128)(2,1)S(1)}, bf16[40,3072]{1,0:T(8,128)(2,1)S(1)}, u32[]{:S(2)}, u32[]{:S(2)}) collective-permute-start(bf16[40,3072]{1,0:T(8,128)(2,1)S(1)} %get-tuple-element.53), channel_id=1, source_target_pairs={{0,3},{1,2},{2,1},{3,0},{4,7},{5,6},{6,5},{7,4},{8,11},{9,10},{10,... | collective-permute-start | bytes 737288 | tf_op jit(solution)/shard_map/ppermute | solution.py:32
  46.2 13.2 %copy-start.4 = (f32[2688]{0:T(1024)S(1)}, f32[2688]{0:T(1024)}, u32[]{:S(2)}) copy-start(f32[2688]{0:T(1024)} %param.19) | copy-start | bytes 32260
  46.2 13.2 %copy-start.5 = (f32[2688]{0:T(1024)S(1)}, f32[2688]{0:T(1024)}, u32[]{:S(2)}) copy-start(f32[2688]{0:T(1024)} %param.18) | copy-start | bytes 32260
  47.0 15.5 %collective-permute-start.11 = (bf16[112,3072]{1,0:T(8,128)(2,1)S(1)}, bf16[112,3072]{1,0:T(8,128)(2,1)S(1)}, u32[]{:S(2)}, u32[]{:S(2)}) collective-permute-start(bf16[112,3072]{1,0:T(8,128)(2,1)S(1)} %get-tuple-element.56), channel_id=1, source_target_pairs={{0,1},{1,0},{2,3},{3,2},{4,5},{5,4},{6,7},{7,6},{8,9},{9,8},{10,11... | collective-permute-start | bytes 2064392 | tf_op jit(solution)/shard_map/ppermute | solution.py:32
  48.3 15.1 %collective-permute-start.12 = (bf16[112,3072]{1,0:T(8,128)(2,1)S(1)}, bf16[112,3072]{1,0:T(8,128)(2,1)S(1)}, u32[]{:S(2)}, u32[]{:S(2)}) collective-permute-start(bf16[112,3072]{1,0:T(8,128)(2,1)S(1)} %get-tuple-element.57), channel_id=1, source_target_pairs={{0,2},{1,3},{2,0},{3,1},{4,6},{5,7},{6,4},{7,5},{8,10},{9,11},{10,... | collective-permute-start | bytes 2064392 | tf_op jit(solution)/shard_map/ppermute | solution.py:32
  48.6 3.6 %collective-permute-start.13 = (bf16[32,768]{1,0:T(8,128)(2,1)S(1)}, bf16[32,768]{1,0:T(8,128)(2,1)S(1)}, u32[]{:S(2)}, u32[]{:S(2)}) collective-permute-start(bf16[32,768]{1,0:T(8,128)(2,1)S(1)} %get-tuple-element.59), channel_id=1, source_target_pairs={{0,8},{4,12},{8,0},{12,4},{16,24},{20,28},{24,16},{28,20},{1,9},{5... | collective-permute-start | bytes 147464 | tf_op jit(solution)/shard_map/ppermute | solution.py:32
  49.5 4.5 %collective-permute-start.14 = (bf16[32,768]{1,0:T(8,128)(2,1)S(1)}, bf16[32,768]{1,0:T(8,128)(2,1)S(1)}, u32[]{:S(2)}, u32[]{:S(2)}) collective-permute-start(bf16[32,768]{1,0:T(8,128)(2,1)S(1)} %get-tuple-element.60), channel_id=1, source_target_pairs={{0,16},{4,20},{8,24},{12,28},{16,0},{20,4},{24,8},{28,12},{1,17},{... | collective-permute-start | bytes 147464 | tf_op jit(solution)/shard_map/ppermute | solution.py:32
  50.7 5.0 %collective-permute-start.15 = (bf16[32,768]{1,0:T(8,128)(2,1)S(1)}, bf16[32,768]{1,0:T(8,128)(2,1)S(1)}, u32[]{:S(2)}, u32[]{:S(2)}) collective-permute-start(bf16[32,768]{1,0:T(8,128)(2,1)S(1)} %get-tuple-element.61), channel_id=1, source_target_pairs={{0,24},{4,28},{8,16},{12,20},{16,8},{20,12},{24,0},{28,4},{1,25},{... | collective-permute-start | bytes 147464 | tf_op jit(solution)/shard_map/ppermute | solution.py:32
  55.7 4.8 %collective-permute-start.18 = (bf16[32,768]{1,0:T(8,128)(2,1)S(1)}, bf16[32,768]{1,0:T(8,128)(2,1)S(1)}, u32[]{:S(2)}, u32[]{:S(2)}) collective-permute-start(bf16[32,768]{1,0:T(8,128)(2,1)S(1)} %add.29.refs_0_), channel_id=1, source_target_pairs={{0,24},{4,28},{8,16},{12,20},{16,8},{20,12},{24,0},{28,4},{1,25},{... | collective-permute-start | bytes 147464 | tf_op jit(solution)/shard_map/ppermute | solution.py:32
  57.2 4.8 %collective-permute-start.17 = (bf16[32,768]{1,0:T(8,128)(2,1)S(1)}, bf16[32,768]{1,0:T(8,128)(2,1)S(1)}, u32[]{:S(2)}, u32[]{:S(2)}) collective-permute-start(bf16[32,768]{1,0:T(8,128)(2,1)S(1)} %add.29.refs_0_), channel_id=1, source_target_pairs={{0,16},{4,20},{8,24},{12,28},{16,0},{20,4},{24,8},{28,12},{1,17},{... | collective-permute-start | bytes 147464 | tf_op jit(solution)/shard_map/ppermute | solution.py:32
  57.2 4.8 %collective-permute-start.16 = (bf16[32,768]{1,0:T(8,128)(2,1)S(1)}, bf16[32,768]{1,0:T(8,128)(2,1)S(1)}, u32[]{:S(2)}, u32[]{:S(2)}) collective-permute-start(bf16[32,768]{1,0:T(8,128)(2,1)S(1)} %add.29.refs_0_), channel_id=1, source_target_pairs={{0,8},{4,12},{8,0},{12,4},{16,24},{20,28},{24,16},{28,20},{1,9},{5... | collective-permute-start | bytes 147464 | tf_op jit(solution)/shard_map/ppermute | solution.py:32
  60.0 6.5 %copy-start.1 = (f32[2688]{0:T(1024)}, f32[2688]{0:T(1024)S(1)}, u32[]{:S(2)}) copy-start(f32[2688]{0:T(1024)S(1)} %get-tuple-element.76.refs_6_) | copy-start | bytes 32260
  63.5 3.0 %copy-start.3 = (s32[8]{0:T(128)S(1)}, s32[8]{0:T(128)}, u32[]{:S(2)}) copy-start(s32[8]{0:T(128)} %owners.7) | copy-start | bytes 100
  63.5 5.7 %collective-permute-start.21 = (bf16[4,32,768]{2,1,0:T(8,128)(2,1)S(1)}, bf16[4,32,768]{2,1,0:T(8,128)(2,1)S(1)}, u32[]{:S(2)}, u32[]{:S(2)}) collective-permute-start(bf16[4,32,768]{2,1,0:T(8,128)(2,1)S(1)} %stack.35.refs_0_), channel_id=1, source_target_pairs={{0,3},{1,2},{2,1},{3,0},{4,7},{5,6},{6,5},{7,4},{8,11},{9,10},{10,... | collective-permute-start | bytes 589832 | tf_op jit(solution)/shard_map/ppermute | solution.py:32
  65.1 8.7 %collective-permute-start.20 = (bf16[4,32,768]{2,1,0:T(8,128)(2,1)S(1)}, bf16[4,32,768]{2,1,0:T(8,128)(2,1)S(1)}, u32[]{:S(2)}, u32[]{:S(2)}) collective-permute-start(bf16[4,32,768]{2,1,0:T(8,128)(2,1)S(1)} %stack.35.refs_0_), channel_id=1, source_target_pairs={{0,2},{1,3},{2,0},{3,1},{4,6},{5,7},{6,4},{7,5},{8,10},{9,11},{10,... | collective-permute-start | bytes 589832 | tf_op jit(solution)/shard_map/ppermute | solution.py:32
  65.1 8.7 %collective-permute-start.19 = (bf16[4,32,768]{2,1,0:T(8,128)(2,1)S(1)}, bf16[4,32,768]{2,1,0:T(8,128)(2,1)S(1)}, u32[]{:S(2)}, u32[]{:S(2)}) collective-permute-start(bf16[4,32,768]{2,1,0:T(8,128)(2,1)S(1)} %stack.35.refs_0_), channel_id=1, source_target_pairs={{0,1},{1,0},{2,3},{3,2},{4,5},{5,4},{6,7},{7,6},{8,9},{9,8},{10,11... | collective-permute-start | bytes 589832 | tf_op jit(solution)/shard_map/ppermute | solution.py:32
  73.8 5.7 %collective-permute-start.22 = (bf16[4,1,4,32,768]{4,3,2,1,0:T(8,128)(2,1)S(1)}, bf16[4,1,4,32,768]{4,3,2,1,0:T(8,128)(2,1)S(1)}, u32[]{:S(2)}, u32[]{:S(2)}) collective-permute-start(bf16[4,1,4,32,768]{4,3,2,1,0:T(8,128)(2,1)S(1)} %bitcast.13), channel_id=1, source_target_pairs={{0,4},{4,0},{8,12},{12,8},{16,20},{20,16},{24,28},{28,24},{1,5},{5... | collective-permute-start | bytes 2359304 | tf_op jit(solution)/shard_map/ppermute | solution.py:32

commit v17 on v16

--- a/solution.py
+++ b/solution.py
@@ -141,7 +141,9 @@
 
 def right_rows(start, pos, lt_ref, comp_ref, out_ref):
     half, upm, unit, _ = out_ref.shape
-    for t in range(half):
+
+    @pl.loop(0, half)
+    def _(t):
         k = (t + start) ^ pos[0]
         rows = pl.ds(pl.multiple_of(k * upm * unit, upm * unit), upm * unit)
         terms = jnp.dot(lt_ref[rows, :], comp_ref[k], preferred_element_type=F32)

time: 85.9 us -> 86.1 us (level)
  transfers between devices with their start and end apart: 23 -> 23, of which waited for: 14 -> 13; matrix products, arithmetic and copies ran while one was open for 1% -> 1% of each run, Pallas kernels for 24% -> 25%
where the time goes in v17:
time: 86.1 us; the launch traced here: 86 us
  Pallas kernels  32.1 us (37%)
  starting transfers between devices  26.3 us (31%)
  waiting for transfers between devices  25.9 us (30%)
  between operations  0.87 us (1%)
    ppermute x23, starting transfers between devices, exchange(): return lax.ppermute(x, axis, [(i, i ^ distance) for i in range(size)])  26.3 us
    ppermute x23, waiting for transfers between devices, exchange(): return lax.ppermute(x, axis, [(i, i ^ distance) for i in range(size)])  25.9 us
    pallas_call x4, Pallas kernels, outputs(): pl.pallas_call(functools.partial(outputs_kernel, jobs, where, capacity),...  14.2 us
    pallas_call x1, Pallas kernels, left_terms(): pl.pallas_call(left_kernel, grid_spec=pltpu.PrefetchScalarGridSpec(num_sc...  8.26 us
    pallas_call x1, Pallas kernels, base_of(): pl.pallas_call(base_kernel, grid_spec=pltpu.PrefetchScalarGridSpec(num_sc...  3.17 us
    pallas_call x1, Pallas kernels, right_terms(): pl.pallas_call(functools.partial(send_kernel, half), grid_spec=pltpu.Pref...  2.5 us
    pallas_call x1, Pallas kernels, right_terms(): pl.pallas_call(keep_kernel, grid_spec=pltpu.PrefetchScalarGridSpec(num_sc...  1.86 us
  transfers between devices with their start and end apart: 23, of which 13 were waited for; matrix products, arithmetic and copies ran while one was open for 1% of the time, Pallas kernels for 25%

profile of v17, /device:TPU:1, one launch (start us, length us, event | category | flops | bytes accessed | tf_op | source)
XLA Modules:
  0.0 86.0 jit_solution(9265060615361729368)
XLA Ops:
  0.8 3.2 %base.1 = (bf16[2,96,3072]{2,1,0:T(8,128)(2,1)S(1)}, f32[2,96,3072]{2,1,0:T(8,128)S(1)}, f32[2,96,3072]{2,1,0:T(8,128)S(1)}, bf16[176,3072]{1,0:T(8,128)(2,1)S(1)}, bf16[176,3072]{1,0:T(8,128)(2,1)S(1)}) custom-call(s32[8]{0:T(128)S(1)} %stack.34.pos, f32[1,2,96,3072]{3,2,1,0:T(8,128)} %momentum_ref.1, f32[1,2,96,3072]{3,2,1,0:T(8,128)} %master_ref.1), custom_call_target="tpu_custom_call" | custom-call | flops 1000 | bytes 1000 | tf_op jit(solution)/shard_map/base/pallas_call | solution.py:522
  4.0 2.1 %collective-permute-start.6 = (bf16[176,3072]{1,0:T(8,128)(2,1)S(1)}, bf16[176,3072]{1,0:T(8,128)(2,1)S(1)}, u32[]{:S(2)}, u32[]{:S(2)}) collective-permute-start(bf16[176,3072]{1,0:T(8,128)(2,1)S(1)} %get-tuple-element.47), channel_id=1, source_target_pairs={{0,1},{1,0},{2,3},{3,2},{4,5},{5,4},{6,7},{7,6},{8,9},{9,8},{10,11... | collective-permute-start | bytes 3244040 | tf_op jit(solution)/shard_map/ppermute | solution.py:32
  6.1 1.2 %collective-permute-start.7 = (bf16[176,3072]{1,0:T(8,128)(2,1)S(1)}, bf16[176,3072]{1,0:T(8,128)(2,1)S(1)}, u32[]{:S(2)}, u32[]{:S(2)}) collective-permute-start(bf16[176,3072]{1,0:T(8,128)(2,1)S(1)} %get-tuple-element.48), channel_id=1, source_target_pairs={{0,2},{1,3},{2,0},{3,1},{4,6},{5,7},{6,4},{7,5},{8,10},{9,11},{10,... | collective-permute-start | bytes 3244040 | tf_op jit(solution)/shard_map/ppermute | solution.py:32
  7.3 8.3 %left_terms.1 = (bf16[8,192,3072]{2,1,0:T(8,128)(2,1)S(1)}, f32[112,256]{1,0:T(8,128)S(1)}, f32[112,256]{1,0:T(8,128)S(1)}) custom-call(s32[8]{0:T(128)S(1)} %stack.34.pos, bf16[1,8,192,3072]{3,2,1,0:T(8,128)(2,1)} %g_ref.1, bf16[1,8,192,3072]{3,2,1,0:T(8,128)(2,1)} %f_ref.1, bf16[8,32,3072]{2,1,0:T(8,128)(2,1)} %bitcast.19, f32[1,2688]{1,0:T(1,128)S(1)} %copy-done.2), custom_call_target="tpu_custom_call" | custom-call | flops 1000 | bytes 1000 | tf_op jit(solution)/shard_map/left_terms/pallas_call | solution.py:83
  15.6 1.3 %collective-permute-start = (f32[112,256]{1,0:T(8,128)S(1)}, f32[112,256]{1,0:T(8,128)S(1)}, u32[]{:S(2)}, u32[]{:S(2)}) collective-permute-start(f32[112,256]{1,0:T(8,128)S(1)} %get-tuple-element.43), channel_id=1, source_target_pairs={{0,4},{4,0},{8,12},{12,8},{16,20},{20,16},{24,28},{28,24},{1,5},{5... | collective-permute-start | bytes 344072 | tf_op jit(solution)/shard_map/ppermute | solution.py:32
  16.9 1.0 %collective-permute-done.refs_1_ = f32[112,256]{1,0:T(8,128)S(1)} collective-permute-done((f32[112,256]{1,0:T(8,128)S(1)}, f32[112,256]{1,0:T(8,128)S(1)}, u32[]{:S(2)}, u32[]{:S(2)}) %collective-permute-start) | collective-permute-done | bytes 114720 | tf_op jit(solution)/shard_map/ppermute | solution.py:32
  17.9 3.4 %collective-permute-start.3 = (bf16[112,256]{1,0:T(8,128)(2,1)S(1)}, bf16[112,256]{1,0:T(8,128)(2,1)S(1)}, u32[]{:S(2)}, u32[]{:S(2)}) collective-permute-start(bf16[112,256]{1,0:T(8,128)(2,1)S(1)} %add.27.refs_0_), channel_id=1, source_target_pairs={{0,24},{4,28},{8,16},{12,20},{16,8},{20,12},{24,0},{28,4},{1,25},{... | collective-permute-start | bytes 172040 | tf_op jit(solution)/shard_map/ppermute | solution.py:32
  21.6 1.3 %collective-permute-done.3.refs_3_ = bf16[112,256]{1,0:T(8,128)(2,1)S(1)} collective-permute-done((bf16[112,256]{1,0:T(8,128)(2,1)S(1)}, bf16[112,256]{1,0:T(8,128)(2,1)S(1)}, u32[]{:S(2)}, u32[]{:S(2)}) %collective-permute-start.3) | collective-permute-done | bytes 57376 | tf_op jit(solution)/shard_map/ppermute | solution.py:32
  22.9 3.4 %collective-permute-done.2.refs_2_ = bf16[112,256]{1,0:T(8,128)(2,1)S(1)} collective-permute-done((bf16[112,256]{1,0:T(8,128)(2,1)S(1)}, bf16[112,256]{1,0:T(8,128)(2,1)S(1)}, u32[]{:S(2)}, u32[]{:S(2)}) %collective-permute-start.2) | collective-permute-done | bytes 57376 | tf_op jit(solution)/shard_map/ppermute | solution.py:32
  26.4 1.0 %collective-permute-start.4 = (f32[112,256]{1,0:T(8,128)S(1)}, f32[112,256]{1,0:T(8,128)S(1)}, u32[]{:S(2)}, u32[]{:S(2)}) collective-permute-start(f32[112,256]{1,0:T(8,128)S(1)} %add.28.near_ref), channel_id=1, source_target_pairs={{0,4},{4,0},{8,12},{12,8},{16,20},{20,16},{24,28},{28,24},{1,5},{5... | collective-permute-start | bytes 344072 | tf_op jit(solution)/shard_map/ppermute | solution.py:32
  27.4 1.0 %collective-permute-done.4.far_ref = f32[112,256]{1,0:T(8,128)S(1)} collective-permute-done((f32[112,256]{1,0:T(8,128)S(1)}, f32[112,256]{1,0:T(8,128)S(1)}, u32[]{:S(2)}, u32[]{:S(2)}) %collective-permute-start.4) | collective-permute-done | bytes 114720 | tf_op jit(solution)/shard_map/ppermute | solution.py:32
  28.4 2.5 %right_send.1 = (bf16[4,1,32,3072]{3,2,1,0:T(8,128)(2,1)S(1)}, bf16[256,192]{1,0:T(8,128)(2,1)S(1)}, bf16[8,192,32]{2,1,0:T(8,128)(2,1)S(1)}, f32[32,256]{1,0:T(8,128)S(1)}) custom-call(s32[8]{0:T(128)S(1)} %stack.34.pos, f32[112,256]{1,0:T(8,128)S(1)} %add.28.near_ref, f32[112,256]{1,0:T(8,128)S(1)} %collective-permute-done.4.far_ref, ...), custom_call_target="tpu_custom_call" | custom-call | flops 1000 | bytes 1000 | tf_op jit(solution)/shard_map/right_send/pallas_call | solution.py:166
  31.3 1.9 %right_keep.1.refs_0_.keep_ref = f32[4,1,32,3072]{3,2,1,0:T(8,128)S(1)} custom-call(s32[8]{0:T(128)S(1)} %stack.34.pos, bf16[256,192]{1,0:T(8,128)(2,1)S(1)} %get-tuple-element.45.lt_ref, bf16[8,192,3072]{2,1,0:T(8,128)(2,1)S(1)} %get-tuple-element.41.comp_ref), custom_call_target="tpu_custom_call" | custom-call | flops 1000 | bytes 1000 | tf_op jit(solution)/shard_map/right_keep/pallas_call | solution.py:185
  34.5 2.2 %collective-permute-start.10 = (bf16[40,3072]{1,0:T(8,128)(2,1)S(1)}, bf16[40,3072]{1,0:T(8,128)(2,1)S(1)}, u32[]{:S(2)}, u32[]{:S(2)}) collective-permute-start(bf16[40,3072]{1,0:T(8,128)(2,1)S(1)} %get-tuple-element.53), channel_id=1, source_target_pairs={{0,3},{1,2},{2,1},{3,0},{4,7},{5,6},{6,5},{7,4},{8,11},{9,10},{10,... | collective-permute-start | bytes 737288 | tf_op jit(solution)/shard_map/ppermute | solution.py:32
  36.7 4.5 %collective-permute-done.8.refs_0_ = bf16[40,3072]{1,0:T(8,128)(2,1)S(1)} collective-permute-done((bf16[40,3072]{1,0:T(8,128)(2,1)S(1)}, bf16[40,3072]{1,0:T(8,128)(2,1)S(1)}, u32[]{:S(2)}, u32[]{:S(2)}) %collective-permute-start.8) | collective-permute-done | bytes 245792 | tf_op jit(solution)/shard_map/ppermute | solution.py:32
  41.2 5.3 %collective-permute-done.10.refs_2_ = bf16[40,3072]{1,0:T(8,128)(2,1)S(1)} collective-permute-done((bf16[40,3072]{1,0:T(8,128)(2,1)S(1)}, bf16[40,3072]{1,0:T(8,128)(2,1)S(1)}, u32[]{:S(2)}, u32[]{:S(2)}) %collective-permute-start.10) | collective-permute-done | bytes 245792 | tf_op jit(solution)/shard_map/ppermute | solution.py:32
  47.3 1.2 %collective-permute-start.11 = (bf16[112,3072]{1,0:T(8,128)(2,1)S(1)}, bf16[112,3072]{1,0:T(8,128)(2,1)S(1)}, u32[]{:S(2)}, u32[]{:S(2)}) collective-permute-start(bf16[112,3072]{1,0:T(8,128)(2,1)S(1)} %get-tuple-element.56), channel_id=1, source_target_pairs={{0,1},{1,0},{2,3},{3,2},{4,5},{5,4},{6,7},{7,6},{8,9},{9,8},{10,11... | collective-permute-start | bytes 2064392 | tf_op jit(solution)/shard_map/ppermute | solution.py:32
  49.7 1.5 %collective-permute-start.14 = (bf16[32,768]{1,0:T(8,128)(2,1)S(1)}, bf16[32,768]{1,0:T(8,128)(2,1)S(1)}, u32[]{:S(2)}, u32[]{:S(2)}) collective-permute-start(bf16[32,768]{1,0:T(8,128)(2,1)S(1)} %get-tuple-element.60), channel_id=1, source_target_pairs={{0,16},{4,20},{8,24},{12,28},{16,0},{20,4},{24,8},{28,12},{1,17},{... | collective-permute-start | bytes 147464 | tf_op jit(solution)/shard_map/ppermute | solution.py:32
  51.2 1.2 %collective-permute-start.15 = (bf16[32,768]{1,0:T(8,128)(2,1)S(1)}, bf16[32,768]{1,0:T(8,128)(2,1)S(1)}, u32[]{:S(2)}, u32[]{:S(2)}) collective-permute-start(bf16[32,768]{1,0:T(8,128)(2,1)S(1)} %get-tuple-element.61), channel_id=1, source_target_pairs={{0,24},{4,28},{8,16},{12,20},{16,8},{20,12},{24,0},{28,4},{1,25},{... | collective-permute-start | bytes 147464 | tf_op jit(solution)/shard_map/ppermute | solution.py:32
  52.5 1.7 %collective-permute-done.14.refs_2_ = bf16[32,768]{1,0:T(8,128)(2,1)S(1)} collective-permute-done((bf16[32,768]{1,0:T(8,128)(2,1)S(1)}, bf16[32,768]{1,0:T(8,128)(2,1)S(1)}, u32[]{:S(2)}, u32[]{:S(2)}) %collective-permute-start.14) | collective-permute-done | bytes 49184 | tf_op jit(solution)/shard_map/ppermute | solution.py:32
  54.2 1.8 %collective-permute-done.15.refs_3_ = bf16[32,768]{1,0:T(8,128)(2,1)S(1)} collective-permute-done((bf16[32,768]{1,0:T(8,128)(2,1)S(1)}, bf16[32,768]{1,0:T(8,128)(2,1)S(1)}, u32[]{:S(2)}, u32[]{:S(2)}) %collective-permute-start.15) | collective-permute-done | bytes 49184 | tf_op jit(solution)/shard_map/ppermute | solution.py:32
  56.0 1.5 %collective-permute-start.18 = (bf16[32,768]{1,0:T(8,128)(2,1)S(1)}, bf16[32,768]{1,0:T(8,128)(2,1)S(1)}, u32[]{:S(2)}, u32[]{:S(2)}) collective-permute-start(bf16[32,768]{1,0:T(8,128)(2,1)S(1)} %add.29.refs_0_), channel_id=1, source_target_pairs={{0,24},{4,28},{8,16},{12,20},{16,8},{20,12},{24,0},{28,4},{1,25},{... | collective-permute-start | bytes 147464 | tf_op jit(solution)/shard_map/ppermute | solution.py:32
  57.5 2.1 %collective-permute-start.16 = (bf16[32,768]{1,0:T(8,128)(2,1)S(1)}, bf16[32,768]{1,0:T(8,128)(2,1)S(1)}, u32[]{:S(2)}, u32[]{:S(2)}) collective-permute-start(bf16[32,768]{1,0:T(8,128)(2,1)S(1)} %add.29.refs_0_), channel_id=1, source_target_pairs={{0,8},{4,12},{8,0},{12,4},{16,24},{20,28},{24,16},{28,20},{1,9},{5... | collective-permute-start | bytes 147464 | tf_op jit(solution)/shard_map/ppermute | solution.py:32
  60.9 1.5 %collective-permute-done.17.refs_2_ = bf16[32,768]{1,0:T(8,128)(2,1)S(1)} collective-permute-done((bf16[32,768]{1,0:T(8,128)(2,1)S(1)}, bf16[32,768]{1,0:T(8,128)(2,1)S(1)}, u32[]{:S(2)}, u32[]{:S(2)}) %collective-permute-start.17) | collective-permute-done | bytes 49184 | tf_op jit(solution)/shard_map/ppermute | solution.py:32
  63.7 1.6 %collective-permute-start.21 = (bf16[4,32,768]{2,1,0:T(8,128)(2,1)S(1)}, bf16[4,32,768]{2,1,0:T(8,128)(2,1)S(1)}, u32[]{:S(2)}, u32[]{:S(2)}) collective-permute-start(bf16[4,32,768]{2,1,0:T(8,128)(2,1)S(1)} %stack.35.refs_0_), channel_id=1, source_target_pairs={{0,3},{1,2},{2,1},{3,0},{4,7},{5,6},{6,5},{7,4},{8,11},{9,10},{10,... | collective-permute-start | bytes 589832 | tf_op jit(solution)/shard_map/ppermute | solution.py:32
  65.3 1.1 %collective-permute-start.19 = (bf16[4,32,768]{2,1,0:T(8,128)(2,1)S(1)}, bf16[4,32,768]{2,1,0:T(8,128)(2,1)S(1)}, u32[]{:S(2)}, u32[]{:S(2)}) collective-permute-start(bf16[4,32,768]{2,1,0:T(8,128)(2,1)S(1)} %stack.35.refs_0_), channel_id=1, source_target_pairs={{0,1},{1,0},{2,3},{3,2},{4,5},{5,4},{6,7},{7,6},{8,9},{9,8},{10,11... | collective-permute-start | bytes 589832 | tf_op jit(solution)/shard_map/ppermute | solution.py:32
  66.8 2.7 %outputs.4 = (bf16[1,8,192,3072]{3,2,1,0:T(8,128)(2,1)}, bf16[8,96,3072]{2,1,0:T(8,128)(2,1)}, f32[8,128]{1,0:T(8,128)}) custom-call(s32[8]{0:T(128)S(1)} %stack.34.pos, s32[8]{0:T(128)S(1)} %copy-done.3, bf16[8,192,3072]{2,1,0:T(8,128)(2,1)S(1)} %get-tuple-element.41.comp_ref, bf16[8,192,32]{2,1,0:T(8,128)(2,1)S(1)} %get-tuple-element.44.left_ref, ...), custom_call_target="tpu_custom_call" | custom-call | flops 1000 | bytes 1000 | tf_op jit(solution)/shard_map/outputs/pallas_call | solution.py:474
  69.5 2.1 %outputs.5 = (bf16[1,8,192,3072]{3,2,1,0:T(8,128)(2,1)}, bf16[8,96,3072]{2,1,0:T(8,128)(2,1)}, f32[8,128]{1,0:T(8,128)S(1)}) custom-call(s32[8]{0:T(128)S(1)} %stack.34.pos, s32[8]{0:T(128)S(1)} %copy-done.3, bf16[8,192,3072]{2,1,0:T(8,128)(2,1)S(1)} %get-tuple-element.41.comp_ref, ...), custom_call_target="tpu_custom_call", output_to_operand_aliasing={{0}: (7, {}), {1}: (8, {})} | custom-call | flops 1000 | bytes 1000 | tf_op jit(solution)/shard_map/outputs/pallas_call | solution.py:474
  71.6 2.4 %collective-permute-done.20.refs_2_ = bf16[4,32,768]{2,1,0:T(8,128)(2,1)S(1)} collective-permute-done((bf16[4,32,768]{2,1,0:T(8,128)(2,1)S(1)}, bf16[4,32,768]{2,1,0:T(8,128)(2,1)S(1)}, u32[]{:S(2)}, u32[]{:S(2)}) %collective-permute-start.20) | collective-permute-done | bytes 196640 | tf_op jit(solution)/shard_map/ppermute | solution.py:32
  74.1 2.4 %collective-permute-start.22 = (bf16[4,1,4,32,768]{4,3,2,1,0:T(8,128)(2,1)S(1)}, bf16[4,1,4,32,768]{4,3,2,1,0:T(8,128)(2,1)S(1)}, u32[]{:S(2)}, u32[]{:S(2)}) collective-permute-start(bf16[4,1,4,32,768]{4,3,2,1,0:T(8,128)(2,1)S(1)} %bitcast.13), channel_id=1, source_target_pairs={{0,4},{4,0},{8,12},{12,8},{16,20},{20,16},{24,28},{28,24},{1,5},{5... | collective-permute-start | bytes 2359304 | tf_op jit(solution)/shard_map/ppermute | solution.py:32
  76.5 3.3 %outputs.6 = (bf16[1,8,192,3072]{3,2,1,0:T(8,128)(2,1)}, bf16[8,96,3072]{2,1,0:T(8,128)(2,1)}, f32[8,128]{1,0:T(8,128)}) custom-call(s32[8]{0:T(128)S(1)} %stack.34.pos, s32[8]{0:T(128)S(1)} %copy-done.3, bf16[8,192,3072]{2,1,0:T(8,128)(2,1)S(1)} %get-tuple-element.41.comp_ref, ...), custom_call_target="tpu_custom_call", output_to_operand_aliasing={{0}: (7, {}), {1}: (8, {})} | custom-call | flops 1000 | bytes 1000 | tf_op jit(solution)/shard_map/outputs/pallas_call | solution.py:474
  79.8 6.2 %outputs.7 = (bf16[1,8,192,3072]{3,2,1,0:T(8,128)(2,1)}, bf16[8,96,3072]{2,1,0:T(8,128)(2,1)}, f32[1,2,96,3072]{3,2,1,0:T(8,128)}, f32[1,2,96,3072]{3,2,1,0:T(8,128)}, f32[8,128]{1,0:T(8,128)}) custom-call(s32[8]{0:T(128)S(1)} %stack.34.pos, s32[8]{0:T(128)S(1)} %copy-done.3, ...), custom_call_target="tpu_custom_call", output_to_operand_aliasing={{0}: (10, {}), {1}: (11, {})} | custom-call | flops 1000 | bytes 1000 | tf_op jit(solution)/shard_map/outputs/pallas_call | solution.py:474
  (47 shorter events, 7.3 us)
Async XLA Ops:
  0.8 6.5 %copy-start.2 = (f32[1,2688]{1,0:T(1,128)S(1)}, f32[1,2688]{1,0:T(1,128)}, u32[]{:S(2)}) copy-start(f32[1,2688]{1,0:T(1,128)} %vec_ref.1) | copy-start | bytes 32260
  4.0 29.2 %collective-permute-start.6 = (bf16[176,3072]{1,0:T(8,128)(2,1)S(1)}, bf16[176,3072]{1,0:T(8,128)(2,1)S(1)}, u32[]{:S(2)}, u32[]{:S(2)}) collective-permute-start(bf16[176,3072]{1,0:T(8,128)(2,1)S(1)} %get-tuple-element.47), channel_id=1, source_target_pairs={{0,1},{1,0},{2,3},{3,2},{4,5},{5,4},{6,7},{7,6},{8,9},{9,8},{10,11... | collective-permute-start | bytes 3244040 | tf_op jit(solution)/shard_map/ppermute | solution.py:32
  6.1 27.1 %collective-permute-start.7 = (bf16[176,3072]{1,0:T(8,128)(2,1)S(1)}, bf16[176,3072]{1,0:T(8,128)(2,1)S(1)}, u32[]{:S(2)}, u32[]{:S(2)}) collective-permute-start(bf16[176,3072]{1,0:T(8,128)(2,1)S(1)} %get-tuple-element.48), channel_id=1, source_target_pairs={{0,2},{1,3},{2,0},{3,1},{4,6},{5,7},{6,4},{7,5},{8,10},{9,11},{10,... | collective-permute-start | bytes 3244040 | tf_op jit(solution)/shard_map/ppermute | solution.py:32
  7.3 21.0 %copy-start = (f32[8,32,32]{2,1,0:T(8,128)S(1)}, f32[8,32,32]{2,1,0:T(8,128)}, u32[]{:S(2)}) copy-start(f32[8,32,32]{2,1,0:T(8,128)} %gram_ref.1) | copy-start | bytes 98308
  15.6 2.3 %collective-permute-start = (f32[112,256]{1,0:T(8,128)S(1)}, f32[112,256]{1,0:T(8,128)S(1)}, u32[]{:S(2)}, u32[]{:S(2)}) collective-permute-start(f32[112,256]{1,0:T(8,128)S(1)} %get-tuple-element.43), channel_id=1, source_target_pairs={{0,4},{4,0},{8,12},{12,8},{16,20},{20,16},{24,28},{28,24},{1,5},{5... | collective-permute-start | bytes 344072 | tf_op jit(solution)/shard_map/ppermute | solution.py:32
  17.9 5.1 %collective-permute-start.3 = (bf16[112,256]{1,0:T(8,128)(2,1)S(1)}, bf16[112,256]{1,0:T(8,128)(2,1)S(1)}, u32[]{:S(2)}, u32[]{:S(2)}) collective-permute-start(bf16[112,256]{1,0:T(8,128)(2,1)S(1)} %add.27.refs_0_), channel_id=1, source_target_pairs={{0,24},{4,28},{8,16},{12,20},{16,8},{20,12},{24,0},{28,4},{1,25},{... | collective-permute-start | bytes 172040 | tf_op jit(solution)/shard_map/ppermute | solution.py:32
  21.3 5.1 %collective-permute-start.2 = (bf16[112,256]{1,0:T(8,128)(2,1)S(1)}, bf16[112,256]{1,0:T(8,128)(2,1)S(1)}, u32[]{:S(2)}, u32[]{:S(2)}) collective-permute-start(bf16[112,256]{1,0:T(8,128)(2,1)S(1)} %add.27.refs_0_), channel_id=1, source_target_pairs={{0,16},{4,20},{8,24},{12,28},{16,0},{20,4},{24,8},{28,12},{1,17},{... | collective-permute-start | bytes 172040 | tf_op jit(solution)/shard_map/ppermute | solution.py:32
  21.3 5.1 %collective-permute-start.1 = (bf16[112,256]{1,0:T(8,128)(2,1)S(1)}, bf16[112,256]{1,0:T(8,128)(2,1)S(1)}, u32[]{:S(2)}, u32[]{:S(2)}) collective-permute-start(bf16[112,256]{1,0:T(8,128)(2,1)S(1)} %add.27.refs_0_), channel_id=1, source_target_pairs={{0,8},{4,12},{8,0},{12,4},{16,24},{20,28},{24,16},{28,20},{1,9},{5... | collective-permute-start | bytes 172040 | tf_op jit(solution)/shard_map/ppermute | solution.py:32
  26.4 2.0 %collective-permute-start.4 = (f32[112,256]{1,0:T(8,128)S(1)}, f32[112,256]{1,0:T(8,128)S(1)}, u32[]{:S(2)}, u32[]{:S(2)}) collective-permute-start(f32[112,256]{1,0:T(8,128)S(1)} %add.28.near_ref), channel_id=1, source_target_pairs={{0,4},{4,0},{8,12},{12,8},{16,20},{20,16},{24,28},{28,24},{1,5},{5... | collective-permute-start | bytes 344072 | tf_op jit(solution)/shard_map/ppermute | solution.py:32
  30.9 2.3 %collective-permute-start.5 = (bf16[4,1,32,3072]{3,2,1,0:T(8,128)(2,1)S(1)}, bf16[4,1,32,3072]{3,2,1,0:T(8,128)(2,1)S(1)}, u32[]{:S(2)}, u32[]{:S(2)}) collective-permute-start(bf16[4,1,32,3072]{3,2,1,0:T(8,128)(2,1)S(1)} %get-tuple-element.46), channel_id=1, source_target_pairs={{0,4},{4,0},{8,12},{12,8},{16,20},{20,16},{24,28},{28,24},{1,5},{5... | collective-permute-start | bytes 2359304 | tf_op jit(solution)/shard_map/ppermute | solution.py:32
  34.0 7.2 %collective-permute-start.8 = (bf16[40,3072]{1,0:T(8,128)(2,1)S(1)}, bf16[40,3072]{1,0:T(8,128)(2,1)S(1)}, u32[]{:S(2)}, u32[]{:S(2)}) collective-permute-start(bf16[40,3072]{1,0:T(8,128)(2,1)S(1)} %get-tuple-element.51), channel_id=1, source_target_pairs={{0,1},{1,0},{2,3},{3,2},{4,5},{5,4},{6,7},{7,6},{8,9},{9,8},{10,11... | collective-permute-start | bytes 737288 | tf_op jit(solution)/shard_map/ppermute | solution.py:32
  34.3 6.9 %collective-permute-start.9 = (bf16[40,3072]{1,0:T(8,128)(2,1)S(1)}, bf16[40,3072]{1,0:T(8,128)(2,1)S(1)}, u32[]{:S(2)}, u32[]{:S(2)}) collective-permute-start(bf16[40,3072]{1,0:T(8,128)(2,1)S(1)} %get-tuple-element.52), channel_id=1, source_target_pairs={{0,2},{1,3},{2,0},{3,1},{4,6},{5,7},{6,4},{7,5},{8,10},{9,11},{10,... | collective-permute-start | bytes 737288 | tf_op jit(solution)/shard_map/ppermute | solution.py:32
  34.5 12.0 %collective-permute-start.10 = (bf16[40,3072]{1,0:T(8,128)(2,1)S(1)}, bf16[40,3072]{1,0:T(8,128)(2,1)S(1)}, u32[]{:S(2)}, u32[]{:S(2)}) collective-permute-start(bf16[40,3072]{1,0:T(8,128)(2,1)S(1)} %get-tuple-element.53), channel_id=1, source_target_pairs={{0,3},{1,2},{2,1},{3,0},{4,7},{5,6},{6,5},{7,4},{8,11},{9,10},{10,... | collective-permute-start | bytes 737288 | tf_op jit(solution)/shard_map/ppermute | solution.py:32
  46.5 13.2 %copy-start.4 = (f32[2688]{0:T(1024)S(1)}, f32[2688]{0:T(1024)}, u32[]{:S(2)}) copy-start(f32[2688]{0:T(1024)} %param.19) | copy-start | bytes 32260
  46.5 13.2 %copy-start.5 = (f32[2688]{0:T(1024)S(1)}, f32[2688]{0:T(1024)}, u32[]{:S(2)}) copy-start(f32[2688]{0:T(1024)} %param.18) | copy-start | bytes 32260
  47.3 15.5 %collective-permute-start.11 = (bf16[112,3072]{1,0:T(8,128)(2,1)S(1)}, bf16[112,3072]{1,0:T(8,128)(2,1)S(1)}, u32[]{:S(2)}, u32[]{:S(2)}) collective-permute-start(bf16[112,3072]{1,0:T(8,128)(2,1)S(1)} %get-tuple-element.56), channel_id=1, source_target_pairs={{0,1},{1,0},{2,3},{3,2},{4,5},{5,4},{6,7},{7,6},{8,9},{9,8},{10,11... | collective-permute-start | bytes 2064392 | tf_op jit(solution)/shard_map/ppermute | solution.py:32
  48.6 15.1 %collective-permute-start.12 = (bf16[112,3072]{1,0:T(8,128)(2,1)S(1)}, bf16[112,3072]{1,0:T(8,128)(2,1)S(1)}, u32[]{:S(2)}, u32[]{:S(2)}) collective-permute-start(bf16[112,3072]{1,0:T(8,128)(2,1)S(1)} %get-tuple-element.57), channel_id=1, source_target_pairs={{0,2},{1,3},{2,0},{3,1},{4,6},{5,7},{6,4},{7,5},{8,10},{9,11},{10,... | collective-permute-start | bytes 2064392 | tf_op jit(solution)/shard_map/ppermute | solution.py:32
  48.9 3.6 %collective-permute-start.13 = (bf16[32,768]{1,0:T(8,128)(2,1)S(1)}, bf16[32,768]{1,0:T(8,128)(2,1)S(1)}, u32[]{:S(2)}, u32[]{:S(2)}) collective-permute-start(bf16[32,768]{1,0:T(8,128)(2,1)S(1)} %get-tuple-element.59), channel_id=1, source_target_pairs={{0,8},{4,12},{8,0},{12,4},{16,24},{20,28},{24,16},{28,20},{1,9},{5... | collective-permute-start | bytes 147464 | tf_op jit(solution)/shard_map/ppermute | solution.py:32
  49.7 4.5 %collective-permute-start.14 = (bf16[32,768]{1,0:T(8,128)(2,1)S(1)}, bf16[32,768]{1,0:T(8,128)(2,1)S(1)}, u32[]{:S(2)}, u32[]{:S(2)}) collective-permute-start(bf16[32,768]{1,0:T(8,128)(2,1)S(1)} %get-tuple-element.60), channel_id=1, source_target_pairs={{0,16},{4,20},{8,24},{12,28},{16,0},{20,4},{24,8},{28,12},{1,17},{... | collective-permute-start | bytes 147464 | tf_op jit(solution)/shard_map/ppermute | solution.py:32
  51.2 4.8 %collective-permute-start.15 = (bf16[32,768]{1,0:T(8,128)(2,1)S(1)}, bf16[32,768]{1,0:T(8,128)(2,1)S(1)}, u32[]{:S(2)}, u32[]{:S(2)}) collective-permute-start(bf16[32,768]{1,0:T(8,128)(2,1)S(1)} %get-tuple-element.61), channel_id=1, source_target_pairs={{0,24},{4,28},{8,16},{12,20},{16,8},{20,12},{24,0},{28,4},{1,25},{... | collective-permute-start | bytes 147464 | tf_op jit(solution)/shard_map/ppermute | solution.py:32
  56.0 4.8 %collective-permute-start.18 = (bf16[32,768]{1,0:T(8,128)(2,1)S(1)}, bf16[32,768]{1,0:T(8,128)(2,1)S(1)}, u32[]{:S(2)}, u32[]{:S(2)}) collective-permute-start(bf16[32,768]{1,0:T(8,128)(2,1)S(1)} %add.29.refs_0_), channel_id=1, source_target_pairs={{0,24},{4,28},{8,16},{12,20},{16,8},{20,12},{24,0},{28,4},{1,25},{... | collective-permute-start | bytes 147464 | tf_op jit(solution)/shard_map/ppermute | solution.py:32
  57.5 4.9 %collective-permute-start.17 = (bf16[32,768]{1,0:T(8,128)(2,1)S(1)}, bf16[32,768]{1,0:T(8,128)(2,1)S(1)}, u32[]{:S(2)}, u32[]{:S(2)}) collective-permute-start(bf16[32,768]{1,0:T(8,128)(2,1)S(1)} %add.29.refs_0_), channel_id=1, source_target_pairs={{0,16},{4,20},{8,24},{12,28},{16,0},{20,4},{24,8},{28,12},{1,17},{... | collective-permute-start | bytes 147464 | tf_op jit(solution)/shard_map/ppermute | solution.py:32
  57.5 4.9 %collective-permute-start.16 = (bf16[32,768]{1,0:T(8,128)(2,1)S(1)}, bf16[32,768]{1,0:T(8,128)(2,1)S(1)}, u32[]{:S(2)}, u32[]{:S(2)}) collective-permute-start(bf16[32,768]{1,0:T(8,128)(2,1)S(1)} %add.29.refs_0_), channel_id=1, source_target_pairs={{0,8},{4,12},{8,0},{12,4},{16,24},{20,28},{24,16},{28,20},{1,9},{5... | collective-permute-start | bytes 147464 | tf_op jit(solution)/shard_map/ppermute | solution.py:32
  60.3 6.5 %copy-start.1 = (f32[2688]{0:T(1024)}, f32[2688]{0:T(1024)S(1)}, u32[]{:S(2)}) copy-start(f32[2688]{0:T(1024)S(1)} %get-tuple-element.76.refs_6_) | copy-start | bytes 32260
  63.7 3.0 %copy-start.3 = (s32[8]{0:T(128)S(1)}, s32[8]{0:T(128)}, u32[]{:S(2)}) copy-start(s32[8]{0:T(128)} %owners.7) | copy-start | bytes 100
  63.7 5.7 %collective-permute-start.21 = (bf16[4,32,768]{2,1,0:T(8,128)(2,1)S(1)}, bf16[4,32,768]{2,1,0:T(8,128)(2,1)S(1)}, u32[]{:S(2)}, u32[]{:S(2)}) collective-permute-start(bf16[4,32,768]{2,1,0:T(8,128)(2,1)S(1)} %stack.35.refs_0_), channel_id=1, source_target_pairs={{0,3},{1,2},{2,1},{3,0},{4,7},{5,6},{6,5},{7,4},{8,11},{9,10},{10,... | collective-permute-start | bytes 589832 | tf_op jit(solution)/shard_map/ppermute | solution.py:32
  65.3 8.7 %collective-permute-start.20 = (bf16[4,32,768]{2,1,0:T(8,128)(2,1)S(1)}, bf16[4,32,768]{2,1,0:T(8,128)(2,1)S(1)}, u32[]{:S(2)}, u32[]{:S(2)}) collective-permute-start(bf16[4,32,768]{2,1,0:T(8,128)(2,1)S(1)} %stack.35.refs_0_), channel_id=1, source_target_pairs={{0,2},{1,3},{2,0},{3,1},{4,6},{5,7},{6,4},{7,5},{8,10},{9,11},{10,... | collective-permute-start | bytes 589832 | tf_op jit(solution)/shard_map/ppermute | solution.py:32
  65.3 8.7 %collective-permute-start.19 = (bf16[4,32,768]{2,1,0:T(8,128)(2,1)S(1)}, bf16[4,32,768]{2,1,0:T(8,128)(2,1)S(1)}, u32[]{:S(2)}, u32[]{:S(2)}) collective-permute-start(bf16[4,32,768]{2,1,0:T(8,128)(2,1)S(1)} %stack.35.refs_0_), channel_id=1, source_target_pairs={{0,1},{1,0},{2,3},{3,2},{4,5},{5,4},{6,7},{7,6},{8,9},{9,8},{10,11... | collective-permute-start | bytes 589832 | tf_op jit(solution)/shard_map/ppermute | solution.py:32
  74.1 5.7 %collective-permute-start.22 = (bf16[4,1,4,32,768]{4,3,2,1,0:T(8,128)(2,1)S(1)}, bf16[4,1,4,32,768]{4,3,2,1,0:T(8,128)(2,1)S(1)}, u32[]{:S(2)}, u32[]{:S(2)}) collective-permute-start(bf16[4,1,4,32,768]{4,3,2,1,0:T(8,128)(2,1)S(1)} %bitcast.13), channel_id=1, source_target_pairs={{0,4},{4,0},{8,12},{12,8},{16,20},{20,16},{24,28},{28,24},{1,5},{5... | collective-permute-start | bytes 2359304 | tf_op jit(solution)/shard_map/ppermute | solution.py:32
